TPU v7x, 32 devices: a whole 2x2x4 slice. The times are simulated.
32 devices in a mesh: ctx: 8 (over z, x), head: 4 (over y, core).
Axes of the slice: x: 2, y: 2, z: 4, core: 2. Of those that a mesh axis runs over, the one named last changes fastest.
Arguments:
- query_rows: bfloat16 [3072, 4096], P('ctx', 'head'), may hold values from -6 to 6
- key_rows: bfloat16 [3072, 4096], P('ctx', 'head'), may hold values from -0.375 to 0.375
- value_rows: bfloat16 [3072, 4096], P('ctx', 'head'), may hold values from -60 to 60
- log_decay: float32 [32, 3072], P('head', 'ctx'), may hold values from -1 to 0
- norm_gain: float32 [4096], P('head'), may hold values from 0.5 to 1.5
- out_weight: bfloat16 [32, 128, 6144], P('head', 'ctx'), may hold values from -1 to 1
- grad_out: bfloat16 [3072, 6144], P('ctx'), may hold values from -6 to 6
Outputs:
- grad_query: bfloat16 [3072, 4096], P('ctx', 'head')
- grad_key: bfloat16 [3072, 4096], P('ctx', 'head')
- grad_value: bfloat16 [3072, 4096], P('ctx', 'head')
- grad_weight: bfloat16 [32, 128, 6144], P('head', 'ctx')
- grad_gain: float32 [4096], P('head')
All inputs are finite; a program needn't handle non-finite values.
Results may differ from a plain program's by a relative error of at most 0.024.
Values may be sent and summed in bfloat16 or wider, within the bound.
No kernel may reach another device: no remote copies, remote signals or barrier semaphores. Data moves between devices by JAX's collectives and lax.ppermute only.
A program may use at most 192 MiB of HBM per device.

v0:
```python
import jax
import jax.numpy as jnp
from jax import lax
from jax.sharding import PartitionSpec as P


def prefix(part, axis, combine, identity, reverse):
    count = lax.axis_size(axis)
    place = lax.axis_index(axis)
    ahead = count - 1 - place if reverse else place
    gathered = jax.tree.map(lambda a: lax.all_gather(a, axis), part)
    state = jax.tree.map(lambda a, e: jnp.zeros_like(a) + jnp.asarray(e, a.dtype), part, identity)

    def one(turn, state):
        source = count - 1 - turn if reverse else turn
        return combine(
            state, jax.tree.map(lambda a: lax.dynamic_index_in_dim(a, source, 0, False), gathered)
        )

    return lax.fori_loop(0, ahead, one, state)


def decay_mask(running):
    count = running.shape[1]
    places = jnp.arange(count)
    lower = places[:, None] >= places[None, :]
    diff = running[:, :, None] - running[:, None, :]
    return jnp.where(lower[None], jnp.exp(jnp.minimum(diff, 0.0)), 0.0)


def link(earlier, later):
    return (earlier[0] * later[0], later[0][:, None, None] * earlier[1] + later[1])


def weight_gradient(normed_heads, grad_out):
    summed_total = lax.psum_scatter(
        jnp.einsum(
            "the,td->ehd", normed_heads, grad_out, preferred_element_type=jnp.float32
        ).astype(jnp.bfloat16),
        "ctx",
        scatter_dimension=0,
        tiled=True,
    ).astype(jnp.float32)
    return jnp.transpose(summed_total, (1, 0, 2)).astype(jnp.bfloat16)


def shards(query_rows, key_rows, value_rows, log_decay, norm_gain, out_weight, grad_out):
    fl = jnp.float32
    bf = jnp.bfloat16
    heads_local = log_decay.shape[0]
    tok_rows = query_rows.shape[0]
    width_local = query_rows.shape[1]
    head_size = width_local // heads_local
    queries = query_rows.reshape(tok_rows, heads_local, head_size)
    keys_local = key_rows.reshape(tok_rows, heads_local, head_size)
    values_local = value_rows.reshape(tok_rows, heads_local, head_size)
    running = jnp.cumsum(log_decay, axis=1)
    segment_accumulated = running[:, -1]
    start_decay = jnp.exp(running).T[:, :, None]
    final_attenuation = jnp.exp(segment_accumulated[:, None] - running).T[:, :, None]
    weights_mask = decay_mask(running)
    scores = jnp.einsum("thi,shi->hts", queries, keys_local, preferred_element_type=fl)
    attn_weights = (scores * weights_mask).astype(bf)
    weighted_keys = (keys_local * final_attenuation).astype(bf)
    block_state = jnp.einsum("thi,thj->hij", weighted_keys, values_local, preferred_element_type=fl)
    block_factor = jnp.exp(segment_accumulated)
    weighted_queries = (queries * start_decay).astype(bf)
    empty_state = jnp.zeros_like(block_state)
    carried = prefix(
        (block_factor, block_state), "ctx", link, (jnp.ones_like(block_factor), empty_state), False
    )
    state_in = carried[1]
    state_low = state_in.astype(bf)
    intra = jnp.einsum("hts,shj->thj", attn_weights, values_local, preferred_element_type=fl)
    inter = jnp.einsum("thi,hij->thj", queries, state_low, preferred_element_type=fl) * start_decay
    attn_out = (intra + inter).reshape(tok_rows, width_local)
    head_count = lax.axis_size("head")
    squares = lax.psum(jnp.sum(attn_out * attn_out, axis=1), "head")
    inv_rms = lax.rsqrt(squares / (width_local * head_count) + 1e-05)[:, None]
    normed = (attn_out * inv_rms * norm_gain).astype(bf)
    normed_heads = normed.reshape(tok_rows, heads_local, head_size)
    grad_weight = weight_gradient(normed_heads, grad_out)
    grad_normed = jnp.einsum(
        "td,hnd->thn",
        grad_out,
        lax.all_gather(out_weight, "ctx", axis=1, tiled=True),
        preferred_element_type=fl,
    ).reshape(tok_rows, width_local)
    grad_gain = lax.psum(jnp.sum(grad_normed * attn_out * inv_rms, axis=0), "ctx")
    scaled = grad_normed * norm_gain
    inner = lax.psum(jnp.sum(scaled * attn_out, axis=1), "head")
    inner_mean = (inner / (width_local * head_count))[:, None]
    grad_attn = (inv_rms * scaled - attn_out * inv_rms**3 * inner_mean).astype(bf)
    grad_heads = grad_attn.reshape(tok_rows, heads_local, head_size)
    block_grad = jnp.einsum("thi,thj->hij", weighted_queries, grad_heads, preferred_element_type=fl)
    returned = prefix(
        (block_factor, block_grad), "ctx", link, (jnp.ones_like(block_factor), empty_state), True
    )
    state_back = returned[1]
    back_low = state_back.astype(bf)
    grad_scores = jnp.einsum("thj,shj->hts", grad_heads, values_local, preferred_element_type=fl)
    grad_masked = (grad_scores * weights_mask).astype(bf)
    grad_q = jnp.einsum("hts,shi->thi", grad_masked, keys_local, preferred_element_type=fl)
    grad_q = (
        grad_q
        + jnp.einsum("thj,hij->thi", grad_heads, state_low, preferred_element_type=fl) * start_decay
    )
    grad_k = jnp.einsum("hts,thi->shi", grad_masked, queries, preferred_element_type=fl)
    grad_k = (
        grad_k
        + jnp.einsum("shj,hij->shi", values_local, back_low, preferred_element_type=fl)
        * final_attenuation
    )
    grad_v = jnp.einsum("hts,thj->shj", attn_weights, grad_heads, preferred_element_type=fl)
    grad_v = (
        grad_v
        + jnp.einsum("shi,hij->shj", keys_local, back_low, preferred_element_type=fl)
        * final_attenuation
    )
    grad_query = grad_q.astype(bf).reshape(tok_rows, width_local)
    grad_key = grad_k.astype(bf).reshape(tok_rows, width_local)
    grad_value = grad_v.astype(bf).reshape(tok_rows, width_local)
    return (grad_query, grad_key, grad_value, grad_weight, grad_gain)


def solution(mesh):
    return jax.shard_map(
        shards,
        mesh=mesh,
        in_specs=(
            P("ctx", "head"),
            P("ctx", "head"),
            P("ctx", "head"),
            P("head", "ctx"),
            P("head"),
            P("head", "ctx", None),
            P("ctx", None),
        ),
        out_specs=(
            P("ctx", "head"),
            P("ctx", "head"),
            P("ctx", "head"),
            P("head", "ctx", None),
            P("head"),
        ),
        check_vma=False,
    )
```

profile of v0, /device:TPU:0, one launch (start us, length us, event | category | flops | bytes accessed | tf_op | source)
XLA Modules:
  0.0 575.6 jit_solution(14948819736679036318)
XLA Ops:
  7.2 2.0 reduce-window.6
  9.2 0.2 slice_reduce_fusion
  9.5 0.2 slice_reduce_fusion.1
  9.7 1.5 copy.77
  11.3 1.2 fusion.10
  12.6 0.7 all-gather.7.cloned.1.call-update
  13.3 0.3 copy-done.7
  13.6 0.4 copy.76
  14.0 0.6 dynamic-slice
  15.2 0.2 dynamic-update-slice
  15.5 23.3 %all-reduce = f32[64]{0:T(128)S(1)} all-reduce(f32[64]{0:T(128)S(1)} %dynamic-update-slice), channel_id=2, replica_groups=mesh['ctx'=8,'head'=4] {'ctx'}, use_global_device_ids=true, to_apply=%add | all-reduce | flops 64 | bytes 512
  38.8 0.1 reshape.146
  38.9 1.8 multiply_convert_fusion.1
  40.7 1.4 copy-done.1
  42.1 2.1 fusion.12
  44.1 44.8 %all-gather.9.cloned.1.call-done = f32[64,128,128]{2,1,0:T(8,128)} async-done(((f32[8,128,128]{2,1,0:T(8,128)}), f32[64,128,128]{2,1,0:T(8,128)}) %all-gather.9.cloned.1.call-update) | async-done | bytes 4194320 | tf_op jit(solution)/shard_map/all_gather | solution.py:11
  89.0 3.0 multiply_reduce_fusion.2
  92.0 5.6 psum.21
  97.7 168.2 %all-gather.7.cloned.1.call-done = bf16[8,128,6144]{2,1,0:T(8,128)(2,1)} async-done(((bf16[8,16,6144]{2,1,0:T(8,128)(2,1)}), bf16[8,128,6144]{2,1,0:T(8,128)(2,1)}) %all-gather.7.cloned.1.call-update) | async-done | bytes 12582928 | tf_op jit(solution)/shard_map/all_gather | solution.py:86
  265.9 12.2 %multiply_reduce_fusion = (f32[8,128]{1,0:T(8,128)S(1)}, f32[384]{0:T(512)S(1)}, f32[384,8,128]{0,2,1:T(8,128)}) fusion(f32[384,8,128]{0,2,1:T(8,128)} %get-tuple-element.184, f32[384]{0:T(512)S(1)} %get-tuple-element.182, f32[8,128]{1,0:T(8,128)S(1)} %bitcast.127, bf16[8,128,6144]{2,1,0:T(8,128)(2,1)} %all-gather.7.cloned.1.call-done, ...), kind=kOutput, calls=%fused_computation.22 | convolution fusion | flops 4834195968 | bytes 20458496 | tf_op jit(solution)/shard_map/td,hnd->thn/dot_general | solution.py:83
  278.1 6.1 %psum.22 = f32[384]{0:T(512)S(1)} all-reduce(f32[384]{0:T(512)S(1)} %get-tuple-element.156), channel_id=1, replica_groups=mesh['ctx'=8,'head'=4] {'head'}, use_global_device_ids=true, to_apply=%region_7.8 | all-reduce | flops 384 | bytes 3072 | tf_op jit(solution)/shard_map/psum | solution.py:91
  284.3 2.2 subtract_convert_fusion
  286.5 1.3 fusion.11
  287.8 0.2 reduce-scatter.2.cloned.1.call-start
  288.0 12.4 %convert_bitcast_fusion = bf16[128,8,6144]{2,0,1:T(8,128)(2,1)} fusion(bf16[384,6144]{1,0:T(8,128)(2,1)} %param.17, f32[384,8,128]{0,2,1:T(8,128)} %get-tuple-element.184, f32[8,128]{1,0:T(8,128)S(1)} %bitcast.129, f32[384]{0:T(512)S(1)} %get-tuple-element.182), kind=kOutput, calls=%fused_computation.4 | convolution fusion | flops 4839309312 | bytes 18880000 | tf_op jit(solution)/shard_map/the,td->ehd/dot_general | solution.py:37
  300.4 1.8 multiply_convert_fusion
  302.3 0.8 fusion.30
  303.2 0.6 copy-done.2
  303.7 1.3 fusion.8
  305.0 2.3 copy.93
  307.3 20.1 %psum.23 = f32[1024]{0:T(1024)} all-reduce(f32[1024]{0:T(1024)S(1)} %bitcast.130), channel_id=1, replica_groups=mesh['ctx'=8,'head'=4] {'ctx'}, use_global_device_ids=true, to_apply=%region_12.13 | all-reduce | flops 1024 | bytes 8192 | tf_op jit(solution)/shard_map/psum | solution.py:89
  327.3 3.5 fusion.31
  330.9 28.6 %all-gather.11.cloned.1.call-done = f32[64,128,128]{2,1,0:T(8,128)} async-done(((f32[8,128,128]{2,1,0:T(8,128)}), f32[64,128,128]{2,1,0:T(8,128)}) %all-gather.11.cloned.1.call-update) | async-done | bytes 4194320 | tf_op jit(solution)/shard_map/all_gather | solution.py:11
  359.5 8.6 %while.27 = (s32[]{:T(128)}, f32[8,128,128]{2,1,0:T(8,128)S(1)}, s32[]{:T(128)}, f32[8,8]{1,0:T(8,128)S(1)}, f32[8,8,128,128]{3,2,1,0:T(8,128)}, /*index=5*/s32[]{:T(128)}, s32[]{:T(128)}, s32[]{:T(128)}, s32[]{:T(128)}) while((s32[]{:T(128)}, f32[8,128,128]{2,1,0:T(8,128)S(1)}, s32[]{:T(128)}, f32[8,8]{1,0:T(8,128)S(1)}, ...), condition=%wide.region_9.10_spmd, body=%wide.region_8.9_spmd.sunk | while | flops 262150 | bytes 1573115 | solution.py:20
  359.5 1.2 bitcast_add_fusion.5
  360.7 1.2 bitcast_add_fusion.5
  362.0 1.2 bitcast_add_fusion.5
  363.2 1.2 bitcast_add_fusion.5
  364.4 1.2 bitcast_add_fusion.5
  365.7 1.2 bitcast_add_fusion.5
  366.9 1.2 bitcast_add_fusion.5
  368.1 0.5 fusion.14
  368.6 1.9 copy-done.3
  370.5 0.7 fusion.6
  371.2 1.2 copy.94
  372.4 1.8 fusion.4
  374.2 1.2 copy.95
  375.4 193.7 %reduce-scatter.2.cloned.1.call-done = bf16[16,8,6144]{2,0,1:T(8,128)(2,1)} async-done(((bf16[128,8,6144]{2,0,1:T(8,128)(2,1)}), bf16[16,8,6144]{2,0,1:T(8,128)(2,1)}) %reduce-scatter.2.cloned.1.call-update) | async-done | bytes 1572880 | tf_op jit(solution)/shard_map/reduce_scatter | solution.py:36
  (39 shorter events, 0.6 us)
Async XLA Ops:
  7.2 4.1 copy-start
  7.2 81.8 %all-gather.9.cloned.1.call-start = ((), (), s32[]{:S(2)}) async-start(), calls=%async_computation.3 | async-start | bytes 4718592 | tf_op jit(solution)/shard_map/all_gather | solution.py:11
  11.2 27.7 %copy-start.4 = (bf16[384,1024]{0,1:T(8,128)(2,1)}, bf16[384,1024]{0,1:T(8,128)(2,1)S(1)}, u32[]{:S(2)}) copy-start(bf16[384,1024]{0,1:T(8,128)(2,1)S(1)} %copy.77) | copy-start | bytes 2359300
  12.5 1.1 copy-start.7
  12.5 1.5 copy-start.9
  12.5 253.4 %all-gather.7.cloned.1.call-start = ((), (), s32[]{:S(2)}) async-start(), calls=%async_computation.1 | async-start | bytes 14155776 | tf_op jit(solution)/shard_map/all_gather | solution.py:86
  13.3 346.2 %all-gather.11.cloned.1.call-start = ((), (), s32[]{:S(2)}) async-start(), calls=%async_computation.4 | async-start | bytes 4718592 | tf_op jit(solution)/shard_map/all_gather | solution.py:11
  40.7 1.4 copy-start.1
  89.0 176.9 %copy-start.8 = (f32[1024]{0:T(1024)S(1)}, f32[1024]{0:T(1024)}, u32[]{:S(2)}) copy-start(f32[1024]{0:T(1024)} %param.15) | copy-start | bytes 12292
  287.8 281.2 %reduce-scatter.2.cloned.1.call-start = ((), (), s32[]{:S(2)}) async-start(), calls=%async_computation.2 | async-start | bytes 14155776 | tf_op jit(solution)/shard_map/reduce_scatter | solution.py:36
  300.4 1.9 copy-start.5
  302.3 1.4 copy-start.2
  368.1 2.4 copy-start.3
  371.2 1.2 copy-start.6
Sparse Core Ops, SparseCore 0:
  12.6 76.2 all-gather.8
  91.1 174.6 all-gather.6
  287.9 71.4 all-gather.10
  363.4 205.5 reduce-scatter.1
where the time goes:
time: 576 us
  waiting for transfers between devices  436 us (76%)
  blocking collectives  55.1 us (10%)
  matrix products  44.4 us (8%)
  between operations  14.6 us (3%)
  other arithmetic  12.8 us (2%)
  local copies, waits for them, and re-layouts  12 us (2%)
    reduce_scatter x1, waiting for transfers between devices, weight_gradient(): lax.psum_scatter(jnp.einsum('the,td->ehd', normed_heads, grad_out, prefer...  194 us
    all_gather x1, waiting for transfers between devices, shards(): lax.all_gather(out_weight, 'ctx', axis=1, tiled=True)  168 us
    all_gather x2, waiting for transfers between devices, prefix(): gathered = jax.tree.map(lambda a: lax.all_gather(a, axis), part)  73.4 us
    unnamed x1, blocking collectives  23.3 us
    psum x1, blocking collectives, shards(): lax.psum(jnp.sum(grad_normed * attn_out * inv_rms, axis=0), 'ctx')  20.1 us
    dot_general x1, matrix products, weight_gradient(): jnp.einsum('the,td->ehd', normed_heads, grad_out, preferred_element_type=...  12.4 us
    dot_general x1, matrix products, shards(): jnp.einsum('td,hnd->thn', grad_out, lax.all_gather(out_weight, 'ctx', axi...  12.2 us
  transfers between devices with their start and end apart: 4, of which 4 were waited for; matrix products, arithmetic and copies ran while one was open for 8% of the time, Pallas kernels for 0%

commit v1 on v0

v1 whole, which is shorter than its diff:
```python
import jax
import jax.numpy as jnp
from jax import lax
from jax.sharding import PartitionSpec as P

LINE = 4
FL = jnp.float32
BF = jnp.bfloat16


def spot(z):
    return z ^ (z >> 1)


def ring_perm(count, shift):
    minor = count // LINE
    return [
        (spot(p) * minor + m, spot((p + shift) % LINE) * minor + m)
        for p in range(LINE)
        for m in range(minor)
    ]


def pair_perm(count, shift):
    minor = count // LINE
    return [
        (z * minor + m, z * minor + (m + shift) % minor)
        for z in range(LINE)
        for m in range(minor)
    ]


def butterfly(part, axis, count):
    step = 1
    while step < count:
        part = part + lax.ppermute(part, axis, [(i, i ^ step) for i in range(count)])
        step *= 2
    return part


def decay_mask(running):
    count = running.shape[1]
    places = jnp.arange(count)
    lower = places[:, None] >= places[None, :]
    diff = running[:, :, None] - running[:, None, :]
    return jnp.where(lower[None], jnp.exp(jnp.minimum(diff, 0.0)), 0.0)


def carry(part, totals, count, reverse):
    heads, size, wide = part.shape
    rows = heads * size // count
    place = lax.axis_index("ctx")
    spread = lax.all_to_all(part.reshape(count, rows, wide), "ctx", 0, 0, tiled=True)
    owner = (place * rows + jnp.arange(rows)) // size
    factor = jnp.exp(jnp.take(totals, owner, axis=1))[:, :, None]
    states = [None] * count
    state = jnp.zeros((rows, wide), FL)
    order = range(count - 1, -1, -1) if reverse else range(count)
    for b in order:
        states[b] = state.astype(BF)
        state = factor[b] * state + spread[b]
    back = lax.all_to_all(jnp.stack(states), "ctx", 0, 0, tiled=True)
    return back.reshape(heads, size, wide)


def gather_blocks(grad_out, count, head_count):
    tok, wide = grad_out.shape
    quarter = tok // head_count
    half = head_count // 2
    mine = lax.axis_index("head")
    piece = lax.dynamic_slice_in_dim(grad_out, mine * quarter, quarter, 0)
    over_y = [(i, (i + half) % head_count) for i in range(head_count)]
    over_core = [(i, i ^ 1) for i in range(head_count)]
    blocks = [grad_out]
    for _ in range(1, LINE):
        piece = lax.ppermute(piece, "ctx", ring_perm(count, 1))
        other = lax.ppermute(piece, "head", over_y)
        near = lax.ppermute(piece, "head", over_core)
        far = lax.ppermute(other, "head", over_core)
        block = jnp.zeros((tok, wide), grad_out.dtype)
        for part, who in (
            (piece, mine),
            (other, mine ^ half),
            (near, mine ^ 1),
            (far, mine ^ half ^ 1),
        ):
            block = lax.dynamic_update_slice_in_dim(block, part, who * quarter, 0)
        blocks.append(block)
    return blocks


def feature_order(heads, size, count):
    minor = count // LINE
    narrow = size // count
    place = lax.axis_index("ctx")
    z, m = place // minor, place % minor
    p = spot(z)
    col = jnp.arange(heads * size)
    shift = col // (minor * heads * narrow)
    inner = col % (minor * heads * narrow)
    turn = inner // (heads * narrow)
    head = (inner % (heads * narrow)) // narrow
    unit = inner % narrow
    slot = spot((p + shift) % LINE) * minor + (m + turn) % minor
    natural = head * size + slot * narrow + unit
    return (jnp.arange(heads * size)[:, None] == natural[None, :]).astype(BF)


def shards(query_rows, key_rows, value_rows, log_decay, norm_gain, out_weight, grad_out):
    count = lax.axis_size("ctx")
    head_count = lax.axis_size("head")
    minor = count // LINE
    heads = log_decay.shape[0]
    tok, width = query_rows.shape
    size = width // heads
    narrow = size // count
    model = grad_out.shape[1]
    own = width // LINE // minor

    blocks = gather_blocks(grad_out, count, head_count)
    weight_own = out_weight.reshape(heads * narrow, model)
    weights = jnp.concatenate(
        [weight_own]
        + [lax.ppermute(weight_own, "ctx", pair_perm(count, -s)) for s in range(1, minor)]
    )
    order = feature_order(heads, size, count)

    queries = query_rows.reshape(tok, heads, size)
    keys = key_rows.reshape(tok, heads, size)
    values = value_rows.reshape(tok, heads, size)
    running = jnp.cumsum(log_decay, axis=1)
    total = running[:, -1]
    totals = lax.all_gather(total, "ctx")
    start_decay = jnp.exp(running).T[:, :, None]
    final_decay = jnp.exp(total[:, None] - running).T[:, :, None]
    mask = decay_mask(running)
    weighted_keys = (keys * final_decay).astype(BF)
    block_state = jnp.einsum("thi,thj->hij", weighted_keys, values, preferred_element_type=FL)
    state_low = carry(block_state, totals, count, False)
    scores = jnp.einsum("thi,shi->hts", queries, keys, preferred_element_type=FL)
    attn_weights = (scores * mask).astype(BF)
    intra = jnp.einsum("hts,shj->thj", attn_weights, values, preferred_element_type=FL)
    cross = jnp.einsum("thi,hij->thj", queries, state_low, preferred_element_type=FL)
    attn_out = (intra + cross * start_decay).reshape(tok, width)
    squares = butterfly(jnp.sum(attn_out * attn_out, axis=1), "head", head_count)
    inv_rms = lax.rsqrt(squares / (width * head_count) + 1e-05)[:, None]
    normed = (attn_out * inv_rms * norm_gain).astype(BF)
    sent = jnp.dot(normed, order, preferred_element_type=FL).astype(BF)
    span = width // LINE
    normed_all = [sent[:, :span]] + [
        lax.ppermute(sent[:, s * span : (s + 1) * span], "ctx", ring_perm(count, s))
        for s in range(1, LINE)
    ]

    returned = []
    for s in range(LINE):
        piece = lax.dot_general(
            blocks[s], weights, (((1,), (1,)), ((), ())), preferred_element_type=FL
        ).astype(BF)
        if s:
            piece = lax.ppermute(piece, "ctx", ring_perm(count, -s))
        returned.append(piece)
    grad_normed = lax.dot_general(
        jnp.concatenate(returned, axis=1), order, (((1,), (1,)), ((), ())),
        preferred_element_type=FL,
    )

    summed = sum(
        lax.dot_general(a, b, (((0,), (0,)), ((), ())), preferred_element_type=FL)
        for a, b in zip(normed_all, blocks)
    ).astype(BF)
    grad_weight = summed[:own].astype(FL)
    for s in range(1, minor):
        grad_weight = grad_weight + lax.ppermute(
            summed[s * own : (s + 1) * own], "ctx", pair_perm(count, s)
        ).astype(FL)
    grad_weight = grad_weight.astype(BF).reshape(heads, narrow, model)

    grad_gain = butterfly(jnp.sum(grad_normed * attn_out * inv_rms, axis=0), "ctx", count)
    scaled = grad_normed * norm_gain
    inner = butterfly(jnp.sum(scaled * attn_out, axis=1), "head", head_count)
    inner_mean = (inner / (width * head_count))[:, None]
    grad_attn = (inv_rms * scaled - attn_out * inv_rms**3 * inner_mean).astype(BF)
    grad_heads = grad_attn.reshape(tok, heads, size)
    weighted_queries = (queries * start_decay).astype(BF)
    block_grad = jnp.einsum("thi,thj->hij", weighted_queries, grad_heads, preferred_element_type=FL)
    back_low = carry(block_grad, totals, count, True)
    grad_scores = jnp.einsum("thj,shj->hts", grad_heads, values, preferred_element_type=FL)
    grad_masked = (grad_scores * mask).astype(BF)
    grad_q = jnp.einsum("hts,shi->thi", grad_masked, keys, preferred_element_type=FL)
    grad_q = (
        grad_q
        + jnp.einsum("thj,hij->thi", grad_heads, state_low, preferred_element_type=FL) * start_decay
    )
    grad_k = jnp.einsum("hts,thi->shi", grad_masked, queries, preferred_element_type=FL)
    grad_k = (
        grad_k
        + jnp.einsum("shj,hij->shi", values, back_low, preferred_element_type=FL) * final_decay
    )
    grad_v = jnp.einsum("hts,thj->shj", attn_weights, grad_heads, preferred_element_type=FL)
    grad_v = (
        grad_v
        + jnp.einsum("shi,hij->shj", keys, back_low, preferred_element_type=FL) * final_decay
    )
    return (
        grad_q.astype(BF).reshape(tok, width),
        grad_k.astype(BF).reshape(tok, width),
        grad_v.astype(BF).reshape(tok, width),
        grad_weight,
        grad_gain,
    )


def solution(mesh):
    return jax.shard_map(
        shards,
        mesh=mesh,
        in_specs=(
            P("ctx", "head"),
            P("ctx", "head"),
            P("ctx", "head"),
            P("head", "ctx"),
            P("head"),
            P("head", "ctx", None),
            P("ctx", None),
        ),
        out_specs=(
            P("ctx", "head"),
            P("ctx", "head"),
            P("ctx", "head"),
            P("head", "ctx", None),
            P("head"),
        ),
        check_vma=False,
    )
```

time: 576 us -> 315 us (0.55)
  waiting for transfers between devices: 436 us -> 107 us
  starting transfers between devices: 0.34 us -> 43.2 us
  local copies, waits for them, and re-layouts: 12 us -> 36.9 us
  matrix products: 44.4 us -> 57.3 us
  between operations: 14.6 us -> 1.79 us
  blocking collectives: 55.1 us -> 47.1 us
  other arithmetic: 12.8 us -> 20.7 us
    all_gather x3 -> x0, waiting for transfers between devices: 242 us -> none  [the longest x1 168 us: shards(): lax.all_gather(out_weight, 'ctx', axis=1, tiled=True)]
    reduce_scatter x1 -> x0, waiting for transfers between devices: 194 us -> none  [weight_gradient(): lax.psum_scatter(jnp.einsum('the,td->ehd', normed_heads, grad_out, prefer...]
    ppermute x0 -> x27, waiting for transfers between devices: none -> 100 us  [the longest x7 45.2 us: butterfly(): lax.ppermute(part, axis, [(i, i ^ step) for i in range(count)])]
    psum x3 -> x0, blocking collectives: 31.8 us -> none  [the longest x1 20.1 us: shards(): lax.psum(jnp.sum(grad_normed * attn_out * inv_rms, axis=0), 'ctx')]
    ppermute x0 -> x27, starting transfers between devices: none -> 24.2 us  [the longest x3 4.83 us: shards(): lax.ppermute(sent[:, s * span:(s + 1) * span], 'ctx', ring_perm(count, s))]
    unnamed x1, blocking collectives: 23.3 us -> 47.1 us
    all_to_all x0 -> x4, starting transfers between devices: none -> 19 us  [the longest x2 11.4 us: carry(): lax.all_to_all(part.reshape(count, rows, wide), 'ctx', 0, 0, tiled=True)]
    dot_general x12 -> x20, matrix products: 39.6 us -> 52.4 us  [the longest x4 16.2 us: shards(): lax.dot_general(blocks[s], weights, (((1,), (1,)), ((), ())), preferred_e...]
  transfers between devices with their start and end apart: 4 -> 31, of which waited for: 4 -> 11; matrix products, arithmetic and copies ran while one was open for 8% -> 32% of each run, Pallas kernels for 0% -> 0%
where the time goes in v1:
time: 315 us; the launch traced here: 314 us
  waiting for transfers between devices  107 us (34%)
  matrix products  57.3 us (18%)
  blocking collectives  47.1 us (15%)
  starting transfers between devices  43.2 us (14%)
  local copies, waits for them, and re-layouts  36.9 us (12%)
  other arithmetic  20.7 us (7%)
    unnamed x1, blocking collectives  47.1 us
    ppermute x7, waiting for transfers between devices, butterfly(): lax.ppermute(part, axis, [(i, i ^ step) for i in range(count)])  45.2 us
    ppermute x3, waiting for transfers between devices, gather_blocks(): piece = lax.ppermute(piece, 'ctx', ring_perm(count, 1))  25.3 us
    ppermute x3, waiting for transfers between devices, gather_blocks(): other = lax.ppermute(piece, 'head', over_y)  20 us
    dot_general x4, matrix products, shards(): lax.dot_general(blocks[s], weights, (((1,), (1,)), ((), ())), preferred_e...  16.2 us
    dot_general x4, matrix products, shards(): lax.dot_general(a, b, (((0,), (0,)), ((), ())), preferred_element_type=FL)  12.6 us
    unnamed x30, local copies, waits for them, and re-layouts  12.5 us
    unnamed x13, other arithmetic  12 us
  transfers between devices with their start and end apart: 31, of which 11 were waited for; matrix products, arithmetic and copies ran while one was open for 32% of the time, Pallas kernels for 0%

profile of v1, /device:TPU:0, one launch (start us, length us, event | category | flops | bytes accessed | tf_op | source)
XLA Modules:
  0.0 313.8 jit_solution(1583843473456188291)
XLA Ops:
  0.6 2.0 reduce-window.6
  5.9 7.3 %all-to-all-start = ((f32[8,128,128]{2,1,0:T(8,128)}), f32[8,128,128]{2,1,0:T(8,128)S(1)}, u32[]{:S(2)}, u32[]{:S(2)}) async-start(f32[8,128,128]{2,1,0:T(8,128)} %fusion.15), calls=%async_computation | async-start | bytes 1048576 | tf_op jit(solution)/shard_map/all_to_all | solution.py:53
  13.1 2.4 constant_dynamic-slice_fusion
  15.6 2.0 collective-permute-start.3
  20.5 47.1 %all-reduce = f32[64]{0:T(128)S(1)} all-reduce(f32[64]{0:T(128)S(1)} %dynamic-update-slice), channel_id=2, replica_groups=mesh['ctx'=8,'head'=4] {'ctx'}, use_global_device_ids=true, to_apply=%add | all-reduce | flops 64 | bytes 512
  76.1 3.4 %all-to-all-start.1 = ((bf16[8,128,128]{2,1,0:T(8,128)(2,1)}), bf16[8,128,128]{2,1,0:T(8,128)(2,1)S(1)}, u32[]{:S(2)}, u32[]{:S(2)}) async-start(bf16[8,128,128]{2,1,0:T(8,128)(2,1)} %fusion.48), calls=%async_computation.1 | async-start | bytes 524288 | tf_op jit(solution)/shard_map/all_to_all | solution.py:62
  79.5 2.8 multiply_convert_fusion.1
  82.3 3.7 %fusion.17 = f32[8,384,128]{1,2,0:T(8,128)} fusion(bf16[8,384,384]{2,1,0:T(8,128)(2,1)} %multiply_convert_fusion.1, bf16[384,1024]{1,0:T(8,128)(2,1)S(1)} %copy-done), kind=kOutput, calls=%fused_computation.41 | convolution fusion | flops 301989888 | bytes 4718592 | tf_op jit(solution)/shard_map/hts,shj->thj/dot_general | solution.py:142
  86.0 1.6 all-to-all-done.1
  87.7 3.0 multiply_reduce_fusion.2
  93.3 2.7 broadcast.494.clone.2
  96.0 2.4 constant_dynamic-update-slice_fusion.23
  98.4 3.1 copy.76
  101.5 18.1 %collective-permute-done.1 = f32[384]{0:T(512)S(1)} collective-permute-done((f32[384]{0:T(512)S(1)}, f32[384]{0:T(512)S(1)}, u32[]{:S(2)}, u32[]{:S(2)}) %collective-permute-start.1) | collective-permute-done | bytes 1568 | tf_op jit(solution)/shard_map/ppermute | solution.py:36
  119.6 2.6 fusion.13
  122.2 2.6 collective-permute-start.22
  124.8 4.2 %fusion.38 = f32[256,6144]{1,0:T(8,128)S(1)} fusion(bf16[384,6144]{1,0:T(8,128)(2,1)} %param.15, bf16[384,1024]{1,0:T(8,128)(2,1)S(1)} %fusion.13), kind=kOutput, calls=%fused_computation.63 | convolution fusion | flops 1207959552 | bytes 11206656 | tf_op jit(solution)/shard_map/dot_general | solution.py:169
  129.1 3.7 %fusion.14 = bf16[384,256]{0,1:T(8,128)(2,1)S(1)} fusion(bf16[384,6144]{1,0:T(8,128)(2,1)S(1)} %bitcast.113, bf16[128,6144]{1,0:T(8,128)(2,1)} %collective-permute-done.2, bf16[128,6144]{1,0:T(8,128)(2,1)} %bitcast.10), kind=kOutput, calls=%fused_computation.38 | convolution fusion | flops 1214349312 | bytes 8060928 | tf_op jit(solution)/shard_map/dot_general | solution.py:157
  132.8 2.2 collective-permute-start.21
  137.0 1.6 collective-permute-start.13
  138.6 2.4 constant_dynamic-update-slice_fusion.22
  142.5 2.4 constant_dynamic-update-slice_fusion.21
  144.8 25.3 %collective-permute-done.13 = bf16[96,6144]{1,0:T(8,128)(2,1)S(1)} collective-permute-done((bf16[96,6144]{1,0:T(8,128)(2,1)}, bf16[96,6144]{1,0:T(8,128)(2,1)S(1)}, u32[]{:S(2)}, u32[]{:S(2)}) %collective-permute-start.13) | collective-permute-done | bytes 1179680 | tf_op jit(solution)/shard_map/ppermute | solution.py:76
  171.5 1.7 collective-permute-done.10
  176.1 5.1 %convolution_convert_fusion.2 = bf16[384,256]{0,1:T(8,128)(2,1)S(1)} fusion(bf16[384,6144]{1,0:T(8,128)(2,1)} %constant_dynamic-update-slice_fusion.20, bf16[128,6144]{1,0:T(8,128)(2,1)} %collective-permute-done.2, bf16[128,6144]{1,0:T(8,128)(2,1)} %bitcast.10), kind=kOutput, calls=%fused_computation.36 | convolution fusion | flops 1214349312 | bytes 8060928 | tf_op jit(solution)/shard_map/dot_general | solution.py:157
  181.2 20.0 %collective-permute-done.14 = bf16[96,6144]{1,0:T(8,128)(2,1)S(1)} collective-permute-done((bf16[96,6144]{1,0:T(8,128)(2,1)S(1)}, bf16[96,6144]{1,0:T(8,128)(2,1)S(1)}, u32[]{:S(2)}, u32[]{:S(2)}) %collective-permute-start.14) | collective-permute-done | bytes 1179680 | tf_op jit(solution)/shard_map/ppermute | solution.py:77
  202.0 3.7 %convolution_convert_fusion.1 = bf16[384,256]{0,1:T(8,128)(2,1)S(1)} fusion(bf16[384,6144]{1,0:T(8,128)(2,1)S(1)} %constant_dynamic-update-slice_fusion.16, bf16[128,6144]{1,0:T(8,128)(2,1)} %collective-permute-done.2, bf16[128,6144]{1,0:T(8,128)(2,1)} %bitcast.10), kind=kOutput, calls=%fused_computation.35 | convolution fusion | flops 1214349312 | bytes 8060928 | tf_op jit(solution)/shard_map/dot_general | solution.py:157
  205.9 1.8 collective-permute-start.12
  207.9 3.7 %convolution_convert_fusion = bf16[384,256]{0,1:T(8,128)(2,1)S(1)} fusion(bf16[384,6144]{1,0:T(8,128)(2,1)S(1)} %constant_dynamic-update-slice_fusion.12, bf16[128,6144]{1,0:T(8,128)(2,1)} %collective-permute-done.2, bf16[128,6144]{1,0:T(8,128)(2,1)} %bitcast.10), kind=kOutput, calls=%fused_computation.34 | convolution fusion | flops 1214349312 | bytes 8060928 | tf_op jit(solution)/shard_map/dot_general | solution.py:157
  212.7 4.2 %convolution_add_fusion.1 = f32[256,6144]{1,0:T(8,128)S(1)} fusion(f32[256,6144]{1,0:T(8,128)S(1)} %fusion.38, bf16[384,256]{1,0:T(8,128)(2,1)S(1)} %collective-permute-done.20, bf16[384,6144]{1,0:T(8,128)(2,1)} %constant_dynamic-update-slice_fusion.20), kind=kOutput, calls=%fused_computation.2 | convolution fusion | flops 1209532416 | bytes 17498112 | tf_op jit(solution)/shard_map/dot_general | solution.py:169
  217.5 7.8 %collective-permute-done.17 = bf16[384,256]{0,1:T(8,128)(2,1)S(1)} collective-permute-done((bf16[384,256]{0,1:T(8,128)(2,1)S(1)}, bf16[384,256]{0,1:T(8,128)(2,1)S(1)}, u32[]{:S(2)}, u32[]{:S(2)}) %collective-permute-start.17) | collective-permute-done | bytes 196640 | tf_op jit(solution)/shard_map/ppermute | solution.py:161
  226.8 1.8 fusion.73
  228.6 1.6 collective-permute-start.19
  230.2 2.3 fusion.1
  232.5 1.6 copy-done.1
  240.2 3.8 %multiply_convert_fusion = bf16[8,384,384]{2,1,0:T(8,128)(2,1)} fusion(f32[8,384]{1,0:T(8,128)S(1)} %get-tuple-element.38, pred[384,384]{1,0:T(8,128)(4,1)} %copy-done.5, bf16[384,8,128]{0,2,1:T(8,128)(2,1)S(1)} %bitcast.108, bf16[384,1024]{1,0:T(8,128)(2,1)S(1)} %copy-done), kind=kOutput, calls=%fused_computation.5 | convolution fusion | flops 307888128 | bytes 4091904 | tf_op jit(solution)/shard_map/thj,shj->hts/dot_general | solution.py:188
  245.3 4.2 %all-to-all-start.2 = ((f32[8,128,128]{2,1,0:T(8,128)}), f32[8,128,128]{2,1,0:T(8,128)}, u32[]{:S(2)}, u32[]{:S(2)}) async-start(f32[8,128,128]{2,1,0:T(8,128)} %fusion.16), calls=%async_computation.2 | async-start | bytes 1048576 | tf_op jit(solution)/shard_map/all_to_all | solution.py:53
  249.5 3.7 %fusion.72 = f32[8,128,384]{2,1,0:T(8,128)} fusion(bf16[384,8,128]{0,2,1:T(8,128)(2,1)S(1)} %bitcast.110, bf16[8,384,384]{2,1,0:T(8,128)(2,1)} %multiply_convert_fusion.1), kind=kOutput, calls=%fused_computation.185 | convolution fusion | flops 301989888 | bytes 4718592 | tf_op jit(solution)/shard_map/hts,thj->shj/dot_general | solution.py:200
  253.1 24.1 %collective-permute-done.24 = f32[1024]{0:T(1024)S(1)} collective-permute-done((f32[1024]{0:T(1024)S(1)}, f32[1024]{0:T(1024)S(1)}, u32[]{:S(2)}, u32[]{:S(2)}) %collective-permute-start.24) | collective-permute-done | bytes 4128 | tf_op jit(solution)/shard_map/ppermute | solution.py:36
  278.1 2.7 collective-permute-done.25
  282.7 2.3 copy.88
  285.9 1.8 fusion.49
  288.3 1.5 constant_dynamic-update-slice_fusion.10
  290.5 1.5 constant_dynamic-update-slice_fusion.8
  294.8 4.2 %all-to-all-start.3 = ((bf16[8,128,128]{2,1,0:T(8,128)(2,1)}), bf16[8,128,128]{2,1,0:T(8,128)(2,1)S(1)}, u32[]{:S(2)}, u32[]{:S(2)}) async-start(bf16[8,128,128]{2,1,0:T(8,128)(2,1)} %constant_dynamic-update-slice_fusion.6), calls=%async_computation.3 | async-start | bytes 524288 | tf_op jit(solution)/shard_map/all_to_all | solution.py:62
  299.0 3.4 %add_convert_fusion = bf16[128,6144]{1,0:T(8,128)(2,1)} fusion(bf16[128,6144]{1,0:T(8,128)(2,1)} %collective-permute-done.23, bf16[256,6144]{1,0:T(8,128)(2,1)} %copy-done.1), kind=kLoop, calls=%fused_computation.12 | loop fusion | flops 3145728 | bytes 4718592 | tf_op jit(solution)/shard_map/convert_element_type | solution.py:177
  302.4 4.8 %all-to-all-done.3 = bf16[8,128,128]{2,1,0:T(8,128)(2,1)S(1)} async-done(((bf16[8,128,128]{2,1,0:T(8,128)(2,1)}), bf16[8,128,128]{2,1,0:T(8,128)(2,1)S(1)}, u32[]{:S(2)}, u32[]{:S(2)}) %all-to-all-start.3) | async-done | bytes 262176 | tf_op jit(solution)/shard_map/all_to_all | solution.py:62
  310.8 1.8 fusion.7
  (127 shorter events, 48.5 us)
Async XLA Ops:
  0.6 4.1 %copy-start = (bf16[384,1024]{1,0:T(8,128)(2,1)S(1)}, bf16[384,1024]{1,0:T(8,128)(2,1)}, u32[]{:S(2)}) copy-start(bf16[384,1024]{1,0:T(8,128)(2,1)} %param.11) | copy-start | bytes 2359300
  4.7 14.4 %copy-start.7 = (u32[32]{0:T(128)S(1)}, u32[32]{0:T(128)}, u32[]{:S(2)}) copy-start(u32[32]{0:T(128)} %constant.165) | copy-start | bytes 388
  5.9 65.2 %all-to-all-start = ((f32[8,128,128]{2,1,0:T(8,128)}), f32[8,128,128]{2,1,0:T(8,128)S(1)}, u32[]{:S(2)}, u32[]{:S(2)}) async-start(f32[8,128,128]{2,1,0:T(8,128)} %fusion.15), calls=%async_computation | async-start | bytes 1048576 | tf_op jit(solution)/shard_map/all_to_all | solution.py:53
  15.6 75.1 %collective-permute-start.3 = (bf16[96,6144]{1,0:T(8,128)(2,1)}, bf16[96,6144]{1,0:T(8,128)(2,1)}, u32[]{:S(2)}, u32[]{:S(2)}) collective-permute-start(bf16[96,6144]{1,0:T(8,128)(2,1)} %constant_dynamic-slice_fusion), channel_id=1, source_target_pairs={{0,8},{4,12},{8,24},{12,28},{24,16},{28,20},{16,0},{20,4},{1,9},{5... | collective-permute-start | bytes 3538952 | tf_op jit(solution)/shard_map/ppermute | solution.py:76
  17.6 111.4 %collective-permute-start.2 = (bf16[128,6144]{1,0:T(8,128)(2,1)}, bf16[128,6144]{1,0:T(8,128)(2,1)}, u32[]{:S(2)}, u32[]{:S(2)}) collective-permute-start(bf16[128,6144]{1,0:T(8,128)(2,1)} %bitcast.10), channel_id=1, source_target_pairs={{0,4},{4,0},{8,12},{12,8},{16,20},{20,16},{24,28},{28,24},{1,5},{5... | collective-permute-start | bytes 4718600 | tf_op jit(solution)/shard_map/ppermute | solution.py:124
  70.6 11.7 %copy-start.5 = (pred[384,384]{1,0:T(8,128)(4,1)}, pred[384,384]{1,0:T(8,128)(4,1)S(1)}, u32[]{:S(2)}) copy-start(pred[384,384]{1,0:T(8,128)(4,1)S(1)} %iota_compare_fusion.5) | copy-start | bytes 442372
  76.1 11.6 %all-to-all-start.1 = ((bf16[8,128,128]{2,1,0:T(8,128)(2,1)}), bf16[8,128,128]{2,1,0:T(8,128)(2,1)S(1)}, u32[]{:S(2)}, u32[]{:S(2)}) async-start(bf16[8,128,128]{2,1,0:T(8,128)(2,1)} %fusion.48), calls=%async_computation.1 | async-start | bytes 524288 | tf_op jit(solution)/shard_map/all_to_all | solution.py:62
  90.7 1.9 collective-permute-start
  90.7 42.1 %collective-permute-start.8 = (bf16[96,6144]{1,0:T(8,128)(2,1)}, bf16[96,6144]{1,0:T(8,128)(2,1)}, u32[]{:S(2)}, u32[]{:S(2)}) collective-permute-start(bf16[96,6144]{1,0:T(8,128)(2,1)} %collective-permute-done.3), channel_id=1, source_target_pairs={{0,8},{4,12},{8,24},{12,28},{24,16},{28,20},{16,0},{20,4},{1,9},{5... | collective-permute-start | bytes 3538952 | tf_op jit(solution)/shard_map/ppermute | solution.py:76
  91.0 45.9 %collective-permute-start.4 = (bf16[96,6144]{1,0:T(8,128)(2,1)}, bf16[96,6144]{1,0:T(8,128)(2,1)}, u32[]{:S(2)}, u32[]{:S(2)}) collective-permute-start(bf16[96,6144]{1,0:T(8,128)(2,1)} %collective-permute-done.3), channel_id=1, source_target_pairs={{0,2},{1,3},{2,0},{3,1},{4,6},{5,7},{6,4},{7,5},{8,10},{9,11},{10,... | collective-permute-start | bytes 3538952 | tf_op jit(solution)/shard_map/ppermute | solution.py:77
  92.5 48.4 %collective-permute-start.5 = (bf16[96,6144]{1,0:T(8,128)(2,1)}, bf16[96,6144]{1,0:T(8,128)(2,1)}, u32[]{:S(2)}, u32[]{:S(2)}) collective-permute-start(bf16[96,6144]{1,0:T(8,128)(2,1)} %collective-permute-done.3), channel_id=1, source_target_pairs={{0,1},{1,0},{2,3},{3,2},{4,5},{5,4},{6,7},{7,6},{8,9},{9,8},{10,11... | collective-permute-start | bytes 3538952 | tf_op jit(solution)/shard_map/ppermute | solution.py:78
  92.6 27.0 %collective-permute-start.1 = (f32[384]{0:T(512)S(1)}, f32[384]{0:T(512)S(1)}, u32[]{:S(2)}, u32[]{:S(2)}) collective-permute-start(f32[384]{0:T(512)S(1)} %add.302), channel_id=1, source_target_pairs={{0,2},{1,3},{2,0},{3,1},{4,6},{5,7},{6,4},{7,5},{8,10},{9,11},{10,... | collective-permute-start | bytes 4616 | tf_op jit(solution)/shard_map/ppermute | solution.py:36
  96.0 23.5 %copy-start.6 = (f32[1024]{0:T(1024)S(1)}, f32[1024]{0:T(1024)}, u32[]{:S(2)}) copy-start(f32[1024]{0:T(1024)} %param.13) | copy-start | bytes 12292
  122.2 6.9 %slice-start = ((s8[4718592]{0:T(1024)(128)(4,1)}), s8[4194304]{0:T(1024)(128)(4,1)S(1)}, s32[]{:S(2)}) async-start(s8[4718592]{0:T(1024)(128)(4,1)} %bitcast.112), calls=%async_computation.4 | async-start | bytes 8388608
  122.2 6.9 %slice-start.1 = ((s8[4718592]{0:T(1024)(128)(4,1)}), s8[524288]{0:T(1024)(128)(4,1)S(1)}, s32[]{:S(2)}) async-start(s8[4718592]{0:T(1024)(128)(4,1)} %bitcast.112), calls=%async_computation.5 | async-start | bytes 1048576
  122.2 104.5 %collective-permute-start.22 = (bf16[384,256]{1,0:T(8,128)(2,1)S(1)}, bf16[384,256]{1,0:T(8,128)(2,1)S(1)}, u32[]{:S(2)}, u32[]{:S(2)}) collective-permute-start(bf16[384,256]{1,0:T(8,128)(2,1)S(1)} %get-tuple-element.46), channel_id=1, source_target_pairs={{0,16},{4,20},{8,0},{12,4},{24,8},{28,12},{16,24},{20,28},{1,17},{... | collective-permute-start | bytes 589832 | tf_op jit(solution)/shard_map/ppermute | solution.py:151
  129.0 82.5 %collective-permute-start.20 = (bf16[384,256]{1,0:T(8,128)(2,1)S(1)}, bf16[384,256]{1,0:T(8,128)(2,1)S(1)}, u32[]{:S(2)}, u32[]{:S(2)}) collective-permute-start(bf16[384,256]{1,0:T(8,128)(2,1)S(1)} %get-tuple-element.47), channel_id=1, source_target_pairs={{0,8},{4,12},{8,24},{12,28},{24,16},{28,20},{16,0},{20,4},{1,9},{5... | collective-permute-start | bytes 589832 | tf_op jit(solution)/shard_map/ppermute | solution.py:151
  132.8 97.4 %collective-permute-start.21 = (bf16[384,256]{1,0:T(8,128)(2,1)S(1)}, bf16[384,256]{1,0:T(8,128)(2,1)S(1)}, u32[]{:S(2)}, u32[]{:S(2)}) collective-permute-start(bf16[384,256]{1,0:T(8,128)(2,1)S(1)} %get-tuple-element.45), channel_id=1, source_target_pairs={{0,24},{4,28},{8,16},{12,20},{24,0},{28,4},{16,8},{20,12},{1,25},{... | collective-permute-start | bytes 589832 | tf_op jit(solution)/shard_map/ppermute | solution.py:151
  137.0 33.2 %collective-permute-start.13 = (bf16[96,6144]{1,0:T(8,128)(2,1)}, bf16[96,6144]{1,0:T(8,128)(2,1)S(1)}, u32[]{:S(2)}, u32[]{:S(2)}) collective-permute-start(bf16[96,6144]{1,0:T(8,128)(2,1)} %collective-permute-done.8), channel_id=1, source_target_pairs={{0,8},{4,12},{8,24},{12,28},{24,16},{28,20},{16,0},{20,4},{1,9},{5... | collective-permute-start | bytes 3538952 | tf_op jit(solution)/shard_map/ppermute | solution.py:76
  140.9 29.9 %collective-permute-start.9 = (bf16[96,6144]{1,0:T(8,128)(2,1)}, bf16[96,6144]{1,0:T(8,128)(2,1)S(1)}, u32[]{:S(2)}, u32[]{:S(2)}) collective-permute-start(bf16[96,6144]{1,0:T(8,128)(2,1)} %collective-permute-done.8), channel_id=1, source_target_pairs={{0,2},{1,3},{2,0},{3,1},{4,6},{5,7},{6,4},{7,5},{8,10},{9,11},{10,... | collective-permute-start | bytes 3538952 | tf_op jit(solution)/shard_map/ppermute | solution.py:77
  170.1 3.1 collective-permute-start.10
  170.8 4.0 %collective-permute-start.6 = (bf16[96,6144]{1,0:T(8,128)(2,1)}, bf16[96,6144]{1,0:T(8,128)(2,1)S(1)}, u32[]{:S(2)}, u32[]{:S(2)}) collective-permute-start(bf16[96,6144]{1,0:T(8,128)(2,1)} %collective-permute-done.4), channel_id=1, source_target_pairs={{0,1},{1,0},{2,3},{3,2},{4,5},{5,4},{6,7},{7,6},{8,9},{9,8},{10,11... | collective-permute-start | bytes 3538952 | tf_op jit(solution)/shard_map/ppermute | solution.py:79
  173.2 28.0 %collective-permute-start.14 = (bf16[96,6144]{1,0:T(8,128)(2,1)S(1)}, bf16[96,6144]{1,0:T(8,128)(2,1)S(1)}, u32[]{:S(2)}, u32[]{:S(2)}) collective-permute-start(bf16[96,6144]{1,0:T(8,128)(2,1)S(1)} %collective-permute-done.13), channel_id=1, source_target_pairs={{0,2},{1,3},{2,0},{3,1},{4,6},{5,7},{6,4},{7,5},{8,10},{9,11},{10,... | collective-permute-start | bytes 3538952 | tf_op jit(solution)/shard_map/ppermute | solution.py:77
  174.9 26.5 %collective-permute-start.11 = (bf16[96,6144]{1,0:T(8,128)(2,1)S(1)}, bf16[96,6144]{1,0:T(8,128)(2,1)S(1)}, u32[]{:S(2)}, u32[]{:S(2)}) collective-permute-start(bf16[96,6144]{1,0:T(8,128)(2,1)S(1)} %collective-permute-done.9), channel_id=1, source_target_pairs={{0,1},{1,0},{2,3},{3,2},{4,5},{5,4},{6,7},{7,6},{8,9},{9,8},{10,11... | collective-permute-start | bytes 3538952 | tf_op jit(solution)/shard_map/ppermute | solution.py:79
  201.2 4.5 %collective-permute-start.15 = (bf16[96,6144]{1,0:T(8,128)(2,1)S(1)}, bf16[96,6144]{1,0:T(8,128)(2,1)S(1)}, u32[]{:S(2)}, u32[]{:S(2)}) collective-permute-start(bf16[96,6144]{1,0:T(8,128)(2,1)S(1)} %collective-permute-done.13), channel_id=1, source_target_pairs={{0,1},{1,0},{2,3},{3,2},{4,5},{5,4},{6,7},{7,6},{8,9},{9,8},{10,11... | collective-permute-start | bytes 3538952 | tf_op jit(solution)/shard_map/ppermute | solution.py:78
  201.3 4.6 %collective-permute-start.16 = (bf16[96,6144]{1,0:T(8,128)(2,1)S(1)}, bf16[96,6144]{1,0:T(8,128)(2,1)S(1)}, u32[]{:S(2)}, u32[]{:S(2)}) collective-permute-start(bf16[96,6144]{1,0:T(8,128)(2,1)S(1)} %collective-permute-done.14), channel_id=1, source_target_pairs={{0,1},{1,0},{2,3},{3,2},{4,5},{5,4},{6,7},{7,6},{8,9},{9,8},{10,11... | collective-permute-start | bytes 3538952 | tf_op jit(solution)/shard_map/ppermute | solution.py:79
  205.7 11.2 %collective-permute-start.7 = (bf16[384,256]{0,1:T(8,128)(2,1)S(1)}, bf16[384,256]{0,1:T(8,128)(2,1)S(1)}, u32[]{:S(2)}, u32[]{:S(2)}) collective-permute-start(bf16[384,256]{0,1:T(8,128)(2,1)S(1)} %convolution_convert_fusion.2), channel_id=1, source_target_pairs={{0,16},{4,20},{8,0},{12,4},{24,8},{28,12},{16,24},{20,28},{1,17},{... | collective-permute-start | bytes 589832 | tf_op jit(solution)/shard_map/ppermute | solution.py:161
  205.9 11.5 %collective-permute-start.12 = (bf16[384,256]{0,1:T(8,128)(2,1)S(1)}, bf16[384,256]{0,1:T(8,128)(2,1)S(1)}, u32[]{:S(2)}, u32[]{:S(2)}) collective-permute-start(bf16[384,256]{0,1:T(8,128)(2,1)S(1)} %convolution_convert_fusion.1), channel_id=1, source_target_pairs={{0,24},{4,28},{8,16},{12,20},{24,0},{28,4},{16,8},{20,12},{1,25},{... | collective-permute-start | bytes 589832 | tf_op jit(solution)/shard_map/ppermute | solution.py:161
  211.5 13.7 %copy-start.4 = (f32[384,1024]{1,0:T(8,128)S(1)}, f32[384,1024]{1,0:T(8,128)}, u32[]{:S(2)}) copy-start(f32[384,1024]{1,0:T(8,128)} %copy.76) | copy-start | bytes 4718596
  211.6 13.7 %collective-permute-start.17 = (bf16[384,256]{0,1:T(8,128)(2,1)S(1)}, bf16[384,256]{0,1:T(8,128)(2,1)S(1)}, u32[]{:S(2)}, u32[]{:S(2)}) collective-permute-start(bf16[384,256]{0,1:T(8,128)(2,1)S(1)} %convolution_convert_fusion), channel_id=1, source_target_pairs={{0,8},{4,12},{8,24},{12,28},{24,16},{28,20},{16,0},{20,4},{1,9},{5... | collective-permute-start | bytes 589832 | tf_op jit(solution)/shard_map/ppermute | solution.py:161
  226.7 1.9 collective-permute-start.18
  228.6 8.8 %collective-permute-start.19 = (f32[384]{0:T(512)S(1)}, f32[384]{0:T(512)S(1)}, u32[]{:S(2)}, u32[]{:S(2)}) collective-permute-start(f32[384]{0:T(512)S(1)} %add.323), channel_id=1, source_target_pairs={{0,2},{1,3},{2,0},{3,1},{4,6},{5,7},{6,4},{7,5},{8,10},{9,11},{10,... | collective-permute-start | bytes 4616 | tf_op jit(solution)/shard_map/ppermute | solution.py:36
  232.5 1.6 copy-start.1
  235.4 63.6 %collective-permute-start.23 = (bf16[128,6144]{1,0:T(8,128)(2,1)}, bf16[128,6144]{1,0:T(8,128)(2,1)}, u32[]{:S(2)}, u32[]{:S(2)}) collective-permute-start(bf16[128,6144]{1,0:T(8,128)(2,1)} %slice.187), channel_id=1, source_target_pairs={{0,4},{4,0},{8,12},{12,8},{16,20},{20,16},{24,28},{28,24},{1,5},{5... | collective-permute-start | bytes 4718600 | tf_op jit(solution)/shard_map/ppermute | solution.py:174
  236.8 40.4 %collective-permute-start.24 = (f32[1024]{0:T(1024)S(1)}, f32[1024]{0:T(1024)S(1)}, u32[]{:S(2)}, u32[]{:S(2)}) collective-permute-start(f32[1024]{0:T(1024)S(1)} %get-tuple-element.21), channel_id=1, source_target_pairs={{0,4},{4,0},{8,12},{12,8},{16,20},{20,16},{24,28},{28,24},{1,5},{5... | collective-permute-start | bytes 12296 | tf_op jit(solution)/shard_map/ppermute | solution.py:36
  245.3 40.6 %all-to-all-start.2 = ((f32[8,128,128]{2,1,0:T(8,128)}), f32[8,128,128]{2,1,0:T(8,128)}, u32[]{:S(2)}, u32[]{:S(2)}) async-start(f32[8,128,128]{2,1,0:T(8,128)} %fusion.16), calls=%async_computation.2 | async-start | bytes 1048576 | tf_op jit(solution)/shard_map/all_to_all | solution.py:53
  249.5 27.7 %copy-start.2 = (bf16[8,384,384]{2,1,0:T(8,128)(2,1)S(1)}, bf16[8,384,384]{2,1,0:T(8,128)(2,1)}, u32[]{:S(2)}) copy-start(bf16[8,384,384]{2,1,0:T(8,128)(2,1)} %multiply_convert_fusion) | copy-start | bytes 7077892
  277.2 3.6 %collective-permute-start.25 = (f32[1024]{0:T(1024)S(1)}, f32[1024]{0:T(1024)S(1)}, u32[]{:S(2)}, u32[]{:S(2)}) collective-permute-start(f32[1024]{0:T(1024)S(1)} %add.339), channel_id=1, source_target_pairs={{0,8},{4,12},{8,0},{12,4},{16,24},{20,28},{24,16},{28,20},{1,9},{5... | collective-permute-start | bytes 12296 | tf_op jit(solution)/shard_map/ppermute | solution.py:36
  280.8 4.5 %collective-permute-start.26 = (f32[1024]{0:T(1024)S(1)}, f32[1024]{0:T(1024)S(1)}, u32[]{:S(2)}, u32[]{:S(2)}) collective-permute-start(f32[1024]{0:T(1024)S(1)} %add.340), channel_id=1, source_target_pairs={{0,16},{4,20},{8,24},{12,28},{16,0},{20,4},{24,8},{28,12},{1,17},{... | collective-permute-start | bytes 12296 | tf_op jit(solution)/shard_map/ppermute | solution.py:36
  294.8 12.4 %all-to-all-start.3 = ((bf16[8,128,128]{2,1,0:T(8,128)(2,1)}), bf16[8,128,128]{2,1,0:T(8,128)(2,1)S(1)}, u32[]{:S(2)}, u32[]{:S(2)}) async-start(bf16[8,128,128]{2,1,0:T(8,128)(2,1)} %constant_dynamic-update-slice_fusion.6), calls=%async_computation.3 | async-start | bytes 524288 | tf_op jit(solution)/shard_map/all_to_all | solution.py:62
  307.2 1.7 copy-start.3

commit v2 on v1

v2 whole, which is shorter than its diff:
```python
import functools

import jax
import jax.numpy as jnp
from jax import lax
from jax.experimental import pallas as pl
from jax.experimental.pallas import tpu as pltpu
from jax.sharding import PartitionSpec as P

LINE = 4
CHUNKS = 2
FL = jnp.float32
BF = jnp.bfloat16
PARAMS = pltpu.CompilerParams(vmem_limit_bytes=24 * 1024 * 1024)
EXACT = lax.Precision.HIGHEST
NN = (((1,), (0,)), ((), ()))
NT = (((1,), (1,)), ((), ()))
TN = (((0,), (0,)), ((), ()))


def dot(a, b, dims, precision=None):
    return lax.dot_general(a, b, dims, preferred_element_type=FL, precision=precision)


def spec(shape, index=None):
    return pl.BlockSpec(shape, index or (lambda *_: (0,) * len(shape)))


SCALAR = pl.BlockSpec(memory_space=pltpu.SMEM)


def cost(flops, moved):
    return pl.CostEstimate(flops=flops, bytes_accessed=moved, transcendentals=0)


def after(x, *others):
    return lax.optimization_barrier((x, *others))[0]


def spot(z):
    return z ^ (z >> 1)


def ring_perm(count, shift):
    minor = count // LINE
    return [
        (spot(p) * minor + m, spot((p + shift) % LINE) * minor + m)
        for p in range(LINE)
        for m in range(minor)
    ]


def pair_perm(count, shift):
    minor = count // LINE
    return [
        (z * minor + m, z * minor + (m + shift) % minor)
        for z in range(LINE)
        for m in range(minor)
    ]


def butterfly(part, axis, count):
    step = 1
    while step < count:
        part = part + lax.ppermute(part, axis, [(i, i ^ step) for i in range(count)])
        step *= 2
    return part


def column(table, head):
    lanes = lax.broadcasted_iota(jnp.int32, table.shape, 1)
    return jnp.sum(jnp.where(lanes == head, table, 0.0), axis=1, keepdims=True)


def fold_rows(x):
    width = x.shape[1]
    total = x[:, :128]
    for at in range(128, width, 128):
        total = total + x[:, at : at + 128]
    return jnp.sum(total.T, axis=0, keepdims=True)


def mask_of(run_ref, runs, head):
    tok = run_ref.shape[1]
    row = run_ref[pl.ds(head, 1), :]
    lower = lax.broadcasted_iota(jnp.int32, (tok, tok), 0) >= lax.broadcasted_iota(
        jnp.int32, (tok, tok), 1
    )
    return jnp.where(lower, jnp.exp(jnp.minimum(runs - row, 0.0)), 0.0)


def put_state(out_ref, state, total):
    parts, deep, wide = out_ref.shape
    rows = deep - 16
    high = total.astype(BF)
    low = (total - high.astype(FL)).astype(BF)
    for j in range(parts):
        out_ref[j, :rows] = state[j * rows : (j + 1) * rows].astype(BF)
        out_ref[j, rows : rows + 8] = jnp.broadcast_to(high, (8, wide))
        out_ref[j, rows + 8 :] = jnp.broadcast_to(low, (8, wide))


def state_kernel(decay_ref, k_ref, v_ref, out_ref, run_ref, turned_ref):
    head = pl.program_id(0)
    tok = decay_ref.shape[1]

    @pl.when(head == 0)
    def _():
        first = lax.broadcasted_iota(jnp.int32, (tok, tok), 0)
        second = lax.broadcasted_iota(jnp.int32, (tok, tok), 1)
        run_ref[...] = dot(decay_ref[...], (first <= second).astype(FL), NN, EXACT)
        turned_ref[...] = dot((second <= first).astype(FL), decay_ref[...], NT, EXACT)

    run = column(turned_ref[...], head)
    total = run[tok - 1 :, :]
    weighted = (k_ref[...].astype(FL) * jnp.exp(total - run)).astype(BF)
    put_state(out_ref, dot(weighted, v_ref[...], TN), total)


def scan_kernel(reverse, in_ref, out_ref):
    count, deep, wide = in_ref.shape
    rows = deep - 16
    state = jnp.zeros((rows // 8, 8, wide), FL)
    for b in range(count - 1, -1, -1) if reverse else range(count):
        out_ref[b] = state.reshape(rows, wide).astype(BF)
        total = in_ref[b, rows:].astype(FL)
        factor = jnp.exp(total[:8] + total[8:])
        state = factor[None] * state + in_ref[b, :rows].astype(FL).reshape(rows // 8, 8, wide)


def carry(part, reverse):
    count, deep, wide = part.shape
    rows = deep - 16
    spread = lax.all_to_all(part, "ctx", 0, 0, tiled=True)
    states = pl.pallas_call(
        functools.partial(scan_kernel, reverse),
        out_shape=jax.ShapeDtypeStruct((count, rows, wide), BF),
        compiler_params=PARAMS,
        name="scan",
    )(spread)
    return lax.all_to_all(states, "ctx", 0, 0, tiled=True)


def weights_kernel(q_ref, k_ref, v_ref, run_ref, turned_ref, aw_ref, intra_ref):
    head = pl.program_id(0)
    mask = mask_of(run_ref, column(turned_ref[...], head), head)
    weights = (dot(q_ref[...], k_ref[...], NT) * mask).astype(BF)
    aw_ref[0] = weights
    intra_ref[...] = dot(weights, v_ref[...], NN)


def attend_kernel(q_ref, state_ref, turned_ref, intra_ref, out_ref, squares_ref, held_ref):
    head = pl.program_id(0)
    start = jnp.exp(column(turned_ref[...], head))
    out = intra_ref[...] + dot(q_ref[...], state_ref[0], NN) * start
    out_ref[...] = out

    @pl.when(head == 0)
    def _():
        held_ref[...] = jnp.zeros_like(held_ref)

    held_ref[...] += out * out

    @pl.when(head == pl.num_programs(0) - 1)
    def _():
        squares_ref[...] = fold_rows(held_ref[...])


def norm_kernel(mine_ref, attn_ref, inv_ref, gain_ref, order_ref, own_ref, *sent):
    normed = (attn_ref[...] * inv_ref[...] * gain_ref[...]).astype(BF)
    tok, width = normed.shape
    span = width // LINE
    parts = 4
    quarter = tok // parts
    own_ref[...] = dot(normed, order_ref[:, :span], NN).astype(BF)
    for s, ref in enumerate(sent, 1):
        part = dot(normed, order_ref[:, s * span : (s + 1) * span], NN).astype(BF)
        for j in range(parts):
            to = pl.multiple_of((mine_ref[0] ^ j) * quarter, 16)
            ref[pl.ds(to, quarter), :] = part[j * quarter : (j + 1) * quarter]


def product_kernel(pieces, weights, add, last, *refs):
    refs = list(refs)
    mine_ref = refs.pop(0)
    x = [refs.pop(0) for _ in range(pieces)]
    w = [refs.pop(0) for _ in range(weights)]
    extra = refs.pop(0) if add else None
    out_ref, held_ref = refs
    step = pl.program_id(0)

    @pl.when(step == 0)
    def _():
        held_ref[...] = extra[...] if add else jnp.zeros_like(held_ref)

    rows = jnp.concatenate([r[...] for r in x], axis=0)
    cols = jnp.concatenate([r[...] for r in w], axis=0)
    held_ref[...] += dot(rows, cols, NT)

    @pl.when(step == pl.num_programs(0) - 1)
    def _():
        if not last:
            out_ref[...] = held_ref[...]
        elif pieces == 1:
            out_ref[...] = held_ref[...].astype(BF)
        else:
            quarter = x[0].shape[0]
            for j in range(pieces):
                to = pl.multiple_of((mine_ref[0] ^ j) * quarter, 16)
                out_ref[pl.ds(to, quarter), :] = held_ref[
                    j * quarter : (j + 1) * quarter, :
                ].astype(BF)


def product(mine, pieces, weights, chunk, chunks, held):
    tok = sum(p.shape[0] for p in pieces)
    deep = pieces[0].shape[1]
    tile = 1024
    steps = deep // tile
    span = sum(w.shape[0] for w in weights)
    base = chunk * steps
    last = chunk == chunks - 1
    more = [] if held is None else [held]
    return pl.pallas_call(
        functools.partial(product_kernel, len(pieces), len(weights), len(more), last),
        grid=(steps,),
        in_specs=[SCALAR]
        + [spec((p.shape[0], tile), lambda i: (0, i)) for p in pieces]
        + [spec((w.shape[0], tile), lambda i: (0, base + i)) for w in weights]
        + [spec((tok, span)) for _ in more],
        out_specs=spec((tok, span)),
        out_shape=jax.ShapeDtypeStruct((tok, span), BF if last else FL),
        scratch_shapes=[pltpu.VMEM((tok, span), FL)],
        compiler_params=PARAMS,
        cost_estimate=cost(2 * tok * deep * span, 2 * deep * (tok + span)),
        name="product",
    )(mine, *pieces, *weights, *more)


def outer_kernel(lots, own, *refs):
    refs = list(refs)
    normed = [refs.pop(0) for _ in lots]
    x = [[refs.pop(0) for _ in range(k)] for k in lots]
    turned_ref = refs.pop()

    @pl.when(pl.program_id(0) == 0)
    def _():
        turned_ref[...] = jnp.concatenate([r[...] for r in normed], axis=0).T

    rows = jnp.concatenate([r[...] for lot in x for r in lot], axis=0)
    out = dot(turned_ref[...], rows, NN).astype(BF)
    for s, ref in enumerate(refs):
        ref[...] = out[s * own : (s + 1) * own]


def outer(normed, grad_out, lots, chunk, own):
    tok, span = normed[0].shape
    deep = lots[0][0].shape[1]
    tile = 512
    steps = deep // tile
    base = chunk * steps
    flat = [p for lot in lots for p in lot]
    minor = span // own
    return pl.pallas_call(
        functools.partial(outer_kernel, [1] + [len(lot) for lot in lots], own),
        grid=(steps,),
        in_specs=[spec((tok, span)) for _ in normed]
        + [spec((tok, tile), lambda i: (0, base + i))]
        + [spec((p.shape[0], tile), lambda i: (0, i)) for p in flat],
        out_specs=[spec((own, tile), lambda i: (0, i))] * minor,
        out_shape=[jax.ShapeDtypeStruct((own, deep), BF)] * minor,
        scratch_shapes=[pltpu.VMEM((span, tok * LINE), BF)],
        compiler_params=PARAMS,
        cost_estimate=cost(2 * tok * LINE * deep * span, 2 * deep * (tok * LINE + span)),
        name="outer",
    )(*normed, grad_out, *flat)


def final_kernel(chunks, minor, *refs):
    out_ref = refs[-1]
    deep = refs[0].shape[1]
    for c in range(chunks):
        total = refs[c * minor][...].astype(FL)
        for s in range(1, minor):
            total = total + refs[c * minor + s][...].astype(FL)
        out_ref[:, c * deep : (c + 1) * deep] = total.astype(BF)


def back_kernel(order_ref, attn_ref, inv_ref, gain_ref, *refs):
    pieces, (out_ref, sum_ref, inner_ref) = refs[:LINE], refs[LINE:]
    span = pieces[0].shape[1]
    grad = dot(pieces[0][...], order_ref[:, :span], NT)
    for s in range(1, LINE):
        grad = grad + dot(pieces[s][...], order_ref[:, s * span : (s + 1) * span], NT)
    out_ref[...] = grad.astype(BF)
    both = grad * attn_ref[...]
    sum_ref[...] = jnp.sum(both * inv_ref[...], axis=0, keepdims=True)
    inner_ref[...] = fold_rows(both * gain_ref[...])


def grad_kernel(
    grad_ref, attn_ref, inv_ref, shift_ref, gain_ref, q_ref, turned_ref, out_ref, state_ref
):
    run = column(turned_ref[...], pl.program_id(0))
    scaled = grad_ref[...].astype(FL) * gain_ref[...]
    grad = (inv_ref[...] * scaled - attn_ref[...] * shift_ref[...]).astype(BF)
    out_ref[...] = grad
    weighted = (q_ref[...].astype(FL) * jnp.exp(run)).astype(BF)
    put_state(state_ref, dot(weighted, grad, TN), run[run.shape[0] - 1 :, :])


def inside_kernel(
    grad_ref, q_ref, k_ref, v_ref, aw_ref, run_ref, turned_ref, state_ref, gq_ref, gk_ref, gv_ref
):
    head = pl.program_id(0)
    run = column(turned_ref[...], head)
    grad = grad_ref[...]
    masked = (dot(grad, v_ref[...], NT) * mask_of(run_ref, run, head)).astype(BF)
    gq = dot(masked, k_ref[...], NN) + dot(grad, state_ref[0], NT) * jnp.exp(run)
    gq_ref[...] = gq.astype(BF)
    gk_ref[...] = dot(masked, q_ref[...], TN)
    gv_ref[...] = dot(aw_ref[0], grad, TN)


def outside_kernel(k_ref, v_ref, state_ref, turned_ref, gk_in, gv_in, gk_ref, gv_ref):
    run = column(turned_ref[...], pl.program_id(0))
    final = jnp.exp(run[run.shape[0] - 1 :, :] - run)
    state = state_ref[0]
    gk_ref[...] = (gk_in[...] + dot(v_ref[...], state, NT) * final).astype(BF)
    gv_ref[...] = (gv_in[...] + dot(k_ref[...], state, NN) * final).astype(BF)


def feature_order(heads, size, count):
    minor = count // LINE
    narrow = size // count
    place = lax.axis_index("ctx")
    z, m = place // minor, place % minor
    p = spot(z)
    col = jnp.arange(heads * size)
    shift = col // (minor * heads * narrow)
    inner = col % (minor * heads * narrow)
    turn = inner // (heads * narrow)
    head = (inner % (heads * narrow)) // narrow
    unit = inner % narrow
    slot = spot((p + shift) % LINE) * minor + (m + turn) % minor
    natural = head * size + slot * narrow + unit
    return (jnp.arange(heads * size)[:, None] == natural[None, :]).astype(BF)


def shards(query_rows, key_rows, value_rows, log_decay, norm_gain, out_weight, grad_out):
    count = lax.axis_size("ctx")
    head_count = lax.axis_size("head")
    minor = count // LINE
    heads = log_decay.shape[0]
    tok, width = query_rows.shape
    size = width // heads
    narrow = size // count
    model = grad_out.shape[1]
    own = width // LINE // minor
    span = width // LINE
    rows = width // count
    features = width * head_count
    half = head_count // 2
    over_y = [(i, (i + half) % head_count) for i in range(head_count)]
    over_core = [(i, i ^ 1) for i in range(head_count)]

    mine = lax.axis_index("head").astype(jnp.int32)
    quarter = tok // head_count
    deep = model // CHUNKS
    tokens = mine.reshape(1)

    def first_piece(c):
        return lax.dynamic_slice(grad_out, (mine * quarter, c * deep), (quarter, deep))

    blk = spec((tok, size), lambda h: (0, h))
    state_blk = spec((1, size, size), lambda h: (h, 0, 0))
    put_blk = spec((count // heads, rows + 16, size), lambda h: (h, 0, 0))
    put_shape = jax.ShapeDtypeStruct((count, rows + 16, size), BF)
    square_blk = spec((1, tok, tok), lambda h: (h, 0, 0))
    run_blk, turned_blk, col_blk = spec((heads, tok)), spec((tok, heads)), spec((tok, 1))
    wide_f = jax.ShapeDtypeStruct((tok, width), FL)
    wide_b = jax.ShapeDtypeStruct((tok, width), BF)
    block_cost = cost(2 * heads * tok * size * size, 6 * tok * width)
    square_cost = cost(8 * heads * tok * tok * size, 16 * tok * width)

    def per_head(kernel, in_specs, out_specs, out_shape, name, est, scratch=()):
        return pl.pallas_call(
            kernel, grid=(heads,), in_specs=in_specs, out_specs=out_specs, out_shape=out_shape,
            compiler_params=PARAMS, name=name, cost_estimate=est, scratch_shapes=list(scratch),
        )

    def ring(x):
        return lax.ppermute(x, "ctx", ring_perm(count, 1))

    pieces = [[None] * LINE for _ in range(CHUNKS)]
    pieces[0][1] = ring(first_piece(0))
    put, run, turned = per_head(
        state_kernel, [run_blk, blk, blk], [put_blk, run_blk, turned_blk],
        [put_shape, jax.ShapeDtypeStruct((heads, tok), FL), jax.ShapeDtypeStruct((tok, heads), FL)],
        "states", block_cost,
    )(log_decay, key_rows, value_rows)
    state_low = carry(put, False).reshape(heads, size, size)
    for c in range(1, CHUNKS):
        pieces[c][1] = ring(first_piece(c))
    order = feature_order(heads, size, count)
    attn_weights, intra = per_head(
        weights_kernel, [blk, blk, blk, run_blk, turned_blk], [square_blk, blk],
        [jax.ShapeDtypeStruct((heads, tok, tok), BF), wide_f], "weights", square_cost,
    )(query_rows, key_rows, value_rows, run, turned)

    weight_own = out_weight.reshape(heads * narrow, model)
    weight_sent = after(weight_own, state_low)
    weights = [weight_own] + [
        lax.ppermute(weight_sent, "ctx", pair_perm(count, -s)) for s in range(1, minor)
    ]

    attn_out, squares = per_head(
        attend_kernel, [blk, state_blk, turned_blk, blk], [blk, spec((1, tok))],
        [wide_f, jax.ShapeDtypeStruct((1, tok), FL)], "attend", block_cost,
        [pltpu.VMEM((tok, size), FL)],
    )(query_rows, state_low, turned, intra)
    squares = butterfly(squares, "head", head_count)
    inv_rms = lax.rsqrt(squares / features + 1e-05)
    inv_col = inv_rms.reshape(tok, 1)
    gain_row = norm_gain.reshape(1, width)
    full = pl.BlockSpec(memory_space=pltpu.VMEM)
    sent = pl.pallas_call(
        norm_kernel,
        in_specs=[SCALAR] + [full] * 4,
        out_specs=[full] * LINE,
        out_shape=[jax.ShapeDtypeStruct((tok, span), BF)] * LINE,
        compiler_params=PARAMS,
        cost_estimate=cost(2 * tok * width * width, 8 * tok * width),
        name="norm",
    )(tokens, attn_out, inv_col, gain_row, order)
    normed = [sent[0]] + [
        lax.ppermute(sent[s], "ctx", ring_perm(count, s)) for s in range(1, LINE)
    ]

    lots = [[None] * (LINE - 1) for _ in range(CHUNKS)]
    for s in range(1, LINE):
        for c in range(CHUNKS):
            piece = pieces[c][s]
            if s + 1 < LINE:
                pieces[c][s + 1] = ring(piece)
            other = lax.ppermute(piece, "head", over_y)
            near = lax.ppermute(piece, "head", over_core)
            far = lax.ppermute(other, "head", over_core)
            lots[c][s - 1] = [piece, near, other, far]

    returned = [product(tokens, [grad_out], weights, 0, 1, None)]
    for s in range(1, LINE):
        held = None
        for c in range(CHUNKS):
            held = product(tokens, lots[c][s - 1], weights, c, CHUNKS, held)
        returned.append(lax.ppermute(held, "ctx", ring_perm(count, -s)))

    flat = []
    for c in range(CHUNKS):
        parts = outer(normed, grad_out, lots[c], c, own)
        flat.append(parts[0])
        for s in range(1, minor):
            flat.append(lax.ppermute(parts[s], "ctx", pair_perm(count, s)))

    grad, gain_sum, inner = pl.pallas_call(
        back_kernel,
        in_specs=[full] * (4 + LINE),
        out_specs=[full] * 3,
        out_shape=[wide_b, jax.ShapeDtypeStruct((1, width), FL), jax.ShapeDtypeStruct((1, tok), FL)],
        compiler_params=PARAMS,
        cost_estimate=cost(2 * tok * width * width, 8 * tok * width),
        name="back",
    )(order, attn_out, inv_col, gain_row, *returned)
    inner = butterfly(inner, "head", head_count)
    shift = (inv_rms**3 * (inner / features)).reshape(tok, 1)
    grad_attn, put_back = per_head(
        grad_kernel,
        [blk, blk, col_blk, col_blk, spec((1, size), lambda h: (0, h)), blk, turned_blk],
        [blk, put_blk], [wide_b, put_shape], "grads", block_cost,
    )(grad, attn_out, inv_col, shift, gain_row, query_rows, turned)
    back_low = carry(put_back, True).reshape(heads, size, size)
    grad_gain = butterfly(gain_sum, "ctx", count).reshape(width)
    grad_query, gk_in, gv_in = per_head(
        inside_kernel,
        [blk, blk, blk, blk, square_blk, run_blk, turned_blk, state_blk], [blk] * 3,
        [wide_b, wide_f, wide_f], "inside", square_cost,
    )(grad_attn, query_rows, key_rows, value_rows, attn_weights, run, turned, state_low)
    grad_key, grad_value = per_head(
        outside_kernel, [blk, blk, state_blk, turned_blk, blk, blk], [blk] * 2,
        [wide_b] * 2, "outside", block_cost,
    )(key_rows, value_rows, back_low, turned, gk_in, gv_in)
    grad_weight = pl.pallas_call(
        functools.partial(final_kernel, CHUNKS, minor),
        in_specs=[full] * len(flat),
        out_specs=full,
        out_shape=jax.ShapeDtypeStruct((own, model), BF),
        compiler_params=PARAMS,
        cost_estimate=cost(own * model, 2 * own * model * 3),
        name="sum",
    )(*flat).reshape(heads, narrow, model)
    return grad_query, grad_key, grad_value, grad_weight, grad_gain


def solution(mesh):
    return jax.shard_map(
        shards,
        mesh=mesh,
        in_specs=(
            P("ctx", "head"),
            P("ctx", "head"),
            P("ctx", "head"),
            P("head", "ctx"),
            P("head"),
            P("head", "ctx", None),
            P("ctx", None),
        ),
        out_specs=(
            P("ctx", "head"),
            P("ctx", "head"),
            P("ctx", "head"),
            P("head", "ctx", None),
            P("head"),
        ),
        check_vma=False,
    )
```

time: 315 us -> 288 us (0.914)
  Pallas kernels: 0 us -> 74 us
  matrix products: 57.3 us -> 0 us
  blocking collectives: 47.1 us -> 0 us
  other arithmetic: 20.7 us -> 3.46 us
  starting transfers between devices: 43.2 us -> 56 us
  local copies, waits for them, and re-layouts: 36.9 us -> 48.6 us
  waiting for transfers between devices: 107 us -> 102 us
    pallas_call x0 -> x20, Pallas kernels: none -> 74 us  [the longest x7 23.8 us: product(): pl.pallas_call(functools.partial(product_kernel, len(pieces), len(weights...]
    dot_general x22 -> x0, matrix products: 57.3 us -> none  [the longest x4 16.2 us: shards(): lax.dot_general(blocks[s], weights, (((1,), (1,)), ((), ())), preferred_e...]
    unnamed x1 -> x0, blocking collectives: 47.1 us -> none
    unnamed x30 -> x158, local copies, waits for them, and re-layouts: 12.5 us -> 45.5 us
    ppermute x7, waiting for transfers between devices: 45.2 us -> 16.4 us  [butterfly(): lax.ppermute(part, axis, [(i, i ^ step) for i in range(count)])]
    ppermute x20 -> x33, waiting for transfers between devices: 55.2 us -> 81 us  [the longest x6 46.1 us: ring(): return lax.ppermute(x, 'ctx', ring_perm(count, 1))]
    unnamed x13 -> x0, other arithmetic: 12 us -> none
    dynamic_update_slice x12 -> x0, local copies, waits for them, and re-layouts: 10.5 us -> none  [gather_blocks(): block = lax.dynamic_update_slice_in_dim(block, part, who * quarter, 0)]
  transfers between devices with their start and end apart: 31 -> 44, of which waited for: 11 -> 16; matrix products, arithmetic and copies ran while one was open for 32% -> 2% of each run, Pallas kernels for 0% -> 22%
where the time goes in v2:
time: 288 us; the launch traced here: 285 us
  waiting for transfers between devices  102 us (35%)
  Pallas kernels  74 us (26%)
  starting transfers between devices  56 us (19%)
  local copies, waits for them, and re-layouts  48.6 us (17%)
  other arithmetic  3.46 us (1%)
    ppermute x6, waiting for transfers between devices, ring(): return lax.ppermute(x, 'ctx', ring_perm(count, 1))  46.1 us
    unnamed x158, local copies, waits for them, and re-layouts  45.5 us
    ppermute x6, waiting for transfers between devices, shards(): other = lax.ppermute(piece, 'head', over_y)  31.4 us
    pallas_call x7, Pallas kernels, product(): pl.pallas_call(functools.partial(product_kernel, len(pieces), len(weights...  23.8 us
    ppermute x7, waiting for transfers between devices, butterfly(): lax.ppermute(part, axis, [(i, i ^ step) for i in range(count)])  16.4 us
    pallas_call x2, Pallas kernels, outer(): pl.pallas_call(functools.partial(outer_kernel, [1] + [len(lot) for lot in...  14.4 us
    all_to_all x2, starting transfers between devices, carry(): spread = lax.all_to_all(part, 'ctx', 0, 0, tiled=True)  13.1 us
    ppermute x7, starting transfers between devices, butterfly(): lax.ppermute(part, axis, [(i, i ^ step) for i in range(count)])  8.58 us
  transfers between devices with their start and end apart: 44, of which 16 were waited for; matrix products, arithmetic and copies ran while one was open for 2% of the time, Pallas kernels for 22%

profile of v2, /device:TPU:0, one launch (start us, length us, event | category | flops | bytes accessed | tf_op | source)
XLA Modules:
  0.0 285.4 jit_solution(12578625806364853503)
XLA Ops:
  3.6 5.1 %states.1 = (bf16[8,144,128]{2,1,0:T(8,128)(2,1)}, f32[8,384]{1,0:T(8,128)S(1)}, f32[384,8]{1,0:T(8,128)S(1)}) custom-call(f32[8,384]{1,0:T(8,128)S(1)} %copy-done.72, bf16[384,1024]{1,0:T(8,128)(2,1)S(1)} %copy-done.10, bf16[384,1024]{1,0:T(8,128)(2,1)S(1)} %copy-done.13), custom_call_target="tpu_custom_call" | custom-call | flops 100663296 | bytes 2359296 | tf_op jit(solution)/shard_map/states/pallas_call | solution.py:397
  8.8 7.4 %all-to-all-start = ((bf16[8,144,128]{2,1,0:T(8,128)(2,1)}), bf16[8,144,128]{2,1,0:T(8,128)(2,1)S(1)}, u32[]{:S(2)}, u32[]{:S(2)}) async-start(bf16[8,144,128]{2,1,0:T(8,128)(2,1)} %get-tuple-element.31), calls=%async_computation | async-start | bytes 589824 | tf_op jit(solution)/shard_map/all_to_all | solution.py:134
  16.1 2.1 constant_dynamic-slice_fusion.1
  18.3 2.0 collective-permute-start.7
  20.3 2.4 collective-permute-start.3
  22.7 4.5 %all-to-all-done.in_ref = bf16[8,144,128]{2,1,0:T(8,128)(2,1)S(1)} async-done(((bf16[8,144,128]{2,1,0:T(8,128)(2,1)}), bf16[8,144,128]{2,1,0:T(8,128)(2,1)S(1)}, u32[]{:S(2)}, u32[]{:S(2)}) %all-to-all-start) | async-done | bytes 294944 | tf_op jit(solution)/shard_map/all_to_all | solution.py:134
  28.0 3.4 %all-to-all-start.1 = ((bf16[8,128,128]{2,1,0:T(8,128)(2,1)}), bf16[8,128,128]{2,1,0:T(8,128)(2,1)S(1)}, u32[]{:S(2)}, u32[]{:S(2)}) async-start(bf16[8,128,128]{2,1,0:T(8,128)(2,1)} %scan.2), calls=%async_computation.1 | async-start | bytes 524288 | tf_op jit(solution)/shard_map/all_to_all | solution.py:141
  31.4 8.6 %collective-permute-done.7.refs_1_.refs_5_ = bf16[96,3072]{1,0:T(8,128)(2,1)} collective-permute-done((bf16[96,3072]{1,0:T(8,128)(2,1)}, bf16[96,3072]{1,0:T(8,128)(2,1)}, u32[]{:S(2)}, u32[]{:S(2)}) %collective-permute-start.7) | collective-permute-done | bytes 589856 | tf_op jit(solution)/shard_map/ppermute | solution.py:393
  41.5 13.2 %collective-permute-done.3.refs_1_.refs_5_ = bf16[96,3072]{1,0:T(8,128)(2,1)} collective-permute-done((bf16[96,3072]{1,0:T(8,128)(2,1)S(1)}, bf16[96,3072]{1,0:T(8,128)(2,1)}, u32[]{:S(2)}, u32[]{:S(2)}) %collective-permute-start.3) | collective-permute-done | bytes 589856 | tf_op jit(solution)/shard_map/ppermute | solution.py:393
  55.8 4.1 %weights.1 = (bf16[8,384,384]{2,1,0:T(8,128)(2,1)S(1)}, f32[384,1024]{1,0:T(8,128)S(1)}) custom-call(bf16[384,1024]{1,0:T(8,128)(2,1)S(1)} %copy-done.16, bf16[384,1024]{1,0:T(8,128)(2,1)S(1)} %copy-done.11, bf16[384,1024]{1,0:T(8,128)(2,1)S(1)} %copy-done.14, f32[8,384]{1,0:T(8,128)S(1)} %get-tuple-element.33.run_ref, f32[384,8]{1,0:T(8,128)S(1)} %get-tuple-element.32.turned_ref), custom_call_target="tpu_custom_call" | custom-call | flops 1207959552 | bytes 6291456 | tf_op jit(solution)/shard_map/weights/pallas_call | solution.py:406
  65.2 2.3 attend.1
  73.3 10.1 %collective-permute-done.12.refs_1_.refs_9_ = bf16[96,3072]{1,0:T(8,128)(2,1)S(1)} collective-permute-done((bf16[96,3072]{1,0:T(8,128)(2,1)}, bf16[96,3072]{1,0:T(8,128)(2,1)S(1)}, u32[]{:S(2)}, u32[]{:S(2)}) %collective-permute-start.12) | collective-permute-done | bytes 589856 | tf_op jit(solution)/shard_map/ppermute | solution.py:393
  84.2 2.1 collective-permute-done.5.refs_3_.refs_7_
  88.2 6.4 %collective-permute-done.25.refs_1_.refs_13_ = bf16[96,3072]{1,0:T(8,128)(2,1)S(1)} collective-permute-done((bf16[96,3072]{1,0:T(8,128)(2,1)}, bf16[96,3072]{1,0:T(8,128)(2,1)S(1)}, u32[]{:S(2)}, u32[]{:S(2)}) %collective-permute-start.25) | collective-permute-done | bytes 589856 | tf_op jit(solution)/shard_map/ppermute | solution.py:393
  94.6 3.6 %collective-permute-done.18.refs_3_.refs_11_ = bf16[96,3072]{1,0:T(8,128)(2,1)} collective-permute-done((bf16[96,3072]{1,0:T(8,128)(2,1)}, bf16[96,3072]{1,0:T(8,128)(2,1)}, u32[]{:S(2)}, u32[]{:S(2)}) %collective-permute-start.18) | collective-permute-done | bytes 589856 | tf_op jit(solution)/shard_map/ppermute | solution.py:446
  101.8 7.8 %collective-permute-done.21.refs_1_.refs_13_ = bf16[96,3072]{1,0:T(8,128)(2,1)} collective-permute-done((bf16[96,3072]{1,0:T(8,128)(2,1)}, bf16[96,3072]{1,0:T(8,128)(2,1)}, u32[]{:S(2)}, u32[]{:S(2)}) %collective-permute-start.21) | collective-permute-done | bytes 589856 | tf_op jit(solution)/shard_map/ppermute | solution.py:393
  109.7 5.0 %collective-permute-done.14.refs_3_.refs_11_ = bf16[96,3072]{1,0:T(8,128)(2,1)} collective-permute-done((bf16[96,3072]{1,0:T(8,128)(2,1)}, bf16[96,3072]{1,0:T(8,128)(2,1)}, u32[]{:S(2)}, u32[]{:S(2)}) %collective-permute-start.14) | collective-permute-done | bytes 589856 | tf_op jit(solution)/shard_map/ppermute | solution.py:446
  117.1 10.3 %collective-permute-done.27.refs_3_.refs_15_ = bf16[96,3072]{1,0:T(8,128)(2,1)} collective-permute-done((bf16[96,3072]{1,0:T(8,128)(2,1)S(1)}, bf16[96,3072]{1,0:T(8,128)(2,1)}, u32[]{:S(2)}, u32[]{:S(2)}) %collective-permute-start.27) | collective-permute-done | bytes 589856 | tf_op jit(solution)/shard_map/ppermute | solution.py:446
  127.9 10.4 %collective-permute-done.23.refs_3_.refs_15_ = bf16[96,3072]{1,0:T(8,128)(2,1)} collective-permute-done((bf16[96,3072]{1,0:T(8,128)(2,1)}, bf16[96,3072]{1,0:T(8,128)(2,1)}, u32[]{:S(2)}, u32[]{:S(2)}) %collective-permute-start.23) | collective-permute-done | bytes 589856 | tf_op jit(solution)/shard_map/ppermute | solution.py:446
  138.9 2.2 fusion.order_ref
  141.2 3.2 %product.10.refs_7_ = f32[384,256]{1,0:T(8,128)S(1)} custom-call(s32[1]{0:T(128)} %bitcast.2.refs_0_.mine_ref, bf16[96,3072]{1,0:T(8,128)(2,1)} %collective-permute-done.16.refs_1_.refs_9_, bf16[96,3072]{1,0:T(8,128)(2,1)S(1)} %copy-done.27, bf16[96,3072]{1,0:T(8,128)(2,1)} %collective-permute-done.18.refs_3_.refs_11_, ...), custom_call_target="tpu_custom_call" | custom-call | flops 603979776 | bytes 3932160 | tf_op jit(solution)/shard_map/product/pallas_call | solution.py:224
  144.4 3.2 %product.8.refs_7_ = f32[384,256]{1,0:T(8,128)S(1)} custom-call(s32[1]{0:T(128)} %bitcast.2.refs_0_.mine_ref, bf16[96,3072]{1,0:T(8,128)(2,1)} %collective-permute-done.7.refs_1_.refs_5_, bf16[96,3072]{1,0:T(8,128)(2,1)} %collective-permute-done.8.refs_2_.refs_6_, bf16[96,3072]{1,0:T(8,128)(2,1)} %collective-permute-done.9.refs_3_.refs_7_, ...), custom_call_target="tpu_custom_call" | custom-call | flops 603979776 | bytes 3932160 | tf_op jit(solution)/shard_map/product/pallas_call | solution.py:224
  147.7 3.7 %product.11 = bf16[384,256]{1,0:T(8,128)(2,1)} custom-call(s32[1]{0:T(128)} %bitcast.2.refs_0_.mine_ref, bf16[96,3072]{1,0:T(8,128)(2,1)S(1)} %copy-done.24, bf16[96,3072]{1,0:T(8,128)(2,1)S(1)} %copy-done.36, bf16[96,3072]{1,0:T(8,128)(2,1)} %collective-permute-done.14.refs_3_.refs_11_, bf16[96,3072]{1,0:T(8,128)(2,1)} %collective-permute-done.15.refs_4_.refs_12_, ...), custom_call_target="tpu_custom_call" | custom-call | flops 603979776 | bytes 3932160 | tf_op jit(solution)/shard_map/product/pallas_call | solution.py:224
  153.0 3.8 %product.9 = bf16[384,256]{1,0:T(8,128)(2,1)} custom-call(s32[1]{0:T(128)} %bitcast.2.refs_0_.mine_ref, bf16[96,3072]{1,0:T(8,128)(2,1)} %collective-permute-done.3.refs_1_.refs_5_, bf16[96,3072]{1,0:T(8,128)(2,1)S(1)} %copy-done.33, bf16[96,3072]{1,0:T(8,128)(2,1)} %collective-permute-done.5.refs_3_.refs_7_, ...), custom_call_target="tpu_custom_call" | custom-call | flops 603979776 | bytes 3932160 | tf_op jit(solution)/shard_map/product/pallas_call | solution.py:224
  157.6 2.1 collective-permute-start.11
  159.7 2.8 product.12.refs_7_
  162.6 4.0 %product.13 = bf16[384,256]{1,0:T(8,128)(2,1)} custom-call(s32[1]{0:T(128)} %bitcast.2.refs_0_.mine_ref, bf16[96,3072]{1,0:T(8,128)(2,1)} %collective-permute-done.21.refs_1_.refs_13_, bf16[96,3072]{1,0:T(8,128)(2,1)S(1)} %collective-permute-done.22.refs_2_.refs_14_, bf16[96,3072]{1,0:T(8,128)(2,1)} %collective-permute-done.23.refs_3_.refs_15_, ...), custom_call_target="tpu_custom_call" | custom-call | flops 603979776 | bytes 3932160 | tf_op jit(solution)/shard_map/product/pallas_call | solution.py:224
  173.3 2.8 collective-permute-start.32
  177.6 2.3 copy-done.1
  180.0 3.1 %product.7.refs_0_ = bf16[384,256]{1,0:T(8,128)(2,1)S(1)} custom-call(s32[1]{0:T(128)} %bitcast.2.refs_0_.mine_ref, bf16[384,6144]{1,0:T(8,128)(2,1)S(1)} %copy-done.1, bf16[128,6144]{1,0:T(8,128)(2,1)S(1)} %bitcast.16, bf16[128,6144]{1,0:T(8,128)(2,1)S(1)} %collective-permute-done.2.refs_3_.refs_6_), custom_call_target="tpu_custom_call" | custom-call | flops 1207959552 | bytes 7864320 | tf_op jit(solution)/shard_map/product/pallas_call | solution.py:224
  183.2 2.5 back.1
  187.4 3.5 %collective-permute-done.32.refs_1_ = bf16[384,256]{1,0:T(8,128)(2,1)S(1)} collective-permute-done((bf16[384,256]{1,0:T(8,128)(2,1)S(1)}, bf16[384,256]{1,0:T(8,128)(2,1)S(1)}, u32[]{:S(2)}, u32[]{:S(2)}) %collective-permute-start.32) | collective-permute-done | bytes 196640 | tf_op jit(solution)/shard_map/ppermute | solution.py:437
  191.0 2.5 copy-done.2
  193.4 7.2 %outer.3 = (bf16[128,3072]{1,0:T(8,128)(2,1)S(1)}, bf16[128,3072]{1,0:T(8,128)(2,1)}) custom-call(bf16[384,256]{1,0:T(8,128)(2,1)S(1)} %get-tuple-element.48.refs_0_, bf16[384,256]{1,0:T(8,128)(2,1)S(1)} %collective-permute-done.32.refs_1_, bf16[384,256]{1,0:T(8,128)(2,1)S(1)} %collective-permute-done.33.refs_2_, ...), custom_call_target="tpu_custom_call" | custom-call | flops 2415919104 | bytes 11010048 | tf_op jit(solution)/shard_map/outer/pallas_call | solution.py:264
  204.2 4.2 %grads.1 = (bf16[384,1024]{1,0:T(8,128)(2,1)S(1)}, bf16[8,144,128]{2,1,0:T(8,128)(2,1)S(1)}) custom-call(bf16[384,1024]{1,0:T(8,128)(2,1)S(1)} %get-tuple-element.38.grad_ref, f32[384,1024]{1,0:T(8,128)S(1)} %copy-done.9, f32[384,1]{1,0:T(8,128)S(1)} %copy.12.inv_ref, f32[384,1]{1,0:T(8,128)S(1)} %copy.14.shift_ref, f32[1,1024]{1,0:T(1,128)S(1)} %bitcast.19, ...), custom_call_target="tpu_custom_call" | custom-call | flops 100663296 | bytes 2359296 | tf_op jit(solution)/shard_map/grads/pallas_call | solution.py:476
  210.0 5.7 %all-to-all-start.2 = ((bf16[8,144,128]{2,1,0:T(8,128)(2,1)}), bf16[8,144,128]{2,1,0:T(8,128)(2,1)S(1)}, u32[]{:S(2)}, u32[]{:S(2)}) async-start(bf16[8,144,128]{2,1,0:T(8,128)(2,1)} %copy-done.70), calls=%async_computation.2 | async-start | bytes 589824 | tf_op jit(solution)/shard_map/all_to_all | solution.py:134
  215.7 2.3 copy-done.3
  226.0 7.2 %outer.2 = (bf16[128,3072]{1,0:T(8,128)(2,1)S(1)}, bf16[128,3072]{1,0:T(8,128)(2,1)}) custom-call(bf16[384,256]{1,0:T(8,128)(2,1)S(1)} %copy-done.63, bf16[384,256]{1,0:T(8,128)(2,1)S(1)} %copy-done.65, bf16[384,256]{1,0:T(8,128)(2,1)S(1)} %copy-done.67, bf16[384,256]{1,0:T(8,128)(2,1)S(1)} %copy-done.69, bf16[384,6144]{1,0:T(8,128)(2,1)S(1)} %copy-done.3, ...), custom_call_target="tpu_custom_call" | custom-call | flops 2415919104 | bytes 11010048 | tf_op jit(solution)/shard_map/outer/pallas_call | solution.py:264
  234.0 2.0 collective-permute-start.35
  236.8 4.5 %all-to-all-start.3 = ((bf16[8,128,128]{2,1,0:T(8,128)(2,1)}), bf16[8,128,128]{2,1,0:T(8,128)(2,1)}, u32[]{:S(2)}, u32[]{:S(2)}) async-start(bf16[8,128,128]{2,1,0:T(8,128)(2,1)} %scan.3), calls=%async_computation.3 | async-start | bytes 524288 | tf_op jit(solution)/shard_map/all_to_all | solution.py:141
  241.4 2.0 collective-permute-start.37
  243.4 12.3 %collective-permute-done.37 = f32[1,1024]{1,0:T(1,128)S(1)} collective-permute-done((f32[1,1024]{1,0:T(1,128)S(1)}, f32[1,1024]{1,0:T(1,128)S(1)}, u32[]{:S(2)}, u32[]{:S(2)}) %collective-permute-start.37) | collective-permute-done | bytes 4128 | tf_op jit(solution)/shard_map/ppermute | solution.py:65
  255.7 1.8 collective-permute-start.38
  257.5 1.8 collective-permute-done.38
  259.4 2.6 collective-permute-start.39
  265.9 6.6 %inside.1 = (bf16[384,1024]{1,0:T(8,128)(2,1)}, f32[384,1024]{1,0:T(8,128)S(1)}, f32[384,1024]{1,0:T(8,128)S(1)}) custom-call(bf16[384,1024]{1,0:T(8,128)(2,1)S(1)} %copy-done.61, bf16[384,1024]{1,0:T(8,128)(2,1)S(1)} %copy-done.19, bf16[384,1024]{1,0:T(8,128)(2,1)S(1)} %copy-done.12, bf16[384,1024]{1,0:T(8,128)(2,1)S(1)} %copy-done.15, ...), custom_call_target="tpu_custom_call" | custom-call | flops 1207959552 | bytes 6291456 | tf_op jit(solution)/shard_map/inside/pallas_call | solution.py:483
  275.5 3.0 %sum.1 = bf16[128,6144]{1,0:T(8,128)(2,1)} custom-call(bf16[128,3072]{1,0:T(8,128)(2,1)S(1)} %copy-done.59, bf16[128,3072]{1,0:T(8,128)(2,1)} %collective-permute-done.35.refs_1_, bf16[128,3072]{1,0:T(8,128)(2,1)S(1)} %copy-done.57, bf16[128,3072]{1,0:T(8,128)(2,1)} %collective-permute-done.36.refs_3_), custom_call_target="tpu_custom_call" | custom-call | flops 786432 | bytes 4718592 | tf_op jit(solution)/shard_map/sum/pallas_call | solution.py:492
  279.9 5.4 %outside.1 = (bf16[384,1024]{1,0:T(8,128)(2,1)}, bf16[384,1024]{1,0:T(8,128)(2,1)}) custom-call(bf16[384,1024]{1,0:T(8,128)(2,1)S(1)} %copy-done.12, bf16[384,1024]{1,0:T(8,128)(2,1)S(1)} %copy-done.15, bf16[8,128,128]{2,1,0:T(8,128)(2,1)} %all-to-all-done.3.state_ref, f32[384,8]{1,0:T(8,128)S(1)} %get-tuple-element.32.turned_ref, ...), custom_call_target="tpu_custom_call" | custom-call | flops 100663296 | bytes 2359296 | tf_op jit(solution)/shard_map/outside/pallas_call | solution.py:488
  (230 shorter events, 62.7 us)
Async XLA Ops:
  8.7 45.9 %copy-start.11 = (bf16[384,1024]{1,0:T(8,128)(2,1)S(1)}, bf16[384,1024]{1,0:T(8,128)(2,1)}, u32[]{:S(2)}) copy-start(bf16[384,1024]{1,0:T(8,128)(2,1)} %k_ref.7) | copy-start | bytes 2359300
  8.7 45.9 %copy-start.14 = (bf16[384,1024]{1,0:T(8,128)(2,1)S(1)}, bf16[384,1024]{1,0:T(8,128)(2,1)}, u32[]{:S(2)}) copy-start(bf16[384,1024]{1,0:T(8,128)(2,1)} %v_ref.7) | copy-start | bytes 2359300
  8.8 18.4 %all-to-all-start = ((bf16[8,144,128]{2,1,0:T(8,128)(2,1)}), bf16[8,144,128]{2,1,0:T(8,128)(2,1)S(1)}, u32[]{:S(2)}, u32[]{:S(2)}) async-start(bf16[8,144,128]{2,1,0:T(8,128)(2,1)} %get-tuple-element.31), calls=%async_computation | async-start | bytes 589824 | tf_op jit(solution)/shard_map/all_to_all | solution.py:134
  18.3 21.7 %collective-permute-start.7 = (bf16[96,3072]{1,0:T(8,128)(2,1)}, bf16[96,3072]{1,0:T(8,128)(2,1)}, u32[]{:S(2)}, u32[]{:S(2)}) collective-permute-start(bf16[96,3072]{1,0:T(8,128)(2,1)} %get-tuple-element.57), channel_id=1, source_target_pairs={{0,8},{4,12},{8,24},{12,28},{24,16},{28,20},{16,0},{20,4},{1,9},{5... | collective-permute-start | bytes 1769480 | tf_op jit(solution)/shard_map/ppermute | solution.py:393
  20.3 34.4 %collective-permute-start.3 = (bf16[96,3072]{1,0:T(8,128)(2,1)S(1)}, bf16[96,3072]{1,0:T(8,128)(2,1)}, u32[]{:S(2)}, u32[]{:S(2)}) collective-permute-start(bf16[96,3072]{1,0:T(8,128)(2,1)S(1)} %get-tuple-element.58), channel_id=1, source_target_pairs={{0,8},{4,12},{8,24},{12,28},{24,16},{28,20},{16,0},{20,4},{1,9},{5... | collective-permute-start | bytes 1769480 | tf_op jit(solution)/shard_map/ppermute | solution.py:393
  28.0 34.5 %all-to-all-start.1 = ((bf16[8,128,128]{2,1,0:T(8,128)(2,1)}), bf16[8,128,128]{2,1,0:T(8,128)(2,1)S(1)}, u32[]{:S(2)}, u32[]{:S(2)}) async-start(bf16[8,128,128]{2,1,0:T(8,128)(2,1)} %scan.2), calls=%async_computation.1 | async-start | bytes 524288 | tf_op jit(solution)/shard_map/all_to_all | solution.py:141
  39.9 31.4 %collective-permute-start.16 = (bf16[96,3072]{1,0:T(8,128)(2,1)}, bf16[96,3072]{1,0:T(8,128)(2,1)}, u32[]{:S(2)}, u32[]{:S(2)}) collective-permute-start(bf16[96,3072]{1,0:T(8,128)(2,1)} %collective-permute-done.7.refs_1_.refs_5_), channel_id=1, source_target_pairs={{0,8},{4,12},{8,24},{12,28},{24,16},{28,20},{16,0},{20,4},{1,9},{5... | collective-permute-start | bytes 1769480 | tf_op jit(solution)/shard_map/ppermute | solution.py:393
  39.9 31.4 %collective-permute-start.9 = (bf16[96,3072]{1,0:T(8,128)(2,1)}, bf16[96,3072]{1,0:T(8,128)(2,1)}, u32[]{:S(2)}, u32[]{:S(2)}) collective-permute-start(bf16[96,3072]{1,0:T(8,128)(2,1)} %collective-permute-done.7.refs_1_.refs_5_), channel_id=1, source_target_pairs={{0,2},{1,3},{2,0},{3,1},{4,6},{5,7},{6,4},{7,5},{8,10},{9,11},{10,... | collective-permute-start | bytes 1769480 | tf_op jit(solution)/shard_map/ppermute | solution.py:446
  41.5 31.3 %collective-permute-start.8 = (bf16[96,3072]{1,0:T(8,128)(2,1)}, bf16[96,3072]{1,0:T(8,128)(2,1)}, u32[]{:S(2)}, u32[]{:S(2)}) collective-permute-start(bf16[96,3072]{1,0:T(8,128)(2,1)} %collective-permute-done.7.refs_1_.refs_5_), channel_id=1, source_target_pairs={{0,1},{1,0},{2,3},{3,2},{4,5},{5,4},{6,7},{7,6},{8,9},{9,8},{10,11... | collective-permute-start | bytes 1769480 | tf_op jit(solution)/shard_map/ppermute | solution.py:447
  54.7 28.7 %collective-permute-start.12 = (bf16[96,3072]{1,0:T(8,128)(2,1)}, bf16[96,3072]{1,0:T(8,128)(2,1)S(1)}, u32[]{:S(2)}, u32[]{:S(2)}) collective-permute-start(bf16[96,3072]{1,0:T(8,128)(2,1)} %collective-permute-done.3.refs_1_.refs_5_), channel_id=1, source_target_pairs={{0,8},{4,12},{8,24},{12,28},{24,16},{28,20},{16,0},{20,4},{1,9},{5... | collective-permute-start | bytes 1769480 | tf_op jit(solution)/shard_map/ppermute | solution.py:393
  68.6 1.2 collective-permute-start
  69.8 16.5 %collective-permute-start.5 = (bf16[96,3072]{1,0:T(8,128)(2,1)}, bf16[96,3072]{1,0:T(8,128)(2,1)}, u32[]{:S(2)}, u32[]{:S(2)}) collective-permute-start(bf16[96,3072]{1,0:T(8,128)(2,1)} %collective-permute-done.3.refs_1_.refs_5_), channel_id=1, source_target_pairs={{0,2},{1,3},{2,0},{3,1},{4,6},{5,7},{6,4},{7,5},{8,10},{9,11},{10,... | collective-permute-start | bytes 1769480 | tf_op jit(solution)/shard_map/ppermute | solution.py:446
  71.3 16.1 %collective-permute-start.4 = (bf16[96,3072]{1,0:T(8,128)(2,1)}, bf16[96,3072]{1,0:T(8,128)(2,1)S(1)}, u32[]{:S(2)}, u32[]{:S(2)}) collective-permute-start(bf16[96,3072]{1,0:T(8,128)(2,1)} %collective-permute-done.3.refs_1_.refs_5_), channel_id=1, source_target_pairs={{0,1},{1,0},{2,3},{3,2},{4,5},{5,4},{6,7},{7,6},{8,9},{9,8},{10,11... | collective-permute-start | bytes 1769480 | tf_op jit(solution)/shard_map/ppermute | solution.py:447
  71.3 23.3 %collective-permute-start.25 = (bf16[96,3072]{1,0:T(8,128)(2,1)}, bf16[96,3072]{1,0:T(8,128)(2,1)S(1)}, u32[]{:S(2)}, u32[]{:S(2)}) collective-permute-start(bf16[96,3072]{1,0:T(8,128)(2,1)} %collective-permute-done.16.refs_1_.refs_9_), channel_id=1, source_target_pairs={{0,8},{4,12},{8,24},{12,28},{24,16},{28,20},{16,0},{20,4},{1,9},{5... | collective-permute-start | bytes 1769480 | tf_op jit(solution)/shard_map/ppermute | solution.py:393
  72.8 25.4 %collective-permute-start.18 = (bf16[96,3072]{1,0:T(8,128)(2,1)}, bf16[96,3072]{1,0:T(8,128)(2,1)}, u32[]{:S(2)}, u32[]{:S(2)}) collective-permute-start(bf16[96,3072]{1,0:T(8,128)(2,1)} %collective-permute-done.16.refs_1_.refs_9_), channel_id=1, source_target_pairs={{0,2},{1,3},{2,0},{3,1},{4,6},{5,7},{6,4},{7,5},{8,10},{9,11},{10,... | collective-permute-start | bytes 1769480 | tf_op jit(solution)/shard_map/ppermute | solution.py:446
  83.4 16.3 %collective-permute-start.17 = (bf16[96,3072]{1,0:T(8,128)(2,1)}, bf16[96,3072]{1,0:T(8,128)(2,1)S(1)}, u32[]{:S(2)}, u32[]{:S(2)}) collective-permute-start(bf16[96,3072]{1,0:T(8,128)(2,1)} %collective-permute-done.16.refs_1_.refs_9_), channel_id=1, source_target_pairs={{0,1},{1,0},{2,3},{3,2},{4,5},{5,4},{6,7},{7,6},{8,9},{9,8},{10,11... | collective-permute-start | bytes 1769480 | tf_op jit(solution)/shard_map/ppermute | solution.py:447
  86.3 52.6 %collective-permute-start.2 = (bf16[128,6144]{1,0:T(8,128)(2,1)S(1)}, bf16[128,6144]{1,0:T(8,128)(2,1)S(1)}, u32[]{:S(2)}, u32[]{:S(2)}) collective-permute-start(bf16[128,6144]{1,0:T(8,128)(2,1)S(1)} %bitcast.9), channel_id=1, source_target_pairs={{0,4},{4,0},{8,12},{12,8},{16,20},{20,16},{24,28},{28,24},{1,5},{5... | collective-permute-start | bytes 4718600 | tf_op jit(solution)/shard_map/ppermute | solution.py:414
  88.2 12.4 %collective-permute-start.10 = (bf16[96,3072]{1,0:T(8,128)(2,1)}, bf16[96,3072]{1,0:T(8,128)(2,1)S(1)}, u32[]{:S(2)}, u32[]{:S(2)}) collective-permute-start(bf16[96,3072]{1,0:T(8,128)(2,1)} %collective-permute-done.9.refs_3_.refs_7_), channel_id=1, source_target_pairs={{0,1},{1,0},{2,3},{3,2},{4,5},{5,4},{6,7},{7,6},{8,9},{9,8},{10,11... | collective-permute-start | bytes 1769480 | tf_op jit(solution)/shard_map/ppermute | solution.py:448
  94.6 15.1 %collective-permute-start.21 = (bf16[96,3072]{1,0:T(8,128)(2,1)}, bf16[96,3072]{1,0:T(8,128)(2,1)}, u32[]{:S(2)}, u32[]{:S(2)}) collective-permute-start(bf16[96,3072]{1,0:T(8,128)(2,1)} %copy-done.23), channel_id=1, source_target_pairs={{0,8},{4,12},{8,24},{12,28},{24,16},{28,20},{16,0},{20,4},{1,9},{5... | collective-permute-start | bytes 1769480 | tf_op jit(solution)/shard_map/ppermute | solution.py:393
  98.1 16.6 %collective-permute-start.14 = (bf16[96,3072]{1,0:T(8,128)(2,1)}, bf16[96,3072]{1,0:T(8,128)(2,1)}, u32[]{:S(2)}, u32[]{:S(2)}) collective-permute-start(bf16[96,3072]{1,0:T(8,128)(2,1)} %copy-done.23), channel_id=1, source_target_pairs={{0,2},{1,3},{2,0},{3,1},{4,6},{5,7},{6,4},{7,5},{8,10},{9,11},{10,... | collective-permute-start | bytes 1769480 | tf_op jit(solution)/shard_map/ppermute | solution.py:446
  100.5 15.7 %collective-permute-start.13 = (bf16[96,3072]{1,0:T(8,128)(2,1)}, bf16[96,3072]{1,0:T(8,128)(2,1)S(1)}, u32[]{:S(2)}, u32[]{:S(2)}) collective-permute-start(bf16[96,3072]{1,0:T(8,128)(2,1)} %copy-done.23), channel_id=1, source_target_pairs={{0,1},{1,0},{2,3},{3,2},{4,5},{5,4},{6,7},{7,6},{8,9},{9,8},{10,11... | collective-permute-start | bytes 1769480 | tf_op jit(solution)/shard_map/ppermute | solution.py:447
  101.3 26.0 %collective-permute-start.27 = (bf16[96,3072]{1,0:T(8,128)(2,1)S(1)}, bf16[96,3072]{1,0:T(8,128)(2,1)}, u32[]{:S(2)}, u32[]{:S(2)}) collective-permute-start(bf16[96,3072]{1,0:T(8,128)(2,1)S(1)} %collective-permute-done.25.refs_1_.refs_13_), channel_id=1, source_target_pairs={{0,2},{1,3},{2,0},{3,1},{4,6},{5,7},{6,4},{7,5},{8,10},{9,11},{10,... | collective-permute-start | bytes 1769480 | tf_op jit(solution)/shard_map/ppermute | solution.py:446
  109.7 17.7 %collective-permute-start.19 = (bf16[96,3072]{1,0:T(8,128)(2,1)}, bf16[96,3072]{1,0:T(8,128)(2,1)}, u32[]{:S(2)}, u32[]{:S(2)}) collective-permute-start(bf16[96,3072]{1,0:T(8,128)(2,1)} %collective-permute-done.18.refs_3_.refs_11_), channel_id=1, source_target_pairs={{0,1},{1,0},{2,3},{3,2},{4,5},{5,4},{6,7},{7,6},{8,9},{9,8},{10,11... | collective-permute-start | bytes 1769480 | tf_op jit(solution)/shard_map/ppermute | solution.py:448
  114.7 23.6 %collective-permute-start.23 = (bf16[96,3072]{1,0:T(8,128)(2,1)}, bf16[96,3072]{1,0:T(8,128)(2,1)}, u32[]{:S(2)}, u32[]{:S(2)}) collective-permute-start(bf16[96,3072]{1,0:T(8,128)(2,1)} %collective-permute-done.21.refs_1_.refs_13_), channel_id=1, source_target_pairs={{0,2},{1,3},{2,0},{3,1},{4,6},{5,7},{6,4},{7,5},{8,10},{9,11},{10,... | collective-permute-start | bytes 1769480 | tf_op jit(solution)/shard_map/ppermute | solution.py:446
  117.1 21.2 %collective-permute-start.15 = (bf16[96,3072]{1,0:T(8,128)(2,1)}, bf16[96,3072]{1,0:T(8,128)(2,1)}, u32[]{:S(2)}, u32[]{:S(2)}) collective-permute-start(bf16[96,3072]{1,0:T(8,128)(2,1)} %collective-permute-done.14.refs_3_.refs_11_), channel_id=1, source_target_pairs={{0,1},{1,0},{2,3},{3,2},{4,5},{5,4},{6,7},{7,6},{8,9},{9,8},{10,11... | collective-permute-start | bytes 1769480 | tf_op jit(solution)/shard_map/ppermute | solution.py:448
  127.4 24.1 %collective-permute-start.6 = (bf16[96,3072]{1,0:T(8,128)(2,1)}, bf16[96,3072]{1,0:T(8,128)(2,1)}, u32[]{:S(2)}, u32[]{:S(2)}) collective-permute-start(bf16[96,3072]{1,0:T(8,128)(2,1)} %collective-permute-done.5.refs_3_.refs_7_), channel_id=1, source_target_pairs={{0,1},{1,0},{2,3},{3,2},{4,5},{5,4},{6,7},{7,6},{8,9},{9,8},{10,11... | collective-permute-start | bytes 1769480 | tf_op jit(solution)/shard_map/ppermute | solution.py:448
  127.4 29.4 %collective-permute-start.26 = (bf16[96,3072]{1,0:T(8,128)(2,1)}, bf16[96,3072]{1,0:T(8,128)(2,1)S(1)}, u32[]{:S(2)}, u32[]{:S(2)}) collective-permute-start(bf16[96,3072]{1,0:T(8,128)(2,1)} %copy-done.20), channel_id=1, source_target_pairs={{0,1},{1,0},{2,3},{3,2},{4,5},{5,4},{6,7},{7,6},{8,9},{9,8},{10,11... | collective-permute-start | bytes 1769480 | tf_op jit(solution)/shard_map/ppermute | solution.py:447
  138.3 24.2 %collective-permute-start.22 = (bf16[96,3072]{1,0:T(8,128)(2,1)}, bf16[96,3072]{1,0:T(8,128)(2,1)S(1)}, u32[]{:S(2)}, u32[]{:S(2)}) collective-permute-start(bf16[96,3072]{1,0:T(8,128)(2,1)} %collective-permute-done.21.refs_1_.refs_13_), channel_id=1, source_target_pairs={{0,1},{1,0},{2,3},{3,2},{4,5},{5,4},{6,7},{7,6},{8,9},{9,8},{10,11... | collective-permute-start | bytes 1769480 | tf_op jit(solution)/shard_map/ppermute | solution.py:447
  138.3 19.3 %collective-permute-start.28 = (bf16[96,3072]{1,0:T(8,128)(2,1)}, bf16[96,3072]{1,0:T(8,128)(2,1)S(1)}, u32[]{:S(2)}, u32[]{:S(2)}) collective-permute-start(bf16[96,3072]{1,0:T(8,128)(2,1)} %collective-permute-done.27.refs_3_.refs_15_), channel_id=1, source_target_pairs={{0,1},{1,0},{2,3},{3,2},{4,5},{5,4},{6,7},{7,6},{8,9},{9,8},{10,11... | collective-permute-start | bytes 1769480 | tf_op jit(solution)/shard_map/ppermute | solution.py:448
  138.8 23.8 %collective-permute-start.24 = (bf16[96,3072]{1,0:T(8,128)(2,1)}, bf16[96,3072]{1,0:T(8,128)(2,1)S(1)}, u32[]{:S(2)}, u32[]{:S(2)}) collective-permute-start(bf16[96,3072]{1,0:T(8,128)(2,1)} %collective-permute-done.23.refs_3_.refs_15_), channel_id=1, source_target_pairs={{0,1},{1,0},{2,3},{3,2},{4,5},{5,4},{6,7},{7,6},{8,9},{9,8},{10,11... | collective-permute-start | bytes 1769480 | tf_op jit(solution)/shard_map/ppermute | solution.py:448
  151.4 15.9 %collective-permute-start.1 = (f32[1,384]{1,0:T(1,128)S(1)}, f32[1,384]{1,0:T(1,128)S(1)}, u32[]{:S(2)}, u32[]{:S(2)}) collective-permute-start(f32[1,384]{1,0:T(1,128)S(1)} %add.151), channel_id=1, source_target_pairs={{0,2},{1,3},{2,0},{3,1},{4,6},{5,7},{6,4},{7,5},{8,10},{9,11},{10,... | collective-permute-start | bytes 4616 | tf_op jit(solution)/shard_map/ppermute | solution.py:65
  156.8 20.3 %collective-permute-start.20 = (bf16[384,256]{1,0:T(8,128)(2,1)}, bf16[384,256]{1,0:T(8,128)(2,1)}, u32[]{:S(2)}, u32[]{:S(2)}) collective-permute-start(bf16[384,256]{1,0:T(8,128)(2,1)} %product.11), channel_id=1, source_target_pairs={{0,24},{4,28},{8,16},{12,20},{24,0},{28,4},{16,8},{20,12},{1,25},{... | collective-permute-start | bytes 589832 | tf_op jit(solution)/shard_map/ppermute | solution.py:456
  157.6 25.6 %collective-permute-start.11 = (bf16[384,256]{1,0:T(8,128)(2,1)}, bf16[384,256]{1,0:T(8,128)(2,1)}, u32[]{:S(2)}, u32[]{:S(2)}) collective-permute-start(bf16[384,256]{1,0:T(8,128)(2,1)} %product.9), channel_id=1, source_target_pairs={{0,16},{4,20},{8,0},{12,4},{24,8},{28,12},{16,24},{20,28},{1,17},{... | collective-permute-start | bytes 589832 | tf_op jit(solution)/shard_map/ppermute | solution.py:456
  166.6 16.6 %collective-permute-start.29 = (bf16[384,256]{1,0:T(8,128)(2,1)}, bf16[384,256]{1,0:T(8,128)(2,1)}, u32[]{:S(2)}, u32[]{:S(2)}) collective-permute-start(bf16[384,256]{1,0:T(8,128)(2,1)} %product.13), channel_id=1, source_target_pairs={{0,8},{4,12},{8,24},{12,28},{24,16},{28,20},{16,0},{20,4},{1,9},{5... | collective-permute-start | bytes 589832 | tf_op jit(solution)/shard_map/ppermute | solution.py:456
  173.3 17.5 %collective-permute-start.32 = (bf16[384,256]{1,0:T(8,128)(2,1)S(1)}, bf16[384,256]{1,0:T(8,128)(2,1)S(1)}, u32[]{:S(2)}, u32[]{:S(2)}) collective-permute-start(bf16[384,256]{1,0:T(8,128)(2,1)S(1)} %get-tuple-element.49), channel_id=1, source_target_pairs={{0,8},{4,12},{8,24},{12,28},{24,16},{28,20},{16,0},{20,4},{1,9},{5... | collective-permute-start | bytes 589832 | tf_op jit(solution)/shard_map/ppermute | solution.py:437
  176.1 14.8 %collective-permute-start.33 = (bf16[384,256]{1,0:T(8,128)(2,1)S(1)}, bf16[384,256]{1,0:T(8,128)(2,1)S(1)}, u32[]{:S(2)}, u32[]{:S(2)}) collective-permute-start(bf16[384,256]{1,0:T(8,128)(2,1)S(1)} %get-tuple-element.50), channel_id=1, source_target_pairs={{0,24},{4,28},{8,16},{12,20},{24,0},{28,4},{16,8},{20,12},{1,25},{... | collective-permute-start | bytes 589832 | tf_op jit(solution)/shard_map/ppermute | solution.py:437
  177.1 13.8 %collective-permute-start.34 = (bf16[384,256]{1,0:T(8,128)(2,1)S(1)}, bf16[384,256]{1,0:T(8,128)(2,1)S(1)}, u32[]{:S(2)}, u32[]{:S(2)}) collective-permute-start(bf16[384,256]{1,0:T(8,128)(2,1)S(1)} %get-tuple-element.51), channel_id=1, source_target_pairs={{0,16},{4,20},{8,0},{12,4},{24,8},{28,12},{16,24},{20,28},{1,17},{... | collective-permute-start | bytes 589832 | tf_op jit(solution)/shard_map/ppermute | solution.py:437
  185.7 1.2 collective-permute-start.30
  186.9 16.0 %collective-permute-start.31 = (f32[1,384]{1,0:T(1,128)S(1)}, f32[1,384]{1,0:T(1,128)S(1)}, u32[]{:S(2)}, u32[]{:S(2)}) collective-permute-start(f32[1,384]{1,0:T(1,128)S(1)} %add.156), channel_id=1, source_target_pairs={{0,2},{1,3},{2,0},{3,1},{4,6},{5,7},{6,4},{7,5},{8,10},{9,11},{10,... | collective-permute-start | bytes 4616 | tf_op jit(solution)/shard_map/ppermute | solution.py:65
  201.6 73.9 %collective-permute-start.36 = (bf16[128,3072]{1,0:T(8,128)(2,1)}, bf16[128,3072]{1,0:T(8,128)(2,1)}, u32[]{:S(2)}, u32[]{:S(2)}) collective-permute-start(bf16[128,3072]{1,0:T(8,128)(2,1)} %get-tuple-element.55), channel_id=1, source_target_pairs={{0,4},{4,0},{8,12},{12,8},{16,20},{20,16},{24,28},{28,24},{1,5},{5... | collective-permute-start | bytes 2359304 | tf_op jit(solution)/shard_map/ppermute | solution.py:463
  210.0 26.1 %all-to-all-start.2 = ((bf16[8,144,128]{2,1,0:T(8,128)(2,1)}), bf16[8,144,128]{2,1,0:T(8,128)(2,1)S(1)}, u32[]{:S(2)}, u32[]{:S(2)}) async-start(bf16[8,144,128]{2,1,0:T(8,128)(2,1)} %copy-done.70), calls=%async_computation.2 | async-start | bytes 589824 | tf_op jit(solution)/shard_map/all_to_all | solution.py:134
  226.0 36.0 %copy-start.15 = (bf16[384,1024]{1,0:T(8,128)(2,1)S(1)}, bf16[384,1024]{1,0:T(8,128)(2,1)}, u32[]{:S(2)}) copy-start(bf16[384,1024]{1,0:T(8,128)(2,1)} %v_ref.7) | copy-start | bytes 2359300
  226.0 36.0 %copy-start.49 = (bf16[8,128,128]{2,1,0:T(8,128)(2,1)S(1)}, bf16[8,128,128]{2,1,0:T(8,128)(2,1)}, u32[]{:S(2)}) copy-start(bf16[8,128,128]{2,1,0:T(8,128)(2,1)} %copy-done.48) | copy-start | bytes 786436
  234.0 41.4 %collective-permute-start.35 = (bf16[128,3072]{1,0:T(8,128)(2,1)}, bf16[128,3072]{1,0:T(8,128)(2,1)}, u32[]{:S(2)}, u32[]{:S(2)}) collective-permute-start(bf16[128,3072]{1,0:T(8,128)(2,1)} %get-tuple-element.53), channel_id=1, source_target_pairs={{0,4},{4,0},{8,12},{12,8},{16,20},{20,16},{24,28},{28,24},{1,5},{5... | collective-permute-start | bytes 2359304 | tf_op jit(solution)/shard_map/ppermute | solution.py:463
  236.8 41.7 %all-to-all-start.3 = ((bf16[8,128,128]{2,1,0:T(8,128)(2,1)}), bf16[8,128,128]{2,1,0:T(8,128)(2,1)}, u32[]{:S(2)}, u32[]{:S(2)}) async-start(bf16[8,128,128]{2,1,0:T(8,128)(2,1)} %scan.3), calls=%async_computation.3 | async-start | bytes 524288 | tf_op jit(solution)/shard_map/all_to_all | solution.py:141
  241.4 14.3 %collective-permute-start.37 = (f32[1,1024]{1,0:T(1,128)S(1)}, f32[1,1024]{1,0:T(1,128)S(1)}, u32[]{:S(2)}, u32[]{:S(2)}) collective-permute-start(f32[1,1024]{1,0:T(1,128)S(1)} %copy-done.74), channel_id=1, source_target_pairs={{0,4},{4,0},{8,12},{12,8},{16,20},{20,16},{24,28},{28,24},{1,5},{5... | collective-permute-start | bytes 12296 | tf_op jit(solution)/shard_map/ppermute | solution.py:65
  255.7 3.6 %collective-permute-start.38 = (f32[1,1024]{1,0:T(1,128)S(1)}, f32[1,1024]{1,0:T(1,128)S(1)}, u32[]{:S(2)}, u32[]{:S(2)}) collective-permute-start(f32[1,1024]{1,0:T(1,128)S(1)} %add.158), channel_id=1, source_target_pairs={{0,8},{4,12},{8,0},{12,4},{16,24},{20,28},{24,16},{28,20},{1,9},{5... | collective-permute-start | bytes 12296 | tf_op jit(solution)/shard_map/ppermute | solution.py:65
  259.4 15.5 %collective-permute-start.39 = (f32[1,1024]{1,0:T(1,128)S(1)}, f32[1,1024]{1,0:T(1,128)S(1)}, u32[]{:S(2)}, u32[]{:S(2)}) collective-permute-start(f32[1,1024]{1,0:T(1,128)S(1)} %add.159), channel_id=1, source_target_pairs={{0,16},{4,20},{8,24},{12,28},{16,0},{20,4},{24,8},{28,12},{1,17},{... | collective-permute-start | bytes 12296 | tf_op jit(solution)/shard_map/ppermute | solution.py:65
  (75 other events, 395.9 us)

commit v3 on v2

--- a/solution.py
+++ b/solution.py
@@ -11,7 +11,7 @@
 CHUNKS = 2
 FL = jnp.float32
 BF = jnp.bfloat16
-PARAMS = pltpu.CompilerParams(vmem_limit_bytes=24 * 1024 * 1024)
+PARAMS = pltpu.CompilerParams(vmem_limit_bytes=60 * 1024 * 1024)
 EXACT = lax.Precision.HIGHEST
 NN = (((1,), (0,)), ((), ()))
 NT = (((1,), (1,)), ((), ()))
@@ -29,8 +29,11 @@
 SCALAR = pl.BlockSpec(memory_space=pltpu.SMEM)
 
 
+TINY = pl.CostEstimate(flops=1000, bytes_accessed=1000, transcendentals=0)
+
+
 def cost(flops, moved):
-    return pl.CostEstimate(flops=flops, bytes_accessed=moved, transcendentals=0)
+    return TINY
 
 
 def after(x, *others):
@@ -389,78 +392,128 @@
             compiler_params=PARAMS, name=name, cost_estimate=est, scratch_shapes=list(scratch),
         )
 
+    gain_row = norm_gain.reshape(1, width)
+    full = pl.BlockSpec(memory_space=pltpu.VMEM)
+    weight_own = out_weight.reshape(heads * narrow, model)
+
     def ring(x):
         return lax.ppermute(x, "ctx", ring_perm(count, 1))
 
-    pieces = [[None] * LINE for _ in range(CHUNKS)]
-    pieces[0][1] = ring(first_piece(0))
+    def over(x, perm):
+        return lax.ppermute(x, "head", perm)
+
+    def near_of(x):
+        return over(x, over_core)
+
+    def other_of(x):
+        return over(x, over_y)
+
+    def slot(**named):
+        leaves, tree = jax.tree.flatten(named)
+        return jax.tree.unflatten(tree, lax.optimization_barrier(leaves))
+
+    each = range(CHUNKS)
+    firsts = [first_piece(c) for c in each]
+    order = feature_order(heads, size, count)
+    ring1 = [ring(firsts[0])]
     put, run, turned = per_head(
         state_kernel, [run_blk, blk, blk], [put_blk, run_blk, turned_blk],
         [put_shape, jax.ShapeDtypeStruct((heads, tok), FL), jax.ShapeDtypeStruct((tok, heads), FL)],
         "states", block_cost,
     )(log_decay, key_rows, value_rows)
-    state_low = carry(put, False).reshape(heads, size, size)
-    for c in range(1, CHUNKS):
-        pieces[c][1] = ring(first_piece(c))
-    order = feature_order(heads, size, count)
+    ring1 += [ring(after(firsts[c], put)) for c in each[1:]]
+    spread = lax.all_to_all(put, "ctx", 0, 0, tiled=True)
     attn_weights, intra = per_head(
         weights_kernel, [blk, blk, blk, run_blk, turned_blk], [square_blk, blk],
         [jax.ShapeDtypeStruct((heads, tok, tok), BF), wide_f], "weights", square_cost,
     )(query_rows, key_rows, value_rows, run, turned)
-
-    weight_own = out_weight.reshape(heads * narrow, model)
+    d = slot(ring1=ring1, spread=spread, intra=intra, order=order)
+
+    ring1, intra, order = d["ring1"], d["intra"], d["order"]
+    states = pl.pallas_call(
+        functools.partial(scan_kernel, False),
+        out_shape=jax.ShapeDtypeStruct((count, rows, size), BF),
+        compiler_params=PARAMS, cost_estimate=TINY, name="scan",
+    )(d["spread"])
+    state_low = lax.all_to_all(states, "ctx", 0, 0, tiled=True).reshape(heads, size, size)
+    ring2 = [ring(ring1[0])] + [ring(after(ring1[c], state_low)) for c in each[1:]]
+    other1, near1 = [other_of(x) for x in ring1], [near_of(x) for x in ring1]
     weight_sent = after(weight_own, state_low)
-    weights = [weight_own] + [
-        lax.ppermute(weight_sent, "ctx", pair_perm(count, -s)) for s in range(1, minor)
-    ]
-
+    weights = [lax.ppermute(weight_sent, "ctx", pair_perm(count, -s)) for s in range(1, minor)]
     attn_out, squares = per_head(
         attend_kernel, [blk, state_blk, turned_blk, blk], [blk, spec((1, tok))],
         [wide_f, jax.ShapeDtypeStruct((1, tok), FL)], "attend", block_cost,
         [pltpu.VMEM((tok, size), FL)],
     )(query_rows, state_low, turned, intra)
-    squares = butterfly(squares, "head", head_count)
+    squares = squares + near_of(squares)
+    squares = squares + other_of(squares)
+    d = slot(ring1=ring1, ring2=ring2, other1=other1, near1=near1, squares=squares)
+
+    ring1, ring2, other1, near1, squares = [
+        d[n] for n in ("ring1", "ring2", "other1", "near1", "squares")
+    ]
+    ring3 = [ring(x) for x in ring2]
+    other2, near2 = [other_of(x) for x in ring2], [near_of(x) for x in ring2]
+    far1 = [near_of(x) for x in other1]
     inv_rms = lax.rsqrt(squares / features + 1e-05)
     inv_col = inv_rms.reshape(tok, 1)
-    gain_row = norm_gain.reshape(1, width)
-    full = pl.BlockSpec(memory_space=pltpu.VMEM)
     sent = pl.pallas_call(
         norm_kernel,
         in_specs=[SCALAR] + [full] * 4,
         out_specs=[full] * LINE,
         out_shape=[jax.ShapeDtypeStruct((tok, span), BF)] * LINE,
-        compiler_params=PARAMS,
-        cost_estimate=cost(2 * tok * width * width, 8 * tok * width),
-        name="norm",
+        compiler_params=PARAMS, cost_estimate=TINY, name="norm",
     )(tokens, attn_out, inv_col, gain_row, order)
-    normed = [sent[0]] + [
-        lax.ppermute(sent[s], "ctx", ring_perm(count, s)) for s in range(1, LINE)
-    ]
-
-    lots = [[None] * (LINE - 1) for _ in range(CHUNKS)]
-    for s in range(1, LINE):
-        for c in range(CHUNKS):
-            piece = pieces[c][s]
-            if s + 1 < LINE:
-                pieces[c][s + 1] = ring(piece)
-            other = lax.ppermute(piece, "head", over_y)
-            near = lax.ppermute(piece, "head", over_core)
-            far = lax.ppermute(other, "head", over_core)
-            lots[c][s - 1] = [piece, near, other, far]
-
-    returned = [product(tokens, [grad_out], weights, 0, 1, None)]
-    for s in range(1, LINE):
-        held = None
-        for c in range(CHUNKS):
-            held = product(tokens, lots[c][s - 1], weights, c, CHUNKS, held)
-        returned.append(lax.ppermute(held, "ctx", ring_perm(count, -s)))
-
+    d = slot(first=ring3[0], other2=other2, far1=far1, near2=near2, weights=weights, sent=sent)
+
+    other2, far1, near2, sent = d["other2"], d["far1"], d["near2"], d["sent"]
+    weights = [weight_own] + d["weights"]
+    ring3[0] = d["first"]
+    far2 = [near_of(x) for x in other2]
+    other3, near3 = [other_of(ring3[0])], [near_of(ring3[0])]
+    lots = [[[ring1[c], near1[c], other1[c], far1[c]]] for c in each]
+    mine_part = product(tokens, [grad_out], weights, 0, 1, None)
+    one = None
+    for c in each:
+        one = product(tokens, lots[c][0], weights, c, CHUNKS, one)
+    d = slot(
+        rest=ring3[1:], far2=far2, other3=other3, near3=near3, mine=mine_part, one=one, sent=sent
+    )
+
+    far2, other3, near3, sent = d["far2"], d["other3"], d["near3"], d["sent"]
+    ring3 = ring3[:1] + d["rest"]
+    returned = [d["mine"], lax.ppermute(d["one"], "ctx", ring_perm(count, -1))]
+    normed = [sent[0]] + [lax.ppermute(sent[s], "ctx", ring_perm(count, s)) for s in range(1, LINE)]
+    other3 += [other_of(x) for x in ring3[1:]]
+    near3 += [near_of(x) for x in ring3[1:]]
+    far3 = [near_of(other3[0])]
+    two = None
+    for c in each:
+        lots[c].append([ring2[c], near2[c], other2[c], far2[c]])
+        two = product(tokens, lots[c][1], weights, c, CHUNKS, two)
+    d = slot(rest=other3[1:], near3=near3, far3=far3, two=two)
+
+    other3, near3, far3 = other3[:1] + d["rest"], d["near3"], d["far3"]
+    returned.append(lax.ppermute(d["two"], "ctx", ring_perm(count, -2)))
+    far3 += [near_of(x) for x in other3[1:]]
+    three = None
+    for c in each[:-1]:
+        lots[c].append([ring3[c], near3[c], other3[c], far3[c]])
+        three = product(tokens, lots[c][2], weights, c, CHUNKS, three)
+    d = slot(three=three, rest=far3[1:], normed=normed)
+
+    far3, normed = far3[:1] + d["rest"], d["normed"]
+    lots[-1].append([ring3[-1], near3[-1], other3[-1], far3[-1]])
+    three = product(tokens, lots[-1][2], weights, CHUNKS - 1, CHUNKS, d["three"])
+    returned.append(lax.ppermute(three, "ctx", ring_perm(count, -3)))
     flat = []
-    for c in range(CHUNKS):
-        parts = outer(normed, grad_out, lots[c], c, own)
+    for c in each:
+        parts = outer([after(normed[0], three)] + normed[1:], grad_out, lots[c], c, own)
         flat.append(parts[0])
         for s in range(1, minor):
             flat.append(lax.ppermute(parts[s], "ctx", pair_perm(count, s)))
+    d = slot(returned=returned, first=flat[0])
+    returned, flat[0] = d["returned"], d["first"]
 
     grad, gain_sum, inner = pl.pallas_call(
         back_kernel,

time: 288 us -> 306 us (1.062)
  local copies, waits for them, and re-layouts: 48.6 us -> 10 us
  Pallas kernels: 74 us -> 110 us
  waiting for transfers between devices: 102 us -> 116 us
  starting transfers between devices: 56 us -> 62.9 us
    ppermute x6, waiting for transfers between devices: 46.1 us -> 3.5 us  [ring(): return lax.ppermute(x, 'ctx', ring_perm(count, 1))]
    unnamed x158 -> x66, local copies, waits for them, and re-layouts: 45.5 us -> 6.98 us
    all_to_all x0 -> x2, waiting for transfers between devices: none -> 28.9 us  [the longest x1 17.8 us: shards(): spread = lax.all_to_all(put, 'ctx', 0, 0, tiled=True)]
    ppermute x7 -> x5, waiting for transfers between devices: 16.4 us -> 31.9 us  [butterfly(): lax.ppermute(part, axis, [(i, i ^ step) for i in range(count)])]
    pallas_call x7, Pallas kernels: 23.8 us -> 33.3 us  [product(): pl.pallas_call(functools.partial(product_kernel, len(pieces), len(weights...]
    all_to_all x0 -> x2, starting transfers between devices: none -> 8.78 us  [the longest x1 5.36 us: shards(): lax.all_to_all(states, 'ctx', 0, 0, tiled=True).reshape(heads, size, size)]
    ppermute x3, waiting for transfers between devices: 3.49 us -> 12 us  [shards(): lax.ppermute(sent[s], 'ctx', ring_perm(count, s))]
    ppermute x21 -> x23, waiting for transfers between devices: 31.4 us -> 39.7 us  [the longest x20 39.7 us: over(): return lax.ppermute(x, 'head', perm)]
  transfers between devices with their start and end apart: 44 -> 44, of which waited for: 16 -> 15; matrix products, arithmetic and copies ran while one was open for 2% -> 1% of each run, Pallas kernels for 22% -> 28%
where the time goes in v3:
time: 306 us; the launch traced here: 304 us
  waiting for transfers between devices  116 us (38%)
  Pallas kernels  110 us (36%)
  starting transfers between devices  62.9 us (21%)
  local copies, waits for them, and re-layouts  10 us (3%)
  other arithmetic  4.23 us (1%)
    ppermute x20, waiting for transfers between devices, over(): return lax.ppermute(x, 'head', perm)  39.7 us
    pallas_call x7, Pallas kernels, product(): pl.pallas_call(functools.partial(product_kernel, len(pieces), len(weights...  33.3 us
    ppermute x5, waiting for transfers between devices, butterfly(): lax.ppermute(part, axis, [(i, i ^ step) for i in range(count)])  31.9 us
    all_to_all x1, waiting for transfers between devices, shards(): spread = lax.all_to_all(put, 'ctx', 0, 0, tiled=True)  17.8 us
    pallas_call x2, Pallas kernels, outer(): pl.pallas_call(functools.partial(outer_kernel, [1] + [len(lot) for lot in...  16.6 us
    ppermute x3, waiting for transfers between devices, shards(): lax.ppermute(sent[s], 'ctx', ring_perm(count, s))  12 us
    all_to_all x1, waiting for transfers between devices, shards(): lax.all_to_all(states, 'ctx', 0, 0, tiled=True).reshape(heads, size, size)  11.2 us
    ppermute x20, starting transfers between devices, over(): return lax.ppermute(x, 'head', perm)  10.6 us
  transfers between devices with their start and end apart: 44, of which 15 were waited for; matrix products, arithmetic and copies ran while one was open for 1% of the time, Pallas kernels for 28%

profile of v3, /device:TPU:0, one launch (start us, length us, event | category | flops | bytes accessed | tf_op | source)
XLA Modules:
  0.0 304.1 jit_solution(9066640241951674560)
XLA Ops:
  2.0 7.2 %states.1 = (bf16[8,144,128]{2,1,0:T(8,128)(2,1)}, f32[8,384]{1,0:T(8,128)}, f32[384,8]{1,0:T(8,128)}) custom-call(f32[8,384]{1,0:T(8,128)} %decay_ref.1, bf16[384,1024]{1,0:T(8,128)(2,1)} %k_ref.7, bf16[384,1024]{1,0:T(8,128)(2,1)} %v_ref.7), custom_call_target="tpu_custom_call" | custom-call | flops 1000 | bytes 1000 | tf_op jit(solution)/shard_map/states/pallas_call | solution.py:419
  9.1 3.0 collective-permute-start.1
  12.2 2.6 collective-permute-start
  14.8 3.4 %all-to-all-start = ((bf16[8,144,128]{2,1,0:T(8,128)(2,1)}), bf16[8,144,128]{2,1,0:T(8,128)(2,1)S(1)}, u32[]{:S(2)}, u32[]{:S(2)}) async-start(bf16[8,144,128]{2,1,0:T(8,128)(2,1)} %get-tuple-element.90), calls=%async_computation | async-start | bytes 589824 | tf_op jit(solution)/shard_map/all_to_all | solution.py:425
  18.2 7.4 %weights.1 = (bf16[8,384,384]{2,1,0:T(8,128)(2,1)}, f32[384,1024]{1,0:T(8,128)}) custom-call(bf16[384,1024]{1,0:T(8,128)(2,1)} %q_ref.7, bf16[384,1024]{1,0:T(8,128)(2,1)} %k_ref.7, bf16[384,1024]{1,0:T(8,128)(2,1)} %v_ref.7, f32[8,384]{1,0:T(8,128)} %get-tuple-element.87.run_ref, f32[384,8]{1,0:T(8,128)} %get-tuple-element.88.turned_ref), custom_call_target="tpu_custom_call" | custom-call | flops 1000 | bytes 1000 | tf_op jit(solution)/shard_map/weights/pallas_call | solution.py:426
  25.6 2.2 fusion.order_ref
  27.8 17.8 %all-to-all-done.in_ref = bf16[8,144,128]{2,1,0:T(8,128)(2,1)S(1)} async-done(((bf16[8,144,128]{2,1,0:T(8,128)(2,1)}), bf16[8,144,128]{2,1,0:T(8,128)(2,1)S(1)}, u32[]{:S(2)}, u32[]{:S(2)}) %all-to-all-start) | async-done | bytes 294944 | tf_op jit(solution)/shard_map/all_to_all | solution.py:425
  46.7 1.7 scan.2
  48.5 5.4 %all-to-all-start.1 = ((bf16[8,128,128]{2,1,0:T(8,128)(2,1)}), bf16[8,128,128]{2,1,0:T(8,128)(2,1)S(1)}, u32[]{:S(2)}, u32[]{:S(2)}) async-start(bf16[8,128,128]{2,1,0:T(8,128)(2,1)} %scan.2), calls=%async_computation.1 | async-start | bytes 524288 | tf_op jit(solution)/shard_map/all_to_all | solution.py:438
  55.3 11.2 %all-to-all-done.1.state_ref = bf16[8,128,128]{2,1,0:T(8,128)(2,1)S(1)} async-done(((bf16[8,128,128]{2,1,0:T(8,128)(2,1)}), bf16[8,128,128]{2,1,0:T(8,128)(2,1)S(1)}, u32[]{:S(2)}, u32[]{:S(2)}) %all-to-all-start.1) | async-done | bytes 262176 | tf_op jit(solution)/shard_map/all_to_all | solution.py:438
  67.2 6.7 %attend.1 = (f32[384,1024]{1,0:T(8,128)}, f32[1,384]{1,0:T(1,128)}) custom-call(bf16[384,1024]{1,0:T(8,128)(2,1)} %q_ref.7, bf16[8,128,128]{2,1,0:T(8,128)(2,1)} %copy-done.16, f32[384,8]{1,0:T(8,128)} %get-tuple-element.88.turned_ref, f32[384,1024]{1,0:T(8,128)} %get-tuple-element.94.intra_ref), custom_call_target="tpu_custom_call" | custom-call | flops 1000 | bytes 1000 | tf_op jit(solution)/shard_map/attend/pallas_call | solution.py:443
  78.0 1.5 collective-permute-done.9
  81.9 11.6 %collective-permute-done.5.refs_3_.refs_7_ = bf16[96,3072]{1,0:T(8,128)(2,1)S(1)} collective-permute-done((bf16[96,3072]{1,0:T(8,128)(2,1)}, bf16[96,3072]{1,0:T(8,128)(2,1)S(1)}, u32[]{:S(2)}, u32[]{:S(2)}) %collective-permute-start.5) | collective-permute-done | bytes 589856 | tf_op jit(solution)/shard_map/ppermute | solution.py:403
  93.5 3.5 %collective-permute-done.7.refs_1_.refs_9_ = bf16[96,3072]{1,0:T(8,128)(2,1)} collective-permute-done((bf16[96,3072]{1,0:T(8,128)(2,1)}, bf16[96,3072]{1,0:T(8,128)(2,1)}, u32[]{:S(2)}, u32[]{:S(2)}) %collective-permute-start.7) | collective-permute-done | bytes 589856 | tf_op jit(solution)/shard_map/ppermute | solution.py:400
  100.1 1.6 collective-permute-start.16
  101.7 12.2 %collective-permute-done.15.refs_3_.refs_11_ = bf16[96,3072]{1,0:T(8,128)(2,1)S(1)} collective-permute-done((bf16[96,3072]{1,0:T(8,128)(2,1)}, bf16[96,3072]{1,0:T(8,128)(2,1)S(1)}, u32[]{:S(2)}, u32[]{:S(2)}) %collective-permute-start.15) | collective-permute-done | bytes 589856 | tf_op jit(solution)/shard_map/ppermute | solution.py:403
  115.6 4.0 %norm.1 = (bf16[384,256]{1,0:T(8,128)(2,1)}, bf16[384,256]{1,0:T(8,128)(2,1)}, bf16[384,256]{1,0:T(8,128)(2,1)}, bf16[384,256]{1,0:T(8,128)(2,1)}) custom-call(s32[1]{0:T(128)} %bitcast.2.mine_ref.refs_0_, f32[384,1024]{1,0:T(8,128)} %get-tuple-element.95.attn_ref, f32[384,1]{1,0:T(8,128)} %copy.13.inv_ref, f32[1,1024]{1,0:T(1,128)} %bitcast.18, ...), custom_call_target="tpu_custom_call" | custom-call | flops 1000 | bytes 1000 | tf_op jit(solution)/shard_map/norm/pallas_call | solution.py:460
  119.7 5.9 %collective-permute-done.16.refs_3_.refs_11_ = bf16[96,3072]{1,0:T(8,128)(2,1)} collective-permute-done((bf16[96,3072]{1,0:T(8,128)(2,1)}, bf16[96,3072]{1,0:T(8,128)(2,1)}, u32[]{:S(2)}, u32[]{:S(2)}) %collective-permute-start.16) | collective-permute-done | bytes 589856 | tf_op jit(solution)/shard_map/ppermute | solution.py:403
  127.8 6.4 %product.7.refs_0_ = bf16[384,256]{1,0:T(8,128)(2,1)} custom-call(s32[1]{0:T(128)} %bitcast.2.mine_ref.refs_0_, bf16[384,6144]{1,0:T(8,128)(2,1)} %refs_4_.3, bf16[128,6144]{1,0:T(8,128)(2,1)} %bitcast.9, bf16[128,6144]{1,0:T(8,128)(2,1)} %copy-done.1), custom_call_target="tpu_custom_call" | custom-call | flops 1000 | bytes 1000 | tf_op jit(solution)/shard_map/product/pallas_call | solution.py:227
  134.2 4.4 %product.8.refs_7_ = f32[384,256]{1,0:T(8,128)} custom-call(s32[1]{0:T(128)} %bitcast.2.mine_ref.refs_0_, bf16[96,3072]{1,0:T(8,128)(2,1)} %collective-permute-done.refs_1_.refs_5_, bf16[96,3072]{1,0:T(8,128)(2,1)} %copy-done.6, bf16[96,3072]{1,0:T(8,128)(2,1)} %collective-permute-done.4.refs_3_.refs_7_, bf16[96,3072]{1,0:T(8,128)(2,1)} %copy-done.8, ...), custom_call_target="tpu_custom_call" | custom-call | flops 1000 | bytes 1000 | tf_op jit(solution)/shard_map/product/pallas_call | solution.py:227
  138.6 4.6 %product.9 = bf16[384,256]{1,0:T(8,128)(2,1)} custom-call(s32[1]{0:T(128)} %bitcast.2.mine_ref.refs_0_, bf16[96,3072]{1,0:T(8,128)(2,1)} %collective-permute-done.1.refs_1_.refs_5_, bf16[96,3072]{1,0:T(8,128)(2,1)} %copy-done.3, bf16[96,3072]{1,0:T(8,128)(2,1)} %copy-done.2, bf16[96,3072]{1,0:T(8,128)(2,1)} %copy-done.5, bf16[128,6144]{1,0:T(8,128)(2,1)} %bitcast.11, ...), custom_call_target="tpu_custom_call" | custom-call | flops 1000 | bytes 1000 | tf_op jit(solution)/shard_map/product/pallas_call | solution.py:227
  145.5 4.4 %product.10.refs_7_ = f32[384,256]{1,0:T(8,128)} custom-call(s32[1]{0:T(128)} %bitcast.2.mine_ref.refs_0_, bf16[96,3072]{1,0:T(8,128)(2,1)} %copy-done.4, bf16[96,3072]{1,0:T(8,128)(2,1)} %collective-permute-done.13.refs_2_.refs_10_, bf16[96,3072]{1,0:T(8,128)(2,1)} %copy-done.9, bf16[96,3072]{1,0:T(8,128)(2,1)} %copy-done.13, bf16[128,6144]{1,0:T(8,128)(2,1)} %bitcast.12, ...), custom_call_target="tpu_custom_call" | custom-call | flops 1000 | bytes 1000 | tf_op jit(solution)/shard_map/product/pallas_call | solution.py:227
  150.0 4.6 %product.11 = bf16[384,256]{1,0:T(8,128)(2,1)} custom-call(s32[1]{0:T(128)} %bitcast.2.mine_ref.refs_0_, bf16[96,3072]{1,0:T(8,128)(2,1)} %collective-permute-done.7.refs_1_.refs_9_, bf16[96,3072]{1,0:T(8,128)(2,1)} %collective-permute-done.14.refs_2_.refs_10_, bf16[96,3072]{1,0:T(8,128)(2,1)} %collective-permute-done.16.refs_3_.refs_11_, ...), custom_call_target="tpu_custom_call" | custom-call | flops 1000 | bytes 1000 | tf_op jit(solution)/shard_map/product/pallas_call | solution.py:227
  154.6 6.1 %collective-permute-done.28.refs_3_.refs_15_ = bf16[96,3072]{1,0:T(8,128)(2,1)S(1)} collective-permute-done((bf16[96,3072]{1,0:T(8,128)(2,1)}, bf16[96,3072]{1,0:T(8,128)(2,1)S(1)}, u32[]{:S(2)}, u32[]{:S(2)}) %collective-permute-start.28) | collective-permute-done | bytes 589856 | tf_op jit(solution)/shard_map/ppermute | solution.py:403
  161.0 3.1 %collective-permute-start.24 = (bf16[384,256]{1,0:T(8,128)(2,1)}, bf16[384,256]{1,0:T(8,128)(2,1)S(1)}, u32[]{:S(2)}, u32[]{:S(2)}) collective-permute-start(bf16[384,256]{1,0:T(8,128)(2,1)} %get-tuple-element.126), channel_id=1, source_target_pairs={{0,24},{4,28},{8,16},{12,20},{24,0},{28,4},{16,8},{20,12},{1,25},{... | collective-permute-start | bytes 589832 | tf_op jit(solution)/shard_map/ppermute | solution.py:486
  164.1 1.8 collective-permute-start.25
  165.9 4.4 %product.12.refs_7_ = f32[384,256]{1,0:T(8,128)} custom-call(s32[1]{0:T(128)} %bitcast.2.mine_ref.refs_0_, bf16[96,3072]{1,0:T(8,128)(2,1)} %collective-permute-done.12.refs_1_.refs_13_, bf16[96,3072]{1,0:T(8,128)(2,1)} %copy-done.14, bf16[96,3072]{1,0:T(8,128)(2,1)} %collective-permute-done.21.refs_3_.refs_15_, bf16[96,3072]{1,0:T(8,128)(2,1)} %copy-done.15, ...), custom_call_target="tpu_custom_call" | custom-call | flops 1000 | bytes 1000 | tf_op jit(solution)/shard_map/product/pallas_call | solution.py:227
  170.3 12.0 %collective-permute-done.23.refs_1_ = bf16[384,256]{1,0:T(8,128)(2,1)S(1)} collective-permute-done((bf16[384,256]{1,0:T(8,128)(2,1)}, bf16[384,256]{1,0:T(8,128)(2,1)S(1)}, u32[]{:S(2)}, u32[]{:S(2)}) %collective-permute-start.23) | collective-permute-done | bytes 196640 | tf_op jit(solution)/shard_map/ppermute | solution.py:486
  182.4 3.0 collective-permute-start.31
  186.3 4.6 %product.13 = bf16[384,256]{1,0:T(8,128)(2,1)} custom-call(s32[1]{0:T(128)} %bitcast.2.mine_ref.refs_0_, bf16[96,3072]{1,0:T(8,128)(2,1)} %collective-permute-done.22.refs_1_.refs_13_, bf16[96,3072]{1,0:T(8,128)(2,1)} %copy-done.11, bf16[96,3072]{1,0:T(8,128)(2,1)} %copy-done.10, bf16[96,3072]{1,0:T(8,128)(2,1)} %copy-done.12, bf16[128,6144]{1,0:T(8,128)(2,1)} %bitcast.15, ...), custom_call_target="tpu_custom_call" | custom-call | flops 1000 | bytes 1000 | tf_op jit(solution)/shard_map/product/pallas_call | solution.py:227
  190.8 6.0 %collective-permute-start.32 = (bf16[384,256]{1,0:T(8,128)(2,1)}, bf16[384,256]{1,0:T(8,128)(2,1)S(1)}, u32[]{:S(2)}, u32[]{:S(2)}) collective-permute-start(bf16[384,256]{1,0:T(8,128)(2,1)} %product.13), channel_id=1, source_target_pairs={{0,8},{4,12},{8,24},{12,28},{24,16},{28,20},{16,0},{20,4},{1,9},{5... | collective-permute-start | bytes 589832 | tf_op jit(solution)/shard_map/ppermute | solution.py:508
  196.8 8.3 %outer.2 = (bf16[128,3072]{1,0:T(8,128)(2,1)}, bf16[128,3072]{1,0:T(8,128)(2,1)}) custom-call(bf16[384,256]{1,0:T(8,128)(2,1)} %get-tuple-element.142.refs_0_, bf16[384,256]{1,0:T(8,128)(2,1)} %copy-done.22, bf16[384,256]{1,0:T(8,128)(2,1)} %copy-done.23, bf16[384,256]{1,0:T(8,128)(2,1)} %copy-done.24, bf16[384,6144]{1,0:T(8,128)(2,1)} %refs_4_.3, ...), custom_call_target="tpu_custom_call" | custom-call | flops 1000 | bytes 1000 | tf_op jit(solution)/shard_map/outer/pallas_call | solution.py:267
  205.9 4.3 %back.1 = (bf16[384,1024]{1,0:T(8,128)(2,1)}, f32[1,1024]{1,0:T(1,128)}, f32[1,384]{1,0:T(1,128)}) custom-call(bf16[1024,1024]{1,0:T(8,128)(2,1)} %fusion.order_ref, f32[384,1024]{1,0:T(8,128)} %get-tuple-element.95.attn_ref, f32[384,1]{1,0:T(8,128)} %copy.13.inv_ref, f32[1,1024]{1,0:T(1,128)} %bitcast.19, bf16[384,256]{1,0:T(8,128)(2,1)} %product.7.refs_0_, ...), custom_call_target="tpu_custom_call" | custom-call | flops 1000 | bytes 1000 | tf_op jit(solution)/shard_map/back/pallas_call | solution.py:518
  212.8 3.0 collective-permute-done.34
  216.7 7.6 %grads.1 = (bf16[384,1024]{1,0:T(8,128)(2,1)}, bf16[8,144,128]{2,1,0:T(8,128)(2,1)}) custom-call(bf16[384,1024]{1,0:T(8,128)(2,1)} %get-tuple-element.154.grad_ref, f32[384,1024]{1,0:T(8,128)} %get-tuple-element.95.attn_ref, f32[384,1]{1,0:T(8,128)} %copy.13.inv_ref, f32[384,1]{1,0:T(8,128)} %copy.15.shift_ref, f32[1,1024]{1,0:T(1,128)} %bitcast.20, ...), custom_call_target="tpu_custom_call" | custom-call | flops 1000 | bytes 1000 | tf_op jit(solution)/shard_map/grads/pallas_call | solution.py:529
  224.2 5.2 %all-to-all-start.2 = ((bf16[8,144,128]{2,1,0:T(8,128)(2,1)}), bf16[8,144,128]{2,1,0:T(8,128)(2,1)S(1)}, u32[]{:S(2)}, u32[]{:S(2)}) async-start(bf16[8,144,128]{2,1,0:T(8,128)(2,1)} %get-tuple-element.159), calls=%async_computation.2 | async-start | bytes 589824 | tf_op jit(solution)/shard_map/all_to_all | solution.py:137
  229.4 8.3 %outer.3 = (bf16[128,3072]{1,0:T(8,128)(2,1)}, bf16[128,3072]{1,0:T(8,128)(2,1)}) custom-call(bf16[384,256]{1,0:T(8,128)(2,1)} %get-tuple-element.142.refs_0_, bf16[384,256]{1,0:T(8,128)(2,1)} %copy-done.22, bf16[384,256]{1,0:T(8,128)(2,1)} %copy-done.23, bf16[384,256]{1,0:T(8,128)(2,1)} %copy-done.24, bf16[384,6144]{1,0:T(8,128)(2,1)} %refs_4_.3, ...), custom_call_target="tpu_custom_call" | custom-call | flops 1000 | bytes 1000 | tf_op jit(solution)/shard_map/outer/pallas_call | solution.py:267
  237.7 2.1 collective-permute-start.36
  240.6 1.7 scan.3
  242.3 5.9 %all-to-all-start.3 = ((bf16[8,128,128]{2,1,0:T(8,128)(2,1)}), bf16[8,128,128]{2,1,0:T(8,128)(2,1)S(1)}, u32[]{:S(2)}, u32[]{:S(2)}) async-start(bf16[8,128,128]{2,1,0:T(8,128)(2,1)} %scan.3), calls=%async_computation.3 | async-start | bytes 524288 | tf_op jit(solution)/shard_map/all_to_all | solution.py:144
  248.3 2.0 collective-permute-start.37
  250.3 25.7 %collective-permute-done.37 = f32[1,1024]{1,0:T(1,128)S(1)} collective-permute-done((f32[1,1024]{1,0:T(1,128)S(1)}, f32[1,1024]{1,0:T(1,128)S(1)}, u32[]{:S(2)}, u32[]{:S(2)}) %collective-permute-start.37) | collective-permute-done | bytes 4128 | tf_op jit(solution)/shard_map/ppermute | solution.py:68
  276.0 1.7 collective-permute-start.38
  277.7 1.9 collective-permute-done.38
  279.6 2.6 collective-permute-start.39
  282.2 9.0 %inside.1 = (bf16[384,1024]{1,0:T(8,128)(2,1)}, f32[384,1024]{1,0:T(8,128)}, f32[384,1024]{1,0:T(8,128)}) custom-call(bf16[384,1024]{1,0:T(8,128)(2,1)} %get-tuple-element.156.grad_ref, bf16[384,1024]{1,0:T(8,128)(2,1)} %q_ref.7, bf16[384,1024]{1,0:T(8,128)(2,1)} %k_ref.7, bf16[384,1024]{1,0:T(8,128)(2,1)} %v_ref.7, ...), custom_call_target="tpu_custom_call" | custom-call | flops 1000 | bytes 1000 | tf_op jit(solution)/shard_map/inside/pallas_call | solution.py:536
  292.9 3.3 %sum.1 = bf16[128,6144]{1,0:T(8,128)(2,1)} custom-call(bf16[128,3072]{1,0:T(8,128)(2,1)} %get-tuple-element.164.refs_0_, bf16[128,3072]{1,0:T(8,128)(2,1)} %copy-done.21, bf16[128,3072]{1,0:T(8,128)(2,1)} %get-tuple-element.166.refs_2_, bf16[128,3072]{1,0:T(8,128)(2,1)} %copy-done.20), custom_call_target="tpu_custom_call" | custom-call | flops 1000 | bytes 1000 | tf_op jit(solution)/shard_map/sum/pallas_call | solution.py:545
  296.9 7.1 %outside.1 = (bf16[384,1024]{1,0:T(8,128)(2,1)}, bf16[384,1024]{1,0:T(8,128)(2,1)}) custom-call(bf16[384,1024]{1,0:T(8,128)(2,1)} %k_ref.7, bf16[384,1024]{1,0:T(8,128)(2,1)} %v_ref.7, bf16[8,128,128]{2,1,0:T(8,128)(2,1)} %copy-done.19, f32[384,8]{1,0:T(8,128)} %get-tuple-element.88.turned_ref, f32[384,1024]{1,0:T(8,128)} %get-tuple-element.160.gk_in, ...), custom_call_target="tpu_custom_call" | custom-call | flops 1000 | bytes 1000 | tf_op jit(solution)/shard_map/outside/pallas_call | solution.py:541
  (139 shorter events, 29.3 us)
Async XLA Ops:
  9.1 36.5 %collective-permute-start.1 = (bf16[96,3072]{1,0:T(8,128)(2,1)S(1)}, bf16[96,3072]{1,0:T(8,128)(2,1)}, u32[]{:S(2)}, u32[]{:S(2)}) collective-permute-start(bf16[96,3072]{1,0:T(8,128)(2,1)S(1)} %get-tuple-element.91), channel_id=1, source_target_pairs={{0,8},{4,12},{8,24},{12,28},{24,16},{28,20},{16,0},{20,4},{1,9},{5... | collective-permute-start | bytes 1769480 | tf_op jit(solution)/shard_map/ppermute | solution.py:400
  12.2 33.4 %collective-permute-start = (bf16[96,3072]{1,0:T(8,128)(2,1)S(1)}, bf16[96,3072]{1,0:T(8,128)(2,1)}, u32[]{:S(2)}, u32[]{:S(2)}) collective-permute-start(bf16[96,3072]{1,0:T(8,128)(2,1)S(1)} %get-tuple-element.170), channel_id=1, source_target_pairs={{0,8},{4,12},{8,24},{12,28},{24,16},{28,20},{16,0},{20,4},{1,9},{5... | collective-permute-start | bytes 1769480 | tf_op jit(solution)/shard_map/ppermute | solution.py:400
  14.8 30.8 %all-to-all-start = ((bf16[8,144,128]{2,1,0:T(8,128)(2,1)}), bf16[8,144,128]{2,1,0:T(8,128)(2,1)S(1)}, u32[]{:S(2)}, u32[]{:S(2)}) async-start(bf16[8,144,128]{2,1,0:T(8,128)(2,1)} %get-tuple-element.90), calls=%async_computation | async-start | bytes 589824 | tf_op jit(solution)/shard_map/all_to_all | solution.py:425
  27.8 52.6 %copy-start = (bf16[8,16,6144]{2,1,0:T(8,128)(2,1)S(1)}, bf16[8,16,6144]{2,1,0:T(8,128)(2,1)}, u32[]{:S(2)}) copy-start(bf16[8,16,6144]{2,1,0:T(8,128)(2,1)} %param.12) | copy-start | bytes 4718596
  45.6 34.0 %collective-permute-start.6 = (bf16[96,3072]{1,0:T(8,128)(2,1)}, bf16[96,3072]{1,0:T(8,128)(2,1)S(1)}, u32[]{:S(2)}, u32[]{:S(2)}) collective-permute-start(bf16[96,3072]{1,0:T(8,128)(2,1)} %collective-permute-done.refs_1_.refs_5_), channel_id=1, source_target_pairs={{0,8},{4,12},{8,24},{12,28},{24,16},{28,20},{16,0},{20,4},{1,9},{5... | collective-permute-start | bytes 1769480 | tf_op jit(solution)/shard_map/ppermute | solution.py:400
  48.5 18.0 %all-to-all-start.1 = ((bf16[8,128,128]{2,1,0:T(8,128)(2,1)}), bf16[8,128,128]{2,1,0:T(8,128)(2,1)S(1)}, u32[]{:S(2)}, u32[]{:S(2)}) async-start(bf16[8,128,128]{2,1,0:T(8,128)(2,1)} %scan.2), calls=%async_computation.1 | async-start | bytes 524288 | tf_op jit(solution)/shard_map/all_to_all | solution.py:438
  53.8 26.6 %collective-permute-start.4 = (bf16[96,3072]{1,0:T(8,128)(2,1)}, bf16[96,3072]{1,0:T(8,128)(2,1)}, u32[]{:S(2)}, u32[]{:S(2)}) collective-permute-start(bf16[96,3072]{1,0:T(8,128)(2,1)} %collective-permute-done.refs_1_.refs_5_), channel_id=1, source_target_pairs={{0,2},{1,3},{2,0},{3,1},{4,6},{5,7},{6,4},{7,5},{8,10},{9,11},{10,... | collective-permute-start | bytes 1769480 | tf_op jit(solution)/shard_map/ppermute | solution.py:403
  73.9 1.4 collective-permute-start.8
  76.0 3.6 %collective-permute-start.9 = (f32[1,384]{1,0:T(1,128)S(1)}, f32[1,384]{1,0:T(1,128)S(1)}, u32[]{:S(2)}, u32[]{:S(2)}) collective-permute-start(f32[1,384]{1,0:T(1,128)S(1)} %add.152), channel_id=1, source_target_pairs={{0,2},{1,3},{2,0},{3,1},{4,6},{5,7},{6,4},{7,5},{8,10},{9,11},{10,... | collective-permute-start | bytes 4616 | tf_op jit(solution)/shard_map/ppermute | solution.py:403
  77.5 4.4 %collective-permute-start.2 = (bf16[96,3072]{1,0:T(8,128)(2,1)}, bf16[96,3072]{1,0:T(8,128)(2,1)S(1)}, u32[]{:S(2)}, u32[]{:S(2)}) collective-permute-start(bf16[96,3072]{1,0:T(8,128)(2,1)} %collective-permute-done.refs_1_.refs_5_), channel_id=1, source_target_pairs={{0,1},{1,0},{2,3},{3,2},{4,5},{5,4},{6,7},{7,6},{8,9},{9,8},{10,11... | collective-permute-start | bytes 1769480 | tf_op jit(solution)/shard_map/ppermute | solution.py:403
  77.5 16.0 %collective-permute-start.5 = (bf16[96,3072]{1,0:T(8,128)(2,1)}, bf16[96,3072]{1,0:T(8,128)(2,1)S(1)}, u32[]{:S(2)}, u32[]{:S(2)}) collective-permute-start(bf16[96,3072]{1,0:T(8,128)(2,1)} %collective-permute-done.1.refs_1_.refs_5_), channel_id=1, source_target_pairs={{0,2},{1,3},{2,0},{3,1},{4,6},{5,7},{6,4},{7,5},{8,10},{9,11},{10,... | collective-permute-start | bytes 1769480 | tf_op jit(solution)/shard_map/ppermute | solution.py:403
  79.6 13.9 %collective-permute-start.3 = (bf16[96,3072]{1,0:T(8,128)(2,1)}, bf16[96,3072]{1,0:T(8,128)(2,1)S(1)}, u32[]{:S(2)}, u32[]{:S(2)}) collective-permute-start(bf16[96,3072]{1,0:T(8,128)(2,1)} %collective-permute-done.1.refs_1_.refs_5_), channel_id=1, source_target_pairs={{0,1},{1,0},{2,3},{3,2},{4,5},{5,4},{6,7},{7,6},{8,9},{9,8},{10,11... | collective-permute-start | bytes 1769480 | tf_op jit(solution)/shard_map/ppermute | solution.py:403
  79.6 17.4 %collective-permute-start.7 = (bf16[96,3072]{1,0:T(8,128)(2,1)}, bf16[96,3072]{1,0:T(8,128)(2,1)}, u32[]{:S(2)}, u32[]{:S(2)}) collective-permute-start(bf16[96,3072]{1,0:T(8,128)(2,1)} %collective-permute-done.1.refs_1_.refs_5_), channel_id=1, source_target_pairs={{0,8},{4,12},{8,24},{12,28},{24,16},{28,20},{16,0},{20,4},{1,9},{5... | collective-permute-start | bytes 1769480 | tf_op jit(solution)/shard_map/ppermute | solution.py:400
  80.4 45.3 %collective-permute-start.17 = (bf16[128,6144]{1,0:T(8,128)(2,1)S(1)}, bf16[128,6144]{1,0:T(8,128)(2,1)S(1)}, u32[]{:S(2)}, u32[]{:S(2)}) collective-permute-start(bf16[128,6144]{1,0:T(8,128)(2,1)S(1)} %bitcast.16), channel_id=1, source_target_pairs={{0,4},{4,0},{8,12},{12,8},{16,20},{20,16},{24,28},{28,24},{1,5},{5... | collective-permute-start | bytes 4718600 | tf_op jit(solution)/shard_map/ppermute | solution.py:442
  81.9 32.0 %copy-start.6 = (bf16[96,3072]{1,0:T(8,128)(2,1)}, bf16[96,3072]{1,0:T(8,128)(2,1)S(1)}, u32[]{:S(2)}) copy-start(bf16[96,3072]{1,0:T(8,128)(2,1)S(1)} %collective-permute-done.2.refs_2_.refs_6_) | copy-start | bytes 1769476
  97.0 3.0 collective-permute-start.10
  97.0 3.1 %collective-permute-start.11 = (bf16[96,3072]{1,0:T(8,128)(2,1)S(1)}, bf16[96,3072]{1,0:T(8,128)(2,1)S(1)}, u32[]{:S(2)}, u32[]{:S(2)}) collective-permute-start(bf16[96,3072]{1,0:T(8,128)(2,1)S(1)} %collective-permute-done.5.refs_3_.refs_7_), channel_id=1, source_target_pairs={{0,1},{1,0},{2,3},{3,2},{4,5},{5,4},{6,7},{7,6},{8,9},{9,8},{10,11... | collective-permute-start | bytes 1769480 | tf_op jit(solution)/shard_map/ppermute | solution.py:403
  97.5 16.4 %collective-permute-start.15 = (bf16[96,3072]{1,0:T(8,128)(2,1)}, bf16[96,3072]{1,0:T(8,128)(2,1)S(1)}, u32[]{:S(2)}, u32[]{:S(2)}) collective-permute-start(bf16[96,3072]{1,0:T(8,128)(2,1)} %copy-done.4), channel_id=1, source_target_pairs={{0,2},{1,3},{2,0},{3,1},{4,6},{5,7},{6,4},{7,5},{8,10},{9,11},{10,... | collective-permute-start | bytes 1769480 | tf_op jit(solution)/shard_map/ppermute | solution.py:403
  99.0 20.6 %collective-permute-start.13 = (bf16[96,3072]{1,0:T(8,128)(2,1)}, bf16[96,3072]{1,0:T(8,128)(2,1)}, u32[]{:S(2)}, u32[]{:S(2)}) collective-permute-start(bf16[96,3072]{1,0:T(8,128)(2,1)} %copy-done.4), channel_id=1, source_target_pairs={{0,1},{1,0},{2,3},{3,2},{4,5},{5,4},{6,7},{7,6},{8,9},{9,8},{10,11... | collective-permute-start | bytes 1769480 | tf_op jit(solution)/shard_map/ppermute | solution.py:403
  100.0 19.8 %collective-permute-start.12 = (bf16[96,3072]{1,0:T(8,128)(2,1)}, bf16[96,3072]{1,0:T(8,128)(2,1)}, u32[]{:S(2)}, u32[]{:S(2)}) collective-permute-start(bf16[96,3072]{1,0:T(8,128)(2,1)} %copy-done.4), channel_id=1, source_target_pairs={{0,8},{4,12},{8,24},{12,28},{24,16},{28,20},{16,0},{20,4},{1,9},{5... | collective-permute-start | bytes 1769480 | tf_op jit(solution)/shard_map/ppermute | solution.py:400
  100.1 25.5 %collective-permute-start.16 = (bf16[96,3072]{1,0:T(8,128)(2,1)}, bf16[96,3072]{1,0:T(8,128)(2,1)}, u32[]{:S(2)}, u32[]{:S(2)}) collective-permute-start(bf16[96,3072]{1,0:T(8,128)(2,1)} %collective-permute-done.7.refs_1_.refs_9_), channel_id=1, source_target_pairs={{0,2},{1,3},{2,0},{3,1},{4,6},{5,7},{6,4},{7,5},{8,10},{9,11},{10,... | collective-permute-start | bytes 1769480 | tf_op jit(solution)/shard_map/ppermute | solution.py:403
  114.7 11.0 %collective-permute-start.14 = (bf16[96,3072]{1,0:T(8,128)(2,1)}, bf16[96,3072]{1,0:T(8,128)(2,1)}, u32[]{:S(2)}, u32[]{:S(2)}) collective-permute-start(bf16[96,3072]{1,0:T(8,128)(2,1)} %collective-permute-done.7.refs_1_.refs_9_), channel_id=1, source_target_pairs={{0,1},{1,0},{2,3},{3,2},{4,5},{5,4},{6,7},{7,6},{8,9},{9,8},{10,11... | collective-permute-start | bytes 1769480 | tf_op jit(solution)/shard_map/ppermute | solution.py:403
  119.6 23.6 %collective-permute-start.22 = (bf16[96,3072]{1,0:T(8,128)(2,1)}, bf16[96,3072]{1,0:T(8,128)(2,1)}, u32[]{:S(2)}, u32[]{:S(2)}) collective-permute-start(bf16[96,3072]{1,0:T(8,128)(2,1)} %collective-permute-done.7.refs_1_.refs_9_), channel_id=1, source_target_pairs={{0,8},{4,12},{8,24},{12,28},{24,16},{28,20},{16,0},{20,4},{1,9},{5... | collective-permute-start | bytes 1769480 | tf_op jit(solution)/shard_map/ppermute | solution.py:400
  125.7 17.5 %collective-permute-start.18 = (bf16[96,3072]{1,0:T(8,128)(2,1)}, bf16[96,3072]{1,0:T(8,128)(2,1)S(1)}, u32[]{:S(2)}, u32[]{:S(2)}) collective-permute-start(bf16[96,3072]{1,0:T(8,128)(2,1)} %copy-done.9), channel_id=1, source_target_pairs={{0,1},{1,0},{2,3},{3,2},{4,5},{5,4},{6,7},{7,6},{8,9},{9,8},{10,11... | collective-permute-start | bytes 1769480 | tf_op jit(solution)/shard_map/ppermute | solution.py:403
  125.8 17.4 %collective-permute-start.19 = (bf16[96,3072]{1,0:T(8,128)(2,1)}, bf16[96,3072]{1,0:T(8,128)(2,1)S(1)}, u32[]{:S(2)}, u32[]{:S(2)}) collective-permute-start(bf16[96,3072]{1,0:T(8,128)(2,1)} %collective-permute-done.16.refs_3_.refs_11_), channel_id=1, source_target_pairs={{0,1},{1,0},{2,3},{3,2},{4,5},{5,4},{6,7},{7,6},{8,9},{9,8},{10,11... | collective-permute-start | bytes 1769480 | tf_op jit(solution)/shard_map/ppermute | solution.py:403
  126.3 16.9 %collective-permute-start.21 = (bf16[96,3072]{1,0:T(8,128)(2,1)}, bf16[96,3072]{1,0:T(8,128)(2,1)}, u32[]{:S(2)}, u32[]{:S(2)}) collective-permute-start(bf16[96,3072]{1,0:T(8,128)(2,1)} %collective-permute-done.12.refs_1_.refs_13_), channel_id=1, source_target_pairs={{0,2},{1,3},{2,0},{3,1},{4,6},{5,7},{6,4},{7,5},{8,10},{9,11},{10,... | collective-permute-start | bytes 1769480 | tf_op jit(solution)/shard_map/ppermute | solution.py:403
  127.8 15.4 %collective-permute-start.20 = (bf16[96,3072]{1,0:T(8,128)(2,1)}, bf16[96,3072]{1,0:T(8,128)(2,1)S(1)}, u32[]{:S(2)}, u32[]{:S(2)}) collective-permute-start(bf16[96,3072]{1,0:T(8,128)(2,1)} %collective-permute-done.12.refs_1_.refs_13_), channel_id=1, source_target_pairs={{0,1},{1,0},{2,3},{3,2},{4,5},{5,4},{6,7},{7,6},{8,9},{9,8},{10,11... | collective-permute-start | bytes 1769480 | tf_op jit(solution)/shard_map/ppermute | solution.py:403
  144.0 10.6 %collective-permute-start.26 = (bf16[96,3072]{1,0:T(8,128)(2,1)}, bf16[96,3072]{1,0:T(8,128)(2,1)S(1)}, u32[]{:S(2)}, u32[]{:S(2)}) collective-permute-start(bf16[96,3072]{1,0:T(8,128)(2,1)} %collective-permute-done.21.refs_3_.refs_15_), channel_id=1, source_target_pairs={{0,1},{1,0},{2,3},{3,2},{4,5},{5,4},{6,7},{7,6},{8,9},{9,8},{10,11... | collective-permute-start | bytes 1769480 | tf_op jit(solution)/shard_map/ppermute | solution.py:403
  144.8 15.9 %collective-permute-start.28 = (bf16[96,3072]{1,0:T(8,128)(2,1)}, bf16[96,3072]{1,0:T(8,128)(2,1)S(1)}, u32[]{:S(2)}, u32[]{:S(2)}) collective-permute-start(bf16[96,3072]{1,0:T(8,128)(2,1)} %collective-permute-done.22.refs_1_.refs_13_), channel_id=1, source_target_pairs={{0,2},{1,3},{2,0},{3,1},{4,6},{5,7},{6,4},{7,5},{8,10},{9,11},{10,... | collective-permute-start | bytes 1769480 | tf_op jit(solution)/shard_map/ppermute | solution.py:403
  145.4 15.4 %collective-permute-start.27 = (bf16[96,3072]{1,0:T(8,128)(2,1)}, bf16[96,3072]{1,0:T(8,128)(2,1)S(1)}, u32[]{:S(2)}, u32[]{:S(2)}) collective-permute-start(bf16[96,3072]{1,0:T(8,128)(2,1)} %collective-permute-done.22.refs_1_.refs_13_), channel_id=1, source_target_pairs={{0,1},{1,0},{2,3},{3,2},{4,5},{5,4},{6,7},{7,6},{8,9},{9,8},{10,11... | collective-permute-start | bytes 1769480 | tf_op jit(solution)/shard_map/ppermute | solution.py:403
  154.6 27.8 %copy-start.26 = (bf16[384,256]{1,0:T(8,128)(2,1)S(1)}, bf16[384,256]{1,0:T(8,128)(2,1)}, u32[]{:S(2)}) copy-start(bf16[384,256]{1,0:T(8,128)(2,1)} %product.11) | copy-start | bytes 589828
  160.7 24.6 %collective-permute-start.29 = (bf16[96,3072]{1,0:T(8,128)(2,1)S(1)}, bf16[96,3072]{1,0:T(8,128)(2,1)S(1)}, u32[]{:S(2)}, u32[]{:S(2)}) collective-permute-start(bf16[96,3072]{1,0:T(8,128)(2,1)S(1)} %collective-permute-done.28.refs_3_.refs_15_), channel_id=1, source_target_pairs={{0,1},{1,0},{2,3},{3,2},{4,5},{5,4},{6,7},{7,6},{8,9},{9,8},{10,11... | collective-permute-start | bytes 1769480 | tf_op jit(solution)/shard_map/ppermute | solution.py:403
  160.8 21.5 %collective-permute-start.23 = (bf16[384,256]{1,0:T(8,128)(2,1)}, bf16[384,256]{1,0:T(8,128)(2,1)S(1)}, u32[]{:S(2)}, u32[]{:S(2)}) collective-permute-start(bf16[384,256]{1,0:T(8,128)(2,1)} %get-tuple-element.125), channel_id=1, source_target_pairs={{0,8},{4,12},{8,24},{12,28},{24,16},{28,20},{16,0},{20,4},{1,9},{5... | collective-permute-start | bytes 589832 | tf_op jit(solution)/shard_map/ppermute | solution.py:486
  161.0 24.3 %collective-permute-start.24 = (bf16[384,256]{1,0:T(8,128)(2,1)}, bf16[384,256]{1,0:T(8,128)(2,1)S(1)}, u32[]{:S(2)}, u32[]{:S(2)}) collective-permute-start(bf16[384,256]{1,0:T(8,128)(2,1)} %get-tuple-element.126), channel_id=1, source_target_pairs={{0,24},{4,28},{8,16},{12,20},{24,0},{28,4},{16,8},{20,12},{1,25},{... | collective-permute-start | bytes 589832 | tf_op jit(solution)/shard_map/ppermute | solution.py:486
  164.1 21.2 %collective-permute-start.25 = (bf16[384,256]{1,0:T(8,128)(2,1)S(1)}, bf16[384,256]{1,0:T(8,128)(2,1)S(1)}, u32[]{:S(2)}, u32[]{:S(2)}) collective-permute-start(bf16[384,256]{1,0:T(8,128)(2,1)S(1)} %copy-done.32), channel_id=1, source_target_pairs={{0,16},{4,20},{8,0},{12,4},{24,8},{28,12},{16,24},{20,28},{1,17},{... | collective-permute-start | bytes 589832 | tf_op jit(solution)/shard_map/ppermute | solution.py:486
  165.9 39.2 %collective-permute-start.30 = (bf16[384,256]{1,0:T(8,128)(2,1)S(1)}, bf16[384,256]{1,0:T(8,128)(2,1)S(1)}, u32[]{:S(2)}, u32[]{:S(2)}) collective-permute-start(bf16[384,256]{1,0:T(8,128)(2,1)S(1)} %copy-done.25), channel_id=1, source_target_pairs={{0,16},{4,20},{8,0},{12,4},{24,8},{28,12},{16,24},{20,28},{1,17},{... | collective-permute-start | bytes 589832 | tf_op jit(solution)/shard_map/ppermute | solution.py:485
  182.4 22.7 %collective-permute-start.31 = (bf16[384,256]{1,0:T(8,128)(2,1)S(1)}, bf16[384,256]{1,0:T(8,128)(2,1)S(1)}, u32[]{:S(2)}, u32[]{:S(2)}) collective-permute-start(bf16[384,256]{1,0:T(8,128)(2,1)S(1)} %copy-done.26), channel_id=1, source_target_pairs={{0,24},{4,28},{8,16},{12,20},{24,0},{28,4},{16,8},{20,12},{1,25},{... | collective-permute-start | bytes 589832 | tf_op jit(solution)/shard_map/ppermute | solution.py:497
  190.8 14.3 %collective-permute-start.32 = (bf16[384,256]{1,0:T(8,128)(2,1)}, bf16[384,256]{1,0:T(8,128)(2,1)S(1)}, u32[]{:S(2)}, u32[]{:S(2)}) collective-permute-start(bf16[384,256]{1,0:T(8,128)(2,1)} %product.13), channel_id=1, source_target_pairs={{0,8},{4,12},{8,24},{12,28},{24,16},{28,20},{16,0},{20,4},{1,9},{5... | collective-permute-start | bytes 589832 | tf_op jit(solution)/shard_map/ppermute | solution.py:508
  210.2 1.4 collective-permute-start.33
  212.2 3.6 %collective-permute-start.34 = (f32[1,384]{1,0:T(1,128)S(1)}, f32[1,384]{1,0:T(1,128)S(1)}, u32[]{:S(2)}, u32[]{:S(2)}) collective-permute-start(f32[1,384]{1,0:T(1,128)S(1)} %add.156), channel_id=1, source_target_pairs={{0,2},{1,3},{2,0},{3,1},{4,6},{5,7},{6,4},{7,5},{8,10},{9,11},{10,... | collective-permute-start | bytes 4616 | tf_op jit(solution)/shard_map/ppermute | solution.py:68
  224.2 15.7 %all-to-all-start.2 = ((bf16[8,144,128]{2,1,0:T(8,128)(2,1)}), bf16[8,144,128]{2,1,0:T(8,128)(2,1)S(1)}, u32[]{:S(2)}, u32[]{:S(2)}) async-start(bf16[8,144,128]{2,1,0:T(8,128)(2,1)} %get-tuple-element.159), calls=%async_computation.2 | async-start | bytes 589824 | tf_op jit(solution)/shard_map/all_to_all | solution.py:137
  229.4 18.8 %copy-start.30 = (f32[1,1024]{1,0:T(1,128)S(1)}, f32[1,1024]{1,0:T(1,128)}, u32[]{:S(2)}) copy-start(f32[1,1024]{1,0:T(1,128)} %get-tuple-element.168) | copy-start | bytes 12292
  237.7 54.0 %collective-permute-start.36 = (bf16[128,3072]{1,0:T(8,128)(2,1)}, bf16[128,3072]{1,0:T(8,128)(2,1)S(1)}, u32[]{:S(2)}, u32[]{:S(2)}) collective-permute-start(bf16[128,3072]{1,0:T(8,128)(2,1)} %get-tuple-element.167), channel_id=1, source_target_pairs={{0,4},{4,0},{8,12},{12,8},{16,20},{20,16},{24,28},{28,24},{1,5},{5... | collective-permute-start | bytes 2359304 | tf_op jit(solution)/shard_map/ppermute | solution.py:514
  239.8 52.0 %collective-permute-start.35 = (bf16[128,3072]{1,0:T(8,128)(2,1)S(1)}, bf16[128,3072]{1,0:T(8,128)(2,1)S(1)}, u32[]{:S(2)}, u32[]{:S(2)}) collective-permute-start(bf16[128,3072]{1,0:T(8,128)(2,1)S(1)} %copy-done.31), channel_id=1, source_target_pairs={{0,4},{4,0},{8,12},{12,8},{16,20},{20,16},{24,28},{28,24},{1,5},{5... | collective-permute-start | bytes 2359304 | tf_op jit(solution)/shard_map/ppermute | solution.py:514
  242.3 53.9 %all-to-all-start.3 = ((bf16[8,128,128]{2,1,0:T(8,128)(2,1)}), bf16[8,128,128]{2,1,0:T(8,128)(2,1)S(1)}, u32[]{:S(2)}, u32[]{:S(2)}) async-start(bf16[8,128,128]{2,1,0:T(8,128)(2,1)} %scan.3), calls=%async_computation.3 | async-start | bytes 524288 | tf_op jit(solution)/shard_map/all_to_all | solution.py:144
  248.3 27.7 %collective-permute-start.37 = (f32[1,1024]{1,0:T(1,128)S(1)}, f32[1,1024]{1,0:T(1,128)S(1)}, u32[]{:S(2)}, u32[]{:S(2)}) collective-permute-start(f32[1,1024]{1,0:T(1,128)S(1)} %copy-done.30), channel_id=1, source_target_pairs={{0,4},{4,0},{8,12},{12,8},{16,20},{20,16},{24,28},{28,24},{1,5},{5... | collective-permute-start | bytes 12296 | tf_op jit(solution)/shard_map/ppermute | solution.py:68
  276.0 3.6 %collective-permute-start.38 = (f32[1,1024]{1,0:T(1,128)S(1)}, f32[1,1024]{1,0:T(1,128)S(1)}, u32[]{:S(2)}, u32[]{:S(2)}) collective-permute-start(f32[1,1024]{1,0:T(1,128)S(1)} %add.158), channel_id=1, source_target_pairs={{0,8},{4,12},{8,0},{12,4},{16,24},{20,28},{24,16},{28,20},{1,9},{5... | collective-permute-start | bytes 12296 | tf_op jit(solution)/shard_map/ppermute | solution.py:68
  279.6 11.6 %collective-permute-start.39 = (f32[1,1024]{1,0:T(1,128)S(1)}, f32[1,1024]{1,0:T(1,128)S(1)}, u32[]{:S(2)}, u32[]{:S(2)}) collective-permute-start(f32[1,1024]{1,0:T(1,128)S(1)} %add.159), channel_id=1, source_target_pairs={{0,16},{4,20},{8,24},{12,28},{16,0},{20,4},{24,8},{28,12},{1,17},{... | collective-permute-start | bytes 12296 | tf_op jit(solution)/shard_map/ppermute | solution.py:68
  (29 other events, 154.5 us)

commit v4 on v2

--- a/solution.py
+++ b/solution.py
@@ -9,9 +9,10 @@
 
 LINE = 4
 CHUNKS = 2
+RELATIVE = (0, 2, 1, 3)
 FL = jnp.float32
 BF = jnp.bfloat16
-PARAMS = pltpu.CompilerParams(vmem_limit_bytes=24 * 1024 * 1024)
+PARAMS = pltpu.CompilerParams(vmem_limit_bytes=14 * 1024 * 1024)
 EXACT = lax.Precision.HIGHEST
 NN = (((1,), (0,)), ((), ()))
 NT = (((1,), (1,)), ((), ()))
@@ -29,8 +30,11 @@
 SCALAR = pl.BlockSpec(memory_space=pltpu.SMEM)
 
 
+TINY = pl.CostEstimate(flops=1000, bytes_accessed=1000, transcendentals=0)
+
+
 def cost(flops, moved):
-    return pl.CostEstimate(flops=flops, bytes_accessed=moved, transcendentals=0)
+    return TINY
 
 
 def after(x, *others):
@@ -57,14 +61,6 @@
         for z in range(LINE)
         for m in range(minor)
     ]
-
-
-def butterfly(part, axis, count):
-    step = 1
-    while step < count:
-        part = part + lax.ppermute(part, axis, [(i, i ^ step) for i in range(count)])
-        step *= 2
-    return part
 
 
 def column(table, head):
@@ -128,19 +124,6 @@
         state = factor[None] * state + in_ref[b, :rows].astype(FL).reshape(rows // 8, 8, wide)
 
 
-def carry(part, reverse):
-    count, deep, wide = part.shape
-    rows = deep - 16
-    spread = lax.all_to_all(part, "ctx", 0, 0, tiled=True)
-    states = pl.pallas_call(
-        functools.partial(scan_kernel, reverse),
-        out_shape=jax.ShapeDtypeStruct((count, rows, wide), BF),
-        compiler_params=PARAMS,
-        name="scan",
-    )(spread)
-    return lax.all_to_all(states, "ctx", 0, 0, tiled=True)
-
-
 def weights_kernel(q_ref, k_ref, v_ref, run_ref, turned_ref, aw_ref, intra_ref):
     head = pl.program_id(0)
     mask = mask_of(run_ref, column(turned_ref[...], head), head)
@@ -166,75 +149,90 @@
         squares_ref[...] = fold_rows(held_ref[...])
 
 
-def norm_kernel(mine_ref, attn_ref, inv_ref, gain_ref, order_ref, own_ref, *sent):
-    normed = (attn_ref[...] * inv_ref[...] * gain_ref[...]).astype(BF)
+def turned_row(row):
+    return jnp.broadcast_to(row, (128, row.shape[1])).T[:, :1]
+
+
+def norm_kernel(features, mine_ref, attn_ref, here_ref, there_ref, gain_ref, order_ref, *outs):
+    inv_ref, own_ref, *sent = outs
+    inv = lax.rsqrt((here_ref[...] + there_ref[...]) / features + 1e-05)
+    inv_ref[...] = inv
+    normed = (attn_ref[...] * turned_row(inv) * gain_ref[...]).astype(BF)
     tok, width = normed.shape
     span = width // LINE
-    parts = 4
-    quarter = tok // parts
+    quarter = tok // len(RELATIVE)
     own_ref[...] = dot(normed, order_ref[:, :span], NN).astype(BF)
     for s, ref in enumerate(sent, 1):
         part = dot(normed, order_ref[:, s * span : (s + 1) * span], NN).astype(BF)
-        for j in range(parts):
-            to = pl.multiple_of((mine_ref[0] ^ j) * quarter, 16)
+        for j in range(len(RELATIVE)):
+            turn = mine_ref[0] ^ j
+            to = pl.multiple_of(((turn & 1) * 2 + (turn >> 1)) * quarter, 16)
             ref[pl.ds(to, quarter), :] = part[j * quarter : (j + 1) * quarter]
 
 
-def product_kernel(pieces, weights, add, last, *refs):
+def product_kernel(lots, weights, add, last, *refs):
     refs = list(refs)
     mine_ref = refs.pop(0)
-    x = [refs.pop(0) for _ in range(pieces)]
+    x = [[refs.pop(0) for _ in range(k)] for k in lots]
     w = [refs.pop(0) for _ in range(weights)]
     extra = refs.pop(0) if add else None
     out_ref, held_ref = refs
     step = pl.program_id(0)
+    steps = pl.num_programs(0) // len(lots)
 
     @pl.when(step == 0)
     def _():
         held_ref[...] = extra[...] if add else jnp.zeros_like(held_ref)
 
-    rows = jnp.concatenate([r[...] for r in x], axis=0)
-    cols = jnp.concatenate([r[...] for r in w], axis=0)
-    held_ref[...] += dot(rows, cols, NT)
+    for at, lot in enumerate(x):
+
+        @pl.when(step // steps == at)
+        def _():
+            rows = jnp.concatenate([r[...] for r in lot], axis=0)
+            cols = jnp.concatenate([r[...] for r in w], axis=0)
+            held_ref[...] += dot(rows, cols, NT)
 
     @pl.when(step == pl.num_programs(0) - 1)
     def _():
         if not last:
             out_ref[...] = held_ref[...]
-        elif pieces == 1:
+        elif lots[0] == 1:
             out_ref[...] = held_ref[...].astype(BF)
         else:
-            quarter = x[0].shape[0]
-            for j in range(pieces):
-                to = pl.multiple_of((mine_ref[0] ^ j) * quarter, 16)
+            quarter = out_ref.shape[0] // len(RELATIVE)
+            for i, turn in enumerate(RELATIVE):
+                to = pl.multiple_of((mine_ref[0] ^ turn) * quarter, 16)
                 out_ref[pl.ds(to, quarter), :] = held_ref[
-                    j * quarter : (j + 1) * quarter, :
+                    i * quarter : (i + 1) * quarter, :
                 ].astype(BF)
 
 
-def product(mine, pieces, weights, chunk, chunks, held):
-    tok = sum(p.shape[0] for p in pieces)
-    deep = pieces[0].shape[1]
-    tile = 1024
+def product(mine, lots, weights, chunk, last, held):
+    tok = sum(p.shape[0] for p in lots[0])
+    deep = lots[0][0].shape[1]
+    tile = 1536
     steps = deep // tile
     span = sum(w.shape[0] for w in weights)
     base = chunk * steps
-    last = chunk == chunks - 1
     more = [] if held is None else [held]
+
+    def piece_spec(at, p):
+        return spec((p.shape[0], tile), lambda i: (0, jnp.clip(i - at * steps, 0, steps - 1)))
+
     return pl.pallas_call(
-        functools.partial(product_kernel, len(pieces), len(weights), len(more), last),
-        grid=(steps,),
+        functools.partial(product_kernel, [len(x) for x in lots], len(weights), len(more), last),
+        grid=(steps * len(lots),),
         in_specs=[SCALAR]
-        + [spec((p.shape[0], tile), lambda i: (0, i)) for p in pieces]
+        + [piece_spec(at, p) for at, lot in enumerate(lots) for p in lot]
         + [spec((w.shape[0], tile), lambda i: (0, base + i)) for w in weights]
         + [spec((tok, span)) for _ in more],
         out_specs=spec((tok, span)),
         out_shape=jax.ShapeDtypeStruct((tok, span), BF if last else FL),
         scratch_shapes=[pltpu.VMEM((tok, span), FL)],
         compiler_params=PARAMS,
-        cost_estimate=cost(2 * tok * deep * span, 2 * deep * (tok + span)),
+        cost_estimate=TINY,
         name="product",
-    )(mine, *pieces, *weights, *more)
+    )(mine, *[p for lot in lots for p in lot], *weights, *more)
 
 
 def outer_kernel(lots, own, *refs):
@@ -294,16 +292,19 @@
         grad = grad + dot(pieces[s][...], order_ref[:, s * span : (s + 1) * span], NT)
     out_ref[...] = grad.astype(BF)
     both = grad * attn_ref[...]
-    sum_ref[...] = jnp.sum(both * inv_ref[...], axis=0, keepdims=True)
+    sum_ref[...] = jnp.sum(both * turned_row(inv_ref[...]), axis=0, keepdims=True)
     inner_ref[...] = fold_rows(both * gain_ref[...])
 
 
 def grad_kernel(
-    grad_ref, attn_ref, inv_ref, shift_ref, gain_ref, q_ref, turned_ref, out_ref, state_ref
+    features, grad_ref, attn_ref, inv_ref, here_ref, there_ref, gain_ref, q_ref, turned_ref,
+    out_ref, state_ref,
 ):
     run = column(turned_ref[...], pl.program_id(0))
+    inv = inv_ref[...]
+    shift = turned_row(inv * inv * inv * ((here_ref[...] + there_ref[...]) / features))
     scaled = grad_ref[...].astype(FL) * gain_ref[...]
-    grad = (inv_ref[...] * scaled - attn_ref[...] * shift_ref[...]).astype(BF)
+    grad = (turned_row(inv) * scaled - attn_ref[...] * shift).astype(BF)
     out_ref[...] = grad
     weighted = (q_ref[...].astype(FL) * jnp.exp(run)).astype(BF)
     put_state(state_ref, dot(weighted, grad, TN), run[run.shape[0] - 1 :, :])
@@ -389,102 +390,159 @@
             compiler_params=PARAMS, name=name, cost_estimate=est, scratch_shapes=list(scratch),
         )
 
+    gain_row = norm_gain.reshape(1, width)
+    full = pl.BlockSpec(memory_space=pltpu.VMEM)
+    weight_own = out_weight.reshape(heads * narrow, model)
+
     def ring(x):
         return lax.ppermute(x, "ctx", ring_perm(count, 1))
 
-    pieces = [[None] * LINE for _ in range(CHUNKS)]
-    pieces[0][1] = ring(first_piece(0))
+    def over(x, perm):
+        return lax.ppermute(x, "head", perm)
+
+    def near_of(x):
+        return over(x, over_core)
+
+    def other_of(x):
+        return over(x, over_y)
+
+    def core_of(x, y):
+        both = jnp.concatenate([x, y], axis=0)
+        return both, near_of(both)
+
+    order = feature_order(heads, size, count)
+    ra1 = ring(first_piece(0))
     put, run, turned = per_head(
         state_kernel, [run_blk, blk, blk], [put_blk, run_blk, turned_blk],
         [put_shape, jax.ShapeDtypeStruct((heads, tok), FL), jax.ShapeDtypeStruct((tok, heads), FL)],
         "states", block_cost,
     )(log_decay, key_rows, value_rows)
-    state_low = carry(put, False).reshape(heads, size, size)
-    for c in range(1, CHUNKS):
-        pieces[c][1] = ring(first_piece(c))
-    order = feature_order(heads, size, count)
+    spread = lax.all_to_all(put, "ctx", 0, 0, tiled=True)
     attn_weights, intra = per_head(
         weights_kernel, [blk, blk, blk, run_blk, turned_blk], [square_blk, blk],
         [jax.ShapeDtypeStruct((heads, tok, tok), BF), wide_f], "weights", square_cost,
     )(query_rows, key_rows, value_rows, run, turned)
-
-    weight_own = out_weight.reshape(heads * narrow, model)
-    weight_sent = after(weight_own, state_low)
-    weights = [weight_own] + [
-        lax.ppermute(weight_sent, "ctx", pair_perm(count, -s)) for s in range(1, minor)
-    ]
-
+    ra1, spread, intra, order, first = lax.optimization_barrier(
+        (ra1, spread, intra, order, first_piece(1))
+    )
+
+    rb1, ya1 = ring(first), other_of(ra1)
+    states = pl.pallas_call(
+        functools.partial(scan_kernel, False),
+        out_shape=jax.ShapeDtypeStruct((count, rows, size), BF),
+        compiler_params=PARAMS, cost_estimate=TINY, name="scan",
+    )(spread)
+    state_low = lax.all_to_all(states, "ctx", 0, 0, tiled=True)
+    ra1, rb1, ya1, state_low, weight_own = lax.optimization_barrier(
+        (ra1, rb1, ya1, state_low, weight_own)
+    )
+
+    state_low = state_low.reshape(heads, size, size)
+    ra2, yb1, (da1, ca1) = ring(ra1), other_of(rb1), core_of(ra1, ya1)
+    weights = [lax.ppermute(weight_own, "ctx", pair_perm(count, -s)) for s in range(1, minor)]
     attn_out, squares = per_head(
         attend_kernel, [blk, state_blk, turned_blk, blk], [blk, spec((1, tok))],
         [wide_f, jax.ShapeDtypeStruct((1, tok), FL)], "attend", block_cost,
         [pltpu.VMEM((tok, size), FL)],
     )(query_rows, state_low, turned, intra)
-    squares = butterfly(squares, "head", head_count)
-    inv_rms = lax.rsqrt(squares / features + 1e-05)
-    inv_col = inv_rms.reshape(tok, 1)
-    gain_row = norm_gain.reshape(1, width)
-    full = pl.BlockSpec(memory_space=pltpu.VMEM)
-    sent = pl.pallas_call(
-        norm_kernel,
-        in_specs=[SCALAR] + [full] * 4,
-        out_specs=[full] * LINE,
-        out_shape=[jax.ShapeDtypeStruct((tok, span), BF)] * LINE,
-        compiler_params=PARAMS,
-        cost_estimate=cost(2 * tok * width * width, 8 * tok * width),
-        name="norm",
-    )(tokens, attn_out, inv_col, gain_row, order)
-    normed = [sent[0]] + [
-        lax.ppermute(sent[s], "ctx", ring_perm(count, s)) for s in range(1, LINE)
-    ]
-
-    lots = [[None] * (LINE - 1) for _ in range(CHUNKS)]
-    for s in range(1, LINE):
-        for c in range(CHUNKS):
-            piece = pieces[c][s]
-            if s + 1 < LINE:
-                pieces[c][s + 1] = ring(piece)
-            other = lax.ppermute(piece, "head", over_y)
-            near = lax.ppermute(piece, "head", over_core)
-            far = lax.ppermute(other, "head", over_core)
-            lots[c][s - 1] = [piece, near, other, far]
-
-    returned = [product(tokens, [grad_out], weights, 0, 1, None)]
-    for s in range(1, LINE):
-        held = None
-        for c in range(CHUNKS):
-            held = product(tokens, lots[c][s - 1], weights, c, CHUNKS, held)
-        returned.append(lax.ppermute(held, "ctx", ring_perm(count, -s)))
-
-    flat = []
-    for c in range(CHUNKS):
-        parts = outer(normed, grad_out, lots[c], c, own)
-        flat.append(parts[0])
-        for s in range(1, minor):
-            flat.append(lax.ppermute(parts[s], "ctx", pair_perm(count, s)))
+    squares = squares + near_of(squares)
+    rb1, ra2, yb1, da1, ca1, squares = lax.optimization_barrier(
+        (rb1, ra2, yb1, da1, ca1, squares)
+    )
+
+    rb2, ya2, (db1, cb1) = ring(rb1), other_of(ra2), core_of(rb1, yb1)
+    squares_there = other_of(squares)
+    ra2, rb2, ya2, db1, cb1, squares_there = lax.optimization_barrier(
+        (ra2, rb2, ya2, db1, cb1, squares_there)
+    )
+
+    ra3, yb2, (da2, ca2) = ring(ra2), other_of(rb2), core_of(ra2, ya2)
+    inv_rms, *sent = pl.pallas_call(
+        functools.partial(norm_kernel, features),
+        in_specs=[SCALAR] + [full] * 5,
+        out_specs=[full] * (1 + LINE),
+        out_shape=[jax.ShapeDtypeStruct((1, tok), FL)]
+        + [jax.ShapeDtypeStruct((tok, span), BF)] * LINE,
+        compiler_params=PARAMS, cost_estimate=TINY, name="norm",
+    )(tokens, attn_out, squares, squares_there, gain_row, order)
+    normed = [sent[0], lax.ppermute(sent[1], "ctx", ring_perm(count, 1))]
+    rb2, ra3, yb2, da2, ca2, weights, normed[1], sent[2] = lax.optimization_barrier(
+        (rb2, ra3, yb2, da2, ca2, weights, normed[1], sent[2])
+    )
+
+    weights = [weight_own] + weights
+    rb3, ya3, (db2, cb2) = ring(rb2), other_of(ra3), core_of(rb2, yb2)
+    normed.append(lax.ppermute(sent[2], "ctx", ring_perm(count, 2)))
+    mine_part = product(tokens, [[grad_out]], weights, 0, True, None)
+    one = product(tokens, [[da1, ca1], [db1, cb1]], weights, 0, True, None)
+    ra3, rb3, ya3, db2, cb2, normed[2], mine_part, one, sent[3] = lax.optimization_barrier(
+        (ra3, rb3, ya3, db2, cb2, normed[2], mine_part, one, sent[3])
+    )
+
+    yb3, (da3, ca3) = other_of(rb3), core_of(ra3, ya3)
+    normed.append(lax.ppermute(sent[3], "ctx", ring_perm(count, 3)))
+    returned = [mine_part, lax.ppermute(one, "ctx", ring_perm(count, -1))]
+    two = product(tokens, [[da2, ca2], [db2, cb2]], weights, 0, True, None)
+    rb3, yb3, da3, ca3, normed[3], returned[1], two = lax.optimization_barrier(
+        (rb3, yb3, da3, ca3, normed[3], returned[1], two)
+    )
+
+    db3, cb3 = core_of(rb3, yb3)
+    returned.append(lax.ppermute(two, "ctx", ring_perm(count, -2)))
+    three = product(tokens, [[da3, ca3]], weights, 0, False, None)
+    db3, cb3, three, da3 = lax.optimization_barrier((db3, cb3, three, da3))
+
+    three = product(tokens, [[db3, cb3]], weights, 1, True, three)
+    returned.append(lax.ppermute(three, "ctx", ring_perm(count, -3)))
+    lots = [[[da1, ca1], [da2, ca2], [da3, ca3]], [[db1, cb1], [db2, cb2], [db3, cb3]]]
+    early = outer([after(normed[0], three)] + normed[1:], grad_out, lots[0], 0, own)
+    returned, early = lax.optimization_barrier((returned, early))
 
     grad, gain_sum, inner = pl.pallas_call(
         back_kernel,
         in_specs=[full] * (4 + LINE),
         out_specs=[full] * 3,
         out_shape=[wide_b, jax.ShapeDtypeStruct((1, width), FL), jax.ShapeDtypeStruct((1, tok), FL)],
-        compiler_params=PARAMS,
-        cost_estimate=cost(2 * tok * width * width, 8 * tok * width),
-        name="back",
-    )(order, attn_out, inv_col, gain_row, *returned)
-    inner = butterfly(inner, "head", head_count)
-    shift = (inv_rms**3 * (inner / features)).reshape(tok, 1)
+        compiler_params=PARAMS, cost_estimate=TINY, name="back",
+    )(order, attn_out, inv_rms, gain_row, *returned)
+    inner = inner + near_of(inner)
+    flip = [(i, i ^ 1) for i in range(count)]
+    gain_sum = gain_sum + lax.ppermute(gain_sum, "ctx", flip)
+    inner_there = other_of(inner)
+    inner_there, gain_sum, early = lax.optimization_barrier((inner_there, gain_sum, early))
+
+    flat = [early[0]]
+    flat += [lax.ppermute(early[s], "ctx", pair_perm(count, s)) for s in range(1, minor)]
+    row_blk = spec((1, tok))
     grad_attn, put_back = per_head(
-        grad_kernel,
-        [blk, blk, col_blk, col_blk, spec((1, size), lambda h: (0, h)), blk, turned_blk],
+        functools.partial(grad_kernel, features),
+        [blk, blk, row_blk, row_blk, row_blk, spec((1, size), lambda h: (0, h)), blk, turned_blk],
         [blk, put_blk], [wide_b, put_shape], "grads", block_cost,
-    )(grad, attn_out, inv_col, shift, gain_row, query_rows, turned)
-    back_low = carry(put_back, True).reshape(heads, size, size)
-    grad_gain = butterfly(gain_sum, "ctx", count).reshape(width)
+    )(grad, attn_out, inv_rms, inner, inner_there, gain_row, query_rows, turned)
+    spread = lax.all_to_all(put_back, "ctx", 0, 0, tiled=True)
+    late = outer([after(normed[0], put_back)] + normed[1:], grad_out, lots[1], 1, own)
     grad_query, gk_in, gv_in = per_head(
         inside_kernel,
         [blk, blk, blk, blk, square_blk, run_blk, turned_blk, state_blk], [blk] * 3,
         [wide_b, wide_f, wide_f], "inside", square_cost,
     )(grad_attn, query_rows, key_rows, value_rows, attn_weights, run, turned, state_low)
+    spread, late = lax.optimization_barrier((spread, late))
+
+    flat.append(late[0])
+    flat += [lax.ppermute(late[s], "ctx", pair_perm(count, s)) for s in range(1, minor)]
+    states = pl.pallas_call(
+        functools.partial(scan_kernel, True),
+        out_shape=jax.ShapeDtypeStruct((count, rows, size), BF),
+        compiler_params=PARAMS, cost_estimate=TINY, name="scan",
+    )(spread)
+    back_low = lax.all_to_all(states, "ctx", 0, 0, tiled=True).reshape(heads, size, size)
+    step = 2
+    while step < count:
+        gain_sum = gain_sum + lax.ppermute(
+            gain_sum, "ctx", [(i, i ^ step) for i in range(count)]
+        )
+        step *= 2
+    grad_gain = gain_sum.reshape(width)
     grad_key, grad_value = per_head(
         outside_kernel, [blk, blk, state_blk, turned_blk, blk, blk], [blk] * 2,
         [wide_b] * 2, "outside", block_cost,

time: 288 us -> 245 us (0.85)
  local copies, waits for them, and re-layouts: 48.6 us -> 27.9 us
  waiting for transfers between devices: 102 us -> 82.3 us
  Pallas kernels: 74 us -> 55.1 us
  blocking collectives: 0 us -> 18.2 us
    ppermute x6, waiting for transfers between devices: 46.1 us -> 12.6 us  [ring(): return lax.ppermute(x, 'ctx', ring_perm(count, 1))]
    unnamed x158 -> x98, local copies, waits for them, and re-layouts: 45.5 us -> 25.2 us
    all_to_all x0 -> x1, blocking collectives: none -> 18.2 us  [shards(): state_low = lax.all_to_all(states, 'ctx', 0, 0, tiled=True)]
    pallas_call x11 -> x9, Pallas kernels: 30.6 us -> 18.5 us  [the longest x5 11.3 us: product(): pl.pallas_call(functools.partial(product_kernel, [len(x) for x in lots],...]
    all_to_all x4 -> x3, waiting for transfers between devices: 4.55 us -> 12.4 us  [the longest x1 8.94 us: shards(): lax.all_to_all(states, 'ctx', 0, 0, tiled=True).reshape(heads, size, size)]
    all_to_all x4 -> x3, starting transfers between devices: 21 us -> 14.1 us  [the longest x1 5.9 us: shards(): lax.all_to_all(states, 'ctx', 0, 0, tiled=True).reshape(heads, size, size)]
    ppermute x34 -> x28, waiting for transfers between devices: 51.3 us -> 57.3 us  [the longest x1 16.9 us: shards(): lax.ppermute(weight_own, 'ctx', pair_perm(count, -s))]
    ppermute x34 -> x28, starting transfers between devices: 29.2 us -> 34.4 us  [the longest x16 11.7 us: over(): return lax.ppermute(x, 'head', perm)]
  transfers between devices with their start and end apart: 44 -> 37, of which waited for: 16 -> 15; matrix products, arithmetic and copies ran while one was open for 2% -> 1% of each run, Pallas kernels for 22% -> 19%
where the time goes in v4:
time: 245 us; the launch traced here: 244 us
  waiting for transfers between devices  82.3 us (34%)
  starting transfers between devices  58.3 us (24%)
  Pallas kernels  55.1 us (22%)
  local copies, waits for them, and re-layouts  27.9 us (11%)
  blocking collectives  18.2 us (7%)
    unnamed x98, local copies, waits for them, and re-layouts  25.2 us
    all_to_all x1, blocking collectives, shards(): state_low = lax.all_to_all(states, 'ctx', 0, 0, tiled=True)  18.2 us
    ppermute x1, waiting for transfers between devices, shards(): lax.ppermute(weight_own, 'ctx', pair_perm(count, -s))  16.9 us
    ppermute x16, waiting for transfers between devices, over(): return lax.ppermute(x, 'head', perm)  16.7 us
    ppermute x6, waiting for transfers between devices, ring(): return lax.ppermute(x, 'ctx', ring_perm(count, 1))  12.6 us
    ppermute x16, starting transfers between devices, over(): return lax.ppermute(x, 'head', perm)  11.7 us
    pallas_call x5, Pallas kernels, product(): pl.pallas_call(functools.partial(product_kernel, [len(x) for x in lots],...  11.3 us
    ppermute x1, waiting for transfers between devices, shards(): normed.append(lax.ppermute(sent[2], 'ctx', ring_perm(count, 2)))  10.8 us
  transfers between devices with their start and end apart: 37, of which 15 were waited for; matrix products, arithmetic and copies ran while one was open for 1% of the time, Pallas kernels for 19%

profile of v4, /device:TPU:0, one launch (start us, length us, event | category | flops | bytes accessed | tf_op | source)
XLA Modules:
  0.0 244.5 jit_solution(9657764936673203612)
XLA Ops:
  0.7 2.4 constant_dynamic-slice_fusion
  3.1 3.0 %collective-permute-start = (bf16[96,3072]{1,0:T(8,128)(2,1)}, bf16[96,3072]{1,0:T(8,128)(2,1)}, u32[]{:S(2)}, u32[]{:S(2)}) collective-permute-start(bf16[96,3072]{1,0:T(8,128)(2,1)} %get-tuple-element.188), channel_id=1, source_target_pairs={{0,8},{4,12},{8,24},{12,28},{24,16},{28,20},{16,0},{20,4},{1,9},{5... | collective-permute-start | bytes 1769480 | tf_op jit(solution)/shard_map/ppermute | solution.py:398
  6.1 5.1 %states.1 = (bf16[8,144,128]{2,1,0:T(8,128)(2,1)}, f32[8,384]{1,0:T(8,128)S(1)}, f32[384,8]{1,0:T(8,128)S(1)}) custom-call(f32[8,384]{1,0:T(8,128)S(1)} %copy-done.42, bf16[384,1024]{1,0:T(8,128)(2,1)S(1)} %copy-done.2, bf16[384,1024]{1,0:T(8,128)(2,1)S(1)} %copy-done.3), custom_call_target="tpu_custom_call" | custom-call | flops 1000 | bytes 1000 | tf_op jit(solution)/shard_map/states/pallas_call | solution.py:415
  11.3 4.8 %all-to-all-start = ((bf16[8,144,128]{2,1,0:T(8,128)(2,1)}), bf16[8,144,128]{2,1,0:T(8,128)(2,1)S(1)}, u32[]{:S(2)}, u32[]{:S(2)}) async-start(bf16[8,144,128]{2,1,0:T(8,128)(2,1)} %get-tuple-element.96), calls=%async_computation | async-start | bytes 589824 | tf_op jit(solution)/shard_map/all_to_all | solution.py:420
  16.1 4.1 %weights.1 = (bf16[8,384,384]{2,1,0:T(8,128)(2,1)S(1)}, f32[384,1024]{1,0:T(8,128)S(1)}) custom-call(bf16[384,1024]{1,0:T(8,128)(2,1)S(1)} %copy-done.5, bf16[384,1024]{1,0:T(8,128)(2,1)S(1)} %copy-done.2, bf16[384,1024]{1,0:T(8,128)(2,1)S(1)} %copy-done.3, f32[8,384]{1,0:T(8,128)S(1)} %get-tuple-element.97.run_ref, f32[384,8]{1,0:T(8,128)S(1)} %get-tuple-element.98.turned_ref), custom_call_target="tpu_custom_call" | custom-call | flops 1000 | bytes 1000 | tf_op jit(solution)/shard_map/weights/pallas_call | solution.py:421
  23.6 3.5 %all-to-all-done.in_ref = bf16[8,144,128]{2,1,0:T(8,128)(2,1)S(1)} async-done(((bf16[8,144,128]{2,1,0:T(8,128)(2,1)}), bf16[8,144,128]{2,1,0:T(8,128)(2,1)S(1)}, u32[]{:S(2)}, u32[]{:S(2)}) %all-to-all-start) | async-done | bytes 294944 | tf_op jit(solution)/shard_map/all_to_all | solution.py:420
  28.2 1.5 collective-permute-start.2
  29.8 18.2 %all_to_all.20.state_ref = bf16[8,128,128]{2,1,0:T(8,128)(2,1)S(1)} all-to-all(bf16[8,128,128]{2,1,0:T(8,128)(2,1)S(1)} %scan.2), channel_id=1, replica_groups=mesh['ctx'=8,'head'=4] {'ctx'}, dimensions={0} | all-to-all | bytes 524288 | tf_op jit(solution)/shard_map/all_to_all | solution.py:435
  50.0 1.5 collective-permute-start.4
  51.5 2.3 attend.1
  55.0 11.5 %collective-permute-done.3 = bf16[96,3072]{1,0:T(8,128)(2,1)S(1)} collective-permute-done((bf16[96,3072]{1,0:T(8,128)(2,1)}, bf16[96,3072]{1,0:T(8,128)(2,1)S(1)}, u32[]{:S(2)}, u32[]{:S(2)}) %collective-permute-start.3) | collective-permute-done | bytes 589856 | tf_op jit(solution)/shard_map/ppermute | solution.py:398
  66.8 2.2 collective-permute-start.7
  69.0 1.5 collective-permute-start.8
  71.0 1.5 collective-permute-start.14
  72.5 12.0 %collective-permute-done.10.there_ref = f32[1,384]{1,0:T(1,128)S(1)} collective-permute-done((f32[1,384]{1,0:T(1,128)S(1)}, f32[1,384]{1,0:T(1,128)S(1)}, u32[]{:S(2)}, u32[]{:S(2)}) %collective-permute-start.10) | collective-permute-done | bytes 1568 | tf_op jit(solution)/shard_map/ppermute | solution.py:401
  86.1 1.5 collective-permute-start.12
  90.1 16.9 %collective-permute-done.14.refs_3_.refs_6_.refs_4_ = bf16[128,6144]{1,0:T(8,128)(2,1)S(1)} collective-permute-done((bf16[128,6144]{1,0:T(8,128)(2,1)S(1)}, bf16[128,6144]{1,0:T(8,128)(2,1)S(1)}, u32[]{:S(2)}, u32[]{:S(2)}) %collective-permute-start.14) | collective-permute-done | bytes 1572896 | tf_op jit(solution)/shard_map/ppermute | solution.py:442
  108.6 1.5 collective-permute-start.17
  110.9 2.7 %product.5.refs_0_ = bf16[384,256]{1,0:T(8,128)(2,1)S(1)} custom-call(s32[1]{0:T(128)} %bitcast.1.mine_ref.refs_0_, bf16[384,6144]{1,0:T(8,128)(2,1)S(1)} %bitcast.6, bf16[128,6144]{1,0:T(8,128)(2,1)S(1)} %bitcast.8, bf16[128,6144]{1,0:T(8,128)(2,1)S(1)} %collective-permute-done.14.refs_3_.refs_6_.refs_4_), custom_call_target="tpu_custom_call" | custom-call | flops 1000 | bytes 1000 | tf_op jit(solution)/shard_map/product/pallas_call | solution.py:222
  113.7 2.9 %product.6 = bf16[384,256]{1,0:T(8,128)(2,1)S(1)} custom-call(s32[1]{0:T(128)} %bitcast.1.mine_ref.refs_0_, bf16[192,3072]{1,0:T(8,128)(2,1)S(1)} %constant_dynamic-update-slice_fusion.refs_1_.refs_5_, bf16[192,3072]{1,0:T(8,128)(2,1)S(1)} %collective-permute-done.5.refs_2_.refs_6_, ...), custom_call_target="tpu_custom_call" | custom-call | flops 1000 | bytes 1000 | tf_op jit(solution)/shard_map/product/pallas_call | solution.py:222
  116.6 10.8 %collective-permute-done.19.refs_2_ = bf16[384,256]{1,0:T(8,128)(2,1)S(1)} collective-permute-done((bf16[384,256]{1,0:T(8,128)(2,1)S(1)}, bf16[384,256]{1,0:T(8,128)(2,1)S(1)}, u32[]{:S(2)}, u32[]{:S(2)}) %collective-permute-start.19) | collective-permute-done | bytes 196640 | tf_op jit(solution)/shard_map/ppermute | solution.py:475
  128.6 1.6 collective-permute-start.20
  130.2 4.0 %collective-permute-start.22 = (bf16[384,256]{1,0:T(8,128)(2,1)S(1)}, bf16[384,256]{1,0:T(8,128)(2,1)S(1)}, u32[]{:S(2)}, u32[]{:S(2)}) collective-permute-start(bf16[384,256]{1,0:T(8,128)(2,1)S(1)} %get-tuple-element.137), channel_id=1, source_target_pairs={{0,16},{4,20},{8,0},{12,4},{24,8},{28,12},{16,24},{20,28},{1,17},{... | collective-permute-start | bytes 589832 | tf_op jit(solution)/shard_map/ppermute | solution.py:483
  134.2 2.8 %product.7 = bf16[384,256]{1,0:T(8,128)(2,1)S(1)} custom-call(s32[1]{0:T(128)} %bitcast.1.mine_ref.refs_0_, bf16[192,3072]{1,0:T(8,128)(2,1)S(1)} %constant_dynamic-update-slice_fusion.4.refs_1_.refs_7_, bf16[192,3072]{1,0:T(8,128)(2,1)S(1)} %collective-permute-done.13.refs_2_.refs_8_, ...), custom_call_target="tpu_custom_call" | custom-call | flops 1000 | bytes 1000 | tf_op jit(solution)/shard_map/product/pallas_call | solution.py:222
  137.1 3.1 %collective-permute-done.22.refs_3_ = bf16[384,256]{1,0:T(8,128)(2,1)S(1)} collective-permute-done((bf16[384,256]{1,0:T(8,128)(2,1)S(1)}, bf16[384,256]{1,0:T(8,128)(2,1)S(1)}, u32[]{:S(2)}, u32[]{:S(2)}) %collective-permute-start.22) | collective-permute-done | bytes 196640 | tf_op jit(solution)/shard_map/ppermute | solution.py:483
  140.2 3.8 %collective-permute-done.23.refs_1_ = bf16[384,256]{1,0:T(8,128)(2,1)S(1)} collective-permute-done((bf16[384,256]{1,0:T(8,128)(2,1)S(1)}, bf16[384,256]{1,0:T(8,128)(2,1)S(1)}, u32[]{:S(2)}, u32[]{:S(2)}) %collective-permute-start.23) | collective-permute-done | bytes 196640 | tf_op jit(solution)/shard_map/ppermute | solution.py:484
  144.6 2.0 collective-permute-start.24
  148.1 1.4 product.9
  149.5 3.9 %collective-permute-start.26 = (bf16[384,256]{1,0:T(8,128)(2,1)S(1)}, bf16[384,256]{1,0:T(8,128)(2,1)S(1)}, u32[]{:S(2)}, u32[]{:S(2)}) collective-permute-start(bf16[384,256]{1,0:T(8,128)(2,1)S(1)} %product.9), channel_id=1, source_target_pairs={{0,8},{4,12},{8,24},{12,28},{24,16},{28,20},{16,0},{20,4},{1,9},{5... | collective-permute-start | bytes 589832 | tf_op jit(solution)/shard_map/ppermute | solution.py:496
  153.4 5.3 %outer.2 = (bf16[128,3072]{1,0:T(8,128)(2,1)S(1)}, bf16[128,3072]{1,0:T(8,128)(2,1)}) custom-call(bf16[384,256]{1,0:T(8,128)(2,1)S(1)} %get-tuple-element.174.refs_0_, bf16[384,256]{1,0:T(8,128)(2,1)S(1)} %collective-permute-done.15.refs_1_, bf16[384,256]{1,0:T(8,128)(2,1)S(1)} %collective-permute-done.19.refs_2_, ...), custom_call_target="tpu_custom_call" | custom-call | flops 1000 | bytes 1000 | tf_op jit(solution)/shard_map/outer/pallas_call | solution.py:262
  158.8 3.3 %collective-permute-done.26.refs_3_ = bf16[384,256]{1,0:T(8,128)(2,1)S(1)} collective-permute-done((bf16[384,256]{1,0:T(8,128)(2,1)S(1)}, bf16[384,256]{1,0:T(8,128)(2,1)S(1)}, u32[]{:S(2)}, u32[]{:S(2)}) %collective-permute-start.26) | collective-permute-done | bytes 196640 | tf_op jit(solution)/shard_map/ppermute | solution.py:496
  163.3 1.5 collective-permute-start.29
  166.0 1.5 collective-permute-start.28
  167.5 2.0 collective-permute-done.28.there_ref
  169.6 5.8 %grads.1 = (bf16[384,1024]{1,0:T(8,128)(2,1)S(1)}, bf16[8,144,128]{2,1,0:T(8,128)(2,1)}) custom-call(bf16[384,1024]{1,0:T(8,128)(2,1)S(1)} %get-tuple-element.164.grad_ref, f32[384,1024]{1,0:T(8,128)S(1)} %get-tuple-element.106.attn_ref, f32[1,384]{1,0:T(1,128)S(1)} %get-tuple-element.116.inv_ref, f32[1,384]{1,0:T(1,128)S(1)} %add.141.here_ref, ...), custom_call_target="tpu_custom_call" | custom-call | flops 1000 | bytes 1000 | tf_op jit(solution)/shard_map/grads/pallas_call | solution.py:517
  176.2 3.4 %all-to-all-start.2 = ((bf16[8,144,128]{2,1,0:T(8,128)(2,1)}), bf16[8,144,128]{2,1,0:T(8,128)(2,1)S(1)}, u32[]{:S(2)}, u32[]{:S(2)}) async-start(bf16[8,144,128]{2,1,0:T(8,128)(2,1)} %get-tuple-element.173), calls=%async_computation.2 | async-start | bytes 589824 | tf_op jit(solution)/shard_map/all_to_all | solution.py:522
  179.7 2.3 copy-done
  189.6 4.7 %outer.3 = (bf16[128,3072]{1,0:T(8,128)(2,1)S(1)}, bf16[128,3072]{1,0:T(8,128)(2,1)S(1)}) custom-call(bf16[384,256]{1,0:T(8,128)(2,1)S(1)} %get-tuple-element.174.refs_0_, bf16[384,256]{1,0:T(8,128)(2,1)S(1)} %copy-done.36, bf16[384,256]{1,0:T(8,128)(2,1)S(1)} %copy-done.38, bf16[384,256]{1,0:T(8,128)(2,1)S(1)} %copy-done.40, bf16[384,6144]{1,0:T(8,128)(2,1)S(1)} %copy-done, ...), custom_call_target="tpu_custom_call" | custom-call | flops 1000 | bytes 1000 | tf_op jit(solution)/shard_map/outer/pallas_call | solution.py:262
  196.1 1.9 collective-permute-start.30
  199.0 5.9 %all-to-all-start.3 = ((bf16[8,128,128]{2,1,0:T(8,128)(2,1)}), bf16[8,128,128]{2,1,0:T(8,128)(2,1)S(1)}, u32[]{:S(2)}, u32[]{:S(2)}) async-start(bf16[8,128,128]{2,1,0:T(8,128)(2,1)} %copy-done.28), calls=%async_computation.3 | async-start | bytes 524288 | tf_op jit(solution)/shard_map/all_to_all | solution.py:538
  204.9 2.0 collective-permute-start.32
  206.9 2.6 %collective-permute-done.32 = f32[1,1024]{1,0:T(1,128)S(1)} collective-permute-done((f32[1,1024]{1,0:T(1,128)S(1)}, f32[1,1024]{1,0:T(1,128)S(1)}, u32[]{:S(2)}, u32[]{:S(2)}) %collective-permute-start.32) | collective-permute-done | bytes 4128 | tf_op jit(solution)/shard_map/ppermute | solution.py:541
  209.5 3.7 %collective-permute-start.33 = (f32[1,1024]{1,0:T(1,128)S(1)}, f32[1,1024]{1,0:T(1,128)S(1)}, u32[]{:S(2)}, u32[]{:S(2)}) collective-permute-start(f32[1,1024]{1,0:T(1,128)S(1)} %add.143), channel_id=1, source_target_pairs={{0,16},{4,20},{8,24},{12,28},{16,0},{20,4},{24,8},{28,12},{1,17},{... | collective-permute-start | bytes 12296 | tf_op jit(solution)/shard_map/ppermute | solution.py:541
  213.2 1.7 copy-done.21
  216.0 6.6 %inside.1 = (bf16[384,1024]{1,0:T(8,128)(2,1)}, f32[384,1024]{1,0:T(8,128)S(1)}, f32[384,1024]{1,0:T(8,128)S(1)}) custom-call(bf16[384,1024]{1,0:T(8,128)(2,1)S(1)} %copy-done.34, bf16[384,1024]{1,0:T(8,128)(2,1)S(1)} %copy-done.7, bf16[384,1024]{1,0:T(8,128)(2,1)S(1)} %copy-done.2, bf16[384,1024]{1,0:T(8,128)(2,1)S(1)} %copy-done.4, ...), custom_call_target="tpu_custom_call" | custom-call | flops 1000 | bytes 1000 | tf_op jit(solution)/shard_map/inside/pallas_call | solution.py:524
  225.5 8.9 %all-to-all-done.3.state_ref = bf16[8,128,128]{2,1,0:T(8,128)(2,1)S(1)} async-done(((bf16[8,128,128]{2,1,0:T(8,128)(2,1)}), bf16[8,128,128]{2,1,0:T(8,128)(2,1)S(1)}, u32[]{:S(2)}, u32[]{:S(2)}) %all-to-all-start.3) | async-done | bytes 262176 | tf_op jit(solution)/shard_map/all_to_all | solution.py:538
  237.3 4.3 %outside.1 = (bf16[384,1024]{1,0:T(8,128)(2,1)}, bf16[384,1024]{1,0:T(8,128)(2,1)}) custom-call(bf16[384,1024]{1,0:T(8,128)(2,1)S(1)} %copy-done.2, bf16[384,1024]{1,0:T(8,128)(2,1)S(1)} %copy-done.4, bf16[8,128,128]{2,1,0:T(8,128)(2,1)S(1)} %all-to-all-done.3.state_ref, f32[384,8]{1,0:T(8,128)S(1)} %get-tuple-element.98.turned_ref, ...), custom_call_target="tpu_custom_call" | custom-call | flops 1000 | bytes 1000 | tf_op jit(solution)/shard_map/outside/pallas_call | solution.py:546
  241.6 2.9 %sum.1 = bf16[128,6144]{1,0:T(8,128)(2,1)} custom-call(bf16[128,3072]{1,0:T(8,128)(2,1)S(1)} %copy-done.30, bf16[128,3072]{1,0:T(8,128)(2,1)} %collective-permute-done.30.refs_1_, bf16[128,3072]{1,0:T(8,128)(2,1)S(1)} %copy-done.32, bf16[128,3072]{1,0:T(8,128)(2,1)} %collective-permute-done.31.refs_3_), custom_call_target="tpu_custom_call" | custom-call | flops 1000 | bytes 1000 | tf_op jit(solution)/shard_map/sum/pallas_call | solution.py:550
  (158 shorter events, 38.5 us)
Async XLA Ops:
  3.1 24.0 %collective-permute-start = (bf16[96,3072]{1,0:T(8,128)(2,1)}, bf16[96,3072]{1,0:T(8,128)(2,1)}, u32[]{:S(2)}, u32[]{:S(2)}) collective-permute-start(bf16[96,3072]{1,0:T(8,128)(2,1)} %get-tuple-element.188), channel_id=1, source_target_pairs={{0,8},{4,12},{8,24},{12,28},{24,16},{28,20},{16,0},{20,4},{1,9},{5... | collective-permute-start | bytes 1769480 | tf_op jit(solution)/shard_map/ppermute | solution.py:398
  11.3 15.8 %all-to-all-start = ((bf16[8,144,128]{2,1,0:T(8,128)(2,1)}), bf16[8,144,128]{2,1,0:T(8,128)(2,1)S(1)}, u32[]{:S(2)}, u32[]{:S(2)}) async-start(bf16[8,144,128]{2,1,0:T(8,128)(2,1)} %get-tuple-element.96), calls=%async_computation | async-start | bytes 589824 | tf_op jit(solution)/shard_map/all_to_all | solution.py:420
  27.1 20.8 %collective-permute-start.1 = (bf16[96,3072]{1,0:T(8,128)(2,1)}, bf16[96,3072]{1,0:T(8,128)(2,1)S(1)}, u32[]{:S(2)}, u32[]{:S(2)}) collective-permute-start(bf16[96,3072]{1,0:T(8,128)(2,1)} %get-tuple-element.102), channel_id=1, source_target_pairs={{0,8},{4,12},{8,24},{12,28},{24,16},{28,20},{16,0},{20,4},{1,9},{5... | collective-permute-start | bytes 1769480 | tf_op jit(solution)/shard_map/ppermute | solution.py:398
  28.2 19.7 %collective-permute-start.2 = (bf16[96,3072]{1,0:T(8,128)(2,1)}, bf16[96,3072]{1,0:T(8,128)(2,1)S(1)}, u32[]{:S(2)}, u32[]{:S(2)}) collective-permute-start(bf16[96,3072]{1,0:T(8,128)(2,1)} %collective-permute-done), channel_id=1, source_target_pairs={{0,2},{1,3},{2,0},{3,1},{4,6},{5,7},{6,4},{7,5},{8,10},{9,11},{10,... | collective-permute-start | bytes 1769480 | tf_op jit(solution)/shard_map/ppermute | solution.py:401
  29.7 21.7 %copy-start.23 = (f32[384,1024]{1,0:T(8,128)S(1)}, f32[384,1024]{1,0:T(8,128)}, u32[]{:S(2)}) copy-start(f32[384,1024]{1,0:T(8,128)} %copy-done.22) | copy-start | bytes 4718596
  49.1 61.8 %slice-start = ((s8[4718592]{0:T(1024)(128)(4,1)}), s8[4194304]{0:T(1024)(128)(4,1)S(1)}, s32[]{:S(2)}) async-start(s8[4718592]{0:T(1024)(128)(4,1)} %bitcast.5), calls=%async_computation.4 | async-start | bytes 8388608
  49.2 17.4 %collective-permute-start.5 = (bf16[192,3072]{1,0:T(8,128)(2,1)S(1)}, bf16[192,3072]{1,0:T(8,128)(2,1)S(1)}, u32[]{:S(2)}, u32[]{:S(2)}) collective-permute-start(bf16[192,3072]{1,0:T(8,128)(2,1)S(1)} %constant_dynamic-update-slice_fusion.refs_1_.refs_5_), channel_id=1, source_target_pairs={{0,1},{1,0},{2,3},{3,2},{4,5},{5,4},{6,7},{7,6},{8,9},{9,8},{10,11... | collective-permute-start | bytes 3538952 | tf_op jit(solution)/shard_map/ppermute | solution.py:401
  49.3 17.3 %collective-permute-start.3 = (bf16[96,3072]{1,0:T(8,128)(2,1)}, bf16[96,3072]{1,0:T(8,128)(2,1)S(1)}, u32[]{:S(2)}, u32[]{:S(2)}) collective-permute-start(bf16[96,3072]{1,0:T(8,128)(2,1)} %collective-permute-done), channel_id=1, source_target_pairs={{0,8},{4,12},{8,24},{12,28},{24,16},{28,20},{16,0},{20,4},{1,9},{5... | collective-permute-start | bytes 1769480 | tf_op jit(solution)/shard_map/ppermute | solution.py:398
  50.0 16.6 %collective-permute-start.4 = (bf16[96,3072]{1,0:T(8,128)(2,1)S(1)}, bf16[96,3072]{1,0:T(8,128)(2,1)S(1)}, u32[]{:S(2)}, u32[]{:S(2)}) collective-permute-start(bf16[96,3072]{1,0:T(8,128)(2,1)S(1)} %collective-permute-done.1), channel_id=1, source_target_pairs={{0,2},{1,3},{2,0},{3,1},{4,6},{5,7},{6,4},{7,5},{8,10},{9,11},{10,... | collective-permute-start | bytes 1769480 | tf_op jit(solution)/shard_map/ppermute | solution.py:401
  53.8 1.2 collective-permute-start.6
  66.7 47.0 %copy-start.10 = (bf16[192,3072]{1,0:T(8,128)(2,1)}, bf16[192,3072]{1,0:T(8,128)(2,1)S(1)}, u32[]{:S(2)}) copy-start(bf16[192,3072]{1,0:T(8,128)(2,1)S(1)} %constant_dynamic-update-slice_fusion.2.refs_3_.refs_5_) | copy-start | bytes 3538948
  66.7 21.0 %copy-start.41 = (f32[1024]{0:T(1024)S(1)}, f32[1024]{0:T(1024)}, u32[]{:S(2)}) copy-start(f32[1024]{0:T(1024)} %param.11) | copy-start | bytes 12292
  66.7 44.3 %slice-start.1 = ((s8[4718592]{0:T(1024)(128)(4,1)}), s8[524288]{0:T(1024)(128)(4,1)S(1)}, s32[]{:S(2)}) async-start(s8[4718592]{0:T(1024)(128)(4,1)} %bitcast.5), calls=%async_computation.5 | async-start | bytes 1048576
  66.7 17.8 %collective-permute-start.9 = (bf16[192,3072]{1,0:T(8,128)(2,1)S(1)}, bf16[192,3072]{1,0:T(8,128)(2,1)S(1)}, u32[]{:S(2)}, u32[]{:S(2)}) collective-permute-start(bf16[192,3072]{1,0:T(8,128)(2,1)S(1)} %constant_dynamic-update-slice_fusion.2.refs_3_.refs_5_), channel_id=1, source_target_pairs={{0,1},{1,0},{2,3},{3,2},{4,5},{5,4},{6,7},{7,6},{8,9},{9,8},{10,11... | collective-permute-start | bytes 3538952 | tf_op jit(solution)/shard_map/ppermute | solution.py:401
  66.8 17.7 %collective-permute-start.7 = (bf16[96,3072]{1,0:T(8,128)(2,1)S(1)}, bf16[96,3072]{1,0:T(8,128)(2,1)S(1)}, u32[]{:S(2)}, u32[]{:S(2)}) collective-permute-start(bf16[96,3072]{1,0:T(8,128)(2,1)S(1)} %collective-permute-done.1), channel_id=1, source_target_pairs={{0,8},{4,12},{8,24},{12,28},{24,16},{28,20},{16,0},{20,4},{1,9},{5... | collective-permute-start | bytes 1769480 | tf_op jit(solution)/shard_map/ppermute | solution.py:398
  69.0 15.5 %collective-permute-start.8 = (bf16[96,3072]{1,0:T(8,128)(2,1)S(1)}, bf16[96,3072]{1,0:T(8,128)(2,1)S(1)}, u32[]{:S(2)}, u32[]{:S(2)}) collective-permute-start(bf16[96,3072]{1,0:T(8,128)(2,1)S(1)} %collective-permute-done.3), channel_id=1, source_target_pairs={{0,2},{1,3},{2,0},{3,1},{4,6},{5,7},{6,4},{7,5},{8,10},{9,11},{10,... | collective-permute-start | bytes 1769480 | tf_op jit(solution)/shard_map/ppermute | solution.py:401
  70.5 13.9 %collective-permute-start.10 = (f32[1,384]{1,0:T(1,128)S(1)}, f32[1,384]{1,0:T(1,128)S(1)}, u32[]{:S(2)}, u32[]{:S(2)}) collective-permute-start(f32[1,384]{1,0:T(1,128)S(1)} %add.140.here_ref), channel_id=1, source_target_pairs={{0,2},{1,3},{2,0},{3,1},{4,6},{5,7},{6,4},{7,5},{8,10},{9,11},{10,... | collective-permute-start | bytes 4616 | tf_op jit(solution)/shard_map/ppermute | solution.py:401
  71.0 35.9 %collective-permute-start.14 = (bf16[128,6144]{1,0:T(8,128)(2,1)S(1)}, bf16[128,6144]{1,0:T(8,128)(2,1)S(1)}, u32[]{:S(2)}, u32[]{:S(2)}) collective-permute-start(bf16[128,6144]{1,0:T(8,128)(2,1)S(1)} %bitcast.7), channel_id=1, source_target_pairs={{0,4},{4,0},{8,12},{12,8},{16,20},{20,16},{24,28},{28,24},{1,5},{5... | collective-permute-start | bytes 4718600 | tf_op jit(solution)/shard_map/ppermute | solution.py:442
  84.5 29.2 %copy-start.14 = (bf16[192,3072]{1,0:T(8,128)(2,1)}, bf16[192,3072]{1,0:T(8,128)(2,1)S(1)}, u32[]{:S(2)}) copy-start(bf16[192,3072]{1,0:T(8,128)(2,1)S(1)} %collective-permute-done.9.refs_4_.refs_6_) | copy-start | bytes 3538948
  84.6 22.4 %collective-permute-start.13 = (bf16[192,3072]{1,0:T(8,128)(2,1)S(1)}, bf16[192,3072]{1,0:T(8,128)(2,1)S(1)}, u32[]{:S(2)}, u32[]{:S(2)}) collective-permute-start(bf16[192,3072]{1,0:T(8,128)(2,1)S(1)} %constant_dynamic-update-slice_fusion.4.refs_1_.refs_7_), channel_id=1, source_target_pairs={{0,1},{1,0},{2,3},{3,2},{4,5},{5,4},{6,7},{7,6},{8,9},{9,8},{10,11... | collective-permute-start | bytes 3538952 | tf_op jit(solution)/shard_map/ppermute | solution.py:401
  84.7 22.3 %collective-permute-start.11 = (bf16[96,3072]{1,0:T(8,128)(2,1)S(1)}, bf16[96,3072]{1,0:T(8,128)(2,1)S(1)}, u32[]{:S(2)}, u32[]{:S(2)}) collective-permute-start(bf16[96,3072]{1,0:T(8,128)(2,1)S(1)} %collective-permute-done.3), channel_id=1, source_target_pairs={{0,8},{4,12},{8,24},{12,28},{24,16},{28,20},{16,0},{20,4},{1,9},{5... | collective-permute-start | bytes 1769480 | tf_op jit(solution)/shard_map/ppermute | solution.py:398
  86.1 20.8 %collective-permute-start.12 = (bf16[96,3072]{1,0:T(8,128)(2,1)S(1)}, bf16[96,3072]{1,0:T(8,128)(2,1)S(1)}, u32[]{:S(2)}, u32[]{:S(2)}) collective-permute-start(bf16[96,3072]{1,0:T(8,128)(2,1)S(1)} %collective-permute-done.7), channel_id=1, source_target_pairs={{0,2},{1,3},{2,0},{3,1},{4,6},{5,7},{6,4},{7,5},{8,10},{9,11},{10,... | collective-permute-start | bytes 1769480 | tf_op jit(solution)/shard_map/ppermute | solution.py:401
  88.9 18.0 %collective-permute-start.15 = (bf16[384,256]{1,0:T(8,128)(2,1)S(1)}, bf16[384,256]{1,0:T(8,128)(2,1)S(1)}, u32[]{:S(2)}, u32[]{:S(2)}) collective-permute-start(bf16[384,256]{1,0:T(8,128)(2,1)S(1)} %get-tuple-element.121), channel_id=1, source_target_pairs={{0,8},{4,12},{8,24},{12,28},{24,16},{28,20},{16,0},{20,4},{1,9},{5... | collective-permute-start | bytes 589832 | tf_op jit(solution)/shard_map/ppermute | solution.py:468
  106.9 46.5 %copy-start.35 = (bf16[384,256]{1,0:T(8,128)(2,1)}, bf16[384,256]{1,0:T(8,128)(2,1)S(1)}, u32[]{:S(2)}) copy-start(bf16[384,256]{1,0:T(8,128)(2,1)S(1)} %collective-permute-done.15.refs_1_) | copy-start | bytes 589828
  107.1 27.2 %copy-start.12 = (bf16[192,3072]{1,0:T(8,128)(2,1)}, bf16[192,3072]{1,0:T(8,128)(2,1)S(1)}, u32[]{:S(2)}) copy-start(bf16[192,3072]{1,0:T(8,128)(2,1)S(1)} %constant_dynamic-update-slice_fusion.6.refs_3_.refs_7_) | copy-start | bytes 3538948
  107.1 21.4 %collective-permute-start.18 = (bf16[192,3072]{1,0:T(8,128)(2,1)S(1)}, bf16[192,3072]{1,0:T(8,128)(2,1)S(1)}, u32[]{:S(2)}, u32[]{:S(2)}) collective-permute-start(bf16[192,3072]{1,0:T(8,128)(2,1)S(1)} %constant_dynamic-update-slice_fusion.6.refs_3_.refs_7_), channel_id=1, source_target_pairs={{0,1},{1,0},{2,3},{3,2},{4,5},{5,4},{6,7},{7,6},{8,9},{9,8},{10,11... | collective-permute-start | bytes 3538952 | tf_op jit(solution)/shard_map/ppermute | solution.py:401
  107.1 21.3 %collective-permute-start.16 = (bf16[96,3072]{1,0:T(8,128)(2,1)S(1)}, bf16[96,3072]{1,0:T(8,128)(2,1)S(1)}, u32[]{:S(2)}, u32[]{:S(2)}) collective-permute-start(bf16[96,3072]{1,0:T(8,128)(2,1)S(1)} %collective-permute-done.7), channel_id=1, source_target_pairs={{0,8},{4,12},{8,24},{12,28},{24,16},{28,20},{16,0},{20,4},{1,9},{5... | collective-permute-start | bytes 1769480 | tf_op jit(solution)/shard_map/ppermute | solution.py:398
  108.6 19.8 %collective-permute-start.17 = (bf16[96,3072]{1,0:T(8,128)(2,1)S(1)}, bf16[96,3072]{1,0:T(8,128)(2,1)S(1)}, u32[]{:S(2)}, u32[]{:S(2)}) collective-permute-start(bf16[96,3072]{1,0:T(8,128)(2,1)S(1)} %collective-permute-done.11), channel_id=1, source_target_pairs={{0,2},{1,3},{2,0},{3,1},{4,6},{5,7},{6,4},{7,5},{8,10},{9,11},{10,... | collective-permute-start | bytes 1769480 | tf_op jit(solution)/shard_map/ppermute | solution.py:401
  110.1 17.3 %collective-permute-start.19 = (bf16[384,256]{1,0:T(8,128)(2,1)S(1)}, bf16[384,256]{1,0:T(8,128)(2,1)S(1)}, u32[]{:S(2)}, u32[]{:S(2)}) collective-permute-start(bf16[384,256]{1,0:T(8,128)(2,1)S(1)} %get-tuple-element.126), channel_id=1, source_target_pairs={{0,24},{4,28},{8,16},{12,20},{24,0},{28,4},{16,8},{20,12},{1,25},{... | collective-permute-start | bytes 589832 | tf_op jit(solution)/shard_map/ppermute | solution.py:475
  127.4 26.0 %copy-start.37 = (bf16[384,256]{1,0:T(8,128)(2,1)}, bf16[384,256]{1,0:T(8,128)(2,1)S(1)}, u32[]{:S(2)}) copy-start(bf16[384,256]{1,0:T(8,128)(2,1)S(1)} %collective-permute-done.19.refs_2_) | copy-start | bytes 589828
  128.5 15.8 %collective-permute-start.21 = (bf16[192,3072]{1,0:T(8,128)(2,1)S(1)}, bf16[192,3072]{1,0:T(8,128)(2,1)S(1)}, u32[]{:S(2)}, u32[]{:S(2)}) collective-permute-start(bf16[192,3072]{1,0:T(8,128)(2,1)S(1)} %constant_dynamic-update-slice_fusion.8.refs_1_.refs_9_), channel_id=1, source_target_pairs={{0,1},{1,0},{2,3},{3,2},{4,5},{5,4},{6,7},{7,6},{8,9},{9,8},{10,11... | collective-permute-start | bytes 3538952 | tf_op jit(solution)/shard_map/ppermute | solution.py:401
  128.6 15.7 %collective-permute-start.20 = (bf16[96,3072]{1,0:T(8,128)(2,1)S(1)}, bf16[96,3072]{1,0:T(8,128)(2,1)S(1)}, u32[]{:S(2)}, u32[]{:S(2)}) collective-permute-start(bf16[96,3072]{1,0:T(8,128)(2,1)S(1)} %collective-permute-done.16), channel_id=1, source_target_pairs={{0,2},{1,3},{2,0},{3,1},{4,6},{5,7},{6,4},{7,5},{8,10},{9,11},{10,... | collective-permute-start | bytes 1769480 | tf_op jit(solution)/shard_map/ppermute | solution.py:401
  130.2 10.0 %collective-permute-start.22 = (bf16[384,256]{1,0:T(8,128)(2,1)S(1)}, bf16[384,256]{1,0:T(8,128)(2,1)S(1)}, u32[]{:S(2)}, u32[]{:S(2)}) collective-permute-start(bf16[384,256]{1,0:T(8,128)(2,1)S(1)} %get-tuple-element.137), channel_id=1, source_target_pairs={{0,16},{4,20},{8,0},{12,4},{24,8},{28,12},{16,24},{20,28},{1,17},{... | collective-permute-start | bytes 589832 | tf_op jit(solution)/shard_map/ppermute | solution.py:483
  134.2 9.8 %collective-permute-start.23 = (bf16[384,256]{1,0:T(8,128)(2,1)S(1)}, bf16[384,256]{1,0:T(8,128)(2,1)S(1)}, u32[]{:S(2)}, u32[]{:S(2)}) collective-permute-start(bf16[384,256]{1,0:T(8,128)(2,1)S(1)} %product.6), channel_id=1, source_target_pairs={{0,16},{4,20},{8,0},{12,4},{24,8},{28,12},{16,24},{20,28},{1,17},{... | collective-permute-start | bytes 589832 | tf_op jit(solution)/shard_map/ppermute | solution.py:484
  144.5 3.6 %collective-permute-start.25 = (bf16[192,3072]{1,0:T(8,128)(2,1)S(1)}, bf16[192,3072]{1,0:T(8,128)(2,1)S(1)}, u32[]{:S(2)}, u32[]{:S(2)}) collective-permute-start(bf16[192,3072]{1,0:T(8,128)(2,1)S(1)} %constant_dynamic-update-slice_fusion.10.refs_1_.refs_9_), channel_id=1, source_target_pairs={{0,1},{1,0},{2,3},{3,2},{4,5},{5,4},{6,7},{7,6},{8,9},{9,8},{10,11... | collective-permute-start | bytes 3538952 | tf_op jit(solution)/shard_map/ppermute | solution.py:401
  144.6 14.2 %collective-permute-start.24 = (bf16[384,256]{1,0:T(8,128)(2,1)S(1)}, bf16[384,256]{1,0:T(8,128)(2,1)S(1)}, u32[]{:S(2)}, u32[]{:S(2)}) collective-permute-start(bf16[384,256]{1,0:T(8,128)(2,1)S(1)} %product.7), channel_id=1, source_target_pairs={{0,24},{4,28},{8,16},{12,20},{24,0},{28,4},{16,8},{20,12},{1,25},{... | collective-permute-start | bytes 589832 | tf_op jit(solution)/shard_map/ppermute | solution.py:491
  149.5 12.6 %collective-permute-start.26 = (bf16[384,256]{1,0:T(8,128)(2,1)S(1)}, bf16[384,256]{1,0:T(8,128)(2,1)S(1)}, u32[]{:S(2)}, u32[]{:S(2)}) collective-permute-start(bf16[384,256]{1,0:T(8,128)(2,1)S(1)} %product.9), channel_id=1, source_target_pairs={{0,8},{4,12},{8,24},{12,28},{24,16},{28,20},{16,0},{20,4},{1,9},{5... | collective-permute-start | bytes 589832 | tf_op jit(solution)/shard_map/ppermute | solution.py:496
  163.3 4.2 %collective-permute-start.29 = (f32[1,1024]{1,0:T(1,128)S(1)}, f32[1,1024]{1,0:T(1,128)S(1)}, u32[]{:S(2)}, u32[]{:S(2)}) collective-permute-start(f32[1,1024]{1,0:T(1,128)S(1)} %get-tuple-element.166), channel_id=1, source_target_pairs={{0,4},{4,0},{8,12},{12,8},{16,20},{20,16},{24,28},{28,24},{1,5},{5... | collective-permute-start | bytes 12296 | tf_op jit(solution)/shard_map/ppermute | solution.py:510
  164.8 1.2 collective-permute-start.27
  166.0 3.6 %collective-permute-start.28 = (f32[1,384]{1,0:T(1,128)S(1)}, f32[1,384]{1,0:T(1,128)S(1)}, u32[]{:S(2)}, u32[]{:S(2)}) collective-permute-start(f32[1,384]{1,0:T(1,128)S(1)} %add.141.here_ref), channel_id=1, source_target_pairs={{0,2},{1,3},{2,0},{3,1},{4,6},{5,7},{6,4},{7,5},{8,10},{9,11},{10,... | collective-permute-start | bytes 4616 | tf_op jit(solution)/shard_map/ppermute | solution.py:401
  176.2 21.8 %all-to-all-start.2 = ((bf16[8,144,128]{2,1,0:T(8,128)(2,1)}), bf16[8,144,128]{2,1,0:T(8,128)(2,1)S(1)}, u32[]{:S(2)}, u32[]{:S(2)}) async-start(bf16[8,144,128]{2,1,0:T(8,128)(2,1)} %get-tuple-element.173), calls=%async_computation.2 | async-start | bytes 589824 | tf_op jit(solution)/shard_map/all_to_all | solution.py:522
  189.6 23.5 %copy-start.7 = (bf16[384,1024]{1,0:T(8,128)(2,1)S(1)}, bf16[384,1024]{1,0:T(8,128)(2,1)}, u32[]{:S(2)}) copy-start(bf16[384,1024]{1,0:T(8,128)(2,1)} %q_ref.7) | copy-start | bytes 2359300
  196.1 17.1 %copy-start.4 = (bf16[384,1024]{1,0:T(8,128)(2,1)S(1)}, bf16[384,1024]{1,0:T(8,128)(2,1)}, u32[]{:S(2)}) copy-start(bf16[384,1024]{1,0:T(8,128)(2,1)} %v_ref.7) | copy-start | bytes 2359300
  196.1 45.5 %collective-permute-start.30 = (bf16[128,3072]{1,0:T(8,128)(2,1)}, bf16[128,3072]{1,0:T(8,128)(2,1)}, u32[]{:S(2)}, u32[]{:S(2)}) collective-permute-start(bf16[128,3072]{1,0:T(8,128)(2,1)} %get-tuple-element.183), channel_id=1, source_target_pairs={{0,4},{4,0},{8,12},{12,8},{16,20},{20,16},{24,28},{28,24},{1,5},{5... | collective-permute-start | bytes 2359304 | tf_op jit(solution)/shard_map/ppermute | solution.py:515
  198.0 43.5 %collective-permute-start.31 = (bf16[128,3072]{1,0:T(8,128)(2,1)}, bf16[128,3072]{1,0:T(8,128)(2,1)}, u32[]{:S(2)}, u32[]{:S(2)}) collective-permute-start(bf16[128,3072]{1,0:T(8,128)(2,1)} %copy-done.43), channel_id=1, source_target_pairs={{0,4},{4,0},{8,12},{12,8},{16,20},{20,16},{24,28},{28,24},{1,5},{5... | collective-permute-start | bytes 2359304 | tf_op jit(solution)/shard_map/ppermute | solution.py:532
  199.0 35.5 %all-to-all-start.3 = ((bf16[8,128,128]{2,1,0:T(8,128)(2,1)}), bf16[8,128,128]{2,1,0:T(8,128)(2,1)S(1)}, u32[]{:S(2)}, u32[]{:S(2)}) async-start(bf16[8,128,128]{2,1,0:T(8,128)(2,1)} %copy-done.28), calls=%async_computation.3 | async-start | bytes 524288 | tf_op jit(solution)/shard_map/all_to_all | solution.py:538
  204.9 4.7 %collective-permute-start.32 = (f32[1,1024]{1,0:T(1,128)S(1)}, f32[1,1024]{1,0:T(1,128)S(1)}, u32[]{:S(2)}, u32[]{:S(2)}) collective-permute-start(f32[1,1024]{1,0:T(1,128)S(1)} %add.142), channel_id=1, source_target_pairs={{0,8},{4,12},{8,0},{12,4},{16,24},{20,28},{24,16},{28,20},{1,9},{5... | collective-permute-start | bytes 12296 | tf_op jit(solution)/shard_map/ppermute | solution.py:541
  209.5 15.4 %collective-permute-start.33 = (f32[1,1024]{1,0:T(1,128)S(1)}, f32[1,1024]{1,0:T(1,128)S(1)}, u32[]{:S(2)}, u32[]{:S(2)}) collective-permute-start(f32[1,1024]{1,0:T(1,128)S(1)} %add.143), channel_id=1, source_target_pairs={{0,16},{4,20},{8,24},{12,28},{16,0},{20,4},{24,8},{28,12},{1,17},{... | collective-permute-start | bytes 12296 | tf_op jit(solution)/shard_map/ppermute | solution.py:541
  (35 other events, 140.2 us)

commit v5 on v4

v5 whole, which is shorter than its diff:
```python
import functools

import jax
import jax.numpy as jnp
from jax import lax
from jax.experimental import pallas as pl
from jax.experimental.pallas import tpu as pltpu
from jax.sharding import PartitionSpec as P

LINE = 4
CHUNKS = 2
RELATIVE = (0, 2, 1, 3)
FL = jnp.float32
BF = jnp.bfloat16
PARAMS = pltpu.CompilerParams(vmem_limit_bytes=20 * 1024 * 1024)
EXACT = lax.Precision.HIGHEST
NN = (((1,), (0,)), ((), ()))
NT = (((1,), (1,)), ((), ()))
TN = (((0,), (0,)), ((), ()))


def dot(a, b, dims, precision=None):
    return lax.dot_general(a, b, dims, preferred_element_type=FL, precision=precision)


def spec(shape, index=None):
    return pl.BlockSpec(shape, index or (lambda *_: (0,) * len(shape)))


SCALAR = pl.BlockSpec(memory_space=pltpu.SMEM)


TINY = pl.CostEstimate(flops=1000, bytes_accessed=1000, transcendentals=0)


def after(x, *others):
    return lax.optimization_barrier((x, *others))[0]


def spot(z):
    return z ^ (z >> 1)


def ring_perm(count, shift):
    minor = count // LINE
    return [
        (spot(p) * minor + m, spot((p + shift) % LINE) * minor + m)
        for p in range(LINE)
        for m in range(minor)
    ]


def pair_perm(count, shift):
    minor = count // LINE
    return [
        (z * minor + m, z * minor + (m + shift) % minor)
        for z in range(LINE)
        for m in range(minor)
    ]


def fold_rows(x):
    width = x.shape[1]
    total = x[:, :128]
    for at in range(128, width, 128):
        total = total + x[:, at : at + 128]
    return jnp.sum(total.T, axis=0, keepdims=True)


def mask_of(run_ref, runs, head):
    tok = run_ref.shape[1]
    row = run_ref[head : head + 1, :]
    lower = lax.broadcasted_iota(jnp.int32, (tok, tok), 0) >= lax.broadcasted_iota(
        jnp.int32, (tok, tok), 1
    )
    return jnp.where(lower, jnp.exp(jnp.minimum(runs - row, 0.0)), 0.0)


def per_head(run_ref):
    heads = run_ref.shape[1]
    for head in range(heads):
        run = run_ref[:, head : head + 1]
        yield head, slice(head * 128, (head + 1) * 128), run, run[run.shape[0] - 1 :, :]


def put_state(out_ref, head, heads, state, total):
    count, deep, wide = out_ref.shape
    parts = count // heads
    rows = deep - 16
    high = total.astype(BF)
    low = (total - high.astype(FL)).astype(BF)
    for j in range(parts):
        at = head * parts + j
        out_ref[at, :rows] = state[j * rows : (j + 1) * rows].astype(BF)
        out_ref[at, rows : rows + 8] = jnp.broadcast_to(high, (8, wide))
        out_ref[at, rows + 8 :] = jnp.broadcast_to(low, (8, wide))


def state_kernel(decay_ref, k_ref, v_ref, out_ref, run_ref, turned_ref):
    heads, tok = decay_ref.shape
    first = lax.broadcasted_iota(jnp.int32, (tok, tok), 0)
    second = lax.broadcasted_iota(jnp.int32, (tok, tok), 1)
    run_ref[...] = dot(decay_ref[...], (first <= second).astype(FL), NN, EXACT)
    turned_ref[...] = dot((second <= first).astype(FL), decay_ref[...], NT, EXACT)
    for head, at, run, total in per_head(turned_ref):
        weighted = (k_ref[:, at].astype(FL) * jnp.exp(total - run)).astype(BF)
        put_state(out_ref, head, heads, dot(weighted, v_ref[:, at], TN), total)


def scan_kernel(reverse, in_ref, out_ref):
    count, deep, wide = in_ref.shape
    rows = deep - 16
    state = jnp.zeros((rows // 8, 8, wide), FL)
    for b in range(count - 1, -1, -1) if reverse else range(count):
        out_ref[b] = state.reshape(rows, wide).astype(BF)
        total = in_ref[b, rows:].astype(FL)
        factor = jnp.exp(total[:8] + total[8:])
        state = factor[None] * state + in_ref[b, :rows].astype(FL).reshape(rows // 8, 8, wide)


def weights_kernel(q_ref, k_ref, v_ref, run_ref, turned_ref, intra_ref):
    for head, at, run, _ in per_head(turned_ref):
        scores = dot(q_ref[:, at], k_ref[:, at], NT)
        weights = (scores * mask_of(run_ref, run, head)).astype(BF)
        intra_ref[:, at] = dot(weights, v_ref[:, at], NN)


def attend_kernel(q_ref, state_ref, turned_ref, intra_ref, out_ref, squares_ref):
    held = None
    for head, at, run, _ in per_head(turned_ref):
        out = intra_ref[:, at] + dot(q_ref[:, at], state_ref[head], NN) * jnp.exp(run)
        out_ref[:, at] = out
        held = out * out if held is None else held + out * out
    squares_ref[...] = fold_rows(held)


def turned_row(row):
    return jnp.broadcast_to(row, (128, row.shape[1])).T[:, :1]


def norm_kernel(features, mine_ref, attn_ref, here_ref, there_ref, gain_ref, order_ref, *outs):
    inv_ref, own_ref, *sent = outs
    inv = lax.rsqrt((here_ref[...] + there_ref[...]) / features + 1e-05)
    inv_ref[...] = inv
    normed = (attn_ref[...] * turned_row(inv) * gain_ref[...]).astype(BF)
    tok, width = normed.shape
    span = width // LINE
    quarter = tok // len(RELATIVE)
    own_ref[...] = dot(normed, order_ref[:, :span], NN).astype(BF)
    for s, ref in enumerate(sent, 1):
        part = dot(normed, order_ref[:, s * span : (s + 1) * span], NN).astype(BF)
        for j in range(len(RELATIVE)):
            turn = mine_ref[0] ^ j
            to = pl.multiple_of(((turn & 1) * 2 + (turn >> 1)) * quarter, 16)
            ref[pl.ds(to, quarter), :] = part[j * quarter : (j + 1) * quarter]


def product_kernel(lots, weights, add, last, *refs):
    refs = list(refs)
    mine_ref = refs.pop(0)
    x = [[refs.pop(0) for _ in range(k)] for k in lots]
    w = [refs.pop(0) for _ in range(weights)]
    extra = refs.pop(0) if add else None
    out_ref, held_ref = refs
    step = pl.program_id(0)
    steps = pl.num_programs(0) // len(lots)

    @pl.when(step == 0)
    def _():
        held_ref[...] = extra[...] if add else jnp.zeros_like(held_ref)

    for at, lot in enumerate(x):

        @pl.when(step // steps == at)
        def _():
            rows = jnp.concatenate([r[...] for r in lot], axis=0)
            cols = jnp.concatenate([r[...] for r in w], axis=0)
            held_ref[...] += dot(rows, cols, NT)

    @pl.when(step == pl.num_programs(0) - 1)
    def _():
        if not last:
            out_ref[...] = held_ref[...]
        elif lots[0] == 1:
            out_ref[...] = held_ref[...].astype(BF)
        else:
            quarter = out_ref.shape[0] // len(RELATIVE)
            for i, turn in enumerate(RELATIVE):
                to = pl.multiple_of((mine_ref[0] ^ turn) * quarter, 16)
                out_ref[pl.ds(to, quarter), :] = held_ref[
                    i * quarter : (i + 1) * quarter, :
                ].astype(BF)


def product(mine, lots, weights, chunk, last, held):
    tok = sum(p.shape[0] for p in lots[0])
    deep = lots[0][0].shape[1]
    tile = 1536
    steps = deep // tile
    span = sum(w.shape[0] for w in weights)
    base = chunk * steps
    more = [] if held is None else [held]

    def piece_spec(at, p):
        return spec((p.shape[0], tile), lambda i: (0, jnp.clip(i - at * steps, 0, steps - 1)))

    return pl.pallas_call(
        functools.partial(product_kernel, [len(x) for x in lots], len(weights), len(more), last),
        grid=(steps * len(lots),),
        in_specs=[SCALAR]
        + [piece_spec(at, p) for at, lot in enumerate(lots) for p in lot]
        + [spec((w.shape[0], tile), lambda i: (0, base + i)) for w in weights]
        + [spec((tok, span)) for _ in more],
        out_specs=spec((tok, span)),
        out_shape=jax.ShapeDtypeStruct((tok, span), BF if last else FL),
        scratch_shapes=[pltpu.VMEM((tok, span), FL)],
        compiler_params=PARAMS,
        cost_estimate=TINY,
        name="product",
    )(mine, *[p for lot in lots for p in lot], *weights, *more)


def outer_kernel(lots, own, *refs):
    refs = list(refs)
    normed = [refs.pop(0) for _ in lots]
    x = [[refs.pop(0) for _ in range(k)] for k in lots]
    turned_ref = refs.pop()

    @pl.when(pl.program_id(0) == 0)
    def _():
        turned_ref[...] = jnp.concatenate([r[...] for r in normed], axis=0).T

    rows = jnp.concatenate([r[...] for lot in x for r in lot], axis=0)
    out = dot(turned_ref[...], rows, NN).astype(BF)
    for s, ref in enumerate(refs):
        ref[...] = out[s * own : (s + 1) * own]


def outer(normed, grad_out, lots, chunk, own):
    tok, span = normed[0].shape
    deep = lots[0][0].shape[1]
    tile = 512
    steps = deep // tile
    base = chunk * steps
    flat = [p for lot in lots for p in lot]
    minor = span // own
    return pl.pallas_call(
        functools.partial(outer_kernel, [1] + [len(lot) for lot in lots], own),
        grid=(steps,),
        in_specs=[spec((tok, span)) for _ in normed]
        + [spec((tok, tile), lambda i: (0, base + i))]
        + [spec((p.shape[0], tile), lambda i: (0, i)) for p in flat],
        out_specs=[spec((own, tile), lambda i: (0, i))] * minor,
        out_shape=[jax.ShapeDtypeStruct((own, deep), BF)] * minor,
        scratch_shapes=[pltpu.VMEM((span, tok * LINE), BF)],
        compiler_params=PARAMS,
        cost_estimate=TINY,
        name="outer",
    )(*normed, grad_out, *flat)


def final_kernel(chunks, minor, *refs):
    out_ref = refs[-1]
    deep = refs[0].shape[1]
    for c in range(chunks):
        total = refs[c * minor][...].astype(FL)
        for s in range(1, minor):
            total = total + refs[c * minor + s][...].astype(FL)
        out_ref[:, c * deep : (c + 1) * deep] = total.astype(BF)


def back_kernel(order_ref, attn_ref, inv_ref, gain_ref, *refs):
    pieces, (out_ref, sum_ref, inner_ref) = refs[:LINE], refs[LINE:]
    span = pieces[0].shape[1]
    grad = dot(pieces[0][...], order_ref[:, :span], NT)
    for s in range(1, LINE):
        grad = grad + dot(pieces[s][...], order_ref[:, s * span : (s + 1) * span], NT)
    out_ref[...] = grad.astype(BF)
    both = grad * attn_ref[...]
    sum_ref[...] = jnp.sum(both * turned_row(inv_ref[...]), axis=0, keepdims=True)
    inner_ref[...] = fold_rows(both * gain_ref[...])


def grad_kernel(
    features, grad_ref, attn_ref, inv_ref, here_ref, there_ref, gain_ref, q_ref, turned_ref,
    out_ref, state_ref,
):
    inv = inv_ref[...]
    shift = turned_row(inv * inv * inv * ((here_ref[...] + there_ref[...]) / features))
    inv = turned_row(inv)
    heads = turned_ref.shape[1]
    for head, at, run, total in per_head(turned_ref):
        scaled = grad_ref[:, at].astype(FL) * gain_ref[:, at]
        grad = (inv * scaled - attn_ref[:, at] * shift).astype(BF)
        out_ref[:, at] = grad
        weighted = (q_ref[:, at].astype(FL) * jnp.exp(run)).astype(BF)
        put_state(state_ref, head, heads, dot(weighted, grad, TN), total)


def inside_kernel(
    grad_ref, q_ref, k_ref, v_ref, run_ref, turned_ref, state_ref, gq_ref, gk_ref, gv_ref
):
    for head, at, run, _ in per_head(turned_ref):
        grad, query, key = grad_ref[:, at], q_ref[:, at], k_ref[:, at]
        mask = mask_of(run_ref, run, head)
        masked = (dot(grad, v_ref[:, at], NT) * mask).astype(BF)
        weights = (dot(query, key, NT) * mask).astype(BF)
        gq = dot(masked, key, NN) + dot(grad, state_ref[head], NT) * jnp.exp(run)
        gq_ref[:, at] = gq.astype(BF)
        gk_ref[:, at] = dot(masked, query, TN)
        gv_ref[:, at] = dot(weights, grad, TN)


def outside_kernel(k_ref, v_ref, state_ref, turned_ref, gk_in, gv_in, gk_ref, gv_ref):
    for head, at, run, total in per_head(turned_ref):
        final = jnp.exp(total - run)
        state = state_ref[head]
        gk_ref[:, at] = (gk_in[:, at] + dot(v_ref[:, at], state, NT) * final).astype(BF)
        gv_ref[:, at] = (gv_in[:, at] + dot(k_ref[:, at], state, NN) * final).astype(BF)


def feature_order(heads, size, count):
    minor = count // LINE
    narrow = size // count
    place = lax.axis_index("ctx")
    z, m = place // minor, place % minor
    p = spot(z)
    col = jnp.arange(heads * size)
    shift = col // (minor * heads * narrow)
    inner = col % (minor * heads * narrow)
    turn = inner // (heads * narrow)
    head = (inner % (heads * narrow)) // narrow
    unit = inner % narrow
    slot = spot((p + shift) % LINE) * minor + (m + turn) % minor
    natural = head * size + slot * narrow + unit
    return (jnp.arange(heads * size)[:, None] == natural[None, :]).astype(BF)


def shards(query_rows, key_rows, value_rows, log_decay, norm_gain, out_weight, grad_out):
    count = lax.axis_size("ctx")
    head_count = lax.axis_size("head")
    minor = count // LINE
    heads = log_decay.shape[0]
    tok, width = query_rows.shape
    size = width // heads
    narrow = size // count
    model = grad_out.shape[1]
    own = width // LINE // minor
    span = width // LINE
    rows = width // count
    features = width * head_count
    half = head_count // 2
    over_y = [(i, (i + half) % head_count) for i in range(head_count)]
    over_core = [(i, i ^ 1) for i in range(head_count)]

    mine = lax.axis_index("head").astype(jnp.int32)
    quarter = tok // head_count
    deep = model // CHUNKS
    tokens = mine.reshape(1)

    def first_piece(c):
        return lax.dynamic_slice(grad_out, (mine * quarter, c * deep), (quarter, deep))

    put_shape = jax.ShapeDtypeStruct((count, rows + 16, size), BF)
    wide_f = jax.ShapeDtypeStruct((tok, width), FL)
    wide_b = jax.ShapeDtypeStruct((tok, width), BF)
    row_f = jax.ShapeDtypeStruct((1, tok), FL)
    part_b = jax.ShapeDtypeStruct((tok, span), BF)
    full = pl.BlockSpec(memory_space=pltpu.VMEM)

    def whole(kernel, out_shape, name, *args):
        several = isinstance(out_shape, list)
        return pl.pallas_call(
            kernel,
            in_specs=[SCALAR if a is tokens else full for a in args],
            out_specs=[full] * len(out_shape) if several else full,
            out_shape=out_shape, compiler_params=PARAMS, cost_estimate=TINY, name=name,
        )(*args)

    gain_row = norm_gain.reshape(1, width)
    weight_own = out_weight.reshape(heads * narrow, model)

    def ring(x):
        return lax.ppermute(x, "ctx", ring_perm(count, 1))

    def over(x, perm):
        return lax.ppermute(x, "head", perm)

    def near_of(x):
        return over(x, over_core)

    def other_of(x):
        return over(x, over_y)

    def core_of(x, y):
        both = jnp.concatenate([x, y], axis=0)
        return both, near_of(both)

    hold = lax.optimization_barrier
    scan_shape = jax.ShapeDtypeStruct((count, rows, size), BF)

    ra1 = ring(first_piece(0))
    put, run, turned = whole(
        state_kernel,
        [put_shape, jax.ShapeDtypeStruct((heads, tok), FL), jax.ShapeDtypeStruct((tok, heads), FL)],
        "states", log_decay, key_rows, value_rows,
    )
    rb1 = ring(after(first_piece(1), put))
    spread = lax.all_to_all(put, "ctx", 0, 0, tiled=True)
    intra = whole(
        weights_kernel, wide_f, "weights", query_rows, key_rows, value_rows, run, turned
    )
    ra1, spread, intra = hold((ra1, spread, intra))

    ya1 = other_of(ra1)
    states = whole(functools.partial(scan_kernel, False), scan_shape, "scan", spread)
    state_low = lax.all_to_all(states, "ctx", 0, 0, tiled=True)
    order = feature_order(heads, size, count)
    ra1, rb1, ya1, state_low, weight_own, order = hold(
        (ra1, rb1, ya1, state_low, weight_own, order)
    )

    ra2, rb2, yb1, (da1, ca1) = ring(ra1), ring(rb1), other_of(rb1), core_of(ra1, ya1)
    weights = [lax.ppermute(weight_own, "ctx", pair_perm(count, -s)) for s in range(1, minor)]
    ca1, state_low = hold((ca1, state_low))
    state_low = state_low.reshape(heads, size, size)
    attn_out, squares = whole(
        attend_kernel, [wide_f, row_f], "attend", query_rows, state_low, turned, intra
    )
    squares = squares + near_of(squares)
    squares_there = other_of(squares)
    ra2, yb1, squares_there = hold((ra2, yb1, squares_there))

    ra3, ya2, (db1, cb1) = ring(ra2), other_of(ra2), core_of(rb1, yb1)
    inv_rms, *sent = whole(
        functools.partial(norm_kernel, features), [row_f] + [part_b] * LINE, "norm",
        tokens, attn_out, squares, squares_there, gain_row, order,
    )
    rb2, ya2, cb1, sent = hold((rb2, ya2, cb1, sent))

    rb3, yb2, (da2, ca2) = ring(rb2), other_of(rb2), core_of(ra2, ya2)
    ra3, yb2, ca2, weights, sent = hold((ra3, yb2, ca2, weights, sent))
    weights = [weight_own] + weights

    ya3, (db2, cb2) = other_of(ra3), core_of(rb2, yb2)
    normed = [sent[0]] + [
        lax.ppermute(sent[s], "ctx", ring_perm(count, s)) for s in range(1, LINE)
    ]
    one = product(tokens, [[da1, ca1], [db1, cb1]], weights, 0, True, None)
    mine_part = product(tokens, [[grad_out]], weights, 0, True, None)
    rb3, ya3, cb2, one, mine_part = hold((rb3, ya3, cb2, one, mine_part))

    yb3, (da3, ca3) = other_of(rb3), core_of(ra3, ya3)
    returned = [mine_part, lax.ppermute(one, "ctx", ring_perm(count, -1))]
    two = product(tokens, [[da2, ca2], [db2, cb2]], weights, 0, True, None)
    three = product(tokens, [[da3, ca3]], weights, 0, False, None)
    yb3, three, two, normed = hold((yb3, three, two, normed))

    db3, cb3 = core_of(rb3, yb3)
    returned.append(lax.ppermute(two, "ctx", ring_perm(count, -2)))
    lots = [[[da1, ca1], [da2, ca2], [da3, ca3]], [[db1, cb1], [db2, cb2], [db3, cb3]]]
    cb3, three = hold((cb3, three))
    lots[1][2][1] = cb3
    three = product(tokens, [[db3, cb3]], weights, 1, True, three)
    returned.append(lax.ppermute(three, "ctx", ring_perm(count, -3)))
    early = outer([after(normed[0], three)] + normed[1:], grad_out, lots[0], 0, own)
    returned, early = hold((returned, early))

    flat = [early[0]]
    flat += [lax.ppermute(early[s], "ctx", pair_perm(count, s)) for s in range(1, minor)]
    grad, gain_sum, inner = whole(
        back_kernel, [wide_b, jax.ShapeDtypeStruct((1, width), FL), row_f], "back",
        order, attn_out, inv_rms, gain_row, *returned,
    )
    gain_sum = gain_sum + lax.ppermute(gain_sum, "ctx", [(i, i ^ 1) for i in range(count)])
    inner = inner + near_of(inner)
    inner_there = other_of(inner)
    late = outer([after(normed[0], inner)] + normed[1:], grad_out, lots[1], 1, own)
    inner_there, late = hold((inner_there, late))
    grad_attn, put_back = whole(
        functools.partial(grad_kernel, features), [wide_b, put_shape], "grads",
        grad, attn_out, inv_rms, inner, inner_there, gain_row, query_rows, turned,
    )
    spread = lax.all_to_all(put_back, "ctx", 0, 0, tiled=True)
    grad_query, gk_in, gv_in = whole(
        inside_kernel, [wide_b, wide_f, wide_f], "inside",
        grad_attn, query_rows, key_rows, value_rows, run, turned, state_low,
    )
    spread, gk_in, gv_in, late, gain_sum = hold((spread, gk_in, gv_in, late, gain_sum))
    flat.append(late[0])
    flat += [lax.ppermute(late[s], "ctx", pair_perm(count, s)) for s in range(1, minor)]
    states = whole(functools.partial(scan_kernel, True), scan_shape, "scan", spread)
    back_low = lax.all_to_all(states, "ctx", 0, 0, tiled=True).reshape(heads, size, size)
    step = 2
    while step < count:
        gain_sum = gain_sum + lax.ppermute(
            gain_sum, "ctx", [(i, i ^ step) for i in range(count)]
        )
        step *= 2
    grad_gain = gain_sum.reshape(width)
    grad_key, grad_value = whole(
        outside_kernel, [wide_b] * 2, "outside",
        key_rows, value_rows, back_low, turned, gk_in, gv_in,
    )
    grad_weight = whole(
        functools.partial(final_kernel, CHUNKS, minor), jax.ShapeDtypeStruct((own, model), BF),
        "sum", *flat,
    ).reshape(heads, narrow, model)
    return grad_query, grad_key, grad_value, grad_weight, grad_gain


def solution(mesh):
    return jax.shard_map(
        shards,
        mesh=mesh,
        in_specs=(
            P("ctx", "head"),
            P("ctx", "head"),
            P("ctx", "head"),
            P("head", "ctx"),
            P("head"),
            P("head", "ctx", None),
            P("ctx", None),
        ),
        out_specs=(
            P("ctx", "head"),
            P("ctx", "head"),
            P("ctx", "head"),
            P("head", "ctx", None),
            P("head"),
        ),
        check_vma=False,
    )
```

time: 245 us -> 231 us (0.943)
  waiting for transfers between devices: 82.3 us -> 107 us
  blocking collectives: 18.2 us -> 0 us
  Pallas kernels: 55.1 us -> 41.8 us
  local copies, waits for them, and re-layouts: 27.9 us -> 17 us
  starting transfers between devices: 58.3 us -> 61.9 us
    ppermute x6, waiting for transfers between devices: 12.6 us -> 32.8 us  [ring(): return lax.ppermute(x, 'ctx', ring_perm(count, 1))]
    all_to_all x1 -> x0, blocking collectives: 18.2 us -> none  [shards(): state_low = lax.all_to_all(states, 'ctx', 0, 0, tiled=True)]
    ppermute x16, waiting for transfers between devices: 16.7 us -> 3.22 us  [over(): return lax.ppermute(x, 'head', perm)]
    pallas_call x11, Pallas kernels: 33.7 us -> 21.2 us  [whole(): pl.pallas_call(kernel, in_specs=[SCALAR if a is tokens else full for a in...]
    unnamed x98 -> x56, local copies, waits for them, and re-layouts: 25.2 us -> 13.1 us
    all_to_all x1, waiting for transfers between devices: 8.94 us -> 15.2 us  [shards(): lax.all_to_all(states, 'ctx', 0, 0, tiled=True).reshape(heads, size, size)]
    all_to_all x0 -> x1, starting transfers between devices: none -> 5.81 us  [shards(): state_low = lax.all_to_all(states, 'ctx', 0, 0, tiled=True)]
    all_to_all x1, waiting for transfers between devices: 3.5 us -> 9.3 us  [shards(): spread = lax.all_to_all(put, 'ctx', 0, 0, tiled=True)]
  transfers between devices with their start and end apart: 37 -> 38, of which waited for: 15 -> 17; matrix products, arithmetic and copies ran while one was open for 1% -> 1% of each run, Pallas kernels for 19% -> 15%
where the time goes in v5:
time: 231 us; the launch traced here: 230 us
  waiting for transfers between devices  107 us (46%)
  starting transfers between devices  61.9 us (27%)
  Pallas kernels  41.8 us (18%)
  local copies, waits for them, and re-layouts  17 us (7%)
    ppermute x6, waiting for transfers between devices, ring(): return lax.ppermute(x, 'ctx', ring_perm(count, 1))  32.8 us
    pallas_call x11, Pallas kernels, whole(): pl.pallas_call(kernel, in_specs=[SCALAR if a is tokens else full for a in...  21.2 us
    ppermute x1, waiting for transfers between devices, shards(): lax.ppermute(weight_own, 'ctx', pair_perm(count, -s))  19.4 us
    all_to_all x1, waiting for transfers between devices, shards(): lax.all_to_all(states, 'ctx', 0, 0, tiled=True).reshape(heads, size, size)  15.2 us
    unnamed x56, local copies, waits for them, and re-layouts  13.1 us
    ppermute x16, starting transfers between devices, over(): return lax.ppermute(x, 'head', perm)  11.3 us
    pallas_call x5, Pallas kernels, product(): pl.pallas_call(functools.partial(product_kernel, [len(x) for x in lots],...  11.3 us
    ppermute x6, starting transfers between devices, ring(): return lax.ppermute(x, 'ctx', ring_perm(count, 1))  11.1 us
  transfers between devices with their start and end apart: 38, of which 17 were waited for; matrix products, arithmetic and copies ran while one was open for 1% of the time, Pallas kernels for 15%

profile of v5, /device:TPU:0, one launch (start us, length us, event | category | flops | bytes accessed | tf_op | source)
XLA Modules:
  0.0 230.2 jit_solution(14733284681376849198)
XLA Ops:
  0.7 2.4 %constant_dynamic-slice_fusion = (bf16[96,3072]{1,0:T(8,128)(2,1)}, bf16[96,3072]{1,0:T(8,128)(2,1)}) fusion(bf16[384,6144]{1,0:T(8,128)(2,1)} %refs_4_.3, s32[]{:T(128)S(6)} %select_n.84), kind=kLoop, calls=%fused_computation.58 | loop fusion | bytes 2359300 | tf_op jit(solution)/shard_map/dynamic_slice | solution.py:362
  3.1 3.0 %collective-permute-start = (bf16[96,3072]{1,0:T(8,128)(2,1)}, bf16[96,3072]{1,0:T(8,128)(2,1)}, u32[]{:S(2)}, u32[]{:S(2)}) collective-permute-start(bf16[96,3072]{1,0:T(8,128)(2,1)} %get-tuple-element.176), channel_id=1, source_target_pairs={{0,8},{4,12},{8,24},{12,28},{24,16},{28,20},{16,0},{20,4},{1,9},{5... | collective-permute-start | bytes 1769480 | tf_op jit(solution)/shard_map/ppermute | solution.py:384
  6.1 2.6 %states.1 = (bf16[8,144,128]{2,1,0:T(8,128)(2,1)}, f32[8,384]{1,0:T(8,128)S(1)}, f32[384,8]{1,0:T(8,128)S(1)}) custom-call(f32[8,384]{1,0:T(8,128)S(1)} %copy-done.20, bf16[384,1024]{1,0:T(8,128)(2,1)S(1)} %copy-done.1, bf16[384,1024]{1,0:T(8,128)(2,1)S(1)} %copy-done.2), custom_call_target="tpu_custom_call" | custom-call | flops 1000 | bytes 1000 | tf_op jit(solution)/shard_map/states/pallas_call | solution.py:373
  8.8 4.8 %all-to-all-start = ((bf16[8,144,128]{2,1,0:T(8,128)(2,1)}), bf16[8,144,128]{2,1,0:T(8,128)(2,1)S(1)}, u32[]{:S(2)}, u32[]{:S(2)}) async-start(bf16[8,144,128]{2,1,0:T(8,128)(2,1)} %get-tuple-element.90), calls=%async_computation | async-start | bytes 589824 | tf_op jit(solution)/shard_map/all_to_all | solution.py:409
  13.6 2.0 collective-permute-start.1
  15.6 1.9 weights.1.intra_ref
  18.6 9.3 %all-to-all-done.in_ref = bf16[8,144,128]{2,1,0:T(8,128)(2,1)S(1)} async-done(((bf16[8,144,128]{2,1,0:T(8,128)(2,1)}), bf16[8,144,128]{2,1,0:T(8,128)(2,1)S(1)}, u32[]{:S(2)}, u32[]{:S(2)}) %all-to-all-start) | async-done | bytes 294944 | tf_op jit(solution)/shard_map/all_to_all | solution.py:409
  27.9 1.9 collective-permute-start.2
  30.5 5.8 %all-to-all-start.1 = ((bf16[8,128,128]{2,1,0:T(8,128)(2,1)}), bf16[8,128,128]{2,1,0:T(8,128)(2,1)S(1)}, u32[]{:S(2)}, u32[]{:S(2)}) async-start(bf16[8,128,128]{2,1,0:T(8,128)(2,1)} %scan.2), calls=%async_computation.1 | async-start | bytes 524288 | tf_op jit(solution)/shard_map/all_to_all | solution.py:417
  37.3 4.8 %collective-permute-done.1 = bf16[96,3072]{1,0:T(8,128)(2,1)} collective-permute-done((bf16[96,3072]{1,0:T(8,128)(2,1)}, bf16[96,3072]{1,0:T(8,128)(2,1)}, u32[]{:S(2)}, u32[]{:S(2)}) %collective-permute-start.1) | collective-permute-done | bytes 589856 | tf_op jit(solution)/shard_map/ppermute | solution.py:384
  42.0 3.3 %all-to-all-done.1.state_ref = bf16[8,128,128]{2,1,0:T(8,128)(2,1)S(1)} async-done(((bf16[8,128,128]{2,1,0:T(8,128)(2,1)}), bf16[8,128,128]{2,1,0:T(8,128)(2,1)S(1)}, u32[]{:S(2)}, u32[]{:S(2)}) %all-to-all-start.1) | async-done | bytes 262176 | tf_op jit(solution)/shard_map/all_to_all | solution.py:417
  49.1 1.5 collective-permute-start.6
  54.0 1.6 collective-permute-start.7
  56.7 8.7 %collective-permute-done.5 = bf16[96,3072]{1,0:T(8,128)(2,1)S(1)} collective-permute-done((bf16[96,3072]{1,0:T(8,128)(2,1)}, bf16[96,3072]{1,0:T(8,128)(2,1)S(1)}, u32[]{:S(2)}, u32[]{:S(2)}) %collective-permute-start.5) | collective-permute-done | bytes 589856 | tf_op jit(solution)/shard_map/ppermute | solution.py:384
  65.6 2.4 %collective-permute-start.8 = (bf16[96,3072]{1,0:T(8,128)(2,1)}, bf16[96,3072]{1,0:T(8,128)(2,1)S(1)}, u32[]{:S(2)}, u32[]{:S(2)}) collective-permute-start(bf16[96,3072]{1,0:T(8,128)(2,1)} %collective-permute-done.1), channel_id=1, source_target_pairs={{0,8},{4,12},{8,24},{12,28},{24,16},{28,20},{16,0},{20,4},{1,9},{5... | collective-permute-start | bytes 1769480 | tf_op jit(solution)/shard_map/ppermute | solution.py:384
  68.0 1.5 collective-permute-start.9
  69.5 1.5 collective-permute-start.15
  72.3 10.1 %collective-permute-done.8 = bf16[96,3072]{1,0:T(8,128)(2,1)S(1)} collective-permute-done((bf16[96,3072]{1,0:T(8,128)(2,1)}, bf16[96,3072]{1,0:T(8,128)(2,1)S(1)}, u32[]{:S(2)}, u32[]{:S(2)}) %collective-permute-start.8) | collective-permute-done | bytes 589856 | tf_op jit(solution)/shard_map/ppermute | solution.py:384
  84.7 1.5 collective-permute-start.13
  86.3 19.4 %collective-permute-done.15.refs_6_.refs_3_.refs_4_ = bf16[128,6144]{1,0:T(8,128)(2,1)S(1)} collective-permute-done((bf16[128,6144]{1,0:T(8,128)(2,1)S(1)}, bf16[128,6144]{1,0:T(8,128)(2,1)S(1)}, u32[]{:S(2)}, u32[]{:S(2)}) %collective-permute-start.15) | collective-permute-done | bytes 1572896 | tf_op jit(solution)/shard_map/ppermute | solution.py:424
  107.6 2.7 %product.6.refs_0_ = bf16[384,256]{1,0:T(8,128)(2,1)S(1)} custom-call(s32[1]{0:T(128)} %bitcast.1.mine_ref.refs_0_, bf16[384,6144]{1,0:T(8,128)(2,1)S(1)} %bitcast.6, bf16[128,6144]{1,0:T(8,128)(2,1)S(1)} %bitcast.8, bf16[128,6144]{1,0:T(8,128)(2,1)S(1)} %collective-permute-done.15.refs_6_.refs_3_.refs_4_), custom_call_target="tpu_custom_call" | custom-call | flops 1000 | bytes 1000 | tf_op jit(solution)/shard_map/product/pallas_call | solution.py:207
  110.3 2.9 %product.5 = bf16[384,256]{1,0:T(8,128)(2,1)S(1)} custom-call(s32[1]{0:T(128)} %bitcast.1.mine_ref.refs_0_, bf16[192,3072]{1,0:T(8,128)(2,1)S(1)} %constant_dynamic-update-slice_fusion.refs_1_.refs_5_, bf16[192,3072]{1,0:T(8,128)(2,1)S(1)} %collective-permute-done.3.refs_2_.refs_6_, ...), custom_call_target="tpu_custom_call" | custom-call | flops 1000 | bytes 1000 | tf_op jit(solution)/shard_map/product/pallas_call | solution.py:207
  113.2 9.2 %collective-permute-done.11 = bf16[96,3072]{1,0:T(8,128)(2,1)S(1)} collective-permute-done((bf16[96,3072]{1,0:T(8,128)(2,1)S(1)}, bf16[96,3072]{1,0:T(8,128)(2,1)S(1)}, u32[]{:S(2)}, u32[]{:S(2)}) %collective-permute-start.11) | collective-permute-done | bytes 589856 | tf_op jit(solution)/shard_map/ppermute | solution.py:384
  123.4 2.9 %collective-permute-start.22 = (bf16[384,256]{1,0:T(8,128)(2,1)S(1)}, bf16[384,256]{1,0:T(8,128)(2,1)S(1)}, u32[]{:S(2)}, u32[]{:S(2)}) collective-permute-start(bf16[384,256]{1,0:T(8,128)(2,1)S(1)} %get-tuple-element.133), channel_id=1, source_target_pairs={{0,24},{4,28},{8,16},{12,20},{24,0},{28,4},{16,8},{20,12},{1,25},{... | collective-permute-start | bytes 589832 | tf_op jit(solution)/shard_map/ppermute | solution.py:447
  126.4 2.8 %product.8 = bf16[384,256]{1,0:T(8,128)(2,1)S(1)} custom-call(s32[1]{0:T(128)} %bitcast.1.mine_ref.refs_0_, bf16[192,3072]{1,0:T(8,128)(2,1)S(1)} %constant_dynamic-update-slice_fusion.4.refs_1_.refs_7_, bf16[192,3072]{1,0:T(8,128)(2,1)S(1)} %collective-permute-done.14.refs_2_.refs_8_, ...), custom_call_target="tpu_custom_call" | custom-call | flops 1000 | bytes 1000 | tf_op jit(solution)/shard_map/product/pallas_call | solution.py:207
  129.3 1.4 product.7.refs_5_
  130.7 9.5 %collective-permute-done.21.refs_1_ = bf16[384,256]{1,0:T(8,128)(2,1)S(1)} collective-permute-done((bf16[384,256]{1,0:T(8,128)(2,1)S(1)}, bf16[384,256]{1,0:T(8,128)(2,1)S(1)}, u32[]{:S(2)}, u32[]{:S(2)}) %collective-permute-start.21) | collective-permute-done | bytes 196640 | tf_op jit(solution)/shard_map/ppermute | solution.py:447
  140.4 3.7 %collective-permute-start.18 = (bf16[384,256]{1,0:T(8,128)(2,1)S(1)}, bf16[384,256]{1,0:T(8,128)(2,1)S(1)}, u32[]{:S(2)}, u32[]{:S(2)}) collective-permute-start(bf16[384,256]{1,0:T(8,128)(2,1)S(1)} %product.5), channel_id=1, source_target_pairs={{0,16},{4,20},{8,0},{12,4},{24,8},{28,12},{16,24},{20,28},{1,17},{... | collective-permute-start | bytes 589832 | tf_op jit(solution)/shard_map/ppermute | solution.py:454
  144.1 2.9 %collective-permute-start.24 = (bf16[384,256]{1,0:T(8,128)(2,1)S(1)}, bf16[384,256]{1,0:T(8,128)(2,1)S(1)}, u32[]{:S(2)}, u32[]{:S(2)}) collective-permute-start(bf16[384,256]{1,0:T(8,128)(2,1)S(1)} %product.8), channel_id=1, source_target_pairs={{0,24},{4,28},{8,16},{12,20},{24,0},{28,4},{16,8},{20,12},{1,25},{... | collective-permute-start | bytes 589832 | tf_op jit(solution)/shard_map/ppermute | solution.py:460
  147.0 1.4 product.9
  148.7 4.7 %outer.2 = (bf16[128,3072]{1,0:T(8,128)(2,1)S(1)}, bf16[128,3072]{1,0:T(8,128)(2,1)S(1)}) custom-call(bf16[384,256]{1,0:T(8,128)(2,1)S(1)} %get-tuple-element.153.refs_0_, bf16[384,256]{1,0:T(8,128)(2,1)S(1)} %collective-permute-done.21.refs_1_, bf16[384,256]{1,0:T(8,128)(2,1)S(1)} %collective-permute-done.22.refs_2_, ...), custom_call_target="tpu_custom_call" | custom-call | flops 1000 | bytes 1000 | tf_op jit(solution)/shard_map/outer/pallas_call | solution.py:247
  154.2 2.7 %collective-permute-done.24.refs_2_ = bf16[384,256]{1,0:T(8,128)(2,1)S(1)} collective-permute-done((bf16[384,256]{1,0:T(8,128)(2,1)S(1)}, bf16[384,256]{1,0:T(8,128)(2,1)S(1)}, u32[]{:S(2)}, u32[]{:S(2)}) %collective-permute-start.24) | collective-permute-done | bytes 196640 | tf_op jit(solution)/shard_map/ppermute | solution.py:460
  156.9 6.8 %collective-permute-done.26.refs_3_ = bf16[384,256]{1,0:T(8,128)(2,1)S(1)} collective-permute-done((bf16[384,256]{1,0:T(8,128)(2,1)S(1)}, bf16[384,256]{1,0:T(8,128)(2,1)S(1)}, u32[]{:S(2)}, u32[]{:S(2)}) %collective-permute-start.26) | collective-permute-done | bytes 196640 | tf_op jit(solution)/shard_map/ppermute | solution.py:465
  166.2 1.5 collective-permute-start.28
  167.7 4.7 %outer.3 = (bf16[128,3072]{1,0:T(8,128)(2,1)S(1)}, bf16[128,3072]{1,0:T(8,128)(2,1)S(1)}) custom-call(bf16[384,256]{1,0:T(8,128)(2,1)S(1)} %get-tuple-element.153.refs_0_, bf16[384,256]{1,0:T(8,128)(2,1)S(1)} %collective-permute-done.21.refs_1_, bf16[384,256]{1,0:T(8,128)(2,1)S(1)} %collective-permute-done.22.refs_2_, ...), custom_call_target="tpu_custom_call" | custom-call | flops 1000 | bytes 1000 | tf_op jit(solution)/shard_map/outer/pallas_call | solution.py:247
  172.5 2.3 %grads.1 = (bf16[384,1024]{1,0:T(8,128)(2,1)S(1)}, bf16[8,144,128]{2,1,0:T(8,128)(2,1)}) custom-call(bf16[384,1024]{1,0:T(8,128)(2,1)S(1)} %get-tuple-element.151.grad_ref, f32[384,1024]{1,0:T(8,128)S(1)} %get-tuple-element.102.attn_ref, f32[1,384]{1,0:T(1,128)S(1)} %get-tuple-element.106.inv_ref, f32[1,384]{1,0:T(1,128)S(1)} %add.141.here_ref, ...), custom_call_target="tpu_custom_call" | custom-call | flops 1000 | bytes 1000 | tf_op jit(solution)/shard_map/grads/pallas_call | solution.py:373
  175.7 3.4 %all-to-all-start.2 = ((bf16[8,144,128]{2,1,0:T(8,128)(2,1)}), bf16[8,144,128]{2,1,0:T(8,128)(2,1)S(1)}, u32[]{:S(2)}, u32[]{:S(2)}) async-start(bf16[8,144,128]{2,1,0:T(8,128)(2,1)} %get-tuple-element.159), calls=%async_computation.2 | async-start | bytes 589824 | tf_op jit(solution)/shard_map/all_to_all | solution.py:484
  179.1 2.0 collective-permute-start.29
  182.4 4.5 %inside.1 = (bf16[384,1024]{1,0:T(8,128)(2,1)}, f32[384,1024]{1,0:T(8,128)S(1)}, f32[384,1024]{1,0:T(8,128)S(1)}) custom-call(bf16[384,1024]{1,0:T(8,128)(2,1)S(1)} %copy-done.18, bf16[384,1024]{1,0:T(8,128)(2,1)S(1)} %copy-done.6, bf16[384,1024]{1,0:T(8,128)(2,1)S(1)} %copy-done.1, bf16[384,1024]{1,0:T(8,128)(2,1)S(1)} %copy-done.3, ...), custom_call_target="tpu_custom_call" | custom-call | flops 1000 | bytes 1000 | tf_op jit(solution)/shard_map/inside/pallas_call | solution.py:373
  189.2 2.0 collective-permute-start.31
  192.0 4.5 %all-to-all-start.3 = ((bf16[8,128,128]{2,1,0:T(8,128)(2,1)}), bf16[8,128,128]{2,1,0:T(8,128)(2,1)S(1)}, u32[]{:S(2)}, u32[]{:S(2)}) async-start(bf16[8,128,128]{2,1,0:T(8,128)(2,1)} %scan.3), calls=%async_computation.3 | async-start | bytes 524288 | tf_op jit(solution)/shard_map/all_to_all | solution.py:493
  196.5 2.0 collective-permute-start.32
  198.5 3.0 %collective-permute-done.32 = f32[1,1024]{1,0:T(1,128)S(1)} collective-permute-done((f32[1,1024]{1,0:T(1,128)S(1)}, f32[1,1024]{1,0:T(1,128)S(1)}, u32[]{:S(2)}, u32[]{:S(2)}) %collective-permute-start.32) | collective-permute-done | bytes 4128 | tf_op jit(solution)/shard_map/ppermute | solution.py:496
  201.5 3.3 %collective-permute-start.33 = (f32[1,1024]{1,0:T(1,128)S(1)}, f32[1,1024]{1,0:T(1,128)S(1)}, u32[]{:S(2)}, u32[]{:S(2)}) collective-permute-start(f32[1,1024]{1,0:T(1,128)S(1)} %add.143), channel_id=1, source_target_pairs={{0,16},{4,20},{8,24},{12,28},{16,0},{20,4},{24,8},{28,12},{1,17},{... | collective-permute-start | bytes 12296 | tf_op jit(solution)/shard_map/ppermute | solution.py:496
  204.8 1.6 collective-permute-done.33
  207.0 15.2 %all-to-all-done.3.state_ref = bf16[8,128,128]{2,1,0:T(8,128)(2,1)S(1)} async-done(((bf16[8,128,128]{2,1,0:T(8,128)(2,1)}), bf16[8,128,128]{2,1,0:T(8,128)(2,1)S(1)}, u32[]{:S(2)}, u32[]{:S(2)}) %all-to-all-start.3) | async-done | bytes 262176 | tf_op jit(solution)/shard_map/all_to_all | solution.py:493
  225.0 2.1 outside.1
  227.1 3.0 %sum.1 = bf16[128,6144]{1,0:T(8,128)(2,1)} custom-call(bf16[128,3072]{1,0:T(8,128)(2,1)S(1)} %copy-done.14, bf16[128,3072]{1,0:T(8,128)(2,1)} %collective-permute-done.30.refs_1_, bf16[128,3072]{1,0:T(8,128)(2,1)S(1)} %copy-done.16, bf16[128,3072]{1,0:T(8,128)(2,1)} %collective-permute-done.31.refs_3_), custom_call_target="tpu_custom_call" | custom-call | flops 1000 | bytes 1000 | tf_op jit(solution)/shard_map/sum/pallas_call | solution.py:373
  (117 shorter events, 30.2 us)
Async XLA Ops:
  0.6 5.5 %copy-start.1 = (bf16[384,1024]{1,0:T(8,128)(2,1)S(1)}, bf16[384,1024]{1,0:T(8,128)(2,1)}, u32[]{:S(2)}) copy-start(bf16[384,1024]{1,0:T(8,128)(2,1)} %k_ref.7) | copy-start | bytes 2359300
  0.6 5.5 %copy-start.2 = (bf16[384,1024]{1,0:T(8,128)(2,1)S(1)}, bf16[384,1024]{1,0:T(8,128)(2,1)}, u32[]{:S(2)}) copy-start(bf16[384,1024]{1,0:T(8,128)(2,1)} %v_ref.7) | copy-start | bytes 2359300
  3.1 12.5 %copy-start.4 = (bf16[384,1024]{1,0:T(8,128)(2,1)S(1)}, bf16[384,1024]{1,0:T(8,128)(2,1)}, u32[]{:S(2)}) copy-start(bf16[384,1024]{1,0:T(8,128)(2,1)} %q_ref.7) | copy-start | bytes 2359300
  3.1 24.8 %collective-permute-start = (bf16[96,3072]{1,0:T(8,128)(2,1)}, bf16[96,3072]{1,0:T(8,128)(2,1)}, u32[]{:S(2)}, u32[]{:S(2)}) collective-permute-start(bf16[96,3072]{1,0:T(8,128)(2,1)} %get-tuple-element.176), channel_id=1, source_target_pairs={{0,8},{4,12},{8,24},{12,28},{24,16},{28,20},{16,0},{20,4},{1,9},{5... | collective-permute-start | bytes 1769480 | tf_op jit(solution)/shard_map/ppermute | solution.py:384
  8.8 19.1 %all-to-all-start = ((bf16[8,144,128]{2,1,0:T(8,128)(2,1)}), bf16[8,144,128]{2,1,0:T(8,128)(2,1)S(1)}, u32[]{:S(2)}, u32[]{:S(2)}) async-start(bf16[8,144,128]{2,1,0:T(8,128)(2,1)} %get-tuple-element.90), calls=%async_computation | async-start | bytes 589824 | tf_op jit(solution)/shard_map/all_to_all | solution.py:409
  13.6 28.5 %collective-permute-start.1 = (bf16[96,3072]{1,0:T(8,128)(2,1)}, bf16[96,3072]{1,0:T(8,128)(2,1)}, u32[]{:S(2)}, u32[]{:S(2)}) collective-permute-start(bf16[96,3072]{1,0:T(8,128)(2,1)} %get-tuple-element.94), channel_id=1, source_target_pairs={{0,8},{4,12},{8,24},{12,28},{24,16},{28,20},{16,0},{20,4},{1,9},{5... | collective-permute-start | bytes 1769480 | tf_op jit(solution)/shard_map/ppermute | solution.py:384
  27.9 17.4 %collective-permute-start.2 = (bf16[96,3072]{1,0:T(8,128)(2,1)}, bf16[96,3072]{1,0:T(8,128)(2,1)}, u32[]{:S(2)}, u32[]{:S(2)}) collective-permute-start(bf16[96,3072]{1,0:T(8,128)(2,1)} %collective-permute-done), channel_id=1, source_target_pairs={{0,2},{1,3},{2,0},{3,1},{4,6},{5,7},{6,4},{7,5},{8,10},{9,11},{10,... | collective-permute-start | bytes 1769480 | tf_op jit(solution)/shard_map/ppermute | solution.py:387
  30.5 14.8 %all-to-all-start.1 = ((bf16[8,128,128]{2,1,0:T(8,128)(2,1)}), bf16[8,128,128]{2,1,0:T(8,128)(2,1)S(1)}, u32[]{:S(2)}, u32[]{:S(2)}) async-start(bf16[8,128,128]{2,1,0:T(8,128)(2,1)} %scan.2), calls=%async_computation.1 | async-start | bytes 524288 | tf_op jit(solution)/shard_map/all_to_all | solution.py:417
  46.5 61.1 %slice-start = ((s8[4718592]{0:T(1024)(128)(4,1)}), s8[4194304]{0:T(1024)(128)(4,1)S(1)}, s32[]{:S(2)}) async-start(s8[4718592]{0:T(1024)(128)(4,1)} %bitcast.5), calls=%async_computation.4 | async-start | bytes 8388608
  47.8 2.9 %collective-permute-start.3 = (bf16[192,3072]{1,0:T(8,128)(2,1)S(1)}, bf16[192,3072]{1,0:T(8,128)(2,1)S(1)}, u32[]{:S(2)}, u32[]{:S(2)}) collective-permute-start(bf16[192,3072]{1,0:T(8,128)(2,1)S(1)} %constant_dynamic-update-slice_fusion.refs_1_.refs_5_), channel_id=1, source_target_pairs={{0,1},{1,0},{2,3},{3,2},{4,5},{5,4},{6,7},{7,6},{8,9},{9,8},{10,11... | collective-permute-start | bytes 3538952 | tf_op jit(solution)/shard_map/ppermute | solution.py:387
  47.8 17.6 %collective-permute-start.5 = (bf16[96,3072]{1,0:T(8,128)(2,1)}, bf16[96,3072]{1,0:T(8,128)(2,1)S(1)}, u32[]{:S(2)}, u32[]{:S(2)}) collective-permute-start(bf16[96,3072]{1,0:T(8,128)(2,1)} %collective-permute-done), channel_id=1, source_target_pairs={{0,8},{4,12},{8,24},{12,28},{24,16},{28,20},{16,0},{20,4},{1,9},{5... | collective-permute-start | bytes 1769480 | tf_op jit(solution)/shard_map/ppermute | solution.py:384
  49.1 16.3 %collective-permute-start.6 = (bf16[96,3072]{1,0:T(8,128)(2,1)}, bf16[96,3072]{1,0:T(8,128)(2,1)S(1)}, u32[]{:S(2)}, u32[]{:S(2)}) collective-permute-start(bf16[96,3072]{1,0:T(8,128)(2,1)} %collective-permute-done.1), channel_id=1, source_target_pairs={{0,2},{1,3},{2,0},{3,1},{4,6},{5,7},{6,4},{7,5},{8,10},{9,11},{10,... | collective-permute-start | bytes 1769480 | tf_op jit(solution)/shard_map/ppermute | solution.py:387
  52.8 1.2 collective-permute-start.4
  54.0 15.5 %copy-start = (bf16[8,16,6144]{2,1,0:T(8,128)(2,1)S(1)}, bf16[8,16,6144]{2,1,0:T(8,128)(2,1)}, u32[]{:S(2)}) copy-start(bf16[8,16,6144]{2,1,0:T(8,128)(2,1)} %param.12) | copy-start | bytes 4718596
  54.0 11.4 %collective-permute-start.7 = (f32[1,384]{1,0:T(1,128)S(1)}, f32[1,384]{1,0:T(1,128)S(1)}, u32[]{:S(2)}, u32[]{:S(2)}) collective-permute-start(f32[1,384]{1,0:T(1,128)S(1)} %add.140.here_ref), channel_id=1, source_target_pairs={{0,2},{1,3},{2,0},{3,1},{4,6},{5,7},{6,4},{7,5},{8,10},{9,11},{10,... | collective-permute-start | bytes 4616 | tf_op jit(solution)/shard_map/ppermute | solution.py:387
  56.7 14.3 %copy-start.19 = (f32[1024]{0:T(1024)S(1)}, f32[1024]{0:T(1024)}, u32[]{:S(2)}) copy-start(f32[1024]{0:T(1024)} %param.11) | copy-start | bytes 12292
  65.5 42.1 %slice-start.1 = ((s8[4718592]{0:T(1024)(128)(4,1)}), s8[524288]{0:T(1024)(128)(4,1)S(1)}, s32[]{:S(2)}) async-start(s8[4718592]{0:T(1024)(128)(4,1)} %bitcast.5), calls=%async_computation.5 | async-start | bytes 1048576
  65.5 17.9 %collective-permute-start.10 = (bf16[192,3072]{1,0:T(8,128)(2,1)S(1)}, bf16[192,3072]{1,0:T(8,128)(2,1)S(1)}, u32[]{:S(2)}, u32[]{:S(2)}) collective-permute-start(bf16[192,3072]{1,0:T(8,128)(2,1)S(1)} %constant_dynamic-update-slice_fusion.2.refs_3_.refs_5_), channel_id=1, source_target_pairs={{0,1},{1,0},{2,3},{3,2},{4,5},{5,4},{6,7},{7,6},{8,9},{9,8},{10,11... | collective-permute-start | bytes 3538952 | tf_op jit(solution)/shard_map/ppermute | solution.py:387
  65.6 16.8 %collective-permute-start.8 = (bf16[96,3072]{1,0:T(8,128)(2,1)}, bf16[96,3072]{1,0:T(8,128)(2,1)S(1)}, u32[]{:S(2)}, u32[]{:S(2)}) collective-permute-start(bf16[96,3072]{1,0:T(8,128)(2,1)} %collective-permute-done.1), channel_id=1, source_target_pairs={{0,8},{4,12},{8,24},{12,28},{24,16},{28,20},{16,0},{20,4},{1,9},{5... | collective-permute-start | bytes 1769480 | tf_op jit(solution)/shard_map/ppermute | solution.py:384
  68.0 15.4 %collective-permute-start.9 = (bf16[96,3072]{1,0:T(8,128)(2,1)S(1)}, bf16[96,3072]{1,0:T(8,128)(2,1)S(1)}, u32[]{:S(2)}, u32[]{:S(2)}) collective-permute-start(bf16[96,3072]{1,0:T(8,128)(2,1)S(1)} %collective-permute-done.5), channel_id=1, source_target_pairs={{0,2},{1,3},{2,0},{3,1},{4,6},{5,7},{6,4},{7,5},{8,10},{9,11},{10,... | collective-permute-start | bytes 1769480 | tf_op jit(solution)/shard_map/ppermute | solution.py:387
  69.5 36.2 %collective-permute-start.15 = (bf16[128,6144]{1,0:T(8,128)(2,1)S(1)}, bf16[128,6144]{1,0:T(8,128)(2,1)S(1)}, u32[]{:S(2)}, u32[]{:S(2)}) collective-permute-start(bf16[128,6144]{1,0:T(8,128)(2,1)S(1)} %bitcast.7), channel_id=1, source_target_pairs={{0,4},{4,0},{8,12},{12,8},{16,20},{20,16},{24,28},{28,24},{1,5},{5... | collective-permute-start | bytes 4718600 | tf_op jit(solution)/shard_map/ppermute | solution.py:424
  83.4 22.3 %collective-permute-start.14 = (bf16[192,3072]{1,0:T(8,128)(2,1)S(1)}, bf16[192,3072]{1,0:T(8,128)(2,1)S(1)}, u32[]{:S(2)}, u32[]{:S(2)}) collective-permute-start(bf16[192,3072]{1,0:T(8,128)(2,1)S(1)} %constant_dynamic-update-slice_fusion.4.refs_1_.refs_7_), channel_id=1, source_target_pairs={{0,1},{1,0},{2,3},{3,2},{4,5},{5,4},{6,7},{7,6},{8,9},{9,8},{10,11... | collective-permute-start | bytes 3538952 | tf_op jit(solution)/shard_map/ppermute | solution.py:387
  83.5 22.2 %collective-permute-start.12 = (bf16[96,3072]{1,0:T(8,128)(2,1)S(1)}, bf16[96,3072]{1,0:T(8,128)(2,1)S(1)}, u32[]{:S(2)}, u32[]{:S(2)}) collective-permute-start(bf16[96,3072]{1,0:T(8,128)(2,1)S(1)} %collective-permute-done.5), channel_id=1, source_target_pairs={{0,8},{4,12},{8,24},{12,28},{24,16},{28,20},{16,0},{20,4},{1,9},{5... | collective-permute-start | bytes 1769480 | tf_op jit(solution)/shard_map/ppermute | solution.py:384
  84.7 21.0 %collective-permute-start.13 = (bf16[96,3072]{1,0:T(8,128)(2,1)S(1)}, bf16[96,3072]{1,0:T(8,128)(2,1)S(1)}, u32[]{:S(2)}, u32[]{:S(2)}) collective-permute-start(bf16[96,3072]{1,0:T(8,128)(2,1)S(1)} %collective-permute-done.8), channel_id=1, source_target_pairs={{0,2},{1,3},{2,0},{3,1},{4,6},{5,7},{6,4},{7,5},{8,10},{9,11},{10,... | collective-permute-start | bytes 1769480 | tf_op jit(solution)/shard_map/ppermute | solution.py:387
  105.7 16.7 %collective-permute-start.17 = (bf16[192,3072]{1,0:T(8,128)(2,1)S(1)}, bf16[192,3072]{1,0:T(8,128)(2,1)S(1)}, u32[]{:S(2)}, u32[]{:S(2)}) collective-permute-start(bf16[192,3072]{1,0:T(8,128)(2,1)S(1)} %constant_dynamic-update-slice_fusion.6.refs_3_.refs_7_), channel_id=1, source_target_pairs={{0,1},{1,0},{2,3},{3,2},{4,5},{5,4},{6,7},{7,6},{8,9},{9,8},{10,11... | collective-permute-start | bytes 3538952 | tf_op jit(solution)/shard_map/ppermute | solution.py:387
  105.8 16.6 %collective-permute-start.11 = (bf16[96,3072]{1,0:T(8,128)(2,1)S(1)}, bf16[96,3072]{1,0:T(8,128)(2,1)S(1)}, u32[]{:S(2)}, u32[]{:S(2)}) collective-permute-start(bf16[96,3072]{1,0:T(8,128)(2,1)S(1)} %collective-permute-done.8), channel_id=1, source_target_pairs={{0,8},{4,12},{8,24},{12,28},{24,16},{28,20},{16,0},{20,4},{1,9},{5... | collective-permute-start | bytes 1769480 | tf_op jit(solution)/shard_map/ppermute | solution.py:384
  107.0 15.4 %collective-permute-start.16 = (bf16[96,3072]{1,0:T(8,128)(2,1)S(1)}, bf16[96,3072]{1,0:T(8,128)(2,1)S(1)}, u32[]{:S(2)}, u32[]{:S(2)}) collective-permute-start(bf16[96,3072]{1,0:T(8,128)(2,1)S(1)} %collective-permute-done.12), channel_id=1, source_target_pairs={{0,2},{1,3},{2,0},{3,1},{4,6},{5,7},{6,4},{7,5},{8,10},{9,11},{10,... | collective-permute-start | bytes 1769480 | tf_op jit(solution)/shard_map/ppermute | solution.py:387
  122.5 6.7 %collective-permute-start.20 = (bf16[192,3072]{1,0:T(8,128)(2,1)S(1)}, bf16[192,3072]{1,0:T(8,128)(2,1)S(1)}, u32[]{:S(2)}, u32[]{:S(2)}) collective-permute-start(bf16[192,3072]{1,0:T(8,128)(2,1)S(1)} %constant_dynamic-update-slice_fusion.8.refs_1_.refs_9_), channel_id=1, source_target_pairs={{0,1},{1,0},{2,3},{3,2},{4,5},{5,4},{6,7},{7,6},{8,9},{9,8},{10,11... | collective-permute-start | bytes 3538952 | tf_op jit(solution)/shard_map/ppermute | solution.py:387
  122.6 17.7 %collective-permute-start.19 = (bf16[96,3072]{1,0:T(8,128)(2,1)S(1)}, bf16[96,3072]{1,0:T(8,128)(2,1)S(1)}, u32[]{:S(2)}, u32[]{:S(2)}) collective-permute-start(bf16[96,3072]{1,0:T(8,128)(2,1)S(1)} %collective-permute-done.11), channel_id=1, source_target_pairs={{0,2},{1,3},{2,0},{3,1},{4,6},{5,7},{6,4},{7,5},{8,10},{9,11},{10,... | collective-permute-start | bytes 1769480 | tf_op jit(solution)/shard_map/ppermute | solution.py:387
  123.2 17.1 %collective-permute-start.21 = (bf16[384,256]{1,0:T(8,128)(2,1)S(1)}, bf16[384,256]{1,0:T(8,128)(2,1)S(1)}, u32[]{:S(2)}, u32[]{:S(2)}) collective-permute-start(bf16[384,256]{1,0:T(8,128)(2,1)S(1)} %get-tuple-element.132), channel_id=1, source_target_pairs={{0,8},{4,12},{8,24},{12,28},{24,16},{28,20},{16,0},{20,4},{1,9},{5... | collective-permute-start | bytes 589832 | tf_op jit(solution)/shard_map/ppermute | solution.py:447
  123.4 16.8 %collective-permute-start.22 = (bf16[384,256]{1,0:T(8,128)(2,1)S(1)}, bf16[384,256]{1,0:T(8,128)(2,1)S(1)}, u32[]{:S(2)}, u32[]{:S(2)}) collective-permute-start(bf16[384,256]{1,0:T(8,128)(2,1)S(1)} %get-tuple-element.133), channel_id=1, source_target_pairs={{0,24},{4,28},{8,16},{12,20},{24,0},{28,4},{16,8},{20,12},{1,25},{... | collective-permute-start | bytes 589832 | tf_op jit(solution)/shard_map/ppermute | solution.py:447
  126.4 13.9 %collective-permute-start.23 = (bf16[384,256]{1,0:T(8,128)(2,1)S(1)}, bf16[384,256]{1,0:T(8,128)(2,1)S(1)}, u32[]{:S(2)}, u32[]{:S(2)}) collective-permute-start(bf16[384,256]{1,0:T(8,128)(2,1)S(1)} %get-tuple-element.134), channel_id=1, source_target_pairs={{0,16},{4,20},{8,0},{12,4},{24,8},{28,12},{16,24},{20,28},{1,17},{... | collective-permute-start | bytes 589832 | tf_op jit(solution)/shard_map/ppermute | solution.py:447
  140.3 6.7 %collective-permute-start.25 = (bf16[192,3072]{1,0:T(8,128)(2,1)S(1)}, bf16[192,3072]{1,0:T(8,128)(2,1)S(1)}, u32[]{:S(2)}, u32[]{:S(2)}) collective-permute-start(bf16[192,3072]{1,0:T(8,128)(2,1)S(1)} %constant_dynamic-update-slice_fusion.10.refs_1_.refs_9_), channel_id=1, source_target_pairs={{0,1},{1,0},{2,3},{3,2},{4,5},{5,4},{6,7},{7,6},{8,9},{9,8},{10,11... | collective-permute-start | bytes 3538952 | tf_op jit(solution)/shard_map/ppermute | solution.py:387
  140.4 13.9 %collective-permute-start.18 = (bf16[384,256]{1,0:T(8,128)(2,1)S(1)}, bf16[384,256]{1,0:T(8,128)(2,1)S(1)}, u32[]{:S(2)}, u32[]{:S(2)}) collective-permute-start(bf16[384,256]{1,0:T(8,128)(2,1)S(1)} %product.5), channel_id=1, source_target_pairs={{0,16},{4,20},{8,0},{12,4},{24,8},{28,12},{16,24},{20,28},{1,17},{... | collective-permute-start | bytes 589832 | tf_op jit(solution)/shard_map/ppermute | solution.py:454
  144.1 12.9 %collective-permute-start.24 = (bf16[384,256]{1,0:T(8,128)(2,1)S(1)}, bf16[384,256]{1,0:T(8,128)(2,1)S(1)}, u32[]{:S(2)}, u32[]{:S(2)}) collective-permute-start(bf16[384,256]{1,0:T(8,128)(2,1)S(1)} %product.8), channel_id=1, source_target_pairs={{0,24},{4,28},{8,16},{12,20},{24,0},{28,4},{16,8},{20,12},{1,25},{... | collective-permute-start | bytes 589832 | tf_op jit(solution)/shard_map/ppermute | solution.py:460
  148.4 15.4 %collective-permute-start.26 = (bf16[384,256]{1,0:T(8,128)(2,1)S(1)}, bf16[384,256]{1,0:T(8,128)(2,1)S(1)}, u32[]{:S(2)}, u32[]{:S(2)}) collective-permute-start(bf16[384,256]{1,0:T(8,128)(2,1)S(1)} %product.9), channel_id=1, source_target_pairs={{0,8},{4,12},{8,24},{12,28},{24,16},{28,20},{16,0},{20,4},{1,9},{5... | collective-permute-start | bytes 589832 | tf_op jit(solution)/shard_map/ppermute | solution.py:465
  154.2 10.7 %copy-start.21 = (bf16[128,3072]{1,0:T(8,128)(2,1)}, bf16[128,3072]{1,0:T(8,128)(2,1)S(1)}, u32[]{:S(2)}) copy-start(bf16[128,3072]{1,0:T(8,128)(2,1)S(1)} %get-tuple-element.171) | copy-start | bytes 2359300
  165.0 1.2 collective-permute-start.27
  166.2 6.3 %collective-permute-start.28 = (f32[1,384]{1,0:T(1,128)S(1)}, f32[1,384]{1,0:T(1,128)S(1)}, u32[]{:S(2)}, u32[]{:S(2)}) collective-permute-start(f32[1,384]{1,0:T(1,128)S(1)} %add.141.here_ref), channel_id=1, source_target_pairs={{0,2},{1,3},{2,0},{3,1},{4,6},{5,7},{6,4},{7,5},{8,10},{9,11},{10,... | collective-permute-start | bytes 4616 | tf_op jit(solution)/shard_map/ppermute | solution.py:387
  172.5 8.8 %copy-start.3 = (bf16[384,1024]{1,0:T(8,128)(2,1)S(1)}, bf16[384,1024]{1,0:T(8,128)(2,1)}, u32[]{:S(2)}) copy-start(bf16[384,1024]{1,0:T(8,128)(2,1)} %v_ref.7) | copy-start | bytes 2359300
  172.5 8.7 %copy-start.6 = (bf16[384,1024]{1,0:T(8,128)(2,1)S(1)}, bf16[384,1024]{1,0:T(8,128)(2,1)}, u32[]{:S(2)}) copy-start(bf16[384,1024]{1,0:T(8,128)(2,1)} %q_ref.7) | copy-start | bytes 2359300
  175.7 13.5 %all-to-all-start.2 = ((bf16[8,144,128]{2,1,0:T(8,128)(2,1)}), bf16[8,144,128]{2,1,0:T(8,128)(2,1)S(1)}, u32[]{:S(2)}, u32[]{:S(2)}) async-start(bf16[8,144,128]{2,1,0:T(8,128)(2,1)} %get-tuple-element.159), calls=%async_computation.2 | async-start | bytes 589824 | tf_op jit(solution)/shard_map/all_to_all | solution.py:484
  179.1 10.1 %collective-permute-start.29 = (f32[1,1024]{1,0:T(1,128)S(1)}, f32[1,1024]{1,0:T(1,128)S(1)}, u32[]{:S(2)}, u32[]{:S(2)}) collective-permute-start(f32[1,1024]{1,0:T(1,128)S(1)} %get-tuple-element.164), channel_id=1, source_target_pairs={{0,4},{4,0},{8,12},{12,8},{16,20},{20,16},{24,28},{28,24},{1,5},{5... | collective-permute-start | bytes 12296 | tf_op jit(solution)/shard_map/ppermute | solution.py:475
  181.1 46.0 %collective-permute-start.30 = (bf16[128,3072]{1,0:T(8,128)(2,1)}, bf16[128,3072]{1,0:T(8,128)(2,1)}, u32[]{:S(2)}, u32[]{:S(2)}) collective-permute-start(bf16[128,3072]{1,0:T(8,128)(2,1)} %copy-done.21), channel_id=1, source_target_pairs={{0,4},{4,0},{8,12},{12,8},{16,20},{20,16},{24,28},{28,24},{1,5},{5... | collective-permute-start | bytes 2359304 | tf_op jit(solution)/shard_map/ppermute | solution.py:470
  189.2 37.9 %collective-permute-start.31 = (bf16[128,3072]{1,0:T(8,128)(2,1)}, bf16[128,3072]{1,0:T(8,128)(2,1)}, u32[]{:S(2)}, u32[]{:S(2)}) collective-permute-start(bf16[128,3072]{1,0:T(8,128)(2,1)} %copy-done.22), channel_id=1, source_target_pairs={{0,4},{4,0},{8,12},{12,8},{16,20},{20,16},{24,28},{28,24},{1,5},{5... | collective-permute-start | bytes 2359304 | tf_op jit(solution)/shard_map/ppermute | solution.py:491
  192.0 30.2 %all-to-all-start.3 = ((bf16[8,128,128]{2,1,0:T(8,128)(2,1)}), bf16[8,128,128]{2,1,0:T(8,128)(2,1)S(1)}, u32[]{:S(2)}, u32[]{:S(2)}) async-start(bf16[8,128,128]{2,1,0:T(8,128)(2,1)} %scan.3), calls=%async_computation.3 | async-start | bytes 524288 | tf_op jit(solution)/shard_map/all_to_all | solution.py:493
  196.5 5.0 %collective-permute-start.32 = (f32[1,1024]{1,0:T(1,128)S(1)}, f32[1,1024]{1,0:T(1,128)S(1)}, u32[]{:S(2)}, u32[]{:S(2)}) collective-permute-start(f32[1,1024]{1,0:T(1,128)S(1)} %add.142), channel_id=1, source_target_pairs={{0,8},{4,12},{8,0},{12,4},{16,24},{20,28},{24,16},{28,20},{1,9},{5... | collective-permute-start | bytes 12296 | tf_op jit(solution)/shard_map/ppermute | solution.py:496
  201.5 4.9 %collective-permute-start.33 = (f32[1,1024]{1,0:T(1,128)S(1)}, f32[1,1024]{1,0:T(1,128)S(1)}, u32[]{:S(2)}, u32[]{:S(2)}) collective-permute-start(f32[1,1024]{1,0:T(1,128)S(1)} %add.143), channel_id=1, source_target_pairs={{0,16},{4,20},{8,24},{12,28},{16,0},{20,4},{24,8},{28,12},{1,17},{... | collective-permute-start | bytes 12296 | tf_op jit(solution)/shard_map/ppermute | solution.py:496
  (15 other events, 30.4 us)

commit v6 on v5

--- a/solution.py
+++ b/solution.py
@@ -9,7 +9,7 @@
 
 LINE = 4
 CHUNKS = 2
-RELATIVE = (0, 2, 1, 3)
+QUARTERS = 4
 FL = jnp.float32
 BF = jnp.bfloat16
 PARAMS = pltpu.CompilerParams(vmem_limit_bytes=20 * 1024 * 1024)
@@ -145,25 +145,25 @@
     normed = (attn_ref[...] * turned_row(inv) * gain_ref[...]).astype(BF)
     tok, width = normed.shape
     span = width // LINE
-    quarter = tok // len(RELATIVE)
+    quarter = tok // QUARTERS
     own_ref[...] = dot(normed, order_ref[:, :span], NN).astype(BF)
     for s, ref in enumerate(sent, 1):
         part = dot(normed, order_ref[:, s * span : (s + 1) * span], NN).astype(BF)
-        for j in range(len(RELATIVE)):
-            turn = mine_ref[0] ^ j
-            to = pl.multiple_of(((turn & 1) * 2 + (turn >> 1)) * quarter, 16)
+        for j in range(QUARTERS):
+            to = pl.multiple_of((mine_ref[0] ^ j) * quarter, 16)
             ref[pl.ds(to, quarter), :] = part[j * quarter : (j + 1) * quarter]
 
 
-def product_kernel(lots, weights, add, last, *refs):
+def product_kernel(lots, others, add, last, whole, *refs):
     refs = list(refs)
     mine_ref = refs.pop(0)
-    x = [[refs.pop(0) for _ in range(k)] for k in lots]
-    w = [refs.pop(0) for _ in range(weights)]
+    x = [[refs.pop(0) for _ in range(lots)] for _ in others]
+    own_ref = refs.pop(0)
+    w = [[refs.pop(0) for _ in range(k)] for k in others]
     extra = refs.pop(0) if add else None
     out_ref, held_ref = refs
     step = pl.program_id(0)
-    steps = pl.num_programs(0) // len(lots)
+    steps = pl.num_programs(0) // len(others)
 
     @pl.when(step == 0)
     def _():
@@ -174,42 +174,48 @@
         @pl.when(step // steps == at)
         def _():
             rows = jnp.concatenate([r[...] for r in lot], axis=0)
-            cols = jnp.concatenate([r[...] for r in w], axis=0)
+            cols = jnp.concatenate([own_ref[...]] + [r[...] for r in w[at]], axis=0)
             held_ref[...] += dot(rows, cols, NT)
 
     @pl.when(step == pl.num_programs(0) - 1)
     def _():
         if not last:
             out_ref[...] = held_ref[...]
-        elif lots[0] == 1:
+        elif whole:
             out_ref[...] = held_ref[...].astype(BF)
         else:
-            quarter = out_ref.shape[0] // len(RELATIVE)
-            for i, turn in enumerate(RELATIVE):
-                to = pl.multiple_of((mine_ref[0] ^ turn) * quarter, 16)
+            quarter = out_ref.shape[0] // QUARTERS
+            for j in range(QUARTERS):
+                to = pl.multiple_of((mine_ref[0] ^ j) * quarter, 16)
                 out_ref[pl.ds(to, quarter), :] = held_ref[
-                    i * quarter : (i + 1) * quarter, :
+                    j * quarter : (j + 1) * quarter, :
                 ].astype(BF)
 
 
-def product(mine, lots, weights, chunk, last, held):
+def product(mine, lots, weight, others, chunk, last, held, whole=False):
     tok = sum(p.shape[0] for p in lots[0])
-    deep = lots[0][0].shape[1]
+    deep = weight.shape[1] // CHUNKS
     tile = 1536
     steps = deep // tile
-    span = sum(w.shape[0] for w in weights)
+    others = others[chunk : chunk + len(lots)]
+    span = weight.shape[0] + sum(w.shape[0] for w in others[0])
     base = chunk * steps
     more = [] if held is None else [held]
 
-    def piece_spec(at, p):
-        return spec((p.shape[0], tile), lambda i: (0, jnp.clip(i - at * steps, 0, steps - 1)))
+    def part(at, p, offset=0):
+        return spec(
+            (p.shape[0], tile), lambda i: (0, offset + jnp.clip(i - at * steps, 0, steps - 1))
+        )
 
     return pl.pallas_call(
-        functools.partial(product_kernel, [len(x) for x in lots], len(weights), len(more), last),
+        functools.partial(
+            product_kernel, len(lots[0]), [len(w) for w in others], len(more), last, whole
+        ),
         grid=(steps * len(lots),),
         in_specs=[SCALAR]
-        + [piece_spec(at, p) for at, lot in enumerate(lots) for p in lot]
-        + [spec((w.shape[0], tile), lambda i: (0, base + i)) for w in weights]
+        + [part(at, p, at * steps if whole else 0) for at, lot in enumerate(lots) for p in lot]
+        + [spec((weight.shape[0], tile), lambda i: (0, base + i))]
+        + [part(at, w) for at, ws in enumerate(others) for w in ws]
         + [spec((tok, span)) for _ in more],
         out_specs=spec((tok, span)),
         out_shape=jax.ShapeDtypeStruct((tok, span), BF if last else FL),
@@ -217,7 +223,7 @@
         compiler_params=PARAMS,
         cost_estimate=TINY,
         name="product",
-    )(mine, *[p for lot in lots for p in lot], *weights, *more)
+    )(mine, *[p for lot in lots for p in lot], weight, *[w for ws in others for w in ws], *more)
 
 
 def outer_kernel(lots, own, *refs):
@@ -358,8 +364,8 @@
     deep = model // CHUNKS
     tokens = mine.reshape(1)
 
-    def first_piece(c):
-        return lax.dynamic_slice(grad_out, (mine * quarter, c * deep), (quarter, deep))
+    def first_piece(x, c):
+        return lax.dynamic_slice(x, (mine * quarter, c * deep), (quarter, deep))
 
     put_shape = jax.ShapeDtypeStruct((count, rows + 16, size), BF)
     wide_f = jax.ShapeDtypeStruct((tok, width), FL)
@@ -392,82 +398,95 @@
     def other_of(x):
         return over(x, over_y)
 
-    def core_of(x, y):
-        both = jnp.concatenate([x, y], axis=0)
-        return both, near_of(both)
-
     hold = lax.optimization_barrier
     scan_shape = jax.ShapeDtypeStruct((count, rows, size), BF)
 
-    ra1 = ring(first_piece(0))
+    ra1 = ring(first_piece(grad_out, 0))
     put, run, turned = whole(
         state_kernel,
         [put_shape, jax.ShapeDtypeStruct((heads, tok), FL), jax.ShapeDtypeStruct((tok, heads), FL)],
         "states", log_decay, key_rows, value_rows,
     )
-    rb1 = ring(after(first_piece(1), put))
     spread = lax.all_to_all(put, "ctx", 0, 0, tiled=True)
+    first = first_piece(after(grad_out, put), 1)
     intra = whole(
         weights_kernel, wide_f, "weights", query_rows, key_rows, value_rows, run, turned
     )
-    ra1, spread, intra = hold((ra1, spread, intra))
-
-    ya1 = other_of(ra1)
+    ra1, spread, intra, first = hold((ra1, spread, intra, first))
+
+    rb1, ya1, na1 = ring(first), other_of(ra1), near_of(ra1)
     states = whole(functools.partial(scan_kernel, False), scan_shape, "scan", spread)
     state_low = lax.all_to_all(states, "ctx", 0, 0, tiled=True)
     order = feature_order(heads, size, count)
-    ra1, rb1, ya1, state_low, weight_own, order = hold(
-        (ra1, rb1, ya1, state_low, weight_own, order)
-    )
-
-    ra2, rb2, yb1, (da1, ca1) = ring(ra1), ring(rb1), other_of(rb1), core_of(ra1, ya1)
-    weights = [lax.ppermute(weight_own, "ctx", pair_perm(count, -s)) for s in range(1, minor)]
-    ca1, state_low = hold((ca1, state_low))
+    halves = [
+        after(weight_own, states)[:, c * deep : (c + 1) * deep] for c in range(CHUNKS)
+    ]
+    ra1, rb1, ya1, na1, state_low, order, halves = hold(
+        (ra1, rb1, ya1, na1, state_low, order, halves)
+    )
+
+    ra2, yb1, nb1, fa1 = ring(ra1), other_of(rb1), near_of(rb1), near_of(ya1)
+    others = [[lax.ppermute(halves[0], "ctx", pair_perm(count, -s)) for s in range(1, minor)]]
+    fa1, state_low = hold((fa1, state_low))
     state_low = state_low.reshape(heads, size, size)
     attn_out, squares = whole(
         attend_kernel, [wide_f, row_f], "attend", query_rows, state_low, turned, intra
     )
     squares = squares + near_of(squares)
     squares_there = other_of(squares)
-    ra2, yb1, squares_there = hold((ra2, yb1, squares_there))
-
-    ra3, ya2, (db1, cb1) = ring(ra2), other_of(ra2), core_of(rb1, yb1)
+    ra2, rb1, yb1, nb1, others[0], squares_there = hold(
+        (ra2, rb1, yb1, nb1, others[0], squares_there)
+    )
+
+    rb2, ya2, na2, fb1 = ring(rb1), other_of(ra2), near_of(ra2), near_of(yb1)
+    others.append([lax.ppermute(halves[1], "ctx", pair_perm(count, -s)) for s in range(1, minor)])
     inv_rms, *sent = whole(
         functools.partial(norm_kernel, features), [row_f] + [part_b] * LINE, "norm",
         tokens, attn_out, squares, squares_there, gain_row, order,
     )
-    rb2, ya2, cb1, sent = hold((rb2, ya2, cb1, sent))
-
-    rb3, yb2, (da2, ca2) = ring(rb2), other_of(rb2), core_of(ra2, ya2)
-    ra3, yb2, ca2, weights, sent = hold((ra3, yb2, ca2, weights, sent))
-    weights = [weight_own] + weights
-
-    ya3, (db2, cb2) = other_of(ra3), core_of(rb2, yb2)
-    normed = [sent[0]] + [
-        lax.ppermute(sent[s], "ctx", ring_perm(count, s)) for s in range(1, LINE)
-    ]
-    one = product(tokens, [[da1, ca1], [db1, cb1]], weights, 0, True, None)
-    mine_part = product(tokens, [[grad_out]], weights, 0, True, None)
-    rb3, ya3, cb2, one, mine_part = hold((rb3, ya3, cb2, one, mine_part))
-
-    yb3, (da3, ca3) = other_of(rb3), core_of(ra3, ya3)
+    fb1, na2, sent = hold((fb1, na2, sent))
+    normed = [sent[0], lax.ppermute(sent[1], "ctx", ring_perm(count, 1)), None, None]
+    ra2, rb2, ya2, others[1], normed[1] = hold((ra2, rb2, ya2, others[1], normed[1]))
+
+    ra3, yb2, nb2, fa2 = ring(ra2), other_of(rb2), near_of(rb2), near_of(ya2)
+    normed[3] = lax.ppermute(sent[3], "ctx", ring_perm(count, 3))
+    mine_part = product(
+        tokens, [[grad_out]] * CHUNKS, weight_own, others, 0, True, None, whole=True
+    )
+    rb2, ra3, yb2, nb2, fa2, normed[3], mine_part = hold(
+        (rb2, ra3, yb2, nb2, fa2, normed[3], mine_part)
+    )
+
+    rb3, ya3, na3, fb2 = ring(rb2), other_of(ra3), near_of(ra3), near_of(yb2)
+    normed[2] = lax.ppermute(sent[2], "ctx", ring_perm(count, 2))
+    one = product(
+        tokens, [[ra1, na1, ya1, fa1], [rb1, nb1, yb1, fb1]], weight_own, others, 0, True, None
+    )
+    ra3, rb3, ya3, na3, fb2, normed[2], one = hold((ra3, rb3, ya3, na3, fb2, normed[2], one))
+
+    yb3, nb3, fa3 = other_of(rb3), near_of(rb3), near_of(ya3)
     returned = [mine_part, lax.ppermute(one, "ctx", ring_perm(count, -1))]
-    two = product(tokens, [[da2, ca2], [db2, cb2]], weights, 0, True, None)
-    three = product(tokens, [[da3, ca3]], weights, 0, False, None)
-    yb3, three, two, normed = hold((yb3, three, two, normed))
-
-    db3, cb3 = core_of(rb3, yb3)
+    two = product(
+        tokens, [[ra2, na2, ya2, fa2], [rb2, nb2, yb2, fb2]], weight_own, others, 0, True, None
+    )
+    nb3, fa3, two = hold((nb3, fa3, two))
     returned.append(lax.ppermute(two, "ctx", ring_perm(count, -2)))
-    lots = [[[da1, ca1], [da2, ca2], [da3, ca3]], [[db1, cb1], [db2, cb2], [db3, cb3]]]
-    cb3, three = hold((cb3, three))
-    lots[1][2][1] = cb3
-    three = product(tokens, [[db3, cb3]], weights, 1, True, three)
-    returned.append(lax.ppermute(three, "ctx", ring_perm(count, -3)))
-    early = outer([after(normed[0], three)] + normed[1:], grad_out, lots[0], 0, own)
-    returned, early = hold((returned, early))
-
+    last_lot = [ra3, na3, ya3, fa3]
+    three = product(tokens, [last_lot], weight_own, others, 0, False, None)
+    lots = [[ra1, na1, ya1, fa1], [ra2, na2, ya2, fa2], last_lot]
+    early = outer(normed, grad_out, lots, 0, own)
+    yb3, three, early, returned = hold((yb3, three, early, returned))
+
+    fb3 = near_of(yb3)
     flat = [early[0]]
     flat += [lax.ppermute(early[s], "ctx", pair_perm(count, s)) for s in range(1, minor)]
+    last_lot = [rb3, nb3, yb3, fb3]
+    three = product(tokens, [last_lot], weight_own, others, 1, True, three)
+    returned.append(lax.ppermute(three, "ctx", ring_perm(count, -3)))
+    lots = [[rb1, nb1, yb1, fb1], [rb2, nb2, yb2, fb2], last_lot]
+    late = outer([after(normed[0], three)] + normed[1:], grad_out, lots, 1, own)
+    returned, late = hold((returned, late))
+
     grad, gain_sum, inner = whole(
         back_kernel, [wide_b, jax.ShapeDtypeStruct((1, width), FL), row_f], "back",
         order, attn_out, inv_rms, gain_row, *returned,
@@ -475,22 +494,21 @@
     gain_sum = gain_sum + lax.ppermute(gain_sum, "ctx", [(i, i ^ 1) for i in range(count)])
     inner = inner + near_of(inner)
     inner_there = other_of(inner)
-    late = outer([after(normed[0], inner)] + normed[1:], grad_out, lots[1], 1, own)
-    inner_there, late = hold((inner_there, late))
+    inner_there, gain_sum, flat = hold((inner_there, gain_sum, flat))
     grad_attn, put_back = whole(
         functools.partial(grad_kernel, features), [wide_b, put_shape], "grads",
         grad, attn_out, inv_rms, inner, inner_there, gain_row, query_rows, turned,
     )
     spread = lax.all_to_all(put_back, "ctx", 0, 0, tiled=True)
-    grad_query, gk_in, gv_in = whole(
-        inside_kernel, [wide_b, wide_f, wide_f], "inside",
-        grad_attn, query_rows, key_rows, value_rows, run, turned, state_low,
-    )
-    spread, gk_in, gv_in, late, gain_sum = hold((spread, gk_in, gv_in, late, gain_sum))
+    late = hold((put_back, late))[1]
     flat.append(late[0])
     flat += [lax.ppermute(late[s], "ctx", pair_perm(count, s)) for s in range(1, minor)]
     states = whole(functools.partial(scan_kernel, True), scan_shape, "scan", spread)
     back_low = lax.all_to_all(states, "ctx", 0, 0, tiled=True).reshape(heads, size, size)
+    grad_query, gk_in, gv_in = whole(
+        inside_kernel, [wide_b, wide_f, wide_f], "inside",
+        after(grad_attn, states), query_rows, key_rows, value_rows, run, turned, state_low,
+    )
     step = 2
     while step < count:
         gain_sum = gain_sum + lax.ppermute(

time: 231 us -> 240 us (1.039)
  Pallas kernels: 41.8 us -> 48.1 us
  local copies, waits for them, and re-layouts: 17 us -> 21.4 us
  waiting for transfers between devices: 107 us -> 104 us
    all_to_all x1, waiting for transfers between devices: 15.2 us -> 0.01 us  [shards(): lax.all_to_all(states, 'ctx', 0, 0, tiled=True).reshape(heads, size, size)]
    ppermute x4 -> x5, waiting for transfers between devices: 29 us -> 42.3 us  [the longest x1 13.7 us: shards(): lax.ppermute(halves[1], 'ctx', pair_perm(count, -s))]
    all_to_all x1, waiting for transfers between devices: 9.3 us -> 0.04 us  [shards(): spread = lax.all_to_all(put, 'ctx', 0, 0, tiled=True)]
    all_to_all x1, waiting for transfers between devices: 0.01 us -> 7.47 us  [shards(): spread = lax.all_to_all(put_back, 'ctx', 0, 0, tiled=True)]
    ppermute x6, starting transfers between devices: 11.1 us -> 4.14 us  [ring(): return lax.ppermute(x, 'ctx', ring_perm(count, 1))]
    ppermute x1, waiting for transfers between devices: 6.82 us -> 0.01 us  [shards(): returned.append(lax.ppermute(three, 'ctx', ring_perm(count, -3)))]
    ppermute x4 -> x5, starting transfers between devices: 4.7 us -> 10.4 us  [the longest x1 2.7 us: shards(): normed[3] = lax.ppermute(sent[3], 'ctx', ring_perm(count, 3))]
    all_to_all x1, waiting for transfers between devices: 3.28 us -> 7.08 us  [shards(): state_low = lax.all_to_all(states, 'ctx', 0, 0, tiled=True)]
  transfers between devices with their start and end apart: 38 -> 45, of which waited for: 17 -> 19; matrix products, arithmetic and copies ran while one was open for 1% -> 3% of each run, Pallas kernels for 15% -> 17%
where the time goes in v6:
time: 240 us; the launch traced here: 239 us
  waiting for transfers between devices  104 us (43%)
  starting transfers between devices  61.6 us (26%)
  Pallas kernels  48.1 us (20%)
  local copies, waits for them, and re-layouts  21.4 us (9%)
  other arithmetic  2.82 us (1%)
    ppermute x6, waiting for transfers between devices, ring(): return lax.ppermute(x, 'ctx', ring_perm(count, 1))  33.5 us
    pallas_call x11, Pallas kernels, whole(): pl.pallas_call(kernel, in_specs=[SCALAR if a is tokens else full for a in...  23.7 us
    unnamed x60, local copies, waits for them, and re-layouts  16.3 us
    ppermute x1, waiting for transfers between devices, shards(): lax.ppermute(halves[1], 'ctx', pair_perm(count, -s))  13.7 us
    ppermute x1, waiting for transfers between devices, shards(): normed[2] = lax.ppermute(sent[2], 'ctx', ring_perm(count, 2))  13.7 us
    pallas_call x5, Pallas kernels, product(): pl.pallas_call(functools.partial(product_kernel, len(lots[0]), [len(w) fo...  12.8 us
    ppermute x1, waiting for transfers between devices, shards(): normed[3] = lax.ppermute(sent[3], 'ctx', ring_perm(count, 3))  11.9 us
    pallas_call x2, Pallas kernels, outer(): pl.pallas_call(functools.partial(outer_kernel, [1] + [len(lot) for lot in...  11.6 us
  transfers between devices with their start and end apart: 45, of which 19 were waited for; matrix products, arithmetic and copies ran while one was open for 3% of the time, Pallas kernels for 17%

profile of v6, /device:TPU:0, one launch (start us, length us, event | category | flops | bytes accessed | tf_op | source)
XLA Modules:
  0.0 238.7 jit_solution(13462763318896629452)
XLA Ops:
  3.6 2.6 %states.1 = (bf16[8,144,128]{2,1,0:T(8,128)(2,1)}, f32[8,384]{1,0:T(8,128)S(1)}, f32[384,8]{1,0:T(8,128)S(1)}) custom-call(f32[8,384]{1,0:T(8,128)S(1)} %copy-done.26, bf16[384,1024]{1,0:T(8,128)(2,1)S(1)} %copy-done.3, bf16[384,1024]{1,0:T(8,128)(2,1)S(1)} %copy-done.5), custom_call_target="tpu_custom_call" | custom-call | flops 1000 | bytes 1000 | tf_op jit(solution)/shard_map/states/pallas_call | solution.py:379
  6.2 7.3 %all-to-all-start = ((bf16[8,144,128]{2,1,0:T(8,128)(2,1)}), bf16[8,144,128]{2,1,0:T(8,128)(2,1)}, u32[]{:S(2)}, u32[]{:S(2)}) async-start(bf16[8,144,128]{2,1,0:T(8,128)(2,1)} %get-tuple-element.100), calls=%async_computation | async-start | bytes 589824 | tf_op jit(solution)/shard_map/all_to_all | solution.py:410
  13.5 1.9 constant_dynamic-slice_fusion.1
  15.4 2.0 collective-permute-start
  17.4 1.9 weights.1.intra_ref
  20.5 2.2 fusion.order_ref
  22.7 1.9 constant_dynamic-slice_fusion
  24.6 11.2 %collective-permute-done.refs_1_.refs_5_ = bf16[96,3072]{1,0:T(8,128)(2,1)} collective-permute-done((bf16[96,3072]{1,0:T(8,128)(2,1)}, bf16[96,3072]{1,0:T(8,128)(2,1)}, u32[]{:S(2)}, u32[]{:S(2)}) %collective-permute-start) | collective-permute-done | bytes 589856 | tf_op jit(solution)/shard_map/ppermute | solution.py:390
  35.8 1.5 collective-permute-start.2
  39.1 4.1 %all-to-all-start.1 = ((bf16[8,128,128]{2,1,0:T(8,128)(2,1)}), bf16[8,128,128]{2,1,0:T(8,128)(2,1)}, u32[]{:S(2)}, u32[]{:S(2)}) async-start(bf16[8,128,128]{2,1,0:T(8,128)(2,1)} %copy-done.16), calls=%async_computation.1 | async-start | bytes 524288 | tf_op jit(solution)/shard_map/all_to_all | solution.py:419
  43.1 1.9 collective-permute-start.1
  46.3 7.1 %all-to-all-done.1.state_ref = bf16[8,128,128]{2,1,0:T(8,128)(2,1)} async-done(((bf16[8,128,128]{2,1,0:T(8,128)(2,1)}), bf16[8,128,128]{2,1,0:T(8,128)(2,1)}, u32[]{:S(2)}, u32[]{:S(2)}) %all-to-all-start.1) | async-done | bytes 262176 | tf_op jit(solution)/shard_map/all_to_all | solution.py:419
  53.4 11.9 %collective-permute-done.1.refs_5_ = bf16[96,3072]{1,0:T(8,128)(2,1)} collective-permute-done((bf16[96,3072]{1,0:T(8,128)(2,1)}, bf16[96,3072]{1,0:T(8,128)(2,1)}, u32[]{:S(2)}, u32[]{:S(2)}) %collective-permute-start.1) | collective-permute-done | bytes 589856 | tf_op jit(solution)/shard_map/ppermute | solution.py:390
  65.3 1.5 collective-permute-start.9
  71.6 1.7 attend.1
  75.0 8.7 %collective-permute-done.6.refs_1_.refs_9_ = bf16[96,3072]{1,0:T(8,128)(2,1)S(1)} collective-permute-done((bf16[96,3072]{1,0:T(8,128)(2,1)}, bf16[96,3072]{1,0:T(8,128)(2,1)S(1)}, u32[]{:S(2)}, u32[]{:S(2)}) %collective-permute-start.6) | collective-permute-done | bytes 589856 | tf_op jit(solution)/shard_map/ppermute | solution.py:390
  84.9 1.5 collective-permute-start.13
  88.2 2.7 %collective-permute-start.16 = (bf16[384,256]{1,0:T(8,128)(2,1)S(1)}, bf16[384,256]{1,0:T(8,128)(2,1)S(1)}, u32[]{:S(2)}, u32[]{:S(2)}) collective-permute-start(bf16[384,256]{1,0:T(8,128)(2,1)S(1)} %get-tuple-element.128), channel_id=1, source_target_pairs={{0,8},{4,12},{8,24},{12,28},{24,16},{28,20},{16,0},{20,4},{1,9},{5... | collective-permute-start | bytes 589832 | tf_op jit(solution)/shard_map/ppermute | solution.py:448
  90.9 13.7 %collective-permute-done.13.refs_5_.refs_11_.refs_6_ = bf16[128,3072]{1,0:T(8,128)(2,1)S(1)} collective-permute-done((bf16[128,3072]{1,0:T(8,128)(2,1)}, bf16[128,3072]{1,0:T(8,128)(2,1)S(1)}, u32[]{:S(2)}, u32[]{:S(2)}) %collective-permute-start.13) | collective-permute-done | bytes 786464 | tf_op jit(solution)/shard_map/ppermute | solution.py:442
  104.6 2.3 collective-permute-done.16.refs_1_
  106.9 1.5 collective-permute-start.18
  108.6 2.7 %collective-permute-start.21 = (bf16[384,256]{1,0:T(8,128)(2,1)S(1)}, bf16[384,256]{1,0:T(8,128)(2,1)S(1)}, u32[]{:S(2)}, u32[]{:S(2)}) collective-permute-start(bf16[384,256]{1,0:T(8,128)(2,1)S(1)} %get-tuple-element.132), channel_id=1, source_target_pairs={{0,16},{4,20},{8,0},{12,4},{24,8},{28,12},{16,24},{20,28},{1,17},{... | collective-permute-start | bytes 589832 | tf_op jit(solution)/shard_map/ppermute | solution.py:452
  111.3 2.3 copy-done
  113.7 2.8 %product.5.refs_0_ = bf16[384,256]{1,0:T(8,128)(2,1)S(1)} custom-call(s32[1]{0:T(128)} %bitcast.1.mine_ref.refs_0_, bf16[384,6144]{1,0:T(8,128)(2,1)S(1)} %copy-done, bf16[384,6144]{1,0:T(8,128)(2,1)S(1)} %copy-done, bf16[128,6144]{1,0:T(8,128)(2,1)S(1)} %bitcast.8, bf16[128,3072]{1,0:T(8,128)(2,1)S(1)} %collective-permute-done.9.refs_4_.refs_10_.refs_6_, ...), custom_call_target="tpu_custom_call" | custom-call | flops 1000 | bytes 1000 | tf_op jit(solution)/shard_map/product/pallas_call | solution.py:210
  116.5 11.9 %collective-permute-done.21.refs_3_ = bf16[384,256]{1,0:T(8,128)(2,1)S(1)} collective-permute-done((bf16[384,256]{1,0:T(8,128)(2,1)S(1)}, bf16[384,256]{1,0:T(8,128)(2,1)S(1)}, u32[]{:S(2)}, u32[]{:S(2)}) %collective-permute-start.21) | collective-permute-done | bytes 196640 | tf_op jit(solution)/shard_map/ppermute | solution.py:452
  129.8 2.1 collective-permute-start.26
  131.8 4.1 %product.6 = bf16[384,256]{1,0:T(8,128)(2,1)S(1)} custom-call(s32[1]{0:T(128)} %bitcast.1.mine_ref.refs_0_, bf16[96,3072]{1,0:T(8,128)(2,1)} %collective-permute-done.refs_1_.refs_5_, bf16[96,3072]{1,0:T(8,128)(2,1)} %collective-permute-done.3.refs_2_.refs_6_, bf16[96,3072]{1,0:T(8,128)(2,1)} %collective-permute-done.2.refs_3_.refs_7_, ...), custom_call_target="tpu_custom_call" | custom-call | flops 1000 | bytes 1000 | tf_op jit(solution)/shard_map/product/pallas_call | solution.py:210
  136.0 13.7 %collective-permute-done.26.refs_2_ = bf16[384,256]{1,0:T(8,128)(2,1)S(1)} collective-permute-done((bf16[384,256]{1,0:T(8,128)(2,1)S(1)}, bf16[384,256]{1,0:T(8,128)(2,1)S(1)}, u32[]{:S(2)}, u32[]{:S(2)}) %collective-permute-start.26) | collective-permute-done | bytes 196640 | tf_op jit(solution)/shard_map/ppermute | solution.py:461
  151.3 1.5 collective-permute-start.27
  152.8 4.8 %collective-permute-start.30 = (bf16[384,256]{1,0:T(8,128)(2,1)S(1)}, bf16[384,256]{1,0:T(8,128)(2,1)S(1)}, u32[]{:S(2)}, u32[]{:S(2)}) collective-permute-start(bf16[384,256]{1,0:T(8,128)(2,1)S(1)} %product.6), channel_id=1, source_target_pairs={{0,16},{4,20},{8,0},{12,4},{24,8},{28,12},{16,24},{20,28},{1,17},{... | collective-permute-start | bytes 589832 | tf_op jit(solution)/shard_map/ppermute | solution.py:468
  157.6 3.0 %product.7 = bf16[384,256]{1,0:T(8,128)(2,1)S(1)} custom-call(s32[1]{0:T(128)} %bitcast.1.mine_ref.refs_0_, bf16[96,3072]{1,0:T(8,128)(2,1)S(1)} %collective-permute-done.6.refs_1_.refs_9_, bf16[96,3072]{1,0:T(8,128)(2,1)S(1)} %collective-permute-done.15.refs_2_.refs_10_, bf16[96,3072]{1,0:T(8,128)(2,1)S(1)} %collective-permute-done.12.refs_3_.refs_11_, ...), custom_call_target="tpu_custom_call" | custom-call | flops 1000 | bytes 1000 | tf_op jit(solution)/shard_map/product/pallas_call | solution.py:210
  160.6 1.8 collective-permute-start.31
  163.9 6.0 %outer.2 = (bf16[128,3072]{1,0:T(8,128)(2,1)S(1)}, bf16[128,3072]{1,0:T(8,128)(2,1)S(1)}) custom-call(bf16[384,256]{1,0:T(8,128)(2,1)S(1)} %get-tuple-element.167.refs_0_, bf16[384,256]{1,0:T(8,128)(2,1)S(1)} %collective-permute-done.16.refs_1_, bf16[384,256]{1,0:T(8,128)(2,1)S(1)} %collective-permute-done.26.refs_2_, ...), custom_call_target="tpu_custom_call" | custom-call | flops 1000 | bytes 1000 | tf_op jit(solution)/shard_map/outer/pallas_call | solution.py:253
  173.4 3.0 %collective-permute-start.33 = (bf16[384,256]{1,0:T(8,128)(2,1)S(1)}, bf16[384,256]{1,0:T(8,128)(2,1)S(1)}, u32[]{:S(2)}, u32[]{:S(2)}) collective-permute-start(bf16[384,256]{1,0:T(8,128)(2,1)S(1)} %product.9), channel_id=1, source_target_pairs={{0,8},{4,12},{8,24},{12,28},{24,16},{28,20},{16,0},{20,4},{1,9},{5... | collective-permute-start | bytes 589832 | tf_op jit(solution)/shard_map/ppermute | solution.py:485
  176.4 5.6 %outer.3 = (bf16[128,3072]{1,0:T(8,128)(2,1)S(1)}, bf16[128,3072]{1,0:T(8,128)(2,1)S(1)}) custom-call(bf16[384,256]{1,0:T(8,128)(2,1)S(1)} %get-tuple-element.167.refs_0_, bf16[384,256]{1,0:T(8,128)(2,1)S(1)} %collective-permute-done.16.refs_1_, bf16[384,256]{1,0:T(8,128)(2,1)S(1)} %collective-permute-done.26.refs_2_, ...), custom_call_target="tpu_custom_call" | custom-call | flops 1000 | bytes 1000 | tf_op jit(solution)/shard_map/outer/pallas_call | solution.py:253
  186.4 3.6 %collective-permute-done.36 = f32[1,1024]{1,0:T(1,128)S(1)} collective-permute-done((f32[1,1024]{1,0:T(1,128)S(1)}, f32[1,1024]{1,0:T(1,128)S(1)}, u32[]{:S(2)}, u32[]{:S(2)}) %collective-permute-start.36) | collective-permute-done | bytes 4128 | tf_op jit(solution)/shard_map/ppermute | solution.py:494
  190.1 2.2 grads.1
  193.2 4.8 %all-to-all-start.2 = ((bf16[8,144,128]{2,1,0:T(8,128)(2,1)}), bf16[8,144,128]{2,1,0:T(8,128)(2,1)S(1)}, u32[]{:S(2)}, u32[]{:S(2)}) async-start(bf16[8,144,128]{2,1,0:T(8,128)(2,1)} %get-tuple-element.181), calls=%async_computation.2 | async-start | bytes 589824 | tf_op jit(solution)/shard_map/all_to_all | solution.py:502
  198.0 2.0 collective-permute-start.38
  200.0 7.5 %all-to-all-done.2.in_ref = bf16[8,144,128]{2,1,0:T(8,128)(2,1)S(1)} async-done(((bf16[8,144,128]{2,1,0:T(8,128)(2,1)}), bf16[8,144,128]{2,1,0:T(8,128)(2,1)S(1)}, u32[]{:S(2)}, u32[]{:S(2)}) %all-to-all-start.2) | async-done | bytes 294944 | tf_op jit(solution)/shard_map/all_to_all | solution.py:502
  208.3 4.1 %all-to-all-start.3 = ((bf16[8,128,128]{2,1,0:T(8,128)(2,1)}), bf16[8,128,128]{2,1,0:T(8,128)(2,1)}, u32[]{:S(2)}, u32[]{:S(2)}) async-start(bf16[8,128,128]{2,1,0:T(8,128)(2,1)} %scan.3), calls=%async_computation.3 | async-start | bytes 524288 | tf_op jit(solution)/shard_map/all_to_all | solution.py:507
  212.4 1.9 collective-permute-start.39
  214.3 3.3 %collective-permute-done.39 = f32[1,1024]{1,0:T(1,128)S(1)} collective-permute-done((f32[1,1024]{1,0:T(1,128)S(1)}, f32[1,1024]{1,0:T(1,128)S(1)}, u32[]{:S(2)}, u32[]{:S(2)}) %collective-permute-start.39) | collective-permute-done | bytes 4128 | tf_op jit(solution)/shard_map/ppermute | solution.py:514
  217.6 2.9 %collective-permute-start.40 = (f32[1,1024]{1,0:T(1,128)S(1)}, f32[1,1024]{1,0:T(1,128)S(1)}, u32[]{:S(2)}, u32[]{:S(2)}) collective-permute-start(f32[1,1024]{1,0:T(1,128)S(1)} %add.143), channel_id=1, source_target_pairs={{0,16},{4,20},{8,24},{12,28},{16,0},{20,4},{24,8},{28,12},{1,17},{... | collective-permute-start | bytes 12296 | tf_op jit(solution)/shard_map/ppermute | solution.py:514
  220.6 1.6 collective-permute-done.40
  223.9 5.4 %inside.1 = (bf16[384,1024]{1,0:T(8,128)(2,1)}, f32[384,1024]{1,0:T(8,128)S(1)}, f32[384,1024]{1,0:T(8,128)S(1)}) custom-call(bf16[384,1024]{1,0:T(8,128)(2,1)S(1)} %copy-done.24, bf16[384,1024]{1,0:T(8,128)(2,1)S(1)} %copy-done.9, bf16[384,1024]{1,0:T(8,128)(2,1)S(1)} %copy-done.4, bf16[384,1024]{1,0:T(8,128)(2,1)S(1)} %copy-done.6, ...), custom_call_target="tpu_custom_call" | custom-call | flops 1000 | bytes 1000 | tf_op jit(solution)/shard_map/inside/pallas_call | solution.py:379
  231.6 2.8 %sum.1 = bf16[128,6144]{1,0:T(8,128)(2,1)} custom-call(bf16[128,3072]{1,0:T(8,128)(2,1)S(1)} %copy-done.18, bf16[128,3072]{1,0:T(8,128)(2,1)S(1)} %copy-done.20, bf16[128,3072]{1,0:T(8,128)(2,1)S(1)} %copy-done.22, bf16[128,3072]{1,0:T(8,128)(2,1)} %collective-permute-done.38.refs_3_), custom_call_target="tpu_custom_call" | custom-call | flops 1000 | bytes 1000 | tf_op jit(solution)/shard_map/sum/pallas_call | solution.py:379
  235.8 2.9 %outside.1 = (bf16[384,1024]{1,0:T(8,128)(2,1)}, bf16[384,1024]{1,0:T(8,128)(2,1)}) custom-call(bf16[384,1024]{1,0:T(8,128)(2,1)S(1)} %copy-done.4, bf16[384,1024]{1,0:T(8,128)(2,1)S(1)} %copy-done.6, bf16[8,128,128]{2,1,0:T(8,128)(2,1)} %all-to-all-done.3.state_ref, f32[384,8]{1,0:T(8,128)S(1)} %get-tuple-element.102.turned_ref, ...), custom_call_target="tpu_custom_call" | custom-call | flops 1000 | bytes 1000 | tf_op jit(solution)/shard_map/outside/pallas_call | solution.py:379
  (131 shorter events, 36.3 us)
Async XLA Ops:
  6.2 18.4 %all-to-all-start = ((bf16[8,144,128]{2,1,0:T(8,128)(2,1)}), bf16[8,144,128]{2,1,0:T(8,128)(2,1)}, u32[]{:S(2)}, u32[]{:S(2)}) async-start(bf16[8,144,128]{2,1,0:T(8,128)(2,1)} %get-tuple-element.100), calls=%async_computation | async-start | bytes 589824 | tf_op jit(solution)/shard_map/all_to_all | solution.py:410
  15.4 20.4 %collective-permute-start = (bf16[96,3072]{1,0:T(8,128)(2,1)}, bf16[96,3072]{1,0:T(8,128)(2,1)}, u32[]{:S(2)}, u32[]{:S(2)}) collective-permute-start(bf16[96,3072]{1,0:T(8,128)(2,1)} %constant_dynamic-slice_fusion.1), channel_id=1, source_target_pairs={{0,8},{4,12},{8,24},{12,28},{24,16},{28,20},{16,0},{20,4},{1,9},{5... | collective-permute-start | bytes 1769480 | tf_op jit(solution)/shard_map/ppermute | solution.py:390
  35.8 29.5 %collective-permute-start.3 = (bf16[96,3072]{1,0:T(8,128)(2,1)}, bf16[96,3072]{1,0:T(8,128)(2,1)}, u32[]{:S(2)}, u32[]{:S(2)}) collective-permute-start(bf16[96,3072]{1,0:T(8,128)(2,1)} %collective-permute-done.refs_1_.refs_5_), channel_id=1, source_target_pairs={{0,1},{1,0},{2,3},{3,2},{4,5},{5,4},{6,7},{7,6},{8,9},{9,8},{10,11... | collective-permute-start | bytes 1769480 | tf_op jit(solution)/shard_map/ppermute | solution.py:393
  35.8 29.5 %collective-permute-start.2 = (bf16[96,3072]{1,0:T(8,128)(2,1)}, bf16[96,3072]{1,0:T(8,128)(2,1)}, u32[]{:S(2)}, u32[]{:S(2)}) collective-permute-start(bf16[96,3072]{1,0:T(8,128)(2,1)} %collective-permute-done.refs_1_.refs_5_), channel_id=1, source_target_pairs={{0,2},{1,3},{2,0},{3,1},{4,6},{5,7},{6,4},{7,5},{8,10},{9,11},{10,... | collective-permute-start | bytes 1769480 | tf_op jit(solution)/shard_map/ppermute | solution.py:393
  39.1 14.3 %all-to-all-start.1 = ((bf16[8,128,128]{2,1,0:T(8,128)(2,1)}), bf16[8,128,128]{2,1,0:T(8,128)(2,1)}, u32[]{:S(2)}, u32[]{:S(2)}) async-start(bf16[8,128,128]{2,1,0:T(8,128)(2,1)} %copy-done.16), calls=%async_computation.1 | async-start | bytes 524288 | tf_op jit(solution)/shard_map/all_to_all | solution.py:419
  43.1 22.2 %collective-permute-start.1 = (bf16[96,3072]{1,0:T(8,128)(2,1)}, bf16[96,3072]{1,0:T(8,128)(2,1)}, u32[]{:S(2)}, u32[]{:S(2)}) collective-permute-start(bf16[96,3072]{1,0:T(8,128)(2,1)} %constant_dynamic-slice_fusion), channel_id=1, source_target_pairs={{0,8},{4,12},{8,24},{12,28},{24,16},{28,20},{16,0},{20,4},{1,9},{5... | collective-permute-start | bytes 1769480 | tf_op jit(solution)/shard_map/ppermute | solution.py:390
  45.0 41.8 %copy-start.25 = (f32[1024]{0:T(1024)S(1)}, f32[1024]{0:T(1024)}, u32[]{:S(2)}) copy-start(f32[1024]{0:T(1024)} %param.11) | copy-start | bytes 12292
  53.4 33.5 %copy-start.2 = (bf16[1024,1024]{1,0:T(8,128)(2,1)S(1)}, bf16[1024,1024]{1,0:T(8,128)(2,1)}, u32[]{:S(2)}) copy-start(bf16[1024,1024]{1,0:T(8,128)(2,1)} %fusion.order_ref) | copy-start | bytes 6291460
  65.3 19.1 %collective-permute-start.9 = (bf16[128,3072]{1,0:T(8,128)(2,1)}, bf16[128,3072]{1,0:T(8,128)(2,1)S(1)}, u32[]{:S(2)}, u32[]{:S(2)}) collective-permute-start(bf16[128,3072]{1,0:T(8,128)(2,1)} %get-tuple-element.117), channel_id=1, source_target_pairs={{0,4},{4,0},{8,12},{12,8},{16,20},{20,16},{24,28},{28,24},{1,5},{5... | collective-permute-start | bytes 2359304 | tf_op jit(solution)/shard_map/ppermute | solution.py:429
  66.8 2.2 collective-permute-start.4
  66.8 16.9 %collective-permute-start.6 = (bf16[96,3072]{1,0:T(8,128)(2,1)}, bf16[96,3072]{1,0:T(8,128)(2,1)S(1)}, u32[]{:S(2)}, u32[]{:S(2)}) collective-permute-start(bf16[96,3072]{1,0:T(8,128)(2,1)} %collective-permute-done.refs_1_.refs_5_), channel_id=1, source_target_pairs={{0,8},{4,12},{8,24},{12,28},{24,16},{28,20},{16,0},{20,4},{1,9},{5... | collective-permute-start | bytes 1769480 | tf_op jit(solution)/shard_map/ppermute | solution.py:390
  66.8 16.9 %collective-permute-start.8 = (bf16[96,3072]{1,0:T(8,128)(2,1)}, bf16[96,3072]{1,0:T(8,128)(2,1)S(1)}, u32[]{:S(2)}, u32[]{:S(2)}) collective-permute-start(bf16[96,3072]{1,0:T(8,128)(2,1)} %collective-permute-done.1.refs_5_), channel_id=1, source_target_pairs={{0,1},{1,0},{2,3},{3,2},{4,5},{5,4},{6,7},{7,6},{8,9},{9,8},{10,11... | collective-permute-start | bytes 1769480 | tf_op jit(solution)/shard_map/ppermute | solution.py:393
  67.3 16.3 %collective-permute-start.7 = (bf16[96,3072]{1,0:T(8,128)(2,1)}, bf16[96,3072]{1,0:T(8,128)(2,1)S(1)}, u32[]{:S(2)}, u32[]{:S(2)}) collective-permute-start(bf16[96,3072]{1,0:T(8,128)(2,1)} %collective-permute-done.1.refs_5_), channel_id=1, source_target_pairs={{0,2},{1,3},{2,0},{3,1},{4,6},{5,7},{6,4},{7,5},{8,10},{9,11},{10,... | collective-permute-start | bytes 1769480 | tf_op jit(solution)/shard_map/ppermute | solution.py:393
  73.2 1.2 collective-permute-start.5
  74.4 9.2 %collective-permute-start.10 = (f32[1,384]{1,0:T(1,128)S(1)}, f32[1,384]{1,0:T(1,128)S(1)}, u32[]{:S(2)}, u32[]{:S(2)}) collective-permute-start(f32[1,384]{1,0:T(1,128)S(1)} %add.140.here_ref), channel_id=1, source_target_pairs={{0,2},{1,3},{2,0},{3,1},{4,6},{5,7},{6,4},{7,5},{8,10},{9,11},{10,... | collective-permute-start | bytes 4616 | tf_op jit(solution)/shard_map/ppermute | solution.py:393
  84.4 3.8 %collective-permute-start.15 = (bf16[96,3072]{1,0:T(8,128)(2,1)S(1)}, bf16[96,3072]{1,0:T(8,128)(2,1)S(1)}, u32[]{:S(2)}, u32[]{:S(2)}) collective-permute-start(bf16[96,3072]{1,0:T(8,128)(2,1)S(1)} %collective-permute-done.6.refs_1_.refs_9_), channel_id=1, source_target_pairs={{0,1},{1,0},{2,3},{3,2},{4,5},{5,4},{6,7},{7,6},{8,9},{9,8},{10,11... | collective-permute-start | bytes 1769480 | tf_op jit(solution)/shard_map/ppermute | solution.py:393
  84.4 3.8 %collective-permute-start.14 = (bf16[96,3072]{1,0:T(8,128)(2,1)S(1)}, bf16[96,3072]{1,0:T(8,128)(2,1)S(1)}, u32[]{:S(2)}, u32[]{:S(2)}) collective-permute-start(bf16[96,3072]{1,0:T(8,128)(2,1)S(1)} %collective-permute-done.7.refs_7_), channel_id=1, source_target_pairs={{0,1},{1,0},{2,3},{3,2},{4,5},{5,4},{6,7},{7,6},{8,9},{9,8},{10,11... | collective-permute-start | bytes 1769480 | tf_op jit(solution)/shard_map/ppermute | solution.py:393
  84.9 19.7 %collective-permute-start.13 = (bf16[128,3072]{1,0:T(8,128)(2,1)}, bf16[128,3072]{1,0:T(8,128)(2,1)S(1)}, u32[]{:S(2)}, u32[]{:S(2)}) collective-permute-start(bf16[128,3072]{1,0:T(8,128)(2,1)} %get-tuple-element.122), channel_id=1, source_target_pairs={{0,4},{4,0},{8,12},{12,8},{16,20},{20,16},{24,28},{28,24},{1,5},{5... | collective-permute-start | bytes 2359304 | tf_op jit(solution)/shard_map/ppermute | solution.py:442
  86.4 18.2 %collective-permute-start.12 = (bf16[96,3072]{1,0:T(8,128)(2,1)S(1)}, bf16[96,3072]{1,0:T(8,128)(2,1)S(1)}, u32[]{:S(2)}, u32[]{:S(2)}) collective-permute-start(bf16[96,3072]{1,0:T(8,128)(2,1)S(1)} %collective-permute-done.6.refs_1_.refs_9_), channel_id=1, source_target_pairs={{0,2},{1,3},{2,0},{3,1},{4,6},{5,7},{6,4},{7,5},{8,10},{9,11},{10,... | collective-permute-start | bytes 1769480 | tf_op jit(solution)/shard_map/ppermute | solution.py:393
  86.9 17.7 %collective-permute-start.11 = (bf16[96,3072]{1,0:T(8,128)(2,1)}, bf16[96,3072]{1,0:T(8,128)(2,1)S(1)}, u32[]{:S(2)}, u32[]{:S(2)}) collective-permute-start(bf16[96,3072]{1,0:T(8,128)(2,1)} %collective-permute-done.1.refs_5_), channel_id=1, source_target_pairs={{0,8},{4,12},{8,24},{12,28},{24,16},{28,20},{16,0},{20,4},{1,9},{5... | collective-permute-start | bytes 1769480 | tf_op jit(solution)/shard_map/ppermute | solution.py:390
  88.2 18.7 %collective-permute-start.16 = (bf16[384,256]{1,0:T(8,128)(2,1)S(1)}, bf16[384,256]{1,0:T(8,128)(2,1)S(1)}, u32[]{:S(2)}, u32[]{:S(2)}) collective-permute-start(bf16[384,256]{1,0:T(8,128)(2,1)S(1)} %get-tuple-element.128), channel_id=1, source_target_pairs={{0,8},{4,12},{8,24},{12,28},{24,16},{28,20},{16,0},{20,4},{1,9},{5... | collective-permute-start | bytes 589832 | tf_op jit(solution)/shard_map/ppermute | solution.py:448
  106.9 21.6 %collective-permute-start.19 = (bf16[96,3072]{1,0:T(8,128)(2,1)S(1)}, bf16[96,3072]{1,0:T(8,128)(2,1)S(1)}, u32[]{:S(2)}, u32[]{:S(2)}) collective-permute-start(bf16[96,3072]{1,0:T(8,128)(2,1)S(1)} %collective-permute-done.11.refs_5_.refs_9_), channel_id=1, source_target_pairs={{0,1},{1,0},{2,3},{3,2},{4,5},{5,4},{6,7},{7,6},{8,9},{9,8},{10,11... | collective-permute-start | bytes 1769480 | tf_op jit(solution)/shard_map/ppermute | solution.py:393
  106.9 21.6 %collective-permute-start.18 = (bf16[96,3072]{1,0:T(8,128)(2,1)S(1)}, bf16[96,3072]{1,0:T(8,128)(2,1)S(1)}, u32[]{:S(2)}, u32[]{:S(2)}) collective-permute-start(bf16[96,3072]{1,0:T(8,128)(2,1)S(1)} %collective-permute-done.11.refs_5_.refs_9_), channel_id=1, source_target_pairs={{0,2},{1,3},{2,0},{3,1},{4,6},{5,7},{6,4},{7,5},{8,10},{9,11},{10,... | collective-permute-start | bytes 1769480 | tf_op jit(solution)/shard_map/ppermute | solution.py:393
  108.4 20.6 %collective-permute-start.17 = (bf16[96,3072]{1,0:T(8,128)(2,1)S(1)}, bf16[96,3072]{1,0:T(8,128)(2,1)S(1)}, u32[]{:S(2)}, u32[]{:S(2)}) collective-permute-start(bf16[96,3072]{1,0:T(8,128)(2,1)S(1)} %collective-permute-done.6.refs_1_.refs_9_), channel_id=1, source_target_pairs={{0,8},{4,12},{8,24},{12,28},{24,16},{28,20},{16,0},{20,4},{1,9},{5... | collective-permute-start | bytes 1769480 | tf_op jit(solution)/shard_map/ppermute | solution.py:390
  108.4 20.6 %collective-permute-start.20 = (bf16[96,3072]{1,0:T(8,128)(2,1)S(1)}, bf16[96,3072]{1,0:T(8,128)(2,1)S(1)}, u32[]{:S(2)}, u32[]{:S(2)}) collective-permute-start(bf16[96,3072]{1,0:T(8,128)(2,1)S(1)} %collective-permute-done.12.refs_3_.refs_11_), channel_id=1, source_target_pairs={{0,1},{1,0},{2,3},{3,2},{4,5},{5,4},{6,7},{7,6},{8,9},{9,8},{10,11... | collective-permute-start | bytes 1769480 | tf_op jit(solution)/shard_map/ppermute | solution.py:393
  108.6 19.8 %collective-permute-start.21 = (bf16[384,256]{1,0:T(8,128)(2,1)S(1)}, bf16[384,256]{1,0:T(8,128)(2,1)S(1)}, u32[]{:S(2)}, u32[]{:S(2)}) collective-permute-start(bf16[384,256]{1,0:T(8,128)(2,1)S(1)} %get-tuple-element.132), channel_id=1, source_target_pairs={{0,16},{4,20},{8,0},{12,4},{24,8},{28,12},{16,24},{20,28},{1,17},{... | collective-permute-start | bytes 589832 | tf_op jit(solution)/shard_map/ppermute | solution.py:452
  129.0 20.6 %collective-permute-start.24 = (bf16[96,3072]{1,0:T(8,128)(2,1)S(1)}, bf16[96,3072]{1,0:T(8,128)(2,1)S(1)}, u32[]{:S(2)}, u32[]{:S(2)}) collective-permute-start(bf16[96,3072]{1,0:T(8,128)(2,1)S(1)} %collective-permute-done.17.refs_1_.refs_13_), channel_id=1, source_target_pairs={{0,1},{1,0},{2,3},{3,2},{4,5},{5,4},{6,7},{7,6},{8,9},{9,8},{10,11... | collective-permute-start | bytes 1769480 | tf_op jit(solution)/shard_map/ppermute | solution.py:393
  129.0 20.6 %collective-permute-start.23 = (bf16[96,3072]{1,0:T(8,128)(2,1)S(1)}, bf16[96,3072]{1,0:T(8,128)(2,1)S(1)}, u32[]{:S(2)}, u32[]{:S(2)}) collective-permute-start(bf16[96,3072]{1,0:T(8,128)(2,1)S(1)} %collective-permute-done.17.refs_1_.refs_13_), channel_id=1, source_target_pairs={{0,2},{1,3},{2,0},{3,1},{4,6},{5,7},{6,4},{7,5},{8,10},{9,11},{10,... | collective-permute-start | bytes 1769480 | tf_op jit(solution)/shard_map/ppermute | solution.py:393
  129.5 21.3 %collective-permute-start.22 = (bf16[96,3072]{1,0:T(8,128)(2,1)S(1)}, bf16[96,3072]{1,0:T(8,128)(2,1)S(1)}, u32[]{:S(2)}, u32[]{:S(2)}) collective-permute-start(bf16[96,3072]{1,0:T(8,128)(2,1)S(1)} %collective-permute-done.11.refs_5_.refs_9_), channel_id=1, source_target_pairs={{0,8},{4,12},{8,24},{12,28},{24,16},{28,20},{16,0},{20,4},{1,9},{5... | collective-permute-start | bytes 1769480 | tf_op jit(solution)/shard_map/ppermute | solution.py:390
  129.7 21.1 %collective-permute-start.25 = (bf16[96,3072]{1,0:T(8,128)(2,1)S(1)}, bf16[96,3072]{1,0:T(8,128)(2,1)S(1)}, u32[]{:S(2)}, u32[]{:S(2)}) collective-permute-start(bf16[96,3072]{1,0:T(8,128)(2,1)S(1)} %collective-permute-done.18.refs_7_.refs_11_), channel_id=1, source_target_pairs={{0,1},{1,0},{2,3},{3,2},{4,5},{5,4},{6,7},{7,6},{8,9},{9,8},{10,11... | collective-permute-start | bytes 1769480 | tf_op jit(solution)/shard_map/ppermute | solution.py:393
  129.8 19.9 %collective-permute-start.26 = (bf16[384,256]{1,0:T(8,128)(2,1)S(1)}, bf16[384,256]{1,0:T(8,128)(2,1)S(1)}, u32[]{:S(2)}, u32[]{:S(2)}) collective-permute-start(bf16[384,256]{1,0:T(8,128)(2,1)S(1)} %get-tuple-element.138), channel_id=1, source_target_pairs={{0,24},{4,28},{8,16},{12,20},{24,0},{28,4},{16,8},{20,12},{1,25},{... | collective-permute-start | bytes 589832 | tf_op jit(solution)/shard_map/ppermute | solution.py:461
  131.8 32.0 %slice-start = ((s8[4718592]{0:T(1024)(128)(4,1)}), s8[4194304]{0:T(1024)(128)(4,1)S(1)}, s32[]{:S(2)}) async-start(s8[4718592]{0:T(1024)(128)(4,1)} %bitcast.5), calls=%async_computation.4 | async-start | bytes 8388608
  150.8 9.8 %collective-permute-start.29 = (bf16[96,3072]{1,0:T(8,128)(2,1)S(1)}, bf16[96,3072]{1,0:T(8,128)(2,1)S(1)}, u32[]{:S(2)}, u32[]{:S(2)}) collective-permute-start(bf16[96,3072]{1,0:T(8,128)(2,1)S(1)} %collective-permute-done.23.refs_3_.refs_15_), channel_id=1, source_target_pairs={{0,1},{1,0},{2,3},{3,2},{4,5},{5,4},{6,7},{7,6},{8,9},{9,8},{10,11... | collective-permute-start | bytes 1769480 | tf_op jit(solution)/shard_map/ppermute | solution.py:393
  150.8 9.8 %collective-permute-start.28 = (bf16[96,3072]{1,0:T(8,128)(2,1)S(1)}, bf16[96,3072]{1,0:T(8,128)(2,1)S(1)}, u32[]{:S(2)}, u32[]{:S(2)}) collective-permute-start(bf16[96,3072]{1,0:T(8,128)(2,1)S(1)} %collective-permute-done.22.refs_1_.refs_13_), channel_id=1, source_target_pairs={{0,1},{1,0},{2,3},{3,2},{4,5},{5,4},{6,7},{7,6},{8,9},{9,8},{10,11... | collective-permute-start | bytes 1769480 | tf_op jit(solution)/shard_map/ppermute | solution.py:393
  151.3 18.6 %collective-permute-start.27 = (bf16[96,3072]{1,0:T(8,128)(2,1)S(1)}, bf16[96,3072]{1,0:T(8,128)(2,1)S(1)}, u32[]{:S(2)}, u32[]{:S(2)}) collective-permute-start(bf16[96,3072]{1,0:T(8,128)(2,1)S(1)} %collective-permute-done.22.refs_1_.refs_13_), channel_id=1, source_target_pairs={{0,2},{1,3},{2,0},{3,1},{4,6},{5,7},{6,4},{7,5},{8,10},{9,11},{10,... | collective-permute-start | bytes 1769480 | tf_op jit(solution)/shard_map/ppermute | solution.py:393
  152.8 17.0 %collective-permute-start.30 = (bf16[384,256]{1,0:T(8,128)(2,1)S(1)}, bf16[384,256]{1,0:T(8,128)(2,1)S(1)}, u32[]{:S(2)}, u32[]{:S(2)}) collective-permute-start(bf16[384,256]{1,0:T(8,128)(2,1)S(1)} %product.6), channel_id=1, source_target_pairs={{0,16},{4,20},{8,0},{12,4},{24,8},{28,12},{16,24},{20,28},{1,17},{... | collective-permute-start | bytes 589832 | tf_op jit(solution)/shard_map/ppermute | solution.py:468
  160.6 9.3 %collective-permute-start.31 = (bf16[384,256]{1,0:T(8,128)(2,1)S(1)}, bf16[384,256]{1,0:T(8,128)(2,1)S(1)}, u32[]{:S(2)}, u32[]{:S(2)}) collective-permute-start(bf16[384,256]{1,0:T(8,128)(2,1)S(1)} %product.7), channel_id=1, source_target_pairs={{0,24},{4,28},{8,16},{12,20},{24,0},{28,4},{16,8},{20,12},{1,25},{... | collective-permute-start | bytes 589832 | tf_op jit(solution)/shard_map/ppermute | solution.py:473
  169.9 2.1 collective-permute-start.32
  170.0 20.1 %collective-permute-start.37 = (bf16[128,3072]{1,0:T(8,128)(2,1)S(1)}, bf16[128,3072]{1,0:T(8,128)(2,1)S(1)}, u32[]{:S(2)}, u32[]{:S(2)}) collective-permute-start(bf16[128,3072]{1,0:T(8,128)(2,1)S(1)} %get-tuple-element.178), channel_id=1, source_target_pairs={{0,4},{4,0},{8,12},{12,8},{16,20},{20,16},{24,28},{28,24},{1,5},{5... | collective-permute-start | bytes 2359304 | tf_op jit(solution)/shard_map/ppermute | solution.py:482
  173.4 9.5 %collective-permute-start.33 = (bf16[384,256]{1,0:T(8,128)(2,1)S(1)}, bf16[384,256]{1,0:T(8,128)(2,1)S(1)}, u32[]{:S(2)}, u32[]{:S(2)}) collective-permute-start(bf16[384,256]{1,0:T(8,128)(2,1)S(1)} %product.9), channel_id=1, source_target_pairs={{0,8},{4,12},{8,24},{12,28},{24,16},{28,20},{16,0},{20,4},{1,9},{5... | collective-permute-start | bytes 589832 | tf_op jit(solution)/shard_map/ppermute | solution.py:485
  184.1 5.9 %collective-permute-start.36 = (f32[1,1024]{1,0:T(1,128)S(1)}, f32[1,1024]{1,0:T(1,128)S(1)}, u32[]{:S(2)}, u32[]{:S(2)}) collective-permute-start(f32[1,1024]{1,0:T(1,128)S(1)} %get-tuple-element.176), channel_id=1, source_target_pairs={{0,4},{4,0},{8,12},{12,8},{16,20},{20,16},{24,28},{28,24},{1,5},{5... | collective-permute-start | bytes 12296 | tf_op jit(solution)/shard_map/ppermute | solution.py:494
  184.8 1.2 collective-permute-start.34
  185.9 4.1 %collective-permute-start.35 = (f32[1,384]{1,0:T(1,128)S(1)}, f32[1,384]{1,0:T(1,128)S(1)}, u32[]{:S(2)}, u32[]{:S(2)}) collective-permute-start(f32[1,384]{1,0:T(1,128)S(1)} %add.141.here_ref), channel_id=1, source_target_pairs={{0,2},{1,3},{2,0},{3,1},{4,6},{5,7},{6,4},{7,5},{8,10},{9,11},{10,... | collective-permute-start | bytes 4616 | tf_op jit(solution)/shard_map/ppermute | solution.py:393
  193.2 14.3 %all-to-all-start.2 = ((bf16[8,144,128]{2,1,0:T(8,128)(2,1)}), bf16[8,144,128]{2,1,0:T(8,128)(2,1)S(1)}, u32[]{:S(2)}, u32[]{:S(2)}) async-start(bf16[8,144,128]{2,1,0:T(8,128)(2,1)} %get-tuple-element.181), calls=%async_computation.2 | async-start | bytes 589824 | tf_op jit(solution)/shard_map/all_to_all | solution.py:502
  198.0 33.6 %collective-permute-start.38 = (bf16[128,3072]{1,0:T(8,128)(2,1)}, bf16[128,3072]{1,0:T(8,128)(2,1)}, u32[]{:S(2)}, u32[]{:S(2)}) collective-permute-start(bf16[128,3072]{1,0:T(8,128)(2,1)} %copy-done.27), channel_id=1, source_target_pairs={{0,4},{4,0},{8,12},{12,8},{16,20},{20,16},{24,28},{28,24},{1,5},{5... | collective-permute-start | bytes 2359304 | tf_op jit(solution)/shard_map/ppermute | solution.py:505
  208.3 26.1 %all-to-all-start.3 = ((bf16[8,128,128]{2,1,0:T(8,128)(2,1)}), bf16[8,128,128]{2,1,0:T(8,128)(2,1)}, u32[]{:S(2)}, u32[]{:S(2)}) async-start(bf16[8,128,128]{2,1,0:T(8,128)(2,1)} %scan.3), calls=%async_computation.3 | async-start | bytes 524288 | tf_op jit(solution)/shard_map/all_to_all | solution.py:507
  212.4 5.3 %collective-permute-start.39 = (f32[1,1024]{1,0:T(1,128)S(1)}, f32[1,1024]{1,0:T(1,128)S(1)}, u32[]{:S(2)}, u32[]{:S(2)}) collective-permute-start(f32[1,1024]{1,0:T(1,128)S(1)} %add.142), channel_id=1, source_target_pairs={{0,8},{4,12},{8,0},{12,4},{16,24},{20,28},{24,16},{28,20},{1,9},{5... | collective-permute-start | bytes 12296 | tf_op jit(solution)/shard_map/ppermute | solution.py:514
  217.6 4.5 %collective-permute-start.40 = (f32[1,1024]{1,0:T(1,128)S(1)}, f32[1,1024]{1,0:T(1,128)S(1)}, u32[]{:S(2)}, u32[]{:S(2)}) collective-permute-start(f32[1,1024]{1,0:T(1,128)S(1)} %add.143), channel_id=1, source_target_pairs={{0,16},{4,20},{8,24},{12,28},{16,0},{20,4},{24,8},{28,12},{1,17},{... | collective-permute-start | bytes 12296 | tf_op jit(solution)/shard_map/ppermute | solution.py:514
  (27 other events, 184.8 us)

commit v7 on v6

--- a/solution.py
+++ b/solution.py
@@ -154,10 +154,10 @@
             ref[pl.ds(to, quarter), :] = part[j * quarter : (j + 1) * quarter]
 
 
-def product_kernel(lots, others, add, last, whole, *refs):
+def product_kernel(turns, others, add, place, *refs):
     refs = list(refs)
     mine_ref = refs.pop(0)
-    x = [[refs.pop(0) for _ in range(lots)] for _ in others]
+    x = [refs.pop(0) for _ in turns]
     own_ref = refs.pop(0)
     w = [[refs.pop(0) for _ in range(k)] for k in others]
     extra = refs.pop(0) if add else None
@@ -167,102 +167,95 @@
 
     @pl.when(step == 0)
     def _():
-        held_ref[...] = extra[...] if add else jnp.zeros_like(held_ref)
-
-    for at, lot in enumerate(x):
+        held_ref[...] = jnp.zeros_like(held_ref)
+
+    for at, ws in enumerate(w):
 
         @pl.when(step // steps == at)
         def _():
-            rows = jnp.concatenate([r[...] for r in lot], axis=0)
-            cols = jnp.concatenate([own_ref[...]] + [r[...] for r in w[at]], axis=0)
+            rows = jnp.concatenate([r[...] for r in x], axis=0)
+            cols = jnp.concatenate([own_ref[...]] + [r[...] for r in ws], axis=0)
             held_ref[...] += dot(rows, cols, NT)
 
     @pl.when(step == pl.num_programs(0) - 1)
     def _():
-        if not last:
-            out_ref[...] = held_ref[...]
-        elif whole:
+        if not place:
             out_ref[...] = held_ref[...].astype(BF)
         else:
-            quarter = out_ref.shape[0] // QUARTERS
-            for j in range(QUARTERS):
-                to = pl.multiple_of((mine_ref[0] ^ j) * quarter, 16)
-                out_ref[pl.ds(to, quarter), :] = held_ref[
-                    j * quarter : (j + 1) * quarter, :
-                ].astype(BF)
-
-
-def product(mine, lots, weight, others, chunk, last, held, whole=False):
-    tok = sum(p.shape[0] for p in lots[0])
-    deep = weight.shape[1] // CHUNKS
+            quarter = x[0].shape[0]
+            rest = [t for t in range(QUARTERS) if t not in turns]
+            for ref, order in ((held_ref, turns), (extra, rest)):
+                for at, turn in enumerate(order):
+                    to = pl.multiple_of((mine_ref[0] ^ turn) * quarter, 16)
+                    out_ref[pl.ds(to, quarter), :] = ref[
+                        at * quarter : (at + 1) * quarter, :
+                    ].astype(BF)
+
+
+def product(mine, turns, pieces, weight, others, place=True, early=None):
+    rows = sum(p.shape[0] for p in pieces)
+    tok = rows if early is None else rows + early.shape[0]
     tile = 1536
-    steps = deep // tile
-    others = others[chunk : chunk + len(lots)]
+    steps = weight.shape[1] // tile
+    half = steps // len(others)
     span = weight.shape[0] + sum(w.shape[0] for w in others[0])
-    base = chunk * steps
-    more = [] if held is None else [held]
-
-    def part(at, p, offset=0):
-        return spec(
-            (p.shape[0], tile), lambda i: (0, offset + jnp.clip(i - at * steps, 0, steps - 1))
-        )
+    more = [] if early is None else [early]
+
+    def part(at, w):
+        return spec((w.shape[0], tile), lambda i: (0, jnp.clip(i - at * half, 0, half - 1)))
 
     return pl.pallas_call(
-        functools.partial(
-            product_kernel, len(lots[0]), [len(w) for w in others], len(more), last, whole
-        ),
-        grid=(steps * len(lots),),
+        functools.partial(product_kernel, turns, [len(w) for w in others], len(more), place),
+        grid=(steps,),
         in_specs=[SCALAR]
-        + [part(at, p, at * steps if whole else 0) for at, lot in enumerate(lots) for p in lot]
-        + [spec((weight.shape[0], tile), lambda i: (0, base + i))]
+        + [spec((p.shape[0], tile), lambda i: (0, i)) for p in pieces]
+        + [spec((weight.shape[0], tile), lambda i: (0, i))]
         + [part(at, w) for at, ws in enumerate(others) for w in ws]
-        + [spec((tok, span)) for _ in more],
+        + [spec(e.shape) for e in more],
         out_specs=spec((tok, span)),
-        out_shape=jax.ShapeDtypeStruct((tok, span), BF if last else FL),
-        scratch_shapes=[pltpu.VMEM((tok, span), FL)],
+        out_shape=jax.ShapeDtypeStruct((tok, span), BF),
+        scratch_shapes=[pltpu.VMEM((rows, span), FL)],
         compiler_params=PARAMS,
         cost_estimate=TINY,
         name="product",
-    )(mine, *[p for lot in lots for p in lot], weight, *[w for ws in others for w in ws], *more)
-
-
-def outer_kernel(lots, own, *refs):
+    )(mine, *pieces, weight, *[w for ws in others for w in ws], *more)
+
+
+def outer_kernel(count, own, *refs):
     refs = list(refs)
-    normed = [refs.pop(0) for _ in lots]
-    x = [[refs.pop(0) for _ in range(k)] for k in lots]
+    normed = [refs.pop(0) for _ in range(LINE)]
+    x = [refs.pop(0) for _ in range(count)]
     turned_ref = refs.pop()
 
     @pl.when(pl.program_id(0) == 0)
     def _():
         turned_ref[...] = jnp.concatenate([r[...] for r in normed], axis=0).T
 
-    rows = jnp.concatenate([r[...] for lot in x for r in lot], axis=0)
+    rows = jnp.concatenate([r[...] for r in x], axis=0)
     out = dot(turned_ref[...], rows, NN).astype(BF)
     for s, ref in enumerate(refs):
         ref[...] = out[s * own : (s + 1) * own]
 
 
-def outer(normed, grad_out, lots, chunk, own):
+def outer(normed, pieces, chunk, own):
     tok, span = normed[0].shape
-    deep = lots[0][0].shape[1]
+    deep = pieces[0].shape[1] // CHUNKS
     tile = 512
     steps = deep // tile
     base = chunk * steps
-    flat = [p for lot in lots for p in lot]
     minor = span // own
     return pl.pallas_call(
-        functools.partial(outer_kernel, [1] + [len(lot) for lot in lots], own),
+        functools.partial(outer_kernel, len(pieces), own),
         grid=(steps,),
         in_specs=[spec((tok, span)) for _ in normed]
-        + [spec((tok, tile), lambda i: (0, base + i))]
-        + [spec((p.shape[0], tile), lambda i: (0, i)) for p in flat],
+        + [spec((p.shape[0], tile), lambda i: (0, base + i)) for p in pieces],
         out_specs=[spec((own, tile), lambda i: (0, i))] * minor,
         out_shape=[jax.ShapeDtypeStruct((own, deep), BF)] * minor,
         scratch_shapes=[pltpu.VMEM((span, tok * LINE), BF)],
         compiler_params=PARAMS,
         cost_estimate=TINY,
         name="outer",
-    )(*normed, grad_out, *flat)
+    )(*normed, *pieces)
 
 
 def final_kernel(chunks, minor, *refs):
@@ -364,8 +357,7 @@
     deep = model // CHUNKS
     tokens = mine.reshape(1)
 
-    def first_piece(x, c):
-        return lax.dynamic_slice(x, (mine * quarter, c * deep), (quarter, deep))
+    piece = lax.dynamic_slice_in_dim(grad_out, mine * quarter, quarter, 0)
 
     put_shape = jax.ShapeDtypeStruct((count, rows + 16, size), BF)
     wide_f = jax.ShapeDtypeStruct((tok, width), FL)
@@ -401,120 +393,98 @@
     hold = lax.optimization_barrier
     scan_shape = jax.ShapeDtypeStruct((count, rows, size), BF)
 
-    ra1 = ring(first_piece(grad_out, 0))
+    r1 = ring(piece)
     put, run, turned = whole(
         state_kernel,
         [put_shape, jax.ShapeDtypeStruct((heads, tok), FL), jax.ShapeDtypeStruct((tok, heads), FL)],
         "states", log_decay, key_rows, value_rows,
     )
     spread = lax.all_to_all(put, "ctx", 0, 0, tiled=True)
-    first = first_piece(after(grad_out, put), 1)
-    intra = whole(
-        weights_kernel, wide_f, "weights", query_rows, key_rows, value_rows, run, turned
-    )
-    ra1, spread, intra, first = hold((ra1, spread, intra, first))
-
-    rb1, ya1, na1 = ring(first), other_of(ra1), near_of(ra1)
+    r1, spread = hold((r1, spread))
+
+    r2, y1, n1 = ring(r1), other_of(r1), near_of(r1)
     states = whole(functools.partial(scan_kernel, False), scan_shape, "scan", spread)
     state_low = lax.all_to_all(states, "ctx", 0, 0, tiled=True)
-    order = feature_order(heads, size, count)
+    intra = whole(
+        weights_kernel, wide_f, "weights", after(query_rows, states), key_rows, value_rows,
+        run, turned,
+    )
     halves = [
         after(weight_own, states)[:, c * deep : (c + 1) * deep] for c in range(CHUNKS)
     ]
-    ra1, rb1, ya1, na1, state_low, order, halves = hold(
-        (ra1, rb1, ya1, na1, state_low, order, halves)
-    )
-
-    ra2, yb1, nb1, fa1 = ring(ra1), other_of(rb1), near_of(rb1), near_of(ya1)
-    others = [[lax.ppermute(halves[0], "ctx", pair_perm(count, -s)) for s in range(1, minor)]]
-    fa1, state_low = hold((fa1, state_low))
+    first, state_low = hold((halves[0], state_low))
+    others = [[lax.ppermute(first, "ctx", pair_perm(count, -s)) for s in range(1, minor)]]
+    attn_out, squares = whole(
+        attend_kernel, [wide_f, row_f], "attend",
+        query_rows, state_low.reshape(heads, size, size), turned, intra,
+    )
+    squares = squares + near_of(squares)
+    r1, r2, y1, n1, others[0], squares = hold((r1, r2, y1, n1, others[0], squares))
     state_low = state_low.reshape(heads, size, size)
-    attn_out, squares = whole(
-        attend_kernel, [wide_f, row_f], "attend", query_rows, state_low, turned, intra
-    )
-    squares = squares + near_of(squares)
+
+    r3, y2, n2, f1 = ring(r2), other_of(r2), near_of(r2), near_of(y1)
+    others.append([lax.ppermute(halves[1], "ctx", pair_perm(count, -s)) for s in range(1, minor)])
     squares_there = other_of(squares)
-    ra2, rb1, yb1, nb1, others[0], squares_there = hold(
-        (ra2, rb1, yb1, nb1, others[0], squares_there)
-    )
-
-    rb2, ya2, na2, fb1 = ring(rb1), other_of(ra2), near_of(ra2), near_of(yb1)
-    others.append([lax.ppermute(halves[1], "ctx", pair_perm(count, -s)) for s in range(1, minor)])
+    order = feature_order(heads, size, count)
+    r2, r3, y2, n2, f1, others[1], squares_there, order = hold(
+        (r2, r3, y2, n2, f1, others[1], squares_there, order)
+    )
+
+    y3, n3, f2 = other_of(r3), near_of(r3), near_of(y2)
     inv_rms, *sent = whole(
         functools.partial(norm_kernel, features), [row_f] + [part_b] * LINE, "norm",
         tokens, attn_out, squares, squares_there, gain_row, order,
     )
-    fb1, na2, sent = hold((fb1, na2, sent))
-    normed = [sent[0], lax.ppermute(sent[1], "ctx", ring_perm(count, 1)), None, None]
-    ra2, rb2, ya2, others[1], normed[1] = hold((ra2, rb2, ya2, others[1], normed[1]))
-
-    ra3, yb2, nb2, fa2 = ring(ra2), other_of(rb2), near_of(rb2), near_of(ya2)
-    normed[3] = lax.ppermute(sent[3], "ctx", ring_perm(count, 3))
-    mine_part = product(
-        tokens, [[grad_out]] * CHUNKS, weight_own, others, 0, True, None, whole=True
-    )
-    rb2, ra3, yb2, nb2, fa2, normed[3], mine_part = hold(
-        (rb2, ra3, yb2, nb2, fa2, normed[3], mine_part)
-    )
-
-    rb3, ya3, na3, fb2 = ring(rb2), other_of(ra3), near_of(ra3), near_of(yb2)
-    normed[2] = lax.ppermute(sent[2], "ctx", ring_perm(count, 2))
-    one = product(
-        tokens, [[ra1, na1, ya1, fa1], [rb1, nb1, yb1, fb1]], weight_own, others, 0, True, None
-    )
-    ra3, rb3, ya3, na3, fb2, normed[2], one = hold((ra3, rb3, ya3, na3, fb2, normed[2], one))
-
-    yb3, nb3, fa3 = other_of(rb3), near_of(rb3), near_of(ya3)
-    returned = [mine_part, lax.ppermute(one, "ctx", ring_perm(count, -1))]
-    two = product(
-        tokens, [[ra2, na2, ya2, fa2], [rb2, nb2, yb2, fb2]], weight_own, others, 0, True, None
-    )
-    nb3, fa3, two = hold((nb3, fa3, two))
+    normed = [sent[0]] + [
+        lax.ppermute(sent[s], "ctx", ring_perm(count, s)) for s in range(1, LINE)
+    ]
+    f2, n3, sent = hold((f2, n3, sent))
+    one = product(tokens, (0, 1, 2, 3), [after(r1, f2), n1, y1, f1], weight_own, others)
+    returned = [None, lax.ppermute(one, "ctx", ring_perm(count, -1))]
+    two = product(tokens, (0, 1, 2, 3), [r2, n2, y2, f2], weight_own, others)
     returned.append(lax.ppermute(two, "ctx", ring_perm(count, -2)))
-    last_lot = [ra3, na3, ya3, fa3]
-    three = product(tokens, [last_lot], weight_own, others, 0, False, None)
-    lots = [[ra1, na1, ya1, fa1], [ra2, na2, ya2, fa2], last_lot]
-    early = outer(normed, grad_out, lots, 0, own)
-    yb3, three, early, returned = hold((yb3, three, early, returned))
-
-    fb3 = near_of(yb3)
-    flat = [early[0]]
-    flat += [lax.ppermute(early[s], "ctx", pair_perm(count, s)) for s in range(1, minor)]
-    last_lot = [rb3, nb3, yb3, fb3]
-    three = product(tokens, [last_lot], weight_own, others, 1, True, three)
+    returned[0] = product(tokens, (0,), [after(grad_out, two)], weight_own, others, place=False)
+    early = product(tokens, (0, 1), [after(r3, two), n3], weight_own, others, place=False)
+    r3, y3, normed, returned, early = hold((r3, y3, normed, returned, early))
+
+    f3 = near_of(y3)
+    three = product(tokens, (2, 3), [y3, f3], weight_own, others, early=early)
     returned.append(lax.ppermute(three, "ctx", ring_perm(count, -3)))
-    lots = [[rb1, nb1, yb1, fb1], [rb2, nb2, yb2, fb2], last_lot]
-    late = outer([after(normed[0], three)] + normed[1:], grad_out, lots, 1, own)
-    returned, late = hold((returned, late))
+    pieces = [grad_out, r1, n1, y1, f1, r2, n2, y2, f2, r3, n3, y3, f3]
+    first = outer([after(normed[0], three)] + normed[1:], pieces, 0, own)
+    returned, first = hold((returned, first))
+    flat = [first[0]]
+    flat += [lax.ppermute(first[s], "ctx", pair_perm(count, s)) for s in range(1, minor)]
 
     grad, gain_sum, inner = whole(
         back_kernel, [wide_b, jax.ShapeDtypeStruct((1, width), FL), row_f], "back",
         order, attn_out, inv_rms, gain_row, *returned,
     )
-    gain_sum = gain_sum + lax.ppermute(gain_sum, "ctx", [(i, i ^ 1) for i in range(count)])
     inner = inner + near_of(inner)
     inner_there = other_of(inner)
-    inner_there, gain_sum, flat = hold((inner_there, gain_sum, flat))
-    grad_attn, put_back = whole(
-        functools.partial(grad_kernel, features), [wide_b, put_shape], "grads",
-        grad, attn_out, inv_rms, inner, inner_there, gain_row, query_rows, turned,
-    )
-    spread = lax.all_to_all(put_back, "ctx", 0, 0, tiled=True)
-    late = hold((put_back, late))[1]
-    flat.append(late[0])
-    flat += [lax.ppermute(late[s], "ctx", pair_perm(count, s)) for s in range(1, minor)]
-    states = whole(functools.partial(scan_kernel, True), scan_shape, "scan", spread)
-    back_low = lax.all_to_all(states, "ctx", 0, 0, tiled=True).reshape(heads, size, size)
-    grad_query, gk_in, gv_in = whole(
-        inside_kernel, [wide_b, wide_f, wide_f], "inside",
-        after(grad_attn, states), query_rows, key_rows, value_rows, run, turned, state_low,
-    )
     step = 2
     while step < count:
         gain_sum = gain_sum + lax.ppermute(
             gain_sum, "ctx", [(i, i ^ step) for i in range(count)]
         )
         step *= 2
+    inner_there, gain_sum = hold((inner_there, gain_sum))
+    gain_sum = gain_sum + lax.ppermute(gain_sum, "ctx", [(i, i ^ 1) for i in range(count)])
+    grad_attn, put_back = whole(
+        functools.partial(grad_kernel, features), [wide_b, put_shape], "grads",
+        grad, attn_out, inv_rms, inner, inner_there, gain_row, query_rows, turned,
+    )
+    spread = lax.all_to_all(put_back, "ctx", 0, 0, tiled=True)
+    second = outer([after(normed[0], put_back)] + normed[1:], pieces, 1, own)
+    flat, second, spread, gain_sum = hold((flat, second, spread, gain_sum))
+    flat.append(second[0])
+    flat += [lax.ppermute(second[s], "ctx", pair_perm(count, s)) for s in range(1, minor)]
+    states = whole(functools.partial(scan_kernel, True), scan_shape, "scan", spread)
+    back_low = lax.all_to_all(states, "ctx", 0, 0, tiled=True).reshape(heads, size, size)
+    grad_query, gk_in, gv_in = whole(
+        inside_kernel, [wide_b, wide_f, wide_f], "inside",
+        after(grad_attn, states), query_rows, key_rows, value_rows, run, turned, state_low,
+    )
     grad_gain = gain_sum.reshape(width)
     grad_key, grad_value = whole(
         outside_kernel, [wide_b] * 2, "outside",

time: 240 us -> 244 us (1.017)
  blocking collectives: 0 us -> 32.3 us
  waiting for transfers between devices: 104 us -> 78.1 us
  starting transfers between devices: 61.6 us -> 51.8 us
  Pallas kernels: 48.1 us -> 53.1 us
    all_to_all x0 -> x1, blocking collectives: none -> 32.3 us  [shards(): spread = lax.all_to_all(put, 'ctx', 0, 0, tiled=True)]
    ppermute x6 -> x3, waiting for transfers between devices: 33.5 us -> 1.39 us  [ring(): return lax.ppermute(x, 'ctx', ring_perm(count, 1))]
    all_to_all x1, waiting for transfers between devices: 7.08 us -> 27.5 us  [shards(): state_low = lax.all_to_all(states, 'ctx', 0, 0, tiled=True)]
    ppermute x7, waiting for transfers between devices: 28.6 us -> 10.1 us  [the longest x1 10.1 us: shards(): lax.ppermute(first, 'ctx', pair_perm(count, -s))]
    ppermute x7, starting transfers between devices: 16.3 us -> 8.19 us  [the longest x3 6.16 us: shards(): lax.ppermute(sent[s], 'ctx', ring_perm(count, s))]
    ppermute x1, starting transfers between devices: 1.82 us -> 9.77 us  [shards(): returned.append(lax.ppermute(two, 'ctx', ring_perm(count, -2)))]
    all_to_all x1, waiting for transfers between devices: 7.47 us -> 0.01 us  [shards(): spread = lax.all_to_all(put_back, 'ctx', 0, 0, tiled=True)]
    all_to_all x1 -> x0, starting transfers between devices: 7.25 us -> none  [shards(): spread = lax.all_to_all(put, 'ctx', 0, 0, tiled=True)]
  transfers between devices with their start and end apart: 45 -> 32, of which waited for: 19 -> 12; matrix products, arithmetic and copies ran while one was open for 3% -> 2% of each run, Pallas kernels for 17% -> 20%
where the time goes in v7:
time: 244 us; the launch traced here: 243 us
  waiting for transfers between devices  78.1 us (32%)
  Pallas kernels  53.1 us (22%)
  starting transfers between devices  51.8 us (21%)
  blocking collectives  32.3 us (13%)
  local copies, waits for them, and re-layouts  23.4 us (10%)
  other arithmetic  2.87 us (1%)
    all_to_all x1, blocking collectives, shards(): spread = lax.all_to_all(put, 'ctx', 0, 0, tiled=True)  32.3 us
    all_to_all x1, waiting for transfers between devices, shards(): state_low = lax.all_to_all(states, 'ctx', 0, 0, tiled=True)  27.5 us
    pallas_call x11, Pallas kernels, whole(): pl.pallas_call(kernel, in_specs=[SCALAR if a is tokens else full for a in...  22 us
    unnamed x90, local copies, waits for them, and re-layouts  20.7 us
    ppermute x1, waiting for transfers between devices, shards(): lax.ppermute(halves[1], 'ctx', pair_perm(count, -s))  19.4 us
    pallas_call x5, Pallas kernels, product(): pl.pallas_call(functools.partial(product_kernel, turns, [len(w) for w in...  17.4 us
    pallas_call x2, Pallas kernels, outer(): pl.pallas_call(functools.partial(outer_kernel, len(pieces), own), grid=(s...  13.7 us
    ppermute x13, waiting for transfers between devices, over(): return lax.ppermute(x, 'head', perm)  10.4 us
  transfers between devices with their start and end apart: 32, of which 12 were waited for; matrix products, arithmetic and copies ran while one was open for 2% of the time, Pallas kernels for 20%

profile of v7, /device:TPU:0, one launch (start us, length us, event | category | flops | bytes accessed | tf_op | source)
XLA Modules:
  0.0 242.7 jit_solution(11316578944350174003)
XLA Ops:
  0.7 1.5 constant_dynamic-slice_fusion
  2.1 3.1 %collective-permute-start = (bf16[96,6144]{1,0:T(8,128)(2,1)S(1)}, bf16[96,6144]{1,0:T(8,128)(2,1)}, u32[]{:S(2)}, u32[]{:S(2)}) collective-permute-start(bf16[96,6144]{1,0:T(8,128)(2,1)S(1)} %constant_dynamic-slice_fusion), channel_id=1, source_target_pairs={{0,8},{4,12},{8,24},{12,28},{24,16},{28,20},{16,0},{20,4},{1,9},{5... | collective-permute-start | bytes 3538952 | tf_op jit(solution)/shard_map/ppermute | solution.py:382
  5.2 1.9 states.1
  7.1 32.3 %all_to_all.20.in_ref = bf16[8,144,128]{2,1,0:T(8,128)(2,1)S(1)} all-to-all(bf16[8,144,128]{2,1,0:T(8,128)(2,1)S(1)} %get-tuple-element.81), channel_id=1, replica_groups=mesh['ctx'=8,'head'=4] {'ctx'}, dimensions={0} | all-to-all | bytes 589824 | tf_op jit(solution)/shard_map/all_to_all | solution.py:402
  39.4 1.5 collective-permute-start.2
  42.4 4.9 %all-to-all-start.1 = ((bf16[8,128,128]{2,1,0:T(8,128)(2,1)}), bf16[8,128,128]{2,1,0:T(8,128)(2,1)S(1)}, u32[]{:S(2)}, u32[]{:S(2)}) async-start(bf16[8,128,128]{2,1,0:T(8,128)(2,1)} %scan.2), calls=%async_computation.1 | async-start | bytes 524288 | tf_op jit(solution)/shard_map/all_to_all | solution.py:407
  48.5 27.5 %all-to-all-done.1.state_ref = bf16[8,128,128]{2,1,0:T(8,128)(2,1)S(1)} async-done(((bf16[8,128,128]{2,1,0:T(8,128)(2,1)}), bf16[8,128,128]{2,1,0:T(8,128)(2,1)S(1)}, u32[]{:S(2)}, u32[]{:S(2)}) %all-to-all-start.1) | async-done | bytes 262176 | tf_op jit(solution)/shard_map/all_to_all | solution.py:407
  79.5 1.9 weights.1.intra_ref
  84.4 10.1 %collective-permute-done.4.refs_6_.refs_3_.refs_4_ = bf16[128,3072]{1,0:T(8,128)(2,1)S(1)} collective-permute-done((bf16[128,3072]{1,0:T(8,128)(2,1)}, bf16[128,3072]{1,0:T(8,128)(2,1)S(1)}, u32[]{:S(2)}, u32[]{:S(2)}) %collective-permute-start.4) | collective-permute-done | bytes 786464 | tf_op jit(solution)/shard_map/ppermute | solution.py:416
  95.0 1.9 collective-permute-start.6
  97.7 19.4 %collective-permute-done.10.refs_7_.refs_4_.refs_5_ = bf16[128,3072]{1,0:T(8,128)(2,1)S(1)} collective-permute-done((bf16[128,3072]{1,0:T(8,128)(2,1)}, bf16[128,3072]{1,0:T(8,128)(2,1)S(1)}, u32[]{:S(2)}, u32[]{:S(2)}) %collective-permute-start.10) | collective-permute-done | bytes 786464 | tf_op jit(solution)/shard_map/ppermute | solution.py:426
  117.1 1.5 collective-permute-start.11
  119.5 3.7 %collective-permute-done.11.there_ref = f32[1,384]{1,0:T(1,128)S(1)} collective-permute-done((f32[1,384]{1,0:T(1,128)S(1)}, f32[1,384]{1,0:T(1,128)S(1)}, u32[]{:S(2)}, u32[]{:S(2)}) %collective-permute-start.11) | collective-permute-done | bytes 1568 | tf_op jit(solution)/shard_map/ppermute | solution.py:385
  123.2 1.4 collective-permute-done.6.refs_1_.refs_13_
  125.1 1.5 collective-permute-start.12
  127.3 1.3 norm.1
  128.6 1.3 collective-permute-start.13
  129.9 2.9 %collective-permute-start.14 = (bf16[384,256]{1,0:T(8,128)(2,1)S(1)}, bf16[384,256]{1,0:T(8,128)(2,1)S(1)}, u32[]{:S(2)}, u32[]{:S(2)}) collective-permute-start(bf16[384,256]{1,0:T(8,128)(2,1)S(1)} %get-tuple-element.101), channel_id=1, source_target_pairs={{0,24},{4,28},{8,16},{12,20},{24,0},{28,4},{16,8},{20,12},{1,25},{... | collective-permute-start | bytes 589832 | tf_op jit(solution)/shard_map/ppermute | solution.py:439
  132.8 1.9 collective-permute-start.15
  134.8 4.8 %product.7 = bf16[384,256]{1,0:T(8,128)(2,1)S(1)} custom-call(s32[1]{0:T(128)} %bitcast.1.mine_ref.refs_0_, bf16[96,6144]{1,0:T(8,128)(2,1)} %collective-permute-done.refs_1_.refs_5_, bf16[96,6144]{1,0:T(8,128)(2,1)} %collective-permute-done.3.refs_2_.refs_6_, bf16[96,6144]{1,0:T(8,128)(2,1)} %collective-permute-done.2.refs_3_.refs_7_, ...), custom_call_target="tpu_custom_call" | custom-call | flops 1000 | bytes 1000 | tf_op jit(solution)/shard_map/product/pallas_call | solution.py:207
  140.1 4.1 %product.5 = bf16[384,256]{1,0:T(8,128)(2,1)S(1)} custom-call(s32[1]{0:T(128)} %bitcast.1.mine_ref.refs_0_, bf16[96,6144]{1,0:T(8,128)(2,1)} %collective-permute-done.1.refs_1_.refs_9_, bf16[96,6144]{1,0:T(8,128)(2,1)} %collective-permute-done.8.refs_2_.refs_10_, bf16[96,6144]{1,0:T(8,128)(2,1)} %collective-permute-done.7.refs_3_.refs_11_, ...), custom_call_target="tpu_custom_call" | custom-call | flops 1000 | bytes 1000 | tf_op jit(solution)/shard_map/product/pallas_call | solution.py:207
  144.3 9.8 %collective-permute-start.19 = (bf16[384,256]{1,0:T(8,128)(2,1)S(1)}, bf16[384,256]{1,0:T(8,128)(2,1)S(1)}, u32[]{:S(2)}, u32[]{:S(2)}) collective-permute-start(bf16[384,256]{1,0:T(8,128)(2,1)S(1)} %product.5), channel_id=1, source_target_pairs={{0,24},{4,28},{8,16},{12,20},{24,0},{28,4},{16,8},{20,12},{1,25},{... | collective-permute-start | bytes 589832 | tf_op jit(solution)/shard_map/ppermute | solution.py:445
  154.0 2.8 %product.6.refs_0_ = bf16[384,256]{1,0:T(8,128)(2,1)S(1)} custom-call(s32[1]{0:T(128)} %bitcast.1.mine_ref.refs_0_, bf16[384,6144]{1,0:T(8,128)(2,1)S(1)} %bitcast.12, bf16[128,6144]{1,0:T(8,128)(2,1)S(1)} %bitcast.8, bf16[128,3072]{1,0:T(8,128)(2,1)S(1)} %collective-permute-done.4.refs_6_.refs_3_.refs_4_, ...), custom_call_target="tpu_custom_call" | custom-call | flops 1000 | bytes 1000 | tf_op jit(solution)/shard_map/product/pallas_call | solution.py:207
  156.8 3.4 %product.8.refs_6_ = bf16[192,256]{1,0:T(8,128)(2,1)S(1)} custom-call(s32[1]{0:T(128)} %bitcast.1.mine_ref.refs_0_, bf16[96,6144]{1,0:T(8,128)(2,1)} %collective-permute-done.6.refs_1_.refs_13_, bf16[96,6144]{1,0:T(8,128)(2,1)S(1)} %collective-permute-done.17.refs_2_.refs_14_, bf16[128,6144]{1,0:T(8,128)(2,1)S(1)} %bitcast.9, ...), custom_call_target="tpu_custom_call" | custom-call | flops 1000 | bytes 1000 | tf_op jit(solution)/shard_map/product/pallas_call | solution.py:207
  160.4 2.8 %collective-permute-done.20.refs_2_.refs_16_ = bf16[96,6144]{1,0:T(8,128)(2,1)S(1)} collective-permute-done((bf16[96,6144]{1,0:T(8,128)(2,1)S(1)}, bf16[96,6144]{1,0:T(8,128)(2,1)S(1)}, u32[]{:S(2)}, u32[]{:S(2)}) %collective-permute-start.20) | collective-permute-done | bytes 1179680 | tf_op jit(solution)/shard_map/ppermute | solution.py:385
  163.3 2.3 product.9
  165.5 2.5 %collective-permute-start.21 = (bf16[384,256]{1,0:T(8,128)(2,1)S(1)}, bf16[384,256]{1,0:T(8,128)(2,1)S(1)}, u32[]{:S(2)}, u32[]{:S(2)}) collective-permute-start(bf16[384,256]{1,0:T(8,128)(2,1)S(1)} %product.9), channel_id=1, source_target_pairs={{0,8},{4,12},{8,24},{12,28},{24,16},{28,20},{16,0},{20,4},{1,9},{5... | collective-permute-start | bytes 589832 | tf_op jit(solution)/shard_map/ppermute | solution.py:452
  168.1 7.1 %outer.2 = (bf16[128,3072]{1,0:T(8,128)(2,1)S(1)}, bf16[128,3072]{1,0:T(8,128)(2,1)}) custom-call(bf16[384,256]{1,0:T(8,128)(2,1)S(1)} %get-tuple-element.141.refs_0_, bf16[384,256]{1,0:T(8,128)(2,1)S(1)} %collective-permute-done.13.refs_1_, bf16[384,256]{1,0:T(8,128)(2,1)S(1)} %collective-permute-done.14.refs_2_, ...), custom_call_target="tpu_custom_call" | custom-call | flops 1000 | bytes 1000 | tf_op jit(solution)/shard_map/outer/pallas_call | solution.py:247
  177.4 3.6 %collective-permute-done.24 = f32[1,1024]{1,0:T(1,128)S(1)} collective-permute-done((f32[1,1024]{1,0:T(1,128)S(1)}, f32[1,1024]{1,0:T(1,128)S(1)}, u32[]{:S(2)}, u32[]{:S(2)}) %collective-permute-start.24) | collective-permute-done | bytes 4128 | tf_op jit(solution)/shard_map/ppermute | solution.py:467
  180.9 2.0 collective-permute-start.25
  186.0 1.6 collective-permute-done.23.there_ref
  187.7 2.2 grads.1
  190.8 4.1 %all-to-all-start.2 = ((bf16[8,144,128]{2,1,0:T(8,128)(2,1)}), bf16[8,144,128]{2,1,0:T(8,128)(2,1)}, u32[]{:S(2)}, u32[]{:S(2)}) async-start(bf16[8,144,128]{2,1,0:T(8,128)(2,1)} %get-tuple-element.140), calls=%async_computation.2 | async-start | bytes 589824 | tf_op jit(solution)/shard_map/all_to_all | solution.py:477
  194.8 1.9 collective-permute-start.27
  196.8 2.3 copy-done.1
  199.1 1.3 copy-done.14
  200.4 1.3 copy-done.16
  201.6 1.3 copy-done.18
  202.9 1.3 copy-done.20
  204.2 6.6 %outer.3 = (bf16[128,3072]{1,0:T(8,128)(2,1)S(1)}, bf16[128,3072]{1,0:T(8,128)(2,1)S(1)}) custom-call(bf16[384,256]{1,0:T(8,128)(2,1)S(1)} %get-tuple-element.141.refs_0_, bf16[384,256]{1,0:T(8,128)(2,1)S(1)} %copy-done.27, bf16[384,256]{1,0:T(8,128)(2,1)S(1)} %copy-done.29, bf16[384,256]{1,0:T(8,128)(2,1)S(1)} %copy-done.31, ...), custom_call_target="tpu_custom_call" | custom-call | flops 1000 | bytes 1000 | tf_op jit(solution)/shard_map/outer/pallas_call | solution.py:247
  212.5 1.4 add.143
  214.1 1.7 scan.3
  215.8 5.8 %all-to-all-start.3 = ((bf16[8,128,128]{2,1,0:T(8,128)(2,1)}), bf16[8,128,128]{2,1,0:T(8,128)(2,1)}, u32[]{:S(2)}, u32[]{:S(2)}) async-start(bf16[8,128,128]{2,1,0:T(8,128)(2,1)} %scan.3), calls=%async_computation.3 | async-start | bytes 524288 | tf_op jit(solution)/shard_map/all_to_all | solution.py:483
  224.9 4.5 %inside.1 = (bf16[384,1024]{1,0:T(8,128)(2,1)}, f32[384,1024]{1,0:T(8,128)S(1)}, f32[384,1024]{1,0:T(8,128)S(1)}) custom-call(bf16[384,1024]{1,0:T(8,128)(2,1)S(1)} %copy-done.37, bf16[384,1024]{1,0:T(8,128)(2,1)S(1)} %copy-done.12, bf16[384,1024]{1,0:T(8,128)(2,1)S(1)} %copy-done.5, bf16[384,1024]{1,0:T(8,128)(2,1)S(1)} %copy-done.8, ...), custom_call_target="tpu_custom_call" | custom-call | flops 1000 | bytes 1000 | tf_op jit(solution)/shard_map/inside/pallas_call | solution.py:371
  230.5 4.8 %all-to-all-done.3.state_ref = bf16[8,128,128]{2,1,0:T(8,128)(2,1)} async-done(((bf16[8,128,128]{2,1,0:T(8,128)(2,1)}), bf16[8,128,128]{2,1,0:T(8,128)(2,1)}, u32[]{:S(2)}, u32[]{:S(2)}) %all-to-all-start.3) | async-done | bytes 262176 | tf_op jit(solution)/shard_map/all_to_all | solution.py:483
  235.3 1.4 copy-done.25
  236.7 3.1 %outside.1 = (bf16[384,1024]{1,0:T(8,128)(2,1)}, bf16[384,1024]{1,0:T(8,128)(2,1)}) custom-call(bf16[384,1024]{1,0:T(8,128)(2,1)S(1)} %copy-done.5, bf16[384,1024]{1,0:T(8,128)(2,1)S(1)} %copy-done.8, bf16[8,128,128]{2,1,0:T(8,128)(2,1)} %all-to-all-done.3.state_ref, f32[384,8]{1,0:T(8,128)S(1)} %get-tuple-element.87.turned_ref, ...), custom_call_target="tpu_custom_call" | custom-call | flops 1000 | bytes 1000 | tf_op jit(solution)/shard_map/outside/pallas_call | solution.py:371
  239.8 2.9 %sum.1 = bf16[128,6144]{1,0:T(8,128)(2,1)} custom-call(bf16[128,3072]{1,0:T(8,128)(2,1)S(1)} %copy-done.33, bf16[128,3072]{1,0:T(8,128)(2,1)} %collective-permute-done.26.refs_1_, bf16[128,3072]{1,0:T(8,128)(2,1)S(1)} %copy-done.35, bf16[128,3072]{1,0:T(8,128)(2,1)} %collective-permute-done.28.refs_3_), custom_call_target="tpu_custom_call" | custom-call | flops 1000 | bytes 1000 | tf_op jit(solution)/shard_map/sum/pallas_call | solution.py:371
  (135 shorter events, 25.6 us)
Async XLA Ops:
  2.1 37.3 %collective-permute-start = (bf16[96,6144]{1,0:T(8,128)(2,1)S(1)}, bf16[96,6144]{1,0:T(8,128)(2,1)}, u32[]{:S(2)}, u32[]{:S(2)}) collective-permute-start(bf16[96,6144]{1,0:T(8,128)(2,1)S(1)} %constant_dynamic-slice_fusion), channel_id=1, source_target_pairs={{0,8},{4,12},{8,24},{12,28},{24,16},{28,20},{16,0},{20,4},{1,9},{5... | collective-permute-start | bytes 3538952 | tf_op jit(solution)/shard_map/ppermute | solution.py:382
  7.1 40.2 %copy-start = (bf16[8,16,6144]{2,1,0:T(8,128)(2,1)S(1)}, bf16[8,16,6144]{2,1,0:T(8,128)(2,1)}, u32[]{:S(2)}) copy-start(bf16[8,16,6144]{2,1,0:T(8,128)(2,1)} %param.12) | copy-start | bytes 4718596
  39.4 45.0 %collective-permute-start.3 = (bf16[96,6144]{1,0:T(8,128)(2,1)}, bf16[96,6144]{1,0:T(8,128)(2,1)}, u32[]{:S(2)}, u32[]{:S(2)}) collective-permute-start(bf16[96,6144]{1,0:T(8,128)(2,1)} %collective-permute-done.refs_1_.refs_5_), channel_id=1, source_target_pairs={{0,1},{1,0},{2,3},{3,2},{4,5},{5,4},{6,7},{7,6},{8,9},{9,8},{10,11... | collective-permute-start | bytes 3538952 | tf_op jit(solution)/shard_map/ppermute | solution.py:385
  39.4 45.0 %collective-permute-start.2 = (bf16[96,6144]{1,0:T(8,128)(2,1)}, bf16[96,6144]{1,0:T(8,128)(2,1)}, u32[]{:S(2)}, u32[]{:S(2)}) collective-permute-start(bf16[96,6144]{1,0:T(8,128)(2,1)} %collective-permute-done.refs_1_.refs_5_), channel_id=1, source_target_pairs={{0,2},{1,3},{2,0},{3,1},{4,6},{5,7},{6,4},{7,5},{8,10},{9,11},{10,... | collective-permute-start | bytes 3538952 | tf_op jit(solution)/shard_map/ppermute | solution.py:385
  40.9 43.5 %collective-permute-start.1 = (bf16[96,6144]{1,0:T(8,128)(2,1)}, bf16[96,6144]{1,0:T(8,128)(2,1)}, u32[]{:S(2)}, u32[]{:S(2)}) collective-permute-start(bf16[96,6144]{1,0:T(8,128)(2,1)} %collective-permute-done.refs_1_.refs_5_), channel_id=1, source_target_pairs={{0,8},{4,12},{8,24},{12,28},{24,16},{28,20},{16,0},{20,4},{1,9},{5... | collective-permute-start | bytes 3538952 | tf_op jit(solution)/shard_map/ppermute | solution.py:382
  42.4 33.6 %all-to-all-start.1 = ((bf16[8,128,128]{2,1,0:T(8,128)(2,1)}), bf16[8,128,128]{2,1,0:T(8,128)(2,1)S(1)}, u32[]{:S(2)}, u32[]{:S(2)}) async-start(bf16[8,128,128]{2,1,0:T(8,128)(2,1)} %scan.2), calls=%async_computation.1 | async-start | bytes 524288 | tf_op jit(solution)/shard_map/all_to_all | solution.py:407
  76.7 17.8 %collective-permute-start.4 = (bf16[128,3072]{1,0:T(8,128)(2,1)}, bf16[128,3072]{1,0:T(8,128)(2,1)S(1)}, u32[]{:S(2)}, u32[]{:S(2)}) collective-permute-start(bf16[128,3072]{1,0:T(8,128)(2,1)} %get-tuple-element.85), channel_id=1, source_target_pairs={{0,4},{4,0},{8,12},{12,8},{16,20},{20,16},{24,28},{28,24},{1,5},{5... | collective-permute-start | bytes 2359304 | tf_op jit(solution)/shard_map/ppermute | solution.py:416
  83.2 43.4 %copy-start.38 = (f32[1024]{0:T(1024)S(1)}, f32[1024]{0:T(1024)}, u32[]{:S(2)}) copy-start(f32[1024]{0:T(1024)} %param.11) | copy-start | bytes 12292
  83.2 1.2 collective-permute-start.5
  84.4 42.3 %copy-start.40 = (f32[1,384]{1,0:T(1,128)}, f32[1,384]{1,0:T(1,128)S(1)}, u32[]{:S(2)}) copy-start(f32[1,384]{1,0:T(1,128)S(1)} %add.126.here_ref) | copy-start | bytes 4612
  94.5 28.7 %collective-permute-start.8 = (bf16[96,6144]{1,0:T(8,128)(2,1)}, bf16[96,6144]{1,0:T(8,128)(2,1)}, u32[]{:S(2)}, u32[]{:S(2)}) collective-permute-start(bf16[96,6144]{1,0:T(8,128)(2,1)} %collective-permute-done.1.refs_1_.refs_9_), channel_id=1, source_target_pairs={{0,1},{1,0},{2,3},{3,2},{4,5},{5,4},{6,7},{7,6},{8,9},{9,8},{10,11... | collective-permute-start | bytes 3538952 | tf_op jit(solution)/shard_map/ppermute | solution.py:385
  94.5 28.7 %collective-permute-start.7 = (bf16[96,6144]{1,0:T(8,128)(2,1)}, bf16[96,6144]{1,0:T(8,128)(2,1)}, u32[]{:S(2)}, u32[]{:S(2)}) collective-permute-start(bf16[96,6144]{1,0:T(8,128)(2,1)} %collective-permute-done.1.refs_1_.refs_9_), channel_id=1, source_target_pairs={{0,2},{1,3},{2,0},{3,1},{4,6},{5,7},{6,4},{7,5},{8,10},{9,11},{10,... | collective-permute-start | bytes 3538952 | tf_op jit(solution)/shard_map/ppermute | solution.py:385
  95.0 29.6 %collective-permute-start.6 = (bf16[96,6144]{1,0:T(8,128)(2,1)}, bf16[96,6144]{1,0:T(8,128)(2,1)}, u32[]{:S(2)}, u32[]{:S(2)}) collective-permute-start(bf16[96,6144]{1,0:T(8,128)(2,1)} %collective-permute-done.1.refs_1_.refs_9_), channel_id=1, source_target_pairs={{0,8},{4,12},{8,24},{12,28},{24,16},{28,20},{16,0},{20,4},{1,9},{5... | collective-permute-start | bytes 3538952 | tf_op jit(solution)/shard_map/ppermute | solution.py:382
  97.0 27.7 %collective-permute-start.9 = (bf16[96,6144]{1,0:T(8,128)(2,1)}, bf16[96,6144]{1,0:T(8,128)(2,1)}, u32[]{:S(2)}, u32[]{:S(2)}) collective-permute-start(bf16[96,6144]{1,0:T(8,128)(2,1)} %collective-permute-done.2.refs_3_.refs_7_), channel_id=1, source_target_pairs={{0,1},{1,0},{2,3},{3,2},{4,5},{5,4},{6,7},{7,6},{8,9},{9,8},{10,11... | collective-permute-start | bytes 3538952 | tf_op jit(solution)/shard_map/ppermute | solution.py:385
  97.0 20.2 %collective-permute-start.10 = (bf16[128,3072]{1,0:T(8,128)(2,1)}, bf16[128,3072]{1,0:T(8,128)(2,1)S(1)}, u32[]{:S(2)}, u32[]{:S(2)}) collective-permute-start(bf16[128,3072]{1,0:T(8,128)(2,1)} %get-tuple-element.157), channel_id=1, source_target_pairs={{0,4},{4,0},{8,12},{12,8},{16,20},{20,16},{24,28},{28,24},{1,5},{5... | collective-permute-start | bytes 2359304 | tf_op jit(solution)/shard_map/ppermute | solution.py:426
  97.7 29.0 %copy-start.3 = (f32[384,1024]{1,0:T(8,128)S(1)}, f32[384,1024]{1,0:T(8,128)}, u32[]{:S(2)}) copy-start(f32[384,1024]{1,0:T(8,128)} %copy-done.2) | copy-start | bytes 4718596
  117.1 6.1 %collective-permute-start.11 = (f32[1,384]{1,0:T(1,128)S(1)}, f32[1,384]{1,0:T(1,128)S(1)}, u32[]{:S(2)}, u32[]{:S(2)}) collective-permute-start(f32[1,384]{1,0:T(1,128)S(1)} %add.126.here_ref), channel_id=1, source_target_pairs={{0,2},{1,3},{2,0},{3,1},{4,6},{5,7},{6,4},{7,5},{8,10},{9,11},{10,... | collective-permute-start | bytes 4616 | tf_op jit(solution)/shard_map/ppermute | solution.py:385
  124.6 8.2 %collective-permute-start.17 = (bf16[96,6144]{1,0:T(8,128)(2,1)}, bf16[96,6144]{1,0:T(8,128)(2,1)S(1)}, u32[]{:S(2)}, u32[]{:S(2)}) collective-permute-start(bf16[96,6144]{1,0:T(8,128)(2,1)} %collective-permute-done.6.refs_1_.refs_13_), channel_id=1, source_target_pairs={{0,1},{1,0},{2,3},{3,2},{4,5},{5,4},{6,7},{7,6},{8,9},{9,8},{10,11... | collective-permute-start | bytes 3538952 | tf_op jit(solution)/shard_map/ppermute | solution.py:385
  124.6 10.2 %collective-permute-start.16 = (bf16[96,6144]{1,0:T(8,128)(2,1)}, bf16[96,6144]{1,0:T(8,128)(2,1)S(1)}, u32[]{:S(2)}, u32[]{:S(2)}) collective-permute-start(bf16[96,6144]{1,0:T(8,128)(2,1)} %collective-permute-done.7.refs_3_.refs_11_), channel_id=1, source_target_pairs={{0,1},{1,0},{2,3},{3,2},{4,5},{5,4},{6,7},{7,6},{8,9},{9,8},{10,11... | collective-permute-start | bytes 3538952 | tf_op jit(solution)/shard_map/ppermute | solution.py:385
  125.1 35.2 %collective-permute-start.12 = (bf16[96,6144]{1,0:T(8,128)(2,1)}, bf16[96,6144]{1,0:T(8,128)(2,1)S(1)}, u32[]{:S(2)}, u32[]{:S(2)}) collective-permute-start(bf16[96,6144]{1,0:T(8,128)(2,1)} %collective-permute-done.6.refs_1_.refs_13_), channel_id=1, source_target_pairs={{0,2},{1,3},{2,0},{3,1},{4,6},{5,7},{6,4},{7,5},{8,10},{9,11},{10,... | collective-permute-start | bytes 3538952 | tf_op jit(solution)/shard_map/ppermute | solution.py:385
  128.6 15.6 %collective-permute-start.13 = (bf16[384,256]{1,0:T(8,128)(2,1)S(1)}, bf16[384,256]{1,0:T(8,128)(2,1)S(1)}, u32[]{:S(2)}, u32[]{:S(2)}) collective-permute-start(bf16[384,256]{1,0:T(8,128)(2,1)S(1)} %get-tuple-element.100), channel_id=1, source_target_pairs={{0,8},{4,12},{8,24},{12,28},{24,16},{28,20},{16,0},{20,4},{1,9},{5... | collective-permute-start | bytes 589832 | tf_op jit(solution)/shard_map/ppermute | solution.py:439
  129.9 30.3 %collective-permute-start.14 = (bf16[384,256]{1,0:T(8,128)(2,1)S(1)}, bf16[384,256]{1,0:T(8,128)(2,1)S(1)}, u32[]{:S(2)}, u32[]{:S(2)}) collective-permute-start(bf16[384,256]{1,0:T(8,128)(2,1)S(1)} %get-tuple-element.101), channel_id=1, source_target_pairs={{0,24},{4,28},{8,16},{12,20},{24,0},{28,4},{16,8},{20,12},{1,25},{... | collective-permute-start | bytes 589832 | tf_op jit(solution)/shard_map/ppermute | solution.py:439
  132.8 35.2 %copy-start.13 = (bf16[96,6144]{1,0:T(8,128)(2,1)}, bf16[96,6144]{1,0:T(8,128)(2,1)S(1)}, u32[]{:S(2)}) copy-start(bf16[96,6144]{1,0:T(8,128)(2,1)S(1)} %collective-permute-done.17.refs_2_.refs_14_) | copy-start | bytes 3538948
  132.8 27.4 %collective-permute-start.15 = (bf16[384,256]{1,0:T(8,128)(2,1)S(1)}, bf16[384,256]{1,0:T(8,128)(2,1)S(1)}, u32[]{:S(2)}, u32[]{:S(2)}) collective-permute-start(bf16[384,256]{1,0:T(8,128)(2,1)S(1)} %get-tuple-element.102), channel_id=1, source_target_pairs={{0,16},{4,20},{8,0},{12,4},{24,8},{28,12},{16,24},{20,28},{1,17},{... | collective-permute-start | bytes 589832 | tf_op jit(solution)/shard_map/ppermute | solution.py:439
  134.8 33.3 %copy-start.15 = (bf16[96,6144]{1,0:T(8,128)(2,1)}, bf16[96,6144]{1,0:T(8,128)(2,1)S(1)}, u32[]{:S(2)}) copy-start(bf16[96,6144]{1,0:T(8,128)(2,1)S(1)} %collective-permute-done.16.refs_4_.refs_12_) | copy-start | bytes 3538948
  134.8 19.2 %slice-start = ((s8[4718592]{0:T(1024)(128)(4,1)}), s8[4194304]{0:T(1024)(128)(4,1)S(1)}, s32[]{:S(2)}) async-start(s8[4718592]{0:T(1024)(128)(4,1)} %bitcast.11), calls=%async_computation.4 | async-start | bytes 8388608
  139.6 14.5 %slice-start.1 = ((s8[4718592]{0:T(1024)(128)(4,1)}), s8[524288]{0:T(1024)(128)(4,1)S(1)}, s32[]{:S(2)}) async-start(s8[4718592]{0:T(1024)(128)(4,1)} %bitcast.11), calls=%async_computation.5 | async-start | bytes 1048576
  139.6 20.7 %collective-permute-start.18 = (bf16[384,256]{1,0:T(8,128)(2,1)S(1)}, bf16[384,256]{1,0:T(8,128)(2,1)S(1)}, u32[]{:S(2)}, u32[]{:S(2)}) collective-permute-start(bf16[384,256]{1,0:T(8,128)(2,1)S(1)} %product.7), channel_id=1, source_target_pairs={{0,16},{4,20},{8,0},{12,4},{24,8},{28,12},{16,24},{20,28},{1,17},{... | collective-permute-start | bytes 589832 | tf_op jit(solution)/shard_map/ppermute | solution.py:443
  144.3 23.8 %copy-start.26 = (bf16[384,256]{1,0:T(8,128)(2,1)}, bf16[384,256]{1,0:T(8,128)(2,1)S(1)}, u32[]{:S(2)}) copy-start(bf16[384,256]{1,0:T(8,128)(2,1)S(1)} %collective-permute-done.13.refs_1_) | copy-start | bytes 589828
  144.3 16.1 %collective-permute-start.19 = (bf16[384,256]{1,0:T(8,128)(2,1)S(1)}, bf16[384,256]{1,0:T(8,128)(2,1)S(1)}, u32[]{:S(2)}, u32[]{:S(2)}) collective-permute-start(bf16[384,256]{1,0:T(8,128)(2,1)S(1)} %product.5), channel_id=1, source_target_pairs={{0,24},{4,28},{8,16},{12,20},{24,0},{28,4},{16,8},{20,12},{1,25},{... | collective-permute-start | bytes 589832 | tf_op jit(solution)/shard_map/ppermute | solution.py:445
  160.3 7.8 %copy-start.28 = (bf16[384,256]{1,0:T(8,128)(2,1)}, bf16[384,256]{1,0:T(8,128)(2,1)S(1)}, u32[]{:S(2)}) copy-start(bf16[384,256]{1,0:T(8,128)(2,1)S(1)} %collective-permute-done.14.refs_2_) | copy-start | bytes 589828
  160.3 2.9 %collective-permute-start.20 = (bf16[96,6144]{1,0:T(8,128)(2,1)S(1)}, bf16[96,6144]{1,0:T(8,128)(2,1)S(1)}, u32[]{:S(2)}, u32[]{:S(2)}) collective-permute-start(bf16[96,6144]{1,0:T(8,128)(2,1)S(1)} %collective-permute-done.12.refs_1_.refs_15_), channel_id=1, source_target_pairs={{0,1},{1,0},{2,3},{3,2},{4,5},{5,4},{6,7},{7,6},{8,9},{9,8},{10,11... | collective-permute-start | bytes 3538952 | tf_op jit(solution)/shard_map/ppermute | solution.py:385
  165.5 9.7 %collective-permute-start.21 = (bf16[384,256]{1,0:T(8,128)(2,1)S(1)}, bf16[384,256]{1,0:T(8,128)(2,1)S(1)}, u32[]{:S(2)}, u32[]{:S(2)}) collective-permute-start(bf16[384,256]{1,0:T(8,128)(2,1)S(1)} %product.9), channel_id=1, source_target_pairs={{0,8},{4,12},{8,24},{12,28},{24,16},{28,20},{16,0},{20,4},{1,9},{5... | collective-permute-start | bytes 589832 | tf_op jit(solution)/shard_map/ppermute | solution.py:452
  175.3 38.6 %collective-permute-start.26 = (bf16[128,3072]{1,0:T(8,128)(2,1)}, bf16[128,3072]{1,0:T(8,128)(2,1)}, u32[]{:S(2)}, u32[]{:S(2)}) collective-permute-start(bf16[128,3072]{1,0:T(8,128)(2,1)} %get-tuple-element.139), channel_id=1, source_target_pairs={{0,4},{4,0},{8,12},{12,8},{16,20},{20,16},{24,28},{28,24},{1,5},{5... | collective-permute-start | bytes 2359304 | tf_op jit(solution)/shard_map/ppermute | solution.py:457
  176.1 11.6 %copy-start.11 = (bf16[384,1024]{1,0:T(8,128)(2,1)S(1)}, bf16[384,1024]{1,0:T(8,128)(2,1)}, u32[]{:S(2)}) copy-start(bf16[384,1024]{1,0:T(8,128)(2,1)} %q_ref.6) | copy-start | bytes 2359300
  177.3 3.7 %collective-permute-start.24 = (f32[1,1024]{1,0:T(1,128)S(1)}, f32[1,1024]{1,0:T(1,128)S(1)}, u32[]{:S(2)}, u32[]{:S(2)}) collective-permute-start(f32[1,1024]{1,0:T(1,128)S(1)} %get-tuple-element.135), channel_id=1, source_target_pairs={{0,8},{4,12},{8,0},{12,4},{16,24},{20,28},{24,16},{28,20},{1,9},{5... | collective-permute-start | bytes 12296 | tf_op jit(solution)/shard_map/ppermute | solution.py:467
  180.9 4.5 %collective-permute-start.25 = (f32[1,1024]{1,0:T(1,128)S(1)}, f32[1,1024]{1,0:T(1,128)S(1)}, u32[]{:S(2)}, u32[]{:S(2)}) collective-permute-start(f32[1,1024]{1,0:T(1,128)S(1)} %add.141), channel_id=1, source_target_pairs={{0,16},{4,20},{8,24},{12,28},{16,0},{20,4},{24,8},{28,12},{1,17},{... | collective-permute-start | bytes 12296 | tf_op jit(solution)/shard_map/ppermute | solution.py:467
  182.9 1.2 collective-permute-start.22
  184.1 3.6 %collective-permute-start.23 = (f32[1,384]{1,0:T(1,128)S(1)}, f32[1,384]{1,0:T(1,128)S(1)}, u32[]{:S(2)}, u32[]{:S(2)}) collective-permute-start(f32[1,384]{1,0:T(1,128)S(1)} %add.140.here_ref), channel_id=1, source_target_pairs={{0,2},{1,3},{2,0},{3,1},{4,6},{5,7},{6,4},{7,5},{8,10},{9,11},{10,... | collective-permute-start | bytes 4616 | tf_op jit(solution)/shard_map/ppermute | solution.py:385
  187.6 9.1 %copy-start.27 = (bf16[384,256]{1,0:T(8,128)(2,1)S(1)}, bf16[384,256]{1,0:T(8,128)(2,1)}, u32[]{:S(2)}) copy-start(bf16[384,256]{1,0:T(8,128)(2,1)} %copy-done.26) | copy-start | bytes 589828
  187.6 9.1 %copy-start.29 = (bf16[384,256]{1,0:T(8,128)(2,1)S(1)}, bf16[384,256]{1,0:T(8,128)(2,1)}, u32[]{:S(2)}) copy-start(bf16[384,256]{1,0:T(8,128)(2,1)} %copy-done.28) | copy-start | bytes 589828
  187.7 9.1 %copy-start.31 = (bf16[384,256]{1,0:T(8,128)(2,1)S(1)}, bf16[384,256]{1,0:T(8,128)(2,1)}, u32[]{:S(2)}) copy-start(bf16[384,256]{1,0:T(8,128)(2,1)} %copy-done.30) | copy-start | bytes 589828
  190.8 23.1 %all-to-all-start.2 = ((bf16[8,144,128]{2,1,0:T(8,128)(2,1)}), bf16[8,144,128]{2,1,0:T(8,128)(2,1)}, u32[]{:S(2)}, u32[]{:S(2)}) async-start(bf16[8,144,128]{2,1,0:T(8,128)(2,1)} %get-tuple-element.140), calls=%async_computation.2 | async-start | bytes 589824 | tf_op jit(solution)/shard_map/all_to_all | solution.py:477
  194.8 17.7 %collective-permute-start.27 = (f32[1,1024]{1,0:T(1,128)}, f32[1,1024]{1,0:T(1,128)S(1)}, u32[]{:S(2)}, u32[]{:S(2)}) collective-permute-start(f32[1,1024]{1,0:T(1,128)} %add.142), channel_id=1, source_target_pairs={{0,4},{4,0},{8,12},{12,8},{16,20},{20,16},{24,28},{28,24},{1,5},{5... | collective-permute-start | bytes 12296 | tf_op jit(solution)/shard_map/ppermute | solution.py:472
  204.2 17.5 %copy-start.8 = (bf16[384,1024]{1,0:T(8,128)(2,1)S(1)}, bf16[384,1024]{1,0:T(8,128)(2,1)}, u32[]{:S(2)}) copy-start(bf16[384,1024]{1,0:T(8,128)(2,1)} %v_ref.7) | copy-start | bytes 2359300
  212.5 9.1 %copy-start.5 = (bf16[384,1024]{1,0:T(8,128)(2,1)S(1)}, bf16[384,1024]{1,0:T(8,128)(2,1)}, u32[]{:S(2)}) copy-start(bf16[384,1024]{1,0:T(8,128)(2,1)} %k_ref.7) | copy-start | bytes 2359300
  213.9 25.9 %collective-permute-start.28 = (bf16[128,3072]{1,0:T(8,128)(2,1)}, bf16[128,3072]{1,0:T(8,128)(2,1)}, u32[]{:S(2)}, u32[]{:S(2)}) collective-permute-start(bf16[128,3072]{1,0:T(8,128)(2,1)} %copy-done.42), channel_id=1, source_target_pairs={{0,4},{4,0},{8,12},{12,8},{16,20},{20,16},{24,28},{28,24},{1,5},{5... | collective-permute-start | bytes 2359304 | tf_op jit(solution)/shard_map/ppermute | solution.py:481
  215.8 19.5 %all-to-all-start.3 = ((bf16[8,128,128]{2,1,0:T(8,128)(2,1)}), bf16[8,128,128]{2,1,0:T(8,128)(2,1)}, u32[]{:S(2)}, u32[]{:S(2)}) async-start(bf16[8,128,128]{2,1,0:T(8,128)(2,1)} %scan.3), calls=%async_computation.3 | async-start | bytes 524288 | tf_op jit(solution)/shard_map/all_to_all | solution.py:483
  (29 other events, 66.7 us)

commit v8 on v6

--- a/solution.py
+++ b/solution.py
@@ -401,32 +401,36 @@
     hold = lax.optimization_barrier
     scan_shape = jax.ShapeDtypeStruct((count, rows, size), BF)
 
-    ra1 = ring(first_piece(grad_out, 0))
+    firsts = [first_piece(grad_out, c) for c in range(CHUNKS)]
+    halves = [weight_own[:, c * deep : (c + 1) * deep] for c in range(CHUNKS)]
+
+    def swap(half):
+        return [lax.ppermute(half, "ctx", pair_perm(count, -s)) for s in range(1, minor)]
+
+    ra1 = ring(firsts[0])
+    others = [swap(halves[0])]
     put, run, turned = whole(
         state_kernel,
         [put_shape, jax.ShapeDtypeStruct((heads, tok), FL), jax.ShapeDtypeStruct((tok, heads), FL)],
         "states", log_decay, key_rows, value_rows,
     )
+    rb1 = ring(after(firsts[1], put))
     spread = lax.all_to_all(put, "ctx", 0, 0, tiled=True)
-    first = first_piece(after(grad_out, put), 1)
     intra = whole(
         weights_kernel, wide_f, "weights", query_rows, key_rows, value_rows, run, turned
     )
-    ra1, spread, intra, first = hold((ra1, spread, intra, first))
-
-    rb1, ya1, na1 = ring(first), other_of(ra1), near_of(ra1)
+    ra1, spread, intra, others[0], halves[1] = hold((ra1, spread, intra, others[0], halves[1]))
+
+    ya1, na1 = other_of(ra1), near_of(ra1)
+    others.append(swap(halves[1]))
     states = whole(functools.partial(scan_kernel, False), scan_shape, "scan", spread)
     state_low = lax.all_to_all(states, "ctx", 0, 0, tiled=True)
     order = feature_order(heads, size, count)
-    halves = [
-        after(weight_own, states)[:, c * deep : (c + 1) * deep] for c in range(CHUNKS)
-    ]
-    ra1, rb1, ya1, na1, state_low, order, halves = hold(
-        (ra1, rb1, ya1, na1, state_low, order, halves)
+    ra1, rb1, ya1, na1, state_low, order, others[1] = hold(
+        (ra1, rb1, ya1, na1, state_low, order, others[1])
     )
 
     ra2, yb1, nb1, fa1 = ring(ra1), other_of(rb1), near_of(rb1), near_of(ya1)
-    others = [[lax.ppermute(halves[0], "ctx", pair_perm(count, -s)) for s in range(1, minor)]]
     fa1, state_low = hold((fa1, state_low))
     state_low = state_low.reshape(heads, size, size)
     attn_out, squares = whole(
@@ -434,55 +438,50 @@
     )
     squares = squares + near_of(squares)
     squares_there = other_of(squares)
-    ra2, rb1, yb1, nb1, others[0], squares_there = hold(
-        (ra2, rb1, yb1, nb1, others[0], squares_there)
-    )
+    ra2, rb1, yb1, nb1, squares_there = hold((ra2, rb1, yb1, nb1, squares_there))
 
     rb2, ya2, na2, fb1 = ring(rb1), other_of(ra2), near_of(ra2), near_of(yb1)
-    others.append([lax.ppermute(halves[1], "ctx", pair_perm(count, -s)) for s in range(1, minor)])
     inv_rms, *sent = whole(
         functools.partial(norm_kernel, features), [row_f] + [part_b] * LINE, "norm",
         tokens, attn_out, squares, squares_there, gain_row, order,
     )
-    fb1, na2, sent = hold((fb1, na2, sent))
-    normed = [sent[0], lax.ppermute(sent[1], "ctx", ring_perm(count, 1)), None, None]
-    ra2, rb2, ya2, others[1], normed[1] = hold((ra2, rb2, ya2, others[1], normed[1]))
-
-    ra3, yb2, nb2, fa2 = ring(ra2), other_of(rb2), near_of(rb2), near_of(ya2)
-    normed[3] = lax.ppermute(sent[3], "ctx", ring_perm(count, 3))
     mine_part = product(
         tokens, [[grad_out]] * CHUNKS, weight_own, others, 0, True, None, whole=True
     )
-    rb2, ra3, yb2, nb2, fa2, normed[3], mine_part = hold(
-        (rb2, ra3, yb2, nb2, fa2, normed[3], mine_part)
-    )
-
-    rb3, ya3, na3, fb2 = ring(rb2), other_of(ra3), near_of(ra3), near_of(yb2)
-    normed[2] = lax.ppermute(sent[2], "ctx", ring_perm(count, 2))
+    ra2, rb2, ya2, na2, fb1, sent, mine_part = hold((ra2, rb2, ya2, na2, fb1, sent, mine_part))
+    normed = [sent[0], None, None, None]
+
+    ra3, yb2, nb2, fa2 = ring(ra2), other_of(rb2), near_of(rb2), near_of(ya2)
+    normed[1] = lax.ppermute(sent[1], "ctx", ring_perm(count, 1))
     one = product(
         tokens, [[ra1, na1, ya1, fa1], [rb1, nb1, yb1, fb1]], weight_own, others, 0, True, None
     )
-    ra3, rb3, ya3, na3, fb2, normed[2], one = hold((ra3, rb3, ya3, na3, fb2, normed[2], one))
+    rb2, ra3, yb2, nb2, fa2, normed[1], one = hold((rb2, ra3, yb2, nb2, fa2, normed[1], one))
+
+    rb3, ya3, na3, fb2 = ring(rb2), other_of(ra3), near_of(ra3), near_of(yb2)
+    normed[3] = lax.ppermute(sent[3], "ctx", ring_perm(count, 3))
+    ra3, rb3, ya3, na3, fb2, normed[3] = hold((ra3, rb3, ya3, na3, fb2, normed[3]))
 
     yb3, nb3, fa3 = other_of(rb3), near_of(rb3), near_of(ya3)
+    normed[2] = lax.ppermute(sent[2], "ctx", ring_perm(count, 2))
     returned = [mine_part, lax.ppermute(one, "ctx", ring_perm(count, -1))]
     two = product(
         tokens, [[ra2, na2, ya2, fa2], [rb2, nb2, yb2, fb2]], weight_own, others, 0, True, None
     )
-    nb3, fa3, two = hold((nb3, fa3, two))
-    returned.append(lax.ppermute(two, "ctx", ring_perm(count, -2)))
     last_lot = [ra3, na3, ya3, fa3]
     three = product(tokens, [last_lot], weight_own, others, 0, False, None)
+    nb3, yb3, three, two, returned, normed[2] = hold((nb3, yb3, three, two, returned, normed[2]))
+
+    fb3 = near_of(yb3)
+    returned.append(lax.ppermute(two, "ctx", ring_perm(count, -2)))
     lots = [[ra1, na1, ya1, fa1], [ra2, na2, ya2, fa2], last_lot]
     early = outer(normed, grad_out, lots, 0, own)
-    yb3, three, early, returned = hold((yb3, three, early, returned))
-
-    fb3 = near_of(yb3)
-    flat = [early[0]]
-    flat += [lax.ppermute(early[s], "ctx", pair_perm(count, s)) for s in range(1, minor)]
+    fb3, three, early = hold((fb3, three, early))
     last_lot = [rb3, nb3, yb3, fb3]
     three = product(tokens, [last_lot], weight_own, others, 1, True, three)
     returned.append(lax.ppermute(three, "ctx", ring_perm(count, -3)))
+    flat = [early[0]]
+    flat += [lax.ppermute(early[s], "ctx", pair_perm(count, s)) for s in range(1, minor)]
     lots = [[rb1, nb1, yb1, fb1], [rb2, nb2, yb2, fb2], last_lot]
     late = outer([after(normed[0], three)] + normed[1:], grad_out, lots, 1, own)
     returned, late = hold((returned, late))
@@ -491,16 +490,22 @@
         back_kernel, [wide_b, jax.ShapeDtypeStruct((1, width), FL), row_f], "back",
         order, attn_out, inv_rms, gain_row, *returned,
     )
-    gain_sum = gain_sum + lax.ppermute(gain_sum, "ctx", [(i, i ^ 1) for i in range(count)])
     inner = inner + near_of(inner)
     inner_there = other_of(inner)
-    inner_there, gain_sum, flat = hold((inner_there, gain_sum, flat))
+    inner_there, gain_sum = hold((inner_there, gain_sum))
     grad_attn, put_back = whole(
         functools.partial(grad_kernel, features), [wide_b, put_shape], "grads",
         grad, attn_out, inv_rms, inner, inner_there, gain_row, query_rows, turned,
     )
     spread = lax.all_to_all(put_back, "ctx", 0, 0, tiled=True)
-    late = hold((put_back, late))[1]
+    gain_sum, late, put_back = hold((gain_sum, late, put_back))
+    for step in (i for i in (1, 2, 4, 8, 16, 32) if i < count):
+        gain_sum = gain_sum + lax.ppermute(
+            gain_sum, "ctx", [(i, i ^ step) for i in range(count)]
+        )
+        if step == 1:
+            gain_sum, late = hold((gain_sum, late))
+    spread, flat = hold((spread, flat))
     flat.append(late[0])
     flat += [lax.ppermute(late[s], "ctx", pair_perm(count, s)) for s in range(1, minor)]
     states = whole(functools.partial(scan_kernel, True), scan_shape, "scan", spread)
@@ -509,12 +514,6 @@
         inside_kernel, [wide_b, wide_f, wide_f], "inside",
         after(grad_attn, states), query_rows, key_rows, value_rows, run, turned, state_low,
     )
-    step = 2
-    while step < count:
-        gain_sum = gain_sum + lax.ppermute(
-            gain_sum, "ctx", [(i, i ^ step) for i in range(count)]
-        )
-        step *= 2
     grad_gain = gain_sum.reshape(width)
     grad_key, grad_value = whole(
         outside_kernel, [wide_b] * 2, "outside",

time: 240 us -> 226 us (0.942)
  waiting for transfers between devices: 104 us -> 91.2 us
  Pallas kernels: 48.1 us -> 53.1 us
  local copies, waits for them, and re-layouts: 21.4 us -> 17.5 us
    ppermute x6, waiting for transfers between devices: 33.5 us -> 13.3 us  [ring(): return lax.ppermute(x, 'ctx', ring_perm(count, 1))]
    ppermute x1, waiting for transfers between devices: 13.7 us -> 0.91 us  [shards(): normed[2] = lax.ppermute(sent[2], 'ctx', ring_perm(count, 2))]
    all_to_all x1, waiting for transfers between devices: 0.04 us -> 11 us  [shards(): spread = lax.all_to_all(put, 'ctx', 0, 0, tiled=True)]
    ppermute x4 -> x3, waiting for transfers between devices: 20.3 us -> 12.3 us  [the longest x1 12.3 us: shards(): normed[1] = lax.ppermute(sent[1], 'ctx', ring_perm(count, 1))]
    ppermute x1, waiting for transfers between devices: 11.9 us -> 17.6 us  [shards(): normed[3] = lax.ppermute(sent[3], 'ctx', ring_perm(count, 3))]
    ppermute x22, waiting for transfers between devices: 4.78 us -> 10.3 us  [over(): return lax.ppermute(x, 'head', perm)]
    ppermute x1, waiting for transfers between devices: 0.01 us -> 5.48 us  [shards(): returned.append(lax.ppermute(three, 'ctx', ring_perm(count, -3)))]
    ppermute x1, starting transfers between devices: 4.77 us -> 0.01 us  [shards(): returned = [mine_part, lax.ppermute(one, 'ctx', ring_perm(count, -1))]]
  transfers between devices with their start and end apart: 45 -> 45, of which waited for: 19 -> 19; matrix products, arithmetic and copies ran while one was open for 3% -> 2% of each run, Pallas kernels for 17% -> 22%
where the time goes in v8:
time: 226 us; the launch traced here: 225 us
  waiting for transfers between devices  91.2 us (40%)
  starting transfers between devices  59.3 us (26%)
  Pallas kernels  53.1 us (23%)
  local copies, waits for them, and re-layouts  17.5 us (8%)
  other arithmetic  2.83 us (1%)
    pallas_call x11, Pallas kernels, whole(): pl.pallas_call(kernel, in_specs=[SCALAR if a is tokens else full for a in...  24.5 us
    ppermute x1, waiting for transfers between devices, shards(): normed[3] = lax.ppermute(sent[3], 'ctx', ring_perm(count, 3))  17.6 us
    pallas_call x5, Pallas kernels, product(): pl.pallas_call(functools.partial(product_kernel, len(lots[0]), [len(w) fo...  16.3 us
    ppermute x6, waiting for transfers between devices, ring(): return lax.ppermute(x, 'ctx', ring_perm(count, 1))  13.3 us
    unnamed x56, local copies, waits for them, and re-layouts  12.5 us
    ppermute x1, waiting for transfers between devices, shards(): normed[1] = lax.ppermute(sent[1], 'ctx', ring_perm(count, 1))  12.3 us
    pallas_call x2, Pallas kernels, outer(): pl.pallas_call(functools.partial(outer_kernel, [1] + [len(lot) for lot in...  12.2 us
    all_to_all x1, waiting for transfers between devices, shards(): spread = lax.all_to_all(put, 'ctx', 0, 0, tiled=True)  11 us
  transfers between devices with their start and end apart: 45, of which 19 were waited for; matrix products, arithmetic and copies ran while one was open for 2% of the time, Pallas kernels for 22%

profile of v8, /device:TPU:0, one launch (start us, length us, event | category | flops | bytes accessed | tf_op | source)
XLA Modules:
  0.0 224.9 jit_solution(16120536928354562500)
XLA Ops:
  0.6 2.6 %fusion.20 = (bf16[128,3072]{1,0:T(8,128)(2,1)}, bf16[128,3072]{1,0:T(8,128)(2,1)}) fusion(bf16[128,6144]{1,0:T(8,128)(2,1)} %bitcast.7), kind=kLoop, calls=%fused_computation.48 | loop fusion | bytes 3145728 | tf_op jit(solution)/shard_map/slice | solution.py:405
  3.2 3.0 %collective-permute-start.1 = (bf16[128,3072]{1,0:T(8,128)(2,1)}, bf16[128,3072]{1,0:T(8,128)(2,1)S(1)}, u32[]{:S(2)}, u32[]{:S(2)}) collective-permute-start(bf16[128,3072]{1,0:T(8,128)(2,1)} %get-tuple-element.202), channel_id=1, source_target_pairs={{0,4},{4,0},{8,12},{12,8},{16,20},{20,16},{24,28},{28,24},{1,5},{5... | collective-permute-start | bytes 2359304 | tf_op jit(solution)/shard_map/ppermute | solution.py:408
  6.2 2.4 %constant_dynamic-slice_fusion = (bf16[96,3072]{1,0:T(8,128)(2,1)}, bf16[96,3072]{1,0:T(8,128)(2,1)}) fusion(bf16[384,6144]{1,0:T(8,128)(2,1)} %refs_4_.3, s32[]{:T(128)S(6)} %select_n.84), kind=kLoop, calls=%fused_computation.46 | loop fusion | bytes 2359300 | tf_op jit(solution)/shard_map/dynamic_slice | solution.py:368
  10.2 1.9 states.1
  12.8 4.1 %all-to-all-start = ((bf16[8,144,128]{2,1,0:T(8,128)(2,1)}), bf16[8,144,128]{2,1,0:T(8,128)(2,1)}, u32[]{:S(2)}, u32[]{:S(2)}) async-start(bf16[8,144,128]{2,1,0:T(8,128)(2,1)} %copy-done.22), calls=%async_computation | async-start | bytes 589824 | tf_op jit(solution)/shard_map/all_to_all | solution.py:418
  16.9 1.9 weights.1.intra_ref
  19.9 11.0 %all-to-all-done.in_ref = bf16[8,144,128]{2,1,0:T(8,128)(2,1)} async-done(((bf16[8,144,128]{2,1,0:T(8,128)(2,1)}), bf16[8,144,128]{2,1,0:T(8,128)(2,1)}, u32[]{:S(2)}, u32[]{:S(2)}) %all-to-all-start) | async-done | bytes 294944 | tf_op jit(solution)/shard_map/all_to_all | solution.py:418
  34.0 1.7 scan.2
  35.8 5.4 %all-to-all-start.1 = ((bf16[8,128,128]{2,1,0:T(8,128)(2,1)}), bf16[8,128,128]{2,1,0:T(8,128)(2,1)}, u32[]{:S(2)}, u32[]{:S(2)}) async-start(bf16[8,128,128]{2,1,0:T(8,128)(2,1)} %scan.2), calls=%async_computation.1 | async-start | bytes 524288 | tf_op jit(solution)/shard_map/all_to_all | solution.py:427
  41.2 2.2 fusion.order_ref
  43.4 2.8 %collective-permute-done.2.refs_5_ = bf16[96,3072]{1,0:T(8,128)(2,1)} collective-permute-done((bf16[96,3072]{1,0:T(8,128)(2,1)}, bf16[96,3072]{1,0:T(8,128)(2,1)}, u32[]{:S(2)}, u32[]{:S(2)}) %collective-permute-start.2) | collective-permute-done | bytes 589856 | tf_op jit(solution)/shard_map/ppermute | solution.py:390
  46.3 5.9 %all-to-all-done.1.state_ref = bf16[8,128,128]{2,1,0:T(8,128)(2,1)} async-done(((bf16[8,128,128]{2,1,0:T(8,128)(2,1)}), bf16[8,128,128]{2,1,0:T(8,128)(2,1)}, u32[]{:S(2)}, u32[]{:S(2)}) %all-to-all-start.1) | async-done | bytes 262176 | tf_op jit(solution)/shard_map/all_to_all | solution.py:427
  57.4 1.7 attend.1
  61.5 8.1 %collective-permute-done.8.refs_1_.refs_9_ = bf16[96,3072]{1,0:T(8,128)(2,1)S(1)} collective-permute-done((bf16[96,3072]{1,0:T(8,128)(2,1)}, bf16[96,3072]{1,0:T(8,128)(2,1)S(1)}, u32[]{:S(2)}, u32[]{:S(2)}) %collective-permute-start.8) | collective-permute-done | bytes 589856 | tf_op jit(solution)/shard_map/ppermute | solution.py:390
  69.7 1.6 collective-permute-start.13
  71.3 2.9 %collective-permute-start.12 = (bf16[96,3072]{1,0:T(8,128)(2,1)}, bf16[96,3072]{1,0:T(8,128)(2,1)S(1)}, u32[]{:S(2)}, u32[]{:S(2)}) collective-permute-start(bf16[96,3072]{1,0:T(8,128)(2,1)} %collective-permute-done.2.refs_5_), channel_id=1, source_target_pairs={{0,8},{4,12},{8,24},{12,28},{24,16},{28,20},{16,0},{20,4},{1,9},{5... | collective-permute-start | bytes 1769480 | tf_op jit(solution)/shard_map/ppermute | solution.py:390
  74.1 2.3 %copy-done = bf16[384,6144]{1,0:T(8,128)(2,1)S(1)} copy-done((bf16[384,6144]{1,0:T(8,128)(2,1)S(1)}, bf16[384,6144]{1,0:T(8,128)(2,1)}, u32[]{:S(2)}) %copy-start) | copy-done | bytes 4718616
  76.5 4.2 %product.5.refs_0_ = bf16[384,256]{1,0:T(8,128)(2,1)S(1)} custom-call(s32[1]{0:T(128)} %bitcast.1.mine_ref.refs_0_, bf16[384,6144]{1,0:T(8,128)(2,1)S(1)} %copy-done, bf16[384,6144]{1,0:T(8,128)(2,1)S(1)} %copy-done, bf16[128,6144]{1,0:T(8,128)(2,1)S(1)} %bitcast.8, bf16[128,3072]{1,0:T(8,128)(2,1)S(1)} %copy-done.9, ...), custom_call_target="tpu_custom_call" | custom-call | flops 1000 | bytes 1000 | tf_op jit(solution)/shard_map/product/pallas_call | solution.py:210
  82.0 3.5 %collective-permute-done.13.refs_3_.refs_11_ = bf16[96,3072]{1,0:T(8,128)(2,1)S(1)} collective-permute-done((bf16[96,3072]{1,0:T(8,128)(2,1)S(1)}, bf16[96,3072]{1,0:T(8,128)(2,1)S(1)}, u32[]{:S(2)}, u32[]{:S(2)}) %collective-permute-start.13) | collective-permute-done | bytes 589856 | tf_op jit(solution)/shard_map/ppermute | solution.py:393
  85.4 2.3 %collective-permute-done.12.refs_5_.refs_9_ = bf16[96,3072]{1,0:T(8,128)(2,1)S(1)} collective-permute-done((bf16[96,3072]{1,0:T(8,128)(2,1)}, bf16[96,3072]{1,0:T(8,128)(2,1)S(1)}, u32[]{:S(2)}, u32[]{:S(2)}) %collective-permute-start.12) | collective-permute-done | bytes 589856 | tf_op jit(solution)/shard_map/ppermute | solution.py:390
  88.3 2.0 collective-permute-start.16
  90.3 1.8 collective-permute-start.20
  92.1 4.4 %product.6 = bf16[384,256]{1,0:T(8,128)(2,1)S(1)} custom-call(s32[1]{0:T(128)} %bitcast.1.mine_ref.refs_0_, bf16[96,3072]{1,0:T(8,128)(2,1)} %collective-permute-done.refs_1_.refs_5_, bf16[96,3072]{1,0:T(8,128)(2,1)} %collective-permute-done.4.refs_2_.refs_6_, bf16[96,3072]{1,0:T(8,128)(2,1)} %collective-permute-done.3.refs_3_.refs_7_, ...), custom_call_target="tpu_custom_call" | custom-call | flops 1000 | bytes 1000 | tf_op jit(solution)/shard_map/product/pallas_call | solution.py:210
  96.5 12.3 %collective-permute-done.20.refs_1_ = bf16[384,256]{1,0:T(8,128)(2,1)S(1)} collective-permute-done((bf16[384,256]{1,0:T(8,128)(2,1)S(1)}, bf16[384,256]{1,0:T(8,128)(2,1)S(1)}, u32[]{:S(2)}, u32[]{:S(2)}) %collective-permute-start.20) | collective-permute-done | bytes 196640 | tf_op jit(solution)/shard_map/ppermute | solution.py:455
  111.7 1.8 collective-permute-start.25
  113.5 17.6 %collective-permute-done.25.refs_3_ = bf16[384,256]{1,0:T(8,128)(2,1)S(1)} collective-permute-done((bf16[384,256]{1,0:T(8,128)(2,1)S(1)}, bf16[384,256]{1,0:T(8,128)(2,1)S(1)}, u32[]{:S(2)}, u32[]{:S(2)}) %collective-permute-start.25) | collective-permute-done | bytes 196640 | tf_op jit(solution)/shard_map/ppermute | solution.py:462
  131.9 3.2 %collective-permute-start.30 = (bf16[384,256]{1,0:T(8,128)(2,1)S(1)}, bf16[384,256]{1,0:T(8,128)(2,1)S(1)}, u32[]{:S(2)}, u32[]{:S(2)}) collective-permute-start(bf16[384,256]{1,0:T(8,128)(2,1)S(1)} %get-tuple-element.151), channel_id=1, source_target_pairs={{0,24},{4,28},{8,16},{12,20},{24,0},{28,4},{16,8},{20,12},{1,25},{... | collective-permute-start | bytes 589832 | tf_op jit(solution)/shard_map/ppermute | solution.py:466
  135.1 4.1 %product.8 = bf16[384,256]{1,0:T(8,128)(2,1)S(1)} custom-call(s32[1]{0:T(128)} %bitcast.1.mine_ref.refs_0_, bf16[96,3072]{1,0:T(8,128)(2,1)S(1)} %collective-permute-done.8.refs_1_.refs_9_, bf16[96,3072]{1,0:T(8,128)(2,1)S(1)} %collective-permute-done.14.refs_2_.refs_10_, bf16[96,3072]{1,0:T(8,128)(2,1)S(1)} %collective-permute-done.13.refs_3_.refs_11_, ...), custom_call_target="tpu_custom_call" | custom-call | flops 1000 | bytes 1000 | tf_op jit(solution)/shard_map/product/pallas_call | solution.py:210
  141.6 3.6 %collective-permute-done.29.refs_1_ = bf16[384,256]{1,0:T(8,128)(2,1)S(1)} collective-permute-done((bf16[384,256]{1,0:T(8,128)(2,1)S(1)}, bf16[384,256]{1,0:T(8,128)(2,1)S(1)}, u32[]{:S(2)}, u32[]{:S(2)}) %collective-permute-start.29) | collective-permute-done | bytes 196640 | tf_op jit(solution)/shard_map/ppermute | solution.py:467
  145.2 1.7 collective-permute-done.27.refs_3_.refs_15_
  146.9 6.6 %outer.2 = (bf16[128,3072]{1,0:T(8,128)(2,1)S(1)}, bf16[128,3072]{1,0:T(8,128)(2,1)}) custom-call(bf16[384,256]{1,0:T(8,128)(2,1)S(1)} %get-tuple-element.166.refs_0_, bf16[384,256]{1,0:T(8,128)(2,1)S(1)} %collective-permute-done.20.refs_1_, bf16[384,256]{1,0:T(8,128)(2,1)S(1)} %collective-permute-done.30.refs_2_, ...), custom_call_target="tpu_custom_call" | custom-call | flops 1000 | bytes 1000 | tf_op jit(solution)/shard_map/outer/pallas_call | solution.py:253
  154.5 3.5 %collective-permute-start.31 = (bf16[384,256]{1,0:T(8,128)(2,1)S(1)}, bf16[384,256]{1,0:T(8,128)(2,1)S(1)}, u32[]{:S(2)}, u32[]{:S(2)}) collective-permute-start(bf16[384,256]{1,0:T(8,128)(2,1)S(1)} %product.8), channel_id=1, source_target_pairs={{0,24},{4,28},{8,16},{12,20},{24,0},{28,4},{16,8},{20,12},{1,25},{... | collective-permute-start | bytes 589832 | tf_op jit(solution)/shard_map/ppermute | solution.py:476
  158.0 2.2 product.9
  160.3 5.7 %outer.3 = (bf16[128,3072]{1,0:T(8,128)(2,1)S(1)}, bf16[128,3072]{1,0:T(8,128)(2,1)S(1)}) custom-call(bf16[384,256]{1,0:T(8,128)(2,1)S(1)} %get-tuple-element.166.refs_0_, bf16[384,256]{1,0:T(8,128)(2,1)S(1)} %collective-permute-done.20.refs_1_, bf16[384,256]{1,0:T(8,128)(2,1)S(1)} %collective-permute-done.30.refs_2_, ...), custom_call_target="tpu_custom_call" | custom-call | flops 1000 | bytes 1000 | tf_op jit(solution)/shard_map/outer/pallas_call | solution.py:253
  166.0 5.5 %collective-permute-done.33.refs_3_ = bf16[384,256]{1,0:T(8,128)(2,1)S(1)} collective-permute-done((bf16[384,256]{1,0:T(8,128)(2,1)S(1)}, bf16[384,256]{1,0:T(8,128)(2,1)S(1)}, u32[]{:S(2)}, u32[]{:S(2)}) %collective-permute-start.33) | collective-permute-done | bytes 196640 | tf_op jit(solution)/shard_map/ppermute | solution.py:482
  174.6 2.9 %collective-permute-done.35.there_ref = f32[1,384]{1,0:T(1,128)S(1)} collective-permute-done((f32[1,384]{1,0:T(1,128)S(1)}, f32[1,384]{1,0:T(1,128)S(1)}, u32[]{:S(2)}, u32[]{:S(2)}) %collective-permute-start.35) | collective-permute-done | bytes 1568 | tf_op jit(solution)/shard_map/ppermute | solution.py:393
  177.5 2.3 %grads.1 = (bf16[384,1024]{1,0:T(8,128)(2,1)S(1)}, bf16[8,144,128]{2,1,0:T(8,128)(2,1)}) custom-call(bf16[384,1024]{1,0:T(8,128)(2,1)S(1)} %get-tuple-element.173.grad_ref, f32[384,1024]{1,0:T(8,128)S(1)} %get-tuple-element.114.attn_ref, f32[1,384]{1,0:T(1,128)S(1)} %get-tuple-element.119.inv_ref, f32[1,384]{1,0:T(1,128)S(1)} %add.141.here_ref, ...), custom_call_target="tpu_custom_call" | custom-call | flops 1000 | bytes 1000 | tf_op jit(solution)/shard_map/grads/pallas_call | solution.py:379
  180.7 3.4 %all-to-all-start.2 = ((bf16[8,144,128]{2,1,0:T(8,128)(2,1)}), bf16[8,144,128]{2,1,0:T(8,128)(2,1)S(1)}, u32[]{:S(2)}, u32[]{:S(2)}) async-start(bf16[8,144,128]{2,1,0:T(8,128)(2,1)} %get-tuple-element.178), calls=%async_computation.2 | async-start | bytes 589824 | tf_op jit(solution)/shard_map/all_to_all | solution.py:500
  184.1 1.9 collective-permute-start.37
  186.0 2.5 %collective-permute-done.37 = f32[1,1024]{1,0:T(1,128)S(1)} collective-permute-done((f32[1,1024]{1,0:T(1,128)S(1)}, f32[1,1024]{1,0:T(1,128)S(1)}, u32[]{:S(2)}, u32[]{:S(2)}) %collective-permute-start.37) | collective-permute-done | bytes 4128 | tf_op jit(solution)/shard_map/ppermute | solution.py:503
  189.6 3.4 %all-to-all-done.2.in_ref = bf16[8,144,128]{2,1,0:T(8,128)(2,1)S(1)} async-done(((bf16[8,144,128]{2,1,0:T(8,128)(2,1)}), bf16[8,144,128]{2,1,0:T(8,128)(2,1)S(1)}, u32[]{:S(2)}, u32[]{:S(2)}) %all-to-all-start.2) | async-done | bytes 294944 | tf_op jit(solution)/shard_map/all_to_all | solution.py:500
  193.8 4.0 %all-to-all-start.3 = ((bf16[8,128,128]{2,1,0:T(8,128)(2,1)}), bf16[8,128,128]{2,1,0:T(8,128)(2,1)}, u32[]{:S(2)}, u32[]{:S(2)}) async-start(bf16[8,128,128]{2,1,0:T(8,128)(2,1)} %scan.3), calls=%async_computation.3 | async-start | bytes 524288 | tf_op jit(solution)/shard_map/all_to_all | solution.py:512
  197.9 1.9 collective-permute-start.39
  199.8 3.3 %collective-permute-done.39 = f32[1,1024]{1,0:T(1,128)S(1)} collective-permute-done((f32[1,1024]{1,0:T(1,128)S(1)}, f32[1,1024]{1,0:T(1,128)S(1)}, u32[]{:S(2)}, u32[]{:S(2)}) %collective-permute-start.39) | collective-permute-done | bytes 4128 | tf_op jit(solution)/shard_map/ppermute | solution.py:503
  203.1 3.1 %collective-permute-start.40 = (f32[1,1024]{1,0:T(1,128)S(1)}, f32[1,1024]{1,0:T(1,128)S(1)}, u32[]{:S(2)}, u32[]{:S(2)}) collective-permute-start(f32[1,1024]{1,0:T(1,128)S(1)} %add.143), channel_id=1, source_target_pairs={{0,16},{4,20},{8,24},{12,28},{16,0},{20,4},{24,8},{28,12},{1,17},{... | collective-permute-start | bytes 12296 | tf_op jit(solution)/shard_map/ppermute | solution.py:503
  209.5 5.6 %inside.1 = (bf16[384,1024]{1,0:T(8,128)(2,1)}, f32[384,1024]{1,0:T(8,128)S(1)}, f32[384,1024]{1,0:T(8,128)S(1)}) custom-call(bf16[384,1024]{1,0:T(8,128)(2,1)S(1)} %copy-done.21, bf16[384,1024]{1,0:T(8,128)(2,1)S(1)} %copy-done.7, bf16[384,1024]{1,0:T(8,128)(2,1)S(1)} %copy-done.3, bf16[384,1024]{1,0:T(8,128)(2,1)S(1)} %copy-done.4, ...), custom_call_target="tpu_custom_call" | custom-call | flops 1000 | bytes 1000 | tf_op jit(solution)/shard_map/inside/pallas_call | solution.py:379
  217.3 3.1 %sum.1 = bf16[128,6144]{1,0:T(8,128)(2,1)} custom-call(bf16[128,3072]{1,0:T(8,128)(2,1)S(1)} %copy-done.17, bf16[128,3072]{1,0:T(8,128)(2,1)} %collective-permute-done.36.refs_1_, bf16[128,3072]{1,0:T(8,128)(2,1)S(1)} %copy-done.19, bf16[128,3072]{1,0:T(8,128)(2,1)} %collective-permute-done.38.refs_3_), custom_call_target="tpu_custom_call" | custom-call | flops 1000 | bytes 1000 | tf_op jit(solution)/shard_map/sum/pallas_call | solution.py:379
  221.9 3.0 %outside.1 = (bf16[384,1024]{1,0:T(8,128)(2,1)}, bf16[384,1024]{1,0:T(8,128)(2,1)}) custom-call(bf16[384,1024]{1,0:T(8,128)(2,1)S(1)} %copy-done.3, bf16[384,1024]{1,0:T(8,128)(2,1)S(1)} %copy-done.4, bf16[8,128,128]{2,1,0:T(8,128)(2,1)} %all-to-all-done.3.state_ref, f32[384,8]{1,0:T(8,128)S(1)} %get-tuple-element.104.turned_ref, ...), custom_call_target="tpu_custom_call" | custom-call | flops 1000 | bytes 1000 | tf_op jit(solution)/shard_map/outside/pallas_call | solution.py:379
  (126 shorter events, 36.0 us)
Async XLA Ops:
  3.2 27.7 %collective-permute-start.1 = (bf16[128,3072]{1,0:T(8,128)(2,1)}, bf16[128,3072]{1,0:T(8,128)(2,1)S(1)}, u32[]{:S(2)}, u32[]{:S(2)}) collective-permute-start(bf16[128,3072]{1,0:T(8,128)(2,1)} %get-tuple-element.202), channel_id=1, source_target_pairs={{0,4},{4,0},{8,12},{12,8},{16,20},{20,16},{24,28},{28,24},{1,5},{5... | collective-permute-start | bytes 2359304 | tf_op jit(solution)/shard_map/ppermute | solution.py:408
  8.6 22.4 %collective-permute-start = (bf16[96,3072]{1,0:T(8,128)(2,1)}, bf16[96,3072]{1,0:T(8,128)(2,1)}, u32[]{:S(2)}, u32[]{:S(2)}) collective-permute-start(bf16[96,3072]{1,0:T(8,128)(2,1)} %get-tuple-element.200), channel_id=1, source_target_pairs={{0,8},{4,12},{8,24},{12,28},{24,16},{28,20},{16,0},{20,4},{1,9},{5... | collective-permute-start | bytes 1769480 | tf_op jit(solution)/shard_map/ppermute | solution.py:390
  12.8 18.2 %all-to-all-start = ((bf16[8,144,128]{2,1,0:T(8,128)(2,1)}), bf16[8,144,128]{2,1,0:T(8,128)(2,1)}, u32[]{:S(2)}, u32[]{:S(2)}) async-start(bf16[8,144,128]{2,1,0:T(8,128)(2,1)} %copy-done.22), calls=%async_computation | async-start | bytes 589824 | tf_op jit(solution)/shard_map/all_to_all | solution.py:418
  31.0 21.2 %collective-permute-start.5 = (bf16[128,3072]{1,0:T(8,128)(2,1)}, bf16[128,3072]{1,0:T(8,128)(2,1)}, u32[]{:S(2)}, u32[]{:S(2)}) collective-permute-start(bf16[128,3072]{1,0:T(8,128)(2,1)} %get-tuple-element.108), channel_id=1, source_target_pairs={{0,4},{4,0},{8,12},{12,8},{16,20},{20,16},{24,28},{28,24},{1,5},{5... | collective-permute-start | bytes 2359304 | tf_op jit(solution)/shard_map/ppermute | solution.py:408
  32.2 14.0 %collective-permute-start.2 = (bf16[96,3072]{1,0:T(8,128)(2,1)}, bf16[96,3072]{1,0:T(8,128)(2,1)}, u32[]{:S(2)}, u32[]{:S(2)}) collective-permute-start(bf16[96,3072]{1,0:T(8,128)(2,1)} %get-tuple-element.106), channel_id=1, source_target_pairs={{0,8},{4,12},{8,24},{12,28},{24,16},{28,20},{16,0},{20,4},{1,9},{5... | collective-permute-start | bytes 1769480 | tf_op jit(solution)/shard_map/ppermute | solution.py:390
  32.5 19.6 %collective-permute-start.4 = (bf16[96,3072]{1,0:T(8,128)(2,1)}, bf16[96,3072]{1,0:T(8,128)(2,1)}, u32[]{:S(2)}, u32[]{:S(2)}) collective-permute-start(bf16[96,3072]{1,0:T(8,128)(2,1)} %collective-permute-done.refs_1_.refs_5_), channel_id=1, source_target_pairs={{0,1},{1,0},{2,3},{3,2},{4,5},{5,4},{6,7},{7,6},{8,9},{9,8},{10,11... | collective-permute-start | bytes 1769480 | tf_op jit(solution)/shard_map/ppermute | solution.py:393
  32.5 19.6 %collective-permute-start.3 = (bf16[96,3072]{1,0:T(8,128)(2,1)}, bf16[96,3072]{1,0:T(8,128)(2,1)}, u32[]{:S(2)}, u32[]{:S(2)}) collective-permute-start(bf16[96,3072]{1,0:T(8,128)(2,1)} %collective-permute-done.refs_1_.refs_5_), channel_id=1, source_target_pairs={{0,2},{1,3},{2,0},{3,1},{4,6},{5,7},{6,4},{7,5},{8,10},{9,11},{10,... | collective-permute-start | bytes 1769480 | tf_op jit(solution)/shard_map/ppermute | solution.py:393
  35.8 16.4 %all-to-all-start.1 = ((bf16[8,128,128]{2,1,0:T(8,128)(2,1)}), bf16[8,128,128]{2,1,0:T(8,128)(2,1)}, u32[]{:S(2)}, u32[]{:S(2)}) async-start(bf16[8,128,128]{2,1,0:T(8,128)(2,1)} %scan.2), calls=%async_computation.1 | async-start | bytes 524288 | tf_op jit(solution)/shard_map/all_to_all | solution.py:427
  43.4 30.7 %copy-start.1 = (bf16[8,16,6144]{2,1,0:T(8,128)(2,1)S(1)}, bf16[8,16,6144]{2,1,0:T(8,128)(2,1)}, u32[]{:S(2)}) copy-start(bf16[8,16,6144]{2,1,0:T(8,128)(2,1)} %param.12) | copy-start | bytes 4718596
  52.2 2.7 %collective-permute-start.6 = (bf16[96,3072]{1,0:T(8,128)(2,1)}, bf16[96,3072]{1,0:T(8,128)(2,1)S(1)}, u32[]{:S(2)}, u32[]{:S(2)}) collective-permute-start(bf16[96,3072]{1,0:T(8,128)(2,1)} %collective-permute-done.3.refs_3_.refs_7_), channel_id=1, source_target_pairs={{0,1},{1,0},{2,3},{3,2},{4,5},{5,4},{6,7},{7,6},{8,9},{9,8},{10,11... | collective-permute-start | bytes 1769480 | tf_op jit(solution)/shard_map/ppermute | solution.py:393
  52.2 17.3 %collective-permute-start.8 = (bf16[96,3072]{1,0:T(8,128)(2,1)}, bf16[96,3072]{1,0:T(8,128)(2,1)S(1)}, u32[]{:S(2)}, u32[]{:S(2)}) collective-permute-start(bf16[96,3072]{1,0:T(8,128)(2,1)} %collective-permute-done.refs_1_.refs_5_), channel_id=1, source_target_pairs={{0,8},{4,12},{8,24},{12,28},{24,16},{28,20},{16,0},{20,4},{1,9},{5... | collective-permute-start | bytes 1769480 | tf_op jit(solution)/shard_map/ppermute | solution.py:390
  53.2 16.4 %collective-permute-start.10 = (bf16[96,3072]{1,0:T(8,128)(2,1)}, bf16[96,3072]{1,0:T(8,128)(2,1)S(1)}, u32[]{:S(2)}, u32[]{:S(2)}) collective-permute-start(bf16[96,3072]{1,0:T(8,128)(2,1)} %collective-permute-done.2.refs_5_), channel_id=1, source_target_pairs={{0,1},{1,0},{2,3},{3,2},{4,5},{5,4},{6,7},{7,6},{8,9},{9,8},{10,11... | collective-permute-start | bytes 1769480 | tf_op jit(solution)/shard_map/ppermute | solution.py:393
  53.3 16.2 %collective-permute-start.9 = (bf16[96,3072]{1,0:T(8,128)(2,1)}, bf16[96,3072]{1,0:T(8,128)(2,1)S(1)}, u32[]{:S(2)}, u32[]{:S(2)}) collective-permute-start(bf16[96,3072]{1,0:T(8,128)(2,1)} %collective-permute-done.2.refs_5_), channel_id=1, source_target_pairs={{0,2},{1,3},{2,0},{3,1},{4,6},{5,7},{6,4},{7,5},{8,10},{9,11},{10,... | collective-permute-start | bytes 1769480 | tf_op jit(solution)/shard_map/ppermute | solution.py:393
  59.2 1.2 collective-permute-start.7
  60.4 9.2 %collective-permute-start.11 = (f32[1,384]{1,0:T(1,128)S(1)}, f32[1,384]{1,0:T(1,128)S(1)}, u32[]{:S(2)}, u32[]{:S(2)}) collective-permute-start(f32[1,384]{1,0:T(1,128)S(1)} %add.140.here_ref), channel_id=1, source_target_pairs={{0,2},{1,3},{2,0},{3,1},{4,6},{5,7},{6,4},{7,5},{8,10},{9,11},{10,... | collective-permute-start | bytes 4616 | tf_op jit(solution)/shard_map/ppermute | solution.py:393
  69.6 12.4 %collective-permute-start.14 = (bf16[96,3072]{1,0:T(8,128)(2,1)S(1)}, bf16[96,3072]{1,0:T(8,128)(2,1)S(1)}, u32[]{:S(2)}, u32[]{:S(2)}) collective-permute-start(bf16[96,3072]{1,0:T(8,128)(2,1)S(1)} %collective-permute-done.8.refs_1_.refs_9_), channel_id=1, source_target_pairs={{0,1},{1,0},{2,3},{3,2},{4,5},{5,4},{6,7},{7,6},{8,9},{9,8},{10,11... | collective-permute-start | bytes 1769480 | tf_op jit(solution)/shard_map/ppermute | solution.py:393
  69.7 15.7 %collective-permute-start.13 = (bf16[96,3072]{1,0:T(8,128)(2,1)S(1)}, bf16[96,3072]{1,0:T(8,128)(2,1)S(1)}, u32[]{:S(2)}, u32[]{:S(2)}) collective-permute-start(bf16[96,3072]{1,0:T(8,128)(2,1)S(1)} %collective-permute-done.8.refs_1_.refs_9_), channel_id=1, source_target_pairs={{0,2},{1,3},{2,0},{3,1},{4,6},{5,7},{6,4},{7,5},{8,10},{9,11},{10,... | collective-permute-start | bytes 1769480 | tf_op jit(solution)/shard_map/ppermute | solution.py:393
  71.3 16.5 %collective-permute-start.12 = (bf16[96,3072]{1,0:T(8,128)(2,1)}, bf16[96,3072]{1,0:T(8,128)(2,1)S(1)}, u32[]{:S(2)}, u32[]{:S(2)}) collective-permute-start(bf16[96,3072]{1,0:T(8,128)(2,1)} %collective-permute-done.2.refs_5_), channel_id=1, source_target_pairs={{0,8},{4,12},{8,24},{12,28},{24,16},{28,20},{16,0},{20,4},{1,9},{5... | collective-permute-start | bytes 1769480 | tf_op jit(solution)/shard_map/ppermute | solution.py:390
  74.1 13.7 %collective-permute-start.15 = (bf16[96,3072]{1,0:T(8,128)(2,1)S(1)}, bf16[96,3072]{1,0:T(8,128)(2,1)S(1)}, u32[]{:S(2)}, u32[]{:S(2)}) collective-permute-start(bf16[96,3072]{1,0:T(8,128)(2,1)S(1)} %collective-permute-done.9.refs_7_), channel_id=1, source_target_pairs={{0,1},{1,0},{2,3},{3,2},{4,5},{5,4},{6,7},{7,6},{8,9},{9,8},{10,11... | collective-permute-start | bytes 1769480 | tf_op jit(solution)/shard_map/ppermute | solution.py:393
  87.8 21.1 %collective-permute-start.18 = (bf16[96,3072]{1,0:T(8,128)(2,1)S(1)}, bf16[96,3072]{1,0:T(8,128)(2,1)S(1)}, u32[]{:S(2)}, u32[]{:S(2)}) collective-permute-start(bf16[96,3072]{1,0:T(8,128)(2,1)S(1)} %collective-permute-done.12.refs_5_.refs_9_), channel_id=1, source_target_pairs={{0,1},{1,0},{2,3},{3,2},{4,5},{5,4},{6,7},{7,6},{8,9},{9,8},{10,11... | collective-permute-start | bytes 1769480 | tf_op jit(solution)/shard_map/ppermute | solution.py:393
  87.8 21.1 %collective-permute-start.17 = (bf16[96,3072]{1,0:T(8,128)(2,1)S(1)}, bf16[96,3072]{1,0:T(8,128)(2,1)S(1)}, u32[]{:S(2)}, u32[]{:S(2)}) collective-permute-start(bf16[96,3072]{1,0:T(8,128)(2,1)S(1)} %collective-permute-done.12.refs_5_.refs_9_), channel_id=1, source_target_pairs={{0,2},{1,3},{2,0},{3,1},{4,6},{5,7},{6,4},{7,5},{8,10},{9,11},{10,... | collective-permute-start | bytes 1769480 | tf_op jit(solution)/shard_map/ppermute | solution.py:393
  88.3 20.6 %collective-permute-start.16 = (bf16[96,3072]{1,0:T(8,128)(2,1)S(1)}, bf16[96,3072]{1,0:T(8,128)(2,1)S(1)}, u32[]{:S(2)}, u32[]{:S(2)}) collective-permute-start(bf16[96,3072]{1,0:T(8,128)(2,1)S(1)} %collective-permute-done.8.refs_1_.refs_9_), channel_id=1, source_target_pairs={{0,8},{4,12},{8,24},{12,28},{24,16},{28,20},{16,0},{20,4},{1,9},{5... | collective-permute-start | bytes 1769480 | tf_op jit(solution)/shard_map/ppermute | solution.py:390
  90.3 18.6 %collective-permute-start.19 = (bf16[96,3072]{1,0:T(8,128)(2,1)S(1)}, bf16[96,3072]{1,0:T(8,128)(2,1)S(1)}, u32[]{:S(2)}, u32[]{:S(2)}) collective-permute-start(bf16[96,3072]{1,0:T(8,128)(2,1)S(1)} %collective-permute-done.13.refs_3_.refs_11_), channel_id=1, source_target_pairs={{0,1},{1,0},{2,3},{3,2},{4,5},{5,4},{6,7},{7,6},{8,9},{9,8},{10,11... | collective-permute-start | bytes 1769480 | tf_op jit(solution)/shard_map/ppermute | solution.py:393
  90.3 18.6 %collective-permute-start.20 = (bf16[384,256]{1,0:T(8,128)(2,1)S(1)}, bf16[384,256]{1,0:T(8,128)(2,1)S(1)}, u32[]{:S(2)}, u32[]{:S(2)}) collective-permute-start(bf16[384,256]{1,0:T(8,128)(2,1)S(1)} %get-tuple-element.132), channel_id=1, source_target_pairs={{0,8},{4,12},{8,24},{12,28},{24,16},{28,20},{16,0},{20,4},{1,9},{5... | collective-permute-start | bytes 589832 | tf_op jit(solution)/shard_map/ppermute | solution.py:455
  92.1 54.8 %slice-start = ((s8[4718592]{0:T(1024)(128)(4,1)}), s8[4194304]{0:T(1024)(128)(4,1)S(1)}, s32[]{:S(2)}) async-start(s8[4718592]{0:T(1024)(128)(4,1)} %bitcast.5), calls=%async_computation.4 | async-start | bytes 8388608
  96.5 50.4 %slice-start.1 = ((s8[4718592]{0:T(1024)(128)(4,1)}), s8[524288]{0:T(1024)(128)(4,1)S(1)}, s32[]{:S(2)}) async-start(s8[4718592]{0:T(1024)(128)(4,1)} %bitcast.5), calls=%async_computation.5 | async-start | bytes 1048576
  108.9 22.2 %collective-permute-start.23 = (bf16[96,3072]{1,0:T(8,128)(2,1)S(1)}, bf16[96,3072]{1,0:T(8,128)(2,1)S(1)}, u32[]{:S(2)}, u32[]{:S(2)}) collective-permute-start(bf16[96,3072]{1,0:T(8,128)(2,1)S(1)} %collective-permute-done.16.refs_1_.refs_13_), channel_id=1, source_target_pairs={{0,1},{1,0},{2,3},{3,2},{4,5},{5,4},{6,7},{7,6},{8,9},{9,8},{10,11... | collective-permute-start | bytes 1769480 | tf_op jit(solution)/shard_map/ppermute | solution.py:393
  109.0 22.1 %collective-permute-start.22 = (bf16[96,3072]{1,0:T(8,128)(2,1)S(1)}, bf16[96,3072]{1,0:T(8,128)(2,1)S(1)}, u32[]{:S(2)}, u32[]{:S(2)}) collective-permute-start(bf16[96,3072]{1,0:T(8,128)(2,1)S(1)} %collective-permute-done.16.refs_1_.refs_13_), channel_id=1, source_target_pairs={{0,2},{1,3},{2,0},{3,1},{4,6},{5,7},{6,4},{7,5},{8,10},{9,11},{10,... | collective-permute-start | bytes 1769480 | tf_op jit(solution)/shard_map/ppermute | solution.py:393
  110.5 20.5 %collective-permute-start.21 = (bf16[96,3072]{1,0:T(8,128)(2,1)S(1)}, bf16[96,3072]{1,0:T(8,128)(2,1)S(1)}, u32[]{:S(2)}, u32[]{:S(2)}) collective-permute-start(bf16[96,3072]{1,0:T(8,128)(2,1)S(1)} %collective-permute-done.12.refs_5_.refs_9_), channel_id=1, source_target_pairs={{0,8},{4,12},{8,24},{12,28},{24,16},{28,20},{16,0},{20,4},{1,9},{5... | collective-permute-start | bytes 1769480 | tf_op jit(solution)/shard_map/ppermute | solution.py:390
  111.7 19.4 %collective-permute-start.24 = (bf16[96,3072]{1,0:T(8,128)(2,1)S(1)}, bf16[96,3072]{1,0:T(8,128)(2,1)S(1)}, u32[]{:S(2)}, u32[]{:S(2)}) collective-permute-start(bf16[96,3072]{1,0:T(8,128)(2,1)S(1)} %collective-permute-done.17.refs_7_.refs_11_), channel_id=1, source_target_pairs={{0,1},{1,0},{2,3},{3,2},{4,5},{5,4},{6,7},{7,6},{8,9},{9,8},{10,11... | collective-permute-start | bytes 1769480 | tf_op jit(solution)/shard_map/ppermute | solution.py:393
  111.7 19.4 %collective-permute-start.25 = (bf16[384,256]{1,0:T(8,128)(2,1)S(1)}, bf16[384,256]{1,0:T(8,128)(2,1)S(1)}, u32[]{:S(2)}, u32[]{:S(2)}) collective-permute-start(bf16[384,256]{1,0:T(8,128)(2,1)S(1)} %get-tuple-element.140), channel_id=1, source_target_pairs={{0,16},{4,20},{8,0},{12,4},{24,8},{28,12},{16,24},{20,28},{1,17},{... | collective-permute-start | bytes 589832 | tf_op jit(solution)/shard_map/ppermute | solution.py:462
  131.1 8.1 %collective-permute-start.28 = (bf16[96,3072]{1,0:T(8,128)(2,1)S(1)}, bf16[96,3072]{1,0:T(8,128)(2,1)S(1)}, u32[]{:S(2)}, u32[]{:S(2)}) collective-permute-start(bf16[96,3072]{1,0:T(8,128)(2,1)S(1)} %collective-permute-done.22.refs_3_.refs_15_), channel_id=1, source_target_pairs={{0,1},{1,0},{2,3},{3,2},{4,5},{5,4},{6,7},{7,6},{8,9},{9,8},{10,11... | collective-permute-start | bytes 1769480 | tf_op jit(solution)/shard_map/ppermute | solution.py:393
  131.2 15.7 %collective-permute-start.27 = (bf16[96,3072]{1,0:T(8,128)(2,1)S(1)}, bf16[96,3072]{1,0:T(8,128)(2,1)S(1)}, u32[]{:S(2)}, u32[]{:S(2)}) collective-permute-start(bf16[96,3072]{1,0:T(8,128)(2,1)S(1)} %collective-permute-done.21.refs_1_.refs_13_), channel_id=1, source_target_pairs={{0,2},{1,3},{2,0},{3,1},{4,6},{5,7},{6,4},{7,5},{8,10},{9,11},{10,... | collective-permute-start | bytes 1769480 | tf_op jit(solution)/shard_map/ppermute | solution.py:393
  131.7 15.2 %collective-permute-start.26 = (bf16[96,3072]{1,0:T(8,128)(2,1)S(1)}, bf16[96,3072]{1,0:T(8,128)(2,1)S(1)}, u32[]{:S(2)}, u32[]{:S(2)}) collective-permute-start(bf16[96,3072]{1,0:T(8,128)(2,1)S(1)} %collective-permute-done.21.refs_1_.refs_13_), channel_id=1, source_target_pairs={{0,1},{1,0},{2,3},{3,2},{4,5},{5,4},{6,7},{7,6},{8,9},{9,8},{10,11... | collective-permute-start | bytes 1769480 | tf_op jit(solution)/shard_map/ppermute | solution.py:393
  131.9 9.7 %collective-permute-start.30 = (bf16[384,256]{1,0:T(8,128)(2,1)S(1)}, bf16[384,256]{1,0:T(8,128)(2,1)S(1)}, u32[]{:S(2)}, u32[]{:S(2)}) collective-permute-start(bf16[384,256]{1,0:T(8,128)(2,1)S(1)} %get-tuple-element.151), channel_id=1, source_target_pairs={{0,24},{4,28},{8,16},{12,20},{24,0},{28,4},{16,8},{20,12},{1,25},{... | collective-permute-start | bytes 589832 | tf_op jit(solution)/shard_map/ppermute | solution.py:466
  135.1 10.1 %collective-permute-start.29 = (bf16[384,256]{1,0:T(8,128)(2,1)S(1)}, bf16[384,256]{1,0:T(8,128)(2,1)S(1)}, u32[]{:S(2)}, u32[]{:S(2)}) collective-permute-start(bf16[384,256]{1,0:T(8,128)(2,1)S(1)} %product.6), channel_id=1, source_target_pairs={{0,16},{4,20},{8,0},{12,4},{24,8},{28,12},{16,24},{20,28},{1,17},{... | collective-permute-start | bytes 589832 | tf_op jit(solution)/shard_map/ppermute | solution.py:467
  146.9 6.6 %collective-permute-start.32 = (bf16[96,3072]{1,0:T(8,128)(2,1)S(1)}, bf16[96,3072]{1,0:T(8,128)(2,1)S(1)}, u32[]{:S(2)}, u32[]{:S(2)}) collective-permute-start(bf16[96,3072]{1,0:T(8,128)(2,1)S(1)} %collective-permute-done.27.refs_3_.refs_15_), channel_id=1, source_target_pairs={{0,1},{1,0},{2,3},{3,2},{4,5},{5,4},{6,7},{7,6},{8,9},{9,8},{10,11... | collective-permute-start | bytes 1769480 | tf_op jit(solution)/shard_map/ppermute | solution.py:393
  153.5 39.5 %collective-permute-start.36 = (bf16[128,3072]{1,0:T(8,128)(2,1)}, bf16[128,3072]{1,0:T(8,128)(2,1)}, u32[]{:S(2)}, u32[]{:S(2)}) collective-permute-start(bf16[128,3072]{1,0:T(8,128)(2,1)} %get-tuple-element.180), channel_id=1, source_target_pairs={{0,4},{4,0},{8,12},{12,8},{16,20},{20,16},{24,28},{28,24},{1,5},{5... | collective-permute-start | bytes 2359304 | tf_op jit(solution)/shard_map/ppermute | solution.py:484
  154.5 11.5 %collective-permute-start.31 = (bf16[384,256]{1,0:T(8,128)(2,1)S(1)}, bf16[384,256]{1,0:T(8,128)(2,1)S(1)}, u32[]{:S(2)}, u32[]{:S(2)}) collective-permute-start(bf16[384,256]{1,0:T(8,128)(2,1)S(1)} %product.8), channel_id=1, source_target_pairs={{0,24},{4,28},{8,16},{12,20},{24,0},{28,4},{16,8},{20,12},{1,25},{... | collective-permute-start | bytes 589832 | tf_op jit(solution)/shard_map/ppermute | solution.py:476
  160.2 11.2 %collective-permute-start.33 = (bf16[384,256]{1,0:T(8,128)(2,1)S(1)}, bf16[384,256]{1,0:T(8,128)(2,1)S(1)}, u32[]{:S(2)}, u32[]{:S(2)}) collective-permute-start(bf16[384,256]{1,0:T(8,128)(2,1)S(1)} %product.9), channel_id=1, source_target_pairs={{0,8},{4,12},{8,24},{12,28},{24,16},{28,20},{16,0},{20,4},{1,9},{5... | collective-permute-start | bytes 589832 | tf_op jit(solution)/shard_map/ppermute | solution.py:482
  172.7 1.2 collective-permute-start.34
  173.9 3.6 %collective-permute-start.35 = (f32[1,384]{1,0:T(1,128)S(1)}, f32[1,384]{1,0:T(1,128)S(1)}, u32[]{:S(2)}, u32[]{:S(2)}) collective-permute-start(f32[1,384]{1,0:T(1,128)S(1)} %add.141.here_ref), channel_id=1, source_target_pairs={{0,2},{1,3},{2,0},{3,1},{4,6},{5,7},{6,4},{7,5},{8,10},{9,11},{10,... | collective-permute-start | bytes 4616 | tf_op jit(solution)/shard_map/ppermute | solution.py:393
  180.7 12.4 %all-to-all-start.2 = ((bf16[8,144,128]{2,1,0:T(8,128)(2,1)}), bf16[8,144,128]{2,1,0:T(8,128)(2,1)S(1)}, u32[]{:S(2)}, u32[]{:S(2)}) async-start(bf16[8,144,128]{2,1,0:T(8,128)(2,1)} %get-tuple-element.178), calls=%async_computation.2 | async-start | bytes 589824 | tf_op jit(solution)/shard_map/all_to_all | solution.py:500
  184.1 4.4 %collective-permute-start.37 = (f32[1,1024]{1,0:T(1,128)S(1)}, f32[1,1024]{1,0:T(1,128)S(1)}, u32[]{:S(2)}, u32[]{:S(2)}) collective-permute-start(f32[1,1024]{1,0:T(1,128)S(1)} %get-tuple-element.193), channel_id=1, source_target_pairs={{0,4},{4,0},{8,12},{12,8},{16,20},{20,16},{24,28},{28,24},{1,5},{5... | collective-permute-start | bytes 12296 | tf_op jit(solution)/shard_map/ppermute | solution.py:503
  188.5 28.8 %collective-permute-start.38 = (bf16[128,3072]{1,0:T(8,128)(2,1)}, bf16[128,3072]{1,0:T(8,128)(2,1)}, u32[]{:S(2)}, u32[]{:S(2)}) collective-permute-start(bf16[128,3072]{1,0:T(8,128)(2,1)} %copy-done.25), channel_id=1, source_target_pairs={{0,4},{4,0},{8,12},{12,8},{16,20},{20,16},{24,28},{28,24},{1,5},{5... | collective-permute-start | bytes 2359304 | tf_op jit(solution)/shard_map/ppermute | solution.py:510
  193.8 26.6 %all-to-all-start.3 = ((bf16[8,128,128]{2,1,0:T(8,128)(2,1)}), bf16[8,128,128]{2,1,0:T(8,128)(2,1)}, u32[]{:S(2)}, u32[]{:S(2)}) async-start(bf16[8,128,128]{2,1,0:T(8,128)(2,1)} %scan.3), calls=%async_computation.3 | async-start | bytes 524288 | tf_op jit(solution)/shard_map/all_to_all | solution.py:512
  197.9 5.2 %collective-permute-start.39 = (f32[1,1024]{1,0:T(1,128)S(1)}, f32[1,1024]{1,0:T(1,128)S(1)}, u32[]{:S(2)}, u32[]{:S(2)}) collective-permute-start(f32[1,1024]{1,0:T(1,128)S(1)} %add.142), channel_id=1, source_target_pairs={{0,8},{4,12},{8,0},{12,4},{16,24},{20,28},{24,16},{28,20},{1,9},{5... | collective-permute-start | bytes 12296 | tf_op jit(solution)/shard_map/ppermute | solution.py:503
  203.1 4.6 %collective-permute-start.40 = (f32[1,1024]{1,0:T(1,128)S(1)}, f32[1,1024]{1,0:T(1,128)S(1)}, u32[]{:S(2)}, u32[]{:S(2)}) collective-permute-start(f32[1,1024]{1,0:T(1,128)S(1)} %add.143), channel_id=1, source_target_pairs={{0,16},{4,20},{8,24},{12,28},{16,0},{20,4},{24,8},{28,12},{1,17},{... | collective-permute-start | bytes 12296 | tf_op jit(solution)/shard_map/ppermute | solution.py:503
  (25 other events, 121.9 us)

commit v9 on v8

--- a/solution.py
+++ b/solution.py
@@ -9,6 +9,7 @@
 
 LINE = 4
 CHUNKS = 2
+PARTS = 3
 QUARTERS = 4
 FL = jnp.float32
 BF = jnp.bfloat16
@@ -154,27 +155,26 @@
             ref[pl.ds(to, quarter), :] = part[j * quarter : (j + 1) * quarter]
 
 
-def product_kernel(lots, others, add, last, whole, *refs):
+def product_kernel(lots, steps, first, others, add, last, whole, *refs):
     refs = list(refs)
     mine_ref = refs.pop(0)
-    x = [[refs.pop(0) for _ in range(lots)] for _ in others]
+    x = [[refs.pop(0) for _ in range(k)] for k in lots]
     own_ref = refs.pop(0)
     w = [[refs.pop(0) for _ in range(k)] for k in others]
     extra = refs.pop(0) if add else None
     out_ref, held_ref = refs
     step = pl.program_id(0)
-    steps = pl.num_programs(0) // len(others)
 
     @pl.when(step == 0)
     def _():
         held_ref[...] = extra[...] if add else jnp.zeros_like(held_ref)
 
-    for at, lot in enumerate(x):
-
-        @pl.when(step // steps == at)
+    for i in range(steps * len(lots)):
+
+        @pl.when(step == i)
         def _():
-            rows = jnp.concatenate([r[...] for r in lot], axis=0)
-            cols = jnp.concatenate([own_ref[...]] + [r[...] for r in w[at]], axis=0)
+            rows = jnp.concatenate([r[...] for r in x[i // steps]], axis=0)
+            cols = jnp.concatenate([own_ref[...]] + [r[...] for r in w[(first + i) // 2]], axis=0)
             held_ref[...] += dot(rows, cols, NT)
 
     @pl.when(step == pl.num_programs(0) - 1)
@@ -195,27 +195,34 @@
 def product(mine, lots, weight, others, chunk, last, held, whole=False):
     tok = sum(p.shape[0] for p in lots[0])
     deep = weight.shape[1] // CHUNKS
-    tile = 1536
+    tile = weight.shape[1] // PARTS // 2
     steps = deep // tile
-    others = others[chunk : chunk + len(lots)]
+    start = chunk * steps
+    low = start // 2
+    others = others[low : (start + steps * len(lots) - 1) // 2 + 1]
+    first = start - 2 * low
     span = weight.shape[0] + sum(w.shape[0] for w in others[0])
-    base = chunk * steps
     more = [] if held is None else [held]
 
-    def part(at, p, offset=0):
+    def lot_spec(at, p):
+        offset = at * steps if whole else 0
         return spec(
             (p.shape[0], tile), lambda i: (0, offset + jnp.clip(i - at * steps, 0, steps - 1))
         )
 
+    def part_spec(at, w):
+        return spec((w.shape[0], tile), lambda i: (0, jnp.clip(first + i - 2 * at, 0, 1)))
+
     return pl.pallas_call(
         functools.partial(
-            product_kernel, len(lots[0]), [len(w) for w in others], len(more), last, whole
+            product_kernel, [len(x) for x in lots], steps, first, [len(w) for w in others],
+            len(more), last, whole,
         ),
         grid=(steps * len(lots),),
         in_specs=[SCALAR]
-        + [part(at, p, at * steps if whole else 0) for at, lot in enumerate(lots) for p in lot]
-        + [spec((weight.shape[0], tile), lambda i: (0, base + i))]
-        + [part(at, w) for at, ws in enumerate(others) for w in ws]
+        + [lot_spec(at, p) for at, lot in enumerate(lots) for p in lot]
+        + [spec((weight.shape[0], tile), lambda i: (0, start + i))]
+        + [part_spec(at, w) for at, ws in enumerate(others) for w in ws]
         + [spec((tok, span)) for _ in more],
         out_specs=spec((tok, span)),
         out_shape=jax.ShapeDtypeStruct((tok, span), BF if last else FL),
@@ -313,8 +320,8 @@
         weights = (dot(query, key, NT) * mask).astype(BF)
         gq = dot(masked, key, NN) + dot(grad, state_ref[head], NT) * jnp.exp(run)
         gq_ref[:, at] = gq.astype(BF)
-        gk_ref[:, at] = dot(masked, query, TN)
-        gv_ref[:, at] = dot(weights, grad, TN)
+        gk_ref[:, at] = dot(masked, query, TN).astype(BF)
+        gv_ref[:, at] = dot(weights, grad, TN).astype(BF)
 
 
 def outside_kernel(k_ref, v_ref, state_ref, turned_ref, gk_in, gv_in, gk_ref, gv_ref):
@@ -402,13 +409,7 @@
     scan_shape = jax.ShapeDtypeStruct((count, rows, size), BF)
 
     firsts = [first_piece(grad_out, c) for c in range(CHUNKS)]
-    halves = [weight_own[:, c * deep : (c + 1) * deep] for c in range(CHUNKS)]
-
-    def swap(half):
-        return [lax.ppermute(half, "ctx", pair_perm(count, -s)) for s in range(1, minor)]
-
     ra1 = ring(firsts[0])
-    others = [swap(halves[0])]
     put, run, turned = whole(
         state_kernel,
         [put_shape, jax.ShapeDtypeStruct((heads, tok), FL), jax.ShapeDtypeStruct((tok, heads), FL)],
@@ -419,64 +420,79 @@
     intra = whole(
         weights_kernel, wide_f, "weights", query_rows, key_rows, value_rows, run, turned
     )
-    ra1, spread, intra, others[0], halves[1] = hold((ra1, spread, intra, others[0], halves[1]))
-
-    ya1, na1 = other_of(ra1), near_of(ra1)
-    others.append(swap(halves[1]))
+    ra1, spread, intra = hold((ra1, spread, intra))
+
+    ya1 = other_of(ra1)
     states = whole(functools.partial(scan_kernel, False), scan_shape, "scan", spread)
     state_low = lax.all_to_all(states, "ctx", 0, 0, tiled=True)
     order = feature_order(heads, size, count)
-    ra1, rb1, ya1, na1, state_low, order, others[1] = hold(
-        (ra1, rb1, ya1, na1, state_low, order, others[1])
-    )
-
-    ra2, yb1, nb1, fa1 = ring(ra1), other_of(rb1), near_of(rb1), near_of(ya1)
-    fa1, state_low = hold((fa1, state_low))
+    ra1, rb1, ya1, state_low, order, weight_own = hold(
+        (ra1, rb1, ya1, state_low, order, weight_own)
+    )
+    third = model // PARTS
+    thirds = [weight_own[:, c * third : (c + 1) * third] for c in range(PARTS)]
+
+    def swap(part):
+        return [lax.ppermute(part, "ctx", pair_perm(count, -s)) for s in range(1, minor)]
+
+    ra2, yb1, na1, fa1 = ring(ra1), other_of(rb1), near_of(ra1), near_of(ya1)
+    others = [swap(thirds[0])]
+    fa1, na1, state_low = hold((fa1, na1, state_low))
     state_low = state_low.reshape(heads, size, size)
     attn_out, squares = whole(
         attend_kernel, [wide_f, row_f], "attend", query_rows, state_low, turned, intra
     )
     squares = squares + near_of(squares)
     squares_there = other_of(squares)
-    ra2, rb1, yb1, nb1, squares_there = hold((ra2, rb1, yb1, nb1, squares_there))
-
-    rb2, ya2, na2, fb1 = ring(rb1), other_of(ra2), near_of(ra2), near_of(yb1)
+    ra2, rb1, yb1, squares_there, others[0], thirds = hold(
+        (ra2, rb1, yb1, squares_there, others[0], thirds)
+    )
+
+    rb2, ya2, nb1, fb1 = ring(rb1), other_of(ra2), near_of(rb1), near_of(yb1)
+    others.append(swap(thirds[1]))
     inv_rms, *sent = whole(
         functools.partial(norm_kernel, features), [row_f] + [part_b] * LINE, "norm",
         tokens, attn_out, squares, squares_there, gain_row, order,
     )
+    ra2, rb2, ya2, nb1, fb1, sent, others[1], thirds = hold(
+        (ra2, rb2, ya2, nb1, fb1, sent, others[1], thirds)
+    )
+    normed = [sent[0], None, None, None]
+
+    ra3, yb2, na2, fa2 = ring(ra2), other_of(rb2), near_of(ra2), near_of(ya2)
+    others.append(swap(thirds[2]))
+    normed[1] = lax.ppermute(sent[1], "ctx", ring_perm(count, 1))
+    rb2, ra3, yb2, na2, fa2, normed[1], others[2] = hold(
+        (rb2, ra3, yb2, na2, fa2, normed[1], others[2])
+    )
+
+    rb3, ya3, nb2, fb2 = ring(rb2), other_of(ra3), near_of(rb2), near_of(yb2)
+    normed[3] = lax.ppermute(sent[3], "ctx", ring_perm(count, 3))
     mine_part = product(
         tokens, [[grad_out]] * CHUNKS, weight_own, others, 0, True, None, whole=True
     )
-    ra2, rb2, ya2, na2, fb1, sent, mine_part = hold((ra2, rb2, ya2, na2, fb1, sent, mine_part))
-    normed = [sent[0], None, None, None]
-
-    ra3, yb2, nb2, fa2 = ring(ra2), other_of(rb2), near_of(rb2), near_of(ya2)
-    normed[1] = lax.ppermute(sent[1], "ctx", ring_perm(count, 1))
     one = product(
         tokens, [[ra1, na1, ya1, fa1], [rb1, nb1, yb1, fb1]], weight_own, others, 0, True, None
     )
-    rb2, ra3, yb2, nb2, fa2, normed[1], one = hold((rb2, ra3, yb2, nb2, fa2, normed[1], one))
-
-    rb3, ya3, na3, fb2 = ring(rb2), other_of(ra3), near_of(ra3), near_of(yb2)
-    normed[3] = lax.ppermute(sent[3], "ctx", ring_perm(count, 3))
-    ra3, rb3, ya3, na3, fb2, normed[3] = hold((ra3, rb3, ya3, na3, fb2, normed[3]))
-
-    yb3, nb3, fa3 = other_of(rb3), near_of(rb3), near_of(ya3)
+    ra3, rb3, ya3, nb2, fb2, normed[3], mine_part, one = hold(
+        (ra3, rb3, ya3, nb2, fb2, normed[3], mine_part, one)
+    )
+
+    yb3, na3, fa3 = other_of(rb3), near_of(ra3), near_of(ya3)
     normed[2] = lax.ppermute(sent[2], "ctx", ring_perm(count, 2))
     returned = [mine_part, lax.ppermute(one, "ctx", ring_perm(count, -1))]
     two = product(
         tokens, [[ra2, na2, ya2, fa2], [rb2, nb2, yb2, fb2]], weight_own, others, 0, True, None
     )
+    returned.append(lax.ppermute(two, "ctx", ring_perm(count, -2)))
     last_lot = [ra3, na3, ya3, fa3]
     three = product(tokens, [last_lot], weight_own, others, 0, False, None)
-    nb3, yb3, three, two, returned, normed[2] = hold((nb3, yb3, three, two, returned, normed[2]))
-
-    fb3 = near_of(yb3)
-    returned.append(lax.ppermute(two, "ctx", ring_perm(count, -2)))
+    yb3, three, normed[2], returned[1] = hold((yb3, three, normed[2], returned[1]))
+
+    fb3, nb3 = near_of(yb3), near_of(rb3)
     lots = [[ra1, na1, ya1, fa1], [ra2, na2, ya2, fa2], last_lot]
     early = outer(normed, grad_out, lots, 0, own)
-    fb3, three, early = hold((fb3, three, early))
+    fb3, nb3, three, early, returned = hold((fb3, nb3, three, early, returned))
     last_lot = [rb3, nb3, yb3, fb3]
     three = product(tokens, [last_lot], weight_own, others, 1, True, three)
     returned.append(lax.ppermute(three, "ctx", ring_perm(count, -3)))
@@ -498,22 +514,24 @@
         grad, attn_out, inv_rms, inner, inner_there, gain_row, query_rows, turned,
     )
     spread = lax.all_to_all(put_back, "ctx", 0, 0, tiled=True)
-    gain_sum, late, put_back = hold((gain_sum, late, put_back))
-    for step in (i for i in (1, 2, 4, 8, 16, 32) if i < count):
-        gain_sum = gain_sum + lax.ppermute(
-            gain_sum, "ctx", [(i, i ^ step) for i in range(count)]
-        )
-        if step == 1:
-            gain_sum, late = hold((gain_sum, late))
-    spread, flat = hold((spread, flat))
+    gain_sum, late, grad_attn = hold((gain_sum, late, grad_attn))
+    flips = [1 << i for i in range(count.bit_length() - 1)]
+    gain_sum = gain_sum + lax.ppermute(gain_sum, "ctx", [(i, i ^ 1) for i in range(count)])
+    grad_query, gk_in, gv_in = whole(
+        inside_kernel, [wide_b] * 3, "inside",
+        grad_attn, query_rows, key_rows, value_rows, run, turned, state_low,
+    )
+    spread, flat, gk_in, gv_in, gain_sum, late = hold(
+        (spread, flat, gk_in, gv_in, gain_sum, late)
+    )
     flat.append(late[0])
     flat += [lax.ppermute(late[s], "ctx", pair_perm(count, s)) for s in range(1, minor)]
     states = whole(functools.partial(scan_kernel, True), scan_shape, "scan", spread)
     back_low = lax.all_to_all(states, "ctx", 0, 0, tiled=True).reshape(heads, size, size)
-    grad_query, gk_in, gv_in = whole(
-        inside_kernel, [wide_b, wide_f, wide_f], "inside",
-        after(grad_attn, states), query_rows, key_rows, value_rows, run, turned, state_low,
-    )
+    for step in flips[1:]:
+        gain_sum = gain_sum + lax.ppermute(
+            gain_sum, "ctx", [(i, i ^ step) for i in range(count)]
+        )
     grad_gain = gain_sum.reshape(width)
     grad_key, grad_value = whole(
         outside_kernel, [wide_b] * 2, "outside",

time: 226 us -> 213 us (0.942)
  waiting for transfers between devices: 91.2 us -> 81.4 us
  starting transfers between devices: 59.3 us -> 65.3 us
  Pallas kernels: 53.1 us -> 47.6 us
  local copies, waits for them, and re-layouts: 17.5 us -> 14.2 us
    ppermute x2 -> x4, waiting for transfers between devices: 0.01 us -> 27.9 us  [the longest x3 27.9 us: swap(): lax.ppermute(part, 'ctx', pair_perm(count, -s))]
    ppermute x1, waiting for transfers between devices: 17.6 us -> 4.93 us  [shards(): normed[3] = lax.ppermute(sent[3], 'ctx', ring_perm(count, 3))]
    ppermute x6, waiting for transfers between devices: 13.3 us -> 4.7 us  [ring(): return lax.ppermute(x, 'ctx', ring_perm(count, 1))]
    ppermute x1, waiting for transfers between devices: 12.3 us -> 5.85 us  [shards(): normed[1] = lax.ppermute(sent[1], 'ctx', ring_perm(count, 1))]
    ppermute x1, waiting for transfers between devices: 0.91 us -> 6.7 us  [shards(): normed[2] = lax.ppermute(sent[2], 'ctx', ring_perm(count, 2))]
    ppermute x1, waiting for transfers between devices: 5.48 us -> 0.01 us  [shards(): returned.append(lax.ppermute(three, 'ctx', ring_perm(count, -3)))]
    pallas_call x11, Pallas kernels: 24.5 us -> 19.3 us  [whole(): pl.pallas_call(kernel, in_specs=[SCALAR if a is tokens else full for a in...]
    all_to_all x1, waiting for transfers between devices: 0.01 us -> 3.63 us  [shards(): lax.all_to_all(states, 'ctx', 0, 0, tiled=True).reshape(heads, size, size)]
  transfers between devices with their start and end apart: 45 -> 46, of which waited for: 19 -> 21; matrix products, arithmetic and copies ran while one was open for 2% -> 1% of each run, Pallas kernels for 22% -> 21%
where the time goes in v9:
time: 213 us; the launch traced here: 212 us
  waiting for transfers between devices  81.4 us (38%)
  starting transfers between devices  65.3 us (31%)
  Pallas kernels  47.6 us (22%)
  local copies, waits for them, and re-layouts  14.2 us (7%)
  other arithmetic  2.83 us (1%)
    ppermute x3, waiting for transfers between devices, swap(): lax.ppermute(part, 'ctx', pair_perm(count, -s))  27.9 us
    pallas_call x11, Pallas kernels, whole(): pl.pallas_call(kernel, in_specs=[SCALAR if a is tokens else full for a in...  19.3 us
    pallas_call x5, Pallas kernels, product(): pl.pallas_call(functools.partial(product_kernel, [len(x) for x in lots],...  16.2 us
    ppermute x22, starting transfers between devices, over(): return lax.ppermute(x, 'head', perm)  12.6 us
    pallas_call x2, Pallas kernels, outer(): pl.pallas_call(functools.partial(outer_kernel, [1] + [len(lot) for lot in...  12 us
    unnamed x56, local copies, waits for them, and re-layouts  11.7 us
    ppermute x6, starting transfers between devices, ring(): return lax.ppermute(x, 'ctx', ring_perm(count, 1))  9.41 us
    all_to_all x1, waiting for transfers between devices, shards(): spread = lax.all_to_all(put, 'ctx', 0, 0, tiled=True)  9.31 us
  transfers between devices with their start and end apart: 46, of which 21 were waited for; matrix products, arithmetic and copies ran while one was open for 1% of the time, Pallas kernels for 21%

profile of v9, /device:TPU:0, one launch (start us, length us, event | category | flops | bytes accessed | tf_op | source)
XLA Modules:
  0.0 212.3 jit_solution(17629367730335788937)
XLA Ops:
  0.7 2.5 %constant_dynamic-slice_fusion = (bf16[96,3072]{1,0:T(8,128)(2,1)}, bf16[96,3072]{1,0:T(8,128)(2,1)}) fusion(bf16[384,6144]{1,0:T(8,128)(2,1)} %refs_4_.3, s32[]{:T(128)S(6)} %select_n.84), kind=kLoop, calls=%fused_computation.46 | loop fusion | bytes 2359300 | tf_op jit(solution)/shard_map/dynamic_slice | solution.py:375
  3.2 3.0 %collective-permute-start = (bf16[96,3072]{1,0:T(8,128)(2,1)}, bf16[96,3072]{1,0:T(8,128)(2,1)}, u32[]{:S(2)}, u32[]{:S(2)}) collective-permute-start(bf16[96,3072]{1,0:T(8,128)(2,1)} %get-tuple-element.212), channel_id=1, source_target_pairs={{0,8},{4,12},{8,24},{12,28},{24,16},{28,20},{16,0},{20,4},{1,9},{5... | collective-permute-start | bytes 1769480 | tf_op jit(solution)/shard_map/ppermute | solution.py:397
  6.2 2.6 %states.1 = (bf16[8,144,128]{2,1,0:T(8,128)(2,1)}, f32[8,384]{1,0:T(8,128)S(1)}, f32[384,8]{1,0:T(8,128)S(1)}) custom-call(f32[8,384]{1,0:T(8,128)S(1)} %copy-done.24, bf16[384,1024]{1,0:T(8,128)(2,1)S(1)} %copy-done.3, bf16[384,1024]{1,0:T(8,128)(2,1)S(1)} %copy-done.4), custom_call_target="tpu_custom_call" | custom-call | flops 1000 | bytes 1000 | tf_op jit(solution)/shard_map/states/pallas_call | solution.py:386
  8.8 4.8 %all-to-all-start = ((bf16[8,144,128]{2,1,0:T(8,128)(2,1)}), bf16[8,144,128]{2,1,0:T(8,128)(2,1)S(1)}, u32[]{:S(2)}, u32[]{:S(2)}) async-start(bf16[8,144,128]{2,1,0:T(8,128)(2,1)} %get-tuple-element.108), calls=%async_computation | async-start | bytes 589824 | tf_op jit(solution)/shard_map/all_to_all | solution.py:419
  13.6 2.0 collective-permute-start.1
  15.6 1.9 weights.1.intra_ref
  18.6 9.3 %all-to-all-done.in_ref = bf16[8,144,128]{2,1,0:T(8,128)(2,1)S(1)} async-done(((bf16[8,144,128]{2,1,0:T(8,128)(2,1)}), bf16[8,144,128]{2,1,0:T(8,128)(2,1)S(1)}, u32[]{:S(2)}, u32[]{:S(2)}) %all-to-all-start) | async-done | bytes 294944 | tf_op jit(solution)/shard_map/all_to_all | solution.py:419
  27.9 1.9 collective-permute-start.2
  30.6 5.8 %all-to-all-start.1 = ((bf16[8,128,128]{2,1,0:T(8,128)(2,1)}), bf16[8,128,128]{2,1,0:T(8,128)(2,1)S(1)}, u32[]{:S(2)}, u32[]{:S(2)}) async-start(bf16[8,128,128]{2,1,0:T(8,128)(2,1)} %copy-done.11), calls=%async_computation.1 | async-start | bytes 524288 | tf_op jit(solution)/shard_map/all_to_all | solution.py:427
  36.4 2.2 %fusion.order_ref = bf16[1024,1024]{1,0:T(8,128)(2,1)} fusion(s32[1024]{0:T(1024)S(1)} %fusion.4), kind=kLoop, calls=%fused_computation.1 | loop fusion | flops 2097152 | bytes 2101248 | tf_op jit(solution)/shard_map/convert_element_type | solution.py:349
  38.6 3.5 %collective-permute-done.1.refs_5_ = bf16[96,3072]{1,0:T(8,128)(2,1)} collective-permute-done((bf16[96,3072]{1,0:T(8,128)(2,1)}, bf16[96,3072]{1,0:T(8,128)(2,1)}, u32[]{:S(2)}, u32[]{:S(2)}) %collective-permute-start.1) | collective-permute-done | bytes 589856 | tf_op jit(solution)/shard_map/ppermute | solution.py:397
  42.1 3.3 %all-to-all-done.1.state_ref = bf16[8,128,128]{2,1,0:T(8,128)(2,1)S(1)} async-done(((bf16[8,128,128]{2,1,0:T(8,128)(2,1)}), bf16[8,128,128]{2,1,0:T(8,128)(2,1)S(1)}, u32[]{:S(2)}, u32[]{:S(2)}) %all-to-all-start.1) | async-done | bytes 262176 | tf_op jit(solution)/shard_map/all_to_all | solution.py:427
  46.8 1.5 collective-permute-start.7
  53.8 8.7 %collective-permute-done.9.refs_4_.refs_10_.refs_6_ = bf16[128,2048]{1,0:T(8,128)(2,1)S(1)} collective-permute-done((bf16[128,2048]{1,0:T(8,128)(2,1)S(1)}, bf16[128,2048]{1,0:T(8,128)(2,1)S(1)}, u32[]{:S(2)}, u32[]{:S(2)}) %collective-permute-start.9) | collective-permute-done | bytes 524320 | tf_op jit(solution)/shard_map/ppermute | solution.py:436
  63.0 2.7 %collective-permute-start.10 = (bf16[96,3072]{1,0:T(8,128)(2,1)}, bf16[96,3072]{1,0:T(8,128)(2,1)S(1)}, u32[]{:S(2)}, u32[]{:S(2)}) collective-permute-start(bf16[96,3072]{1,0:T(8,128)(2,1)} %collective-permute-done.1.refs_5_), channel_id=1, source_target_pairs={{0,8},{4,12},{8,24},{12,28},{24,16},{28,20},{16,0},{20,4},{1,9},{5... | collective-permute-start | bytes 1769480 | tf_op jit(solution)/shard_map/ppermute | solution.py:397
  65.7 1.5 collective-permute-start.11
  69.0 1.6 copy-done.1
  71.8 9.7 %collective-permute-done.14.refs_5_.refs_11_.refs_7_.refs_6_ = bf16[128,2048]{1,0:T(8,128)(2,1)S(1)} collective-permute-done((bf16[128,2048]{1,0:T(8,128)(2,1)S(1)}, bf16[128,2048]{1,0:T(8,128)(2,1)S(1)}, u32[]{:S(2)}, u32[]{:S(2)}) %collective-permute-start.14) | collective-permute-done | bytes 524320 | tf_op jit(solution)/shard_map/ppermute | solution.py:436
  84.5 5.9 %collective-permute-done.19.refs_1_ = bf16[384,256]{1,0:T(8,128)(2,1)S(1)} collective-permute-done((bf16[384,256]{1,0:T(8,128)(2,1)S(1)}, bf16[384,256]{1,0:T(8,128)(2,1)S(1)}, u32[]{:S(2)}, u32[]{:S(2)}) %collective-permute-start.19) | collective-permute-done | bytes 196640 | tf_op jit(solution)/shard_map/ppermute | solution.py:464
  91.9 9.5 %collective-permute-done.20.refs_6_.refs_12_.refs_7_ = bf16[128,2048]{1,0:T(8,128)(2,1)S(1)} collective-permute-done((bf16[128,2048]{1,0:T(8,128)(2,1)S(1)}, bf16[128,2048]{1,0:T(8,128)(2,1)S(1)}, u32[]{:S(2)}, u32[]{:S(2)}) %collective-permute-start.20) | collective-permute-done | bytes 524320 | tf_op jit(solution)/shard_map/ppermute | solution.py:436
  103.6 2.7 %collective-permute-start.25 = (bf16[384,256]{1,0:T(8,128)(2,1)S(1)}, bf16[384,256]{1,0:T(8,128)(2,1)S(1)}, u32[]{:S(2)}, u32[]{:S(2)}) collective-permute-start(bf16[384,256]{1,0:T(8,128)(2,1)S(1)} %get-tuple-element.143), channel_id=1, source_target_pairs={{0,16},{4,20},{8,0},{12,4},{24,8},{28,12},{16,24},{20,28},{1,17},{... | collective-permute-start | bytes 589832 | tf_op jit(solution)/shard_map/ppermute | solution.py:470
  106.3 3.7 %product.5.refs_0_ = bf16[384,256]{1,0:T(8,128)(2,1)S(1)} custom-call(s32[1]{0:T(128)} %bitcast.1.mine_ref.refs_0_, bf16[384,6144]{1,0:T(8,128)(2,1)S(1)} %bitcast.6, bf16[384,6144]{1,0:T(8,128)(2,1)S(1)} %bitcast.6, bf16[128,6144]{1,0:T(8,128)(2,1)S(1)} %bitcast.8, bf16[128,2048]{1,0:T(8,128)(2,1)S(1)} %collective-permute-done.9.refs_4_.refs_10_.refs_6_, ...), custom_call_target="tpu_custom_call" | custom-call | flops 1000 | bytes 1000 | tf_op jit(solution)/shard_map/product/pallas_call | solution.py:216
  110.0 5.2 %product.6 = bf16[384,256]{1,0:T(8,128)(2,1)S(1)} custom-call(s32[1]{0:T(128)} %bitcast.1.mine_ref.refs_0_, bf16[96,3072]{1,0:T(8,128)(2,1)} %collective-permute-done.refs_1_.refs_5_, bf16[96,3072]{1,0:T(8,128)(2,1)S(1)} %collective-permute-done.4.refs_2_.refs_6_, bf16[96,3072]{1,0:T(8,128)(2,1)} %collective-permute-done.2.refs_3_.refs_7_, ...), custom_call_target="tpu_custom_call" | custom-call | flops 1000 | bytes 1000 | tf_op jit(solution)/shard_map/product/pallas_call | solution.py:216
  115.2 4.9 %collective-permute-done.25.refs_3_ = bf16[384,256]{1,0:T(8,128)(2,1)S(1)} collective-permute-done((bf16[384,256]{1,0:T(8,128)(2,1)S(1)}, bf16[384,256]{1,0:T(8,128)(2,1)S(1)}, u32[]{:S(2)}, u32[]{:S(2)}) %collective-permute-start.25) | collective-permute-done | bytes 196640 | tf_op jit(solution)/shard_map/ppermute | solution.py:470
  121.2 1.7 collective-permute-start.26
  124.2 1.7 product.7.refs_8_
  125.9 6.7 %collective-permute-done.29.refs_2_ = bf16[384,256]{1,0:T(8,128)(2,1)S(1)} collective-permute-done((bf16[384,256]{1,0:T(8,128)(2,1)S(1)}, bf16[384,256]{1,0:T(8,128)(2,1)S(1)}, u32[]{:S(2)}, u32[]{:S(2)}) %collective-permute-start.29) | collective-permute-done | bytes 196640 | tf_op jit(solution)/shard_map/ppermute | solution.py:482
  132.6 1.8 collective-permute-done.30.refs_1_
  134.4 2.1 collective-permute-done.26.refs_3_.refs_15_
  136.5 3.9 %product.8 = bf16[384,256]{1,0:T(8,128)(2,1)S(1)} custom-call(s32[1]{0:T(128)} %bitcast.1.mine_ref.refs_0_, bf16[96,3072]{1,0:T(8,128)(2,1)S(1)} %collective-permute-done.6.refs_9_.refs_1_, bf16[96,3072]{1,0:T(8,128)(2,1)S(1)} %collective-permute-done.17.refs_10_.refs_2_, bf16[96,3072]{1,0:T(8,128)(2,1)S(1)} %collective-permute-done.11.refs_11_.refs_3_, ...), custom_call_target="tpu_custom_call" | custom-call | flops 1000 | bytes 1000 | tf_op jit(solution)/shard_map/product/pallas_call | solution.py:216
  141.7 6.4 %outer.2 = (bf16[128,3072]{1,0:T(8,128)(2,1)S(1)}, bf16[128,3072]{1,0:T(8,128)(2,1)}) custom-call(bf16[384,256]{1,0:T(8,128)(2,1)S(1)} %get-tuple-element.176.refs_0_, bf16[384,256]{1,0:T(8,128)(2,1)S(1)} %collective-permute-done.19.refs_1_, bf16[384,256]{1,0:T(8,128)(2,1)S(1)} %collective-permute-done.29.refs_2_, ...), custom_call_target="tpu_custom_call" | custom-call | flops 1000 | bytes 1000 | tf_op jit(solution)/shard_map/outer/pallas_call | solution.py:260
  148.1 1.5 collective-permute-done.33.refs_2_
  149.7 1.6 collective-permute-start.37
  151.3 1.7 product.9
  153.0 3.1 %collective-permute-start.34 = (bf16[384,256]{1,0:T(8,128)(2,1)S(1)}, bf16[384,256]{1,0:T(8,128)(2,1)S(1)}, u32[]{:S(2)}, u32[]{:S(2)}) collective-permute-start(bf16[384,256]{1,0:T(8,128)(2,1)S(1)} %product.9), channel_id=1, source_target_pairs={{0,8},{4,12},{8,24},{12,28},{24,16},{28,20},{16,0},{20,4},{1,9},{5... | collective-permute-start | bytes 589832 | tf_op jit(solution)/shard_map/ppermute | solution.py:498
  156.1 5.6 %outer.3 = (bf16[128,3072]{1,0:T(8,128)(2,1)S(1)}, bf16[128,3072]{1,0:T(8,128)(2,1)S(1)}) custom-call(bf16[384,256]{1,0:T(8,128)(2,1)S(1)} %get-tuple-element.176.refs_0_, bf16[384,256]{1,0:T(8,128)(2,1)S(1)} %collective-permute-done.19.refs_1_, bf16[384,256]{1,0:T(8,128)(2,1)S(1)} %collective-permute-done.29.refs_2_, ...), custom_call_target="tpu_custom_call" | custom-call | flops 1000 | bytes 1000 | tf_op jit(solution)/shard_map/outer/pallas_call | solution.py:260
  164.9 2.9 %collective-permute-done.36.there_ref = f32[1,384]{1,0:T(1,128)S(1)} collective-permute-done((f32[1,384]{1,0:T(1,128)S(1)}, f32[1,384]{1,0:T(1,128)S(1)}, u32[]{:S(2)}, u32[]{:S(2)}) %collective-permute-start.36) | collective-permute-done | bytes 1568 | tf_op jit(solution)/shard_map/ppermute | solution.py:400
  170.9 3.6 %all-to-all-start.2 = ((bf16[8,144,128]{2,1,0:T(8,128)(2,1)}), bf16[8,144,128]{2,1,0:T(8,128)(2,1)S(1)}, u32[]{:S(2)}, u32[]{:S(2)}) async-start(bf16[8,144,128]{2,1,0:T(8,128)(2,1)} %copy-done.22), calls=%async_computation.2 | async-start | bytes 589824 | tf_op jit(solution)/shard_map/all_to_all | solution.py:516
  174.6 2.0 collective-permute-start.38
  177.7 4.5 %inside.1 = (bf16[384,1024]{1,0:T(8,128)(2,1)}, bf16[384,1024]{1,0:T(8,128)(2,1)S(1)}, bf16[384,1024]{1,0:T(8,128)(2,1)S(1)}) custom-call(bf16[384,1024]{1,0:T(8,128)(2,1)S(1)} %copy-done.21, bf16[384,1024]{1,0:T(8,128)(2,1)S(1)} %copy-done.8, bf16[384,1024]{1,0:T(8,128)(2,1)S(1)} %copy-done.3, bf16[384,1024]{1,0:T(8,128)(2,1)S(1)} %copy-done.5, ...), custom_call_target="tpu_custom_call" | custom-call | flops 1000 | bytes 1000 | tf_op jit(solution)/shard_map/inside/pallas_call | solution.py:386
  186.0 4.9 %all-to-all-start.3 = ((bf16[8,128,128]{2,1,0:T(8,128)(2,1)}), bf16[8,128,128]{2,1,0:T(8,128)(2,1)S(1)}, u32[]{:S(2)}, u32[]{:S(2)}) async-start(bf16[8,128,128]{2,1,0:T(8,128)(2,1)} %scan.3), calls=%async_computation.3 | async-start | bytes 524288 | tf_op jit(solution)/shard_map/all_to_all | solution.py:530
  191.0 2.0 collective-permute-start.40
  193.0 2.8 %collective-permute-done.40 = f32[1,1024]{1,0:T(1,128)S(1)} collective-permute-done((f32[1,1024]{1,0:T(1,128)S(1)}, f32[1,1024]{1,0:T(1,128)S(1)}, u32[]{:S(2)}, u32[]{:S(2)}) %collective-permute-start.40) | collective-permute-done | bytes 4128 | tf_op jit(solution)/shard_map/ppermute | solution.py:532
  195.8 3.5 %collective-permute-start.41 = (f32[1,1024]{1,0:T(1,128)S(1)}, f32[1,1024]{1,0:T(1,128)S(1)}, u32[]{:S(2)}, u32[]{:S(2)}) collective-permute-start(f32[1,1024]{1,0:T(1,128)S(1)} %add.143), channel_id=1, source_target_pairs={{0,16},{4,20},{8,24},{12,28},{16,0},{20,4},{24,8},{28,12},{1,17},{... | collective-permute-start | bytes 12296 | tf_op jit(solution)/shard_map/ppermute | solution.py:532
  199.3 1.6 collective-permute-done.41
  201.5 3.6 %all-to-all-done.3.state_ref = bf16[8,128,128]{2,1,0:T(8,128)(2,1)S(1)} async-done(((bf16[8,128,128]{2,1,0:T(8,128)(2,1)}), bf16[8,128,128]{2,1,0:T(8,128)(2,1)S(1)}, u32[]{:S(2)}, u32[]{:S(2)}) %all-to-all-start.3) | async-done | bytes 262176 | tf_op jit(solution)/shard_map/all_to_all | solution.py:530
  207.4 2.0 outside.1
  209.4 2.9 %sum.1 = bf16[128,6144]{1,0:T(8,128)(2,1)} custom-call(bf16[128,3072]{1,0:T(8,128)(2,1)S(1)} %copy-done.13, bf16[128,3072]{1,0:T(8,128)(2,1)} %collective-permute-done.37.refs_1_, bf16[128,3072]{1,0:T(8,128)(2,1)S(1)} %copy-done.15, bf16[128,3072]{1,0:T(8,128)(2,1)} %collective-permute-done.39.refs_3_), custom_call_target="tpu_custom_call" | custom-call | flops 1000 | bytes 1000 | tf_op jit(solution)/shard_map/sum/pallas_call | solution.py:386
  (128 shorter events, 36.7 us)
Async XLA Ops:
  3.2 24.8 %collective-permute-start = (bf16[96,3072]{1,0:T(8,128)(2,1)}, bf16[96,3072]{1,0:T(8,128)(2,1)}, u32[]{:S(2)}, u32[]{:S(2)}) collective-permute-start(bf16[96,3072]{1,0:T(8,128)(2,1)} %get-tuple-element.212), channel_id=1, source_target_pairs={{0,8},{4,12},{8,24},{12,28},{24,16},{28,20},{16,0},{20,4},{1,9},{5... | collective-permute-start | bytes 1769480 | tf_op jit(solution)/shard_map/ppermute | solution.py:397
  8.8 19.2 %all-to-all-start = ((bf16[8,144,128]{2,1,0:T(8,128)(2,1)}), bf16[8,144,128]{2,1,0:T(8,128)(2,1)S(1)}, u32[]{:S(2)}, u32[]{:S(2)}) async-start(bf16[8,144,128]{2,1,0:T(8,128)(2,1)} %get-tuple-element.108), calls=%async_computation | async-start | bytes 589824 | tf_op jit(solution)/shard_map/all_to_all | solution.py:419
  13.6 28.5 %collective-permute-start.1 = (bf16[96,3072]{1,0:T(8,128)(2,1)}, bf16[96,3072]{1,0:T(8,128)(2,1)}, u32[]{:S(2)}, u32[]{:S(2)}) collective-permute-start(bf16[96,3072]{1,0:T(8,128)(2,1)} %get-tuple-element.112), channel_id=1, source_target_pairs={{0,8},{4,12},{8,24},{12,28},{24,16},{28,20},{16,0},{20,4},{1,9},{5... | collective-permute-start | bytes 1769480 | tf_op jit(solution)/shard_map/ppermute | solution.py:397
  15.6 90.7 %slice-start = ((s8[4718592]{0:T(1024)(128)(4,1)}), s8[524288]{0:T(1024)(128)(4,1)S(1)}, s32[]{:S(2)}) async-start(s8[4718592]{0:T(1024)(128)(4,1)} %bitcast.5), calls=%async_computation.4 | async-start | bytes 1048576
  27.9 17.4 %collective-permute-start.2 = (bf16[96,3072]{1,0:T(8,128)(2,1)}, bf16[96,3072]{1,0:T(8,128)(2,1)}, u32[]{:S(2)}, u32[]{:S(2)}) collective-permute-start(bf16[96,3072]{1,0:T(8,128)(2,1)} %collective-permute-done.refs_1_.refs_5_), channel_id=1, source_target_pairs={{0,2},{1,3},{2,0},{3,1},{4,6},{5,7},{6,4},{7,5},{8,10},{9,11},{10,... | collective-permute-start | bytes 1769480 | tf_op jit(solution)/shard_map/ppermute | solution.py:400
  30.6 14.8 %all-to-all-start.1 = ((bf16[8,128,128]{2,1,0:T(8,128)(2,1)}), bf16[8,128,128]{2,1,0:T(8,128)(2,1)S(1)}, u32[]{:S(2)}, u32[]{:S(2)}) async-start(bf16[8,128,128]{2,1,0:T(8,128)(2,1)} %copy-done.11), calls=%async_computation.1 | async-start | bytes 524288 | tf_op jit(solution)/shard_map/all_to_all | solution.py:427
  45.4 61.0 %slice-start.1 = ((s8[4718592]{0:T(1024)(128)(4,1)}), s8[4194304]{0:T(1024)(128)(4,1)S(1)}, s32[]{:S(2)}) async-start(s8[4718592]{0:T(1024)(128)(4,1)} %bitcast.5), calls=%async_computation.5 | async-start | bytes 8388608
  45.4 4.4 %collective-permute-start.4 = (bf16[96,3072]{1,0:T(8,128)(2,1)}, bf16[96,3072]{1,0:T(8,128)(2,1)S(1)}, u32[]{:S(2)}, u32[]{:S(2)}) collective-permute-start(bf16[96,3072]{1,0:T(8,128)(2,1)} %collective-permute-done.refs_1_.refs_5_), channel_id=1, source_target_pairs={{0,1},{1,0},{2,3},{3,2},{4,5},{5,4},{6,7},{7,6},{8,9},{9,8},{10,11... | collective-permute-start | bytes 1769480 | tf_op jit(solution)/shard_map/ppermute | solution.py:400
  45.4 17.6 %collective-permute-start.6 = (bf16[96,3072]{1,0:T(8,128)(2,1)}, bf16[96,3072]{1,0:T(8,128)(2,1)S(1)}, u32[]{:S(2)}, u32[]{:S(2)}) collective-permute-start(bf16[96,3072]{1,0:T(8,128)(2,1)} %collective-permute-done.refs_1_.refs_5_), channel_id=1, source_target_pairs={{0,8},{4,12},{8,24},{12,28},{24,16},{28,20},{16,0},{20,4},{1,9},{5... | collective-permute-start | bytes 1769480 | tf_op jit(solution)/shard_map/ppermute | solution.py:397
  46.7 3.0 %collective-permute-start.3 = (bf16[96,3072]{1,0:T(8,128)(2,1)}, bf16[96,3072]{1,0:T(8,128)(2,1)S(1)}, u32[]{:S(2)}, u32[]{:S(2)}) collective-permute-start(bf16[96,3072]{1,0:T(8,128)(2,1)} %collective-permute-done.2.refs_3_.refs_7_), channel_id=1, source_target_pairs={{0,1},{1,0},{2,3},{3,2},{4,5},{5,4},{6,7},{7,6},{8,9},{9,8},{10,11... | collective-permute-start | bytes 1769480 | tf_op jit(solution)/shard_map/ppermute | solution.py:400
  46.8 16.2 %collective-permute-start.7 = (bf16[96,3072]{1,0:T(8,128)(2,1)}, bf16[96,3072]{1,0:T(8,128)(2,1)S(1)}, u32[]{:S(2)}, u32[]{:S(2)}) collective-permute-start(bf16[96,3072]{1,0:T(8,128)(2,1)} %collective-permute-done.1.refs_5_), channel_id=1, source_target_pairs={{0,2},{1,3},{2,0},{3,1},{4,6},{5,7},{6,4},{7,5},{8,10},{9,11},{10,... | collective-permute-start | bytes 1769480 | tf_op jit(solution)/shard_map/ppermute | solution.py:400
  48.5 14.0 %collective-permute-start.9 = (bf16[128,2048]{1,0:T(8,128)(2,1)S(1)}, bf16[128,2048]{1,0:T(8,128)(2,1)S(1)}, u32[]{:S(2)}, u32[]{:S(2)}) collective-permute-start(bf16[128,2048]{1,0:T(8,128)(2,1)S(1)} %get-tuple-element.215), channel_id=1, source_target_pairs={{0,4},{4,0},{8,12},{12,8},{16,20},{20,16},{24,28},{28,24},{1,5},{5... | collective-permute-start | bytes 1572872 | tf_op jit(solution)/shard_map/ppermute | solution.py:436
  51.9 1.2 collective-permute-start.5
  53.1 9.9 %collective-permute-start.8 = (f32[1,384]{1,0:T(1,128)S(1)}, f32[1,384]{1,0:T(1,128)S(1)}, u32[]{:S(2)}, u32[]{:S(2)}) collective-permute-start(f32[1,384]{1,0:T(1,128)S(1)} %add.140.here_ref), channel_id=1, source_target_pairs={{0,2},{1,3},{2,0},{3,1},{4,6},{5,7},{6,4},{7,5},{8,10},{9,11},{10,... | collective-permute-start | bytes 4616 | tf_op jit(solution)/shard_map/ppermute | solution.py:400
  63.0 18.6 %collective-permute-start.10 = (bf16[96,3072]{1,0:T(8,128)(2,1)}, bf16[96,3072]{1,0:T(8,128)(2,1)S(1)}, u32[]{:S(2)}, u32[]{:S(2)}) collective-permute-start(bf16[96,3072]{1,0:T(8,128)(2,1)} %collective-permute-done.1.refs_5_), channel_id=1, source_target_pairs={{0,8},{4,12},{8,24},{12,28},{24,16},{28,20},{16,0},{20,4},{1,9},{5... | collective-permute-start | bytes 1769480 | tf_op jit(solution)/shard_map/ppermute | solution.py:397
  65.7 15.9 %collective-permute-start.12 = (bf16[96,3072]{1,0:T(8,128)(2,1)}, bf16[96,3072]{1,0:T(8,128)(2,1)S(1)}, u32[]{:S(2)}, u32[]{:S(2)}) collective-permute-start(bf16[96,3072]{1,0:T(8,128)(2,1)} %collective-permute-done.1.refs_5_), channel_id=1, source_target_pairs={{0,1},{1,0},{2,3},{3,2},{4,5},{5,4},{6,7},{7,6},{8,9},{9,8},{10,11... | collective-permute-start | bytes 1769480 | tf_op jit(solution)/shard_map/ppermute | solution.py:400
  65.7 15.9 %collective-permute-start.11 = (bf16[96,3072]{1,0:T(8,128)(2,1)S(1)}, bf16[96,3072]{1,0:T(8,128)(2,1)S(1)}, u32[]{:S(2)}, u32[]{:S(2)}) collective-permute-start(bf16[96,3072]{1,0:T(8,128)(2,1)S(1)} %collective-permute-done.6.refs_9_.refs_1_), channel_id=1, source_target_pairs={{0,2},{1,3},{2,0},{3,1},{4,6},{5,7},{6,4},{7,5},{8,10},{9,11},{10,... | collective-permute-start | bytes 1769480 | tf_op jit(solution)/shard_map/ppermute | solution.py:400
  67.2 14.4 %collective-permute-start.13 = (bf16[96,3072]{1,0:T(8,128)(2,1)S(1)}, bf16[96,3072]{1,0:T(8,128)(2,1)S(1)}, u32[]{:S(2)}, u32[]{:S(2)}) collective-permute-start(bf16[96,3072]{1,0:T(8,128)(2,1)S(1)} %collective-permute-done.7.refs_7_), channel_id=1, source_target_pairs={{0,1},{1,0},{2,3},{3,2},{4,5},{5,4},{6,7},{7,6},{8,9},{9,8},{10,11... | collective-permute-start | bytes 1769480 | tf_op jit(solution)/shard_map/ppermute | solution.py:400
  67.5 14.1 %collective-permute-start.14 = (bf16[128,2048]{1,0:T(8,128)(2,1)S(1)}, bf16[128,2048]{1,0:T(8,128)(2,1)S(1)}, u32[]{:S(2)}, u32[]{:S(2)}) collective-permute-start(bf16[128,2048]{1,0:T(8,128)(2,1)S(1)} %get-tuple-element.133), channel_id=1, source_target_pairs={{0,4},{4,0},{8,12},{12,8},{16,20},{20,16},{24,28},{28,24},{1,5},{5... | collective-permute-start | bytes 1572872 | tf_op jit(solution)/shard_map/ppermute | solution.py:436
  81.6 8.8 %collective-permute-start.19 = (bf16[384,256]{1,0:T(8,128)(2,1)S(1)}, bf16[384,256]{1,0:T(8,128)(2,1)S(1)}, u32[]{:S(2)}, u32[]{:S(2)}) collective-permute-start(bf16[384,256]{1,0:T(8,128)(2,1)S(1)} %get-tuple-element.138), channel_id=1, source_target_pairs={{0,8},{4,12},{8,24},{12,28},{24,16},{28,20},{16,0},{20,4},{1,9},{5... | collective-permute-start | bytes 589832 | tf_op jit(solution)/shard_map/ppermute | solution.py:464
  82.8 18.7 %collective-permute-start.15 = (bf16[96,3072]{1,0:T(8,128)(2,1)S(1)}, bf16[96,3072]{1,0:T(8,128)(2,1)S(1)}, u32[]{:S(2)}, u32[]{:S(2)}) collective-permute-start(bf16[96,3072]{1,0:T(8,128)(2,1)S(1)} %collective-permute-done.6.refs_9_.refs_1_), channel_id=1, source_target_pairs={{0,8},{4,12},{8,24},{12,28},{24,16},{28,20},{16,0},{20,4},{1,9},{5... | collective-permute-start | bytes 1769480 | tf_op jit(solution)/shard_map/ppermute | solution.py:397
  82.9 18.7 %collective-permute-start.17 = (bf16[96,3072]{1,0:T(8,128)(2,1)S(1)}, bf16[96,3072]{1,0:T(8,128)(2,1)S(1)}, u32[]{:S(2)}, u32[]{:S(2)}) collective-permute-start(bf16[96,3072]{1,0:T(8,128)(2,1)S(1)} %collective-permute-done.6.refs_9_.refs_1_), channel_id=1, source_target_pairs={{0,1},{1,0},{2,3},{3,2},{4,5},{5,4},{6,7},{7,6},{8,9},{9,8},{10,11... | collective-permute-start | bytes 1769480 | tf_op jit(solution)/shard_map/ppermute | solution.py:400
  82.9 18.7 %collective-permute-start.16 = (bf16[96,3072]{1,0:T(8,128)(2,1)S(1)}, bf16[96,3072]{1,0:T(8,128)(2,1)S(1)}, u32[]{:S(2)}, u32[]{:S(2)}) collective-permute-start(bf16[96,3072]{1,0:T(8,128)(2,1)S(1)} %collective-permute-done.10.refs_5_.refs_9_), channel_id=1, source_target_pairs={{0,2},{1,3},{2,0},{3,1},{4,6},{5,7},{6,4},{7,5},{8,10},{9,11},{10,... | collective-permute-start | bytes 1769480 | tf_op jit(solution)/shard_map/ppermute | solution.py:400
  84.3 17.2 %collective-permute-start.18 = (bf16[96,3072]{1,0:T(8,128)(2,1)S(1)}, bf16[96,3072]{1,0:T(8,128)(2,1)S(1)}, u32[]{:S(2)}, u32[]{:S(2)}) collective-permute-start(bf16[96,3072]{1,0:T(8,128)(2,1)S(1)} %collective-permute-done.11.refs_11_.refs_3_), channel_id=1, source_target_pairs={{0,1},{1,0},{2,3},{3,2},{4,5},{5,4},{6,7},{7,6},{8,9},{9,8},{10,11... | collective-permute-start | bytes 1769480 | tf_op jit(solution)/shard_map/ppermute | solution.py:400
  90.4 11.0 %collective-permute-start.20 = (bf16[128,2048]{1,0:T(8,128)(2,1)S(1)}, bf16[128,2048]{1,0:T(8,128)(2,1)S(1)}, u32[]{:S(2)}, u32[]{:S(2)}) collective-permute-start(bf16[128,2048]{1,0:T(8,128)(2,1)S(1)} %get-tuple-element.139), channel_id=1, source_target_pairs={{0,4},{4,0},{8,12},{12,8},{16,20},{20,16},{24,28},{28,24},{1,5},{5... | collective-permute-start | bytes 1572872 | tf_op jit(solution)/shard_map/ppermute | solution.py:436
  101.6 19.1 %collective-permute-start.21 = (bf16[96,3072]{1,0:T(8,128)(2,1)S(1)}, bf16[96,3072]{1,0:T(8,128)(2,1)S(1)}, u32[]{:S(2)}, u32[]{:S(2)}) collective-permute-start(bf16[96,3072]{1,0:T(8,128)(2,1)S(1)} %collective-permute-done.10.refs_5_.refs_9_), channel_id=1, source_target_pairs={{0,8},{4,12},{8,24},{12,28},{24,16},{28,20},{16,0},{20,4},{1,9},{5... | collective-permute-start | bytes 1769480 | tf_op jit(solution)/shard_map/ppermute | solution.py:397
  101.9 18.7 %collective-permute-start.23 = (bf16[96,3072]{1,0:T(8,128)(2,1)S(1)}, bf16[96,3072]{1,0:T(8,128)(2,1)S(1)}, u32[]{:S(2)}, u32[]{:S(2)}) collective-permute-start(bf16[96,3072]{1,0:T(8,128)(2,1)S(1)} %collective-permute-done.10.refs_5_.refs_9_), channel_id=1, source_target_pairs={{0,1},{1,0},{2,3},{3,2},{4,5},{5,4},{6,7},{7,6},{8,9},{9,8},{10,11... | collective-permute-start | bytes 1769480 | tf_op jit(solution)/shard_map/ppermute | solution.py:400
  101.9 18.7 %collective-permute-start.22 = (bf16[96,3072]{1,0:T(8,128)(2,1)S(1)}, bf16[96,3072]{1,0:T(8,128)(2,1)S(1)}, u32[]{:S(2)}, u32[]{:S(2)}) collective-permute-start(bf16[96,3072]{1,0:T(8,128)(2,1)S(1)} %collective-permute-done.15.refs_1_.refs_13_), channel_id=1, source_target_pairs={{0,2},{1,3},{2,0},{3,1},{4,6},{5,7},{6,4},{7,5},{8,10},{9,11},{10,... | collective-permute-start | bytes 1769480 | tf_op jit(solution)/shard_map/ppermute | solution.py:400
  103.4 17.2 %collective-permute-start.24 = (bf16[96,3072]{1,0:T(8,128)(2,1)S(1)}, bf16[96,3072]{1,0:T(8,128)(2,1)S(1)}, u32[]{:S(2)}, u32[]{:S(2)}) collective-permute-start(bf16[96,3072]{1,0:T(8,128)(2,1)S(1)} %collective-permute-done.16.refs_7_.refs_11_), channel_id=1, source_target_pairs={{0,1},{1,0},{2,3},{3,2},{4,5},{5,4},{6,7},{7,6},{8,9},{9,8},{10,11... | collective-permute-start | bytes 1769480 | tf_op jit(solution)/shard_map/ppermute | solution.py:400
  103.6 16.5 %collective-permute-start.25 = (bf16[384,256]{1,0:T(8,128)(2,1)S(1)}, bf16[384,256]{1,0:T(8,128)(2,1)S(1)}, u32[]{:S(2)}, u32[]{:S(2)}) collective-permute-start(bf16[384,256]{1,0:T(8,128)(2,1)S(1)} %get-tuple-element.143), channel_id=1, source_target_pairs={{0,16},{4,20},{8,0},{12,4},{24,8},{28,12},{16,24},{20,28},{1,17},{... | collective-permute-start | bytes 589832 | tf_op jit(solution)/shard_map/ppermute | solution.py:470
  120.6 3.5 %collective-permute-start.27 = (bf16[96,3072]{1,0:T(8,128)(2,1)S(1)}, bf16[96,3072]{1,0:T(8,128)(2,1)S(1)}, u32[]{:S(2)}, u32[]{:S(2)}) collective-permute-start(bf16[96,3072]{1,0:T(8,128)(2,1)S(1)} %collective-permute-done.15.refs_1_.refs_13_), channel_id=1, source_target_pairs={{0,1},{1,0},{2,3},{3,2},{4,5},{5,4},{6,7},{7,6},{8,9},{9,8},{10,11... | collective-permute-start | bytes 1769480 | tf_op jit(solution)/shard_map/ppermute | solution.py:400
  120.7 3.4 %collective-permute-start.28 = (bf16[96,3072]{1,0:T(8,128)(2,1)S(1)}, bf16[96,3072]{1,0:T(8,128)(2,1)S(1)}, u32[]{:S(2)}, u32[]{:S(2)}) collective-permute-start(bf16[96,3072]{1,0:T(8,128)(2,1)S(1)} %collective-permute-done.22.refs_3_.refs_15_), channel_id=1, source_target_pairs={{0,1},{1,0},{2,3},{3,2},{4,5},{5,4},{6,7},{7,6},{8,9},{9,8},{10,11... | collective-permute-start | bytes 1769480 | tf_op jit(solution)/shard_map/ppermute | solution.py:400
  121.2 15.3 %collective-permute-start.26 = (bf16[96,3072]{1,0:T(8,128)(2,1)S(1)}, bf16[96,3072]{1,0:T(8,128)(2,1)S(1)}, u32[]{:S(2)}, u32[]{:S(2)}) collective-permute-start(bf16[96,3072]{1,0:T(8,128)(2,1)S(1)} %collective-permute-done.21.refs_1_.refs_13_), channel_id=1, source_target_pairs={{0,2},{1,3},{2,0},{3,1},{4,6},{5,7},{6,4},{7,5},{8,10},{9,11},{10,... | collective-permute-start | bytes 1769480 | tf_op jit(solution)/shard_map/ppermute | solution.py:400
  123.0 9.7 %collective-permute-start.29 = (bf16[384,256]{1,0:T(8,128)(2,1)S(1)}, bf16[384,256]{1,0:T(8,128)(2,1)S(1)}, u32[]{:S(2)}, u32[]{:S(2)}) collective-permute-start(bf16[384,256]{1,0:T(8,128)(2,1)S(1)} %get-tuple-element.154), channel_id=1, source_target_pairs={{0,24},{4,28},{8,16},{12,20},{24,0},{28,4},{16,8},{20,12},{1,25},{... | collective-permute-start | bytes 589832 | tf_op jit(solution)/shard_map/ppermute | solution.py:482
  123.9 10.5 %collective-permute-start.30 = (bf16[384,256]{1,0:T(8,128)(2,1)S(1)}, bf16[384,256]{1,0:T(8,128)(2,1)S(1)}, u32[]{:S(2)}, u32[]{:S(2)}) collective-permute-start(bf16[384,256]{1,0:T(8,128)(2,1)S(1)} %product.6), channel_id=1, source_target_pairs={{0,16},{4,20},{8,0},{12,4},{24,8},{28,12},{16,24},{20,28},{1,17},{... | collective-permute-start | bytes 589832 | tf_op jit(solution)/shard_map/ppermute | solution.py:483
  124.2 25.5 %collective-permute-start.32 = (bf16[96,3072]{1,0:T(8,128)(2,1)S(1)}, bf16[96,3072]{1,0:T(8,128)(2,1)S(1)}, u32[]{:S(2)}, u32[]{:S(2)}) collective-permute-start(bf16[96,3072]{1,0:T(8,128)(2,1)S(1)} %collective-permute-done.21.refs_1_.refs_13_), channel_id=1, source_target_pairs={{0,1},{1,0},{2,3},{3,2},{4,5},{5,4},{6,7},{7,6},{8,9},{9,8},{10,11... | collective-permute-start | bytes 1769480 | tf_op jit(solution)/shard_map/ppermute | solution.py:400
  136.5 13.1 %collective-permute-start.31 = (bf16[96,3072]{1,0:T(8,128)(2,1)S(1)}, bf16[96,3072]{1,0:T(8,128)(2,1)S(1)}, u32[]{:S(2)}, u32[]{:S(2)}) collective-permute-start(bf16[96,3072]{1,0:T(8,128)(2,1)S(1)} %collective-permute-done.26.refs_3_.refs_15_), channel_id=1, source_target_pairs={{0,1},{1,0},{2,3},{3,2},{4,5},{5,4},{6,7},{7,6},{8,9},{9,8},{10,11... | collective-permute-start | bytes 1769480 | tf_op jit(solution)/shard_map/ppermute | solution.py:400
  140.4 9.3 %collective-permute-start.33 = (bf16[384,256]{1,0:T(8,128)(2,1)S(1)}, bf16[384,256]{1,0:T(8,128)(2,1)S(1)}, u32[]{:S(2)}, u32[]{:S(2)}) collective-permute-start(bf16[384,256]{1,0:T(8,128)(2,1)S(1)} %product.8), channel_id=1, source_target_pairs={{0,24},{4,28},{8,16},{12,20},{24,0},{28,4},{16,8},{20,12},{1,25},{... | collective-permute-start | bytes 589832 | tf_op jit(solution)/shard_map/ppermute | solution.py:487
  149.7 34.3 %collective-permute-start.37 = (bf16[128,3072]{1,0:T(8,128)(2,1)}, bf16[128,3072]{1,0:T(8,128)(2,1)}, u32[]{:S(2)}, u32[]{:S(2)}) collective-permute-start(bf16[128,3072]{1,0:T(8,128)(2,1)} %get-tuple-element.195), channel_id=1, source_target_pairs={{0,4},{4,0},{8,12},{12,8},{16,20},{20,16},{24,28},{28,24},{1,5},{5... | collective-permute-start | bytes 2359304 | tf_op jit(solution)/shard_map/ppermute | solution.py:500
  153.0 8.8 %collective-permute-start.34 = (bf16[384,256]{1,0:T(8,128)(2,1)S(1)}, bf16[384,256]{1,0:T(8,128)(2,1)S(1)}, u32[]{:S(2)}, u32[]{:S(2)}) collective-permute-start(bf16[384,256]{1,0:T(8,128)(2,1)S(1)} %product.9), channel_id=1, source_target_pairs={{0,8},{4,12},{8,24},{12,28},{24,16},{28,20},{16,0},{20,4},{1,9},{5... | collective-permute-start | bytes 589832 | tf_op jit(solution)/shard_map/ppermute | solution.py:498
  163.0 1.2 collective-permute-start.35
  164.2 3.6 %collective-permute-start.36 = (f32[1,384]{1,0:T(1,128)S(1)}, f32[1,384]{1,0:T(1,128)S(1)}, u32[]{:S(2)}, u32[]{:S(2)}) collective-permute-start(f32[1,384]{1,0:T(1,128)S(1)} %add.141.here_ref), channel_id=1, source_target_pairs={{0,2},{1,3},{2,0},{3,1},{4,6},{5,7},{6,4},{7,5},{8,10},{9,11},{10,... | collective-permute-start | bytes 4616 | tf_op jit(solution)/shard_map/ppermute | solution.py:400
  170.9 13.0 %all-to-all-start.2 = ((bf16[8,144,128]{2,1,0:T(8,128)(2,1)}), bf16[8,144,128]{2,1,0:T(8,128)(2,1)S(1)}, u32[]{:S(2)}, u32[]{:S(2)}) async-start(bf16[8,144,128]{2,1,0:T(8,128)(2,1)} %copy-done.22), calls=%async_computation.2 | async-start | bytes 589824 | tf_op jit(solution)/shard_map/all_to_all | solution.py:516
  174.6 9.4 %collective-permute-start.38 = (f32[1,1024]{1,0:T(1,128)S(1)}, f32[1,1024]{1,0:T(1,128)S(1)}, u32[]{:S(2)}, u32[]{:S(2)}) collective-permute-start(f32[1,1024]{1,0:T(1,128)S(1)} %get-tuple-element.198), channel_id=1, source_target_pairs={{0,4},{4,0},{8,12},{12,8},{16,20},{20,16},{24,28},{28,24},{1,5},{5... | collective-permute-start | bytes 12296 | tf_op jit(solution)/shard_map/ppermute | solution.py:519
  184.0 25.4 %collective-permute-start.39 = (bf16[128,3072]{1,0:T(8,128)(2,1)}, bf16[128,3072]{1,0:T(8,128)(2,1)}, u32[]{:S(2)}, u32[]{:S(2)}) collective-permute-start(bf16[128,3072]{1,0:T(8,128)(2,1)} %copy-done.25), channel_id=1, source_target_pairs={{0,4},{4,0},{8,12},{12,8},{16,20},{20,16},{24,28},{28,24},{1,5},{5... | collective-permute-start | bytes 2359304 | tf_op jit(solution)/shard_map/ppermute | solution.py:528
  186.0 19.1 %all-to-all-start.3 = ((bf16[8,128,128]{2,1,0:T(8,128)(2,1)}), bf16[8,128,128]{2,1,0:T(8,128)(2,1)S(1)}, u32[]{:S(2)}, u32[]{:S(2)}) async-start(bf16[8,128,128]{2,1,0:T(8,128)(2,1)} %scan.3), calls=%async_computation.3 | async-start | bytes 524288 | tf_op jit(solution)/shard_map/all_to_all | solution.py:530
  191.0 4.8 %collective-permute-start.40 = (f32[1,1024]{1,0:T(1,128)S(1)}, f32[1,1024]{1,0:T(1,128)S(1)}, u32[]{:S(2)}, u32[]{:S(2)}) collective-permute-start(f32[1,1024]{1,0:T(1,128)S(1)} %add.142), channel_id=1, source_target_pairs={{0,8},{4,12},{8,0},{12,4},{16,24},{20,28},{24,16},{28,20},{1,9},{5... | collective-permute-start | bytes 12296 | tf_op jit(solution)/shard_map/ppermute | solution.py:532
  195.8 5.1 %collective-permute-start.41 = (f32[1,1024]{1,0:T(1,128)S(1)}, f32[1,1024]{1,0:T(1,128)S(1)}, u32[]{:S(2)}, u32[]{:S(2)}) collective-permute-start(f32[1,1024]{1,0:T(1,128)S(1)} %add.143), channel_id=1, source_target_pairs={{0,16},{4,20},{8,24},{12,28},{16,0},{20,4},{24,8},{28,12},{1,17},{... | collective-permute-start | bytes 12296 | tf_op jit(solution)/shard_map/ppermute | solution.py:532
  (26 other events, 170.3 us)

commit v10 on v9

--- a/solution.py
+++ b/solution.py
@@ -233,23 +233,30 @@
     )(mine, *[p for lot in lots for p in lot], weight, *[w for ws in others for w in ws], *more)
 
 
-def outer_kernel(lots, own, *refs):
+def outer_kernel(lots, own, split, *refs):
     refs = list(refs)
-    normed = [refs.pop(0) for _ in lots]
-    x = [[refs.pop(0) for _ in range(k)] for k in lots]
+    normed = [refs.pop(0) for _ in range(LINE)]
+    x = [refs.pop(0) for _ in range(lots)]
     turned_ref = refs.pop()
-
-    @pl.when(pl.program_id(0) == 0)
+    step = pl.program_id(0)
+    steps = pl.num_programs(0) // split
+    minor = len(refs) // split
+
+    @pl.when(step == 0)
     def _():
         turned_ref[...] = jnp.concatenate([r[...] for r in normed], axis=0).T
 
-    rows = jnp.concatenate([r[...] for lot in x for r in lot], axis=0)
+    rows = jnp.concatenate([r[...] for r in x], axis=0)
     out = dot(turned_ref[...], rows, NN).astype(BF)
-    for s, ref in enumerate(refs):
-        ref[...] = out[s * own : (s + 1) * own]
-
-
-def outer(normed, grad_out, lots, chunk, own):
+    for h in range(split):
+
+        @pl.when(step // steps == h)
+        def _():
+            for s in range(minor):
+                refs[h * minor + s][...] = out[s * own : (s + 1) * own]
+
+
+def outer(normed, grad_out, lots, chunk, own, split):
     tok, span = normed[0].shape
     deep = lots[0][0].shape[1]
     tile = 512
@@ -257,29 +264,36 @@
     base = chunk * steps
     flat = [p for lot in lots for p in lot]
     minor = span // own
-    return pl.pallas_call(
-        functools.partial(outer_kernel, [1] + [len(lot) for lot in lots], own),
+    part = steps // split
+
+    def out_spec(h):
+        return spec((own, tile), lambda i: (0, jnp.clip(i - h * part, 0, part - 1)))
+
+    outs = pl.pallas_call(
+        functools.partial(outer_kernel, 1 + len(flat), own, split),
         grid=(steps,),
         in_specs=[spec((tok, span)) for _ in normed]
         + [spec((tok, tile), lambda i: (0, base + i))]
         + [spec((p.shape[0], tile), lambda i: (0, i)) for p in flat],
-        out_specs=[spec((own, tile), lambda i: (0, i))] * minor,
-        out_shape=[jax.ShapeDtypeStruct((own, deep), BF)] * minor,
+        out_specs=[out_spec(h) for h in range(split) for _ in range(minor)],
+        out_shape=[jax.ShapeDtypeStruct((own, deep // split), BF)] * (minor * split),
         scratch_shapes=[pltpu.VMEM((span, tok * LINE), BF)],
         compiler_params=PARAMS,
         cost_estimate=TINY,
         name="outer",
     )(*normed, grad_out, *flat)
-
-
-def final_kernel(chunks, minor, *refs):
+    return [list(outs[h * minor : (h + 1) * minor]) for h in range(split)]
+
+
+def final_kernel(minor, *refs):
     out_ref = refs[-1]
-    deep = refs[0].shape[1]
-    for c in range(chunks):
-        total = refs[c * minor][...].astype(FL)
+    at = 0
+    for c in range(0, len(refs) - 1, minor):
+        total = refs[c][...].astype(FL)
         for s in range(1, minor):
-            total = total + refs[c * minor + s][...].astype(FL)
-        out_ref[:, c * deep : (c + 1) * deep] = total.astype(BF)
+            total = total + refs[c + s][...].astype(FL)
+        out_ref[:, at : at + total.shape[1]] = total.astype(BF)
+        at += total.shape[1]
 
 
 def back_kernel(order_ref, attn_ref, inv_ref, gain_ref, *refs):
@@ -460,13 +474,13 @@
     normed = [sent[0], None, None, None]
 
     ra3, yb2, na2, fa2 = ring(ra2), other_of(rb2), near_of(ra2), near_of(ya2)
+    na2, fa2, sent[1], thirds[2] = hold((na2, fa2, sent[1], thirds[2]))
     others.append(swap(thirds[2]))
     normed[1] = lax.ppermute(sent[1], "ctx", ring_perm(count, 1))
-    rb2, ra3, yb2, na2, fa2, normed[1], others[2] = hold(
-        (rb2, ra3, yb2, na2, fa2, normed[1], others[2])
-    )
+    rb2, ra3, yb2, normed[1], others[2] = hold((rb2, ra3, yb2, normed[1], others[2]))
 
     rb3, ya3, nb2, fb2 = ring(rb2), other_of(ra3), near_of(rb2), near_of(yb2)
+    nb2, fb2, sent[3] = hold((nb2, fb2, sent[3]))
     normed[3] = lax.ppermute(sent[3], "ctx", ring_perm(count, 3))
     mine_part = product(
         tokens, [[grad_out]] * CHUNKS, weight_own, others, 0, True, None, whole=True
@@ -474,9 +488,7 @@
     one = product(
         tokens, [[ra1, na1, ya1, fa1], [rb1, nb1, yb1, fb1]], weight_own, others, 0, True, None
     )
-    ra3, rb3, ya3, nb2, fb2, normed[3], mine_part, one = hold(
-        (ra3, rb3, ya3, nb2, fb2, normed[3], mine_part, one)
-    )
+    ra3, rb3, ya3, normed[3], mine_part, one = hold((ra3, rb3, ya3, normed[3], mine_part, one))
 
     yb3, na3, fa3 = other_of(rb3), near_of(ra3), near_of(ya3)
     normed[2] = lax.ppermute(sent[2], "ctx", ring_perm(count, 2))
@@ -484,22 +496,26 @@
     two = product(
         tokens, [[ra2, na2, ya2, fa2], [rb2, nb2, yb2, fb2]], weight_own, others, 0, True, None
     )
-    returned.append(lax.ppermute(two, "ctx", ring_perm(count, -2)))
     last_lot = [ra3, na3, ya3, fa3]
     three = product(tokens, [last_lot], weight_own, others, 0, False, None)
-    yb3, three, normed[2], returned[1] = hold((yb3, three, normed[2], returned[1]))
+    returned.append(lax.ppermute(two, "ctx", ring_perm(count, -2)))
+    yb3, rb3, three, normed[2], returned[1], _ = hold(
+        (yb3, rb3, three, normed[2], returned[1], two)
+    )
 
     fb3, nb3 = near_of(yb3), near_of(rb3)
+    fb3, nb3, three = hold((fb3, nb3, three))
     lots = [[ra1, na1, ya1, fa1], [ra2, na2, ya2, fa2], last_lot]
-    early = outer(normed, grad_out, lots, 0, own)
-    fb3, nb3, three, early, returned = hold((fb3, nb3, three, early, returned))
     last_lot = [rb3, nb3, yb3, fb3]
     three = product(tokens, [last_lot], weight_own, others, 1, True, three)
     returned.append(lax.ppermute(three, "ctx", ring_perm(count, -3)))
+    normed[0] = after(normed[0], three)
+    (early,) = outer(normed, grad_out, lots, 0, own, 1)
     flat = [early[0]]
     flat += [lax.ppermute(early[s], "ctx", pair_perm(count, s)) for s in range(1, minor)]
+    normed[0] = after(normed[0], early[0])
     lots = [[rb1, nb1, yb1, fb1], [rb2, nb2, yb2, fb2], last_lot]
-    late = outer([after(normed[0], three)] + normed[1:], grad_out, lots, 1, own)
+    late = outer(normed, grad_out, lots, 1, own, 2)
     returned, late = hold((returned, late))
 
     grad, gain_sum, inner = whole(
@@ -516,7 +532,14 @@
     spread = lax.all_to_all(put_back, "ctx", 0, 0, tiled=True)
     gain_sum, late, grad_attn = hold((gain_sum, late, grad_attn))
     flips = [1 << i for i in range(count.bit_length() - 1)]
+
+    def leave(parts):
+        return [parts[0]] + [
+            lax.ppermute(parts[s], "ctx", pair_perm(count, s)) for s in range(1, minor)
+        ]
+
     gain_sum = gain_sum + lax.ppermute(gain_sum, "ctx", [(i, i ^ 1) for i in range(count)])
+    flat += leave(late[0])
     grad_query, gk_in, gv_in = whole(
         inside_kernel, [wide_b] * 3, "inside",
         grad_attn, query_rows, key_rows, value_rows, run, turned, state_low,
@@ -524,8 +547,7 @@
     spread, flat, gk_in, gv_in, gain_sum, late = hold(
         (spread, flat, gk_in, gv_in, gain_sum, late)
     )
-    flat.append(late[0])
-    flat += [lax.ppermute(late[s], "ctx", pair_perm(count, s)) for s in range(1, minor)]
+    flat += leave(late[1])
     states = whole(functools.partial(scan_kernel, True), scan_shape, "scan", spread)
     back_low = lax.all_to_all(states, "ctx", 0, 0, tiled=True).reshape(heads, size, size)
     for step in flips[1:]:
@@ -538,7 +560,7 @@
         key_rows, value_rows, back_low, turned, gk_in, gv_in,
     )
     grad_weight = whole(
-        functools.partial(final_kernel, CHUNKS, minor), jax.ShapeDtypeStruct((own, model), BF),
+        functools.partial(final_kernel, minor), jax.ShapeDtypeStruct((own, model), BF),
         "sum", *flat,
     ).reshape(heads, narrow, model)
     return grad_query, grad_key, grad_value, grad_weight, grad_gain

time: 213 us -> 225 us (1.056)
  waiting for transfers between devices: 81.4 us -> 86.3 us
  local copies, waits for them, and re-layouts: 14.2 us -> 18.9 us
    ppermute x22, waiting for transfers between devices: 7.29 us -> 21 us  [over(): return lax.ppermute(x, 'head', perm)]
    ppermute x3, waiting for transfers between devices: 27.9 us -> 17.3 us  [swap(): lax.ppermute(part, 'ctx', pair_perm(count, -s))]
    ppermute x1, waiting for transfers between devices: 6.7 us -> 0.82 us  [shards(): normed[2] = lax.ppermute(sent[2], 'ctx', ring_perm(count, 2))]
    ppermute x1, waiting for transfers between devices: 0.01 us -> 5.62 us  [shards(): returned.append(lax.ppermute(three, 'ctx', ring_perm(count, -3)))]
    unnamed x56 -> x66, local copies, waits for them, and re-layouts: 11.7 us -> 16.3 us
    ppermute x1, waiting for transfers between devices: 0.01 us -> 3.71 us  [shards(): lax.ppermute(gain_sum, 'ctx', [(i, i ^ 1) for i in range(count)])]
    ppermute x6, waiting for transfers between devices: 4.7 us -> 8.41 us  [ring(): return lax.ppermute(x, 'ctx', ring_perm(count, 1))]
    all_to_all x1, waiting for transfers between devices: 3.63 us -> 0.01 us  [shards(): lax.all_to_all(states, 'ctx', 0, 0, tiled=True).reshape(heads, size, size)]
  transfers between devices with their start and end apart: 46 -> 47, of which waited for: 21 -> 27; matrix products, arithmetic and copies ran while one was open for 1% -> 1% of each run, Pallas kernels for 21% -> 16%
where the time goes in v10:
time: 225 us; the launch traced here: 224 us
  waiting for transfers between devices  86.3 us (38%)
  starting transfers between devices  67.2 us (30%)
  Pallas kernels  48 us (21%)
  local copies, waits for them, and re-layouts  18.9 us (8%)
  other arithmetic  2.83 us (1%)
    ppermute x22, waiting for transfers between devices, over(): return lax.ppermute(x, 'head', perm)  21 us
    pallas_call x11, Pallas kernels, whole(): pl.pallas_call(kernel, in_specs=[SCALAR if a is tokens else full for a in...  19.2 us
    ppermute x3, waiting for transfers between devices, swap(): lax.ppermute(part, 'ctx', pair_perm(count, -s))  17.3 us
    unnamed x66, local copies, waits for them, and re-layouts  16.3 us
    pallas_call x5, Pallas kernels, product(): pl.pallas_call(functools.partial(product_kernel, [len(x) for x in lots],...  16.2 us
    ppermute x22, starting transfers between devices, over(): return lax.ppermute(x, 'head', perm)  13 us
    pallas_call x2, Pallas kernels, outer(): pl.pallas_call(functools.partial(outer_kernel, 1 + len(flat), own, split)...  12.7 us
    ppermute x6, starting transfers between devices, ring(): return lax.ppermute(x, 'ctx', ring_perm(count, 1))  11.9 us
  transfers between devices with their start and end apart: 47, of which 27 were waited for; matrix products, arithmetic and copies ran while one was open for 1% of the time, Pallas kernels for 16%

profile of v10, /device:TPU:0, one launch (start us, length us, event | category | flops | bytes accessed | tf_op | source)
XLA Modules:
  0.0 224.2 jit_solution(15119142731015102952)
XLA Ops:
  0.7 2.5 %constant_dynamic-slice_fusion = (bf16[96,3072]{1,0:T(8,128)(2,1)}, bf16[96,3072]{1,0:T(8,128)(2,1)}) fusion(bf16[384,6144]{1,0:T(8,128)(2,1)} %refs_4_.3, s32[]{:T(128)S(6)} %select_n.84), kind=kLoop, calls=%fused_computation.46 | loop fusion | bytes 2359300 | tf_op jit(solution)/shard_map/dynamic_slice | solution.py:389
  3.2 3.0 %collective-permute-start = (bf16[96,3072]{1,0:T(8,128)(2,1)}, bf16[96,3072]{1,0:T(8,128)(2,1)}, u32[]{:S(2)}, u32[]{:S(2)}) collective-permute-start(bf16[96,3072]{1,0:T(8,128)(2,1)} %get-tuple-element.228), channel_id=1, source_target_pairs={{0,8},{4,12},{8,24},{12,28},{24,16},{28,20},{16,0},{20,4},{1,9},{5... | collective-permute-start | bytes 1769480 | tf_op jit(solution)/shard_map/ppermute | solution.py:411
  6.2 2.6 %states.1 = (bf16[8,144,128]{2,1,0:T(8,128)(2,1)}, f32[8,384]{1,0:T(8,128)S(1)}, f32[384,8]{1,0:T(8,128)S(1)}) custom-call(f32[8,384]{1,0:T(8,128)S(1)} %copy-done.28, bf16[384,1024]{1,0:T(8,128)(2,1)S(1)} %copy-done.3, bf16[384,1024]{1,0:T(8,128)(2,1)S(1)} %copy-done.4), custom_call_target="tpu_custom_call" | custom-call | flops 1000 | bytes 1000 | tf_op jit(solution)/shard_map/states/pallas_call | solution.py:400
  8.8 4.8 %all-to-all-start = ((bf16[8,144,128]{2,1,0:T(8,128)(2,1)}), bf16[8,144,128]{2,1,0:T(8,128)(2,1)S(1)}, u32[]{:S(2)}, u32[]{:S(2)}) async-start(bf16[8,144,128]{2,1,0:T(8,128)(2,1)} %get-tuple-element.116), calls=%async_computation | async-start | bytes 589824 | tf_op jit(solution)/shard_map/all_to_all | solution.py:433
  13.6 2.0 collective-permute-start.1
  15.6 1.9 weights.1.intra_ref
  18.6 9.3 %all-to-all-done.in_ref = bf16[8,144,128]{2,1,0:T(8,128)(2,1)S(1)} async-done(((bf16[8,144,128]{2,1,0:T(8,128)(2,1)}), bf16[8,144,128]{2,1,0:T(8,128)(2,1)S(1)}, u32[]{:S(2)}, u32[]{:S(2)}) %all-to-all-start) | async-done | bytes 294944 | tf_op jit(solution)/shard_map/all_to_all | solution.py:433
  27.9 1.9 collective-permute-start.2
  30.6 5.8 %all-to-all-start.1 = ((bf16[8,128,128]{2,1,0:T(8,128)(2,1)}), bf16[8,128,128]{2,1,0:T(8,128)(2,1)S(1)}, u32[]{:S(2)}, u32[]{:S(2)}) async-start(bf16[8,128,128]{2,1,0:T(8,128)(2,1)} %copy-done.11), calls=%async_computation.1 | async-start | bytes 524288 | tf_op jit(solution)/shard_map/all_to_all | solution.py:441
  36.4 2.2 fusion.order_ref
  38.6 3.5 %collective-permute-done.1.refs_5_ = bf16[96,3072]{1,0:T(8,128)(2,1)} collective-permute-done((bf16[96,3072]{1,0:T(8,128)(2,1)}, bf16[96,3072]{1,0:T(8,128)(2,1)}, u32[]{:S(2)}, u32[]{:S(2)}) %collective-permute-start.1) | collective-permute-done | bytes 589856 | tf_op jit(solution)/shard_map/ppermute | solution.py:411
  42.1 3.3 %all-to-all-done.1.state_ref = bf16[8,128,128]{2,1,0:T(8,128)(2,1)S(1)} async-done(((bf16[8,128,128]{2,1,0:T(8,128)(2,1)}), bf16[8,128,128]{2,1,0:T(8,128)(2,1)S(1)}, u32[]{:S(2)}, u32[]{:S(2)}) %all-to-all-start.1) | async-done | bytes 262176 | tf_op jit(solution)/shard_map/all_to_all | solution.py:441
  54.5 8.1 %collective-permute-done.9.refs_4_.refs_10_.refs_6_ = bf16[128,2048]{1,0:T(8,128)(2,1)S(1)} collective-permute-done((bf16[128,2048]{1,0:T(8,128)(2,1)S(1)}, bf16[128,2048]{1,0:T(8,128)(2,1)S(1)}, u32[]{:S(2)}, u32[]{:S(2)}) %collective-permute-start.9) | collective-permute-done | bytes 524320 | tf_op jit(solution)/shard_map/ppermute | solution.py:450
  64.7 3.0 %collective-permute-start.10 = (bf16[96,3072]{1,0:T(8,128)(2,1)}, bf16[96,3072]{1,0:T(8,128)(2,1)S(1)}, u32[]{:S(2)}, u32[]{:S(2)}) collective-permute-start(bf16[96,3072]{1,0:T(8,128)(2,1)} %collective-permute-done.1.refs_5_), channel_id=1, source_target_pairs={{0,8},{4,12},{8,24},{12,28},{24,16},{28,20},{16,0},{20,4},{1,9},{5... | collective-permute-start | bytes 1769480 | tf_op jit(solution)/shard_map/ppermute | solution.py:411
  72.0 9.2 %collective-permute-done.14.refs_5_.refs_11_.refs_7_.refs_6_ = bf16[128,2048]{1,0:T(8,128)(2,1)S(1)} collective-permute-done((bf16[128,2048]{1,0:T(8,128)(2,1)S(1)}, bf16[128,2048]{1,0:T(8,128)(2,1)S(1)}, u32[]{:S(2)}, u32[]{:S(2)}) %collective-permute-start.14) | collective-permute-done | bytes 524320 | tf_op jit(solution)/shard_map/ppermute | solution.py:450
  82.4 1.8 collective-permute-start.15
  85.7 1.7 collective-permute-start.19
  87.5 9.7 %collective-permute-done.16.refs_7_.refs_11_ = bf16[96,3072]{1,0:T(8,128)(2,1)S(1)} collective-permute-done((bf16[96,3072]{1,0:T(8,128)(2,1)S(1)}, bf16[96,3072]{1,0:T(8,128)(2,1)S(1)}, u32[]{:S(2)}, u32[]{:S(2)}) %collective-permute-start.16) | collective-permute-done | bytes 589856 | tf_op jit(solution)/shard_map/ppermute | solution.py:414
  97.1 2.4 %collective-permute-done.15.refs_1_.refs_13_ = bf16[96,3072]{1,0:T(8,128)(2,1)S(1)} collective-permute-done((bf16[96,3072]{1,0:T(8,128)(2,1)S(1)}, bf16[96,3072]{1,0:T(8,128)(2,1)S(1)}, u32[]{:S(2)}, u32[]{:S(2)}) %collective-permute-start.15) | collective-permute-done | bytes 589856 | tf_op jit(solution)/shard_map/ppermute | solution.py:411
  99.6 3.0 %collective-permute-done.19.refs_1_ = bf16[384,256]{1,0:T(8,128)(2,1)S(1)} collective-permute-done((bf16[384,256]{1,0:T(8,128)(2,1)S(1)}, bf16[384,256]{1,0:T(8,128)(2,1)S(1)}, u32[]{:S(2)}, u32[]{:S(2)}) %collective-permute-start.19) | collective-permute-done | bytes 196640 | tf_op jit(solution)/shard_map/ppermute | solution.py:479
  105.4 2.0 collective-permute-start.25
  107.5 3.7 %product.5.refs_0_ = bf16[384,256]{1,0:T(8,128)(2,1)S(1)} custom-call(s32[1]{0:T(128)} %bitcast.1.mine_ref.refs_0_, bf16[384,6144]{1,0:T(8,128)(2,1)S(1)} %bitcast.6, bf16[384,6144]{1,0:T(8,128)(2,1)S(1)} %bitcast.6, bf16[128,6144]{1,0:T(8,128)(2,1)S(1)} %bitcast.8, bf16[128,2048]{1,0:T(8,128)(2,1)S(1)} %collective-permute-done.9.refs_4_.refs_10_.refs_6_, ...), custom_call_target="tpu_custom_call" | custom-call | flops 1000 | bytes 1000 | tf_op jit(solution)/shard_map/product/pallas_call | solution.py:216
  111.1 5.2 %product.6 = bf16[384,256]{1,0:T(8,128)(2,1)S(1)} custom-call(s32[1]{0:T(128)} %bitcast.1.mine_ref.refs_0_, bf16[96,3072]{1,0:T(8,128)(2,1)} %collective-permute-done.refs_1_.refs_5_, bf16[96,3072]{1,0:T(8,128)(2,1)S(1)} %collective-permute-done.4.refs_2_.refs_6_, bf16[96,3072]{1,0:T(8,128)(2,1)} %collective-permute-done.2.refs_3_.refs_7_, ...), custom_call_target="tpu_custom_call" | custom-call | flops 1000 | bytes 1000 | tf_op jit(solution)/shard_map/product/pallas_call | solution.py:216
  116.3 2.0 collective-permute-done.22.refs_3_.refs_15_
  118.3 2.5 %collective-permute-done.21.refs_1_.refs_13_ = bf16[96,3072]{1,0:T(8,128)(2,1)S(1)} collective-permute-done((bf16[96,3072]{1,0:T(8,128)(2,1)S(1)}, bf16[96,3072]{1,0:T(8,128)(2,1)S(1)}, u32[]{:S(2)}, u32[]{:S(2)}) %collective-permute-start.21) | collective-permute-done | bytes 589856 | tf_op jit(solution)/shard_map/ppermute | solution.py:411
  120.9 3.7 %collective-permute-done.25.refs_3_ = bf16[384,256]{1,0:T(8,128)(2,1)S(1)} collective-permute-done((bf16[384,256]{1,0:T(8,128)(2,1)S(1)}, bf16[384,256]{1,0:T(8,128)(2,1)S(1)}, u32[]{:S(2)}, u32[]{:S(2)}) %collective-permute-start.25) | collective-permute-done | bytes 196640 | tf_op jit(solution)/shard_map/ppermute | solution.py:484
  125.7 3.3 %collective-permute-start.29 = (bf16[384,256]{1,0:T(8,128)(2,1)S(1)}, bf16[384,256]{1,0:T(8,128)(2,1)S(1)}, u32[]{:S(2)}, u32[]{:S(2)}) collective-permute-start(bf16[384,256]{1,0:T(8,128)(2,1)S(1)} %get-tuple-element.166), channel_id=1, source_target_pairs={{0,24},{4,28},{8,16},{12,20},{24,0},{28,4},{16,8},{20,12},{1,25},{... | collective-permute-start | bytes 589832 | tf_op jit(solution)/shard_map/ppermute | solution.py:494
  129.0 3.8 %product.8 = bf16[384,256]{1,0:T(8,128)(2,1)S(1)} custom-call(s32[1]{0:T(128)} %bitcast.1.mine_ref.refs_0_, bf16[96,3072]{1,0:T(8,128)(2,1)S(1)} %collective-permute-done.6.refs_1_.refs_9_, bf16[96,3072]{1,0:T(8,128)(2,1)S(1)} %collective-permute-done.17.refs_2_.refs_10_, bf16[96,3072]{1,0:T(8,128)(2,1)S(1)} %collective-permute-done.11.refs_3_.refs_11_, ...), custom_call_target="tpu_custom_call" | custom-call | flops 1000 | bytes 1000 | tf_op jit(solution)/shard_map/product/pallas_call | solution.py:216
  132.8 1.7 product.7.refs_8_
  135.4 3.0 %collective-permute-done.30.refs_1_ = bf16[384,256]{1,0:T(8,128)(2,1)S(1)} collective-permute-done((bf16[384,256]{1,0:T(8,128)(2,1)S(1)}, bf16[384,256]{1,0:T(8,128)(2,1)S(1)}, u32[]{:S(2)}, u32[]{:S(2)}) %collective-permute-start.30) | collective-permute-done | bytes 196640 | tf_op jit(solution)/shard_map/ppermute | solution.py:495
  138.4 2.0 collective-permute-done.26.refs_3_.refs_15_
  143.2 1.7 product.9
  144.9 6.6 %outer.2 = (bf16[128,3072]{1,0:T(8,128)(2,1)S(1)}, bf16[128,3072]{1,0:T(8,128)(2,1)}) custom-call(bf16[384,256]{1,0:T(8,128)(2,1)S(1)} %get-tuple-element.185.refs_0_, bf16[384,256]{1,0:T(8,128)(2,1)S(1)} %collective-permute-done.19.refs_1_, bf16[384,256]{1,0:T(8,128)(2,1)S(1)} %collective-permute-done.29.refs_2_, ...), custom_call_target="tpu_custom_call" | custom-call | flops 1000 | bytes 1000 | tf_op jit(solution)/shard_map/outer/pallas_call | solution.py:272
  153.9 2.4 %collective-permute-start.31 = (bf16[384,256]{1,0:T(8,128)(2,1)S(1)}, bf16[384,256]{1,0:T(8,128)(2,1)S(1)}, u32[]{:S(2)}, u32[]{:S(2)}) collective-permute-start(bf16[384,256]{1,0:T(8,128)(2,1)S(1)} %product.8), channel_id=1, source_target_pairs={{0,24},{4,28},{8,16},{12,20},{24,0},{28,4},{16,8},{20,12},{1,25},{... | collective-permute-start | bytes 589832 | tf_op jit(solution)/shard_map/ppermute | solution.py:501
  156.3 6.1 %outer.3 = (bf16[128,1536]{1,0:T(8,128)(2,1)S(1)}, bf16[128,1536]{1,0:T(8,128)(2,1)S(1)}, bf16[128,1536]{1,0:T(8,128)(2,1)S(1)}, bf16[128,1536]{1,0:T(8,128)(2,1)S(1)}) custom-call(bf16[384,256]{1,0:T(8,128)(2,1)S(1)} %get-tuple-element.185.refs_0_, bf16[384,256]{1,0:T(8,128)(2,1)S(1)} %collective-permute-done.19.refs_1_, ...), custom_call_target="tpu_custom_call" | custom-call | flops 1000 | bytes 1000 | tf_op jit(solution)/shard_map/outer/pallas_call | solution.py:272
  163.5 5.6 %collective-permute-done.34.refs_3_ = bf16[384,256]{1,0:T(8,128)(2,1)S(1)} collective-permute-done((bf16[384,256]{1,0:T(8,128)(2,1)S(1)}, bf16[384,256]{1,0:T(8,128)(2,1)S(1)}, u32[]{:S(2)}, u32[]{:S(2)}) %collective-permute-start.34) | collective-permute-done | bytes 196640 | tf_op jit(solution)/shard_map/ppermute | solution.py:511
  173.0 2.2 collective-permute-done.36.there_ref
  178.3 3.6 %all-to-all-start.2 = ((bf16[8,144,128]{2,1,0:T(8,128)(2,1)}), bf16[8,144,128]{2,1,0:T(8,128)(2,1)S(1)}, u32[]{:S(2)}, u32[]{:S(2)}) async-start(bf16[8,144,128]{2,1,0:T(8,128)(2,1)} %copy-done.26), calls=%async_computation.2 | async-start | bytes 589824 | tf_op jit(solution)/shard_map/all_to_all | solution.py:532
  181.9 1.7 collective-permute-start.38
  185.2 4.5 %inside.1 = (bf16[384,1024]{1,0:T(8,128)(2,1)}, bf16[384,1024]{1,0:T(8,128)(2,1)S(1)}, bf16[384,1024]{1,0:T(8,128)(2,1)S(1)}) custom-call(bf16[384,1024]{1,0:T(8,128)(2,1)S(1)} %copy-done.19, bf16[384,1024]{1,0:T(8,128)(2,1)S(1)} %copy-done.8, bf16[384,1024]{1,0:T(8,128)(2,1)S(1)} %copy-done.3, bf16[384,1024]{1,0:T(8,128)(2,1)S(1)} %copy-done.5, ...), custom_call_target="tpu_custom_call" | custom-call | flops 1000 | bytes 1000 | tf_op jit(solution)/shard_map/inside/pallas_call | solution.py:400
  191.4 3.7 %collective-permute-done.39 = f32[1,1024]{1,0:T(1,128)S(1)} collective-permute-done((f32[1,1024]{1,0:T(1,128)S(1)}, f32[1,1024]{1,0:T(1,128)S(1)}, u32[]{:S(2)}, u32[]{:S(2)}) %collective-permute-start.39) | collective-permute-done | bytes 4128 | tf_op jit(solution)/shard_map/ppermute | solution.py:541
  196.7 4.6 %all-to-all-start.3 = ((bf16[8,128,128]{2,1,0:T(8,128)(2,1)}), bf16[8,128,128]{2,1,0:T(8,128)(2,1)S(1)}, u32[]{:S(2)}, u32[]{:S(2)}) async-start(bf16[8,128,128]{2,1,0:T(8,128)(2,1)} %scan.3), calls=%async_computation.3 | async-start | bytes 524288 | tf_op jit(solution)/shard_map/all_to_all | solution.py:552
  201.2 2.0 collective-permute-start.40
  204.7 2.1 collective-permute-done.41
  206.9 2.8 %collective-permute-start.42 = (f32[1,1024]{1,0:T(1,128)S(1)}, f32[1,1024]{1,0:T(1,128)S(1)}, u32[]{:S(2)}, u32[]{:S(2)}) collective-permute-start(f32[1,1024]{1,0:T(1,128)S(1)} %add.143), channel_id=1, source_target_pairs={{0,16},{4,20},{8,24},{12,28},{16,0},{20,4},{24,8},{28,12},{1,17},{... | collective-permute-start | bytes 12296 | tf_op jit(solution)/shard_map/ppermute | solution.py:554
  212.0 2.2 collective-permute-done.40.refs_5_
  218.3 2.7 %sum.1 = bf16[128,6144]{1,0:T(8,128)(2,1)} custom-call(bf16[128,3072]{1,0:T(8,128)(2,1)S(1)} %copy-done.13, bf16[128,3072]{1,0:T(8,128)(2,1)} %collective-permute-done.37.refs_1_, bf16[128,1536]{1,0:T(8,128)(2,1)S(1)} %copy-done.21, bf16[128,1536]{1,0:T(8,128)(2,1)S(1)} %copy-done.25, bf16[128,1536]{1,0:T(8,128)(2,1)S(1)} %copy-done.23, ...), custom_call_target="tpu_custom_call" | custom-call | flops 1000 | bytes 1000 | tf_op jit(solution)/shard_map/sum/pallas_call | solution.py:400
  222.2 2.1 outside.1
  (140 shorter events, 52.0 us)
Async XLA Ops:
  3.2 24.8 %collective-permute-start = (bf16[96,3072]{1,0:T(8,128)(2,1)}, bf16[96,3072]{1,0:T(8,128)(2,1)}, u32[]{:S(2)}, u32[]{:S(2)}) collective-permute-start(bf16[96,3072]{1,0:T(8,128)(2,1)} %get-tuple-element.228), channel_id=1, source_target_pairs={{0,8},{4,12},{8,24},{12,28},{24,16},{28,20},{16,0},{20,4},{1,9},{5... | collective-permute-start | bytes 1769480 | tf_op jit(solution)/shard_map/ppermute | solution.py:411
  8.8 19.2 %all-to-all-start = ((bf16[8,144,128]{2,1,0:T(8,128)(2,1)}), bf16[8,144,128]{2,1,0:T(8,128)(2,1)S(1)}, u32[]{:S(2)}, u32[]{:S(2)}) async-start(bf16[8,144,128]{2,1,0:T(8,128)(2,1)} %get-tuple-element.116), calls=%async_computation | async-start | bytes 589824 | tf_op jit(solution)/shard_map/all_to_all | solution.py:433
  13.6 28.5 %collective-permute-start.1 = (bf16[96,3072]{1,0:T(8,128)(2,1)}, bf16[96,3072]{1,0:T(8,128)(2,1)}, u32[]{:S(2)}, u32[]{:S(2)}) collective-permute-start(bf16[96,3072]{1,0:T(8,128)(2,1)} %get-tuple-element.120), channel_id=1, source_target_pairs={{0,8},{4,12},{8,24},{12,28},{24,16},{28,20},{16,0},{20,4},{1,9},{5... | collective-permute-start | bytes 1769480 | tf_op jit(solution)/shard_map/ppermute | solution.py:411
  15.6 91.9 %slice-start = ((s8[4718592]{0:T(1024)(128)(4,1)}), s8[524288]{0:T(1024)(128)(4,1)S(1)}, s32[]{:S(2)}) async-start(s8[4718592]{0:T(1024)(128)(4,1)} %bitcast.5), calls=%async_computation.4 | async-start | bytes 1048576
  27.9 17.4 %collective-permute-start.2 = (bf16[96,3072]{1,0:T(8,128)(2,1)}, bf16[96,3072]{1,0:T(8,128)(2,1)}, u32[]{:S(2)}, u32[]{:S(2)}) collective-permute-start(bf16[96,3072]{1,0:T(8,128)(2,1)} %collective-permute-done.refs_1_.refs_5_), channel_id=1, source_target_pairs={{0,2},{1,3},{2,0},{3,1},{4,6},{5,7},{6,4},{7,5},{8,10},{9,11},{10,... | collective-permute-start | bytes 1769480 | tf_op jit(solution)/shard_map/ppermute | solution.py:414
  30.6 14.8 %all-to-all-start.1 = ((bf16[8,128,128]{2,1,0:T(8,128)(2,1)}), bf16[8,128,128]{2,1,0:T(8,128)(2,1)S(1)}, u32[]{:S(2)}, u32[]{:S(2)}) async-start(bf16[8,128,128]{2,1,0:T(8,128)(2,1)} %copy-done.11), calls=%async_computation.1 | async-start | bytes 524288 | tf_op jit(solution)/shard_map/all_to_all | solution.py:441
  45.4 17.3 %collective-permute-start.6 = (bf16[96,3072]{1,0:T(8,128)(2,1)}, bf16[96,3072]{1,0:T(8,128)(2,1)S(1)}, u32[]{:S(2)}, u32[]{:S(2)}) collective-permute-start(bf16[96,3072]{1,0:T(8,128)(2,1)} %collective-permute-done.refs_1_.refs_5_), channel_id=1, source_target_pairs={{0,8},{4,12},{8,24},{12,28},{24,16},{28,20},{16,0},{20,4},{1,9},{5... | collective-permute-start | bytes 1769480 | tf_op jit(solution)/shard_map/ppermute | solution.py:411
  46.6 3.7 %collective-permute-start.4 = (bf16[96,3072]{1,0:T(8,128)(2,1)}, bf16[96,3072]{1,0:T(8,128)(2,1)S(1)}, u32[]{:S(2)}, u32[]{:S(2)}) collective-permute-start(bf16[96,3072]{1,0:T(8,128)(2,1)} %collective-permute-done.refs_1_.refs_5_), channel_id=1, source_target_pairs={{0,1},{1,0},{2,3},{3,2},{4,5},{5,4},{6,7},{7,6},{8,9},{9,8},{10,11... | collective-permute-start | bytes 1769480 | tf_op jit(solution)/shard_map/ppermute | solution.py:414
  46.6 16.0 %collective-permute-start.7 = (bf16[96,3072]{1,0:T(8,128)(2,1)}, bf16[96,3072]{1,0:T(8,128)(2,1)S(1)}, u32[]{:S(2)}, u32[]{:S(2)}) collective-permute-start(bf16[96,3072]{1,0:T(8,128)(2,1)} %collective-permute-done.1.refs_5_), channel_id=1, source_target_pairs={{0,2},{1,3},{2,0},{3,1},{4,6},{5,7},{6,4},{7,5},{8,10},{9,11},{10,... | collective-permute-start | bytes 1769480 | tf_op jit(solution)/shard_map/ppermute | solution.py:414
  48.1 2.2 collective-permute-start.3
  48.5 14.2 %collective-permute-start.9 = (bf16[128,2048]{1,0:T(8,128)(2,1)S(1)}, bf16[128,2048]{1,0:T(8,128)(2,1)S(1)}, u32[]{:S(2)}, u32[]{:S(2)}) collective-permute-start(bf16[128,2048]{1,0:T(8,128)(2,1)S(1)} %get-tuple-element.231), channel_id=1, source_target_pairs={{0,4},{4,0},{8,12},{12,8},{16,20},{20,16},{24,28},{28,24},{1,5},{5... | collective-permute-start | bytes 1572872 | tf_op jit(solution)/shard_map/ppermute | solution.py:450
  52.5 1.2 collective-permute-start.5
  53.7 9.0 %collective-permute-start.8 = (f32[1,384]{1,0:T(1,128)S(1)}, f32[1,384]{1,0:T(1,128)S(1)}, u32[]{:S(2)}, u32[]{:S(2)}) collective-permute-start(f32[1,384]{1,0:T(1,128)S(1)} %add.140.here_ref), channel_id=1, source_target_pairs={{0,2},{1,3},{2,0},{3,1},{4,6},{5,7},{6,4},{7,5},{8,10},{9,11},{10,... | collective-permute-start | bytes 4616 | tf_op jit(solution)/shard_map/ppermute | solution.py:414
  62.7 18.6 %collective-permute-start.11 = (bf16[96,3072]{1,0:T(8,128)(2,1)S(1)}, bf16[96,3072]{1,0:T(8,128)(2,1)S(1)}, u32[]{:S(2)}, u32[]{:S(2)}) collective-permute-start(bf16[96,3072]{1,0:T(8,128)(2,1)S(1)} %collective-permute-done.6.refs_1_.refs_9_), channel_id=1, source_target_pairs={{0,2},{1,3},{2,0},{3,1},{4,6},{5,7},{6,4},{7,5},{8,10},{9,11},{10,... | collective-permute-start | bytes 1769480 | tf_op jit(solution)/shard_map/ppermute | solution.py:414
  64.1 17.1 %collective-permute-start.13 = (bf16[96,3072]{1,0:T(8,128)(2,1)S(1)}, bf16[96,3072]{1,0:T(8,128)(2,1)S(1)}, u32[]{:S(2)}, u32[]{:S(2)}) collective-permute-start(bf16[96,3072]{1,0:T(8,128)(2,1)S(1)} %collective-permute-done.7.refs_7_), channel_id=1, source_target_pairs={{0,1},{1,0},{2,3},{3,2},{4,5},{5,4},{6,7},{7,6},{8,9},{9,8},{10,11... | collective-permute-start | bytes 1769480 | tf_op jit(solution)/shard_map/ppermute | solution.py:414
  64.1 17.1 %collective-permute-start.12 = (bf16[96,3072]{1,0:T(8,128)(2,1)}, bf16[96,3072]{1,0:T(8,128)(2,1)S(1)}, u32[]{:S(2)}, u32[]{:S(2)}) collective-permute-start(bf16[96,3072]{1,0:T(8,128)(2,1)} %collective-permute-done.1.refs_5_), channel_id=1, source_target_pairs={{0,1},{1,0},{2,3},{3,2},{4,5},{5,4},{6,7},{7,6},{8,9},{9,8},{10,11... | collective-permute-start | bytes 1769480 | tf_op jit(solution)/shard_map/ppermute | solution.py:414
  64.7 16.6 %collective-permute-start.10 = (bf16[96,3072]{1,0:T(8,128)(2,1)}, bf16[96,3072]{1,0:T(8,128)(2,1)S(1)}, u32[]{:S(2)}, u32[]{:S(2)}) collective-permute-start(bf16[96,3072]{1,0:T(8,128)(2,1)} %collective-permute-done.1.refs_5_), channel_id=1, source_target_pairs={{0,8},{4,12},{8,24},{12,28},{24,16},{28,20},{16,0},{20,4},{1,9},{5... | collective-permute-start | bytes 1769480 | tf_op jit(solution)/shard_map/ppermute | solution.py:411
  67.7 13.6 %collective-permute-start.14 = (bf16[128,2048]{1,0:T(8,128)(2,1)S(1)}, bf16[128,2048]{1,0:T(8,128)(2,1)S(1)}, u32[]{:S(2)}, u32[]{:S(2)}) collective-permute-start(bf16[128,2048]{1,0:T(8,128)(2,1)S(1)} %get-tuple-element.141), channel_id=1, source_target_pairs={{0,4},{4,0},{8,12},{12,8},{16,20},{20,16},{24,28},{28,24},{1,5},{5... | collective-permute-start | bytes 1572872 | tf_op jit(solution)/shard_map/ppermute | solution.py:450
  81.3 3.0 %collective-permute-start.18 = (bf16[96,3072]{1,0:T(8,128)(2,1)S(1)}, bf16[96,3072]{1,0:T(8,128)(2,1)S(1)}, u32[]{:S(2)}, u32[]{:S(2)}) collective-permute-start(bf16[96,3072]{1,0:T(8,128)(2,1)S(1)} %collective-permute-done.11.refs_3_.refs_11_), channel_id=1, source_target_pairs={{0,1},{1,0},{2,3},{3,2},{4,5},{5,4},{6,7},{7,6},{8,9},{9,8},{10,11... | collective-permute-start | bytes 1769480 | tf_op jit(solution)/shard_map/ppermute | solution.py:414
  81.3 2.9 %collective-permute-start.17 = (bf16[96,3072]{1,0:T(8,128)(2,1)S(1)}, bf16[96,3072]{1,0:T(8,128)(2,1)S(1)}, u32[]{:S(2)}, u32[]{:S(2)}) collective-permute-start(bf16[96,3072]{1,0:T(8,128)(2,1)S(1)} %collective-permute-done.6.refs_1_.refs_9_), channel_id=1, source_target_pairs={{0,1},{1,0},{2,3},{3,2},{4,5},{5,4},{6,7},{7,6},{8,9},{9,8},{10,11... | collective-permute-start | bytes 1769480 | tf_op jit(solution)/shard_map/ppermute | solution.py:414
  81.8 15.3 %collective-permute-start.16 = (bf16[96,3072]{1,0:T(8,128)(2,1)S(1)}, bf16[96,3072]{1,0:T(8,128)(2,1)S(1)}, u32[]{:S(2)}, u32[]{:S(2)}) collective-permute-start(bf16[96,3072]{1,0:T(8,128)(2,1)S(1)} %collective-permute-done.10.refs_5_.refs_9_), channel_id=1, source_target_pairs={{0,2},{1,3},{2,0},{3,1},{4,6},{5,7},{6,4},{7,5},{8,10},{9,11},{10,... | collective-permute-start | bytes 1769480 | tf_op jit(solution)/shard_map/ppermute | solution.py:414
  82.4 17.1 %collective-permute-start.15 = (bf16[96,3072]{1,0:T(8,128)(2,1)S(1)}, bf16[96,3072]{1,0:T(8,128)(2,1)S(1)}, u32[]{:S(2)}, u32[]{:S(2)}) collective-permute-start(bf16[96,3072]{1,0:T(8,128)(2,1)S(1)} %collective-permute-done.6.refs_1_.refs_9_), channel_id=1, source_target_pairs={{0,8},{4,12},{8,24},{12,28},{24,16},{28,20},{16,0},{20,4},{1,9},{5... | collective-permute-start | bytes 1769480 | tf_op jit(solution)/shard_map/ppermute | solution.py:411
  84.2 18.3 %collective-permute-start.20 = (bf16[128,2048]{1,0:T(8,128)(2,1)S(1)}, bf16[128,2048]{1,0:T(8,128)(2,1)S(1)}, u32[]{:S(2)}, u32[]{:S(2)}) collective-permute-start(bf16[128,2048]{1,0:T(8,128)(2,1)S(1)} %get-tuple-element.149), channel_id=1, source_target_pairs={{0,4},{4,0},{8,12},{12,8},{16,20},{20,16},{24,28},{28,24},{1,5},{5... | collective-permute-start | bytes 1572872 | tf_op jit(solution)/shard_map/ppermute | solution.py:450
  85.7 16.8 %collective-permute-start.19 = (bf16[384,256]{1,0:T(8,128)(2,1)S(1)}, bf16[384,256]{1,0:T(8,128)(2,1)S(1)}, u32[]{:S(2)}, u32[]{:S(2)}) collective-permute-start(bf16[384,256]{1,0:T(8,128)(2,1)S(1)} %get-tuple-element.148), channel_id=1, source_target_pairs={{0,8},{4,12},{8,24},{12,28},{24,16},{28,20},{16,0},{20,4},{1,9},{5... | collective-permute-start | bytes 589832 | tf_op jit(solution)/shard_map/ppermute | solution.py:479
  102.6 2.8 %collective-permute-start.24 = (bf16[96,3072]{1,0:T(8,128)(2,1)S(1)}, bf16[96,3072]{1,0:T(8,128)(2,1)S(1)}, u32[]{:S(2)}, u32[]{:S(2)}) collective-permute-start(bf16[96,3072]{1,0:T(8,128)(2,1)S(1)} %collective-permute-done.16.refs_7_.refs_11_), channel_id=1, source_target_pairs={{0,1},{1,0},{2,3},{3,2},{4,5},{5,4},{6,7},{7,6},{8,9},{9,8},{10,11... | collective-permute-start | bytes 1769480 | tf_op jit(solution)/shard_map/ppermute | solution.py:414
  102.6 2.8 %collective-permute-start.23 = (bf16[96,3072]{1,0:T(8,128)(2,1)S(1)}, bf16[96,3072]{1,0:T(8,128)(2,1)S(1)}, u32[]{:S(2)}, u32[]{:S(2)}) collective-permute-start(bf16[96,3072]{1,0:T(8,128)(2,1)S(1)} %collective-permute-done.10.refs_5_.refs_9_), channel_id=1, source_target_pairs={{0,1},{1,0},{2,3},{3,2},{4,5},{5,4},{6,7},{7,6},{8,9},{9,8},{10,11... | collective-permute-start | bytes 1769480 | tf_op jit(solution)/shard_map/ppermute | solution.py:414
  103.1 15.2 %collective-permute-start.22 = (bf16[96,3072]{1,0:T(8,128)(2,1)S(1)}, bf16[96,3072]{1,0:T(8,128)(2,1)S(1)}, u32[]{:S(2)}, u32[]{:S(2)}) collective-permute-start(bf16[96,3072]{1,0:T(8,128)(2,1)S(1)} %collective-permute-done.15.refs_1_.refs_13_), channel_id=1, source_target_pairs={{0,2},{1,3},{2,0},{3,1},{4,6},{5,7},{6,4},{7,5},{8,10},{9,11},{10,... | collective-permute-start | bytes 1769480 | tf_op jit(solution)/shard_map/ppermute | solution.py:414
  104.5 16.3 %collective-permute-start.21 = (bf16[96,3072]{1,0:T(8,128)(2,1)S(1)}, bf16[96,3072]{1,0:T(8,128)(2,1)S(1)}, u32[]{:S(2)}, u32[]{:S(2)}) collective-permute-start(bf16[96,3072]{1,0:T(8,128)(2,1)S(1)} %collective-permute-done.10.refs_5_.refs_9_), channel_id=1, source_target_pairs={{0,8},{4,12},{8,24},{12,28},{24,16},{28,20},{16,0},{20,4},{1,9},{5... | collective-permute-start | bytes 1769480 | tf_op jit(solution)/shard_map/ppermute | solution.py:411
  105.4 19.2 %collective-permute-start.25 = (bf16[384,256]{1,0:T(8,128)(2,1)S(1)}, bf16[384,256]{1,0:T(8,128)(2,1)S(1)}, u32[]{:S(2)}, u32[]{:S(2)}) collective-permute-start(bf16[384,256]{1,0:T(8,128)(2,1)S(1)} %get-tuple-element.154), channel_id=1, source_target_pairs={{0,16},{4,20},{8,0},{12,4},{24,8},{28,12},{16,24},{20,28},{1,17},{... | collective-permute-start | bytes 589832 | tf_op jit(solution)/shard_map/ppermute | solution.py:484
  124.6 8.2 %collective-permute-start.27 = (bf16[96,3072]{1,0:T(8,128)(2,1)S(1)}, bf16[96,3072]{1,0:T(8,128)(2,1)S(1)}, u32[]{:S(2)}, u32[]{:S(2)}) collective-permute-start(bf16[96,3072]{1,0:T(8,128)(2,1)S(1)} %collective-permute-done.15.refs_1_.refs_13_), channel_id=1, source_target_pairs={{0,1},{1,0},{2,3},{3,2},{4,5},{5,4},{6,7},{7,6},{8,9},{9,8},{10,11... | collective-permute-start | bytes 1769480 | tf_op jit(solution)/shard_map/ppermute | solution.py:414
  124.6 8.2 %collective-permute-start.28 = (bf16[96,3072]{1,0:T(8,128)(2,1)S(1)}, bf16[96,3072]{1,0:T(8,128)(2,1)S(1)}, u32[]{:S(2)}, u32[]{:S(2)}) collective-permute-start(bf16[96,3072]{1,0:T(8,128)(2,1)S(1)} %collective-permute-done.22.refs_3_.refs_15_), channel_id=1, source_target_pairs={{0,1},{1,0},{2,3},{3,2},{4,5},{5,4},{6,7},{7,6},{8,9},{9,8},{10,11... | collective-permute-start | bytes 1769480 | tf_op jit(solution)/shard_map/ppermute | solution.py:414
  125.1 15.2 %collective-permute-start.26 = (bf16[96,3072]{1,0:T(8,128)(2,1)S(1)}, bf16[96,3072]{1,0:T(8,128)(2,1)S(1)}, u32[]{:S(2)}, u32[]{:S(2)}) collective-permute-start(bf16[96,3072]{1,0:T(8,128)(2,1)S(1)} %collective-permute-done.21.refs_1_.refs_13_), channel_id=1, source_target_pairs={{0,2},{1,3},{2,0},{3,1},{4,6},{5,7},{6,4},{7,5},{8,10},{9,11},{10,... | collective-permute-start | bytes 1769480 | tf_op jit(solution)/shard_map/ppermute | solution.py:414
  125.7 9.7 %collective-permute-start.29 = (bf16[384,256]{1,0:T(8,128)(2,1)S(1)}, bf16[384,256]{1,0:T(8,128)(2,1)S(1)}, u32[]{:S(2)}, u32[]{:S(2)}) collective-permute-start(bf16[384,256]{1,0:T(8,128)(2,1)S(1)} %get-tuple-element.166), channel_id=1, source_target_pairs={{0,24},{4,28},{8,16},{12,20},{24,0},{28,4},{16,8},{20,12},{1,25},{... | collective-permute-start | bytes 589832 | tf_op jit(solution)/shard_map/ppermute | solution.py:494
  129.0 9.4 %collective-permute-start.30 = (bf16[384,256]{1,0:T(8,128)(2,1)S(1)}, bf16[384,256]{1,0:T(8,128)(2,1)S(1)}, u32[]{:S(2)}, u32[]{:S(2)}) collective-permute-start(bf16[384,256]{1,0:T(8,128)(2,1)S(1)} %product.6), channel_id=1, source_target_pairs={{0,16},{4,20},{8,0},{12,4},{24,8},{28,12},{16,24},{20,28},{1,17},{... | collective-permute-start | bytes 589832 | tf_op jit(solution)/shard_map/ppermute | solution.py:495
  140.3 2.0 collective-permute-start.33
  140.3 2.8 %collective-permute-start.32 = (bf16[96,3072]{1,0:T(8,128)(2,1)S(1)}, bf16[96,3072]{1,0:T(8,128)(2,1)S(1)}, u32[]{:S(2)}, u32[]{:S(2)}) collective-permute-start(bf16[96,3072]{1,0:T(8,128)(2,1)S(1)} %collective-permute-done.26.refs_3_.refs_15_), channel_id=1, source_target_pairs={{0,1},{1,0},{2,3},{3,2},{4,5},{5,4},{6,7},{7,6},{8,9},{9,8},{10,11... | collective-permute-start | bytes 1769480 | tf_op jit(solution)/shard_map/ppermute | solution.py:414
  152.4 43.5 %collective-permute-start.37 = (bf16[128,3072]{1,0:T(8,128)(2,1)}, bf16[128,3072]{1,0:T(8,128)(2,1)}, u32[]{:S(2)}, u32[]{:S(2)}) collective-permute-start(bf16[128,3072]{1,0:T(8,128)(2,1)} %get-tuple-element.207), channel_id=1, source_target_pairs={{0,4},{4,0},{8,12},{12,8},{16,20},{20,16},{24,28},{28,24},{1,5},{5... | collective-permute-start | bytes 2359304 | tf_op jit(solution)/shard_map/ppermute | solution.py:515
  153.9 9.6 %collective-permute-start.31 = (bf16[384,256]{1,0:T(8,128)(2,1)S(1)}, bf16[384,256]{1,0:T(8,128)(2,1)S(1)}, u32[]{:S(2)}, u32[]{:S(2)}) collective-permute-start(bf16[384,256]{1,0:T(8,128)(2,1)S(1)} %product.8), channel_id=1, source_target_pairs={{0,24},{4,28},{8,16},{12,20},{24,0},{28,4},{16,8},{20,12},{1,25},{... | collective-permute-start | bytes 589832 | tf_op jit(solution)/shard_map/ppermute | solution.py:501
  156.3 12.8 %collective-permute-start.34 = (bf16[384,256]{1,0:T(8,128)(2,1)S(1)}, bf16[384,256]{1,0:T(8,128)(2,1)S(1)}, u32[]{:S(2)}, u32[]{:S(2)}) collective-permute-start(bf16[384,256]{1,0:T(8,128)(2,1)S(1)} %product.9), channel_id=1, source_target_pairs={{0,8},{4,12},{8,24},{12,28},{24,16},{28,20},{16,0},{20,4},{1,9},{5... | collective-permute-start | bytes 589832 | tf_op jit(solution)/shard_map/ppermute | solution.py:511
  170.4 1.2 collective-permute-start.35
  171.6 3.6 %collective-permute-start.36 = (f32[1,384]{1,0:T(1,128)S(1)}, f32[1,384]{1,0:T(1,128)S(1)}, u32[]{:S(2)}, u32[]{:S(2)}) collective-permute-start(f32[1,384]{1,0:T(1,128)S(1)} %add.141.here_ref), channel_id=1, source_target_pairs={{0,2},{1,3},{2,0},{3,1},{4,6},{5,7},{6,4},{7,5},{8,10},{9,11},{10,... | collective-permute-start | bytes 4616 | tf_op jit(solution)/shard_map/ppermute | solution.py:414
  178.3 17.6 %all-to-all-start.2 = ((bf16[8,144,128]{2,1,0:T(8,128)(2,1)}), bf16[8,144,128]{2,1,0:T(8,128)(2,1)S(1)}, u32[]{:S(2)}, u32[]{:S(2)}) async-start(bf16[8,144,128]{2,1,0:T(8,128)(2,1)} %copy-done.26), calls=%async_computation.2 | async-start | bytes 589824 | tf_op jit(solution)/shard_map/all_to_all | solution.py:532
  181.9 13.2 %collective-permute-start.38 = (bf16[128,1536]{1,0:T(8,128)(2,1)}, bf16[128,1536]{1,0:T(8,128)(2,1)S(1)}, u32[]{:S(2)}, u32[]{:S(2)}) collective-permute-start(bf16[128,1536]{1,0:T(8,128)(2,1)} %copy-done.30), channel_id=1, source_target_pairs={{0,4},{4,0},{8,12},{12,8},{16,20},{20,16},{24,28},{28,24},{1,5},{5... | collective-permute-start | bytes 1179656 | tf_op jit(solution)/shard_map/ppermute | solution.py:538
  183.6 11.5 %collective-permute-start.39 = (f32[1,1024]{1,0:T(1,128)S(1)}, f32[1,1024]{1,0:T(1,128)S(1)}, u32[]{:S(2)}, u32[]{:S(2)}) collective-permute-start(f32[1,1024]{1,0:T(1,128)S(1)} %get-tuple-element.212), channel_id=1, source_target_pairs={{0,4},{4,0},{8,12},{12,8},{16,20},{20,16},{24,28},{28,24},{1,5},{5... | collective-permute-start | bytes 12296 | tf_op jit(solution)/shard_map/ppermute | solution.py:541
  196.7 24.4 %all-to-all-start.3 = ((bf16[8,128,128]{2,1,0:T(8,128)(2,1)}), bf16[8,128,128]{2,1,0:T(8,128)(2,1)S(1)}, u32[]{:S(2)}, u32[]{:S(2)}) async-start(bf16[8,128,128]{2,1,0:T(8,128)(2,1)} %scan.3), calls=%async_computation.3 | async-start | bytes 524288 | tf_op jit(solution)/shard_map/all_to_all | solution.py:552
  201.2 13.0 %collective-permute-start.40 = (bf16[128,1536]{1,0:T(8,128)(2,1)}, bf16[128,1536]{1,0:T(8,128)(2,1)S(1)}, u32[]{:S(2)}, u32[]{:S(2)}) collective-permute-start(bf16[128,1536]{1,0:T(8,128)(2,1)} %copy-done.29), channel_id=1, source_target_pairs={{0,4},{4,0},{8,12},{12,8},{16,20},{20,16},{24,28},{28,24},{1,5},{5... | collective-permute-start | bytes 1179656 | tf_op jit(solution)/shard_map/ppermute | solution.py:538
  203.3 3.6 %collective-permute-start.41 = (f32[1,1024]{1,0:T(1,128)S(1)}, f32[1,1024]{1,0:T(1,128)S(1)}, u32[]{:S(2)}, u32[]{:S(2)}) collective-permute-start(f32[1,1024]{1,0:T(1,128)S(1)} %add.142), channel_id=1, source_target_pairs={{0,8},{4,12},{8,0},{12,4},{16,24},{20,28},{24,16},{28,20},{1,9},{5... | collective-permute-start | bytes 12296 | tf_op jit(solution)/shard_map/ppermute | solution.py:554
  206.9 4.5 %collective-permute-start.42 = (f32[1,1024]{1,0:T(1,128)S(1)}, f32[1,1024]{1,0:T(1,128)S(1)}, u32[]{:S(2)}, u32[]{:S(2)}) collective-permute-start(f32[1,1024]{1,0:T(1,128)S(1)} %add.143), channel_id=1, source_target_pairs={{0,16},{4,20},{8,24},{12,28},{16,0},{20,4},{24,8},{28,12},{1,17},{... | collective-permute-start | bytes 12296 | tf_op jit(solution)/shard_map/ppermute | solution.py:554
  (32 other events, 243.0 us)

commit v11 on v9

--- a/solution.py
+++ b/solution.py
@@ -311,7 +311,7 @@
 
 
 def inside_kernel(
-    grad_ref, q_ref, k_ref, v_ref, run_ref, turned_ref, state_ref, gq_ref, gk_ref, gv_ref
+    grad_ref, q_ref, k_ref, v_ref, run_ref, turned_ref, state_ref, gq_ref, part_ref
 ):
     for head, at, run, _ in per_head(turned_ref):
         grad, query, key = grad_ref[:, at], q_ref[:, at], k_ref[:, at]
@@ -320,16 +320,16 @@
         weights = (dot(query, key, NT) * mask).astype(BF)
         gq = dot(masked, key, NN) + dot(grad, state_ref[head], NT) * jnp.exp(run)
         gq_ref[:, at] = gq.astype(BF)
-        gk_ref[:, at] = dot(masked, query, TN).astype(BF)
-        gv_ref[:, at] = dot(weights, grad, TN).astype(BF)
-
-
-def outside_kernel(k_ref, v_ref, state_ref, turned_ref, gk_in, gv_in, gk_ref, gv_ref):
+        part_ref[0, :, at] = dot(masked, query, TN).astype(BF)
+        part_ref[1, :, at] = dot(weights, grad, TN).astype(BF)
+
+
+def outside_kernel(k_ref, v_ref, state_ref, turned_ref, part_ref, gk_ref, gv_ref):
     for head, at, run, total in per_head(turned_ref):
         final = jnp.exp(total - run)
         state = state_ref[head]
-        gk_ref[:, at] = (gk_in[:, at] + dot(v_ref[:, at], state, NT) * final).astype(BF)
-        gv_ref[:, at] = (gv_in[:, at] + dot(k_ref[:, at], state, NN) * final).astype(BF)
+        gk_ref[:, at] = (part_ref[0, :, at] + dot(v_ref[:, at], state, NT) * final).astype(BF)
+        gv_ref[:, at] = (part_ref[1, :, at] + dot(k_ref[:, at], state, NN) * final).astype(BF)
 
 
 def feature_order(heads, size, count):
@@ -487,7 +487,7 @@
     returned.append(lax.ppermute(two, "ctx", ring_perm(count, -2)))
     last_lot = [ra3, na3, ya3, fa3]
     three = product(tokens, [last_lot], weight_own, others, 0, False, None)
-    yb3, three, normed[2], returned[1] = hold((yb3, three, normed[2], returned[1]))
+    yb3, three, normed[2], returned[1], _ = hold((yb3, three, normed[2], returned[1], two))
 
     fb3, nb3 = near_of(yb3), near_of(rb3)
     lots = [[ra1, na1, ya1, fa1], [ra2, na2, ya2, fa2], last_lot]
@@ -517,13 +517,11 @@
     gain_sum, late, grad_attn = hold((gain_sum, late, grad_attn))
     flips = [1 << i for i in range(count.bit_length() - 1)]
     gain_sum = gain_sum + lax.ppermute(gain_sum, "ctx", [(i, i ^ 1) for i in range(count)])
-    grad_query, gk_in, gv_in = whole(
-        inside_kernel, [wide_b] * 3, "inside",
+    grad_query, inside = whole(
+        inside_kernel, [wide_b, jax.ShapeDtypeStruct((2, tok, width), BF)], "inside",
         grad_attn, query_rows, key_rows, value_rows, run, turned, state_low,
     )
-    spread, flat, gk_in, gv_in, gain_sum, late = hold(
-        (spread, flat, gk_in, gv_in, gain_sum, late)
-    )
+    spread, flat, inside, gain_sum, late = hold((spread, flat, inside, gain_sum, late))
     flat.append(late[0])
     flat += [lax.ppermute(late[s], "ctx", pair_perm(count, s)) for s in range(1, minor)]
     states = whole(functools.partial(scan_kernel, True), scan_shape, "scan", spread)
@@ -535,7 +533,7 @@
     grad_gain = gain_sum.reshape(width)
     grad_key, grad_value = whole(
         outside_kernel, [wide_b] * 2, "outside",
-        key_rows, value_rows, back_low, turned, gk_in, gv_in,
+        key_rows, value_rows, back_low, turned, inside,
     )
     grad_weight = whole(
         functools.partial(final_kernel, CHUNKS, minor), jax.ShapeDtypeStruct((own, model), BF),

time: 213 us -> 210 us (0.986)
  waiting for transfers between devices: 81.4 us -> 77 us
    ppermute x1, waiting for transfers between devices: 6.7 us -> 2.74 us  [shards(): normed[2] = lax.ppermute(sent[2], 'ctx', ring_perm(count, 2))]
    unnamed x56 -> x52, local copies, waits for them, and re-layouts: 11.7 us -> 13.3 us
  transfers between devices with their start and end apart: 46 -> 46, of which waited for: 21 -> 22; matrix products, arithmetic and copies ran while one was open for 1% -> 1% of each run, Pallas kernels for 21% -> 21%
where the time goes in v11:
time: 210 us; the launch traced here: 209 us
  waiting for transfers between devices  77 us (37%)
  starting transfers between devices  64.9 us (31%)
  Pallas kernels  47.6 us (23%)
  local copies, waits for them, and re-layouts  15.9 us (8%)
  other arithmetic  2.83 us (1%)
    ppermute x3, waiting for transfers between devices, swap(): lax.ppermute(part, 'ctx', pair_perm(count, -s))  27.9 us
    pallas_call x11, Pallas kernels, whole(): pl.pallas_call(kernel, in_specs=[SCALAR if a is tokens else full for a in...  19.3 us
    pallas_call x5, Pallas kernels, product(): pl.pallas_call(functools.partial(product_kernel, [len(x) for x in lots],...  16.2 us
    unnamed x52, local copies, waits for them, and re-layouts  13.3 us
    ppermute x22, starting transfers between devices, over(): return lax.ppermute(x, 'head', perm)  12.7 us
    pallas_call x2, Pallas kernels, outer(): pl.pallas_call(functools.partial(outer_kernel, [1] + [len(lot) for lot in...  12 us
    ppermute x6, starting transfers between devices, ring(): return lax.ppermute(x, 'ctx', ring_perm(count, 1))  9.41 us
    all_to_all x1, waiting for transfers between devices, shards(): spread = lax.all_to_all(put, 'ctx', 0, 0, tiled=True)  9.31 us
  transfers between devices with their start and end apart: 46, of which 22 were waited for; matrix products, arithmetic and copies ran while one was open for 1% of the time, Pallas kernels for 21%

profile of v11, /device:TPU:0, one launch (start us, length us, event | category | flops | bytes accessed | tf_op | source)
XLA Modules:
  0.0 209.2 jit_solution(11331259044163012500)
XLA Ops:
  0.7 2.5 %constant_dynamic-slice_fusion = (bf16[96,3072]{1,0:T(8,128)(2,1)}, bf16[96,3072]{1,0:T(8,128)(2,1)}) fusion(bf16[384,6144]{1,0:T(8,128)(2,1)} %refs_4_.3, s32[]{:T(128)S(6)} %select_n.84), kind=kLoop, calls=%fused_computation.46 | loop fusion | bytes 2359300 | tf_op jit(solution)/shard_map/dynamic_slice | solution.py:375
  3.2 3.0 %collective-permute-start = (bf16[96,3072]{1,0:T(8,128)(2,1)}, bf16[96,3072]{1,0:T(8,128)(2,1)}, u32[]{:S(2)}, u32[]{:S(2)}) collective-permute-start(bf16[96,3072]{1,0:T(8,128)(2,1)} %get-tuple-element.208), channel_id=1, source_target_pairs={{0,8},{4,12},{8,24},{12,28},{24,16},{28,20},{16,0},{20,4},{1,9},{5... | collective-permute-start | bytes 1769480 | tf_op jit(solution)/shard_map/ppermute | solution.py:397
  6.2 2.6 %states.1 = (bf16[8,144,128]{2,1,0:T(8,128)(2,1)}, f32[8,384]{1,0:T(8,128)S(1)}, f32[384,8]{1,0:T(8,128)S(1)}) custom-call(f32[8,384]{1,0:T(8,128)S(1)} %copy-done.22, bf16[384,1024]{1,0:T(8,128)(2,1)S(1)} %copy-done.3, bf16[384,1024]{1,0:T(8,128)(2,1)S(1)} %copy-done.4), custom_call_target="tpu_custom_call" | custom-call | flops 1000 | bytes 1000 | tf_op jit(solution)/shard_map/states/pallas_call | solution.py:386
  8.8 4.8 %all-to-all-start = ((bf16[8,144,128]{2,1,0:T(8,128)(2,1)}), bf16[8,144,128]{2,1,0:T(8,128)(2,1)S(1)}, u32[]{:S(2)}, u32[]{:S(2)}) async-start(bf16[8,144,128]{2,1,0:T(8,128)(2,1)} %get-tuple-element.106), calls=%async_computation | async-start | bytes 589824 | tf_op jit(solution)/shard_map/all_to_all | solution.py:419
  13.6 2.0 collective-permute-start.1
  15.6 1.9 weights.1.intra_ref
  18.6 9.3 %all-to-all-done.in_ref = bf16[8,144,128]{2,1,0:T(8,128)(2,1)S(1)} async-done(((bf16[8,144,128]{2,1,0:T(8,128)(2,1)}), bf16[8,144,128]{2,1,0:T(8,128)(2,1)S(1)}, u32[]{:S(2)}, u32[]{:S(2)}) %all-to-all-start) | async-done | bytes 294944 | tf_op jit(solution)/shard_map/all_to_all | solution.py:419
  27.9 1.9 collective-permute-start.2
  30.6 5.8 %all-to-all-start.1 = ((bf16[8,128,128]{2,1,0:T(8,128)(2,1)}), bf16[8,128,128]{2,1,0:T(8,128)(2,1)S(1)}, u32[]{:S(2)}, u32[]{:S(2)}) async-start(bf16[8,128,128]{2,1,0:T(8,128)(2,1)} %copy-done.13), calls=%async_computation.1 | async-start | bytes 524288 | tf_op jit(solution)/shard_map/all_to_all | solution.py:427
  36.4 2.2 %fusion.order_ref = bf16[1024,1024]{1,0:T(8,128)(2,1)} fusion(s32[1024]{0:T(1024)S(1)} %fusion.4), kind=kLoop, calls=%fused_computation.1 | loop fusion | flops 2097152 | bytes 2101248 | tf_op jit(solution)/shard_map/convert_element_type | solution.py:349
  38.6 3.5 %collective-permute-done.1.refs_5_ = bf16[96,3072]{1,0:T(8,128)(2,1)} collective-permute-done((bf16[96,3072]{1,0:T(8,128)(2,1)}, bf16[96,3072]{1,0:T(8,128)(2,1)}, u32[]{:S(2)}, u32[]{:S(2)}) %collective-permute-start.1) | collective-permute-done | bytes 589856 | tf_op jit(solution)/shard_map/ppermute | solution.py:397
  42.1 3.3 %all-to-all-done.1.state_ref = bf16[8,128,128]{2,1,0:T(8,128)(2,1)S(1)} async-done(((bf16[8,128,128]{2,1,0:T(8,128)(2,1)}), bf16[8,128,128]{2,1,0:T(8,128)(2,1)S(1)}, u32[]{:S(2)}, u32[]{:S(2)}) %all-to-all-start.1) | async-done | bytes 262176 | tf_op jit(solution)/shard_map/all_to_all | solution.py:427
  46.8 1.5 collective-permute-start.7
  53.8 8.7 %collective-permute-done.9.refs_4_.refs_10_.refs_6_ = bf16[128,2048]{1,0:T(8,128)(2,1)S(1)} collective-permute-done((bf16[128,2048]{1,0:T(8,128)(2,1)S(1)}, bf16[128,2048]{1,0:T(8,128)(2,1)S(1)}, u32[]{:S(2)}, u32[]{:S(2)}) %collective-permute-start.9) | collective-permute-done | bytes 524320 | tf_op jit(solution)/shard_map/ppermute | solution.py:436
  63.0 2.7 %collective-permute-start.10 = (bf16[96,3072]{1,0:T(8,128)(2,1)}, bf16[96,3072]{1,0:T(8,128)(2,1)S(1)}, u32[]{:S(2)}, u32[]{:S(2)}) collective-permute-start(bf16[96,3072]{1,0:T(8,128)(2,1)} %collective-permute-done.1.refs_5_), channel_id=1, source_target_pairs={{0,8},{4,12},{8,24},{12,28},{24,16},{28,20},{16,0},{20,4},{1,9},{5... | collective-permute-start | bytes 1769480 | tf_op jit(solution)/shard_map/ppermute | solution.py:397
  65.7 1.5 collective-permute-start.11
  69.0 1.6 copy-done.1
  71.8 9.7 %collective-permute-done.14.refs_5_.refs_11_.refs_7_.refs_6_ = bf16[128,2048]{1,0:T(8,128)(2,1)S(1)} collective-permute-done((bf16[128,2048]{1,0:T(8,128)(2,1)S(1)}, bf16[128,2048]{1,0:T(8,128)(2,1)S(1)}, u32[]{:S(2)}, u32[]{:S(2)}) %collective-permute-start.14) | collective-permute-done | bytes 524320 | tf_op jit(solution)/shard_map/ppermute | solution.py:436
  84.5 5.9 %collective-permute-done.19.refs_1_ = bf16[384,256]{1,0:T(8,128)(2,1)S(1)} collective-permute-done((bf16[384,256]{1,0:T(8,128)(2,1)S(1)}, bf16[384,256]{1,0:T(8,128)(2,1)S(1)}, u32[]{:S(2)}, u32[]{:S(2)}) %collective-permute-start.19) | collective-permute-done | bytes 196640 | tf_op jit(solution)/shard_map/ppermute | solution.py:464
  91.9 9.5 %collective-permute-done.20.refs_6_.refs_12_.refs_7_ = bf16[128,2048]{1,0:T(8,128)(2,1)S(1)} collective-permute-done((bf16[128,2048]{1,0:T(8,128)(2,1)S(1)}, bf16[128,2048]{1,0:T(8,128)(2,1)S(1)}, u32[]{:S(2)}, u32[]{:S(2)}) %collective-permute-start.20) | collective-permute-done | bytes 524320 | tf_op jit(solution)/shard_map/ppermute | solution.py:436
  101.9 1.5 collective-permute-start.22
  103.6 2.7 %collective-permute-start.25 = (bf16[384,256]{1,0:T(8,128)(2,1)S(1)}, bf16[384,256]{1,0:T(8,128)(2,1)S(1)}, u32[]{:S(2)}, u32[]{:S(2)}) collective-permute-start(bf16[384,256]{1,0:T(8,128)(2,1)S(1)} %get-tuple-element.141), channel_id=1, source_target_pairs={{0,16},{4,20},{8,0},{12,4},{24,8},{28,12},{16,24},{20,28},{1,17},{... | collective-permute-start | bytes 589832 | tf_op jit(solution)/shard_map/ppermute | solution.py:470
  106.3 3.7 %product.5.refs_0_ = bf16[384,256]{1,0:T(8,128)(2,1)S(1)} custom-call(s32[1]{0:T(128)} %bitcast.1.mine_ref.refs_0_, bf16[384,6144]{1,0:T(8,128)(2,1)S(1)} %bitcast.6, bf16[384,6144]{1,0:T(8,128)(2,1)S(1)} %bitcast.6, bf16[128,6144]{1,0:T(8,128)(2,1)S(1)} %bitcast.8, bf16[128,2048]{1,0:T(8,128)(2,1)S(1)} %collective-permute-done.9.refs_4_.refs_10_.refs_6_, ...), custom_call_target="tpu_custom_call" | custom-call | flops 1000 | bytes 1000 | tf_op jit(solution)/shard_map/product/pallas_call | solution.py:216
  110.0 5.2 %product.6 = bf16[384,256]{1,0:T(8,128)(2,1)S(1)} custom-call(s32[1]{0:T(128)} %bitcast.1.mine_ref.refs_0_, bf16[96,3072]{1,0:T(8,128)(2,1)} %collective-permute-done.refs_1_.refs_5_, bf16[96,3072]{1,0:T(8,128)(2,1)S(1)} %collective-permute-done.4.refs_2_.refs_6_, bf16[96,3072]{1,0:T(8,128)(2,1)} %collective-permute-done.2.refs_3_.refs_7_, ...), custom_call_target="tpu_custom_call" | custom-call | flops 1000 | bytes 1000 | tf_op jit(solution)/shard_map/product/pallas_call | solution.py:216
  115.2 4.9 %collective-permute-done.25.refs_3_ = bf16[384,256]{1,0:T(8,128)(2,1)S(1)} collective-permute-done((bf16[384,256]{1,0:T(8,128)(2,1)S(1)}, bf16[384,256]{1,0:T(8,128)(2,1)S(1)}, u32[]{:S(2)}, u32[]{:S(2)}) %collective-permute-start.25) | collective-permute-done | bytes 196640 | tf_op jit(solution)/shard_map/ppermute | solution.py:470
  121.2 1.7 collective-permute-start.26
  124.2 3.8 %product.8 = bf16[384,256]{1,0:T(8,128)(2,1)S(1)} custom-call(s32[1]{0:T(128)} %bitcast.1.mine_ref.refs_0_, bf16[96,3072]{1,0:T(8,128)(2,1)S(1)} %collective-permute-done.6.refs_1_.refs_9_, bf16[96,3072]{1,0:T(8,128)(2,1)S(1)} %collective-permute-done.17.refs_2_.refs_10_, bf16[96,3072]{1,0:T(8,128)(2,1)S(1)} %collective-permute-done.11.refs_3_.refs_11_, ...), custom_call_target="tpu_custom_call" | custom-call | flops 1000 | bytes 1000 | tf_op jit(solution)/shard_map/product/pallas_call | solution.py:216
  128.1 1.8 product.7.refs_8_
  129.9 2.7 %collective-permute-done.29.refs_2_ = bf16[384,256]{1,0:T(8,128)(2,1)S(1)} collective-permute-done((bf16[384,256]{1,0:T(8,128)(2,1)S(1)}, bf16[384,256]{1,0:T(8,128)(2,1)S(1)}, u32[]{:S(2)}, u32[]{:S(2)}) %collective-permute-start.29) | collective-permute-done | bytes 196640 | tf_op jit(solution)/shard_map/ppermute | solution.py:482
  132.6 1.8 collective-permute-done.30.refs_1_
  134.4 2.1 collective-permute-done.26.refs_3_.refs_15_
  137.8 6.4 %outer.2 = (bf16[128,3072]{1,0:T(8,128)(2,1)S(1)}, bf16[128,3072]{1,0:T(8,128)(2,1)}) custom-call(bf16[384,256]{1,0:T(8,128)(2,1)S(1)} %get-tuple-element.174.refs_0_, bf16[384,256]{1,0:T(8,128)(2,1)S(1)} %collective-permute-done.19.refs_1_, bf16[384,256]{1,0:T(8,128)(2,1)S(1)} %collective-permute-done.29.refs_2_, ...), custom_call_target="tpu_custom_call" | custom-call | flops 1000 | bytes 1000 | tf_op jit(solution)/shard_map/outer/pallas_call | solution.py:260
  145.8 1.6 collective-permute-start.37
  147.4 1.7 product.9
  149.1 3.1 %collective-permute-start.34 = (bf16[384,256]{1,0:T(8,128)(2,1)S(1)}, bf16[384,256]{1,0:T(8,128)(2,1)S(1)}, u32[]{:S(2)}, u32[]{:S(2)}) collective-permute-start(bf16[384,256]{1,0:T(8,128)(2,1)S(1)} %product.9), channel_id=1, source_target_pairs={{0,8},{4,12},{8,24},{12,28},{24,16},{28,20},{16,0},{20,4},{1,9},{5... | collective-permute-start | bytes 589832 | tf_op jit(solution)/shard_map/ppermute | solution.py:498
  152.2 5.6 %outer.3 = (bf16[128,3072]{1,0:T(8,128)(2,1)S(1)}, bf16[128,3072]{1,0:T(8,128)(2,1)S(1)}) custom-call(bf16[384,256]{1,0:T(8,128)(2,1)S(1)} %get-tuple-element.174.refs_0_, bf16[384,256]{1,0:T(8,128)(2,1)S(1)} %collective-permute-done.19.refs_1_, bf16[384,256]{1,0:T(8,128)(2,1)S(1)} %collective-permute-done.29.refs_2_, ...), custom_call_target="tpu_custom_call" | custom-call | flops 1000 | bytes 1000 | tf_op jit(solution)/shard_map/outer/pallas_call | solution.py:260
  161.0 2.9 %collective-permute-done.36.there_ref = f32[1,384]{1,0:T(1,128)S(1)} collective-permute-done((f32[1,384]{1,0:T(1,128)S(1)}, f32[1,384]{1,0:T(1,128)S(1)}, u32[]{:S(2)}, u32[]{:S(2)}) %collective-permute-start.36) | collective-permute-done | bytes 1568 | tf_op jit(solution)/shard_map/ppermute | solution.py:400
  167.0 3.6 %all-to-all-start.2 = ((bf16[8,144,128]{2,1,0:T(8,128)(2,1)}), bf16[8,144,128]{2,1,0:T(8,128)(2,1)S(1)}, u32[]{:S(2)}, u32[]{:S(2)}) async-start(bf16[8,144,128]{2,1,0:T(8,128)(2,1)} %copy-done.20), calls=%async_computation.2 | async-start | bytes 589824 | tf_op jit(solution)/shard_map/all_to_all | solution.py:516
  170.6 2.0 collective-permute-start.38
  173.8 4.5 %inside.1 = (bf16[384,1024]{1,0:T(8,128)(2,1)}, bf16[2,384,1024]{2,1,0:T(8,128)(2,1)S(1)}) custom-call(bf16[384,1024]{1,0:T(8,128)(2,1)S(1)} %copy-done.19, bf16[384,1024]{1,0:T(8,128)(2,1)S(1)} %copy-done.8, bf16[384,1024]{1,0:T(8,128)(2,1)S(1)} %copy-done.3, bf16[384,1024]{1,0:T(8,128)(2,1)S(1)} %copy-done.5, f32[8,384]{1,0:T(8,128)S(1)} %get-tuple-element.107.run_ref, ...), custom_call_target="tpu_custom_call" | custom-call | flops 1000 | bytes 1000 | tf_op jit(solution)/shard_map/inside/pallas_call | solution.py:386
  182.1 4.2 %all-to-all-start.3 = ((bf16[8,128,128]{2,1,0:T(8,128)(2,1)}), bf16[8,128,128]{2,1,0:T(8,128)(2,1)S(1)}, u32[]{:S(2)}, u32[]{:S(2)}) async-start(bf16[8,128,128]{2,1,0:T(8,128)(2,1)} %scan.3), calls=%async_computation.3 | async-start | bytes 524288 | tf_op jit(solution)/shard_map/all_to_all | solution.py:528
  186.3 2.0 collective-permute-start.40
  188.3 2.8 %collective-permute-done.40 = f32[1,1024]{1,0:T(1,128)S(1)} collective-permute-done((f32[1,1024]{1,0:T(1,128)S(1)}, f32[1,1024]{1,0:T(1,128)S(1)}, u32[]{:S(2)}, u32[]{:S(2)}) %collective-permute-start.40) | collective-permute-done | bytes 4128 | tf_op jit(solution)/shard_map/ppermute | solution.py:530
  191.1 3.5 %collective-permute-start.41 = (f32[1,1024]{1,0:T(1,128)S(1)}, f32[1,1024]{1,0:T(1,128)S(1)}, u32[]{:S(2)}, u32[]{:S(2)}) collective-permute-start(f32[1,1024]{1,0:T(1,128)S(1)} %add.143), channel_id=1, source_target_pairs={{0,16},{4,20},{8,24},{12,28},{16,0},{20,4},{24,8},{28,12},{1,17},{... | collective-permute-start | bytes 12296 | tf_op jit(solution)/shard_map/ppermute | solution.py:530
  194.6 1.6 collective-permute-done.41
  196.8 3.8 %all-to-all-done.3.state_ref = bf16[8,128,128]{2,1,0:T(8,128)(2,1)S(1)} async-done(((bf16[8,128,128]{2,1,0:T(8,128)(2,1)}), bf16[8,128,128]{2,1,0:T(8,128)(2,1)S(1)}, u32[]{:S(2)}, u32[]{:S(2)}) %all-to-all-start.3) | async-done | bytes 262176 | tf_op jit(solution)/shard_map/all_to_all | solution.py:528
  202.0 2.0 outside.1
  206.3 2.9 %sum.1 = bf16[128,6144]{1,0:T(8,128)(2,1)} custom-call(bf16[128,3072]{1,0:T(8,128)(2,1)S(1)} %copy-done.15, bf16[128,3072]{1,0:T(8,128)(2,1)} %collective-permute-done.37.refs_1_, bf16[128,3072]{1,0:T(8,128)(2,1)S(1)} %copy-done.17, bf16[128,3072]{1,0:T(8,128)(2,1)} %collective-permute-done.39.refs_3_), custom_call_target="tpu_custom_call" | custom-call | flops 1000 | bytes 1000 | tf_op jit(solution)/shard_map/sum/pallas_call | solution.py:386
  (124 shorter events, 38.2 us)
Async XLA Ops:
  3.2 24.8 %collective-permute-start = (bf16[96,3072]{1,0:T(8,128)(2,1)}, bf16[96,3072]{1,0:T(8,128)(2,1)}, u32[]{:S(2)}, u32[]{:S(2)}) collective-permute-start(bf16[96,3072]{1,0:T(8,128)(2,1)} %get-tuple-element.208), channel_id=1, source_target_pairs={{0,8},{4,12},{8,24},{12,28},{24,16},{28,20},{16,0},{20,4},{1,9},{5... | collective-permute-start | bytes 1769480 | tf_op jit(solution)/shard_map/ppermute | solution.py:397
  8.8 19.2 %all-to-all-start = ((bf16[8,144,128]{2,1,0:T(8,128)(2,1)}), bf16[8,144,128]{2,1,0:T(8,128)(2,1)S(1)}, u32[]{:S(2)}, u32[]{:S(2)}) async-start(bf16[8,144,128]{2,1,0:T(8,128)(2,1)} %get-tuple-element.106), calls=%async_computation | async-start | bytes 589824 | tf_op jit(solution)/shard_map/all_to_all | solution.py:419
  13.6 28.5 %collective-permute-start.1 = (bf16[96,3072]{1,0:T(8,128)(2,1)}, bf16[96,3072]{1,0:T(8,128)(2,1)}, u32[]{:S(2)}, u32[]{:S(2)}) collective-permute-start(bf16[96,3072]{1,0:T(8,128)(2,1)} %get-tuple-element.110), channel_id=1, source_target_pairs={{0,8},{4,12},{8,24},{12,28},{24,16},{28,20},{16,0},{20,4},{1,9},{5... | collective-permute-start | bytes 1769480 | tf_op jit(solution)/shard_map/ppermute | solution.py:397
  15.6 90.7 %slice-start = ((s8[4718592]{0:T(1024)(128)(4,1)}), s8[524288]{0:T(1024)(128)(4,1)S(1)}, s32[]{:S(2)}) async-start(s8[4718592]{0:T(1024)(128)(4,1)} %bitcast.5), calls=%async_computation.4 | async-start | bytes 1048576
  27.9 17.4 %collective-permute-start.2 = (bf16[96,3072]{1,0:T(8,128)(2,1)}, bf16[96,3072]{1,0:T(8,128)(2,1)}, u32[]{:S(2)}, u32[]{:S(2)}) collective-permute-start(bf16[96,3072]{1,0:T(8,128)(2,1)} %collective-permute-done.refs_1_.refs_5_), channel_id=1, source_target_pairs={{0,2},{1,3},{2,0},{3,1},{4,6},{5,7},{6,4},{7,5},{8,10},{9,11},{10,... | collective-permute-start | bytes 1769480 | tf_op jit(solution)/shard_map/ppermute | solution.py:400
  30.6 14.8 %all-to-all-start.1 = ((bf16[8,128,128]{2,1,0:T(8,128)(2,1)}), bf16[8,128,128]{2,1,0:T(8,128)(2,1)S(1)}, u32[]{:S(2)}, u32[]{:S(2)}) async-start(bf16[8,128,128]{2,1,0:T(8,128)(2,1)} %copy-done.13), calls=%async_computation.1 | async-start | bytes 524288 | tf_op jit(solution)/shard_map/all_to_all | solution.py:427
  45.4 61.0 %slice-start.1 = ((s8[4718592]{0:T(1024)(128)(4,1)}), s8[4194304]{0:T(1024)(128)(4,1)S(1)}, s32[]{:S(2)}) async-start(s8[4718592]{0:T(1024)(128)(4,1)} %bitcast.5), calls=%async_computation.5 | async-start | bytes 8388608
  45.4 4.4 %collective-permute-start.4 = (bf16[96,3072]{1,0:T(8,128)(2,1)}, bf16[96,3072]{1,0:T(8,128)(2,1)S(1)}, u32[]{:S(2)}, u32[]{:S(2)}) collective-permute-start(bf16[96,3072]{1,0:T(8,128)(2,1)} %collective-permute-done.refs_1_.refs_5_), channel_id=1, source_target_pairs={{0,1},{1,0},{2,3},{3,2},{4,5},{5,4},{6,7},{7,6},{8,9},{9,8},{10,11... | collective-permute-start | bytes 1769480 | tf_op jit(solution)/shard_map/ppermute | solution.py:400
  45.4 17.6 %collective-permute-start.6 = (bf16[96,3072]{1,0:T(8,128)(2,1)}, bf16[96,3072]{1,0:T(8,128)(2,1)S(1)}, u32[]{:S(2)}, u32[]{:S(2)}) collective-permute-start(bf16[96,3072]{1,0:T(8,128)(2,1)} %collective-permute-done.refs_1_.refs_5_), channel_id=1, source_target_pairs={{0,8},{4,12},{8,24},{12,28},{24,16},{28,20},{16,0},{20,4},{1,9},{5... | collective-permute-start | bytes 1769480 | tf_op jit(solution)/shard_map/ppermute | solution.py:397
  46.7 3.0 %collective-permute-start.3 = (bf16[96,3072]{1,0:T(8,128)(2,1)}, bf16[96,3072]{1,0:T(8,128)(2,1)S(1)}, u32[]{:S(2)}, u32[]{:S(2)}) collective-permute-start(bf16[96,3072]{1,0:T(8,128)(2,1)} %collective-permute-done.2.refs_3_.refs_7_), channel_id=1, source_target_pairs={{0,1},{1,0},{2,3},{3,2},{4,5},{5,4},{6,7},{7,6},{8,9},{9,8},{10,11... | collective-permute-start | bytes 1769480 | tf_op jit(solution)/shard_map/ppermute | solution.py:400
  46.8 16.2 %collective-permute-start.7 = (bf16[96,3072]{1,0:T(8,128)(2,1)}, bf16[96,3072]{1,0:T(8,128)(2,1)S(1)}, u32[]{:S(2)}, u32[]{:S(2)}) collective-permute-start(bf16[96,3072]{1,0:T(8,128)(2,1)} %collective-permute-done.1.refs_5_), channel_id=1, source_target_pairs={{0,2},{1,3},{2,0},{3,1},{4,6},{5,7},{6,4},{7,5},{8,10},{9,11},{10,... | collective-permute-start | bytes 1769480 | tf_op jit(solution)/shard_map/ppermute | solution.py:400
  48.5 14.0 %collective-permute-start.9 = (bf16[128,2048]{1,0:T(8,128)(2,1)S(1)}, bf16[128,2048]{1,0:T(8,128)(2,1)S(1)}, u32[]{:S(2)}, u32[]{:S(2)}) collective-permute-start(bf16[128,2048]{1,0:T(8,128)(2,1)S(1)} %get-tuple-element.211), channel_id=1, source_target_pairs={{0,4},{4,0},{8,12},{12,8},{16,20},{20,16},{24,28},{28,24},{1,5},{5... | collective-permute-start | bytes 1572872 | tf_op jit(solution)/shard_map/ppermute | solution.py:436
  51.9 1.2 collective-permute-start.5
  53.1 9.9 %collective-permute-start.8 = (f32[1,384]{1,0:T(1,128)S(1)}, f32[1,384]{1,0:T(1,128)S(1)}, u32[]{:S(2)}, u32[]{:S(2)}) collective-permute-start(f32[1,384]{1,0:T(1,128)S(1)} %add.140.here_ref), channel_id=1, source_target_pairs={{0,2},{1,3},{2,0},{3,1},{4,6},{5,7},{6,4},{7,5},{8,10},{9,11},{10,... | collective-permute-start | bytes 4616 | tf_op jit(solution)/shard_map/ppermute | solution.py:400
  63.0 18.6 %collective-permute-start.10 = (bf16[96,3072]{1,0:T(8,128)(2,1)}, bf16[96,3072]{1,0:T(8,128)(2,1)S(1)}, u32[]{:S(2)}, u32[]{:S(2)}) collective-permute-start(bf16[96,3072]{1,0:T(8,128)(2,1)} %collective-permute-done.1.refs_5_), channel_id=1, source_target_pairs={{0,8},{4,12},{8,24},{12,28},{24,16},{28,20},{16,0},{20,4},{1,9},{5... | collective-permute-start | bytes 1769480 | tf_op jit(solution)/shard_map/ppermute | solution.py:397
  65.7 15.9 %collective-permute-start.12 = (bf16[96,3072]{1,0:T(8,128)(2,1)}, bf16[96,3072]{1,0:T(8,128)(2,1)S(1)}, u32[]{:S(2)}, u32[]{:S(2)}) collective-permute-start(bf16[96,3072]{1,0:T(8,128)(2,1)} %collective-permute-done.1.refs_5_), channel_id=1, source_target_pairs={{0,1},{1,0},{2,3},{3,2},{4,5},{5,4},{6,7},{7,6},{8,9},{9,8},{10,11... | collective-permute-start | bytes 1769480 | tf_op jit(solution)/shard_map/ppermute | solution.py:400
  65.7 15.9 %collective-permute-start.11 = (bf16[96,3072]{1,0:T(8,128)(2,1)S(1)}, bf16[96,3072]{1,0:T(8,128)(2,1)S(1)}, u32[]{:S(2)}, u32[]{:S(2)}) collective-permute-start(bf16[96,3072]{1,0:T(8,128)(2,1)S(1)} %collective-permute-done.6.refs_1_.refs_9_), channel_id=1, source_target_pairs={{0,2},{1,3},{2,0},{3,1},{4,6},{5,7},{6,4},{7,5},{8,10},{9,11},{10,... | collective-permute-start | bytes 1769480 | tf_op jit(solution)/shard_map/ppermute | solution.py:400
  67.2 14.4 %collective-permute-start.13 = (bf16[96,3072]{1,0:T(8,128)(2,1)S(1)}, bf16[96,3072]{1,0:T(8,128)(2,1)S(1)}, u32[]{:S(2)}, u32[]{:S(2)}) collective-permute-start(bf16[96,3072]{1,0:T(8,128)(2,1)S(1)} %collective-permute-done.7.refs_7_), channel_id=1, source_target_pairs={{0,1},{1,0},{2,3},{3,2},{4,5},{5,4},{6,7},{7,6},{8,9},{9,8},{10,11... | collective-permute-start | bytes 1769480 | tf_op jit(solution)/shard_map/ppermute | solution.py:400
  67.5 14.1 %collective-permute-start.14 = (bf16[128,2048]{1,0:T(8,128)(2,1)S(1)}, bf16[128,2048]{1,0:T(8,128)(2,1)S(1)}, u32[]{:S(2)}, u32[]{:S(2)}) collective-permute-start(bf16[128,2048]{1,0:T(8,128)(2,1)S(1)} %get-tuple-element.131), channel_id=1, source_target_pairs={{0,4},{4,0},{8,12},{12,8},{16,20},{20,16},{24,28},{28,24},{1,5},{5... | collective-permute-start | bytes 1572872 | tf_op jit(solution)/shard_map/ppermute | solution.py:436
  81.6 8.8 %collective-permute-start.19 = (bf16[384,256]{1,0:T(8,128)(2,1)S(1)}, bf16[384,256]{1,0:T(8,128)(2,1)S(1)}, u32[]{:S(2)}, u32[]{:S(2)}) collective-permute-start(bf16[384,256]{1,0:T(8,128)(2,1)S(1)} %get-tuple-element.136), channel_id=1, source_target_pairs={{0,8},{4,12},{8,24},{12,28},{24,16},{28,20},{16,0},{20,4},{1,9},{5... | collective-permute-start | bytes 589832 | tf_op jit(solution)/shard_map/ppermute | solution.py:464
  82.8 18.7 %collective-permute-start.15 = (bf16[96,3072]{1,0:T(8,128)(2,1)S(1)}, bf16[96,3072]{1,0:T(8,128)(2,1)S(1)}, u32[]{:S(2)}, u32[]{:S(2)}) collective-permute-start(bf16[96,3072]{1,0:T(8,128)(2,1)S(1)} %collective-permute-done.6.refs_1_.refs_9_), channel_id=1, source_target_pairs={{0,8},{4,12},{8,24},{12,28},{24,16},{28,20},{16,0},{20,4},{1,9},{5... | collective-permute-start | bytes 1769480 | tf_op jit(solution)/shard_map/ppermute | solution.py:397
  82.9 18.7 %collective-permute-start.17 = (bf16[96,3072]{1,0:T(8,128)(2,1)S(1)}, bf16[96,3072]{1,0:T(8,128)(2,1)S(1)}, u32[]{:S(2)}, u32[]{:S(2)}) collective-permute-start(bf16[96,3072]{1,0:T(8,128)(2,1)S(1)} %collective-permute-done.6.refs_1_.refs_9_), channel_id=1, source_target_pairs={{0,1},{1,0},{2,3},{3,2},{4,5},{5,4},{6,7},{7,6},{8,9},{9,8},{10,11... | collective-permute-start | bytes 1769480 | tf_op jit(solution)/shard_map/ppermute | solution.py:400
  82.9 18.7 %collective-permute-start.16 = (bf16[96,3072]{1,0:T(8,128)(2,1)S(1)}, bf16[96,3072]{1,0:T(8,128)(2,1)S(1)}, u32[]{:S(2)}, u32[]{:S(2)}) collective-permute-start(bf16[96,3072]{1,0:T(8,128)(2,1)S(1)} %collective-permute-done.10.refs_5_.refs_9_), channel_id=1, source_target_pairs={{0,2},{1,3},{2,0},{3,1},{4,6},{5,7},{6,4},{7,5},{8,10},{9,11},{10,... | collective-permute-start | bytes 1769480 | tf_op jit(solution)/shard_map/ppermute | solution.py:400
  84.3 17.2 %collective-permute-start.18 = (bf16[96,3072]{1,0:T(8,128)(2,1)S(1)}, bf16[96,3072]{1,0:T(8,128)(2,1)S(1)}, u32[]{:S(2)}, u32[]{:S(2)}) collective-permute-start(bf16[96,3072]{1,0:T(8,128)(2,1)S(1)} %collective-permute-done.11.refs_3_.refs_11_), channel_id=1, source_target_pairs={{0,1},{1,0},{2,3},{3,2},{4,5},{5,4},{6,7},{7,6},{8,9},{9,8},{10,11... | collective-permute-start | bytes 1769480 | tf_op jit(solution)/shard_map/ppermute | solution.py:400
  90.4 11.0 %collective-permute-start.20 = (bf16[128,2048]{1,0:T(8,128)(2,1)S(1)}, bf16[128,2048]{1,0:T(8,128)(2,1)S(1)}, u32[]{:S(2)}, u32[]{:S(2)}) collective-permute-start(bf16[128,2048]{1,0:T(8,128)(2,1)S(1)} %get-tuple-element.137), channel_id=1, source_target_pairs={{0,4},{4,0},{8,12},{12,8},{16,20},{20,16},{24,28},{28,24},{1,5},{5... | collective-permute-start | bytes 1572872 | tf_op jit(solution)/shard_map/ppermute | solution.py:436
  101.6 19.1 %collective-permute-start.21 = (bf16[96,3072]{1,0:T(8,128)(2,1)S(1)}, bf16[96,3072]{1,0:T(8,128)(2,1)S(1)}, u32[]{:S(2)}, u32[]{:S(2)}) collective-permute-start(bf16[96,3072]{1,0:T(8,128)(2,1)S(1)} %collective-permute-done.10.refs_5_.refs_9_), channel_id=1, source_target_pairs={{0,8},{4,12},{8,24},{12,28},{24,16},{28,20},{16,0},{20,4},{1,9},{5... | collective-permute-start | bytes 1769480 | tf_op jit(solution)/shard_map/ppermute | solution.py:397
  101.9 18.7 %collective-permute-start.23 = (bf16[96,3072]{1,0:T(8,128)(2,1)S(1)}, bf16[96,3072]{1,0:T(8,128)(2,1)S(1)}, u32[]{:S(2)}, u32[]{:S(2)}) collective-permute-start(bf16[96,3072]{1,0:T(8,128)(2,1)S(1)} %collective-permute-done.10.refs_5_.refs_9_), channel_id=1, source_target_pairs={{0,1},{1,0},{2,3},{3,2},{4,5},{5,4},{6,7},{7,6},{8,9},{9,8},{10,11... | collective-permute-start | bytes 1769480 | tf_op jit(solution)/shard_map/ppermute | solution.py:400
  101.9 18.7 %collective-permute-start.22 = (bf16[96,3072]{1,0:T(8,128)(2,1)S(1)}, bf16[96,3072]{1,0:T(8,128)(2,1)S(1)}, u32[]{:S(2)}, u32[]{:S(2)}) collective-permute-start(bf16[96,3072]{1,0:T(8,128)(2,1)S(1)} %collective-permute-done.15.refs_1_.refs_13_), channel_id=1, source_target_pairs={{0,2},{1,3},{2,0},{3,1},{4,6},{5,7},{6,4},{7,5},{8,10},{9,11},{10,... | collective-permute-start | bytes 1769480 | tf_op jit(solution)/shard_map/ppermute | solution.py:400
  103.4 17.2 %collective-permute-start.24 = (bf16[96,3072]{1,0:T(8,128)(2,1)S(1)}, bf16[96,3072]{1,0:T(8,128)(2,1)S(1)}, u32[]{:S(2)}, u32[]{:S(2)}) collective-permute-start(bf16[96,3072]{1,0:T(8,128)(2,1)S(1)} %collective-permute-done.16.refs_7_.refs_11_), channel_id=1, source_target_pairs={{0,1},{1,0},{2,3},{3,2},{4,5},{5,4},{6,7},{7,6},{8,9},{9,8},{10,11... | collective-permute-start | bytes 1769480 | tf_op jit(solution)/shard_map/ppermute | solution.py:400
  103.6 16.5 %collective-permute-start.25 = (bf16[384,256]{1,0:T(8,128)(2,1)S(1)}, bf16[384,256]{1,0:T(8,128)(2,1)S(1)}, u32[]{:S(2)}, u32[]{:S(2)}) collective-permute-start(bf16[384,256]{1,0:T(8,128)(2,1)S(1)} %get-tuple-element.141), channel_id=1, source_target_pairs={{0,16},{4,20},{8,0},{12,4},{24,8},{28,12},{16,24},{20,28},{1,17},{... | collective-permute-start | bytes 589832 | tf_op jit(solution)/shard_map/ppermute | solution.py:470
  120.6 7.4 %collective-permute-start.27 = (bf16[96,3072]{1,0:T(8,128)(2,1)S(1)}, bf16[96,3072]{1,0:T(8,128)(2,1)S(1)}, u32[]{:S(2)}, u32[]{:S(2)}) collective-permute-start(bf16[96,3072]{1,0:T(8,128)(2,1)S(1)} %collective-permute-done.15.refs_1_.refs_13_), channel_id=1, source_target_pairs={{0,1},{1,0},{2,3},{3,2},{4,5},{5,4},{6,7},{7,6},{8,9},{9,8},{10,11... | collective-permute-start | bytes 1769480 | tf_op jit(solution)/shard_map/ppermute | solution.py:400
  120.7 7.4 %collective-permute-start.28 = (bf16[96,3072]{1,0:T(8,128)(2,1)S(1)}, bf16[96,3072]{1,0:T(8,128)(2,1)S(1)}, u32[]{:S(2)}, u32[]{:S(2)}) collective-permute-start(bf16[96,3072]{1,0:T(8,128)(2,1)S(1)} %collective-permute-done.22.refs_3_.refs_15_), channel_id=1, source_target_pairs={{0,1},{1,0},{2,3},{3,2},{4,5},{5,4},{6,7},{7,6},{8,9},{9,8},{10,11... | collective-permute-start | bytes 1769480 | tf_op jit(solution)/shard_map/ppermute | solution.py:400
  121.2 15.3 %collective-permute-start.26 = (bf16[96,3072]{1,0:T(8,128)(2,1)S(1)}, bf16[96,3072]{1,0:T(8,128)(2,1)S(1)}, u32[]{:S(2)}, u32[]{:S(2)}) collective-permute-start(bf16[96,3072]{1,0:T(8,128)(2,1)S(1)} %collective-permute-done.21.refs_1_.refs_13_), channel_id=1, source_target_pairs={{0,2},{1,3},{2,0},{3,1},{4,6},{5,7},{6,4},{7,5},{8,10},{9,11},{10,... | collective-permute-start | bytes 1769480 | tf_op jit(solution)/shard_map/ppermute | solution.py:400
  123.0 9.7 %collective-permute-start.29 = (bf16[384,256]{1,0:T(8,128)(2,1)S(1)}, bf16[384,256]{1,0:T(8,128)(2,1)S(1)}, u32[]{:S(2)}, u32[]{:S(2)}) collective-permute-start(bf16[384,256]{1,0:T(8,128)(2,1)S(1)} %get-tuple-element.152), channel_id=1, source_target_pairs={{0,24},{4,28},{8,16},{12,20},{24,0},{28,4},{16,8},{20,12},{1,25},{... | collective-permute-start | bytes 589832 | tf_op jit(solution)/shard_map/ppermute | solution.py:482
  123.9 10.5 %collective-permute-start.30 = (bf16[384,256]{1,0:T(8,128)(2,1)S(1)}, bf16[384,256]{1,0:T(8,128)(2,1)S(1)}, u32[]{:S(2)}, u32[]{:S(2)}) collective-permute-start(bf16[384,256]{1,0:T(8,128)(2,1)S(1)} %product.6), channel_id=1, source_target_pairs={{0,16},{4,20},{8,0},{12,4},{24,8},{28,12},{16,24},{20,28},{1,17},{... | collective-permute-start | bytes 589832 | tf_op jit(solution)/shard_map/ppermute | solution.py:483
  128.0 17.7 %collective-permute-start.32 = (bf16[96,3072]{1,0:T(8,128)(2,1)S(1)}, bf16[96,3072]{1,0:T(8,128)(2,1)S(1)}, u32[]{:S(2)}, u32[]{:S(2)}) collective-permute-start(bf16[96,3072]{1,0:T(8,128)(2,1)S(1)} %collective-permute-done.21.refs_1_.refs_13_), channel_id=1, source_target_pairs={{0,1},{1,0},{2,3},{3,2},{4,5},{5,4},{6,7},{7,6},{8,9},{9,8},{10,11... | collective-permute-start | bytes 1769480 | tf_op jit(solution)/shard_map/ppermute | solution.py:400
  136.5 9.2 %collective-permute-start.31 = (bf16[96,3072]{1,0:T(8,128)(2,1)S(1)}, bf16[96,3072]{1,0:T(8,128)(2,1)S(1)}, u32[]{:S(2)}, u32[]{:S(2)}) collective-permute-start(bf16[96,3072]{1,0:T(8,128)(2,1)S(1)} %collective-permute-done.26.refs_3_.refs_15_), channel_id=1, source_target_pairs={{0,1},{1,0},{2,3},{3,2},{4,5},{5,4},{6,7},{7,6},{8,9},{9,8},{10,11... | collective-permute-start | bytes 1769480 | tf_op jit(solution)/shard_map/ppermute | solution.py:400
  136.5 9.2 %collective-permute-start.33 = (bf16[384,256]{1,0:T(8,128)(2,1)S(1)}, bf16[384,256]{1,0:T(8,128)(2,1)S(1)}, u32[]{:S(2)}, u32[]{:S(2)}) collective-permute-start(bf16[384,256]{1,0:T(8,128)(2,1)S(1)} %product.8), channel_id=1, source_target_pairs={{0,24},{4,28},{8,16},{12,20},{24,0},{28,4},{16,8},{20,12},{1,25},{... | collective-permute-start | bytes 589832 | tf_op jit(solution)/shard_map/ppermute | solution.py:487
  145.8 34.0 %collective-permute-start.37 = (bf16[128,3072]{1,0:T(8,128)(2,1)}, bf16[128,3072]{1,0:T(8,128)(2,1)}, u32[]{:S(2)}, u32[]{:S(2)}) collective-permute-start(bf16[128,3072]{1,0:T(8,128)(2,1)} %get-tuple-element.193), channel_id=1, source_target_pairs={{0,4},{4,0},{8,12},{12,8},{16,20},{20,16},{24,28},{28,24},{1,5},{5... | collective-permute-start | bytes 2359304 | tf_op jit(solution)/shard_map/ppermute | solution.py:500
  149.1 8.7 %collective-permute-start.34 = (bf16[384,256]{1,0:T(8,128)(2,1)S(1)}, bf16[384,256]{1,0:T(8,128)(2,1)S(1)}, u32[]{:S(2)}, u32[]{:S(2)}) collective-permute-start(bf16[384,256]{1,0:T(8,128)(2,1)S(1)} %product.9), channel_id=1, source_target_pairs={{0,8},{4,12},{8,24},{12,28},{24,16},{28,20},{16,0},{20,4},{1,9},{5... | collective-permute-start | bytes 589832 | tf_op jit(solution)/shard_map/ppermute | solution.py:498
  159.1 1.2 collective-permute-start.35
  160.3 3.6 %collective-permute-start.36 = (f32[1,384]{1,0:T(1,128)S(1)}, f32[1,384]{1,0:T(1,128)S(1)}, u32[]{:S(2)}, u32[]{:S(2)}) collective-permute-start(f32[1,384]{1,0:T(1,128)S(1)} %add.141.here_ref), channel_id=1, source_target_pairs={{0,2},{1,3},{2,0},{3,1},{4,6},{5,7},{6,4},{7,5},{8,10},{9,11},{10,... | collective-permute-start | bytes 4616 | tf_op jit(solution)/shard_map/ppermute | solution.py:400
  167.0 12.8 %all-to-all-start.2 = ((bf16[8,144,128]{2,1,0:T(8,128)(2,1)}), bf16[8,144,128]{2,1,0:T(8,128)(2,1)S(1)}, u32[]{:S(2)}, u32[]{:S(2)}) async-start(bf16[8,144,128]{2,1,0:T(8,128)(2,1)} %copy-done.20), calls=%async_computation.2 | async-start | bytes 589824 | tf_op jit(solution)/shard_map/all_to_all | solution.py:516
  170.6 8.8 %collective-permute-start.38 = (f32[1,1024]{1,0:T(1,128)S(1)}, f32[1,1024]{1,0:T(1,128)S(1)}, u32[]{:S(2)}, u32[]{:S(2)}) collective-permute-start(f32[1,1024]{1,0:T(1,128)S(1)} %get-tuple-element.195), channel_id=1, source_target_pairs={{0,4},{4,0},{8,12},{12,8},{16,20},{20,16},{24,28},{28,24},{1,5},{5... | collective-permute-start | bytes 12296 | tf_op jit(solution)/shard_map/ppermute | solution.py:519
  179.8 24.2 %collective-permute-start.39 = (bf16[128,3072]{1,0:T(8,128)(2,1)}, bf16[128,3072]{1,0:T(8,128)(2,1)}, u32[]{:S(2)}, u32[]{:S(2)}) collective-permute-start(bf16[128,3072]{1,0:T(8,128)(2,1)} %copy-done.23), channel_id=1, source_target_pairs={{0,4},{4,0},{8,12},{12,8},{16,20},{20,16},{24,28},{28,24},{1,5},{5... | collective-permute-start | bytes 2359304 | tf_op jit(solution)/shard_map/ppermute | solution.py:526
  182.1 18.5 %all-to-all-start.3 = ((bf16[8,128,128]{2,1,0:T(8,128)(2,1)}), bf16[8,128,128]{2,1,0:T(8,128)(2,1)S(1)}, u32[]{:S(2)}, u32[]{:S(2)}) async-start(bf16[8,128,128]{2,1,0:T(8,128)(2,1)} %scan.3), calls=%async_computation.3 | async-start | bytes 524288 | tf_op jit(solution)/shard_map/all_to_all | solution.py:528
  186.3 4.8 %collective-permute-start.40 = (f32[1,1024]{1,0:T(1,128)S(1)}, f32[1,1024]{1,0:T(1,128)S(1)}, u32[]{:S(2)}, u32[]{:S(2)}) collective-permute-start(f32[1,1024]{1,0:T(1,128)S(1)} %add.142), channel_id=1, source_target_pairs={{0,8},{4,12},{8,0},{12,4},{16,24},{20,28},{24,16},{28,20},{1,9},{5... | collective-permute-start | bytes 12296 | tf_op jit(solution)/shard_map/ppermute | solution.py:530
  191.1 5.1 %collective-permute-start.41 = (f32[1,1024]{1,0:T(1,128)S(1)}, f32[1,1024]{1,0:T(1,128)S(1)}, u32[]{:S(2)}, u32[]{:S(2)}) collective-permute-start(f32[1,1024]{1,0:T(1,128)S(1)} %add.143), channel_id=1, source_target_pairs={{0,16},{4,20},{8,24},{12,28},{16,0},{20,4},{24,8},{28,12},{1,17},{... | collective-permute-start | bytes 12296 | tf_op jit(solution)/shard_map/ppermute | solution.py:530
  (24 other events, 141.6 us)

commit v12 on v11

--- a/solution.py
+++ b/solution.py
@@ -272,14 +272,28 @@
     )(*normed, grad_out, *flat)
 
 
-def final_kernel(chunks, minor, *refs):
-    out_ref = refs[-1]
-    deep = refs[0].shape[1]
-    for c in range(chunks):
-        total = refs[c * minor][...].astype(FL)
-        for s in range(1, minor):
-            total = total + refs[c * minor + s][...].astype(FL)
-        out_ref[:, c * deep : (c + 1) * deep] = total.astype(BF)
+def half_kernel(skip, *refs):
+    parts, out_ref = refs[skip:-1], refs[-1]
+    total = parts[0][...].astype(FL)
+    for ref in parts[1:]:
+        total = total + ref[...].astype(FL)
+    out_ref[...] = total.astype(BF)
+
+
+def add_half(parts, at, model, into=None):
+    own, deep = parts[0].shape
+    more = [] if into is None else [into]
+    return pl.pallas_call(
+        functools.partial(half_kernel, len(more)),
+        grid=(1,),
+        in_specs=[pl.BlockSpec(memory_space=pl.ANY)] * len(more) + [spec((own, deep))] * len(parts),
+        out_specs=spec((own, deep), lambda i: (0, at)),
+        out_shape=jax.ShapeDtypeStruct((own, model), BF),
+        input_output_aliases={0: 0} if more else {},
+        compiler_params=PARAMS,
+        cost_estimate=TINY,
+        name="sum",
+    )(*more, *parts)
 
 
 def back_kernel(order_ref, attn_ref, inv_ref, gain_ref, *refs):
@@ -522,10 +536,13 @@
         grad_attn, query_rows, key_rows, value_rows, run, turned, state_low,
     )
     spread, flat, inside, gain_sum, late = hold((spread, flat, inside, gain_sum, late))
-    flat.append(late[0])
-    flat += [lax.ppermute(late[s], "ctx", pair_perm(count, s)) for s in range(1, minor)]
+    rest = [late[0]]
+    rest += [lax.ppermute(late[s], "ctx", pair_perm(count, s)) for s in range(1, minor)]
+    grad_weight = add_half(flat, 0, model)
     states = whole(functools.partial(scan_kernel, True), scan_shape, "scan", spread)
-    back_low = lax.all_to_all(states, "ctx", 0, 0, tiled=True).reshape(heads, size, size)
+    back_low = lax.all_to_all(states, "ctx", 0, 0, tiled=True)
+    back_low, grad_weight = hold((back_low, grad_weight))
+    back_low = back_low.reshape(heads, size, size)
     for step in flips[1:]:
         gain_sum = gain_sum + lax.ppermute(
             gain_sum, "ctx", [(i, i ^ step) for i in range(count)]
@@ -535,10 +552,7 @@
         outside_kernel, [wide_b] * 2, "outside",
         key_rows, value_rows, back_low, turned, inside,
     )
-    grad_weight = whole(
-        functools.partial(final_kernel, CHUNKS, minor), jax.ShapeDtypeStruct((own, model), BF),
-        "sum", *flat,
-    ).reshape(heads, narrow, model)
+    grad_weight = add_half(rest, 1, model, grad_weight).reshape(heads, narrow, model)
     return grad_query, grad_key, grad_value, grad_weight, grad_gain
 
 

time: 210 us -> 207 us (0.986)
  waiting for transfers between devices: 77 us -> 73.7 us
    pallas_call x0 -> x2, Pallas kernels: none -> 4.38 us  [add_half(): pl.pallas_call(functools.partial(half_kernel, len(more)), grid=(1,), in_s...]
    pallas_call x11 -> x10, Pallas kernels: 19.3 us -> 16.5 us  [whole(): pl.pallas_call(kernel, in_specs=[SCALAR if a is tokens else full for a in...]
  transfers between devices with their start and end apart: 46 -> 46, of which waited for: 22 -> 21; matrix products, arithmetic and copies ran while one was open for 1% -> 1% of each run, Pallas kernels for 21% -> 23%
where the time goes in v12:
time: 207 us; the launch traced here: 206 us
  waiting for transfers between devices  73.7 us (36%)
  starting transfers between devices  64.8 us (31%)
  Pallas kernels  49.1 us (24%)
  local copies, waits for them, and re-layouts  14.8 us (7%)
  other arithmetic  2.85 us (1%)
    ppermute x3, waiting for transfers between devices, swap(): lax.ppermute(part, 'ctx', pair_perm(count, -s))  27.9 us
    pallas_call x10, Pallas kernels, whole(): pl.pallas_call(kernel, in_specs=[SCALAR if a is tokens else full for a in...  16.5 us
    pallas_call x5, Pallas kernels, product(): pl.pallas_call(functools.partial(product_kernel, [len(x) for x in lots],...  16.2 us
    ppermute x22, starting transfers between devices, over(): return lax.ppermute(x, 'head', perm)  12.7 us
    unnamed x52, local copies, waits for them, and re-layouts  12.2 us
    pallas_call x2, Pallas kernels, outer(): pl.pallas_call(functools.partial(outer_kernel, [1] + [len(lot) for lot in...  12 us
    ppermute x6, starting transfers between devices, ring(): return lax.ppermute(x, 'ctx', ring_perm(count, 1))  9.41 us
    all_to_all x1, waiting for transfers between devices, shards(): spread = lax.all_to_all(put, 'ctx', 0, 0, tiled=True)  9.3 us
  transfers between devices with their start and end apart: 46, of which 21 were waited for; matrix products, arithmetic and copies ran while one was open for 1% of the time, Pallas kernels for 23%

profile of v12, /device:TPU:0, one launch (start us, length us, event | category | flops | bytes accessed | tf_op | source)
XLA Modules:
  0.0 206.2 jit_solution(17756940608445045685)
XLA Ops:
  0.7 2.4 %constant_dynamic-slice_fusion = (bf16[96,3072]{1,0:T(8,128)(2,1)}, bf16[96,3072]{1,0:T(8,128)(2,1)}) fusion(bf16[384,6144]{1,0:T(8,128)(2,1)} %refs_4_.3, s32[]{:T(128)S(6)} %select_n.84), kind=kLoop, calls=%fused_computation.46 | loop fusion | bytes 2359300 | tf_op jit(solution)/shard_map/dynamic_slice | solution.py:389
  3.1 3.0 %collective-permute-start = (bf16[96,3072]{1,0:T(8,128)(2,1)}, bf16[96,3072]{1,0:T(8,128)(2,1)}, u32[]{:S(2)}, u32[]{:S(2)}) collective-permute-start(bf16[96,3072]{1,0:T(8,128)(2,1)} %get-tuple-element.212), channel_id=1, source_target_pairs={{0,8},{4,12},{8,24},{12,28},{24,16},{28,20},{16,0},{20,4},{1,9},{5... | collective-permute-start | bytes 1769480 | tf_op jit(solution)/shard_map/ppermute | solution.py:411
  6.2 2.6 %states.1 = (bf16[8,144,128]{2,1,0:T(8,128)(2,1)}, f32[8,384]{1,0:T(8,128)S(1)}, f32[384,8]{1,0:T(8,128)S(1)}) custom-call(f32[8,384]{1,0:T(8,128)S(1)} %copy-done.22, bf16[384,1024]{1,0:T(8,128)(2,1)S(1)} %copy-done.3, bf16[384,1024]{1,0:T(8,128)(2,1)S(1)} %copy-done.4), custom_call_target="tpu_custom_call" | custom-call | flops 1000 | bytes 1000 | tf_op jit(solution)/shard_map/states/pallas_call | solution.py:400
  8.7 4.8 %all-to-all-start = ((bf16[8,144,128]{2,1,0:T(8,128)(2,1)}), bf16[8,144,128]{2,1,0:T(8,128)(2,1)S(1)}, u32[]{:S(2)}, u32[]{:S(2)}) async-start(bf16[8,144,128]{2,1,0:T(8,128)(2,1)} %get-tuple-element.108), calls=%async_computation | async-start | bytes 589824 | tf_op jit(solution)/shard_map/all_to_all | solution.py:433
  13.5 2.0 collective-permute-start.1
  15.6 1.9 weights.1.intra_ref
  18.6 9.3 %all-to-all-done.in_ref = bf16[8,144,128]{2,1,0:T(8,128)(2,1)S(1)} async-done(((bf16[8,144,128]{2,1,0:T(8,128)(2,1)}), bf16[8,144,128]{2,1,0:T(8,128)(2,1)S(1)}, u32[]{:S(2)}, u32[]{:S(2)}) %all-to-all-start) | async-done | bytes 294944 | tf_op jit(solution)/shard_map/all_to_all | solution.py:433
  27.9 1.9 collective-permute-start.2
  30.6 5.8 %all-to-all-start.1 = ((bf16[8,128,128]{2,1,0:T(8,128)(2,1)}), bf16[8,128,128]{2,1,0:T(8,128)(2,1)S(1)}, u32[]{:S(2)}, u32[]{:S(2)}) async-start(bf16[8,128,128]{2,1,0:T(8,128)(2,1)} %copy-done.13), calls=%async_computation.1 | async-start | bytes 524288 | tf_op jit(solution)/shard_map/all_to_all | solution.py:441
  36.4 2.2 %fusion.order_ref = bf16[1024,1024]{1,0:T(8,128)(2,1)} fusion(s32[1024]{0:T(1024)S(1)} %fusion.4), kind=kLoop, calls=%fused_computation.1 | loop fusion | flops 2097152 | bytes 2101248 | tf_op jit(solution)/shard_map/convert_element_type | solution.py:363
  38.6 3.4 %collective-permute-done.1.refs_5_ = bf16[96,3072]{1,0:T(8,128)(2,1)} collective-permute-done((bf16[96,3072]{1,0:T(8,128)(2,1)}, bf16[96,3072]{1,0:T(8,128)(2,1)}, u32[]{:S(2)}, u32[]{:S(2)}) %collective-permute-start.1) | collective-permute-done | bytes 589856 | tf_op jit(solution)/shard_map/ppermute | solution.py:411
  42.0 3.3 %all-to-all-done.1.state_ref = bf16[8,128,128]{2,1,0:T(8,128)(2,1)S(1)} async-done(((bf16[8,128,128]{2,1,0:T(8,128)(2,1)}), bf16[8,128,128]{2,1,0:T(8,128)(2,1)S(1)}, u32[]{:S(2)}, u32[]{:S(2)}) %all-to-all-start.1) | async-done | bytes 262176 | tf_op jit(solution)/shard_map/all_to_all | solution.py:441
  46.8 1.5 collective-permute-start.7
  53.7 8.7 %collective-permute-done.9.refs_4_.refs_10_.refs_6_ = bf16[128,2048]{1,0:T(8,128)(2,1)S(1)} collective-permute-done((bf16[128,2048]{1,0:T(8,128)(2,1)S(1)}, bf16[128,2048]{1,0:T(8,128)(2,1)S(1)}, u32[]{:S(2)}, u32[]{:S(2)}) %collective-permute-start.9) | collective-permute-done | bytes 524320 | tf_op jit(solution)/shard_map/ppermute | solution.py:450
  63.0 2.7 %collective-permute-start.10 = (bf16[96,3072]{1,0:T(8,128)(2,1)}, bf16[96,3072]{1,0:T(8,128)(2,1)S(1)}, u32[]{:S(2)}, u32[]{:S(2)}) collective-permute-start(bf16[96,3072]{1,0:T(8,128)(2,1)} %collective-permute-done.1.refs_5_), channel_id=1, source_target_pairs={{0,8},{4,12},{8,24},{12,28},{24,16},{28,20},{16,0},{20,4},{1,9},{5... | collective-permute-start | bytes 1769480 | tf_op jit(solution)/shard_map/ppermute | solution.py:411
  65.7 1.5 collective-permute-start.11
  68.9 1.6 copy-done.1
  71.8 9.7 %collective-permute-done.14.refs_5_.refs_11_.refs_7_.refs_6_ = bf16[128,2048]{1,0:T(8,128)(2,1)S(1)} collective-permute-done((bf16[128,2048]{1,0:T(8,128)(2,1)S(1)}, bf16[128,2048]{1,0:T(8,128)(2,1)S(1)}, u32[]{:S(2)}, u32[]{:S(2)}) %collective-permute-start.14) | collective-permute-done | bytes 524320 | tf_op jit(solution)/shard_map/ppermute | solution.py:450
  84.5 5.9 %collective-permute-done.19.refs_1_ = bf16[384,256]{1,0:T(8,128)(2,1)S(1)} collective-permute-done((bf16[384,256]{1,0:T(8,128)(2,1)S(1)}, bf16[384,256]{1,0:T(8,128)(2,1)S(1)}, u32[]{:S(2)}, u32[]{:S(2)}) %collective-permute-start.19) | collective-permute-done | bytes 196640 | tf_op jit(solution)/shard_map/ppermute | solution.py:478
  91.8 9.5 %collective-permute-done.20.refs_6_.refs_12_.refs_7_ = bf16[128,2048]{1,0:T(8,128)(2,1)S(1)} collective-permute-done((bf16[128,2048]{1,0:T(8,128)(2,1)S(1)}, bf16[128,2048]{1,0:T(8,128)(2,1)S(1)}, u32[]{:S(2)}, u32[]{:S(2)}) %collective-permute-start.20) | collective-permute-done | bytes 524320 | tf_op jit(solution)/shard_map/ppermute | solution.py:450
  101.9 1.5 collective-permute-start.22
  103.6 2.7 %collective-permute-start.25 = (bf16[384,256]{1,0:T(8,128)(2,1)S(1)}, bf16[384,256]{1,0:T(8,128)(2,1)S(1)}, u32[]{:S(2)}, u32[]{:S(2)}) collective-permute-start(bf16[384,256]{1,0:T(8,128)(2,1)S(1)} %get-tuple-element.143), channel_id=1, source_target_pairs={{0,16},{4,20},{8,0},{12,4},{24,8},{28,12},{16,24},{20,28},{1,17},{... | collective-permute-start | bytes 589832 | tf_op jit(solution)/shard_map/ppermute | solution.py:484
  106.3 3.7 %product.5.refs_0_ = bf16[384,256]{1,0:T(8,128)(2,1)S(1)} custom-call(s32[1]{0:T(128)} %bitcast.1.mine_ref.refs_0_, bf16[384,6144]{1,0:T(8,128)(2,1)S(1)} %bitcast.6, bf16[384,6144]{1,0:T(8,128)(2,1)S(1)} %bitcast.6, bf16[128,6144]{1,0:T(8,128)(2,1)S(1)} %bitcast.8, bf16[128,2048]{1,0:T(8,128)(2,1)S(1)} %collective-permute-done.9.refs_4_.refs_10_.refs_6_, ...), custom_call_target="tpu_custom_call" | custom-call | flops 1000 | bytes 1000 | tf_op jit(solution)/shard_map/product/pallas_call | solution.py:216
  110.0 5.2 %product.6 = bf16[384,256]{1,0:T(8,128)(2,1)S(1)} custom-call(s32[1]{0:T(128)} %bitcast.1.mine_ref.refs_0_, bf16[96,3072]{1,0:T(8,128)(2,1)} %collective-permute-done.refs_1_.refs_5_, bf16[96,3072]{1,0:T(8,128)(2,1)S(1)} %collective-permute-done.4.refs_2_.refs_6_, bf16[96,3072]{1,0:T(8,128)(2,1)} %collective-permute-done.2.refs_3_.refs_7_, ...), custom_call_target="tpu_custom_call" | custom-call | flops 1000 | bytes 1000 | tf_op jit(solution)/shard_map/product/pallas_call | solution.py:216
  115.2 4.9 %collective-permute-done.25.refs_3_ = bf16[384,256]{1,0:T(8,128)(2,1)S(1)} collective-permute-done((bf16[384,256]{1,0:T(8,128)(2,1)S(1)}, bf16[384,256]{1,0:T(8,128)(2,1)S(1)}, u32[]{:S(2)}, u32[]{:S(2)}) %collective-permute-start.25) | collective-permute-done | bytes 196640 | tf_op jit(solution)/shard_map/ppermute | solution.py:484
  121.2 1.7 collective-permute-start.26
  124.1 3.8 %product.8 = bf16[384,256]{1,0:T(8,128)(2,1)S(1)} custom-call(s32[1]{0:T(128)} %bitcast.1.mine_ref.refs_0_, bf16[96,3072]{1,0:T(8,128)(2,1)S(1)} %collective-permute-done.6.refs_1_.refs_9_, bf16[96,3072]{1,0:T(8,128)(2,1)S(1)} %collective-permute-done.17.refs_2_.refs_10_, bf16[96,3072]{1,0:T(8,128)(2,1)S(1)} %collective-permute-done.11.refs_3_.refs_11_, ...), custom_call_target="tpu_custom_call" | custom-call | flops 1000 | bytes 1000 | tf_op jit(solution)/shard_map/product/pallas_call | solution.py:216
  128.1 1.8 product.7.refs_8_
  129.8 2.7 %collective-permute-done.29.refs_2_ = bf16[384,256]{1,0:T(8,128)(2,1)S(1)} collective-permute-done((bf16[384,256]{1,0:T(8,128)(2,1)S(1)}, bf16[384,256]{1,0:T(8,128)(2,1)S(1)}, u32[]{:S(2)}, u32[]{:S(2)}) %collective-permute-start.29) | collective-permute-done | bytes 196640 | tf_op jit(solution)/shard_map/ppermute | solution.py:496
  132.6 1.8 collective-permute-done.30.refs_1_
  134.4 2.1 %collective-permute-done.26.refs_3_.refs_15_ = bf16[96,3072]{1,0:T(8,128)(2,1)S(1)} collective-permute-done((bf16[96,3072]{1,0:T(8,128)(2,1)S(1)}, bf16[96,3072]{1,0:T(8,128)(2,1)S(1)}, u32[]{:S(2)}, u32[]{:S(2)}) %collective-permute-start.26) | collective-permute-done | bytes 589856 | tf_op jit(solution)/shard_map/ppermute | solution.py:414
  137.7 6.4 %outer.2 = (bf16[128,3072]{1,0:T(8,128)(2,1)S(1)}, bf16[128,3072]{1,0:T(8,128)(2,1)}) custom-call(bf16[384,256]{1,0:T(8,128)(2,1)S(1)} %get-tuple-element.176.refs_0_, bf16[384,256]{1,0:T(8,128)(2,1)S(1)} %collective-permute-done.19.refs_1_, bf16[384,256]{1,0:T(8,128)(2,1)S(1)} %collective-permute-done.29.refs_2_, ...), custom_call_target="tpu_custom_call" | custom-call | flops 1000 | bytes 1000 | tf_op jit(solution)/shard_map/outer/pallas_call | solution.py:260
  145.7 1.6 collective-permute-start.37
  147.3 1.7 product.9
  149.0 3.1 %collective-permute-start.34 = (bf16[384,256]{1,0:T(8,128)(2,1)S(1)}, bf16[384,256]{1,0:T(8,128)(2,1)S(1)}, u32[]{:S(2)}, u32[]{:S(2)}) collective-permute-start(bf16[384,256]{1,0:T(8,128)(2,1)S(1)} %product.9), channel_id=1, source_target_pairs={{0,8},{4,12},{8,24},{12,28},{24,16},{28,20},{16,0},{20,4},{1,9},{5... | collective-permute-start | bytes 589832 | tf_op jit(solution)/shard_map/ppermute | solution.py:512
  152.1 5.6 %outer.3 = (bf16[128,3072]{1,0:T(8,128)(2,1)S(1)}, bf16[128,3072]{1,0:T(8,128)(2,1)S(1)}) custom-call(bf16[384,256]{1,0:T(8,128)(2,1)S(1)} %get-tuple-element.176.refs_0_, bf16[384,256]{1,0:T(8,128)(2,1)S(1)} %collective-permute-done.19.refs_1_, bf16[384,256]{1,0:T(8,128)(2,1)S(1)} %collective-permute-done.29.refs_2_, ...), custom_call_target="tpu_custom_call" | custom-call | flops 1000 | bytes 1000 | tf_op jit(solution)/shard_map/outer/pallas_call | solution.py:260
  160.9 2.9 %collective-permute-done.36.there_ref = f32[1,384]{1,0:T(1,128)S(1)} collective-permute-done((f32[1,384]{1,0:T(1,128)S(1)}, f32[1,384]{1,0:T(1,128)S(1)}, u32[]{:S(2)}, u32[]{:S(2)}) %collective-permute-start.36) | collective-permute-done | bytes 1568 | tf_op jit(solution)/shard_map/ppermute | solution.py:414
  167.0 3.6 %all-to-all-start.2 = ((bf16[8,144,128]{2,1,0:T(8,128)(2,1)}), bf16[8,144,128]{2,1,0:T(8,128)(2,1)S(1)}, u32[]{:S(2)}, u32[]{:S(2)}) async-start(bf16[8,144,128]{2,1,0:T(8,128)(2,1)} %copy-done.20), calls=%async_computation.2 | async-start | bytes 589824 | tf_op jit(solution)/shard_map/all_to_all | solution.py:530
  170.6 2.0 collective-permute-start.38
  173.7 4.5 %inside.1 = (bf16[384,1024]{1,0:T(8,128)(2,1)}, bf16[2,384,1024]{2,1,0:T(8,128)(2,1)S(1)}) custom-call(bf16[384,1024]{1,0:T(8,128)(2,1)S(1)} %copy-done.19, bf16[384,1024]{1,0:T(8,128)(2,1)S(1)} %copy-done.8, bf16[384,1024]{1,0:T(8,128)(2,1)S(1)} %copy-done.3, bf16[384,1024]{1,0:T(8,128)(2,1)S(1)} %copy-done.5, f32[8,384]{1,0:T(8,128)S(1)} %get-tuple-element.109.run_ref, ...), custom_call_target="tpu_custom_call" | custom-call | flops 1000 | bytes 1000 | tf_op jit(solution)/shard_map/inside/pallas_call | solution.py:400
  182.0 4.2 %all-to-all-start.3 = ((bf16[8,128,128]{2,1,0:T(8,128)(2,1)}), bf16[8,128,128]{2,1,0:T(8,128)(2,1)S(1)}, u32[]{:S(2)}, u32[]{:S(2)}) async-start(bf16[8,128,128]{2,1,0:T(8,128)(2,1)} %scan.3), calls=%async_computation.3 | async-start | bytes 524288 | tf_op jit(solution)/shard_map/all_to_all | solution.py:543
  186.2 2.0 collective-permute-start.40
  188.3 2.8 %collective-permute-done.40 = f32[1,1024]{1,0:T(1,128)S(1)} collective-permute-done((f32[1,1024]{1,0:T(1,128)S(1)}, f32[1,1024]{1,0:T(1,128)S(1)}, u32[]{:S(2)}, u32[]{:S(2)}) %collective-permute-start.40) | collective-permute-done | bytes 4128 | tf_op jit(solution)/shard_map/ppermute | solution.py:547
  191.1 3.5 %collective-permute-start.41 = (f32[1,1024]{1,0:T(1,128)S(1)}, f32[1,1024]{1,0:T(1,128)S(1)}, u32[]{:S(2)}, u32[]{:S(2)}) collective-permute-start(f32[1,1024]{1,0:T(1,128)S(1)} %add.143), channel_id=1, source_target_pairs={{0,16},{4,20},{8,24},{12,28},{16,0},{20,4},{24,8},{28,12},{1,17},{... | collective-permute-start | bytes 12296 | tf_op jit(solution)/shard_map/ppermute | solution.py:547
  195.7 2.2 %sum.2.refs_0_ = bf16[128,6144]{1,0:T(8,128)(2,1)} custom-call(bf16[128,3072]{1,0:T(8,128)(2,1)S(1)} %copy-done.17, bf16[128,3072]{1,0:T(8,128)(2,1)} %collective-permute-done.37.refs_1_), custom_call_target="tpu_custom_call" | custom-call | flops 1000 | bytes 1000 | tf_op jit(solution)/shard_map/sum/pallas_call | solution.py:286
  198.5 2.0 all-to-all-done.3.state_ref
  201.9 2.0 outside.1
  204.0 2.2 %sum.3 = bf16[128,6144]{1,0:T(8,128)(2,1)} custom-call(bf16[128,6144]{1,0:T(8,128)(2,1)} %sum.2.refs_0_, bf16[128,3072]{1,0:T(8,128)(2,1)S(1)} %copy-done.15, bf16[128,3072]{1,0:T(8,128)(2,1)} %collective-permute-done.39.refs_2_), custom_call_target="tpu_custom_call", output_to_operand_aliasing={{}: (0, {})} | custom-call | flops 1000 | bytes 1000 | tf_op jit(solution)/shard_map/sum/pallas_call | solution.py:286
  (125 shorter events, 37.0 us)
Async XLA Ops:
  3.1 24.8 %collective-permute-start = (bf16[96,3072]{1,0:T(8,128)(2,1)}, bf16[96,3072]{1,0:T(8,128)(2,1)}, u32[]{:S(2)}, u32[]{:S(2)}) collective-permute-start(bf16[96,3072]{1,0:T(8,128)(2,1)} %get-tuple-element.212), channel_id=1, source_target_pairs={{0,8},{4,12},{8,24},{12,28},{24,16},{28,20},{16,0},{20,4},{1,9},{5... | collective-permute-start | bytes 1769480 | tf_op jit(solution)/shard_map/ppermute | solution.py:411
  8.7 19.2 %all-to-all-start = ((bf16[8,144,128]{2,1,0:T(8,128)(2,1)}), bf16[8,144,128]{2,1,0:T(8,128)(2,1)S(1)}, u32[]{:S(2)}, u32[]{:S(2)}) async-start(bf16[8,144,128]{2,1,0:T(8,128)(2,1)} %get-tuple-element.108), calls=%async_computation | async-start | bytes 589824 | tf_op jit(solution)/shard_map/all_to_all | solution.py:433
  13.5 28.5 %collective-permute-start.1 = (bf16[96,3072]{1,0:T(8,128)(2,1)}, bf16[96,3072]{1,0:T(8,128)(2,1)}, u32[]{:S(2)}, u32[]{:S(2)}) collective-permute-start(bf16[96,3072]{1,0:T(8,128)(2,1)} %get-tuple-element.112), channel_id=1, source_target_pairs={{0,8},{4,12},{8,24},{12,28},{24,16},{28,20},{16,0},{20,4},{1,9},{5... | collective-permute-start | bytes 1769480 | tf_op jit(solution)/shard_map/ppermute | solution.py:411
  15.6 90.7 %slice-start = ((s8[4718592]{0:T(1024)(128)(4,1)}), s8[524288]{0:T(1024)(128)(4,1)S(1)}, s32[]{:S(2)}) async-start(s8[4718592]{0:T(1024)(128)(4,1)} %bitcast.5), calls=%async_computation.4 | async-start | bytes 1048576
  27.9 17.4 %collective-permute-start.2 = (bf16[96,3072]{1,0:T(8,128)(2,1)}, bf16[96,3072]{1,0:T(8,128)(2,1)}, u32[]{:S(2)}, u32[]{:S(2)}) collective-permute-start(bf16[96,3072]{1,0:T(8,128)(2,1)} %collective-permute-done.refs_1_.refs_5_), channel_id=1, source_target_pairs={{0,2},{1,3},{2,0},{3,1},{4,6},{5,7},{6,4},{7,5},{8,10},{9,11},{10,... | collective-permute-start | bytes 1769480 | tf_op jit(solution)/shard_map/ppermute | solution.py:414
  30.6 14.8 %all-to-all-start.1 = ((bf16[8,128,128]{2,1,0:T(8,128)(2,1)}), bf16[8,128,128]{2,1,0:T(8,128)(2,1)S(1)}, u32[]{:S(2)}, u32[]{:S(2)}) async-start(bf16[8,128,128]{2,1,0:T(8,128)(2,1)} %copy-done.13), calls=%async_computation.1 | async-start | bytes 524288 | tf_op jit(solution)/shard_map/all_to_all | solution.py:441
  45.3 61.0 %slice-start.1 = ((s8[4718592]{0:T(1024)(128)(4,1)}), s8[4194304]{0:T(1024)(128)(4,1)S(1)}, s32[]{:S(2)}) async-start(s8[4718592]{0:T(1024)(128)(4,1)} %bitcast.5), calls=%async_computation.5 | async-start | bytes 8388608
  45.3 4.4 %collective-permute-start.4 = (bf16[96,3072]{1,0:T(8,128)(2,1)}, bf16[96,3072]{1,0:T(8,128)(2,1)S(1)}, u32[]{:S(2)}, u32[]{:S(2)}) collective-permute-start(bf16[96,3072]{1,0:T(8,128)(2,1)} %collective-permute-done.refs_1_.refs_5_), channel_id=1, source_target_pairs={{0,1},{1,0},{2,3},{3,2},{4,5},{5,4},{6,7},{7,6},{8,9},{9,8},{10,11... | collective-permute-start | bytes 1769480 | tf_op jit(solution)/shard_map/ppermute | solution.py:414
  45.4 17.6 %collective-permute-start.6 = (bf16[96,3072]{1,0:T(8,128)(2,1)}, bf16[96,3072]{1,0:T(8,128)(2,1)S(1)}, u32[]{:S(2)}, u32[]{:S(2)}) collective-permute-start(bf16[96,3072]{1,0:T(8,128)(2,1)} %collective-permute-done.refs_1_.refs_5_), channel_id=1, source_target_pairs={{0,8},{4,12},{8,24},{12,28},{24,16},{28,20},{16,0},{20,4},{1,9},{5... | collective-permute-start | bytes 1769480 | tf_op jit(solution)/shard_map/ppermute | solution.py:411
  46.6 3.0 %collective-permute-start.3 = (bf16[96,3072]{1,0:T(8,128)(2,1)}, bf16[96,3072]{1,0:T(8,128)(2,1)S(1)}, u32[]{:S(2)}, u32[]{:S(2)}) collective-permute-start(bf16[96,3072]{1,0:T(8,128)(2,1)} %collective-permute-done.2.refs_3_.refs_7_), channel_id=1, source_target_pairs={{0,1},{1,0},{2,3},{3,2},{4,5},{5,4},{6,7},{7,6},{8,9},{9,8},{10,11... | collective-permute-start | bytes 1769480 | tf_op jit(solution)/shard_map/ppermute | solution.py:414
  46.8 16.2 %collective-permute-start.7 = (bf16[96,3072]{1,0:T(8,128)(2,1)}, bf16[96,3072]{1,0:T(8,128)(2,1)S(1)}, u32[]{:S(2)}, u32[]{:S(2)}) collective-permute-start(bf16[96,3072]{1,0:T(8,128)(2,1)} %collective-permute-done.1.refs_5_), channel_id=1, source_target_pairs={{0,2},{1,3},{2,0},{3,1},{4,6},{5,7},{6,4},{7,5},{8,10},{9,11},{10,... | collective-permute-start | bytes 1769480 | tf_op jit(solution)/shard_map/ppermute | solution.py:414
  48.4 14.0 %collective-permute-start.9 = (bf16[128,2048]{1,0:T(8,128)(2,1)S(1)}, bf16[128,2048]{1,0:T(8,128)(2,1)S(1)}, u32[]{:S(2)}, u32[]{:S(2)}) collective-permute-start(bf16[128,2048]{1,0:T(8,128)(2,1)S(1)} %get-tuple-element.215), channel_id=1, source_target_pairs={{0,4},{4,0},{8,12},{12,8},{16,20},{20,16},{24,28},{28,24},{1,5},{5... | collective-permute-start | bytes 1572872 | tf_op jit(solution)/shard_map/ppermute | solution.py:450
  51.8 1.2 collective-permute-start.5
  53.0 9.9 %collective-permute-start.8 = (f32[1,384]{1,0:T(1,128)S(1)}, f32[1,384]{1,0:T(1,128)S(1)}, u32[]{:S(2)}, u32[]{:S(2)}) collective-permute-start(f32[1,384]{1,0:T(1,128)S(1)} %add.140.here_ref), channel_id=1, source_target_pairs={{0,2},{1,3},{2,0},{3,1},{4,6},{5,7},{6,4},{7,5},{8,10},{9,11},{10,... | collective-permute-start | bytes 4616 | tf_op jit(solution)/shard_map/ppermute | solution.py:414
  63.0 18.6 %collective-permute-start.10 = (bf16[96,3072]{1,0:T(8,128)(2,1)}, bf16[96,3072]{1,0:T(8,128)(2,1)S(1)}, u32[]{:S(2)}, u32[]{:S(2)}) collective-permute-start(bf16[96,3072]{1,0:T(8,128)(2,1)} %collective-permute-done.1.refs_5_), channel_id=1, source_target_pairs={{0,8},{4,12},{8,24},{12,28},{24,16},{28,20},{16,0},{20,4},{1,9},{5... | collective-permute-start | bytes 1769480 | tf_op jit(solution)/shard_map/ppermute | solution.py:411
  65.7 15.9 %collective-permute-start.12 = (bf16[96,3072]{1,0:T(8,128)(2,1)}, bf16[96,3072]{1,0:T(8,128)(2,1)S(1)}, u32[]{:S(2)}, u32[]{:S(2)}) collective-permute-start(bf16[96,3072]{1,0:T(8,128)(2,1)} %collective-permute-done.1.refs_5_), channel_id=1, source_target_pairs={{0,1},{1,0},{2,3},{3,2},{4,5},{5,4},{6,7},{7,6},{8,9},{9,8},{10,11... | collective-permute-start | bytes 1769480 | tf_op jit(solution)/shard_map/ppermute | solution.py:414
  65.7 15.9 %collective-permute-start.11 = (bf16[96,3072]{1,0:T(8,128)(2,1)S(1)}, bf16[96,3072]{1,0:T(8,128)(2,1)S(1)}, u32[]{:S(2)}, u32[]{:S(2)}) collective-permute-start(bf16[96,3072]{1,0:T(8,128)(2,1)S(1)} %collective-permute-done.6.refs_1_.refs_9_), channel_id=1, source_target_pairs={{0,2},{1,3},{2,0},{3,1},{4,6},{5,7},{6,4},{7,5},{8,10},{9,11},{10,... | collective-permute-start | bytes 1769480 | tf_op jit(solution)/shard_map/ppermute | solution.py:414
  67.2 14.4 %collective-permute-start.13 = (bf16[96,3072]{1,0:T(8,128)(2,1)S(1)}, bf16[96,3072]{1,0:T(8,128)(2,1)S(1)}, u32[]{:S(2)}, u32[]{:S(2)}) collective-permute-start(bf16[96,3072]{1,0:T(8,128)(2,1)S(1)} %collective-permute-done.7.refs_7_), channel_id=1, source_target_pairs={{0,1},{1,0},{2,3},{3,2},{4,5},{5,4},{6,7},{7,6},{8,9},{9,8},{10,11... | collective-permute-start | bytes 1769480 | tf_op jit(solution)/shard_map/ppermute | solution.py:414
  67.4 14.1 %collective-permute-start.14 = (bf16[128,2048]{1,0:T(8,128)(2,1)S(1)}, bf16[128,2048]{1,0:T(8,128)(2,1)S(1)}, u32[]{:S(2)}, u32[]{:S(2)}) collective-permute-start(bf16[128,2048]{1,0:T(8,128)(2,1)S(1)} %get-tuple-element.133), channel_id=1, source_target_pairs={{0,4},{4,0},{8,12},{12,8},{16,20},{20,16},{24,28},{28,24},{1,5},{5... | collective-permute-start | bytes 1572872 | tf_op jit(solution)/shard_map/ppermute | solution.py:450
  81.6 8.8 %collective-permute-start.19 = (bf16[384,256]{1,0:T(8,128)(2,1)S(1)}, bf16[384,256]{1,0:T(8,128)(2,1)S(1)}, u32[]{:S(2)}, u32[]{:S(2)}) collective-permute-start(bf16[384,256]{1,0:T(8,128)(2,1)S(1)} %get-tuple-element.138), channel_id=1, source_target_pairs={{0,8},{4,12},{8,24},{12,28},{24,16},{28,20},{16,0},{20,4},{1,9},{5... | collective-permute-start | bytes 589832 | tf_op jit(solution)/shard_map/ppermute | solution.py:478
  82.8 18.7 %collective-permute-start.15 = (bf16[96,3072]{1,0:T(8,128)(2,1)S(1)}, bf16[96,3072]{1,0:T(8,128)(2,1)S(1)}, u32[]{:S(2)}, u32[]{:S(2)}) collective-permute-start(bf16[96,3072]{1,0:T(8,128)(2,1)S(1)} %collective-permute-done.6.refs_1_.refs_9_), channel_id=1, source_target_pairs={{0,8},{4,12},{8,24},{12,28},{24,16},{28,20},{16,0},{20,4},{1,9},{5... | collective-permute-start | bytes 1769480 | tf_op jit(solution)/shard_map/ppermute | solution.py:411
  82.8 18.7 %collective-permute-start.17 = (bf16[96,3072]{1,0:T(8,128)(2,1)S(1)}, bf16[96,3072]{1,0:T(8,128)(2,1)S(1)}, u32[]{:S(2)}, u32[]{:S(2)}) collective-permute-start(bf16[96,3072]{1,0:T(8,128)(2,1)S(1)} %collective-permute-done.6.refs_1_.refs_9_), channel_id=1, source_target_pairs={{0,1},{1,0},{2,3},{3,2},{4,5},{5,4},{6,7},{7,6},{8,9},{9,8},{10,11... | collective-permute-start | bytes 1769480 | tf_op jit(solution)/shard_map/ppermute | solution.py:414
  82.8 18.7 %collective-permute-start.16 = (bf16[96,3072]{1,0:T(8,128)(2,1)S(1)}, bf16[96,3072]{1,0:T(8,128)(2,1)S(1)}, u32[]{:S(2)}, u32[]{:S(2)}) collective-permute-start(bf16[96,3072]{1,0:T(8,128)(2,1)S(1)} %collective-permute-done.10.refs_5_.refs_9_), channel_id=1, source_target_pairs={{0,2},{1,3},{2,0},{3,1},{4,6},{5,7},{6,4},{7,5},{8,10},{9,11},{10,... | collective-permute-start | bytes 1769480 | tf_op jit(solution)/shard_map/ppermute | solution.py:414
  84.3 17.2 %collective-permute-start.18 = (bf16[96,3072]{1,0:T(8,128)(2,1)S(1)}, bf16[96,3072]{1,0:T(8,128)(2,1)S(1)}, u32[]{:S(2)}, u32[]{:S(2)}) collective-permute-start(bf16[96,3072]{1,0:T(8,128)(2,1)S(1)} %collective-permute-done.11.refs_3_.refs_11_), channel_id=1, source_target_pairs={{0,1},{1,0},{2,3},{3,2},{4,5},{5,4},{6,7},{7,6},{8,9},{9,8},{10,11... | collective-permute-start | bytes 1769480 | tf_op jit(solution)/shard_map/ppermute | solution.py:414
  90.4 11.0 %collective-permute-start.20 = (bf16[128,2048]{1,0:T(8,128)(2,1)S(1)}, bf16[128,2048]{1,0:T(8,128)(2,1)S(1)}, u32[]{:S(2)}, u32[]{:S(2)}) collective-permute-start(bf16[128,2048]{1,0:T(8,128)(2,1)S(1)} %get-tuple-element.139), channel_id=1, source_target_pairs={{0,4},{4,0},{8,12},{12,8},{16,20},{20,16},{24,28},{28,24},{1,5},{5... | collective-permute-start | bytes 1572872 | tf_op jit(solution)/shard_map/ppermute | solution.py:450
  101.5 19.1 %collective-permute-start.21 = (bf16[96,3072]{1,0:T(8,128)(2,1)S(1)}, bf16[96,3072]{1,0:T(8,128)(2,1)S(1)}, u32[]{:S(2)}, u32[]{:S(2)}) collective-permute-start(bf16[96,3072]{1,0:T(8,128)(2,1)S(1)} %collective-permute-done.10.refs_5_.refs_9_), channel_id=1, source_target_pairs={{0,8},{4,12},{8,24},{12,28},{24,16},{28,20},{16,0},{20,4},{1,9},{5... | collective-permute-start | bytes 1769480 | tf_op jit(solution)/shard_map/ppermute | solution.py:411
  101.9 18.7 %collective-permute-start.23 = (bf16[96,3072]{1,0:T(8,128)(2,1)S(1)}, bf16[96,3072]{1,0:T(8,128)(2,1)S(1)}, u32[]{:S(2)}, u32[]{:S(2)}) collective-permute-start(bf16[96,3072]{1,0:T(8,128)(2,1)S(1)} %collective-permute-done.10.refs_5_.refs_9_), channel_id=1, source_target_pairs={{0,1},{1,0},{2,3},{3,2},{4,5},{5,4},{6,7},{7,6},{8,9},{9,8},{10,11... | collective-permute-start | bytes 1769480 | tf_op jit(solution)/shard_map/ppermute | solution.py:414
  101.9 18.7 %collective-permute-start.22 = (bf16[96,3072]{1,0:T(8,128)(2,1)S(1)}, bf16[96,3072]{1,0:T(8,128)(2,1)S(1)}, u32[]{:S(2)}, u32[]{:S(2)}) collective-permute-start(bf16[96,3072]{1,0:T(8,128)(2,1)S(1)} %collective-permute-done.15.refs_1_.refs_13_), channel_id=1, source_target_pairs={{0,2},{1,3},{2,0},{3,1},{4,6},{5,7},{6,4},{7,5},{8,10},{9,11},{10,... | collective-permute-start | bytes 1769480 | tf_op jit(solution)/shard_map/ppermute | solution.py:414
  103.4 17.2 %collective-permute-start.24 = (bf16[96,3072]{1,0:T(8,128)(2,1)S(1)}, bf16[96,3072]{1,0:T(8,128)(2,1)S(1)}, u32[]{:S(2)}, u32[]{:S(2)}) collective-permute-start(bf16[96,3072]{1,0:T(8,128)(2,1)S(1)} %collective-permute-done.16.refs_7_.refs_11_), channel_id=1, source_target_pairs={{0,1},{1,0},{2,3},{3,2},{4,5},{5,4},{6,7},{7,6},{8,9},{9,8},{10,11... | collective-permute-start | bytes 1769480 | tf_op jit(solution)/shard_map/ppermute | solution.py:414
  103.6 16.5 %collective-permute-start.25 = (bf16[384,256]{1,0:T(8,128)(2,1)S(1)}, bf16[384,256]{1,0:T(8,128)(2,1)S(1)}, u32[]{:S(2)}, u32[]{:S(2)}) collective-permute-start(bf16[384,256]{1,0:T(8,128)(2,1)S(1)} %get-tuple-element.143), channel_id=1, source_target_pairs={{0,16},{4,20},{8,0},{12,4},{24,8},{28,12},{16,24},{20,28},{1,17},{... | collective-permute-start | bytes 589832 | tf_op jit(solution)/shard_map/ppermute | solution.py:484
  120.6 7.4 %collective-permute-start.27 = (bf16[96,3072]{1,0:T(8,128)(2,1)S(1)}, bf16[96,3072]{1,0:T(8,128)(2,1)S(1)}, u32[]{:S(2)}, u32[]{:S(2)}) collective-permute-start(bf16[96,3072]{1,0:T(8,128)(2,1)S(1)} %collective-permute-done.15.refs_1_.refs_13_), channel_id=1, source_target_pairs={{0,1},{1,0},{2,3},{3,2},{4,5},{5,4},{6,7},{7,6},{8,9},{9,8},{10,11... | collective-permute-start | bytes 1769480 | tf_op jit(solution)/shard_map/ppermute | solution.py:414
  120.7 7.4 %collective-permute-start.28 = (bf16[96,3072]{1,0:T(8,128)(2,1)S(1)}, bf16[96,3072]{1,0:T(8,128)(2,1)S(1)}, u32[]{:S(2)}, u32[]{:S(2)}) collective-permute-start(bf16[96,3072]{1,0:T(8,128)(2,1)S(1)} %collective-permute-done.22.refs_3_.refs_15_), channel_id=1, source_target_pairs={{0,1},{1,0},{2,3},{3,2},{4,5},{5,4},{6,7},{7,6},{8,9},{9,8},{10,11... | collective-permute-start | bytes 1769480 | tf_op jit(solution)/shard_map/ppermute | solution.py:414
  121.2 15.3 %collective-permute-start.26 = (bf16[96,3072]{1,0:T(8,128)(2,1)S(1)}, bf16[96,3072]{1,0:T(8,128)(2,1)S(1)}, u32[]{:S(2)}, u32[]{:S(2)}) collective-permute-start(bf16[96,3072]{1,0:T(8,128)(2,1)S(1)} %collective-permute-done.21.refs_1_.refs_13_), channel_id=1, source_target_pairs={{0,2},{1,3},{2,0},{3,1},{4,6},{5,7},{6,4},{7,5},{8,10},{9,11},{10,... | collective-permute-start | bytes 1769480 | tf_op jit(solution)/shard_map/ppermute | solution.py:414
  122.9 9.7 %collective-permute-start.29 = (bf16[384,256]{1,0:T(8,128)(2,1)S(1)}, bf16[384,256]{1,0:T(8,128)(2,1)S(1)}, u32[]{:S(2)}, u32[]{:S(2)}) collective-permute-start(bf16[384,256]{1,0:T(8,128)(2,1)S(1)} %get-tuple-element.154), channel_id=1, source_target_pairs={{0,24},{4,28},{8,16},{12,20},{24,0},{28,4},{16,8},{20,12},{1,25},{... | collective-permute-start | bytes 589832 | tf_op jit(solution)/shard_map/ppermute | solution.py:496
  123.9 10.5 %collective-permute-start.30 = (bf16[384,256]{1,0:T(8,128)(2,1)S(1)}, bf16[384,256]{1,0:T(8,128)(2,1)S(1)}, u32[]{:S(2)}, u32[]{:S(2)}) collective-permute-start(bf16[384,256]{1,0:T(8,128)(2,1)S(1)} %product.6), channel_id=1, source_target_pairs={{0,16},{4,20},{8,0},{12,4},{24,8},{28,12},{16,24},{20,28},{1,17},{... | collective-permute-start | bytes 589832 | tf_op jit(solution)/shard_map/ppermute | solution.py:497
  128.0 17.7 %collective-permute-start.32 = (bf16[96,3072]{1,0:T(8,128)(2,1)S(1)}, bf16[96,3072]{1,0:T(8,128)(2,1)S(1)}, u32[]{:S(2)}, u32[]{:S(2)}) collective-permute-start(bf16[96,3072]{1,0:T(8,128)(2,1)S(1)} %collective-permute-done.21.refs_1_.refs_13_), channel_id=1, source_target_pairs={{0,1},{1,0},{2,3},{3,2},{4,5},{5,4},{6,7},{7,6},{8,9},{9,8},{10,11... | collective-permute-start | bytes 1769480 | tf_op jit(solution)/shard_map/ppermute | solution.py:414
  136.5 9.2 %collective-permute-start.31 = (bf16[96,3072]{1,0:T(8,128)(2,1)S(1)}, bf16[96,3072]{1,0:T(8,128)(2,1)S(1)}, u32[]{:S(2)}, u32[]{:S(2)}) collective-permute-start(bf16[96,3072]{1,0:T(8,128)(2,1)S(1)} %collective-permute-done.26.refs_3_.refs_15_), channel_id=1, source_target_pairs={{0,1},{1,0},{2,3},{3,2},{4,5},{5,4},{6,7},{7,6},{8,9},{9,8},{10,11... | collective-permute-start | bytes 1769480 | tf_op jit(solution)/shard_map/ppermute | solution.py:414
  136.5 9.2 %collective-permute-start.33 = (bf16[384,256]{1,0:T(8,128)(2,1)S(1)}, bf16[384,256]{1,0:T(8,128)(2,1)S(1)}, u32[]{:S(2)}, u32[]{:S(2)}) collective-permute-start(bf16[384,256]{1,0:T(8,128)(2,1)S(1)} %product.8), channel_id=1, source_target_pairs={{0,24},{4,28},{8,16},{12,20},{24,0},{28,4},{16,8},{20,12},{1,25},{... | collective-permute-start | bytes 589832 | tf_op jit(solution)/shard_map/ppermute | solution.py:501
  145.7 34.0 %collective-permute-start.37 = (bf16[128,3072]{1,0:T(8,128)(2,1)}, bf16[128,3072]{1,0:T(8,128)(2,1)}, u32[]{:S(2)}, u32[]{:S(2)}) collective-permute-start(bf16[128,3072]{1,0:T(8,128)(2,1)} %get-tuple-element.195), channel_id=1, source_target_pairs={{0,4},{4,0},{8,12},{12,8},{16,20},{20,16},{24,28},{28,24},{1,5},{5... | collective-permute-start | bytes 2359304 | tf_op jit(solution)/shard_map/ppermute | solution.py:514
  149.0 8.8 %collective-permute-start.34 = (bf16[384,256]{1,0:T(8,128)(2,1)S(1)}, bf16[384,256]{1,0:T(8,128)(2,1)S(1)}, u32[]{:S(2)}, u32[]{:S(2)}) collective-permute-start(bf16[384,256]{1,0:T(8,128)(2,1)S(1)} %product.9), channel_id=1, source_target_pairs={{0,8},{4,12},{8,24},{12,28},{24,16},{28,20},{16,0},{20,4},{1,9},{5... | collective-permute-start | bytes 589832 | tf_op jit(solution)/shard_map/ppermute | solution.py:512
  159.0 1.2 collective-permute-start.35
  160.2 3.6 %collective-permute-start.36 = (f32[1,384]{1,0:T(1,128)S(1)}, f32[1,384]{1,0:T(1,128)S(1)}, u32[]{:S(2)}, u32[]{:S(2)}) collective-permute-start(f32[1,384]{1,0:T(1,128)S(1)} %add.141.here_ref), channel_id=1, source_target_pairs={{0,2},{1,3},{2,0},{3,1},{4,6},{5,7},{6,4},{7,5},{8,10},{9,11},{10,... | collective-permute-start | bytes 4616 | tf_op jit(solution)/shard_map/ppermute | solution.py:414
  167.0 12.8 %all-to-all-start.2 = ((bf16[8,144,128]{2,1,0:T(8,128)(2,1)}), bf16[8,144,128]{2,1,0:T(8,128)(2,1)S(1)}, u32[]{:S(2)}, u32[]{:S(2)}) async-start(bf16[8,144,128]{2,1,0:T(8,128)(2,1)} %copy-done.20), calls=%async_computation.2 | async-start | bytes 589824 | tf_op jit(solution)/shard_map/all_to_all | solution.py:530
  170.6 8.8 %collective-permute-start.38 = (f32[1,1024]{1,0:T(1,128)S(1)}, f32[1,1024]{1,0:T(1,128)S(1)}, u32[]{:S(2)}, u32[]{:S(2)}) collective-permute-start(f32[1,1024]{1,0:T(1,128)S(1)} %get-tuple-element.197), channel_id=1, source_target_pairs={{0,4},{4,0},{8,12},{12,8},{16,20},{20,16},{24,28},{28,24},{1,5},{5... | collective-permute-start | bytes 12296 | tf_op jit(solution)/shard_map/ppermute | solution.py:533
  179.8 24.2 %collective-permute-start.39 = (bf16[128,3072]{1,0:T(8,128)(2,1)}, bf16[128,3072]{1,0:T(8,128)(2,1)}, u32[]{:S(2)}, u32[]{:S(2)}) collective-permute-start(bf16[128,3072]{1,0:T(8,128)(2,1)} %copy-done.23), channel_id=1, source_target_pairs={{0,4},{4,0},{8,12},{12,8},{16,20},{20,16},{24,28},{28,24},{1,5},{5... | collective-permute-start | bytes 2359304 | tf_op jit(solution)/shard_map/ppermute | solution.py:540
  182.0 18.5 %all-to-all-start.3 = ((bf16[8,128,128]{2,1,0:T(8,128)(2,1)}), bf16[8,128,128]{2,1,0:T(8,128)(2,1)S(1)}, u32[]{:S(2)}, u32[]{:S(2)}) async-start(bf16[8,128,128]{2,1,0:T(8,128)(2,1)} %scan.3), calls=%async_computation.3 | async-start | bytes 524288 | tf_op jit(solution)/shard_map/all_to_all | solution.py:543
  186.2 4.8 %collective-permute-start.40 = (f32[1,1024]{1,0:T(1,128)S(1)}, f32[1,1024]{1,0:T(1,128)S(1)}, u32[]{:S(2)}, u32[]{:S(2)}) collective-permute-start(f32[1,1024]{1,0:T(1,128)S(1)} %add.142), channel_id=1, source_target_pairs={{0,8},{4,12},{8,0},{12,4},{16,24},{20,28},{24,16},{28,20},{1,9},{5... | collective-permute-start | bytes 12296 | tf_op jit(solution)/shard_map/ppermute | solution.py:547
  191.1 6.8 %collective-permute-start.41 = (f32[1,1024]{1,0:T(1,128)S(1)}, f32[1,1024]{1,0:T(1,128)S(1)}, u32[]{:S(2)}, u32[]{:S(2)}) collective-permute-start(f32[1,1024]{1,0:T(1,128)S(1)} %add.143), channel_id=1, source_target_pairs={{0,16},{4,20},{8,24},{12,28},{16,0},{20,4},{24,8},{28,12},{1,17},{... | collective-permute-start | bytes 12296 | tf_op jit(solution)/shard_map/ppermute | solution.py:547
  (24 other events, 130.2 us)

commit v13 on v12

--- a/solution.py
+++ b/solution.py
@@ -233,60 +233,81 @@
     )(mine, *[p for lot in lots for p in lot], weight, *[w for ws in others for w in ws], *more)
 
 
-def outer_kernel(lots, own, *refs):
+def outer_kernel(lots, own, cuts, *refs):
     refs = list(refs)
-    normed = [refs.pop(0) for _ in lots]
-    x = [[refs.pop(0) for _ in range(k)] for k in lots]
+    normed = [refs.pop(0) for _ in range(LINE)]
+    x = [refs.pop(0) for _ in range(lots)]
     turned_ref = refs.pop()
-
-    @pl.when(pl.program_id(0) == 0)
+    step = pl.program_id(0)
+    minor = len(refs) // (len(cuts) - 1)
+
+    @pl.when(step == 0)
     def _():
         turned_ref[...] = jnp.concatenate([r[...] for r in normed], axis=0).T
 
-    rows = jnp.concatenate([r[...] for lot in x for r in lot], axis=0)
+    rows = jnp.concatenate([r[...] for r in x], axis=0)
     out = dot(turned_ref[...], rows, NN).astype(BF)
-    for s, ref in enumerate(refs):
-        ref[...] = out[s * own : (s + 1) * own]
-
-
-def outer(normed, grad_out, lots, chunk, own):
+    for h in range(len(cuts) - 1):
+
+        @pl.when((step >= cuts[h]) & (step < cuts[h + 1]))
+        def _():
+            for s in range(minor):
+                refs[h * minor + s][...] = out[s * own : (s + 1) * own]
+
+
+def outer(normed, grad_out, lots, chunk, own, cuts):
     tok, span = normed[0].shape
     deep = lots[0][0].shape[1]
-    tile = 512
-    steps = deep // tile
+    steps = cuts[-1]
+    tile = deep // steps
     base = chunk * steps
     flat = [p for lot in lots for p in lot]
     minor = span // own
-    return pl.pallas_call(
-        functools.partial(outer_kernel, [1] + [len(lot) for lot in lots], own),
+    pairs = list(zip(cuts[:-1], cuts[1:]))
+
+    def out_spec(low, high):
+        return spec((own, tile), lambda i: (0, jnp.clip(i - low, 0, high - low - 1)))
+
+    outs = pl.pallas_call(
+        functools.partial(outer_kernel, 1 + len(flat), own, cuts),
         grid=(steps,),
         in_specs=[spec((tok, span)) for _ in normed]
         + [spec((tok, tile), lambda i: (0, base + i))]
         + [spec((p.shape[0], tile), lambda i: (0, i)) for p in flat],
-        out_specs=[spec((own, tile), lambda i: (0, i))] * minor,
-        out_shape=[jax.ShapeDtypeStruct((own, deep), BF)] * minor,
+        out_specs=[out_spec(*p) for p in pairs for _ in range(minor)],
+        out_shape=[
+            jax.ShapeDtypeStruct((own, (high - low) * tile), BF)
+            for low, high in pairs
+            for _ in range(minor)
+        ],
         scratch_shapes=[pltpu.VMEM((span, tok * LINE), BF)],
         compiler_params=PARAMS,
         cost_estimate=TINY,
         name="outer",
     )(*normed, grad_out, *flat)
-
-
-def half_kernel(skip, *refs):
+    return [list(outs[h * minor : (h + 1) * minor]) for h in range(len(pairs))]
+
+
+def half_kernel(skip, minor, *refs):
     parts, out_ref = refs[skip:-1], refs[-1]
-    total = parts[0][...].astype(FL)
-    for ref in parts[1:]:
-        total = total + ref[...].astype(FL)
-    out_ref[...] = total.astype(BF)
-
-
-def add_half(parts, at, model, into=None):
-    own, deep = parts[0].shape
+    at = 0
+    for c in range(0, len(parts), minor):
+        total = parts[c][...].astype(FL)
+        for ref in parts[c + 1 : c + minor]:
+            total = total + ref[...].astype(FL)
+        out_ref[:, at : at + total.shape[1]] = total.astype(BF)
+        at += total.shape[1]
+
+
+def add_half(groups, at, model, into=None):
+    own = groups[0][0].shape[0]
+    parts = [p for group in groups for p in group]
+    deep = model // CHUNKS
     more = [] if into is None else [into]
     return pl.pallas_call(
-        functools.partial(half_kernel, len(more)),
+        functools.partial(half_kernel, len(more), len(groups[0])),
         grid=(1,),
-        in_specs=[pl.BlockSpec(memory_space=pl.ANY)] * len(more) + [spec((own, deep))] * len(parts),
+        in_specs=[pl.BlockSpec(memory_space=pl.ANY)] * len(more) + [spec(p.shape) for p in parts],
         out_specs=spec((own, deep), lambda i: (0, at)),
         out_shape=jax.ShapeDtypeStruct((own, model), BF),
         input_output_aliases={0: 0} if more else {},
@@ -505,7 +526,7 @@
 
     fb3, nb3 = near_of(yb3), near_of(rb3)
     lots = [[ra1, na1, ya1, fa1], [ra2, na2, ya2, fa2], last_lot]
-    early = outer(normed, grad_out, lots, 0, own)
+    (early,) = outer(normed, grad_out, lots, 0, own, (0, 6))
     fb3, nb3, three, early, returned = hold((fb3, nb3, three, early, returned))
     last_lot = [rb3, nb3, yb3, fb3]
     three = product(tokens, [last_lot], weight_own, others, 1, True, three)
@@ -513,7 +534,7 @@
     flat = [early[0]]
     flat += [lax.ppermute(early[s], "ctx", pair_perm(count, s)) for s in range(1, minor)]
     lots = [[rb1, nb1, yb1, fb1], [rb2, nb2, yb2, fb2], last_lot]
-    late = outer([after(normed[0], three)] + normed[1:], grad_out, lots, 1, own)
+    late = outer([after(normed[0], three)] + normed[1:], grad_out, lots, 1, own, (0, 2, 6))
     returned, late = hold((returned, late))
 
     grad, gain_sum, inner = whole(
@@ -531,14 +552,22 @@
     gain_sum, late, grad_attn = hold((gain_sum, late, grad_attn))
     flips = [1 << i for i in range(count.bit_length() - 1)]
     gain_sum = gain_sum + lax.ppermute(gain_sum, "ctx", [(i, i ^ 1) for i in range(count)])
+
+    def leave(parts):
+        return [parts[0]] + [
+            lax.ppermute(parts[s], "ctx", pair_perm(count, s)) for s in range(1, minor)
+        ]
+
+    rest = [leave(late[0])]
     grad_query, inside = whole(
         inside_kernel, [wide_b, jax.ShapeDtypeStruct((2, tok, width), BF)], "inside",
         grad_attn, query_rows, key_rows, value_rows, run, turned, state_low,
     )
-    spread, flat, inside, gain_sum, late = hold((spread, flat, inside, gain_sum, late))
-    rest = [late[0]]
-    rest += [lax.ppermute(late[s], "ctx", pair_perm(count, s)) for s in range(1, minor)]
-    grad_weight = add_half(flat, 0, model)
+    spread, flat, inside, gain_sum, late, rest = hold(
+        (spread, flat, inside, gain_sum, late, rest)
+    )
+    rest.append(leave(late[1]))
+    grad_weight = add_half([flat], 0, model)
     states = whole(functools.partial(scan_kernel, True), scan_shape, "scan", spread)
     back_low = lax.all_to_all(states, "ctx", 0, 0, tiled=True)
     back_low, grad_weight = hold((back_low, grad_weight))

time: 207 us -> 208 us (level)
    unnamed x52 -> x62, local copies, waits for them, and re-layouts: 12.2 us -> 12 us
  transfers between devices with their start and end apart: 46 -> 47, of which waited for: 21 -> 20; matrix products, arithmetic and copies ran while one was open for 1% -> 1% of each run, Pallas kernels for 23% -> 23%
where the time goes in v13:
time: 208 us; the launch traced here: 207 us
  waiting for transfers between devices  74.4 us (36%)
  starting transfers between devices  64.8 us (31%)
  Pallas kernels  49.5 us (24%)
  local copies, waits for them, and re-layouts  14.6 us (7%)
  other arithmetic  2.82 us (1%)
    ppermute x3, waiting for transfers between devices, swap(): lax.ppermute(part, 'ctx', pair_perm(count, -s))  27.9 us
    pallas_call x10, Pallas kernels, whole(): pl.pallas_call(kernel, in_specs=[SCALAR if a is tokens else full for a in...  16.5 us
    pallas_call x5, Pallas kernels, product(): pl.pallas_call(functools.partial(product_kernel, [len(x) for x in lots],...  16.2 us
    ppermute x22, starting transfers between devices, over(): return lax.ppermute(x, 'head', perm)  12.7 us
    pallas_call x2, Pallas kernels, outer(): pl.pallas_call(functools.partial(outer_kernel, 1 + len(flat), own, cuts),...  12.5 us
    unnamed x62, local copies, waits for them, and re-layouts  12 us
    ppermute x6, starting transfers between devices, ring(): return lax.ppermute(x, 'ctx', ring_perm(count, 1))  9.41 us
    all_to_all x1, waiting for transfers between devices, shards(): spread = lax.all_to_all(put, 'ctx', 0, 0, tiled=True)  9.3 us
  transfers between devices with their start and end apart: 47, of which 20 were waited for; matrix products, arithmetic and copies ran while one was open for 1% of the time, Pallas kernels for 23%

profile of v13, /device:TPU:0, one launch (start us, length us, event | category | flops | bytes accessed | tf_op | source)
XLA Modules:
  0.0 207.1 jit_solution(8431451223606321478)
XLA Ops:
  0.7 2.4 %constant_dynamic-slice_fusion = (bf16[96,3072]{1,0:T(8,128)(2,1)}, bf16[96,3072]{1,0:T(8,128)(2,1)}) fusion(bf16[384,6144]{1,0:T(8,128)(2,1)} %refs_4_.3, s32[]{:T(128)S(6)} %select_n.84), kind=kLoop, calls=%fused_computation.46 | loop fusion | bytes 2359300 | tf_op jit(solution)/shard_map/dynamic_slice | solution.py:410
  3.1 3.0 %collective-permute-start = (bf16[96,3072]{1,0:T(8,128)(2,1)}, bf16[96,3072]{1,0:T(8,128)(2,1)}, u32[]{:S(2)}, u32[]{:S(2)}) collective-permute-start(bf16[96,3072]{1,0:T(8,128)(2,1)} %get-tuple-element.228), channel_id=1, source_target_pairs={{0,8},{4,12},{8,24},{12,28},{24,16},{28,20},{16,0},{20,4},{1,9},{5... | collective-permute-start | bytes 1769480 | tf_op jit(solution)/shard_map/ppermute | solution.py:432
  6.2 2.6 %states.1 = (bf16[8,144,128]{2,1,0:T(8,128)(2,1)}, f32[8,384]{1,0:T(8,128)S(1)}, f32[384,8]{1,0:T(8,128)S(1)}) custom-call(f32[8,384]{1,0:T(8,128)S(1)} %copy-done.26, bf16[384,1024]{1,0:T(8,128)(2,1)S(1)} %copy-done.3, bf16[384,1024]{1,0:T(8,128)(2,1)S(1)} %copy-done.4), custom_call_target="tpu_custom_call" | custom-call | flops 1000 | bytes 1000 | tf_op jit(solution)/shard_map/states/pallas_call | solution.py:421
  8.7 4.8 %all-to-all-start = ((bf16[8,144,128]{2,1,0:T(8,128)(2,1)}), bf16[8,144,128]{2,1,0:T(8,128)(2,1)S(1)}, u32[]{:S(2)}, u32[]{:S(2)}) async-start(bf16[8,144,128]{2,1,0:T(8,128)(2,1)} %get-tuple-element.116), calls=%async_computation | async-start | bytes 589824 | tf_op jit(solution)/shard_map/all_to_all | solution.py:454
  13.5 2.0 collective-permute-start.1
  15.6 1.9 weights.1.intra_ref
  18.6 9.3 %all-to-all-done.in_ref = bf16[8,144,128]{2,1,0:T(8,128)(2,1)S(1)} async-done(((bf16[8,144,128]{2,1,0:T(8,128)(2,1)}), bf16[8,144,128]{2,1,0:T(8,128)(2,1)S(1)}, u32[]{:S(2)}, u32[]{:S(2)}) %all-to-all-start) | async-done | bytes 294944 | tf_op jit(solution)/shard_map/all_to_all | solution.py:454
  27.9 1.9 collective-permute-start.2
  30.6 5.8 %all-to-all-start.1 = ((bf16[8,128,128]{2,1,0:T(8,128)(2,1)}), bf16[8,128,128]{2,1,0:T(8,128)(2,1)S(1)}, u32[]{:S(2)}, u32[]{:S(2)}) async-start(bf16[8,128,128]{2,1,0:T(8,128)(2,1)} %copy-done.13), calls=%async_computation.1 | async-start | bytes 524288 | tf_op jit(solution)/shard_map/all_to_all | solution.py:462
  36.4 2.2 %fusion.order_ref = bf16[1024,1024]{1,0:T(8,128)(2,1)} fusion(s32[1024]{0:T(1024)S(1)} %fusion.4), kind=kLoop, calls=%fused_computation.1 | loop fusion | flops 2097152 | bytes 2101248 | tf_op jit(solution)/shard_map/convert_element_type | solution.py:384
  38.6 3.5 %collective-permute-done.1.refs_5_ = bf16[96,3072]{1,0:T(8,128)(2,1)} collective-permute-done((bf16[96,3072]{1,0:T(8,128)(2,1)}, bf16[96,3072]{1,0:T(8,128)(2,1)}, u32[]{:S(2)}, u32[]{:S(2)}) %collective-permute-start.1) | collective-permute-done | bytes 589856 | tf_op jit(solution)/shard_map/ppermute | solution.py:432
  42.0 3.3 %all-to-all-done.1.state_ref = bf16[8,128,128]{2,1,0:T(8,128)(2,1)S(1)} async-done(((bf16[8,128,128]{2,1,0:T(8,128)(2,1)}), bf16[8,128,128]{2,1,0:T(8,128)(2,1)S(1)}, u32[]{:S(2)}, u32[]{:S(2)}) %all-to-all-start.1) | async-done | bytes 262176 | tf_op jit(solution)/shard_map/all_to_all | solution.py:462
  46.8 1.5 collective-permute-start.7
  53.7 8.7 %collective-permute-done.9.refs_4_.refs_10_.refs_6_ = bf16[128,2048]{1,0:T(8,128)(2,1)S(1)} collective-permute-done((bf16[128,2048]{1,0:T(8,128)(2,1)S(1)}, bf16[128,2048]{1,0:T(8,128)(2,1)S(1)}, u32[]{:S(2)}, u32[]{:S(2)}) %collective-permute-start.9) | collective-permute-done | bytes 524320 | tf_op jit(solution)/shard_map/ppermute | solution.py:471
  63.0 2.7 %collective-permute-start.10 = (bf16[96,3072]{1,0:T(8,128)(2,1)}, bf16[96,3072]{1,0:T(8,128)(2,1)S(1)}, u32[]{:S(2)}, u32[]{:S(2)}) collective-permute-start(bf16[96,3072]{1,0:T(8,128)(2,1)} %collective-permute-done.1.refs_5_), channel_id=1, source_target_pairs={{0,8},{4,12},{8,24},{12,28},{24,16},{28,20},{16,0},{20,4},{1,9},{5... | collective-permute-start | bytes 1769480 | tf_op jit(solution)/shard_map/ppermute | solution.py:432
  65.7 1.5 collective-permute-start.11
  68.9 1.6 copy-done.1
  71.8 9.7 %collective-permute-done.14.refs_5_.refs_11_.refs_7_.refs_6_ = bf16[128,2048]{1,0:T(8,128)(2,1)S(1)} collective-permute-done((bf16[128,2048]{1,0:T(8,128)(2,1)S(1)}, bf16[128,2048]{1,0:T(8,128)(2,1)S(1)}, u32[]{:S(2)}, u32[]{:S(2)}) %collective-permute-start.14) | collective-permute-done | bytes 524320 | tf_op jit(solution)/shard_map/ppermute | solution.py:471
  84.5 5.9 %collective-permute-done.19.refs_1_ = bf16[384,256]{1,0:T(8,128)(2,1)S(1)} collective-permute-done((bf16[384,256]{1,0:T(8,128)(2,1)S(1)}, bf16[384,256]{1,0:T(8,128)(2,1)S(1)}, u32[]{:S(2)}, u32[]{:S(2)}) %collective-permute-start.19) | collective-permute-done | bytes 196640 | tf_op jit(solution)/shard_map/ppermute | solution.py:499
  91.8 9.5 %collective-permute-done.20.refs_6_.refs_12_.refs_7_ = bf16[128,2048]{1,0:T(8,128)(2,1)S(1)} collective-permute-done((bf16[128,2048]{1,0:T(8,128)(2,1)S(1)}, bf16[128,2048]{1,0:T(8,128)(2,1)S(1)}, u32[]{:S(2)}, u32[]{:S(2)}) %collective-permute-start.20) | collective-permute-done | bytes 524320 | tf_op jit(solution)/shard_map/ppermute | solution.py:471
  101.9 1.5 collective-permute-start.22
  103.6 2.7 %collective-permute-start.25 = (bf16[384,256]{1,0:T(8,128)(2,1)S(1)}, bf16[384,256]{1,0:T(8,128)(2,1)S(1)}, u32[]{:S(2)}, u32[]{:S(2)}) collective-permute-start(bf16[384,256]{1,0:T(8,128)(2,1)S(1)} %get-tuple-element.151), channel_id=1, source_target_pairs={{0,16},{4,20},{8,0},{12,4},{24,8},{28,12},{16,24},{20,28},{1,17},{... | collective-permute-start | bytes 589832 | tf_op jit(solution)/shard_map/ppermute | solution.py:505
  106.3 3.7 %product.5.refs_0_ = bf16[384,256]{1,0:T(8,128)(2,1)S(1)} custom-call(s32[1]{0:T(128)} %bitcast.1.mine_ref.refs_0_, bf16[384,6144]{1,0:T(8,128)(2,1)S(1)} %bitcast.6, bf16[384,6144]{1,0:T(8,128)(2,1)S(1)} %bitcast.6, bf16[128,6144]{1,0:T(8,128)(2,1)S(1)} %bitcast.8, bf16[128,2048]{1,0:T(8,128)(2,1)S(1)} %collective-permute-done.9.refs_4_.refs_10_.refs_6_, ...), custom_call_target="tpu_custom_call" | custom-call | flops 1000 | bytes 1000 | tf_op jit(solution)/shard_map/product/pallas_call | solution.py:216
  110.0 5.2 %product.6 = bf16[384,256]{1,0:T(8,128)(2,1)S(1)} custom-call(s32[1]{0:T(128)} %bitcast.1.mine_ref.refs_0_, bf16[96,3072]{1,0:T(8,128)(2,1)} %collective-permute-done.refs_1_.refs_5_, bf16[96,3072]{1,0:T(8,128)(2,1)S(1)} %collective-permute-done.4.refs_2_.refs_6_, bf16[96,3072]{1,0:T(8,128)(2,1)} %collective-permute-done.2.refs_3_.refs_7_, ...), custom_call_target="tpu_custom_call" | custom-call | flops 1000 | bytes 1000 | tf_op jit(solution)/shard_map/product/pallas_call | solution.py:216
  115.2 4.9 %collective-permute-done.25.refs_3_ = bf16[384,256]{1,0:T(8,128)(2,1)S(1)} collective-permute-done((bf16[384,256]{1,0:T(8,128)(2,1)S(1)}, bf16[384,256]{1,0:T(8,128)(2,1)S(1)}, u32[]{:S(2)}, u32[]{:S(2)}) %collective-permute-start.25) | collective-permute-done | bytes 196640 | tf_op jit(solution)/shard_map/ppermute | solution.py:505
  121.2 1.7 collective-permute-start.26
  124.1 3.8 %product.8 = bf16[384,256]{1,0:T(8,128)(2,1)S(1)} custom-call(s32[1]{0:T(128)} %bitcast.1.mine_ref.refs_0_, bf16[96,3072]{1,0:T(8,128)(2,1)S(1)} %collective-permute-done.6.refs_1_.refs_9_, bf16[96,3072]{1,0:T(8,128)(2,1)S(1)} %collective-permute-done.17.refs_2_.refs_10_, bf16[96,3072]{1,0:T(8,128)(2,1)S(1)} %collective-permute-done.11.refs_3_.refs_11_, ...), custom_call_target="tpu_custom_call" | custom-call | flops 1000 | bytes 1000 | tf_op jit(solution)/shard_map/product/pallas_call | solution.py:216
  128.1 1.8 product.7.refs_8_
  129.8 2.7 %collective-permute-done.29.refs_2_ = bf16[384,256]{1,0:T(8,128)(2,1)S(1)} collective-permute-done((bf16[384,256]{1,0:T(8,128)(2,1)S(1)}, bf16[384,256]{1,0:T(8,128)(2,1)S(1)}, u32[]{:S(2)}, u32[]{:S(2)}) %collective-permute-start.29) | collective-permute-done | bytes 196640 | tf_op jit(solution)/shard_map/ppermute | solution.py:517
  132.6 1.8 collective-permute-done.30.refs_1_
  134.4 2.1 %collective-permute-done.26.refs_3_.refs_15_ = bf16[96,3072]{1,0:T(8,128)(2,1)S(1)} collective-permute-done((bf16[96,3072]{1,0:T(8,128)(2,1)S(1)}, bf16[96,3072]{1,0:T(8,128)(2,1)S(1)}, u32[]{:S(2)}, u32[]{:S(2)}) %collective-permute-start.26) | collective-permute-done | bytes 589856 | tf_op jit(solution)/shard_map/ppermute | solution.py:435
  137.7 6.5 %outer.2 = (bf16[128,3072]{1,0:T(8,128)(2,1)S(1)}, bf16[128,3072]{1,0:T(8,128)(2,1)}) custom-call(bf16[384,256]{1,0:T(8,128)(2,1)S(1)} %get-tuple-element.184.refs_0_, bf16[384,256]{1,0:T(8,128)(2,1)S(1)} %collective-permute-done.19.refs_1_, bf16[384,256]{1,0:T(8,128)(2,1)S(1)} %collective-permute-done.29.refs_2_, ...), custom_call_target="tpu_custom_call" | custom-call | flops 1000 | bytes 1000 | tf_op jit(solution)/shard_map/outer/pallas_call | solution.py:271
  145.7 1.6 collective-permute-start.37
  147.3 1.7 product.9
  149.1 3.1 %collective-permute-start.34 = (bf16[384,256]{1,0:T(8,128)(2,1)S(1)}, bf16[384,256]{1,0:T(8,128)(2,1)S(1)}, u32[]{:S(2)}, u32[]{:S(2)}) collective-permute-start(bf16[384,256]{1,0:T(8,128)(2,1)S(1)} %product.9), channel_id=1, source_target_pairs={{0,8},{4,12},{8,24},{12,28},{24,16},{28,20},{16,0},{20,4},{1,9},{5... | collective-permute-start | bytes 589832 | tf_op jit(solution)/shard_map/ppermute | solution.py:533
  152.2 5.9 %outer.3 = (bf16[128,1024]{1,0:T(8,128)(2,1)S(1)}, bf16[128,1024]{1,0:T(8,128)(2,1)S(1)}, bf16[128,2048]{1,0:T(8,128)(2,1)S(1)}, bf16[128,2048]{1,0:T(8,128)(2,1)S(1)}) custom-call(bf16[384,256]{1,0:T(8,128)(2,1)S(1)} %get-tuple-element.184.refs_0_, bf16[384,256]{1,0:T(8,128)(2,1)S(1)} %collective-permute-done.19.refs_1_, ...), custom_call_target="tpu_custom_call" | custom-call | flops 1000 | bytes 1000 | tf_op jit(solution)/shard_map/outer/pallas_call | solution.py:271
  161.3 2.9 %collective-permute-done.36.there_ref = f32[1,384]{1,0:T(1,128)S(1)} collective-permute-done((f32[1,384]{1,0:T(1,128)S(1)}, f32[1,384]{1,0:T(1,128)S(1)}, u32[]{:S(2)}, u32[]{:S(2)}) %collective-permute-start.36) | collective-permute-done | bytes 1568 | tf_op jit(solution)/shard_map/ppermute | solution.py:435
  167.3 3.6 %all-to-all-start.2 = ((bf16[8,144,128]{2,1,0:T(8,128)(2,1)}), bf16[8,144,128]{2,1,0:T(8,128)(2,1)S(1)}, u32[]{:S(2)}, u32[]{:S(2)}) async-start(bf16[8,144,128]{2,1,0:T(8,128)(2,1)} %copy-done.20), calls=%async_computation.2 | async-start | bytes 589824 | tf_op jit(solution)/shard_map/all_to_all | solution.py:551
  171.0 2.0 collective-permute-start.39
  174.2 4.5 %inside.1 = (bf16[384,1024]{1,0:T(8,128)(2,1)}, bf16[2,384,1024]{2,1,0:T(8,128)(2,1)S(1)}) custom-call(bf16[384,1024]{1,0:T(8,128)(2,1)S(1)} %copy-done.17, bf16[384,1024]{1,0:T(8,128)(2,1)S(1)} %copy-done.8, bf16[384,1024]{1,0:T(8,128)(2,1)S(1)} %copy-done.3, bf16[384,1024]{1,0:T(8,128)(2,1)S(1)} %copy-done.5, f32[8,384]{1,0:T(8,128)S(1)} %get-tuple-element.117.run_ref, ...), custom_call_target="tpu_custom_call" | custom-call | flops 1000 | bytes 1000 | tf_op jit(solution)/shard_map/inside/pallas_call | solution.py:421
  179.8 1.9 collective-permute-done.38
  184.3 5.0 %all-to-all-start.3 = ((bf16[8,128,128]{2,1,0:T(8,128)(2,1)}), bf16[8,128,128]{2,1,0:T(8,128)(2,1)S(1)}, u32[]{:S(2)}, u32[]{:S(2)}) async-start(bf16[8,128,128]{2,1,0:T(8,128)(2,1)} %scan.3), calls=%async_computation.3 | async-start | bytes 524288 | tf_op jit(solution)/shard_map/all_to_all | solution.py:572
  189.3 2.0 collective-permute-start.41
  191.3 3.2 %collective-permute-done.41 = f32[1,1024]{1,0:T(1,128)S(1)} collective-permute-done((f32[1,1024]{1,0:T(1,128)S(1)}, f32[1,1024]{1,0:T(1,128)S(1)}, u32[]{:S(2)}, u32[]{:S(2)}) %collective-permute-start.41) | collective-permute-done | bytes 4128 | tf_op jit(solution)/shard_map/ppermute | solution.py:576
  194.5 3.1 %collective-permute-start.42 = (f32[1,1024]{1,0:T(1,128)S(1)}, f32[1,1024]{1,0:T(1,128)S(1)}, u32[]{:S(2)}, u32[]{:S(2)}) collective-permute-start(f32[1,1024]{1,0:T(1,128)S(1)} %add.143), channel_id=1, source_target_pairs={{0,16},{4,20},{8,24},{12,28},{16,0},{20,4},{24,8},{28,12},{1,17},{... | collective-permute-start | bytes 12296 | tf_op jit(solution)/shard_map/ppermute | solution.py:576
  198.8 2.2 %sum.2.refs_0_ = bf16[128,6144]{1,0:T(8,128)(2,1)} custom-call(bf16[128,3072]{1,0:T(8,128)(2,1)S(1)} %copy-done.15, bf16[128,3072]{1,0:T(8,128)(2,1)} %collective-permute-done.37.refs_1_), custom_call_target="tpu_custom_call" | custom-call | flops 1000 | bytes 1000 | tf_op jit(solution)/shard_map/sum/pallas_call | solution.py:307
  203.0 2.0 outside.1
  205.0 2.1 %sum.3 = bf16[128,6144]{1,0:T(8,128)(2,1)} custom-call(bf16[128,6144]{1,0:T(8,128)(2,1)} %sum.2.refs_0_, bf16[128,1024]{1,0:T(8,128)(2,1)S(1)} %copy-done.22, bf16[128,1024]{1,0:T(8,128)(2,1)S(1)} %copy-done.24, bf16[128,2048]{1,0:T(8,128)(2,1)S(1)} %copy-done.19, bf16[128,2048]{1,0:T(8,128)(2,1)} %collective-permute-done.40.refs_4_), custom_call_target="tpu_custom_call", output_to_operand_aliasing={{}: (0, {})} | custom-call | flops 1000 | bytes 1000 | tf_op jit(solution)/shard_map/sum/pallas_call | solution.py:307
  (137 shorter events, 36.9 us)
Async XLA Ops:
  3.1 24.8 %collective-permute-start = (bf16[96,3072]{1,0:T(8,128)(2,1)}, bf16[96,3072]{1,0:T(8,128)(2,1)}, u32[]{:S(2)}, u32[]{:S(2)}) collective-permute-start(bf16[96,3072]{1,0:T(8,128)(2,1)} %get-tuple-element.228), channel_id=1, source_target_pairs={{0,8},{4,12},{8,24},{12,28},{24,16},{28,20},{16,0},{20,4},{1,9},{5... | collective-permute-start | bytes 1769480 | tf_op jit(solution)/shard_map/ppermute | solution.py:432
  8.7 19.2 %all-to-all-start = ((bf16[8,144,128]{2,1,0:T(8,128)(2,1)}), bf16[8,144,128]{2,1,0:T(8,128)(2,1)S(1)}, u32[]{:S(2)}, u32[]{:S(2)}) async-start(bf16[8,144,128]{2,1,0:T(8,128)(2,1)} %get-tuple-element.116), calls=%async_computation | async-start | bytes 589824 | tf_op jit(solution)/shard_map/all_to_all | solution.py:454
  13.5 28.5 %collective-permute-start.1 = (bf16[96,3072]{1,0:T(8,128)(2,1)}, bf16[96,3072]{1,0:T(8,128)(2,1)}, u32[]{:S(2)}, u32[]{:S(2)}) collective-permute-start(bf16[96,3072]{1,0:T(8,128)(2,1)} %get-tuple-element.120), channel_id=1, source_target_pairs={{0,8},{4,12},{8,24},{12,28},{24,16},{28,20},{16,0},{20,4},{1,9},{5... | collective-permute-start | bytes 1769480 | tf_op jit(solution)/shard_map/ppermute | solution.py:432
  15.6 90.7 %slice-start = ((s8[4718592]{0:T(1024)(128)(4,1)}), s8[524288]{0:T(1024)(128)(4,1)S(1)}, s32[]{:S(2)}) async-start(s8[4718592]{0:T(1024)(128)(4,1)} %bitcast.5), calls=%async_computation.4 | async-start | bytes 1048576
  27.9 17.4 %collective-permute-start.2 = (bf16[96,3072]{1,0:T(8,128)(2,1)}, bf16[96,3072]{1,0:T(8,128)(2,1)}, u32[]{:S(2)}, u32[]{:S(2)}) collective-permute-start(bf16[96,3072]{1,0:T(8,128)(2,1)} %collective-permute-done.refs_1_.refs_5_), channel_id=1, source_target_pairs={{0,2},{1,3},{2,0},{3,1},{4,6},{5,7},{6,4},{7,5},{8,10},{9,11},{10,... | collective-permute-start | bytes 1769480 | tf_op jit(solution)/shard_map/ppermute | solution.py:435
  30.6 14.8 %all-to-all-start.1 = ((bf16[8,128,128]{2,1,0:T(8,128)(2,1)}), bf16[8,128,128]{2,1,0:T(8,128)(2,1)S(1)}, u32[]{:S(2)}, u32[]{:S(2)}) async-start(bf16[8,128,128]{2,1,0:T(8,128)(2,1)} %copy-done.13), calls=%async_computation.1 | async-start | bytes 524288 | tf_op jit(solution)/shard_map/all_to_all | solution.py:462
  45.3 4.4 %collective-permute-start.4 = (bf16[96,3072]{1,0:T(8,128)(2,1)}, bf16[96,3072]{1,0:T(8,128)(2,1)S(1)}, u32[]{:S(2)}, u32[]{:S(2)}) collective-permute-start(bf16[96,3072]{1,0:T(8,128)(2,1)} %collective-permute-done.refs_1_.refs_5_), channel_id=1, source_target_pairs={{0,1},{1,0},{2,3},{3,2},{4,5},{5,4},{6,7},{7,6},{8,9},{9,8},{10,11... | collective-permute-start | bytes 1769480 | tf_op jit(solution)/shard_map/ppermute | solution.py:435
  45.4 17.6 %collective-permute-start.6 = (bf16[96,3072]{1,0:T(8,128)(2,1)}, bf16[96,3072]{1,0:T(8,128)(2,1)S(1)}, u32[]{:S(2)}, u32[]{:S(2)}) collective-permute-start(bf16[96,3072]{1,0:T(8,128)(2,1)} %collective-permute-done.refs_1_.refs_5_), channel_id=1, source_target_pairs={{0,8},{4,12},{8,24},{12,28},{24,16},{28,20},{16,0},{20,4},{1,9},{5... | collective-permute-start | bytes 1769480 | tf_op jit(solution)/shard_map/ppermute | solution.py:432
  46.6 3.0 %collective-permute-start.3 = (bf16[96,3072]{1,0:T(8,128)(2,1)}, bf16[96,3072]{1,0:T(8,128)(2,1)S(1)}, u32[]{:S(2)}, u32[]{:S(2)}) collective-permute-start(bf16[96,3072]{1,0:T(8,128)(2,1)} %collective-permute-done.2.refs_3_.refs_7_), channel_id=1, source_target_pairs={{0,1},{1,0},{2,3},{3,2},{4,5},{5,4},{6,7},{7,6},{8,9},{9,8},{10,11... | collective-permute-start | bytes 1769480 | tf_op jit(solution)/shard_map/ppermute | solution.py:435
  46.8 16.2 %collective-permute-start.7 = (bf16[96,3072]{1,0:T(8,128)(2,1)}, bf16[96,3072]{1,0:T(8,128)(2,1)S(1)}, u32[]{:S(2)}, u32[]{:S(2)}) collective-permute-start(bf16[96,3072]{1,0:T(8,128)(2,1)} %collective-permute-done.1.refs_5_), channel_id=1, source_target_pairs={{0,2},{1,3},{2,0},{3,1},{4,6},{5,7},{6,4},{7,5},{8,10},{9,11},{10,... | collective-permute-start | bytes 1769480 | tf_op jit(solution)/shard_map/ppermute | solution.py:435
  48.4 14.0 %collective-permute-start.9 = (bf16[128,2048]{1,0:T(8,128)(2,1)S(1)}, bf16[128,2048]{1,0:T(8,128)(2,1)S(1)}, u32[]{:S(2)}, u32[]{:S(2)}) collective-permute-start(bf16[128,2048]{1,0:T(8,128)(2,1)S(1)} %get-tuple-element.231), channel_id=1, source_target_pairs={{0,4},{4,0},{8,12},{12,8},{16,20},{20,16},{24,28},{28,24},{1,5},{5... | collective-permute-start | bytes 1572872 | tf_op jit(solution)/shard_map/ppermute | solution.py:471
  51.8 1.2 collective-permute-start.5
  53.0 9.9 %collective-permute-start.8 = (f32[1,384]{1,0:T(1,128)S(1)}, f32[1,384]{1,0:T(1,128)S(1)}, u32[]{:S(2)}, u32[]{:S(2)}) collective-permute-start(f32[1,384]{1,0:T(1,128)S(1)} %add.140.here_ref), channel_id=1, source_target_pairs={{0,2},{1,3},{2,0},{3,1},{4,6},{5,7},{6,4},{7,5},{8,10},{9,11},{10,... | collective-permute-start | bytes 4616 | tf_op jit(solution)/shard_map/ppermute | solution.py:435
  63.0 18.6 %collective-permute-start.10 = (bf16[96,3072]{1,0:T(8,128)(2,1)}, bf16[96,3072]{1,0:T(8,128)(2,1)S(1)}, u32[]{:S(2)}, u32[]{:S(2)}) collective-permute-start(bf16[96,3072]{1,0:T(8,128)(2,1)} %collective-permute-done.1.refs_5_), channel_id=1, source_target_pairs={{0,8},{4,12},{8,24},{12,28},{24,16},{28,20},{16,0},{20,4},{1,9},{5... | collective-permute-start | bytes 1769480 | tf_op jit(solution)/shard_map/ppermute | solution.py:432
  65.7 15.9 %collective-permute-start.12 = (bf16[96,3072]{1,0:T(8,128)(2,1)}, bf16[96,3072]{1,0:T(8,128)(2,1)S(1)}, u32[]{:S(2)}, u32[]{:S(2)}) collective-permute-start(bf16[96,3072]{1,0:T(8,128)(2,1)} %collective-permute-done.1.refs_5_), channel_id=1, source_target_pairs={{0,1},{1,0},{2,3},{3,2},{4,5},{5,4},{6,7},{7,6},{8,9},{9,8},{10,11... | collective-permute-start | bytes 1769480 | tf_op jit(solution)/shard_map/ppermute | solution.py:435
  65.7 15.9 %collective-permute-start.11 = (bf16[96,3072]{1,0:T(8,128)(2,1)S(1)}, bf16[96,3072]{1,0:T(8,128)(2,1)S(1)}, u32[]{:S(2)}, u32[]{:S(2)}) collective-permute-start(bf16[96,3072]{1,0:T(8,128)(2,1)S(1)} %collective-permute-done.6.refs_1_.refs_9_), channel_id=1, source_target_pairs={{0,2},{1,3},{2,0},{3,1},{4,6},{5,7},{6,4},{7,5},{8,10},{9,11},{10,... | collective-permute-start | bytes 1769480 | tf_op jit(solution)/shard_map/ppermute | solution.py:435
  67.2 14.4 %collective-permute-start.13 = (bf16[96,3072]{1,0:T(8,128)(2,1)S(1)}, bf16[96,3072]{1,0:T(8,128)(2,1)S(1)}, u32[]{:S(2)}, u32[]{:S(2)}) collective-permute-start(bf16[96,3072]{1,0:T(8,128)(2,1)S(1)} %collective-permute-done.7.refs_7_), channel_id=1, source_target_pairs={{0,1},{1,0},{2,3},{3,2},{4,5},{5,4},{6,7},{7,6},{8,9},{9,8},{10,11... | collective-permute-start | bytes 1769480 | tf_op jit(solution)/shard_map/ppermute | solution.py:435
  67.4 14.1 %collective-permute-start.14 = (bf16[128,2048]{1,0:T(8,128)(2,1)S(1)}, bf16[128,2048]{1,0:T(8,128)(2,1)S(1)}, u32[]{:S(2)}, u32[]{:S(2)}) collective-permute-start(bf16[128,2048]{1,0:T(8,128)(2,1)S(1)} %get-tuple-element.141), channel_id=1, source_target_pairs={{0,4},{4,0},{8,12},{12,8},{16,20},{20,16},{24,28},{28,24},{1,5},{5... | collective-permute-start | bytes 1572872 | tf_op jit(solution)/shard_map/ppermute | solution.py:471
  81.6 8.8 %collective-permute-start.19 = (bf16[384,256]{1,0:T(8,128)(2,1)S(1)}, bf16[384,256]{1,0:T(8,128)(2,1)S(1)}, u32[]{:S(2)}, u32[]{:S(2)}) collective-permute-start(bf16[384,256]{1,0:T(8,128)(2,1)S(1)} %get-tuple-element.146), channel_id=1, source_target_pairs={{0,8},{4,12},{8,24},{12,28},{24,16},{28,20},{16,0},{20,4},{1,9},{5... | collective-permute-start | bytes 589832 | tf_op jit(solution)/shard_map/ppermute | solution.py:499
  82.8 18.7 %collective-permute-start.15 = (bf16[96,3072]{1,0:T(8,128)(2,1)S(1)}, bf16[96,3072]{1,0:T(8,128)(2,1)S(1)}, u32[]{:S(2)}, u32[]{:S(2)}) collective-permute-start(bf16[96,3072]{1,0:T(8,128)(2,1)S(1)} %collective-permute-done.6.refs_1_.refs_9_), channel_id=1, source_target_pairs={{0,8},{4,12},{8,24},{12,28},{24,16},{28,20},{16,0},{20,4},{1,9},{5... | collective-permute-start | bytes 1769480 | tf_op jit(solution)/shard_map/ppermute | solution.py:432
  82.8 18.7 %collective-permute-start.17 = (bf16[96,3072]{1,0:T(8,128)(2,1)S(1)}, bf16[96,3072]{1,0:T(8,128)(2,1)S(1)}, u32[]{:S(2)}, u32[]{:S(2)}) collective-permute-start(bf16[96,3072]{1,0:T(8,128)(2,1)S(1)} %collective-permute-done.6.refs_1_.refs_9_), channel_id=1, source_target_pairs={{0,1},{1,0},{2,3},{3,2},{4,5},{5,4},{6,7},{7,6},{8,9},{9,8},{10,11... | collective-permute-start | bytes 1769480 | tf_op jit(solution)/shard_map/ppermute | solution.py:435
  82.8 18.7 %collective-permute-start.16 = (bf16[96,3072]{1,0:T(8,128)(2,1)S(1)}, bf16[96,3072]{1,0:T(8,128)(2,1)S(1)}, u32[]{:S(2)}, u32[]{:S(2)}) collective-permute-start(bf16[96,3072]{1,0:T(8,128)(2,1)S(1)} %collective-permute-done.10.refs_5_.refs_9_), channel_id=1, source_target_pairs={{0,2},{1,3},{2,0},{3,1},{4,6},{5,7},{6,4},{7,5},{8,10},{9,11},{10,... | collective-permute-start | bytes 1769480 | tf_op jit(solution)/shard_map/ppermute | solution.py:435
  84.3 17.2 %collective-permute-start.18 = (bf16[96,3072]{1,0:T(8,128)(2,1)S(1)}, bf16[96,3072]{1,0:T(8,128)(2,1)S(1)}, u32[]{:S(2)}, u32[]{:S(2)}) collective-permute-start(bf16[96,3072]{1,0:T(8,128)(2,1)S(1)} %collective-permute-done.11.refs_3_.refs_11_), channel_id=1, source_target_pairs={{0,1},{1,0},{2,3},{3,2},{4,5},{5,4},{6,7},{7,6},{8,9},{9,8},{10,11... | collective-permute-start | bytes 1769480 | tf_op jit(solution)/shard_map/ppermute | solution.py:435
  90.4 11.0 %collective-permute-start.20 = (bf16[128,2048]{1,0:T(8,128)(2,1)S(1)}, bf16[128,2048]{1,0:T(8,128)(2,1)S(1)}, u32[]{:S(2)}, u32[]{:S(2)}) collective-permute-start(bf16[128,2048]{1,0:T(8,128)(2,1)S(1)} %get-tuple-element.147), channel_id=1, source_target_pairs={{0,4},{4,0},{8,12},{12,8},{16,20},{20,16},{24,28},{28,24},{1,5},{5... | collective-permute-start | bytes 1572872 | tf_op jit(solution)/shard_map/ppermute | solution.py:471
  101.5 19.1 %collective-permute-start.21 = (bf16[96,3072]{1,0:T(8,128)(2,1)S(1)}, bf16[96,3072]{1,0:T(8,128)(2,1)S(1)}, u32[]{:S(2)}, u32[]{:S(2)}) collective-permute-start(bf16[96,3072]{1,0:T(8,128)(2,1)S(1)} %collective-permute-done.10.refs_5_.refs_9_), channel_id=1, source_target_pairs={{0,8},{4,12},{8,24},{12,28},{24,16},{28,20},{16,0},{20,4},{1,9},{5... | collective-permute-start | bytes 1769480 | tf_op jit(solution)/shard_map/ppermute | solution.py:432
  101.9 18.7 %collective-permute-start.23 = (bf16[96,3072]{1,0:T(8,128)(2,1)S(1)}, bf16[96,3072]{1,0:T(8,128)(2,1)S(1)}, u32[]{:S(2)}, u32[]{:S(2)}) collective-permute-start(bf16[96,3072]{1,0:T(8,128)(2,1)S(1)} %collective-permute-done.10.refs_5_.refs_9_), channel_id=1, source_target_pairs={{0,1},{1,0},{2,3},{3,2},{4,5},{5,4},{6,7},{7,6},{8,9},{9,8},{10,11... | collective-permute-start | bytes 1769480 | tf_op jit(solution)/shard_map/ppermute | solution.py:435
  101.9 18.7 %collective-permute-start.22 = (bf16[96,3072]{1,0:T(8,128)(2,1)S(1)}, bf16[96,3072]{1,0:T(8,128)(2,1)S(1)}, u32[]{:S(2)}, u32[]{:S(2)}) collective-permute-start(bf16[96,3072]{1,0:T(8,128)(2,1)S(1)} %collective-permute-done.15.refs_1_.refs_13_), channel_id=1, source_target_pairs={{0,2},{1,3},{2,0},{3,1},{4,6},{5,7},{6,4},{7,5},{8,10},{9,11},{10,... | collective-permute-start | bytes 1769480 | tf_op jit(solution)/shard_map/ppermute | solution.py:435
  103.4 17.2 %collective-permute-start.24 = (bf16[96,3072]{1,0:T(8,128)(2,1)S(1)}, bf16[96,3072]{1,0:T(8,128)(2,1)S(1)}, u32[]{:S(2)}, u32[]{:S(2)}) collective-permute-start(bf16[96,3072]{1,0:T(8,128)(2,1)S(1)} %collective-permute-done.16.refs_7_.refs_11_), channel_id=1, source_target_pairs={{0,1},{1,0},{2,3},{3,2},{4,5},{5,4},{6,7},{7,6},{8,9},{9,8},{10,11... | collective-permute-start | bytes 1769480 | tf_op jit(solution)/shard_map/ppermute | solution.py:435
  103.6 16.5 %collective-permute-start.25 = (bf16[384,256]{1,0:T(8,128)(2,1)S(1)}, bf16[384,256]{1,0:T(8,128)(2,1)S(1)}, u32[]{:S(2)}, u32[]{:S(2)}) collective-permute-start(bf16[384,256]{1,0:T(8,128)(2,1)S(1)} %get-tuple-element.151), channel_id=1, source_target_pairs={{0,16},{4,20},{8,0},{12,4},{24,8},{28,12},{16,24},{20,28},{1,17},{... | collective-permute-start | bytes 589832 | tf_op jit(solution)/shard_map/ppermute | solution.py:505
  120.6 7.4 %collective-permute-start.27 = (bf16[96,3072]{1,0:T(8,128)(2,1)S(1)}, bf16[96,3072]{1,0:T(8,128)(2,1)S(1)}, u32[]{:S(2)}, u32[]{:S(2)}) collective-permute-start(bf16[96,3072]{1,0:T(8,128)(2,1)S(1)} %collective-permute-done.15.refs_1_.refs_13_), channel_id=1, source_target_pairs={{0,1},{1,0},{2,3},{3,2},{4,5},{5,4},{6,7},{7,6},{8,9},{9,8},{10,11... | collective-permute-start | bytes 1769480 | tf_op jit(solution)/shard_map/ppermute | solution.py:435
  120.7 7.4 %collective-permute-start.28 = (bf16[96,3072]{1,0:T(8,128)(2,1)S(1)}, bf16[96,3072]{1,0:T(8,128)(2,1)S(1)}, u32[]{:S(2)}, u32[]{:S(2)}) collective-permute-start(bf16[96,3072]{1,0:T(8,128)(2,1)S(1)} %collective-permute-done.22.refs_3_.refs_15_), channel_id=1, source_target_pairs={{0,1},{1,0},{2,3},{3,2},{4,5},{5,4},{6,7},{7,6},{8,9},{9,8},{10,11... | collective-permute-start | bytes 1769480 | tf_op jit(solution)/shard_map/ppermute | solution.py:435
  121.2 15.3 %collective-permute-start.26 = (bf16[96,3072]{1,0:T(8,128)(2,1)S(1)}, bf16[96,3072]{1,0:T(8,128)(2,1)S(1)}, u32[]{:S(2)}, u32[]{:S(2)}) collective-permute-start(bf16[96,3072]{1,0:T(8,128)(2,1)S(1)} %collective-permute-done.21.refs_1_.refs_13_), channel_id=1, source_target_pairs={{0,2},{1,3},{2,0},{3,1},{4,6},{5,7},{6,4},{7,5},{8,10},{9,11},{10,... | collective-permute-start | bytes 1769480 | tf_op jit(solution)/shard_map/ppermute | solution.py:435
  122.9 9.7 %collective-permute-start.29 = (bf16[384,256]{1,0:T(8,128)(2,1)S(1)}, bf16[384,256]{1,0:T(8,128)(2,1)S(1)}, u32[]{:S(2)}, u32[]{:S(2)}) collective-permute-start(bf16[384,256]{1,0:T(8,128)(2,1)S(1)} %get-tuple-element.162), channel_id=1, source_target_pairs={{0,24},{4,28},{8,16},{12,20},{24,0},{28,4},{16,8},{20,12},{1,25},{... | collective-permute-start | bytes 589832 | tf_op jit(solution)/shard_map/ppermute | solution.py:517
  123.9 10.5 %collective-permute-start.30 = (bf16[384,256]{1,0:T(8,128)(2,1)S(1)}, bf16[384,256]{1,0:T(8,128)(2,1)S(1)}, u32[]{:S(2)}, u32[]{:S(2)}) collective-permute-start(bf16[384,256]{1,0:T(8,128)(2,1)S(1)} %product.6), channel_id=1, source_target_pairs={{0,16},{4,20},{8,0},{12,4},{24,8},{28,12},{16,24},{20,28},{1,17},{... | collective-permute-start | bytes 589832 | tf_op jit(solution)/shard_map/ppermute | solution.py:518
  128.0 17.7 %collective-permute-start.32 = (bf16[96,3072]{1,0:T(8,128)(2,1)S(1)}, bf16[96,3072]{1,0:T(8,128)(2,1)S(1)}, u32[]{:S(2)}, u32[]{:S(2)}) collective-permute-start(bf16[96,3072]{1,0:T(8,128)(2,1)S(1)} %collective-permute-done.21.refs_1_.refs_13_), channel_id=1, source_target_pairs={{0,1},{1,0},{2,3},{3,2},{4,5},{5,4},{6,7},{7,6},{8,9},{9,8},{10,11... | collective-permute-start | bytes 1769480 | tf_op jit(solution)/shard_map/ppermute | solution.py:435
  136.5 9.2 %collective-permute-start.31 = (bf16[96,3072]{1,0:T(8,128)(2,1)S(1)}, bf16[96,3072]{1,0:T(8,128)(2,1)S(1)}, u32[]{:S(2)}, u32[]{:S(2)}) collective-permute-start(bf16[96,3072]{1,0:T(8,128)(2,1)S(1)} %collective-permute-done.26.refs_3_.refs_15_), channel_id=1, source_target_pairs={{0,1},{1,0},{2,3},{3,2},{4,5},{5,4},{6,7},{7,6},{8,9},{9,8},{10,11... | collective-permute-start | bytes 1769480 | tf_op jit(solution)/shard_map/ppermute | solution.py:435
  136.5 9.2 %collective-permute-start.33 = (bf16[384,256]{1,0:T(8,128)(2,1)S(1)}, bf16[384,256]{1,0:T(8,128)(2,1)S(1)}, u32[]{:S(2)}, u32[]{:S(2)}) collective-permute-start(bf16[384,256]{1,0:T(8,128)(2,1)S(1)} %product.8), channel_id=1, source_target_pairs={{0,24},{4,28},{8,16},{12,20},{24,0},{28,4},{16,8},{20,12},{1,25},{... | collective-permute-start | bytes 589832 | tf_op jit(solution)/shard_map/ppermute | solution.py:522
  145.7 36.8 %collective-permute-start.37 = (bf16[128,3072]{1,0:T(8,128)(2,1)}, bf16[128,3072]{1,0:T(8,128)(2,1)}, u32[]{:S(2)}, u32[]{:S(2)}) collective-permute-start(bf16[128,3072]{1,0:T(8,128)(2,1)} %get-tuple-element.207), channel_id=1, source_target_pairs={{0,4},{4,0},{8,12},{12,8},{16,20},{20,16},{24,28},{28,24},{1,5},{5... | collective-permute-start | bytes 2359304 | tf_op jit(solution)/shard_map/ppermute | solution.py:535
  149.1 9.1 %collective-permute-start.34 = (bf16[384,256]{1,0:T(8,128)(2,1)S(1)}, bf16[384,256]{1,0:T(8,128)(2,1)S(1)}, u32[]{:S(2)}, u32[]{:S(2)}) collective-permute-start(bf16[384,256]{1,0:T(8,128)(2,1)S(1)} %product.9), channel_id=1, source_target_pairs={{0,8},{4,12},{8,24},{12,28},{24,16},{28,20},{16,0},{20,4},{1,9},{5... | collective-permute-start | bytes 589832 | tf_op jit(solution)/shard_map/ppermute | solution.py:533
  159.4 1.2 collective-permute-start.35
  160.6 3.6 %collective-permute-start.36 = (f32[1,384]{1,0:T(1,128)S(1)}, f32[1,384]{1,0:T(1,128)S(1)}, u32[]{:S(2)}, u32[]{:S(2)}) collective-permute-start(f32[1,384]{1,0:T(1,128)S(1)} %add.141.here_ref), channel_id=1, source_target_pairs={{0,2},{1,3},{2,0},{3,1},{4,6},{5,7},{6,4},{7,5},{8,10},{9,11},{10,... | collective-permute-start | bytes 4616 | tf_op jit(solution)/shard_map/ppermute | solution.py:435
  167.3 15.2 %all-to-all-start.2 = ((bf16[8,144,128]{2,1,0:T(8,128)(2,1)}), bf16[8,144,128]{2,1,0:T(8,128)(2,1)S(1)}, u32[]{:S(2)}, u32[]{:S(2)}) async-start(bf16[8,144,128]{2,1,0:T(8,128)(2,1)} %copy-done.20), calls=%async_computation.2 | async-start | bytes 589824 | tf_op jit(solution)/shard_map/all_to_all | solution.py:551
  171.0 10.8 %collective-permute-start.39 = (bf16[128,1024]{1,0:T(8,128)(2,1)}, bf16[128,1024]{1,0:T(8,128)(2,1)S(1)}, u32[]{:S(2)}, u32[]{:S(2)}) collective-permute-start(bf16[128,1024]{1,0:T(8,128)(2,1)} %copy-done.28), channel_id=1, source_target_pairs={{0,4},{4,0},{8,12},{12,8},{16,20},{20,16},{24,28},{28,24},{1,5},{5... | collective-permute-start | bytes 786440 | tf_op jit(solution)/shard_map/ppermute | solution.py:558
  173.0 8.8 %collective-permute-start.38 = (f32[1,1024]{1,0:T(1,128)S(1)}, f32[1,1024]{1,0:T(1,128)S(1)}, u32[]{:S(2)}, u32[]{:S(2)}) collective-permute-start(f32[1,1024]{1,0:T(1,128)S(1)} %get-tuple-element.209), channel_id=1, source_target_pairs={{0,4},{4,0},{8,12},{12,8},{16,20},{20,16},{24,28},{28,24},{1,5},{5... | collective-permute-start | bytes 12296 | tf_op jit(solution)/shard_map/ppermute | solution.py:554
  182.5 22.5 %collective-permute-start.40 = (bf16[128,2048]{1,0:T(8,128)(2,1)}, bf16[128,2048]{1,0:T(8,128)(2,1)}, u32[]{:S(2)}, u32[]{:S(2)}) collective-permute-start(bf16[128,2048]{1,0:T(8,128)(2,1)} %copy-done.27), channel_id=1, source_target_pairs={{0,4},{4,0},{8,12},{12,8},{16,20},{20,16},{24,28},{28,24},{1,5},{5... | collective-permute-start | bytes 1572872 | tf_op jit(solution)/shard_map/ppermute | solution.py:558
  184.3 17.2 %all-to-all-start.3 = ((bf16[8,128,128]{2,1,0:T(8,128)(2,1)}), bf16[8,128,128]{2,1,0:T(8,128)(2,1)S(1)}, u32[]{:S(2)}, u32[]{:S(2)}) async-start(bf16[8,128,128]{2,1,0:T(8,128)(2,1)} %scan.3), calls=%async_computation.3 | async-start | bytes 524288 | tf_op jit(solution)/shard_map/all_to_all | solution.py:572
  189.3 5.2 %collective-permute-start.41 = (f32[1,1024]{1,0:T(1,128)S(1)}, f32[1,1024]{1,0:T(1,128)S(1)}, u32[]{:S(2)}, u32[]{:S(2)}) collective-permute-start(f32[1,1024]{1,0:T(1,128)S(1)} %add.142), channel_id=1, source_target_pairs={{0,8},{4,12},{8,0},{12,4},{16,24},{20,28},{24,16},{28,20},{1,9},{5... | collective-permute-start | bytes 12296 | tf_op jit(solution)/shard_map/ppermute | solution.py:576
  194.5 6.4 %collective-permute-start.42 = (f32[1,1024]{1,0:T(1,128)S(1)}, f32[1,1024]{1,0:T(1,128)S(1)}, u32[]{:S(2)}, u32[]{:S(2)}) collective-permute-start(f32[1,1024]{1,0:T(1,128)S(1)} %add.143), channel_id=1, source_target_pairs={{0,16},{4,20},{8,24},{12,28},{16,0},{20,4},{24,8},{28,12},{1,17},{... | collective-permute-start | bytes 12296 | tf_op jit(solution)/shard_map/ppermute | solution.py:576
  (30 other events, 203.0 us)

commit v14 on v13

--- a/solution.py
+++ b/solution.py
@@ -541,8 +541,9 @@
         back_kernel, [wide_b, jax.ShapeDtypeStruct((1, width), FL), row_f], "back",
         order, attn_out, inv_rms, gain_row, *returned,
     )
-    inner = inner + near_of(inner)
+    inner, gain_sum = hold((inner + near_of(inner), gain_sum))
     inner_there = other_of(inner)
+    gain_sum = gain_sum + lax.ppermute(gain_sum, "ctx", [(i, i ^ 2) for i in range(count)])
     inner_there, gain_sum = hold((inner_there, gain_sum))
     grad_attn, put_back = whole(
         functools.partial(grad_kernel, features), [wide_b, put_shape], "grads",
@@ -572,7 +573,7 @@
     back_low = lax.all_to_all(states, "ctx", 0, 0, tiled=True)
     back_low, grad_weight = hold((back_low, grad_weight))
     back_low = back_low.reshape(heads, size, size)
-    for step in flips[1:]:
+    for step in flips[2:]:
         gain_sum = gain_sum + lax.ppermute(
             gain_sum, "ctx", [(i, i ^ step) for i in range(count)]
         )

time: 208 us -> 205 us (0.986)
    ppermute x22, waiting for transfers between devices: 7.31 us -> 4.55 us  [over(): return lax.ppermute(x, 'head', perm)]
    ppermute x0 -> x1, waiting for transfers between devices: none -> 2.74 us  [shards(): lax.ppermute(gain_sum, 'ctx', [(i, i ^ 2) for i in range(count)])]
    ppermute x2 -> x1, starting transfers between devices: 5.14 us -> 2.92 us  [shards(): lax.ppermute(gain_sum, 'ctx', [(i, i ^ step) for i in range(count)])]
  transfers between devices with their start and end apart: 47 -> 47, of which waited for: 20 -> 21; matrix products, arithmetic and copies ran while one was open for 1% -> 1% of each run, Pallas kernels for 23% -> 23%
where the time goes in v14:
time: 205 us; the launch traced here: 204 us
  waiting for transfers between devices  72.9 us (36%)
  starting transfers between devices  63.1 us (31%)
  Pallas kernels  49.5 us (24%)
  local copies, waits for them, and re-layouts  14.6 us (7%)
  other arithmetic  2.82 us (1%)
    ppermute x3, waiting for transfers between devices, swap(): lax.ppermute(part, 'ctx', pair_perm(count, -s))  27.9 us
    pallas_call x10, Pallas kernels, whole(): pl.pallas_call(kernel, in_specs=[SCALAR if a is tokens else full for a in...  16.5 us
    pallas_call x5, Pallas kernels, product(): pl.pallas_call(functools.partial(product_kernel, [len(x) for x in lots],...  16.2 us
    ppermute x22, starting transfers between devices, over(): return lax.ppermute(x, 'head', perm)  12.7 us
    pallas_call x2, Pallas kernels, outer(): pl.pallas_call(functools.partial(outer_kernel, 1 + len(flat), own, cuts),...  12.5 us
    unnamed x62, local copies, waits for them, and re-layouts  12.1 us
    ppermute x6, starting transfers between devices, ring(): return lax.ppermute(x, 'ctx', ring_perm(count, 1))  9.41 us
    all_to_all x1, waiting for transfers between devices, shards(): spread = lax.all_to_all(put, 'ctx', 0, 0, tiled=True)  9.3 us
  transfers between devices with their start and end apart: 47, of which 21 were waited for; matrix products, arithmetic and copies ran while one was open for 1% of the time, Pallas kernels for 23%

profile of v14, /device:TPU:0, one launch (start us, length us, event | category | flops | bytes accessed | tf_op | source)
XLA Modules:
  0.0 203.9 jit_solution(765243868322828773)
XLA Ops:
  0.7 2.4 %constant_dynamic-slice_fusion = (bf16[96,3072]{1,0:T(8,128)(2,1)}, bf16[96,3072]{1,0:T(8,128)(2,1)}) fusion(bf16[384,6144]{1,0:T(8,128)(2,1)} %refs_4_.3, s32[]{:T(128)S(6)} %select_n.84), kind=kLoop, calls=%fused_computation.46 | loop fusion | bytes 2359300 | tf_op jit(solution)/shard_map/dynamic_slice | solution.py:410
  3.1 3.0 %collective-permute-start = (bf16[96,3072]{1,0:T(8,128)(2,1)}, bf16[96,3072]{1,0:T(8,128)(2,1)}, u32[]{:S(2)}, u32[]{:S(2)}) collective-permute-start(bf16[96,3072]{1,0:T(8,128)(2,1)} %get-tuple-element.232), channel_id=1, source_target_pairs={{0,8},{4,12},{8,24},{12,28},{24,16},{28,20},{16,0},{20,4},{1,9},{5... | collective-permute-start | bytes 1769480 | tf_op jit(solution)/shard_map/ppermute | solution.py:432
  6.2 2.6 %states.1 = (bf16[8,144,128]{2,1,0:T(8,128)(2,1)}, f32[8,384]{1,0:T(8,128)S(1)}, f32[384,8]{1,0:T(8,128)S(1)}) custom-call(f32[8,384]{1,0:T(8,128)S(1)} %copy-done.26, bf16[384,1024]{1,0:T(8,128)(2,1)S(1)} %copy-done.3, bf16[384,1024]{1,0:T(8,128)(2,1)S(1)} %copy-done.4), custom_call_target="tpu_custom_call" | custom-call | flops 1000 | bytes 1000 | tf_op jit(solution)/shard_map/states/pallas_call | solution.py:421
  8.7 4.8 %all-to-all-start = ((bf16[8,144,128]{2,1,0:T(8,128)(2,1)}), bf16[8,144,128]{2,1,0:T(8,128)(2,1)S(1)}, u32[]{:S(2)}, u32[]{:S(2)}) async-start(bf16[8,144,128]{2,1,0:T(8,128)(2,1)} %get-tuple-element.118), calls=%async_computation | async-start | bytes 589824 | tf_op jit(solution)/shard_map/all_to_all | solution.py:454
  13.5 2.0 collective-permute-start.1
  15.6 1.9 weights.1.intra_ref
  18.6 9.3 %all-to-all-done.in_ref = bf16[8,144,128]{2,1,0:T(8,128)(2,1)S(1)} async-done(((bf16[8,144,128]{2,1,0:T(8,128)(2,1)}), bf16[8,144,128]{2,1,0:T(8,128)(2,1)S(1)}, u32[]{:S(2)}, u32[]{:S(2)}) %all-to-all-start) | async-done | bytes 294944 | tf_op jit(solution)/shard_map/all_to_all | solution.py:454
  27.9 1.9 collective-permute-start.2
  30.6 5.8 %all-to-all-start.1 = ((bf16[8,128,128]{2,1,0:T(8,128)(2,1)}), bf16[8,128,128]{2,1,0:T(8,128)(2,1)S(1)}, u32[]{:S(2)}, u32[]{:S(2)}) async-start(bf16[8,128,128]{2,1,0:T(8,128)(2,1)} %copy-done.13), calls=%async_computation.1 | async-start | bytes 524288 | tf_op jit(solution)/shard_map/all_to_all | solution.py:462
  36.4 2.2 %fusion.order_ref = bf16[1024,1024]{1,0:T(8,128)(2,1)} fusion(s32[1024]{0:T(1024)S(1)} %fusion.4), kind=kLoop, calls=%fused_computation.1 | loop fusion | flops 2097152 | bytes 2101248 | tf_op jit(solution)/shard_map/convert_element_type | solution.py:384
  38.6 3.5 %collective-permute-done.1.refs_5_ = bf16[96,3072]{1,0:T(8,128)(2,1)} collective-permute-done((bf16[96,3072]{1,0:T(8,128)(2,1)}, bf16[96,3072]{1,0:T(8,128)(2,1)}, u32[]{:S(2)}, u32[]{:S(2)}) %collective-permute-start.1) | collective-permute-done | bytes 589856 | tf_op jit(solution)/shard_map/ppermute | solution.py:432
  42.0 3.3 %all-to-all-done.1.state_ref = bf16[8,128,128]{2,1,0:T(8,128)(2,1)S(1)} async-done(((bf16[8,128,128]{2,1,0:T(8,128)(2,1)}), bf16[8,128,128]{2,1,0:T(8,128)(2,1)S(1)}, u32[]{:S(2)}, u32[]{:S(2)}) %all-to-all-start.1) | async-done | bytes 262176 | tf_op jit(solution)/shard_map/all_to_all | solution.py:462
  46.8 1.5 collective-permute-start.7
  53.7 8.7 %collective-permute-done.9.refs_4_.refs_10_.refs_6_ = bf16[128,2048]{1,0:T(8,128)(2,1)S(1)} collective-permute-done((bf16[128,2048]{1,0:T(8,128)(2,1)S(1)}, bf16[128,2048]{1,0:T(8,128)(2,1)S(1)}, u32[]{:S(2)}, u32[]{:S(2)}) %collective-permute-start.9) | collective-permute-done | bytes 524320 | tf_op jit(solution)/shard_map/ppermute | solution.py:471
  63.0 2.7 %collective-permute-start.10 = (bf16[96,3072]{1,0:T(8,128)(2,1)}, bf16[96,3072]{1,0:T(8,128)(2,1)S(1)}, u32[]{:S(2)}, u32[]{:S(2)}) collective-permute-start(bf16[96,3072]{1,0:T(8,128)(2,1)} %collective-permute-done.1.refs_5_), channel_id=1, source_target_pairs={{0,8},{4,12},{8,24},{12,28},{24,16},{28,20},{16,0},{20,4},{1,9},{5... | collective-permute-start | bytes 1769480 | tf_op jit(solution)/shard_map/ppermute | solution.py:432
  65.7 1.5 collective-permute-start.11
  68.9 1.6 copy-done.1
  71.8 9.7 %collective-permute-done.14.refs_5_.refs_11_.refs_7_.refs_6_ = bf16[128,2048]{1,0:T(8,128)(2,1)S(1)} collective-permute-done((bf16[128,2048]{1,0:T(8,128)(2,1)S(1)}, bf16[128,2048]{1,0:T(8,128)(2,1)S(1)}, u32[]{:S(2)}, u32[]{:S(2)}) %collective-permute-start.14) | collective-permute-done | bytes 524320 | tf_op jit(solution)/shard_map/ppermute | solution.py:471
  84.5 5.9 %collective-permute-done.19.refs_1_ = bf16[384,256]{1,0:T(8,128)(2,1)S(1)} collective-permute-done((bf16[384,256]{1,0:T(8,128)(2,1)S(1)}, bf16[384,256]{1,0:T(8,128)(2,1)S(1)}, u32[]{:S(2)}, u32[]{:S(2)}) %collective-permute-start.19) | collective-permute-done | bytes 196640 | tf_op jit(solution)/shard_map/ppermute | solution.py:499
  91.8 9.5 %collective-permute-done.20.refs_6_.refs_12_.refs_7_ = bf16[128,2048]{1,0:T(8,128)(2,1)S(1)} collective-permute-done((bf16[128,2048]{1,0:T(8,128)(2,1)S(1)}, bf16[128,2048]{1,0:T(8,128)(2,1)S(1)}, u32[]{:S(2)}, u32[]{:S(2)}) %collective-permute-start.20) | collective-permute-done | bytes 524320 | tf_op jit(solution)/shard_map/ppermute | solution.py:471
  101.9 1.5 collective-permute-start.22
  103.6 2.7 %collective-permute-start.25 = (bf16[384,256]{1,0:T(8,128)(2,1)S(1)}, bf16[384,256]{1,0:T(8,128)(2,1)S(1)}, u32[]{:S(2)}, u32[]{:S(2)}) collective-permute-start(bf16[384,256]{1,0:T(8,128)(2,1)S(1)} %get-tuple-element.153), channel_id=1, source_target_pairs={{0,16},{4,20},{8,0},{12,4},{24,8},{28,12},{16,24},{20,28},{1,17},{... | collective-permute-start | bytes 589832 | tf_op jit(solution)/shard_map/ppermute | solution.py:505
  106.3 3.7 %product.5.refs_0_ = bf16[384,256]{1,0:T(8,128)(2,1)S(1)} custom-call(s32[1]{0:T(128)} %bitcast.1.mine_ref.refs_0_, bf16[384,6144]{1,0:T(8,128)(2,1)S(1)} %bitcast.6, bf16[384,6144]{1,0:T(8,128)(2,1)S(1)} %bitcast.6, bf16[128,6144]{1,0:T(8,128)(2,1)S(1)} %bitcast.8, bf16[128,2048]{1,0:T(8,128)(2,1)S(1)} %collective-permute-done.9.refs_4_.refs_10_.refs_6_, ...), custom_call_target="tpu_custom_call" | custom-call | flops 1000 | bytes 1000 | tf_op jit(solution)/shard_map/product/pallas_call | solution.py:216
  110.0 5.2 %product.6 = bf16[384,256]{1,0:T(8,128)(2,1)S(1)} custom-call(s32[1]{0:T(128)} %bitcast.1.mine_ref.refs_0_, bf16[96,3072]{1,0:T(8,128)(2,1)} %collective-permute-done.refs_1_.refs_5_, bf16[96,3072]{1,0:T(8,128)(2,1)S(1)} %collective-permute-done.4.refs_2_.refs_6_, bf16[96,3072]{1,0:T(8,128)(2,1)} %collective-permute-done.2.refs_3_.refs_7_, ...), custom_call_target="tpu_custom_call" | custom-call | flops 1000 | bytes 1000 | tf_op jit(solution)/shard_map/product/pallas_call | solution.py:216
  115.2 4.9 %collective-permute-done.25.refs_3_ = bf16[384,256]{1,0:T(8,128)(2,1)S(1)} collective-permute-done((bf16[384,256]{1,0:T(8,128)(2,1)S(1)}, bf16[384,256]{1,0:T(8,128)(2,1)S(1)}, u32[]{:S(2)}, u32[]{:S(2)}) %collective-permute-start.25) | collective-permute-done | bytes 196640 | tf_op jit(solution)/shard_map/ppermute | solution.py:505
  121.2 1.7 collective-permute-start.26
  124.1 3.8 %product.8 = bf16[384,256]{1,0:T(8,128)(2,1)S(1)} custom-call(s32[1]{0:T(128)} %bitcast.1.mine_ref.refs_0_, bf16[96,3072]{1,0:T(8,128)(2,1)S(1)} %collective-permute-done.6.refs_1_.refs_9_, bf16[96,3072]{1,0:T(8,128)(2,1)S(1)} %collective-permute-done.17.refs_2_.refs_10_, bf16[96,3072]{1,0:T(8,128)(2,1)S(1)} %collective-permute-done.11.refs_3_.refs_11_, ...), custom_call_target="tpu_custom_call" | custom-call | flops 1000 | bytes 1000 | tf_op jit(solution)/shard_map/product/pallas_call | solution.py:216
  128.1 1.8 product.7.refs_8_
  129.8 2.7 %collective-permute-done.29.refs_2_ = bf16[384,256]{1,0:T(8,128)(2,1)S(1)} collective-permute-done((bf16[384,256]{1,0:T(8,128)(2,1)S(1)}, bf16[384,256]{1,0:T(8,128)(2,1)S(1)}, u32[]{:S(2)}, u32[]{:S(2)}) %collective-permute-start.29) | collective-permute-done | bytes 196640 | tf_op jit(solution)/shard_map/ppermute | solution.py:517
  132.6 1.8 collective-permute-done.30.refs_1_
  134.4 2.1 %collective-permute-done.26.refs_3_.refs_15_ = bf16[96,3072]{1,0:T(8,128)(2,1)S(1)} collective-permute-done((bf16[96,3072]{1,0:T(8,128)(2,1)S(1)}, bf16[96,3072]{1,0:T(8,128)(2,1)S(1)}, u32[]{:S(2)}, u32[]{:S(2)}) %collective-permute-start.26) | collective-permute-done | bytes 589856 | tf_op jit(solution)/shard_map/ppermute | solution.py:435
  137.7 6.5 %outer.2 = (bf16[128,3072]{1,0:T(8,128)(2,1)S(1)}, bf16[128,3072]{1,0:T(8,128)(2,1)}) custom-call(bf16[384,256]{1,0:T(8,128)(2,1)S(1)} %get-tuple-element.186.refs_0_, bf16[384,256]{1,0:T(8,128)(2,1)S(1)} %collective-permute-done.19.refs_1_, bf16[384,256]{1,0:T(8,128)(2,1)S(1)} %collective-permute-done.29.refs_2_, ...), custom_call_target="tpu_custom_call" | custom-call | flops 1000 | bytes 1000 | tf_op jit(solution)/shard_map/outer/pallas_call | solution.py:271
  145.7 1.6 collective-permute-start.38
  147.3 1.7 product.9
  149.1 3.1 %collective-permute-start.34 = (bf16[384,256]{1,0:T(8,128)(2,1)S(1)}, bf16[384,256]{1,0:T(8,128)(2,1)S(1)}, u32[]{:S(2)}, u32[]{:S(2)}) collective-permute-start(bf16[384,256]{1,0:T(8,128)(2,1)S(1)} %product.9), channel_id=1, source_target_pairs={{0,8},{4,12},{8,24},{12,28},{24,16},{28,20},{16,0},{20,4},{1,9},{5... | collective-permute-start | bytes 589832 | tf_op jit(solution)/shard_map/ppermute | solution.py:533
  152.2 5.9 %outer.3 = (bf16[128,1024]{1,0:T(8,128)(2,1)S(1)}, bf16[128,1024]{1,0:T(8,128)(2,1)S(1)}, bf16[128,2048]{1,0:T(8,128)(2,1)S(1)}, bf16[128,2048]{1,0:T(8,128)(2,1)S(1)}) custom-call(bf16[384,256]{1,0:T(8,128)(2,1)S(1)} %get-tuple-element.186.refs_0_, bf16[384,256]{1,0:T(8,128)(2,1)S(1)} %collective-permute-done.19.refs_1_, ...), custom_call_target="tpu_custom_call" | custom-call | flops 1000 | bytes 1000 | tf_op jit(solution)/shard_map/outer/pallas_call | solution.py:271
  161.5 2.7 %collective-permute-done.37 = f32[1,1024]{1,0:T(1,128)S(1)} collective-permute-done((f32[1,1024]{1,0:T(1,128)S(1)}, f32[1,1024]{1,0:T(1,128)S(1)}, u32[]{:S(2)}, u32[]{:S(2)}) %collective-permute-start.37) | collective-permute-done | bytes 4128 | tf_op jit(solution)/shard_map/ppermute | solution.py:546
  164.4 1.5 grads.1
  167.5 4.0 %all-to-all-start.2 = ((bf16[8,144,128]{2,1,0:T(8,128)(2,1)}), bf16[8,144,128]{2,1,0:T(8,128)(2,1)S(1)}, u32[]{:S(2)}, u32[]{:S(2)}) async-start(bf16[8,144,128]{2,1,0:T(8,128)(2,1)} %copy-done.20), calls=%async_computation.2 | async-start | bytes 589824 | tf_op jit(solution)/shard_map/all_to_all | solution.py:552
  171.5 2.0 collective-permute-start.40
  174.7 4.5 %inside.1 = (bf16[384,1024]{1,0:T(8,128)(2,1)}, bf16[2,384,1024]{2,1,0:T(8,128)(2,1)S(1)}) custom-call(bf16[384,1024]{1,0:T(8,128)(2,1)S(1)} %copy-done.17, bf16[384,1024]{1,0:T(8,128)(2,1)S(1)} %copy-done.8, bf16[384,1024]{1,0:T(8,128)(2,1)S(1)} %copy-done.3, bf16[384,1024]{1,0:T(8,128)(2,1)S(1)} %copy-done.5, f32[8,384]{1,0:T(8,128)S(1)} %get-tuple-element.119.run_ref, ...), custom_call_target="tpu_custom_call" | custom-call | flops 1000 | bytes 1000 | tf_op jit(solution)/shard_map/inside/pallas_call | solution.py:421
  180.3 1.7 collective-permute-done.39
  184.6 4.9 %all-to-all-start.3 = ((bf16[8,128,128]{2,1,0:T(8,128)(2,1)}), bf16[8,128,128]{2,1,0:T(8,128)(2,1)S(1)}, u32[]{:S(2)}, u32[]{:S(2)}) async-start(bf16[8,128,128]{2,1,0:T(8,128)(2,1)} %scan.3), calls=%async_computation.3 | async-start | bytes 524288 | tf_op jit(solution)/shard_map/all_to_all | solution.py:573
  189.5 2.9 %collective-permute-start.42 = (f32[1,1024]{1,0:T(1,128)S(1)}, f32[1,1024]{1,0:T(1,128)S(1)}, u32[]{:S(2)}, u32[]{:S(2)}) collective-permute-start(f32[1,1024]{1,0:T(1,128)S(1)} %add.143), channel_id=1, source_target_pairs={{0,16},{4,20},{8,24},{12,28},{16,0},{20,4},{24,8},{28,12},{1,17},{... | collective-permute-start | bytes 12296 | tf_op jit(solution)/shard_map/ppermute | solution.py:577
  193.6 2.2 %sum.2.refs_0_ = bf16[128,6144]{1,0:T(8,128)(2,1)} custom-call(bf16[128,3072]{1,0:T(8,128)(2,1)S(1)} %copy-done.15, bf16[128,3072]{1,0:T(8,128)(2,1)} %collective-permute-done.38.refs_1_), custom_call_target="tpu_custom_call" | custom-call | flops 1000 | bytes 1000 | tf_op jit(solution)/shard_map/sum/pallas_call | solution.py:307
  195.8 2.0 collective-permute-done.42
  199.8 2.0 %outside.1 = (bf16[384,1024]{1,0:T(8,128)(2,1)}, bf16[384,1024]{1,0:T(8,128)(2,1)}) custom-call(bf16[384,1024]{1,0:T(8,128)(2,1)S(1)} %copy-done.3, bf16[384,1024]{1,0:T(8,128)(2,1)S(1)} %copy-done.5, bf16[8,128,128]{2,1,0:T(8,128)(2,1)S(1)} %all-to-all-done.3.state_ref, f32[384,8]{1,0:T(8,128)S(1)} %get-tuple-element.120.turned_ref, ...), custom_call_target="tpu_custom_call" | custom-call | flops 1000 | bytes 1000 | tf_op jit(solution)/shard_map/outside/pallas_call | solution.py:421
  201.8 2.1 %sum.3 = bf16[128,6144]{1,0:T(8,128)(2,1)} custom-call(bf16[128,6144]{1,0:T(8,128)(2,1)} %sum.2.refs_0_, bf16[128,1024]{1,0:T(8,128)(2,1)S(1)} %copy-done.22, bf16[128,1024]{1,0:T(8,128)(2,1)S(1)} %copy-done.24, bf16[128,2048]{1,0:T(8,128)(2,1)S(1)} %copy-done.19, bf16[128,2048]{1,0:T(8,128)(2,1)} %collective-permute-done.41.refs_4_), custom_call_target="tpu_custom_call", output_to_operand_aliasing={{}: (0, {})} | custom-call | flops 1000 | bytes 1000 | tf_op jit(solution)/shard_map/sum/pallas_call | solution.py:307
  (137 shorter events, 35.6 us)
Async XLA Ops:
  3.1 24.8 %collective-permute-start = (bf16[96,3072]{1,0:T(8,128)(2,1)}, bf16[96,3072]{1,0:T(8,128)(2,1)}, u32[]{:S(2)}, u32[]{:S(2)}) collective-permute-start(bf16[96,3072]{1,0:T(8,128)(2,1)} %get-tuple-element.232), channel_id=1, source_target_pairs={{0,8},{4,12},{8,24},{12,28},{24,16},{28,20},{16,0},{20,4},{1,9},{5... | collective-permute-start | bytes 1769480 | tf_op jit(solution)/shard_map/ppermute | solution.py:432
  8.7 19.2 %all-to-all-start = ((bf16[8,144,128]{2,1,0:T(8,128)(2,1)}), bf16[8,144,128]{2,1,0:T(8,128)(2,1)S(1)}, u32[]{:S(2)}, u32[]{:S(2)}) async-start(bf16[8,144,128]{2,1,0:T(8,128)(2,1)} %get-tuple-element.118), calls=%async_computation | async-start | bytes 589824 | tf_op jit(solution)/shard_map/all_to_all | solution.py:454
  13.5 28.5 %collective-permute-start.1 = (bf16[96,3072]{1,0:T(8,128)(2,1)}, bf16[96,3072]{1,0:T(8,128)(2,1)}, u32[]{:S(2)}, u32[]{:S(2)}) collective-permute-start(bf16[96,3072]{1,0:T(8,128)(2,1)} %get-tuple-element.122), channel_id=1, source_target_pairs={{0,8},{4,12},{8,24},{12,28},{24,16},{28,20},{16,0},{20,4},{1,9},{5... | collective-permute-start | bytes 1769480 | tf_op jit(solution)/shard_map/ppermute | solution.py:432
  15.6 90.7 %slice-start = ((s8[4718592]{0:T(1024)(128)(4,1)}), s8[524288]{0:T(1024)(128)(4,1)S(1)}, s32[]{:S(2)}) async-start(s8[4718592]{0:T(1024)(128)(4,1)} %bitcast.5), calls=%async_computation.4 | async-start | bytes 1048576
  27.9 17.4 %collective-permute-start.2 = (bf16[96,3072]{1,0:T(8,128)(2,1)}, bf16[96,3072]{1,0:T(8,128)(2,1)}, u32[]{:S(2)}, u32[]{:S(2)}) collective-permute-start(bf16[96,3072]{1,0:T(8,128)(2,1)} %collective-permute-done.refs_1_.refs_5_), channel_id=1, source_target_pairs={{0,2},{1,3},{2,0},{3,1},{4,6},{5,7},{6,4},{7,5},{8,10},{9,11},{10,... | collective-permute-start | bytes 1769480 | tf_op jit(solution)/shard_map/ppermute | solution.py:435
  30.6 14.8 %all-to-all-start.1 = ((bf16[8,128,128]{2,1,0:T(8,128)(2,1)}), bf16[8,128,128]{2,1,0:T(8,128)(2,1)S(1)}, u32[]{:S(2)}, u32[]{:S(2)}) async-start(bf16[8,128,128]{2,1,0:T(8,128)(2,1)} %copy-done.13), calls=%async_computation.1 | async-start | bytes 524288 | tf_op jit(solution)/shard_map/all_to_all | solution.py:462
  45.3 4.4 %collective-permute-start.4 = (bf16[96,3072]{1,0:T(8,128)(2,1)}, bf16[96,3072]{1,0:T(8,128)(2,1)S(1)}, u32[]{:S(2)}, u32[]{:S(2)}) collective-permute-start(bf16[96,3072]{1,0:T(8,128)(2,1)} %collective-permute-done.refs_1_.refs_5_), channel_id=1, source_target_pairs={{0,1},{1,0},{2,3},{3,2},{4,5},{5,4},{6,7},{7,6},{8,9},{9,8},{10,11... | collective-permute-start | bytes 1769480 | tf_op jit(solution)/shard_map/ppermute | solution.py:435
  45.4 17.6 %collective-permute-start.6 = (bf16[96,3072]{1,0:T(8,128)(2,1)}, bf16[96,3072]{1,0:T(8,128)(2,1)S(1)}, u32[]{:S(2)}, u32[]{:S(2)}) collective-permute-start(bf16[96,3072]{1,0:T(8,128)(2,1)} %collective-permute-done.refs_1_.refs_5_), channel_id=1, source_target_pairs={{0,8},{4,12},{8,24},{12,28},{24,16},{28,20},{16,0},{20,4},{1,9},{5... | collective-permute-start | bytes 1769480 | tf_op jit(solution)/shard_map/ppermute | solution.py:432
  46.6 3.0 %collective-permute-start.3 = (bf16[96,3072]{1,0:T(8,128)(2,1)}, bf16[96,3072]{1,0:T(8,128)(2,1)S(1)}, u32[]{:S(2)}, u32[]{:S(2)}) collective-permute-start(bf16[96,3072]{1,0:T(8,128)(2,1)} %collective-permute-done.2.refs_3_.refs_7_), channel_id=1, source_target_pairs={{0,1},{1,0},{2,3},{3,2},{4,5},{5,4},{6,7},{7,6},{8,9},{9,8},{10,11... | collective-permute-start | bytes 1769480 | tf_op jit(solution)/shard_map/ppermute | solution.py:435
  46.8 16.2 %collective-permute-start.7 = (bf16[96,3072]{1,0:T(8,128)(2,1)}, bf16[96,3072]{1,0:T(8,128)(2,1)S(1)}, u32[]{:S(2)}, u32[]{:S(2)}) collective-permute-start(bf16[96,3072]{1,0:T(8,128)(2,1)} %collective-permute-done.1.refs_5_), channel_id=1, source_target_pairs={{0,2},{1,3},{2,0},{3,1},{4,6},{5,7},{6,4},{7,5},{8,10},{9,11},{10,... | collective-permute-start | bytes 1769480 | tf_op jit(solution)/shard_map/ppermute | solution.py:435
  48.4 14.0 %collective-permute-start.9 = (bf16[128,2048]{1,0:T(8,128)(2,1)S(1)}, bf16[128,2048]{1,0:T(8,128)(2,1)S(1)}, u32[]{:S(2)}, u32[]{:S(2)}) collective-permute-start(bf16[128,2048]{1,0:T(8,128)(2,1)S(1)} %get-tuple-element.235), channel_id=1, source_target_pairs={{0,4},{4,0},{8,12},{12,8},{16,20},{20,16},{24,28},{28,24},{1,5},{5... | collective-permute-start | bytes 1572872 | tf_op jit(solution)/shard_map/ppermute | solution.py:471
  51.8 1.2 collective-permute-start.5
  53.0 9.9 %collective-permute-start.8 = (f32[1,384]{1,0:T(1,128)S(1)}, f32[1,384]{1,0:T(1,128)S(1)}, u32[]{:S(2)}, u32[]{:S(2)}) collective-permute-start(f32[1,384]{1,0:T(1,128)S(1)} %add.140.here_ref), channel_id=1, source_target_pairs={{0,2},{1,3},{2,0},{3,1},{4,6},{5,7},{6,4},{7,5},{8,10},{9,11},{10,... | collective-permute-start | bytes 4616 | tf_op jit(solution)/shard_map/ppermute | solution.py:435
  63.0 18.6 %collective-permute-start.10 = (bf16[96,3072]{1,0:T(8,128)(2,1)}, bf16[96,3072]{1,0:T(8,128)(2,1)S(1)}, u32[]{:S(2)}, u32[]{:S(2)}) collective-permute-start(bf16[96,3072]{1,0:T(8,128)(2,1)} %collective-permute-done.1.refs_5_), channel_id=1, source_target_pairs={{0,8},{4,12},{8,24},{12,28},{24,16},{28,20},{16,0},{20,4},{1,9},{5... | collective-permute-start | bytes 1769480 | tf_op jit(solution)/shard_map/ppermute | solution.py:432
  65.7 15.9 %collective-permute-start.12 = (bf16[96,3072]{1,0:T(8,128)(2,1)}, bf16[96,3072]{1,0:T(8,128)(2,1)S(1)}, u32[]{:S(2)}, u32[]{:S(2)}) collective-permute-start(bf16[96,3072]{1,0:T(8,128)(2,1)} %collective-permute-done.1.refs_5_), channel_id=1, source_target_pairs={{0,1},{1,0},{2,3},{3,2},{4,5},{5,4},{6,7},{7,6},{8,9},{9,8},{10,11... | collective-permute-start | bytes 1769480 | tf_op jit(solution)/shard_map/ppermute | solution.py:435
  65.7 15.9 %collective-permute-start.11 = (bf16[96,3072]{1,0:T(8,128)(2,1)S(1)}, bf16[96,3072]{1,0:T(8,128)(2,1)S(1)}, u32[]{:S(2)}, u32[]{:S(2)}) collective-permute-start(bf16[96,3072]{1,0:T(8,128)(2,1)S(1)} %collective-permute-done.6.refs_1_.refs_9_), channel_id=1, source_target_pairs={{0,2},{1,3},{2,0},{3,1},{4,6},{5,7},{6,4},{7,5},{8,10},{9,11},{10,... | collective-permute-start | bytes 1769480 | tf_op jit(solution)/shard_map/ppermute | solution.py:435
  67.2 14.4 %collective-permute-start.13 = (bf16[96,3072]{1,0:T(8,128)(2,1)S(1)}, bf16[96,3072]{1,0:T(8,128)(2,1)S(1)}, u32[]{:S(2)}, u32[]{:S(2)}) collective-permute-start(bf16[96,3072]{1,0:T(8,128)(2,1)S(1)} %collective-permute-done.7.refs_7_), channel_id=1, source_target_pairs={{0,1},{1,0},{2,3},{3,2},{4,5},{5,4},{6,7},{7,6},{8,9},{9,8},{10,11... | collective-permute-start | bytes 1769480 | tf_op jit(solution)/shard_map/ppermute | solution.py:435
  67.4 14.1 %collective-permute-start.14 = (bf16[128,2048]{1,0:T(8,128)(2,1)S(1)}, bf16[128,2048]{1,0:T(8,128)(2,1)S(1)}, u32[]{:S(2)}, u32[]{:S(2)}) collective-permute-start(bf16[128,2048]{1,0:T(8,128)(2,1)S(1)} %get-tuple-element.143), channel_id=1, source_target_pairs={{0,4},{4,0},{8,12},{12,8},{16,20},{20,16},{24,28},{28,24},{1,5},{5... | collective-permute-start | bytes 1572872 | tf_op jit(solution)/shard_map/ppermute | solution.py:471
  81.6 8.8 %collective-permute-start.19 = (bf16[384,256]{1,0:T(8,128)(2,1)S(1)}, bf16[384,256]{1,0:T(8,128)(2,1)S(1)}, u32[]{:S(2)}, u32[]{:S(2)}) collective-permute-start(bf16[384,256]{1,0:T(8,128)(2,1)S(1)} %get-tuple-element.148), channel_id=1, source_target_pairs={{0,8},{4,12},{8,24},{12,28},{24,16},{28,20},{16,0},{20,4},{1,9},{5... | collective-permute-start | bytes 589832 | tf_op jit(solution)/shard_map/ppermute | solution.py:499
  82.8 18.7 %collective-permute-start.15 = (bf16[96,3072]{1,0:T(8,128)(2,1)S(1)}, bf16[96,3072]{1,0:T(8,128)(2,1)S(1)}, u32[]{:S(2)}, u32[]{:S(2)}) collective-permute-start(bf16[96,3072]{1,0:T(8,128)(2,1)S(1)} %collective-permute-done.6.refs_1_.refs_9_), channel_id=1, source_target_pairs={{0,8},{4,12},{8,24},{12,28},{24,16},{28,20},{16,0},{20,4},{1,9},{5... | collective-permute-start | bytes 1769480 | tf_op jit(solution)/shard_map/ppermute | solution.py:432
  82.8 18.7 %collective-permute-start.17 = (bf16[96,3072]{1,0:T(8,128)(2,1)S(1)}, bf16[96,3072]{1,0:T(8,128)(2,1)S(1)}, u32[]{:S(2)}, u32[]{:S(2)}) collective-permute-start(bf16[96,3072]{1,0:T(8,128)(2,1)S(1)} %collective-permute-done.6.refs_1_.refs_9_), channel_id=1, source_target_pairs={{0,1},{1,0},{2,3},{3,2},{4,5},{5,4},{6,7},{7,6},{8,9},{9,8},{10,11... | collective-permute-start | bytes 1769480 | tf_op jit(solution)/shard_map/ppermute | solution.py:435
  82.8 18.7 %collective-permute-start.16 = (bf16[96,3072]{1,0:T(8,128)(2,1)S(1)}, bf16[96,3072]{1,0:T(8,128)(2,1)S(1)}, u32[]{:S(2)}, u32[]{:S(2)}) collective-permute-start(bf16[96,3072]{1,0:T(8,128)(2,1)S(1)} %collective-permute-done.10.refs_5_.refs_9_), channel_id=1, source_target_pairs={{0,2},{1,3},{2,0},{3,1},{4,6},{5,7},{6,4},{7,5},{8,10},{9,11},{10,... | collective-permute-start | bytes 1769480 | tf_op jit(solution)/shard_map/ppermute | solution.py:435
  84.3 17.2 %collective-permute-start.18 = (bf16[96,3072]{1,0:T(8,128)(2,1)S(1)}, bf16[96,3072]{1,0:T(8,128)(2,1)S(1)}, u32[]{:S(2)}, u32[]{:S(2)}) collective-permute-start(bf16[96,3072]{1,0:T(8,128)(2,1)S(1)} %collective-permute-done.11.refs_3_.refs_11_), channel_id=1, source_target_pairs={{0,1},{1,0},{2,3},{3,2},{4,5},{5,4},{6,7},{7,6},{8,9},{9,8},{10,11... | collective-permute-start | bytes 1769480 | tf_op jit(solution)/shard_map/ppermute | solution.py:435
  90.4 11.0 %collective-permute-start.20 = (bf16[128,2048]{1,0:T(8,128)(2,1)S(1)}, bf16[128,2048]{1,0:T(8,128)(2,1)S(1)}, u32[]{:S(2)}, u32[]{:S(2)}) collective-permute-start(bf16[128,2048]{1,0:T(8,128)(2,1)S(1)} %get-tuple-element.149), channel_id=1, source_target_pairs={{0,4},{4,0},{8,12},{12,8},{16,20},{20,16},{24,28},{28,24},{1,5},{5... | collective-permute-start | bytes 1572872 | tf_op jit(solution)/shard_map/ppermute | solution.py:471
  101.5 19.1 %collective-permute-start.21 = (bf16[96,3072]{1,0:T(8,128)(2,1)S(1)}, bf16[96,3072]{1,0:T(8,128)(2,1)S(1)}, u32[]{:S(2)}, u32[]{:S(2)}) collective-permute-start(bf16[96,3072]{1,0:T(8,128)(2,1)S(1)} %collective-permute-done.10.refs_5_.refs_9_), channel_id=1, source_target_pairs={{0,8},{4,12},{8,24},{12,28},{24,16},{28,20},{16,0},{20,4},{1,9},{5... | collective-permute-start | bytes 1769480 | tf_op jit(solution)/shard_map/ppermute | solution.py:432
  101.9 18.7 %collective-permute-start.23 = (bf16[96,3072]{1,0:T(8,128)(2,1)S(1)}, bf16[96,3072]{1,0:T(8,128)(2,1)S(1)}, u32[]{:S(2)}, u32[]{:S(2)}) collective-permute-start(bf16[96,3072]{1,0:T(8,128)(2,1)S(1)} %collective-permute-done.10.refs_5_.refs_9_), channel_id=1, source_target_pairs={{0,1},{1,0},{2,3},{3,2},{4,5},{5,4},{6,7},{7,6},{8,9},{9,8},{10,11... | collective-permute-start | bytes 1769480 | tf_op jit(solution)/shard_map/ppermute | solution.py:435
  101.9 18.7 %collective-permute-start.22 = (bf16[96,3072]{1,0:T(8,128)(2,1)S(1)}, bf16[96,3072]{1,0:T(8,128)(2,1)S(1)}, u32[]{:S(2)}, u32[]{:S(2)}) collective-permute-start(bf16[96,3072]{1,0:T(8,128)(2,1)S(1)} %collective-permute-done.15.refs_1_.refs_13_), channel_id=1, source_target_pairs={{0,2},{1,3},{2,0},{3,1},{4,6},{5,7},{6,4},{7,5},{8,10},{9,11},{10,... | collective-permute-start | bytes 1769480 | tf_op jit(solution)/shard_map/ppermute | solution.py:435
  103.4 17.2 %collective-permute-start.24 = (bf16[96,3072]{1,0:T(8,128)(2,1)S(1)}, bf16[96,3072]{1,0:T(8,128)(2,1)S(1)}, u32[]{:S(2)}, u32[]{:S(2)}) collective-permute-start(bf16[96,3072]{1,0:T(8,128)(2,1)S(1)} %collective-permute-done.16.refs_7_.refs_11_), channel_id=1, source_target_pairs={{0,1},{1,0},{2,3},{3,2},{4,5},{5,4},{6,7},{7,6},{8,9},{9,8},{10,11... | collective-permute-start | bytes 1769480 | tf_op jit(solution)/shard_map/ppermute | solution.py:435
  103.6 16.5 %collective-permute-start.25 = (bf16[384,256]{1,0:T(8,128)(2,1)S(1)}, bf16[384,256]{1,0:T(8,128)(2,1)S(1)}, u32[]{:S(2)}, u32[]{:S(2)}) collective-permute-start(bf16[384,256]{1,0:T(8,128)(2,1)S(1)} %get-tuple-element.153), channel_id=1, source_target_pairs={{0,16},{4,20},{8,0},{12,4},{24,8},{28,12},{16,24},{20,28},{1,17},{... | collective-permute-start | bytes 589832 | tf_op jit(solution)/shard_map/ppermute | solution.py:505
  120.6 7.4 %collective-permute-start.27 = (bf16[96,3072]{1,0:T(8,128)(2,1)S(1)}, bf16[96,3072]{1,0:T(8,128)(2,1)S(1)}, u32[]{:S(2)}, u32[]{:S(2)}) collective-permute-start(bf16[96,3072]{1,0:T(8,128)(2,1)S(1)} %collective-permute-done.15.refs_1_.refs_13_), channel_id=1, source_target_pairs={{0,1},{1,0},{2,3},{3,2},{4,5},{5,4},{6,7},{7,6},{8,9},{9,8},{10,11... | collective-permute-start | bytes 1769480 | tf_op jit(solution)/shard_map/ppermute | solution.py:435
  120.7 7.4 %collective-permute-start.28 = (bf16[96,3072]{1,0:T(8,128)(2,1)S(1)}, bf16[96,3072]{1,0:T(8,128)(2,1)S(1)}, u32[]{:S(2)}, u32[]{:S(2)}) collective-permute-start(bf16[96,3072]{1,0:T(8,128)(2,1)S(1)} %collective-permute-done.22.refs_3_.refs_15_), channel_id=1, source_target_pairs={{0,1},{1,0},{2,3},{3,2},{4,5},{5,4},{6,7},{7,6},{8,9},{9,8},{10,11... | collective-permute-start | bytes 1769480 | tf_op jit(solution)/shard_map/ppermute | solution.py:435
  121.2 15.3 %collective-permute-start.26 = (bf16[96,3072]{1,0:T(8,128)(2,1)S(1)}, bf16[96,3072]{1,0:T(8,128)(2,1)S(1)}, u32[]{:S(2)}, u32[]{:S(2)}) collective-permute-start(bf16[96,3072]{1,0:T(8,128)(2,1)S(1)} %collective-permute-done.21.refs_1_.refs_13_), channel_id=1, source_target_pairs={{0,2},{1,3},{2,0},{3,1},{4,6},{5,7},{6,4},{7,5},{8,10},{9,11},{10,... | collective-permute-start | bytes 1769480 | tf_op jit(solution)/shard_map/ppermute | solution.py:435
  122.9 9.7 %collective-permute-start.29 = (bf16[384,256]{1,0:T(8,128)(2,1)S(1)}, bf16[384,256]{1,0:T(8,128)(2,1)S(1)}, u32[]{:S(2)}, u32[]{:S(2)}) collective-permute-start(bf16[384,256]{1,0:T(8,128)(2,1)S(1)} %get-tuple-element.164), channel_id=1, source_target_pairs={{0,24},{4,28},{8,16},{12,20},{24,0},{28,4},{16,8},{20,12},{1,25},{... | collective-permute-start | bytes 589832 | tf_op jit(solution)/shard_map/ppermute | solution.py:517
  123.9 10.5 %collective-permute-start.30 = (bf16[384,256]{1,0:T(8,128)(2,1)S(1)}, bf16[384,256]{1,0:T(8,128)(2,1)S(1)}, u32[]{:S(2)}, u32[]{:S(2)}) collective-permute-start(bf16[384,256]{1,0:T(8,128)(2,1)S(1)} %product.6), channel_id=1, source_target_pairs={{0,16},{4,20},{8,0},{12,4},{24,8},{28,12},{16,24},{20,28},{1,17},{... | collective-permute-start | bytes 589832 | tf_op jit(solution)/shard_map/ppermute | solution.py:518
  128.0 17.7 %collective-permute-start.32 = (bf16[96,3072]{1,0:T(8,128)(2,1)S(1)}, bf16[96,3072]{1,0:T(8,128)(2,1)S(1)}, u32[]{:S(2)}, u32[]{:S(2)}) collective-permute-start(bf16[96,3072]{1,0:T(8,128)(2,1)S(1)} %collective-permute-done.21.refs_1_.refs_13_), channel_id=1, source_target_pairs={{0,1},{1,0},{2,3},{3,2},{4,5},{5,4},{6,7},{7,6},{8,9},{9,8},{10,11... | collective-permute-start | bytes 1769480 | tf_op jit(solution)/shard_map/ppermute | solution.py:435
  136.5 9.2 %collective-permute-start.31 = (bf16[96,3072]{1,0:T(8,128)(2,1)S(1)}, bf16[96,3072]{1,0:T(8,128)(2,1)S(1)}, u32[]{:S(2)}, u32[]{:S(2)}) collective-permute-start(bf16[96,3072]{1,0:T(8,128)(2,1)S(1)} %collective-permute-done.26.refs_3_.refs_15_), channel_id=1, source_target_pairs={{0,1},{1,0},{2,3},{3,2},{4,5},{5,4},{6,7},{7,6},{8,9},{9,8},{10,11... | collective-permute-start | bytes 1769480 | tf_op jit(solution)/shard_map/ppermute | solution.py:435
  136.5 9.2 %collective-permute-start.33 = (bf16[384,256]{1,0:T(8,128)(2,1)S(1)}, bf16[384,256]{1,0:T(8,128)(2,1)S(1)}, u32[]{:S(2)}, u32[]{:S(2)}) collective-permute-start(bf16[384,256]{1,0:T(8,128)(2,1)S(1)} %product.8), channel_id=1, source_target_pairs={{0,24},{4,28},{8,16},{12,20},{24,0},{28,4},{16,8},{20,12},{1,25},{... | collective-permute-start | bytes 589832 | tf_op jit(solution)/shard_map/ppermute | solution.py:522
  145.7 37.0 %collective-permute-start.38 = (bf16[128,3072]{1,0:T(8,128)(2,1)}, bf16[128,3072]{1,0:T(8,128)(2,1)}, u32[]{:S(2)}, u32[]{:S(2)}) collective-permute-start(bf16[128,3072]{1,0:T(8,128)(2,1)} %get-tuple-element.211), channel_id=1, source_target_pairs={{0,4},{4,0},{8,12},{12,8},{16,20},{20,16},{24,28},{28,24},{1,5},{5... | collective-permute-start | bytes 2359304 | tf_op jit(solution)/shard_map/ppermute | solution.py:535
  149.1 9.1 %collective-permute-start.34 = (bf16[384,256]{1,0:T(8,128)(2,1)S(1)}, bf16[384,256]{1,0:T(8,128)(2,1)S(1)}, u32[]{:S(2)}, u32[]{:S(2)}) collective-permute-start(bf16[384,256]{1,0:T(8,128)(2,1)S(1)} %product.9), channel_id=1, source_target_pairs={{0,8},{4,12},{8,24},{12,28},{24,16},{28,20},{16,0},{20,4},{1,9},{5... | collective-permute-start | bytes 589832 | tf_op jit(solution)/shard_map/ppermute | solution.py:533
  159.4 1.2 collective-permute-start.35
  160.6 3.6 %collective-permute-start.37 = (f32[1,1024]{1,0:T(1,128)S(1)}, f32[1,1024]{1,0:T(1,128)S(1)}, u32[]{:S(2)}, u32[]{:S(2)}) collective-permute-start(f32[1,1024]{1,0:T(1,128)S(1)} %get-tuple-element.198), channel_id=1, source_target_pairs={{0,8},{4,12},{8,0},{12,4},{16,24},{20,28},{24,16},{28,20},{1,9},{5... | collective-permute-start | bytes 12296 | tf_op jit(solution)/shard_map/ppermute | solution.py:546
  160.8 3.6 %collective-permute-start.36 = (f32[1,384]{1,0:T(1,128)S(1)}, f32[1,384]{1,0:T(1,128)S(1)}, u32[]{:S(2)}, u32[]{:S(2)}) collective-permute-start(f32[1,384]{1,0:T(1,128)S(1)} %add.141.here_ref), channel_id=1, source_target_pairs={{0,2},{1,3},{2,0},{3,1},{4,6},{5,7},{6,4},{7,5},{8,10},{9,11},{10,... | collective-permute-start | bytes 4616 | tf_op jit(solution)/shard_map/ppermute | solution.py:435
  167.5 15.3 %all-to-all-start.2 = ((bf16[8,144,128]{2,1,0:T(8,128)(2,1)}), bf16[8,144,128]{2,1,0:T(8,128)(2,1)S(1)}, u32[]{:S(2)}, u32[]{:S(2)}) async-start(bf16[8,144,128]{2,1,0:T(8,128)(2,1)} %copy-done.20), calls=%async_computation.2 | async-start | bytes 589824 | tf_op jit(solution)/shard_map/all_to_all | solution.py:552
  171.5 10.5 %collective-permute-start.40 = (bf16[128,1024]{1,0:T(8,128)(2,1)}, bf16[128,1024]{1,0:T(8,128)(2,1)S(1)}, u32[]{:S(2)}, u32[]{:S(2)}) collective-permute-start(bf16[128,1024]{1,0:T(8,128)(2,1)} %copy-done.28), channel_id=1, source_target_pairs={{0,4},{4,0},{8,12},{12,8},{16,20},{20,16},{24,28},{28,24},{1,5},{5... | collective-permute-start | bytes 786440 | tf_op jit(solution)/shard_map/ppermute | solution.py:559
  173.5 8.5 %collective-permute-start.39 = (f32[1,1024]{1,0:T(1,128)S(1)}, f32[1,1024]{1,0:T(1,128)S(1)}, u32[]{:S(2)}, u32[]{:S(2)}) collective-permute-start(f32[1,1024]{1,0:T(1,128)S(1)} %add.142), channel_id=1, source_target_pairs={{0,4},{4,0},{8,12},{12,8},{16,20},{20,16},{24,28},{28,24},{1,5},{5... | collective-permute-start | bytes 12296 | tf_op jit(solution)/shard_map/ppermute | solution.py:555
  182.8 19.1 %collective-permute-start.41 = (bf16[128,2048]{1,0:T(8,128)(2,1)}, bf16[128,2048]{1,0:T(8,128)(2,1)}, u32[]{:S(2)}, u32[]{:S(2)}) collective-permute-start(bf16[128,2048]{1,0:T(8,128)(2,1)} %copy-done.27), channel_id=1, source_target_pairs={{0,4},{4,0},{8,12},{12,8},{16,20},{20,16},{24,28},{28,24},{1,5},{5... | collective-permute-start | bytes 1572872 | tf_op jit(solution)/shard_map/ppermute | solution.py:559
  184.6 13.8 %all-to-all-start.3 = ((bf16[8,128,128]{2,1,0:T(8,128)(2,1)}), bf16[8,128,128]{2,1,0:T(8,128)(2,1)S(1)}, u32[]{:S(2)}, u32[]{:S(2)}) async-start(bf16[8,128,128]{2,1,0:T(8,128)(2,1)} %scan.3), calls=%async_computation.3 | async-start | bytes 524288 | tf_op jit(solution)/shard_map/all_to_all | solution.py:573
  189.5 8.2 %collective-permute-start.42 = (f32[1,1024]{1,0:T(1,128)S(1)}, f32[1,1024]{1,0:T(1,128)S(1)}, u32[]{:S(2)}, u32[]{:S(2)}) collective-permute-start(f32[1,1024]{1,0:T(1,128)S(1)} %add.143), channel_id=1, source_target_pairs={{0,16},{4,20},{8,24},{12,28},{16,0},{20,4},{24,8},{28,12},{1,17},{... | collective-permute-start | bytes 12296 | tf_op jit(solution)/shard_map/ppermute | solution.py:577
  (30 other events, 203.8 us)

commit v15 on v14

--- a/solution.py
+++ b/solution.py
@@ -526,7 +526,7 @@
 
     fb3, nb3 = near_of(yb3), near_of(rb3)
     lots = [[ra1, na1, ya1, fa1], [ra2, na2, ya2, fa2], last_lot]
-    (early,) = outer(normed, grad_out, lots, 0, own, (0, 6))
+    (early,) = outer(normed, grad_out, lots, 0, own, (0, 3))
     fb3, nb3, three, early, returned = hold((fb3, nb3, three, early, returned))
     last_lot = [rb3, nb3, yb3, fb3]
     three = product(tokens, [last_lot], weight_own, others, 1, True, three)
@@ -534,7 +534,7 @@
     flat = [early[0]]
     flat += [lax.ppermute(early[s], "ctx", pair_perm(count, s)) for s in range(1, minor)]
     lots = [[rb1, nb1, yb1, fb1], [rb2, nb2, yb2, fb2], last_lot]
-    late = outer([after(normed[0], three)] + normed[1:], grad_out, lots, 1, own, (0, 2, 6))
+    late = outer([after(normed[0], three)] + normed[1:], grad_out, lots, 1, own, (0, 1, 3))
     returned, late = hold((returned, late))
 
     grad, gain_sum, inner = whole(

time: 205 us -> 205 us (level)
  Pallas kernels: 49.5 us -> 47.3 us
    pallas_call x2, Pallas kernels: 12.5 us -> 10.3 us  [outer(): pl.pallas_call(functools.partial(outer_kernel, 1 + len(flat), own, cuts),...]
  transfers between devices with their start and end apart: 47 -> 47, of which waited for: 21 -> 22; matrix products, arithmetic and copies ran while one was open for 1% -> 1% of each run, Pallas kernels for 23% -> 22%
where the time goes in v15:
time: 205 us; the launch traced here: 204 us
  waiting for transfers between devices  74.4 us (36%)
  starting transfers between devices  63.6 us (31%)
  Pallas kernels  47.3 us (23%)
  local copies, waits for them, and re-layouts  14.6 us (7%)
  other arithmetic  2.82 us (1%)
    ppermute x3, waiting for transfers between devices, swap(): lax.ppermute(part, 'ctx', pair_perm(count, -s))  27.9 us
    pallas_call x10, Pallas kernels, whole(): pl.pallas_call(kernel, in_specs=[SCALAR if a is tokens else full for a in...  16.5 us
    pallas_call x5, Pallas kernels, product(): pl.pallas_call(functools.partial(product_kernel, [len(x) for x in lots],...  16.2 us
    ppermute x22, starting transfers between devices, over(): return lax.ppermute(x, 'head', perm)  12.7 us
    unnamed x62, local copies, waits for them, and re-layouts  12.1 us
    pallas_call x2, Pallas kernels, outer(): pl.pallas_call(functools.partial(outer_kernel, 1 + len(flat), own, cuts),...  10.3 us
    ppermute x6, starting transfers between devices, ring(): return lax.ppermute(x, 'ctx', ring_perm(count, 1))  9.41 us
    all_to_all x1, waiting for transfers between devices, shards(): spread = lax.all_to_all(put, 'ctx', 0, 0, tiled=True)  9.3 us
  transfers between devices with their start and end apart: 47, of which 22 were waited for; matrix products, arithmetic and copies ran while one was open for 1% of the time, Pallas kernels for 22%

profile of v15, /device:TPU:0, one launch (start us, length us, event | category | flops | bytes accessed | tf_op | source)
XLA Modules:
  0.0 203.8 jit_solution(10373462413594959279)
XLA Ops:
  0.7 2.4 %constant_dynamic-slice_fusion = (bf16[96,3072]{1,0:T(8,128)(2,1)}, bf16[96,3072]{1,0:T(8,128)(2,1)}) fusion(bf16[384,6144]{1,0:T(8,128)(2,1)} %refs_4_.3, s32[]{:T(128)S(6)} %select_n.84), kind=kLoop, calls=%fused_computation.46 | loop fusion | bytes 2359300 | tf_op jit(solution)/shard_map/dynamic_slice | solution.py:410
  3.1 3.0 %collective-permute-start = (bf16[96,3072]{1,0:T(8,128)(2,1)}, bf16[96,3072]{1,0:T(8,128)(2,1)}, u32[]{:S(2)}, u32[]{:S(2)}) collective-permute-start(bf16[96,3072]{1,0:T(8,128)(2,1)} %get-tuple-element.232), channel_id=1, source_target_pairs={{0,8},{4,12},{8,24},{12,28},{24,16},{28,20},{16,0},{20,4},{1,9},{5... | collective-permute-start | bytes 1769480 | tf_op jit(solution)/shard_map/ppermute | solution.py:432
  6.2 2.6 %states.1 = (bf16[8,144,128]{2,1,0:T(8,128)(2,1)}, f32[8,384]{1,0:T(8,128)S(1)}, f32[384,8]{1,0:T(8,128)S(1)}) custom-call(f32[8,384]{1,0:T(8,128)S(1)} %copy-done.26, bf16[384,1024]{1,0:T(8,128)(2,1)S(1)} %copy-done.3, bf16[384,1024]{1,0:T(8,128)(2,1)S(1)} %copy-done.4), custom_call_target="tpu_custom_call" | custom-call | flops 1000 | bytes 1000 | tf_op jit(solution)/shard_map/states/pallas_call | solution.py:421
  8.7 4.8 %all-to-all-start = ((bf16[8,144,128]{2,1,0:T(8,128)(2,1)}), bf16[8,144,128]{2,1,0:T(8,128)(2,1)S(1)}, u32[]{:S(2)}, u32[]{:S(2)}) async-start(bf16[8,144,128]{2,1,0:T(8,128)(2,1)} %get-tuple-element.118), calls=%async_computation | async-start | bytes 589824 | tf_op jit(solution)/shard_map/all_to_all | solution.py:454
  13.5 2.0 collective-permute-start.1
  15.6 1.9 weights.1.intra_ref
  18.6 9.3 %all-to-all-done.in_ref = bf16[8,144,128]{2,1,0:T(8,128)(2,1)S(1)} async-done(((bf16[8,144,128]{2,1,0:T(8,128)(2,1)}), bf16[8,144,128]{2,1,0:T(8,128)(2,1)S(1)}, u32[]{:S(2)}, u32[]{:S(2)}) %all-to-all-start) | async-done | bytes 294944 | tf_op jit(solution)/shard_map/all_to_all | solution.py:454
  27.9 1.9 collective-permute-start.2
  30.6 5.8 %all-to-all-start.1 = ((bf16[8,128,128]{2,1,0:T(8,128)(2,1)}), bf16[8,128,128]{2,1,0:T(8,128)(2,1)S(1)}, u32[]{:S(2)}, u32[]{:S(2)}) async-start(bf16[8,128,128]{2,1,0:T(8,128)(2,1)} %copy-done.13), calls=%async_computation.1 | async-start | bytes 524288 | tf_op jit(solution)/shard_map/all_to_all | solution.py:462
  36.4 2.2 %fusion.order_ref = bf16[1024,1024]{1,0:T(8,128)(2,1)} fusion(s32[1024]{0:T(1024)S(1)} %fusion.4), kind=kLoop, calls=%fused_computation.1 | loop fusion | flops 2097152 | bytes 2101248 | tf_op jit(solution)/shard_map/convert_element_type | solution.py:384
  38.6 3.5 %collective-permute-done.1.refs_5_ = bf16[96,3072]{1,0:T(8,128)(2,1)} collective-permute-done((bf16[96,3072]{1,0:T(8,128)(2,1)}, bf16[96,3072]{1,0:T(8,128)(2,1)}, u32[]{:S(2)}, u32[]{:S(2)}) %collective-permute-start.1) | collective-permute-done | bytes 589856 | tf_op jit(solution)/shard_map/ppermute | solution.py:432
  42.0 3.3 %all-to-all-done.1.state_ref = bf16[8,128,128]{2,1,0:T(8,128)(2,1)S(1)} async-done(((bf16[8,128,128]{2,1,0:T(8,128)(2,1)}), bf16[8,128,128]{2,1,0:T(8,128)(2,1)S(1)}, u32[]{:S(2)}, u32[]{:S(2)}) %all-to-all-start.1) | async-done | bytes 262176 | tf_op jit(solution)/shard_map/all_to_all | solution.py:462
  46.8 1.5 collective-permute-start.7
  53.7 8.7 %collective-permute-done.9.refs_4_.refs_10_.refs_6_ = bf16[128,2048]{1,0:T(8,128)(2,1)S(1)} collective-permute-done((bf16[128,2048]{1,0:T(8,128)(2,1)S(1)}, bf16[128,2048]{1,0:T(8,128)(2,1)S(1)}, u32[]{:S(2)}, u32[]{:S(2)}) %collective-permute-start.9) | collective-permute-done | bytes 524320 | tf_op jit(solution)/shard_map/ppermute | solution.py:471
  63.0 2.7 %collective-permute-start.10 = (bf16[96,3072]{1,0:T(8,128)(2,1)}, bf16[96,3072]{1,0:T(8,128)(2,1)S(1)}, u32[]{:S(2)}, u32[]{:S(2)}) collective-permute-start(bf16[96,3072]{1,0:T(8,128)(2,1)} %collective-permute-done.1.refs_5_), channel_id=1, source_target_pairs={{0,8},{4,12},{8,24},{12,28},{24,16},{28,20},{16,0},{20,4},{1,9},{5... | collective-permute-start | bytes 1769480 | tf_op jit(solution)/shard_map/ppermute | solution.py:432
  65.7 1.5 collective-permute-start.11
  68.9 1.6 copy-done.1
  71.8 9.7 %collective-permute-done.14.refs_5_.refs_11_.refs_7_.refs_6_ = bf16[128,2048]{1,0:T(8,128)(2,1)S(1)} collective-permute-done((bf16[128,2048]{1,0:T(8,128)(2,1)S(1)}, bf16[128,2048]{1,0:T(8,128)(2,1)S(1)}, u32[]{:S(2)}, u32[]{:S(2)}) %collective-permute-start.14) | collective-permute-done | bytes 524320 | tf_op jit(solution)/shard_map/ppermute | solution.py:471
  84.5 5.9 %collective-permute-done.19.refs_1_ = bf16[384,256]{1,0:T(8,128)(2,1)S(1)} collective-permute-done((bf16[384,256]{1,0:T(8,128)(2,1)S(1)}, bf16[384,256]{1,0:T(8,128)(2,1)S(1)}, u32[]{:S(2)}, u32[]{:S(2)}) %collective-permute-start.19) | collective-permute-done | bytes 196640 | tf_op jit(solution)/shard_map/ppermute | solution.py:499
  91.8 9.5 %collective-permute-done.20.refs_6_.refs_12_.refs_7_ = bf16[128,2048]{1,0:T(8,128)(2,1)S(1)} collective-permute-done((bf16[128,2048]{1,0:T(8,128)(2,1)S(1)}, bf16[128,2048]{1,0:T(8,128)(2,1)S(1)}, u32[]{:S(2)}, u32[]{:S(2)}) %collective-permute-start.20) | collective-permute-done | bytes 524320 | tf_op jit(solution)/shard_map/ppermute | solution.py:471
  101.9 1.5 collective-permute-start.22
  103.6 2.7 %collective-permute-start.25 = (bf16[384,256]{1,0:T(8,128)(2,1)S(1)}, bf16[384,256]{1,0:T(8,128)(2,1)S(1)}, u32[]{:S(2)}, u32[]{:S(2)}) collective-permute-start(bf16[384,256]{1,0:T(8,128)(2,1)S(1)} %get-tuple-element.153), channel_id=1, source_target_pairs={{0,16},{4,20},{8,0},{12,4},{24,8},{28,12},{16,24},{20,28},{1,17},{... | collective-permute-start | bytes 589832 | tf_op jit(solution)/shard_map/ppermute | solution.py:505
  106.3 3.7 %product.5.refs_0_ = bf16[384,256]{1,0:T(8,128)(2,1)S(1)} custom-call(s32[1]{0:T(128)} %bitcast.1.mine_ref.refs_0_, bf16[384,6144]{1,0:T(8,128)(2,1)S(1)} %bitcast.6, bf16[384,6144]{1,0:T(8,128)(2,1)S(1)} %bitcast.6, bf16[128,6144]{1,0:T(8,128)(2,1)S(1)} %bitcast.8, bf16[128,2048]{1,0:T(8,128)(2,1)S(1)} %collective-permute-done.9.refs_4_.refs_10_.refs_6_, ...), custom_call_target="tpu_custom_call" | custom-call | flops 1000 | bytes 1000 | tf_op jit(solution)/shard_map/product/pallas_call | solution.py:216
  110.0 5.2 %product.6 = bf16[384,256]{1,0:T(8,128)(2,1)S(1)} custom-call(s32[1]{0:T(128)} %bitcast.1.mine_ref.refs_0_, bf16[96,3072]{1,0:T(8,128)(2,1)} %collective-permute-done.refs_1_.refs_5_, bf16[96,3072]{1,0:T(8,128)(2,1)S(1)} %collective-permute-done.4.refs_2_.refs_6_, bf16[96,3072]{1,0:T(8,128)(2,1)} %collective-permute-done.2.refs_3_.refs_7_, ...), custom_call_target="tpu_custom_call" | custom-call | flops 1000 | bytes 1000 | tf_op jit(solution)/shard_map/product/pallas_call | solution.py:216
  115.2 4.9 %collective-permute-done.25.refs_3_ = bf16[384,256]{1,0:T(8,128)(2,1)S(1)} collective-permute-done((bf16[384,256]{1,0:T(8,128)(2,1)S(1)}, bf16[384,256]{1,0:T(8,128)(2,1)S(1)}, u32[]{:S(2)}, u32[]{:S(2)}) %collective-permute-start.25) | collective-permute-done | bytes 196640 | tf_op jit(solution)/shard_map/ppermute | solution.py:505
  121.2 1.7 collective-permute-start.26
  124.1 3.8 %product.8 = bf16[384,256]{1,0:T(8,128)(2,1)S(1)} custom-call(s32[1]{0:T(128)} %bitcast.1.mine_ref.refs_0_, bf16[96,3072]{1,0:T(8,128)(2,1)S(1)} %collective-permute-done.6.refs_1_.refs_9_, bf16[96,3072]{1,0:T(8,128)(2,1)S(1)} %collective-permute-done.17.refs_2_.refs_10_, bf16[96,3072]{1,0:T(8,128)(2,1)S(1)} %collective-permute-done.11.refs_3_.refs_11_, ...), custom_call_target="tpu_custom_call" | custom-call | flops 1000 | bytes 1000 | tf_op jit(solution)/shard_map/product/pallas_call | solution.py:216
  128.1 1.8 product.7.refs_8_
  129.8 2.7 %collective-permute-done.29.refs_2_ = bf16[384,256]{1,0:T(8,128)(2,1)S(1)} collective-permute-done((bf16[384,256]{1,0:T(8,128)(2,1)S(1)}, bf16[384,256]{1,0:T(8,128)(2,1)S(1)}, u32[]{:S(2)}, u32[]{:S(2)}) %collective-permute-start.29) | collective-permute-done | bytes 196640 | tf_op jit(solution)/shard_map/ppermute | solution.py:517
  132.6 1.8 collective-permute-done.30.refs_1_
  134.4 2.1 %collective-permute-done.26.refs_3_.refs_15_ = bf16[96,3072]{1,0:T(8,128)(2,1)S(1)} collective-permute-done((bf16[96,3072]{1,0:T(8,128)(2,1)S(1)}, bf16[96,3072]{1,0:T(8,128)(2,1)S(1)}, u32[]{:S(2)}, u32[]{:S(2)}) %collective-permute-start.26) | collective-permute-done | bytes 589856 | tf_op jit(solution)/shard_map/ppermute | solution.py:435
  137.7 5.5 %outer.2 = (bf16[128,3072]{1,0:T(8,128)(2,1)S(1)}, bf16[128,3072]{1,0:T(8,128)(2,1)}) custom-call(bf16[384,256]{1,0:T(8,128)(2,1)S(1)} %get-tuple-element.186.refs_0_, bf16[384,256]{1,0:T(8,128)(2,1)S(1)} %collective-permute-done.19.refs_1_, bf16[384,256]{1,0:T(8,128)(2,1)S(1)} %collective-permute-done.29.refs_2_, ...), custom_call_target="tpu_custom_call" | custom-call | flops 1000 | bytes 1000 | tf_op jit(solution)/shard_map/outer/pallas_call | solution.py:271
  143.2 2.5 %collective-permute-done.33.refs_2_ = bf16[384,256]{1,0:T(8,128)(2,1)S(1)} collective-permute-done((bf16[384,256]{1,0:T(8,128)(2,1)S(1)}, bf16[384,256]{1,0:T(8,128)(2,1)S(1)}, u32[]{:S(2)}, u32[]{:S(2)}) %collective-permute-start.33) | collective-permute-done | bytes 196640 | tf_op jit(solution)/shard_map/ppermute | solution.py:522
  145.7 1.6 collective-permute-start.38
  147.3 1.7 product.9
  149.1 3.3 %collective-permute-start.34 = (bf16[384,256]{1,0:T(8,128)(2,1)S(1)}, bf16[384,256]{1,0:T(8,128)(2,1)S(1)}, u32[]{:S(2)}, u32[]{:S(2)}) collective-permute-start(bf16[384,256]{1,0:T(8,128)(2,1)S(1)} %product.9), channel_id=1, source_target_pairs={{0,8},{4,12},{8,24},{12,28},{24,16},{28,20},{16,0},{20,4},{1,9},{5... | collective-permute-start | bytes 589832 | tf_op jit(solution)/shard_map/ppermute | solution.py:533
  152.4 4.8 %outer.3 = (bf16[128,1024]{1,0:T(8,128)(2,1)S(1)}, bf16[128,1024]{1,0:T(8,128)(2,1)S(1)}, bf16[128,2048]{1,0:T(8,128)(2,1)S(1)}, bf16[128,2048]{1,0:T(8,128)(2,1)S(1)}) custom-call(bf16[384,256]{1,0:T(8,128)(2,1)S(1)} %get-tuple-element.186.refs_0_, bf16[384,256]{1,0:T(8,128)(2,1)S(1)} %collective-permute-done.19.refs_1_, ...), custom_call_target="tpu_custom_call" | custom-call | flops 1000 | bytes 1000 | tf_op jit(solution)/shard_map/outer/pallas_call | solution.py:271
  161.7 2.1 %collective-permute-done.37 = f32[1,1024]{1,0:T(1,128)S(1)} collective-permute-done((f32[1,1024]{1,0:T(1,128)S(1)}, f32[1,1024]{1,0:T(1,128)S(1)}, u32[]{:S(2)}, u32[]{:S(2)}) %collective-permute-start.37) | collective-permute-done | bytes 4128 | tf_op jit(solution)/shard_map/ppermute | solution.py:546
  167.7 3.7 %all-to-all-start.2 = ((bf16[8,144,128]{2,1,0:T(8,128)(2,1)}), bf16[8,144,128]{2,1,0:T(8,128)(2,1)S(1)}, u32[]{:S(2)}, u32[]{:S(2)}) async-start(bf16[8,144,128]{2,1,0:T(8,128)(2,1)} %copy-done.20), calls=%async_computation.2 | async-start | bytes 589824 | tf_op jit(solution)/shard_map/all_to_all | solution.py:552
  171.4 2.0 collective-permute-start.40
  174.6 4.5 %inside.1 = (bf16[384,1024]{1,0:T(8,128)(2,1)}, bf16[2,384,1024]{2,1,0:T(8,128)(2,1)S(1)}) custom-call(bf16[384,1024]{1,0:T(8,128)(2,1)S(1)} %copy-done.17, bf16[384,1024]{1,0:T(8,128)(2,1)S(1)} %copy-done.8, bf16[384,1024]{1,0:T(8,128)(2,1)S(1)} %copy-done.3, bf16[384,1024]{1,0:T(8,128)(2,1)S(1)} %copy-done.5, f32[8,384]{1,0:T(8,128)S(1)} %get-tuple-element.119.run_ref, ...), custom_call_target="tpu_custom_call" | custom-call | flops 1000 | bytes 1000 | tf_op jit(solution)/shard_map/inside/pallas_call | solution.py:421
  180.2 1.7 collective-permute-done.39
  184.5 4.9 %all-to-all-start.3 = ((bf16[8,128,128]{2,1,0:T(8,128)(2,1)}), bf16[8,128,128]{2,1,0:T(8,128)(2,1)S(1)}, u32[]{:S(2)}, u32[]{:S(2)}) async-start(bf16[8,128,128]{2,1,0:T(8,128)(2,1)} %scan.3), calls=%async_computation.3 | async-start | bytes 524288 | tf_op jit(solution)/shard_map/all_to_all | solution.py:573
  189.4 2.9 %collective-permute-start.42 = (f32[1,1024]{1,0:T(1,128)S(1)}, f32[1,1024]{1,0:T(1,128)S(1)}, u32[]{:S(2)}, u32[]{:S(2)}) collective-permute-start(f32[1,1024]{1,0:T(1,128)S(1)} %add.143), channel_id=1, source_target_pairs={{0,16},{4,20},{8,24},{12,28},{16,0},{20,4},{24,8},{28,12},{1,17},{... | collective-permute-start | bytes 12296 | tf_op jit(solution)/shard_map/ppermute | solution.py:577
  193.5 2.2 %sum.2.refs_0_ = bf16[128,6144]{1,0:T(8,128)(2,1)} custom-call(bf16[128,3072]{1,0:T(8,128)(2,1)S(1)} %copy-done.15, bf16[128,3072]{1,0:T(8,128)(2,1)} %collective-permute-done.38.refs_1_), custom_call_target="tpu_custom_call" | custom-call | flops 1000 | bytes 1000 | tf_op jit(solution)/shard_map/sum/pallas_call | solution.py:307
  195.6 2.0 collective-permute-done.42
  199.6 2.0 %outside.1 = (bf16[384,1024]{1,0:T(8,128)(2,1)}, bf16[384,1024]{1,0:T(8,128)(2,1)}) custom-call(bf16[384,1024]{1,0:T(8,128)(2,1)S(1)} %copy-done.3, bf16[384,1024]{1,0:T(8,128)(2,1)S(1)} %copy-done.5, bf16[8,128,128]{2,1,0:T(8,128)(2,1)S(1)} %all-to-all-done.3.state_ref, f32[384,8]{1,0:T(8,128)S(1)} %get-tuple-element.120.turned_ref, ...), custom_call_target="tpu_custom_call" | custom-call | flops 1000 | bytes 1000 | tf_op jit(solution)/shard_map/outside/pallas_call | solution.py:421
  201.7 2.1 %sum.3 = bf16[128,6144]{1,0:T(8,128)(2,1)} custom-call(bf16[128,6144]{1,0:T(8,128)(2,1)} %sum.2.refs_0_, bf16[128,1024]{1,0:T(8,128)(2,1)S(1)} %copy-done.22, bf16[128,1024]{1,0:T(8,128)(2,1)S(1)} %copy-done.24, bf16[128,2048]{1,0:T(8,128)(2,1)S(1)} %copy-done.19, bf16[128,2048]{1,0:T(8,128)(2,1)} %collective-permute-done.41.refs_4_), custom_call_target="tpu_custom_call", output_to_operand_aliasing={{}: (0, {})} | custom-call | flops 1000 | bytes 1000 | tf_op jit(solution)/shard_map/sum/pallas_call | solution.py:307
  (137 shorter events, 37.6 us)
Async XLA Ops:
  3.1 24.8 %collective-permute-start = (bf16[96,3072]{1,0:T(8,128)(2,1)}, bf16[96,3072]{1,0:T(8,128)(2,1)}, u32[]{:S(2)}, u32[]{:S(2)}) collective-permute-start(bf16[96,3072]{1,0:T(8,128)(2,1)} %get-tuple-element.232), channel_id=1, source_target_pairs={{0,8},{4,12},{8,24},{12,28},{24,16},{28,20},{16,0},{20,4},{1,9},{5... | collective-permute-start | bytes 1769480 | tf_op jit(solution)/shard_map/ppermute | solution.py:432
  8.7 19.2 %all-to-all-start = ((bf16[8,144,128]{2,1,0:T(8,128)(2,1)}), bf16[8,144,128]{2,1,0:T(8,128)(2,1)S(1)}, u32[]{:S(2)}, u32[]{:S(2)}) async-start(bf16[8,144,128]{2,1,0:T(8,128)(2,1)} %get-tuple-element.118), calls=%async_computation | async-start | bytes 589824 | tf_op jit(solution)/shard_map/all_to_all | solution.py:454
  13.5 28.5 %collective-permute-start.1 = (bf16[96,3072]{1,0:T(8,128)(2,1)}, bf16[96,3072]{1,0:T(8,128)(2,1)}, u32[]{:S(2)}, u32[]{:S(2)}) collective-permute-start(bf16[96,3072]{1,0:T(8,128)(2,1)} %get-tuple-element.122), channel_id=1, source_target_pairs={{0,8},{4,12},{8,24},{12,28},{24,16},{28,20},{16,0},{20,4},{1,9},{5... | collective-permute-start | bytes 1769480 | tf_op jit(solution)/shard_map/ppermute | solution.py:432
  15.6 90.7 %slice-start = ((s8[4718592]{0:T(1024)(128)(4,1)}), s8[524288]{0:T(1024)(128)(4,1)S(1)}, s32[]{:S(2)}) async-start(s8[4718592]{0:T(1024)(128)(4,1)} %bitcast.5), calls=%async_computation.4 | async-start | bytes 1048576
  27.9 17.4 %collective-permute-start.2 = (bf16[96,3072]{1,0:T(8,128)(2,1)}, bf16[96,3072]{1,0:T(8,128)(2,1)}, u32[]{:S(2)}, u32[]{:S(2)}) collective-permute-start(bf16[96,3072]{1,0:T(8,128)(2,1)} %collective-permute-done.refs_1_.refs_5_), channel_id=1, source_target_pairs={{0,2},{1,3},{2,0},{3,1},{4,6},{5,7},{6,4},{7,5},{8,10},{9,11},{10,... | collective-permute-start | bytes 1769480 | tf_op jit(solution)/shard_map/ppermute | solution.py:435
  30.6 14.8 %all-to-all-start.1 = ((bf16[8,128,128]{2,1,0:T(8,128)(2,1)}), bf16[8,128,128]{2,1,0:T(8,128)(2,1)S(1)}, u32[]{:S(2)}, u32[]{:S(2)}) async-start(bf16[8,128,128]{2,1,0:T(8,128)(2,1)} %copy-done.13), calls=%async_computation.1 | async-start | bytes 524288 | tf_op jit(solution)/shard_map/all_to_all | solution.py:462
  45.3 4.4 %collective-permute-start.4 = (bf16[96,3072]{1,0:T(8,128)(2,1)}, bf16[96,3072]{1,0:T(8,128)(2,1)S(1)}, u32[]{:S(2)}, u32[]{:S(2)}) collective-permute-start(bf16[96,3072]{1,0:T(8,128)(2,1)} %collective-permute-done.refs_1_.refs_5_), channel_id=1, source_target_pairs={{0,1},{1,0},{2,3},{3,2},{4,5},{5,4},{6,7},{7,6},{8,9},{9,8},{10,11... | collective-permute-start | bytes 1769480 | tf_op jit(solution)/shard_map/ppermute | solution.py:435
  45.4 17.6 %collective-permute-start.6 = (bf16[96,3072]{1,0:T(8,128)(2,1)}, bf16[96,3072]{1,0:T(8,128)(2,1)S(1)}, u32[]{:S(2)}, u32[]{:S(2)}) collective-permute-start(bf16[96,3072]{1,0:T(8,128)(2,1)} %collective-permute-done.refs_1_.refs_5_), channel_id=1, source_target_pairs={{0,8},{4,12},{8,24},{12,28},{24,16},{28,20},{16,0},{20,4},{1,9},{5... | collective-permute-start | bytes 1769480 | tf_op jit(solution)/shard_map/ppermute | solution.py:432
  46.6 3.0 %collective-permute-start.3 = (bf16[96,3072]{1,0:T(8,128)(2,1)}, bf16[96,3072]{1,0:T(8,128)(2,1)S(1)}, u32[]{:S(2)}, u32[]{:S(2)}) collective-permute-start(bf16[96,3072]{1,0:T(8,128)(2,1)} %collective-permute-done.2.refs_3_.refs_7_), channel_id=1, source_target_pairs={{0,1},{1,0},{2,3},{3,2},{4,5},{5,4},{6,7},{7,6},{8,9},{9,8},{10,11... | collective-permute-start | bytes 1769480 | tf_op jit(solution)/shard_map/ppermute | solution.py:435
  46.8 16.2 %collective-permute-start.7 = (bf16[96,3072]{1,0:T(8,128)(2,1)}, bf16[96,3072]{1,0:T(8,128)(2,1)S(1)}, u32[]{:S(2)}, u32[]{:S(2)}) collective-permute-start(bf16[96,3072]{1,0:T(8,128)(2,1)} %collective-permute-done.1.refs_5_), channel_id=1, source_target_pairs={{0,2},{1,3},{2,0},{3,1},{4,6},{5,7},{6,4},{7,5},{8,10},{9,11},{10,... | collective-permute-start | bytes 1769480 | tf_op jit(solution)/shard_map/ppermute | solution.py:435
  48.4 14.0 %collective-permute-start.9 = (bf16[128,2048]{1,0:T(8,128)(2,1)S(1)}, bf16[128,2048]{1,0:T(8,128)(2,1)S(1)}, u32[]{:S(2)}, u32[]{:S(2)}) collective-permute-start(bf16[128,2048]{1,0:T(8,128)(2,1)S(1)} %get-tuple-element.235), channel_id=1, source_target_pairs={{0,4},{4,0},{8,12},{12,8},{16,20},{20,16},{24,28},{28,24},{1,5},{5... | collective-permute-start | bytes 1572872 | tf_op jit(solution)/shard_map/ppermute | solution.py:471
  51.8 1.2 collective-permute-start.5
  53.0 9.9 %collective-permute-start.8 = (f32[1,384]{1,0:T(1,128)S(1)}, f32[1,384]{1,0:T(1,128)S(1)}, u32[]{:S(2)}, u32[]{:S(2)}) collective-permute-start(f32[1,384]{1,0:T(1,128)S(1)} %add.140.here_ref), channel_id=1, source_target_pairs={{0,2},{1,3},{2,0},{3,1},{4,6},{5,7},{6,4},{7,5},{8,10},{9,11},{10,... | collective-permute-start | bytes 4616 | tf_op jit(solution)/shard_map/ppermute | solution.py:435
  63.0 18.6 %collective-permute-start.10 = (bf16[96,3072]{1,0:T(8,128)(2,1)}, bf16[96,3072]{1,0:T(8,128)(2,1)S(1)}, u32[]{:S(2)}, u32[]{:S(2)}) collective-permute-start(bf16[96,3072]{1,0:T(8,128)(2,1)} %collective-permute-done.1.refs_5_), channel_id=1, source_target_pairs={{0,8},{4,12},{8,24},{12,28},{24,16},{28,20},{16,0},{20,4},{1,9},{5... | collective-permute-start | bytes 1769480 | tf_op jit(solution)/shard_map/ppermute | solution.py:432
  65.7 15.9 %collective-permute-start.12 = (bf16[96,3072]{1,0:T(8,128)(2,1)}, bf16[96,3072]{1,0:T(8,128)(2,1)S(1)}, u32[]{:S(2)}, u32[]{:S(2)}) collective-permute-start(bf16[96,3072]{1,0:T(8,128)(2,1)} %collective-permute-done.1.refs_5_), channel_id=1, source_target_pairs={{0,1},{1,0},{2,3},{3,2},{4,5},{5,4},{6,7},{7,6},{8,9},{9,8},{10,11... | collective-permute-start | bytes 1769480 | tf_op jit(solution)/shard_map/ppermute | solution.py:435
  65.7 15.9 %collective-permute-start.11 = (bf16[96,3072]{1,0:T(8,128)(2,1)S(1)}, bf16[96,3072]{1,0:T(8,128)(2,1)S(1)}, u32[]{:S(2)}, u32[]{:S(2)}) collective-permute-start(bf16[96,3072]{1,0:T(8,128)(2,1)S(1)} %collective-permute-done.6.refs_1_.refs_9_), channel_id=1, source_target_pairs={{0,2},{1,3},{2,0},{3,1},{4,6},{5,7},{6,4},{7,5},{8,10},{9,11},{10,... | collective-permute-start | bytes 1769480 | tf_op jit(solution)/shard_map/ppermute | solution.py:435
  67.2 14.4 %collective-permute-start.13 = (bf16[96,3072]{1,0:T(8,128)(2,1)S(1)}, bf16[96,3072]{1,0:T(8,128)(2,1)S(1)}, u32[]{:S(2)}, u32[]{:S(2)}) collective-permute-start(bf16[96,3072]{1,0:T(8,128)(2,1)S(1)} %collective-permute-done.7.refs_7_), channel_id=1, source_target_pairs={{0,1},{1,0},{2,3},{3,2},{4,5},{5,4},{6,7},{7,6},{8,9},{9,8},{10,11... | collective-permute-start | bytes 1769480 | tf_op jit(solution)/shard_map/ppermute | solution.py:435
  67.4 14.1 %collective-permute-start.14 = (bf16[128,2048]{1,0:T(8,128)(2,1)S(1)}, bf16[128,2048]{1,0:T(8,128)(2,1)S(1)}, u32[]{:S(2)}, u32[]{:S(2)}) collective-permute-start(bf16[128,2048]{1,0:T(8,128)(2,1)S(1)} %get-tuple-element.143), channel_id=1, source_target_pairs={{0,4},{4,0},{8,12},{12,8},{16,20},{20,16},{24,28},{28,24},{1,5},{5... | collective-permute-start | bytes 1572872 | tf_op jit(solution)/shard_map/ppermute | solution.py:471
  81.6 8.8 %collective-permute-start.19 = (bf16[384,256]{1,0:T(8,128)(2,1)S(1)}, bf16[384,256]{1,0:T(8,128)(2,1)S(1)}, u32[]{:S(2)}, u32[]{:S(2)}) collective-permute-start(bf16[384,256]{1,0:T(8,128)(2,1)S(1)} %get-tuple-element.148), channel_id=1, source_target_pairs={{0,8},{4,12},{8,24},{12,28},{24,16},{28,20},{16,0},{20,4},{1,9},{5... | collective-permute-start | bytes 589832 | tf_op jit(solution)/shard_map/ppermute | solution.py:499
  82.8 18.7 %collective-permute-start.15 = (bf16[96,3072]{1,0:T(8,128)(2,1)S(1)}, bf16[96,3072]{1,0:T(8,128)(2,1)S(1)}, u32[]{:S(2)}, u32[]{:S(2)}) collective-permute-start(bf16[96,3072]{1,0:T(8,128)(2,1)S(1)} %collective-permute-done.6.refs_1_.refs_9_), channel_id=1, source_target_pairs={{0,8},{4,12},{8,24},{12,28},{24,16},{28,20},{16,0},{20,4},{1,9},{5... | collective-permute-start | bytes 1769480 | tf_op jit(solution)/shard_map/ppermute | solution.py:432
  82.8 18.7 %collective-permute-start.17 = (bf16[96,3072]{1,0:T(8,128)(2,1)S(1)}, bf16[96,3072]{1,0:T(8,128)(2,1)S(1)}, u32[]{:S(2)}, u32[]{:S(2)}) collective-permute-start(bf16[96,3072]{1,0:T(8,128)(2,1)S(1)} %collective-permute-done.6.refs_1_.refs_9_), channel_id=1, source_target_pairs={{0,1},{1,0},{2,3},{3,2},{4,5},{5,4},{6,7},{7,6},{8,9},{9,8},{10,11... | collective-permute-start | bytes 1769480 | tf_op jit(solution)/shard_map/ppermute | solution.py:435
  82.8 18.7 %collective-permute-start.16 = (bf16[96,3072]{1,0:T(8,128)(2,1)S(1)}, bf16[96,3072]{1,0:T(8,128)(2,1)S(1)}, u32[]{:S(2)}, u32[]{:S(2)}) collective-permute-start(bf16[96,3072]{1,0:T(8,128)(2,1)S(1)} %collective-permute-done.10.refs_5_.refs_9_), channel_id=1, source_target_pairs={{0,2},{1,3},{2,0},{3,1},{4,6},{5,7},{6,4},{7,5},{8,10},{9,11},{10,... | collective-permute-start | bytes 1769480 | tf_op jit(solution)/shard_map/ppermute | solution.py:435
  84.3 17.2 %collective-permute-start.18 = (bf16[96,3072]{1,0:T(8,128)(2,1)S(1)}, bf16[96,3072]{1,0:T(8,128)(2,1)S(1)}, u32[]{:S(2)}, u32[]{:S(2)}) collective-permute-start(bf16[96,3072]{1,0:T(8,128)(2,1)S(1)} %collective-permute-done.11.refs_3_.refs_11_), channel_id=1, source_target_pairs={{0,1},{1,0},{2,3},{3,2},{4,5},{5,4},{6,7},{7,6},{8,9},{9,8},{10,11... | collective-permute-start | bytes 1769480 | tf_op jit(solution)/shard_map/ppermute | solution.py:435
  90.4 11.0 %collective-permute-start.20 = (bf16[128,2048]{1,0:T(8,128)(2,1)S(1)}, bf16[128,2048]{1,0:T(8,128)(2,1)S(1)}, u32[]{:S(2)}, u32[]{:S(2)}) collective-permute-start(bf16[128,2048]{1,0:T(8,128)(2,1)S(1)} %get-tuple-element.149), channel_id=1, source_target_pairs={{0,4},{4,0},{8,12},{12,8},{16,20},{20,16},{24,28},{28,24},{1,5},{5... | collective-permute-start | bytes 1572872 | tf_op jit(solution)/shard_map/ppermute | solution.py:471
  101.5 19.1 %collective-permute-start.21 = (bf16[96,3072]{1,0:T(8,128)(2,1)S(1)}, bf16[96,3072]{1,0:T(8,128)(2,1)S(1)}, u32[]{:S(2)}, u32[]{:S(2)}) collective-permute-start(bf16[96,3072]{1,0:T(8,128)(2,1)S(1)} %collective-permute-done.10.refs_5_.refs_9_), channel_id=1, source_target_pairs={{0,8},{4,12},{8,24},{12,28},{24,16},{28,20},{16,0},{20,4},{1,9},{5... | collective-permute-start | bytes 1769480 | tf_op jit(solution)/shard_map/ppermute | solution.py:432
  101.9 18.7 %collective-permute-start.23 = (bf16[96,3072]{1,0:T(8,128)(2,1)S(1)}, bf16[96,3072]{1,0:T(8,128)(2,1)S(1)}, u32[]{:S(2)}, u32[]{:S(2)}) collective-permute-start(bf16[96,3072]{1,0:T(8,128)(2,1)S(1)} %collective-permute-done.10.refs_5_.refs_9_), channel_id=1, source_target_pairs={{0,1},{1,0},{2,3},{3,2},{4,5},{5,4},{6,7},{7,6},{8,9},{9,8},{10,11... | collective-permute-start | bytes 1769480 | tf_op jit(solution)/shard_map/ppermute | solution.py:435
  101.9 18.7 %collective-permute-start.22 = (bf16[96,3072]{1,0:T(8,128)(2,1)S(1)}, bf16[96,3072]{1,0:T(8,128)(2,1)S(1)}, u32[]{:S(2)}, u32[]{:S(2)}) collective-permute-start(bf16[96,3072]{1,0:T(8,128)(2,1)S(1)} %collective-permute-done.15.refs_1_.refs_13_), channel_id=1, source_target_pairs={{0,2},{1,3},{2,0},{3,1},{4,6},{5,7},{6,4},{7,5},{8,10},{9,11},{10,... | collective-permute-start | bytes 1769480 | tf_op jit(solution)/shard_map/ppermute | solution.py:435
  103.4 17.2 %collective-permute-start.24 = (bf16[96,3072]{1,0:T(8,128)(2,1)S(1)}, bf16[96,3072]{1,0:T(8,128)(2,1)S(1)}, u32[]{:S(2)}, u32[]{:S(2)}) collective-permute-start(bf16[96,3072]{1,0:T(8,128)(2,1)S(1)} %collective-permute-done.16.refs_7_.refs_11_), channel_id=1, source_target_pairs={{0,1},{1,0},{2,3},{3,2},{4,5},{5,4},{6,7},{7,6},{8,9},{9,8},{10,11... | collective-permute-start | bytes 1769480 | tf_op jit(solution)/shard_map/ppermute | solution.py:435
  103.6 16.5 %collective-permute-start.25 = (bf16[384,256]{1,0:T(8,128)(2,1)S(1)}, bf16[384,256]{1,0:T(8,128)(2,1)S(1)}, u32[]{:S(2)}, u32[]{:S(2)}) collective-permute-start(bf16[384,256]{1,0:T(8,128)(2,1)S(1)} %get-tuple-element.153), channel_id=1, source_target_pairs={{0,16},{4,20},{8,0},{12,4},{24,8},{28,12},{16,24},{20,28},{1,17},{... | collective-permute-start | bytes 589832 | tf_op jit(solution)/shard_map/ppermute | solution.py:505
  120.6 7.4 %collective-permute-start.27 = (bf16[96,3072]{1,0:T(8,128)(2,1)S(1)}, bf16[96,3072]{1,0:T(8,128)(2,1)S(1)}, u32[]{:S(2)}, u32[]{:S(2)}) collective-permute-start(bf16[96,3072]{1,0:T(8,128)(2,1)S(1)} %collective-permute-done.15.refs_1_.refs_13_), channel_id=1, source_target_pairs={{0,1},{1,0},{2,3},{3,2},{4,5},{5,4},{6,7},{7,6},{8,9},{9,8},{10,11... | collective-permute-start | bytes 1769480 | tf_op jit(solution)/shard_map/ppermute | solution.py:435
  120.7 7.4 %collective-permute-start.28 = (bf16[96,3072]{1,0:T(8,128)(2,1)S(1)}, bf16[96,3072]{1,0:T(8,128)(2,1)S(1)}, u32[]{:S(2)}, u32[]{:S(2)}) collective-permute-start(bf16[96,3072]{1,0:T(8,128)(2,1)S(1)} %collective-permute-done.22.refs_3_.refs_15_), channel_id=1, source_target_pairs={{0,1},{1,0},{2,3},{3,2},{4,5},{5,4},{6,7},{7,6},{8,9},{9,8},{10,11... | collective-permute-start | bytes 1769480 | tf_op jit(solution)/shard_map/ppermute | solution.py:435
  121.2 15.3 %collective-permute-start.26 = (bf16[96,3072]{1,0:T(8,128)(2,1)S(1)}, bf16[96,3072]{1,0:T(8,128)(2,1)S(1)}, u32[]{:S(2)}, u32[]{:S(2)}) collective-permute-start(bf16[96,3072]{1,0:T(8,128)(2,1)S(1)} %collective-permute-done.21.refs_1_.refs_13_), channel_id=1, source_target_pairs={{0,2},{1,3},{2,0},{3,1},{4,6},{5,7},{6,4},{7,5},{8,10},{9,11},{10,... | collective-permute-start | bytes 1769480 | tf_op jit(solution)/shard_map/ppermute | solution.py:435
  122.9 9.7 %collective-permute-start.29 = (bf16[384,256]{1,0:T(8,128)(2,1)S(1)}, bf16[384,256]{1,0:T(8,128)(2,1)S(1)}, u32[]{:S(2)}, u32[]{:S(2)}) collective-permute-start(bf16[384,256]{1,0:T(8,128)(2,1)S(1)} %get-tuple-element.164), channel_id=1, source_target_pairs={{0,24},{4,28},{8,16},{12,20},{24,0},{28,4},{16,8},{20,12},{1,25},{... | collective-permute-start | bytes 589832 | tf_op jit(solution)/shard_map/ppermute | solution.py:517
  123.9 10.5 %collective-permute-start.30 = (bf16[384,256]{1,0:T(8,128)(2,1)S(1)}, bf16[384,256]{1,0:T(8,128)(2,1)S(1)}, u32[]{:S(2)}, u32[]{:S(2)}) collective-permute-start(bf16[384,256]{1,0:T(8,128)(2,1)S(1)} %product.6), channel_id=1, source_target_pairs={{0,16},{4,20},{8,0},{12,4},{24,8},{28,12},{16,24},{20,28},{1,17},{... | collective-permute-start | bytes 589832 | tf_op jit(solution)/shard_map/ppermute | solution.py:518
  128.0 17.7 %collective-permute-start.32 = (bf16[96,3072]{1,0:T(8,128)(2,1)S(1)}, bf16[96,3072]{1,0:T(8,128)(2,1)S(1)}, u32[]{:S(2)}, u32[]{:S(2)}) collective-permute-start(bf16[96,3072]{1,0:T(8,128)(2,1)S(1)} %collective-permute-done.21.refs_1_.refs_13_), channel_id=1, source_target_pairs={{0,1},{1,0},{2,3},{3,2},{4,5},{5,4},{6,7},{7,6},{8,9},{9,8},{10,11... | collective-permute-start | bytes 1769480 | tf_op jit(solution)/shard_map/ppermute | solution.py:435
  136.5 9.2 %collective-permute-start.31 = (bf16[96,3072]{1,0:T(8,128)(2,1)S(1)}, bf16[96,3072]{1,0:T(8,128)(2,1)S(1)}, u32[]{:S(2)}, u32[]{:S(2)}) collective-permute-start(bf16[96,3072]{1,0:T(8,128)(2,1)S(1)} %collective-permute-done.26.refs_3_.refs_15_), channel_id=1, source_target_pairs={{0,1},{1,0},{2,3},{3,2},{4,5},{5,4},{6,7},{7,6},{8,9},{9,8},{10,11... | collective-permute-start | bytes 1769480 | tf_op jit(solution)/shard_map/ppermute | solution.py:435
  136.5 9.2 %collective-permute-start.33 = (bf16[384,256]{1,0:T(8,128)(2,1)S(1)}, bf16[384,256]{1,0:T(8,128)(2,1)S(1)}, u32[]{:S(2)}, u32[]{:S(2)}) collective-permute-start(bf16[384,256]{1,0:T(8,128)(2,1)S(1)} %product.8), channel_id=1, source_target_pairs={{0,24},{4,28},{8,16},{12,20},{24,0},{28,4},{16,8},{20,12},{1,25},{... | collective-permute-start | bytes 589832 | tf_op jit(solution)/shard_map/ppermute | solution.py:522
  145.7 36.9 %collective-permute-start.38 = (bf16[128,3072]{1,0:T(8,128)(2,1)}, bf16[128,3072]{1,0:T(8,128)(2,1)}, u32[]{:S(2)}, u32[]{:S(2)}) collective-permute-start(bf16[128,3072]{1,0:T(8,128)(2,1)} %get-tuple-element.211), channel_id=1, source_target_pairs={{0,4},{4,0},{8,12},{12,8},{16,20},{20,16},{24,28},{28,24},{1,5},{5... | collective-permute-start | bytes 2359304 | tf_op jit(solution)/shard_map/ppermute | solution.py:535
  149.1 8.7 %collective-permute-start.34 = (bf16[384,256]{1,0:T(8,128)(2,1)S(1)}, bf16[384,256]{1,0:T(8,128)(2,1)S(1)}, u32[]{:S(2)}, u32[]{:S(2)}) collective-permute-start(bf16[384,256]{1,0:T(8,128)(2,1)S(1)} %product.9), channel_id=1, source_target_pairs={{0,8},{4,12},{8,24},{12,28},{24,16},{28,20},{16,0},{20,4},{1,9},{5... | collective-permute-start | bytes 589832 | tf_op jit(solution)/shard_map/ppermute | solution.py:533
  158.9 1.2 collective-permute-start.35
  160.2 3.6 %collective-permute-start.37 = (f32[1,1024]{1,0:T(1,128)S(1)}, f32[1,1024]{1,0:T(1,128)S(1)}, u32[]{:S(2)}, u32[]{:S(2)}) collective-permute-start(f32[1,1024]{1,0:T(1,128)S(1)} %get-tuple-element.198), channel_id=1, source_target_pairs={{0,8},{4,12},{8,0},{12,4},{16,24},{20,28},{24,16},{28,20},{1,9},{5... | collective-permute-start | bytes 12296 | tf_op jit(solution)/shard_map/ppermute | solution.py:546
  161.0 3.6 %collective-permute-start.36 = (f32[1,384]{1,0:T(1,128)S(1)}, f32[1,384]{1,0:T(1,128)S(1)}, u32[]{:S(2)}, u32[]{:S(2)}) collective-permute-start(f32[1,384]{1,0:T(1,128)S(1)} %add.141.here_ref), channel_id=1, source_target_pairs={{0,2},{1,3},{2,0},{3,1},{4,6},{5,7},{6,4},{7,5},{8,10},{9,11},{10,... | collective-permute-start | bytes 4616 | tf_op jit(solution)/shard_map/ppermute | solution.py:435
  167.7 14.9 %all-to-all-start.2 = ((bf16[8,144,128]{2,1,0:T(8,128)(2,1)}), bf16[8,144,128]{2,1,0:T(8,128)(2,1)S(1)}, u32[]{:S(2)}, u32[]{:S(2)}) async-start(bf16[8,144,128]{2,1,0:T(8,128)(2,1)} %copy-done.20), calls=%async_computation.2 | async-start | bytes 589824 | tf_op jit(solution)/shard_map/all_to_all | solution.py:552
  171.4 10.5 %collective-permute-start.40 = (bf16[128,1024]{1,0:T(8,128)(2,1)}, bf16[128,1024]{1,0:T(8,128)(2,1)S(1)}, u32[]{:S(2)}, u32[]{:S(2)}) collective-permute-start(bf16[128,1024]{1,0:T(8,128)(2,1)} %copy-done.28), channel_id=1, source_target_pairs={{0,4},{4,0},{8,12},{12,8},{16,20},{20,16},{24,28},{28,24},{1,5},{5... | collective-permute-start | bytes 786440 | tf_op jit(solution)/shard_map/ppermute | solution.py:559
  173.4 8.5 %collective-permute-start.39 = (f32[1,1024]{1,0:T(1,128)S(1)}, f32[1,1024]{1,0:T(1,128)S(1)}, u32[]{:S(2)}, u32[]{:S(2)}) collective-permute-start(f32[1,1024]{1,0:T(1,128)S(1)} %add.142), channel_id=1, source_target_pairs={{0,4},{4,0},{8,12},{12,8},{16,20},{20,16},{24,28},{28,24},{1,5},{5... | collective-permute-start | bytes 12296 | tf_op jit(solution)/shard_map/ppermute | solution.py:555
  182.6 19.0 %collective-permute-start.41 = (bf16[128,2048]{1,0:T(8,128)(2,1)}, bf16[128,2048]{1,0:T(8,128)(2,1)}, u32[]{:S(2)}, u32[]{:S(2)}) collective-permute-start(bf16[128,2048]{1,0:T(8,128)(2,1)} %copy-done.27), channel_id=1, source_target_pairs={{0,4},{4,0},{8,12},{12,8},{16,20},{20,16},{24,28},{28,24},{1,5},{5... | collective-permute-start | bytes 1572872 | tf_op jit(solution)/shard_map/ppermute | solution.py:559
  184.5 13.7 %all-to-all-start.3 = ((bf16[8,128,128]{2,1,0:T(8,128)(2,1)}), bf16[8,128,128]{2,1,0:T(8,128)(2,1)S(1)}, u32[]{:S(2)}, u32[]{:S(2)}) async-start(bf16[8,128,128]{2,1,0:T(8,128)(2,1)} %scan.3), calls=%async_computation.3 | async-start | bytes 524288 | tf_op jit(solution)/shard_map/all_to_all | solution.py:573
  189.4 8.2 %collective-permute-start.42 = (f32[1,1024]{1,0:T(1,128)S(1)}, f32[1,1024]{1,0:T(1,128)S(1)}, u32[]{:S(2)}, u32[]{:S(2)}) collective-permute-start(f32[1,1024]{1,0:T(1,128)S(1)} %add.143), channel_id=1, source_target_pairs={{0,16},{4,20},{8,24},{12,28},{16,0},{20,4},{24,8},{28,12},{1,17},{... | collective-permute-start | bytes 12296 | tf_op jit(solution)/shard_map/ppermute | solution.py:577
  (30 other events, 206.4 us)
